TPU v7x, 32 devices: a whole 2x2x4 slice. The times are simulated.
32 devices in a mesh: groups: 2 (over y), orb: 4 (over z), fit: 2 (over x), sub: 2 (over core).
Axes of the slice: x: 2, y: 2, z: 4, core: 2. Of those that a mesh axis runs over, the one named last changes fastest.
Arguments:
- blocks: float32 [16, 256, 2048], P(('groups', 'orb'), None, 'fit'), parts along dimension 0, may hold values from -4 to 4
- pno_coefficients: float32 [32, 64, 256], P(('groups', 'orb', 'sub')), parts along dimension 0, may hold values from -0.375 to 0.375
- domain_map: int32 [32, 256], P(('groups', 'orb', 'sub')), parts along dimension 0, may hold values from -1 to 255, as said below
- pair_first: int32 [32], P('groups'), parts along dimension 0, may hold values from 0 to 7, as said below
- pair_second: int32 [32], P('groups'), parts along dimension 0, may hold values from 0 to 7, as said below
- pno_ranks: int32 [32], P('groups'), parts along dimension 0, may hold values from 8 to 64
- neighbours: int32 [32, 4], P('groups'), parts along dimension 0, may hold values from 0 to 15, as said below
- couplings: float32 [32, 4], P(('groups', 'orb', 'sub')), parts along dimension 0, may hold values from -0.3 to 0.3
- intersections: float32 [32, 4, 4096], P(('groups', 'orb', 'sub')), parts along dimension 0, may hold values from -0.75 to 0.75
- pno_energy: float32 [32, 64], P(('groups', 'orb', 'sub')), parts along dimension 0, may hold values from 0.3 to 3
- occ_energy: float32 [16], P('groups'), parts along dimension 0, may hold values from -1.2 to -0.3
Outputs:
- amplitudes: float32 [32, 4096], P(('groups', 'orb', 'sub')), parts along dimension 0
- gradient: float32 [16, 256, 2048], P(('groups', 'orb'), 'sub', 'fit'), parts along dimension 0
There are 2 independent parts, one for each index of `groups`. A program takes and returns all parts, laid end to end along the dimension named above; each array names one. Nothing has to cross between parts.
Inputs may be any that keep to these rules, and one draw needn't show every extreme that they name: `pair_first`: pair p belongs to orbital owner p // 4; its first orbital is one of that owner's 2 orbitals, o * 2 to (o + 1) * 2 - 1. `pair_second`: not below the pair's first orbital; among the owner's own orbitals or those of owner o + 1; for the last owner among its own. `neighbours`: device d holds pairs d * 2 to (d + 1) * 2 - 1. The neighbour pairs of one device's pairs lie on other devices, at most 2 of them on any one device. `domain_map`: in each row the entries other than -1 are distinct.
All inputs are finite; a program needn't handle non-finite values.
Results may differ from a plain program's by a relative error of at most 0.0003.
Values sent between devices are 32-bit elements; how exact they have to be, the bound alone decides.
No kernel may reach another device: no remote copies, remote signals or barrier semaphores. Data moves between devices by JAX's collectives and lax.ppermute only.
A program may use at most 64 MiB of HBM per device.

v0:
```python
import jax
import jax.numpy as jnp
from jax import lax
from jax.sharding import PartitionSpec as P

ITERS = 2


highest = lax.Precision.HIGHEST


def shifted(value, axis, steps):
    count = lax.axis_size(axis)
    initial, last = (max(0, -steps), min(count, count - steps))
    return lax.ppermute(value, axis, [(source, source + steps) for source in range(initial, last)])


def one_hot(indices, count):
    return (indices[:, None] == jnp.arange(count, dtype=jnp.int32)[None, :]).astype(jnp.float32)


def body(
    blocks,
    pno_coefficients,
    domain_map,
    pair_first,
    pair_second,
    pno_ranks,
    neighbours,
    couplings,
    intersections,
    pno_energy,
    occ_energy,
):
    orbital_count = blocks.shape[0]
    pao_count = blocks.shape[1]
    pair_count = pno_coefficients.shape[0]
    pno_count = pno_coefficients.shape[1]
    link_count = couplings.shape[1]
    square = pno_count * pno_count
    owner_index = lax.axis_index("orb")
    device_index = lax.axis_index(("orb", "sub"))
    pair_start = device_index * pair_count
    first_global = lax.dynamic_slice_in_dim(pair_first, pair_start, pair_count)
    second_global = lax.dynamic_slice_in_dim(pair_second, pair_start, pair_count)
    rank_local = lax.dynamic_slice_in_dim(pno_ranks, pair_start, pair_count)
    wanted = lax.dynamic_slice_in_dim(neighbours, pair_start, pair_count).reshape(-1)
    base_orbital = owner_index * orbital_count
    first_local = first_global - base_orbital
    second_local = second_global - base_orbital
    pao_range = jnp.arange(pao_count, dtype=jnp.int32)
    select = (domain_map[:, :, None] == pao_range[None, None, :]).astype(jnp.float32)
    mapped = jnp.einsum("pna,pac->pnc", pno_coefficients, select, precision=highest)
    left_factor = jnp.einsum(
        "pna,paf->pnf", pno_coefficients, blocks[first_local], precision=highest
    )
    above_blocks = shifted(blocks, "orb", -1)
    window = jnp.concatenate([blocks, above_blocks], axis=0)
    right_factor = jnp.einsum("pnc,pcf->pnf", mapped, window[second_local], precision=highest)
    partial_sums = jnp.einsum("pnf,pmf->pnm", left_factor, right_factor, precision=highest).reshape(
        pair_count, square
    )
    integrals = lax.psum(partial_sums, "fit")
    levels = jnp.arange(pno_count, dtype=jnp.int32)
    kept_levels = (levels[None, :] < rank_local[:, None]).astype(jnp.float32)
    pair_mask = (kept_levels[:, :, None] * kept_levels[:, None, :]).reshape(pair_count, square)
    occ_count = occ_energy.shape[0]
    first_level = jnp.dot(one_hot(first_global, occ_count), occ_energy, precision=highest)
    second_level = jnp.dot(one_hot(second_global, occ_count), occ_energy, precision=highest)
    denominator = (pno_energy[:, :, None] + pno_energy[:, None, :]).reshape(pair_count, square) - (
        first_level + second_level
    )[:, None]
    integrals = integrals * pair_mask
    amplitudes = -integrals / denominator
    intersection = intersections.reshape(pair_count, link_count, pno_count, pno_count)
    for sweep_index in range(ITERS):
        shard_rows = lax.all_gather(amplitudes, ("orb", "sub"), axis=0, tiled=True)
        row_ids = jnp.arange(shard_rows.shape[0], dtype=jnp.int32)
        chooser = (wanted[:, None] == row_ids[None, :]).astype(jnp.float32)
        fetched = jnp.dot(chooser, shard_rows, precision=highest)
        partner_amps = fetched.reshape(pair_count, link_count, pno_count, pno_count)
        inner_left = jnp.einsum("pkab,pkbc->pkac", intersection, partner_amps, precision=highest)
        sandwich = jnp.einsum("pkac,pkdc->pkad", inner_left, intersection, precision=highest)
        coupled = jnp.einsum("pk,pkad->pad", couplings, sandwich, precision=highest).reshape(
            pair_count, square
        )
        amplitudes = pair_mask * (coupled - integrals) / denominator
    square_amps = amplitudes.reshape(pair_count, pno_count, pno_count)
    weights = (2.0 * square_amps - jnp.swapaxes(square_amps, 1, 2)) * pair_mask.reshape(
        pair_count, pno_count, pno_count
    )
    first_half = jnp.einsum("pnm,pmf->pnf", weights, right_factor, precision=highest)
    first_term = jnp.einsum("pna,pnf->paf", pno_coefficients, first_half, precision=highest)
    second_half = jnp.einsum("pmn,pmf->pnf", weights, left_factor, precision=highest)
    second_term = jnp.einsum("pnc,pnf->pcf", mapped, second_half, precision=highest)
    window_gradient = jnp.einsum(
        "po,paf->oaf", one_hot(first_local, 2 * orbital_count), first_term, precision=highest
    )
    window_gradient = window_gradient + jnp.einsum(
        "po,paf->oaf", one_hot(second_local, 2 * orbital_count), second_term, precision=highest
    )
    spill_over = shifted(window_gradient[orbital_count:], "orb", 1)
    own_gradient = window_gradient[:orbital_count] + spill_over
    gradient = lax.psum_scatter(own_gradient, "sub", scatter_dimension=1, tiled=True)
    return (amplitudes, gradient)


def solution(mesh):
    in_specs = (
        P(("groups", "orb"), None, "fit"),
        P(("groups", "orb", "sub"), None, None),
        P(("groups", "orb", "sub"), None),
        P("groups"),
        P("groups"),
        P("groups"),
        P("groups", None),
        P(("groups", "orb", "sub"), None),
        P(("groups", "orb", "sub"), None, None),
        P(("groups", "orb", "sub"), None),
        P("groups"),
    )
    out_specs = (P(("groups", "orb", "sub"), None), P(("groups", "orb"), "sub", "fit"))
    return jax.shard_map(body, mesh=mesh, in_specs=in_specs, out_specs=out_specs, check_vma=False)
```

profile of v0, /device:TPU:0, one launch (start us, length us, event | category | flops | bytes accessed | tf_op | source)
XLA Modules:
  0.0 216.7 jit_solution(4996796773287796597)
XLA Ops:
  7.2 1.3 collective-permute-start
  8.5 1.3 compare_select_fusion
  9.9 2.3 %gather_fusion = f32[2,256,1024]{2,1,0:T(8,128)S(1)} fusion(f32[2,256,1024]{2,1,0:T(8,128)} %param.11, s32[1024]{0:T(1024)S(1)} %pad_clamp_fusion.1), kind=kCustom, calls=%fused_computation | custom fusion | bytes 4194312 | tf_op jit(solution)/shard_map/gather | solution.py:55
  12.6 0.7 mul.47
  13.4 0.7 add.52
  14.3 0.2 reshape.82
  14.5 0.2 convolution_bitcast_fusion
  14.7 0.2 fusion.3
  14.9 1.0 fusion.4
  16.0 1.5 fusion.39
  17.4 40.7 %collective-permute-done = f32[2,256,1024]{2,1,0:T(8,128)} collective-permute-done((f32[2,256,1024]{2,1,0:T(8,128)}, f32[2,256,1024]{2,1,0:T(8,128)}, u32[]{:S(2)}, u32[]{:S(2)}) %collective-permute-start) | collective-permute-done | bytes 2097184 | tf_op jit(solution)/shard_map/ppermute | solution.py:15
  58.1 4.1 %pad_maximum_fusion = f32[4,256,1024]{2,1,0:T(8,128)} fusion(f32[2,256,1024]{2,1,0:T(8,128)} %collective-permute-done, f32[2,256,1024]{2,1,0:T(8,128)S(1)} %copy-done.1), kind=kLoop, calls=%fused_computation.2 | loop fusion | flops 1048576 | bytes 8388608 | tf_op jit(solution)/shard_map/concatenate | solution.py:58
  62.2 2.9 %gather_fusion.1 = f32[2,256,1024]{2,1,0:T(8,128)S(1)} fusion(f32[4,256,1024]{2,1,0:T(8,128)} %pad_maximum_fusion, s32[1024]{0:T(1024)S(1)} %pad_clamp_fusion), kind=kCustom, calls=%fused_computation.1 | custom fusion | bytes 4194312 | tf_op jit(solution)/shard_map/gather | solution.py:59
  65.1 2.3 %fusion.40 = f32[2,64,1024]{2,1,0:T(8,128)S(1)} fusion(f32[2,256,64]{1,2,0:T(8,128)} %fusion.4, f32[2,256,1024]{2,1,0:T(8,128)S(1)} %gather_fusion.1), kind=kOutput, calls=%fused_computation.62 | convolution fusion | flops 402653184 | bytes 2752512 | tf_op jit(solution)/shard_map/pnc,pcf->pnf/dot_general | solution.py:59
  67.4 0.6 fusion.41
  68.1 8.5 %psum.7 = f32[2,4096]{1,0:T(2,128)S(1)} all-reduce(f32[2,4096]{1,0:T(2,128)S(1)} %reshape.80), channel_id=1, replica_groups=mesh['groups'=2,'orb'=4,'fit'=2,'sub'=2] {'fit'}, use_global_device_ids=true, to_apply=%region_0.0 | all-reduce | flops 8192 | bytes 65536 | tf_op jit(solution)/shard_map/psum | solution.py:63
  76.6 0.9 fusion.11
  77.5 14.4 %all-gather = f32[8,2,4096]{2,1,0:T(2,128)S(1)} all-gather(f32[1,2,4096]{2,1,0:T(2,128)S(1)} %get-tuple-element.6), channel_id=1, replica_groups=mesh['groups'=2,'orb'=4,'fit'=2,'sub'=2] {'orb','sub'}, dimensions={0}, use_global_device_ids=true | all-gather | bytes 294912 | tf_op jit(solution)/shard_map/all_gather | solution.py:77
  91.9 0.2 reshape.106
  92.1 0.3 fusion.18
  92.3 0.1 reshape.81
  92.4 0.6 fusion.42
  93.1 0.6 fusion.43
  93.7 0.7 fusion.7
  94.6 14.5 %all-gather.1 = f32[8,2,4096]{2,1,0:T(2,128)S(1)} all-gather(f32[1,2,4096]{2,1,0:T(2,128)S(1)} %fusion.12), channel_id=1, replica_groups=mesh['groups'=2,'orb'=4,'fit'=2,'sub'=2] {'orb','sub'}, dimensions={0}, use_global_device_ids=true | all-gather | bytes 294912 | tf_op jit(solution)/shard_map/all_gather | solution.py:77
  109.1 0.2 reshape.108
  109.3 0.3 fusion.17
  109.5 0.1 reshape.84
  109.6 0.6 fusion.44
  110.3 0.6 fusion.45
  110.9 0.7 fusion.5
  111.8 0.1 reshape.86
  112.0 0.6 fusion.13
  112.6 0.7 fusion.15
  113.3 3.2 %fusion.47 = f32[2,256,1024]{2,1,0:T(8,128)} fusion(f32[2,256,64]{1,2,0:T(8,128)S(1)} %copy-done.3, f32[2,64,1024]{2,1,0:T(8,128)S(1)} %fusion.13), kind=kOutput, calls=%fused_computation.69 | convolution fusion | flops 402653184 | bytes 2752512 | tf_op jit(solution)/shard_map/pnc,pnf->pcf/dot_general | solution.py:95
  116.5 3.2 %fusion.46 = f32[2,1024,256]{2,1,0:T(8,128)} fusion(f32[2,64,1024]{2,1,0:T(8,128)S(1)} %fusion.15, f32[2,64,256]{2,1,0:T(8,128)S(1)} %copy-done), kind=kOutput, calls=%fused_computation.68 | convolution fusion | flops 402653184 | bytes 2752512 | tf_op jit(solution)/shard_map/pna,pnf->paf/dot_general | solution.py:93
  119.7 2.9 %copy.26 = f32[2,1024,256]{1,0,2:T(2,128)S(1)} copy(f32[2,1024,256]{2,1,0:T(8,128)} %fusion.46) | data formatting | bytes 4194304 | tf_op jit(solution)/shard_map/pna,pnf->paf/dot_general | solution.py:93
  122.7 5.3 %fusion = f32[4,256,1024]{2,0,1:T(4,128)S(1)} fusion(f32[2,1024,256]{1,0,2:T(2,128)S(1)} %copy.26, s32[2]{0:T(128)S(1)} %copy-done.11), kind=kOutput, calls=%fused_computation.5 | convolution fusion | flops 25165832 | bytes 6291464 | tf_op jit(solution)/shard_map/po,paf->oaf/dot_general | solution.py:96
  128.0 6.3 %convolution_add_fusion = f32[4,256,1024]{2,0,1:T(4,128)S(1)} fusion(f32[4,256,1024]{2,0,1:T(4,128)S(1)} %fusion, f32[2,256,1024]{2,1,0:T(8,128)S(1)} %copy-done.2, s32[2]{0:T(128)S(1)} %copy-done.13), kind=kOutput, calls=%fused_computation.3 | convolution fusion | flops 26214408 | bytes 10485768 | tf_op jit(solution)/shard_map/po,paf->oaf/dot_general | solution.py:99
  134.2 1.1 slice.13
  135.3 1.7 collective-permute-start.1
  137.0 45.3 %collective-permute-done.1 = f32[2,256,1024]{2,0,1:T(2,128)S(1)} collective-permute-done((f32[2,256,1024]{2,0,1:T(2,128)S(1)}, f32[2,256,1024]{2,0,1:T(2,128)S(1)}, u32[]{:S(2)}, u32[]{:S(2)}) %collective-permute-start.1) | collective-permute-done | bytes 2097184 | tf_op jit(solution)/shard_map/ppermute | solution.py:15
  182.3 2.5 %slice_add_fusion = f32[2,256,1024]{2,0,1:T(2,128)} fusion(f32[2,256,1024]{2,0,1:T(2,128)S(1)} %collective-permute-done.1, f32[4,256,1024]{2,0,1:T(4,128)S(1)} %convolution_add_fusion), kind=kLoop, calls=%fused_computation.4 | loop fusion | flops 524288 | bytes 6291456 | tf_op jit(solution)/shard_map/add | solution.py:103
  184.9 0.6 copy-done.16
  185.5 0.6 dynamic-slice
  186.7 20.5 %all-reduce.3.cloned.1.call-done = f32[2,256,1024]{2,0,1:T(2,128)} async-done(((f32[2,256,1024]{2,0,1:T(2,128)}), f32[2,256,1024]{2,0,1:T(2,128)}) %all-reduce.3.cloned.1.call-update) | async-done | bytes 2097168
  207.2 1.3 constant_dynamic-slice_fusion
  208.5 1.3 copy.20
  (51 shorter events, 1.4 us)
Async XLA Ops:
  7.2 7.8 %copy-start = (f32[2,64,256]{2,1,0:T(8,128)S(1)}, f32[2,64,256]{2,1,0:T(8,128)}, u32[]{:S(2)}) copy-start(f32[2,64,256]{2,1,0:T(8,128)} %param.12) | copy-start | bytes 393220
  7.2 200.0 %all-reduce.3.cloned.1.call-start = ((), (), s32[]{:S(2)}) async-start(), calls=%async_computation | async-start | bytes 4194304
  7.2 50.9 %collective-permute-start = (f32[2,256,1024]{2,1,0:T(8,128)}, f32[2,256,1024]{2,1,0:T(8,128)}, u32[]{:S(2)}, u32[]{:S(2)}) collective-permute-start(f32[2,256,1024]{2,1,0:T(8,128)} %param.11), channel_id=1, source_target_pairs={{4,0},{8,4},{12,8},{5,1},{9,5},{13,9},{6,2},{10,6},{14,10},{7,3},{... | collective-permute-start | bytes 6291464 | tf_op jit(solution)/shard_map/ppermute | solution.py:15
  9.8 2.4 %copy-start.14 = (s32[16]{0:T(128)S(1)}, s32[16]{0:T(128)}, u32[]{:S(2)}) copy-start(s32[16]{0:T(128)} %param.16) | copy-start | bytes 196
  9.8 3.4 %copy-start.9 = (f32[2,64]{1,0:T(2,128)S(1)}, f32[2,64]{1,0:T(2,128)}, u32[]{:S(2)}) copy-start(f32[2,64]{1,0:T(2,128)} %param.20) | copy-start | bytes 1540
  9.9 4.2 %copy-start.12 = (s32[16,4]{0,1:T(4,128)S(1)}, s32[16,4]{0,1:T(4,128)}, u32[]{:S(2)}) copy-start(s32[16,4]{0,1:T(4,128)} %param.17) | copy-start | bytes 772
  9.9 4.5 %copy-start.6 = (f32[2,4,4096]{2,1,0:T(4,128)S(1)}, f32[2,4,4096]{2,1,0:T(4,128)}, u32[]{:S(2)}) copy-start(f32[2,4,4096]{2,1,0:T(4,128)} %param.19) | copy-start | bytes 393220
  9.9 4.6 %copy-start.15 = (f32[8]{0:T(128)S(1)}, f32[8]{0:T(128)}, u32[]{:S(2)}) copy-start(f32[8]{0:T(128)} %param.21) | copy-start | bytes 100
  9.9 5.0 %copy-start.10 = (s32[2,256]{1,0:T(2,128)S(1)}, s32[2,256]{1,0:T(2,128)}, u32[]{:S(2)}) copy-start(s32[2,256]{1,0:T(2,128)} %param.13) | copy-start | bytes 6148
  14.5 43.6 %copy-start.1 = (f32[2,256,1024]{2,1,0:T(8,128)S(1)}, f32[2,256,1024]{2,1,0:T(8,128)}, u32[]{:S(2)}) copy-start(f32[2,256,1024]{2,1,0:T(8,128)} %param.11) | copy-start | bytes 6291460
  67.4 26.3 %copy-start.8 = (f32[2,4]{1,0:T(2,128)S(1)}, f32[2,4]{1,0:T(2,128)}, u32[]{:S(2)}) copy-start(f32[2,4]{1,0:T(2,128)} %param.18) | copy-start | bytes 100
  68.0 26.5 %copy-start.4 = (f32[2,4096]{1,0:T(2,128)S(1)}, f32[2,4096]{1,0:T(2,128)}, u32[]{:S(2)}) copy-start(f32[2,4096]{1,0:T(2,128)} %mul.47) | copy-start | bytes 98308
  68.0 26.5 %copy-start.5 = (f32[2,4096]{1,0:T(2,128)S(1)}, f32[2,4096]{1,0:T(2,128)}, u32[]{:S(2)}) copy-start(f32[2,4096]{1,0:T(2,128)} %add.52) | copy-start | bytes 98308
  110.3 3.1 %copy-start.3 = (f32[2,256,64]{1,2,0:T(8,128)S(1)}, f32[2,256,64]{1,2,0:T(8,128)}, u32[]{:S(2)}) copy-start(f32[2,256,64]{1,2,0:T(8,128)} %fusion.4) | copy-start | bytes 393220
  111.8 4.7 %copy-start.7 = (f32[2,4096]{1,0:T(2,128)}, f32[2,4096]{1,0:T(2,128)S(1)}, u32[]{:S(2)}) copy-start(f32[2,4096]{1,0:T(2,128)S(1)} %multiply_divide_fusion) | copy-start | bytes 98308
  119.7 2.9 %copy-start.11 = (s32[2]{0:T(128)S(1)}, s32[2]{0:T(128)}, u32[]{:S(2)}) copy-start(s32[2]{0:T(128)} %get-tuple-element.15) | copy-start | bytes 28
  122.6 5.3 %copy-start.2 = (f32[2,256,1024]{2,1,0:T(8,128)S(1)}, f32[2,256,1024]{2,1,0:T(8,128)}, u32[]{:S(2)}) copy-start(f32[2,256,1024]{2,1,0:T(8,128)} %fusion.47) | copy-start | bytes 6291460
  122.6 5.3 %copy-start.13 = (s32[2]{0:T(128)S(1)}, s32[2]{0:T(128)}, u32[]{:S(2)}) copy-start(s32[2]{0:T(128)} %get-tuple-element.9) | copy-start | bytes 28
  135.3 47.0 %collective-permute-start.1 = (f32[2,256,1024]{2,0,1:T(2,128)S(1)}, f32[2,256,1024]{2,0,1:T(2,128)S(1)}, u32[]{:S(2)}, u32[]{:S(2)}) collective-permute-start(f32[2,256,1024]{2,0,1:T(2,128)S(1)} %slice.13), channel_id=1, source_target_pairs={{0,4},{4,8},{8,12},{1,5},{5,9},{9,13},{2,6},{6,10},{10,14},{3,7},{... | collective-permute-start | bytes 6291464 | tf_op jit(solution)/shard_map/ppermute | solution.py:15
  184.8 0.7 copy-start.16
Sparse Core Ops, SparseCore 0:
  185.0 22.1 all-reduce.2
where the time goes:
time: 217 us
  waiting for transfers between devices  106 us (49%)
  blocking collectives  37.4 us (17%)
  matrix products  29.3 us (14%)
  local copies, waits for them, and re-layouts  16.1 us (7%)
  between operations  15.1 us (7%)
  other arithmetic  9.23 us (4%)
  starting transfers between devices  2.99 us (1%)
    ppermute x2, waiting for transfers between devices, shifted(): lax.ppermute(value, axis, [(source, source + steps) for source in range(i...  86 us
    all_gather x2, blocking collectives, body(): shard_rows = lax.all_gather(amplitudes, ('orb', 'sub'), axis=0, tiled=True)  28.9 us
    unnamed x2, waiting for transfers between devices  20.5 us
    psum x1, blocking collectives, body(): integrals = lax.psum(partial_sums, 'fit')  8.51 us
    dot_general x1, matrix products, body(): jnp.einsum('po,paf->oaf', one_hot(second_local, 2 * orbital_count), secon...  6.28 us
    dot_general x1, matrix products, body(): jnp.einsum('po,paf->oaf', one_hot(first_local, 2 * orbital_count), first_...  5.28 us
  transfers between devices with their start and end apart: 3, of which 3 were waited for; matrix products, arithmetic and copies ran while one was open for 4% of the time, Pallas kernels for 0%

commit v1 on v0

v1 whole, which is shorter than its diff:
```python
import functools

import jax
import jax.numpy as jnp
from jax import lax
from jax.experimental import pallas as pl
from jax.experimental.pallas import tpu as pltpu
from jax.sharding import PartitionSpec as P

ITERS = 2
SMALL = 4
MIB = 1 << 20
EXTRA = 8

high = lax.Precision.HIGH
smem = pl.BlockSpec(memory_space=pltpu.SMEM)
vmem = pl.BlockSpec(memory_space=pltpu.VMEM)


def mm(a, b, contract=((1,), (0,))):
    return lax.dot_general(
        a, b, (contract, ((), ())), precision=high, preferred_element_type=jnp.float32
    )


def shifted(value, axis, steps):
    count = lax.axis_size(axis)
    initial, last = (max(0, -steps), min(count, count - steps))
    return lax.ppermute(value, axis, [(source, source + steps) for source in range(initial, last)])


def swapped(value, axis):
    return lax.ppermute(value, axis, [(0, 1), (1, 0)])


def owners_of(value):
    count = lax.axis_size("orb")
    if count > SMALL or count & (count - 1):
        return [lax.all_gather(value, "orb", axis=0, tiled=False)]
    return [value[None]] + [
        lax.ppermute(value, "orb", [(s, s ^ step) for s in range(count)])[None]
        for step in range(1, count)
    ]


def f32(flag):
    return flag.astype(jnp.float32)


class Sizes:
    def __init__(self, blocks, pno_coefficients, couplings):
        self.orbitals, self.paos, self.fits = blocks.shape
        self.pairs, self.pnos = pno_coefficients.shape[:2]
        self.links = couplings.shape[1]
        self.subs = lax.axis_size("sub")
        self.owners = lax.axis_size("orb")
        self.own = self.pairs * self.subs
        self.total = self.own * self.owners


def call(kernel, outs, ins, args, scratch=(), limit=16):
    return pl.pallas_call(
        kernel,
        out_shape=[jax.ShapeDtypeStruct(shape, jnp.float32) for shape in outs],
        in_specs=ins,
        out_specs=[vmem] * len(outs),
        scratch_shapes=list(scratch),
        compiler_params=pltpu.CompilerParams(vmem_limit_bytes=limit * MIB),
    )(*args)


def left_kernel(z, first, c_ref, map_ref, b_ref, lm_ref):
    owner, sub = lax.axis_index("orb"), lax.axis_index("sub")
    start = owner * z.own + sub * z.pairs
    rows = lax.broadcasted_iota(jnp.int32, (z.paos, z.paos), 0)
    for p in range(z.pairs):
        c = c_ref[p]
        select = f32(map_ref[p : p + 1, :] == rows)
        lm_ref[p, :, z.fits :] = mm(c, select, ((1,), (1,)))
        lm_ref[p, :, : z.fits] = mm(c, b_ref[first[start + p] - owner * z.orbitals])


def here_kernel(z, second, lm_ref, other_ref, b_ref, right_ref, sums_ref):
    owner, sub = lax.axis_index("orb"), lax.axis_index("sub")
    for side, ref in enumerate((lm_ref, other_ref)):
        start = owner * z.own + (sub if side == 0 else 1 - sub) * z.pairs
        for p in range(z.pairs):
            j = second[start + p] - owner * z.orbitals
            local = jnp.where(j < z.orbitals, 1.0, 0.0)
            mapped = ref[p, :, z.fits :] * local
            right = mm(mapped, b_ref[jnp.minimum(j, z.orbitals - 1)])
            right_ref[side * z.pairs + p] = right
            if side == 0:
                sums_ref[:, p * z.pnos : (p + 1) * z.pnos] = mm(
                    ref[p, :, : z.fits], right, ((1,), (1,))
                )


def below_kernel(z, second, below_ref, sums_ref, b_ref, right_ref, both_ref):
    owner, sub = lax.axis_index("orb"), lax.axis_index("sub")
    start = jnp.maximum(owner - 1, 0) * z.own + sub * z.pairs
    both_ref[0] = sums_ref[...]
    for p in range(z.pairs):
        j = second[start + p] - owner * z.orbitals
        held = jnp.where(j >= 0, 1.0, 0.0)
        mapped = below_ref[p, :, z.fits :] * held
        right = mm(mapped, b_ref[jnp.clip(j, 0, z.orbitals - 1)])
        right_ref[p] = right
        both_ref[1, :, p * z.pnos : (p + 1) * z.pnos] = mm(
            below_ref[p, :, : z.fits], right, ((1,), (1,))
        )


def final_kernel(z, part_count, *refs):
    (first, second, ranks, near, occupied, c_ref, c_other, lm_ref, lm_other, below_ref,
     below_other, here_ref, down_ref, down_other) = refs[:14]
    refs = refs[14:]
    packs, packs_other = refs[:part_count], refs[part_count : 2 * part_count]
    refs = refs[2 * part_count :]
    sums, sums_other = refs[:part_count], refs[part_count : 2 * part_count]
    amp_ref, grad_ref, s_ref, energy, total, start_amp, next_amp, inverse, diag, rows_ref = refs[
        2 * part_count :
    ]
    owner, sub = lax.axis_index("orb"), lax.axis_index("sub")
    n = z.pnos
    diag[...] = jnp.zeros_like(diag)

    def every_owner(action):
        for step in range(part_count):
            if part_count == 1 and z.owners > 1:
                @pl.loop(0, z.owners)
                def _(index):
                    action(step, index, index)
            else:
                action(step, 0, owner ^ step)

    def collect_pack(step, slot, who):
        for side, ref in ((sub, packs[step]), (1 - sub, packs_other[step])):
            for p in range(z.pairs):
                pair = who * z.own + side * z.pairs + p
                s_ref[pair] = ref[slot, p, :n, :]
                energy[pair] = ref[slot, p, n:, :]

    def collect_own(step, slot, who):
        for side, ref in ((sub, sums[step]), (1 - sub, sums_other[step])):
            for p in range(z.pairs):
                pair = who * z.own + side * z.pairs + p
                total[pair] = ref[slot, 0, :, p * n : (p + 1) * n]

    def collect_below(step, slot, who):
        @pl.when(who > 0)
        def _():
            for side, ref in ((sub, sums[step]), (1 - sub, sums_other[step])):
                for p in range(z.pairs):
                    pair = (who - 1) * z.own + side * z.pairs + p
                    total[pair] = total[pair] + ref[slot, 1, :, p * n : (p + 1) * n]

    every_owner(collect_pack)
    every_owner(collect_own)
    every_owner(collect_below)

    row_ids = lax.broadcasted_iota(jnp.int32, (n, n), 0)
    column_ids = lax.broadcasted_iota(jnp.int32, (n, n), 1)
    unroll = 4 if z.owners <= SMALL else 1

    def prepare(pair):
        level = energy[pair, 0:1, :n] * jnp.ones((n, 1), jnp.float32)
        shift = occupied[first[pair]] + occupied[second[pair]]
        rank = ranks[pair]
        kept = f32((row_ids < rank) & (column_ids < rank))
        scale = kept / (level + level.T - shift)
        inverse[pair] = scale
        start_amp[pair] = -total[pair] * scale

    def updated(pair, source, slot):
        for k in range(z.links):
            diag[slot, k * n : (k + 1) * n, k * n : (k + 1) * n] = source[near[pair, k]]
        s = s_ref[pair]
        inner = mm(s, diag[slot]) * energy[pair, 1:2, :]
        coupled = mm(inner, s, ((1,), (1,)))
        return (coupled - total[pair]) * inverse[pair]

    def over_pairs(action):
        if z.owners <= SMALL:
            for pair in range(z.total):
                action(pair, pair % 4)
        else:
            @pl.loop(0, z.total)
            def _(pair):
                action(pair, 0)

    over_pairs(lambda pair, slot: prepare(pair))

    def sweep(pair, slot):
        next_amp[pair] = updated(pair, start_amp, slot)

    over_pairs(sweep)

    half = z.paos // z.subs
    lanes = pl.ds(pl.multiple_of(sub * half, half), half)
    mapped_lanes = pl.ds(pl.multiple_of(z.fits + sub * half, half), half)
    orbital_base = owner * z.orbitals

    def place(index, value, orbital):
        for o in range(z.orbitals):
            rows_ref[index * n : (index + 1) * n, o * half : (o + 1) * half] = jnp.where(
                orbital == o, value, 0.0
            )

    def weights_of(pair, slot):
        amps = updated(pair, next_amp, slot)
        return amps, 2.0 * amps - amps.T

    slot = 0
    for side in range(z.subs):
        for p in range(z.pairs):
            index = side * z.pairs + p
            which = (sub if side == 0 else 1 - sub) * z.pairs + p
            pair = owner * z.own + which
            amps, weights = weights_of(pair, slot % 4)
            slot += 1
            if side == 0:
                amp_ref[p] = amps
            c = (c_ref if side == 0 else c_other)[p, :, lanes]
            mapped = (lm_ref if side == 0 else lm_other)[p, :, mapped_lanes]
            place(index, mm(weights.T, c), first[pair] - orbital_base)
            place(z.own + index, mm(weights, mapped), second[pair] - orbital_base)
            pair = jnp.maximum(owner - 1, 0) * z.own + which
            amps, weights = weights_of(pair, slot % 4)
            slot += 1
            mapped = (below_ref if side == 0 else below_other)[p, :, mapped_lanes]
            place(2 * z.own + index, mm(weights, mapped), second[pair] - orbital_base)

    width = z.own * n

    def factor(own, other, columns):
        return jnp.concatenate([own[:, :, columns], other[:, :, columns]]).reshape(width, -1)

    step = 256
    for start in range(0, z.fits, step):
        columns = slice(start, start + step)
        right = here_ref[:, :, columns].reshape(width, -1) + factor(down_ref, down_other, columns)
        value = mm(rows_ref[:width], right, ((0,), (0,)))
        value += mm(rows_ref[width : 2 * width], factor(lm_ref, lm_other, columns), ((0,), (0,)))
        value += mm(
            rows_ref[2 * width :], factor(below_ref, below_other, columns), ((0,), (0,))
        )
        grad_ref[:, :, columns] = value.reshape(z.orbitals, half, step)


def body(
    blocks,
    pno_coefficients,
    domain_map,
    pair_first,
    pair_second,
    pno_ranks,
    neighbours,
    couplings,
    intersections,
    pno_energy,
    occ_energy,
):
    z = Sizes(blocks, pno_coefficients, couplings)
    n, wide = z.pnos, z.fits + z.paos

    (lm,) = call(
        functools.partial(left_kernel, z),
        [(z.pairs, n, wide)],
        [smem, vmem, vmem, vmem],
        (pair_first, pno_coefficients, domain_map, blocks),
    )
    below = shifted(lm, "orb", 1)
    lm_other = swapped(lm, "sub")
    c_other = swapped(pno_coefficients, "sub")

    later = lax.optimization_barrier((intersections, pno_energy, couplings, lm))
    intersection, energy, coupling, lm = later
    pack = jnp.concatenate(
        [
            intersection.reshape(z.pairs, z.links, n, n)
            .transpose(0, 2, 1, 3)
            .reshape(z.pairs, n, z.links * n),
            jnp.pad(energy, ((0, 0), (0, (z.links - 1) * n)))[:, None, :],
            jnp.repeat(coupling, n, axis=1)[:, None, :],
            jnp.zeros((z.pairs, EXTRA - 2, z.links * n), jnp.float32),
        ],
        axis=1,
    )
    packs = owners_of(pack)
    packs_other = [swapped(part, "sub") for part in packs]

    right_here, sums = call(
        functools.partial(here_kernel, z),
        [(z.own, n, z.fits), (n, z.pairs * n)],
        [smem, vmem, vmem, vmem],
        (pair_second, lm, lm_other, blocks),
    )
    right_below, both = call(
        functools.partial(below_kernel, z),
        [(z.pairs, n, z.fits), (2, n, z.pairs * n)],
        [smem, vmem, vmem, vmem],
        (pair_second, below, sums, blocks),
    )
    if lax.axis_size("fit") == 2:
        both = both + swapped(both, "fit")
    else:
        both = lax.psum(both, "fit")
    parts = owners_of(both)
    parts_other = [swapped(part, "sub") for part in parts]
    down = shifted(right_below, "orb", -1)
    down_other = swapped(down, "sub")
    below_other = swapped(below, "sub")

    args = (
        pair_first, pair_second, pno_ranks, neighbours, occ_energy,
        pno_coefficients, c_other, lm, lm_other, below, below_other,
        right_here, down, down_other, *packs, *packs_other, *parts, *parts_other,
    )
    square = (z.total, n, n)
    amplitudes, gradient = call(
        functools.partial(final_kernel, z, len(packs)),
        [(z.pairs, n, n), (z.orbitals, z.paos // z.subs, z.fits)],
        [smem] * 5 + [vmem] * (len(args) - 5),
        args,
        [
            pltpu.VMEM((z.total, n, z.links * n), jnp.float32),
            pltpu.VMEM((z.total, EXTRA, z.links * n), jnp.float32),
            pltpu.VMEM(square, jnp.float32),
            pltpu.VMEM(square, jnp.float32),
            pltpu.VMEM(square, jnp.float32),
            pltpu.VMEM(square, jnp.float32),
            pltpu.VMEM((4, z.links * n, z.links * n), jnp.float32),
            pltpu.VMEM((3 * z.own * n, z.orbitals * (z.paos // z.subs)), jnp.float32),
        ],
        limit=48,
    )
    return (amplitudes.reshape(z.pairs, -1), gradient)


def solution(mesh):
    in_specs = (
        P(("groups", "orb"), None, "fit"),
        P(("groups", "orb", "sub"), None, None),
        P(("groups", "orb", "sub"), None),
        P("groups"),
        P("groups"),
        P("groups"),
        P("groups", None),
        P(("groups", "orb", "sub"), None),
        P(("groups", "orb", "sub"), None, None),
        P(("groups", "orb", "sub"), None),
        P("groups"),
    )
    out_specs = (P(("groups", "orb", "sub"), None), P(("groups", "orb"), "sub", "fit"))
    return jax.shard_map(body, mesh=mesh, in_specs=in_specs, out_specs=out_specs, check_vma=False)
```

time: 217 us -> 97.1 us (0.45)
  waiting for transfers between devices: 106 us -> 40.7 us
  blocking collectives: 37.4 us -> 0 us
  matrix products: 29.3 us -> 0 us
  Pallas kernels: 0 us -> 19 us
  starting transfers between devices: 2.99 us -> 17.9 us
  between operations: 15.1 us -> 0.83 us
  other arithmetic: 9.23 us -> 0.94 us
    ppermute x2, waiting for transfers between devices: 86 us -> 25 us  [shifted(): lax.ppermute(value, axis, [(source, source + steps) for source in range(i...]
    dot_general x20 -> x0, matrix products: 29.3 us -> none  [the longest x1 6.28 us: body(): jnp.einsum('po,paf->oaf', one_hot(second_local, 2 * orbital_count), secon...]
    all_gather x2 -> x0, blocking collectives: 28.9 us -> none  [body(): shard_rows = lax.all_gather(amplitudes, ('orb', 'sub'), axis=0, tiled=True)]
    unnamed x2 -> x0, waiting for transfers between devices: 20.5 us -> none
    pallas_call x0 -> x4, Pallas kernels: none -> 19 us  [call(): pl.pallas_call(kernel, out_shape=[jax.ShapeDtypeStruct(shape, jnp.float32...]
    ppermute x0 -> x19, waiting for transfers between devices: none -> 15.7 us  [the longest x6 14.3 us: owners_of(): lax.ppermute(value, 'orb', [(s, s ^ step) for s in range(count)])[None]]
    ppermute x0 -> x19, starting transfers between devices: none -> 12.1 us  [the longest x6 8.77 us: owners_of(): lax.ppermute(value, 'orb', [(s, s ^ step) for s in range(count)])[None]]
    unnamed x39 -> x59, local copies, waits for them, and re-layouts: 4.24 us -> 14.8 us
  transfers between devices with their start and end apart: 3 -> 21, of which waited for: 3 -> 9; matrix products, arithmetic and copies ran while one was open for 4% -> 2% of each run, Pallas kernels for 0% -> 2%
where the time goes in v1:
time: 97.1 us; the launch traced here: 96.5 us
  waiting for transfers between devices  40.7 us (42%)
  Pallas kernels  19 us (20%)
  starting transfers between devices  17.9 us (18%)
  local copies, waits for them, and re-layouts  17.2 us (18%)
    ppermute x2, waiting for transfers between devices, shifted(): lax.ppermute(value, axis, [(source, source + steps) for source in range(i...  25 us
    pallas_call x4, Pallas kernels, call(): pl.pallas_call(kernel, out_shape=[jax.ShapeDtypeStruct(shape, jnp.float32...  19 us
    unnamed x59, local copies, waits for them, and re-layouts  14.8 us
    ppermute x6, waiting for transfers between devices, owners_of(): lax.ppermute(value, 'orb', [(s, s ^ step) for s in range(count)])[None]  14.3 us
    ppermute x6, starting transfers between devices, owners_of(): lax.ppermute(value, 'orb', [(s, s ^ step) for s in range(count)])[None]  8.77 us
    ppermute x2, starting transfers between devices, shifted(): lax.ppermute(value, axis, [(source, source + steps) for source in range(i...  5.81 us
    ppermute x13, starting transfers between devices, swapped(): return lax.ppermute(value, axis, [(0, 1), (1, 0)])  3.37 us
  transfers between devices with their start and end apart: 21, of which 9 were waited for; matrix products, arithmetic and copies ran while one was open for 2% of the time, Pallas kernels for 2%

profile of v1, /device:TPU:0, one launch (start us, length us, event | category | flops | bytes accessed | tf_op | source)
XLA Modules:
  0.0 96.5 jit_solution(2951840156517162952)
XLA Ops:
  0.6 1.6 %copy-done = f32[2,256,1024]{2,1,0:T(8,128)S(1)} copy-done((f32[2,256,1024]{2,1,0:T(8,128)S(1)}, f32[2,256,1024]{2,1,0:T(8,128)}, u32[]{:S(2)}) %copy-start) | copy-done | bytes 2097176
  2.2 0.7 copy-done.20
  2.9 0.7 copy-done.21
  3.6 1.9 %shard_map.122.lm_ref.refs_7_ = f32[2,64,1280]{2,1,0:T(8,128)S(1)} custom-call(s32[16]{0:T(128)S(1)} %copy-done.21, f32[2,64,256]{2,1,0:T(8,128)} %refs_5_.1, s32[2,256]{1,0:T(2,128)S(1)} %copy-done.20, f32[2,256,1024]{2,1,0:T(8,128)S(1)} %copy-done), custom_call_target="tpu_custom_call" | custom-call | tf_op jit(solution)/shard_map/pallas_call | solution.py:62
  5.5 0.5 collective-permute-start.1
  6.0 4.5 %collective-permute-start.2 = (f32[2,64,1280]{2,1,0:T(8,128)S(1)}, f32[2,64,1280]{2,1,0:T(8,128)S(1)}, u32[]{:S(2)}, u32[]{:S(2)}) collective-permute-start(f32[2,64,1280]{2,1,0:T(8,128)S(1)} %shard_map.122.lm_ref.refs_7_), channel_id=1, source_target_pairs={{0,4},{4,8},{8,12},{1,5},{5,9},{9,13},{2,6},{6,10},{10,14},{3,7},{... | collective-permute-start | bytes 1966088 | tf_op jit(solution)/shard_map/ppermute | solution.py:29
  10.6 2.0 %shard_map.123 = (f32[4,64,1024]{2,1,0:T(8,128)S(1)}, f32[64,128]{1,0:T(8,128)S(1)}) custom-call(s32[16]{0:T(128)S(1)} %copy-done.19, f32[2,64,1280]{2,1,0:T(8,128)S(1)} %shard_map.122.lm_ref.refs_7_, f32[2,64,1280]{2,1,0:T(8,128)S(1)} %collective-permute-done.1.other_ref.refs_8_, f32[2,256,1024]{2,1,0:T(8,128)S(1)} %copy-done.1), custom_call_target="tpu_custom_call" | custom-call | tf_op jit(solution)/shard_map/pallas_call | solution.py:62
  12.6 1.0 %copy-done.2 = f32[4,64,1024]{2,1,0:T(8,128)} copy-done((f32[4,64,1024]{2,1,0:T(8,128)}, f32[4,64,1024]{2,1,0:T(8,128)S(1)}, u32[]{:S(2)}) %copy-start.2) | copy-done | bytes 1048600
  13.6 11.5 %collective-permute-done.2.below_ref.refs_9_ = f32[2,64,1280]{2,1,0:T(8,128)S(1)} collective-permute-done((f32[2,64,1280]{2,1,0:T(8,128)S(1)}, f32[2,64,1280]{2,1,0:T(8,128)S(1)}, u32[]{:S(2)}, u32[]{:S(2)}) %collective-permute-start.2) | collective-permute-done | bytes 655392 | tf_op jit(solution)/shard_map/ppermute | solution.py:29
  25.1 2.2 %shard_map.124 = (f32[2,64,1024]{2,1,0:T(8,128)}, f32[2,64,128]{2,1,0:T(8,128)S(1)}) custom-call(s32[16]{0:T(128)S(1)} %copy-done.19, f32[2,64,1280]{2,1,0:T(8,128)S(1)} %collective-permute-done.2.below_ref.refs_9_, f32[64,128]{1,0:T(8,128)S(1)} %get-tuple-element.14.sums_ref, f32[2,256,1024]{2,1,0:T(8,128)S(1)} %copy-done.1), custom_call_target="tpu_custom_call" | custom-call | tf_op jit(solution)/shard_map/pallas_call | solution.py:62
  27.3 1.3 %collective-permute-start.4 = (f32[2,64,1024]{2,1,0:T(8,128)}, f32[2,64,1024]{2,1,0:T(8,128)S(1)}, u32[]{:S(2)}, u32[]{:S(2)}) collective-permute-start(f32[2,64,1024]{2,1,0:T(8,128)} %get-tuple-element.15), channel_id=1, source_target_pairs={{4,0},{8,4},{12,8},{5,1},{9,5},{13,9},{6,2},{10,6},{14,10},{7,3},{... | collective-permute-start | bytes 1572872 | tf_op jit(solution)/shard_map/ppermute | solution.py:29
  28.9 0.2 reshape.13
  29.1 0.2 copy.16
  29.3 0.2 reshape.14
  29.6 0.5 collective-permute-start.3
  30.2 13.5 %collective-permute-done.4.refs_12_ = f32[2,64,1024]{2,1,0:T(8,128)S(1)} collective-permute-done((f32[2,64,1024]{2,1,0:T(8,128)}, f32[2,64,1024]{2,1,0:T(8,128)S(1)}, u32[]{:S(2)}, u32[]{:S(2)}) %collective-permute-start.4) | collective-permute-done | bytes 524320 | tf_op jit(solution)/shard_map/ppermute | solution.py:29
  43.7 2.7 %collective-permute-start.7 = (f32[2,72,256]{2,1,0:T(8,128)S(1)}, f32[2,72,256]{2,1,0:T(8,128)S(1)}, u32[]{:S(2)}, u32[]{:S(2)}) collective-permute-start(f32[2,72,256]{2,1,0:T(8,128)S(1)} %get-tuple-element.22), channel_id=1, source_target_pairs={{0,8},{4,12},{8,0},{12,4},{1,9},{5,13},{9,1},{13,5},{2,10},{6,14},... | collective-permute-start | bytes 442376 | tf_op jit(solution)/shard_map/ppermute | solution.py:41
  46.5 1.6 %collective-permute-start.8 = (f32[2,72,256]{2,1,0:T(8,128)S(1)}, f32[2,72,256]{2,1,0:T(8,128)S(1)}, u32[]{:S(2)}, u32[]{:S(2)}) collective-permute-start(f32[2,72,256]{2,1,0:T(8,128)S(1)} %get-tuple-element.22), channel_id=1, source_target_pairs={{0,12},{4,8},{8,4},{12,0},{1,13},{5,9},{9,5},{13,1},{2,14},{6,10},... | collective-permute-start | bytes 442376 | tf_op jit(solution)/shard_map/ppermute | solution.py:41
  48.1 6.3 %collective-permute-done.7 = f32[2,72,256]{2,1,0:T(8,128)S(1)} collective-permute-done((f32[2,72,256]{2,1,0:T(8,128)S(1)}, f32[2,72,256]{2,1,0:T(8,128)S(1)}, u32[]{:S(2)}, u32[]{:S(2)}) %collective-permute-start.7) | collective-permute-done | bytes 147488 | tf_op jit(solution)/shard_map/ppermute | solution.py:41
  54.5 1.5 %collective-permute-start.13 = (f32[2,64,128]{2,1,0:T(8,128)S(1)}, f32[2,64,128]{2,1,0:T(8,128)S(1)}, u32[]{:S(2)}, u32[]{:S(2)}) collective-permute-start(f32[2,64,128]{2,1,0:T(8,128)S(1)} %get-tuple-element.19), channel_id=1, source_target_pairs={{0,2},{2,0},{1,3},{3,1},{4,6},{6,4},{5,7},{7,5},{8,10},{10,8},{9,1... | collective-permute-start | bytes 196616 | tf_op jit(solution)/shard_map/ppermute | solution.py:33
  56.0 2.6 %collective-permute-done.8 = f32[2,72,256]{2,1,0:T(8,128)S(1)} collective-permute-done((f32[2,72,256]{2,1,0:T(8,128)S(1)}, f32[2,72,256]{2,1,0:T(8,128)S(1)}, u32[]{:S(2)}, u32[]{:S(2)}) %collective-permute-start.8) | collective-permute-done | bytes 147488 | tf_op jit(solution)/shard_map/ppermute | solution.py:41
  58.5 0.7 copy-done.5
  59.2 0.5 collective-permute-start.12
  59.7 0.6 copy-done.7
  60.3 0.9 add.5
  61.2 0.6 copy-done.9
  61.9 0.7 copy-done.11
  62.5 2.5 %collective-permute-start.16 = (f32[2,64,128]{2,1,0:T(8,128)S(1)}, f32[2,64,128]{2,1,0:T(8,128)}, u32[]{:S(2)}, u32[]{:S(2)}) collective-permute-start(f32[2,64,128]{2,1,0:T(8,128)S(1)} %add.5), channel_id=1, source_target_pairs={{0,12},{4,8},{8,4},{12,0},{1,13},{5,9},{9,5},{13,1},{2,14},{6,10},... | collective-permute-start | bytes 196616 | tf_op jit(solution)/shard_map/ppermute | solution.py:41
  65.0 0.7 copy-done.13
  65.7 1.5 %collective-permute-start.15 = (f32[2,64,128]{2,1,0:T(8,128)S(1)}, f32[2,64,128]{2,1,0:T(8,128)}, u32[]{:S(2)}, u32[]{:S(2)}) collective-permute-start(f32[2,64,128]{2,1,0:T(8,128)S(1)} %add.5), channel_id=1, source_target_pairs={{0,8},{4,12},{8,0},{12,4},{1,9},{5,13},{9,1},{13,5},{2,10},{6,14},... | collective-permute-start | bytes 196616 | tf_op jit(solution)/shard_map/ppermute | solution.py:41
  67.2 0.6 copy-done.15
  67.8 0.4 collective-permute-start.14
  68.2 0.8 collective-permute-done.16
  69.0 4.2 %collective-permute-done.15 = f32[2,64,128]{2,1,0:T(8,128)} collective-permute-done((f32[2,64,128]{2,1,0:T(8,128)S(1)}, f32[2,64,128]{2,1,0:T(8,128)}, u32[]{:S(2)}, u32[]{:S(2)}) %collective-permute-start.15) | collective-permute-done | bytes 65568 | tf_op jit(solution)/shard_map/ppermute | solution.py:41
  73.3 0.3 collective-permute-done.14
  73.6 0.2 collective-permute-start.18
  73.9 1.0 %collective-permute-done.19.refs_28_ = f32[1,2,64,128]{3,2,1,0:T(8,128)} collective-permute-done((f32[1,2,64,128]{3,2,1,0:T(8,128)}, f32[1,2,64,128]{3,2,1,0:T(8,128)}, u32[]{:S(2)}, u32[]{:S(2)}) %collective-permute-start.19) | collective-permute-done | bytes 65568 | tf_op jit(solution)/shard_map/ppermute | solution.py:33
  74.9 0.4 collective-permute-done.18.refs_27_
  75.2 0.9 copy-done.4
  76.2 0.9 copy-done.6
  77.1 0.9 copy-done.8
  78.0 0.9 copy-done.10
  78.9 0.9 copy-done.12
  79.8 0.9 copy-done.14
  80.7 0.8 copy-done.16
  81.5 12.8 %shard_map.125 = (f32[2,64,64]{2,1,0:T(8,128)S(1)}, f32[2,128,1024]{2,1,0:T(8,128)}) custom-call(s32[16]{0:T(128)S(1)} %copy-done.22, s32[16]{0:T(128)S(1)} %copy-done.19, s32[16]{0:T(128)S(1)} %copy-done.23, s32[16,4]{1,0:T(8,128)S(1)} %copy.14.refs_3_, f32[8]{0:T(128)S(1)} %copy-done.24, f32[2,64,256]{2,1,0:T(8,128)} %refs_5_.1, ...), custom_call_target="tpu_custom_call" | custom-call | tf_op jit(solution)/shard_map/pallas_call | solution.py:62
  94.4 0.6 copy-done.18
  95.0 1.5 %reshape.15 = f32[2,4096]{1,0:T(2,128)} reshape(f32[2,64,64]{2,1,0:T(8,128)} %copy-done.18) | data formatting | bytes 65536 | tf_op jit(solution)/shard_map/reshape | solution.py:338
  (69 shorter events, 0.7 us)
Async XLA Ops:
  0.6 1.6 %copy-start = (f32[2,256,1024]{2,1,0:T(8,128)S(1)}, f32[2,256,1024]{2,1,0:T(8,128)}, u32[]{:S(2)}) copy-start(f32[2,256,1024]{2,1,0:T(8,128)} %b_ref.5) | copy-start | bytes 6291460
  2.2 0.7 copy-start.20
  2.9 0.7 copy-start.21
  3.6 7.0 %copy-start.1 = (f32[2,256,1024]{2,1,0:T(8,128)S(1)}, f32[2,256,1024]{2,1,0:T(8,128)}, u32[]{:S(2)}) copy-start(f32[2,256,1024]{2,1,0:T(8,128)} %b_ref.5) | copy-start | bytes 6291460
  3.6 7.0 %copy-start.19 = (s32[16]{0:T(128)S(1)}, s32[16]{0:T(128)}, u32[]{:S(2)}) copy-start(s32[16]{0:T(128)} %refs_1_.1) | copy-start | bytes 196
  5.5 5.1 %collective-permute-start.1 = (f32[2,64,1280]{2,1,0:T(8,128)S(1)}, f32[2,64,1280]{2,1,0:T(8,128)S(1)}, u32[]{:S(2)}, u32[]{:S(2)}) collective-permute-start(f32[2,64,1280]{2,1,0:T(8,128)S(1)} %shard_map.122.lm_ref.refs_7_), channel_id=1, source_target_pairs={{0,1},{1,0},{2,3},{3,2},{4,5},{5,4},{6,7},{7,6},{8,9},{9,8},{10,11... | collective-permute-start | bytes 1966088 | tf_op jit(solution)/shard_map/ppermute | solution.py:33
  6.0 19.1 %collective-permute-start.2 = (f32[2,64,1280]{2,1,0:T(8,128)S(1)}, f32[2,64,1280]{2,1,0:T(8,128)S(1)}, u32[]{:S(2)}, u32[]{:S(2)}) collective-permute-start(f32[2,64,1280]{2,1,0:T(8,128)S(1)} %shard_map.122.lm_ref.refs_7_), channel_id=1, source_target_pairs={{0,4},{4,8},{8,12},{1,5},{5,9},{9,13},{2,6},{6,10},{10,14},{3,7},{... | collective-permute-start | bytes 1966088 | tf_op jit(solution)/shard_map/ppermute | solution.py:29
  12.6 1.0 %copy-start.2 = (f32[4,64,1024]{2,1,0:T(8,128)}, f32[4,64,1024]{2,1,0:T(8,128)S(1)}, u32[]{:S(2)}) copy-start(f32[4,64,1024]{2,1,0:T(8,128)S(1)} %get-tuple-element.13.refs_11_) | copy-start | bytes 3145732
  13.6 15.1 %copy-start.27 = (f32[2,64]{1,0:T(2,128)S(1)}, f32[2,64]{1,0:T(2,128)}, u32[]{:S(2)}) copy-start(f32[2,64]{1,0:T(2,128)} %param.20) | copy-start | bytes 1540
  13.6 15.2 %copy-start.28 = (f32[2,4]{1,0:T(2,128)S(1)}, f32[2,4]{1,0:T(2,128)}, u32[]{:S(2)}) copy-start(f32[2,4]{1,0:T(2,128)} %param.18) | copy-start | bytes 100
  13.6 15.3 %copy-start.25 = (f32[2,4,4096]{2,1,0:T(4,128)S(1)}, f32[2,4,4096]{2,1,0:T(4,128)}, u32[]{:S(2)}) copy-start(f32[2,4,4096]{2,1,0:T(4,128)} %param.19) | copy-start | bytes 393220
  25.1 48.7 %copy-start.26 = (s32[16,4]{0,1:T(4,128)S(1)}, s32[16,4]{0,1:T(4,128)}, u32[]{:S(2)}) copy-start(s32[16,4]{0,1:T(4,128)} %param.17) | copy-start | bytes 772
  25.1 50.1 %copy-start.22 = (s32[16]{0:T(128)S(1)}, s32[16]{0:T(128)}, u32[]{:S(2)}) copy-start(s32[16]{0:T(128)} %refs_0_.1) | copy-start | bytes 196
  25.1 50.1 %copy-start.23 = (s32[16]{0:T(128)S(1)}, s32[16]{0:T(128)}, u32[]{:S(2)}) copy-start(s32[16]{0:T(128)} %refs_2_.1) | copy-start | bytes 196
  25.1 50.1 %copy-start.24 = (f32[8]{0:T(128)S(1)}, f32[8]{0:T(128)}, u32[]{:S(2)}) copy-start(f32[8]{0:T(128)} %refs_4_.1) | copy-start | bytes 100
  27.3 31.9 %copy-start.17 = (f32[2,64,128]{2,1,0:T(8,128)}, f32[2,64,128]{2,1,0:T(8,128)S(1)}, u32[]{:S(2)}) copy-start(f32[2,64,128]{2,1,0:T(8,128)S(1)} %get-tuple-element.19) | copy-start | bytes 196612
  27.3 16.4 %collective-permute-start.4 = (f32[2,64,1024]{2,1,0:T(8,128)}, f32[2,64,1024]{2,1,0:T(8,128)S(1)}, u32[]{:S(2)}, u32[]{:S(2)}) collective-permute-start(f32[2,64,1024]{2,1,0:T(8,128)} %get-tuple-element.15), channel_id=1, source_target_pairs={{4,0},{8,4},{12,8},{5,1},{9,5},{13,9},{6,2},{10,6},{14,10},{7,3},{... | collective-permute-start | bytes 1572872 | tf_op jit(solution)/shard_map/ppermute | solution.py:29
  28.6 17.8 %collective-permute-start = (f32[2,64,256]{2,1,0:T(8,128)}, f32[2,64,256]{2,1,0:T(8,128)}, u32[]{:S(2)}, u32[]{:S(2)}) collective-permute-start(f32[2,64,256]{2,1,0:T(8,128)} %refs_5_.1), channel_id=1, source_target_pairs={{0,1},{1,0},{2,3},{3,2},{4,5},{5,4},{6,7},{7,6},{8,9},{9,8},{10,11... | collective-permute-start | bytes 393224 | tf_op jit(solution)/shard_map/ppermute | solution.py:33
  29.6 45.6 %collective-permute-start.3 = (f32[2,64,1280]{2,1,0:T(8,128)S(1)}, f32[2,64,1280]{2,1,0:T(8,128)S(1)}, u32[]{:S(2)}, u32[]{:S(2)}) collective-permute-start(f32[2,64,1280]{2,1,0:T(8,128)S(1)} %collective-permute-done.2.below_ref.refs_9_), channel_id=1, source_target_pairs={{0,1},{1,0},{2,3},{3,2},{4,5},{5,4},{6,7},{7,6},{8,9},{9,8},{10,11... | collective-permute-start | bytes 1966088 | tf_op jit(solution)/shard_map/ppermute | solution.py:33
  30.1 16.3 %collective-permute-start.9 = (f32[1,2,72,256]{3,2,1,0:T(8,128)S(1)}, f32[1,2,72,256]{3,2,1,0:T(8,128)S(1)}, u32[]{:S(2)}, u32[]{:S(2)}) collective-permute-start(f32[1,2,72,256]{3,2,1,0:T(8,128)S(1)} %get-tuple-element.23.refs_14_), channel_id=1, source_target_pairs={{0,1},{1,0},{2,3},{3,2},{4,5},{5,4},{6,7},{7,6},{8,9},{9,8},{10,11... | collective-permute-start | bytes 442376 | tf_op jit(solution)/shard_map/ppermute | solution.py:33
  43.7 31.5 %collective-permute-start.5 = (f32[2,64,1024]{2,1,0:T(8,128)S(1)}, f32[2,64,1024]{2,1,0:T(8,128)}, u32[]{:S(2)}, u32[]{:S(2)}) collective-permute-start(f32[2,64,1024]{2,1,0:T(8,128)S(1)} %collective-permute-done.4.refs_12_), channel_id=1, source_target_pairs={{0,1},{1,0},{2,3},{3,2},{4,5},{5,4},{6,7},{7,6},{8,9},{9,8},{10,11... | collective-permute-start | bytes 1572872 | tf_op jit(solution)/shard_map/ppermute | solution.py:33
  43.7 10.7 %collective-permute-start.7 = (f32[2,72,256]{2,1,0:T(8,128)S(1)}, f32[2,72,256]{2,1,0:T(8,128)S(1)}, u32[]{:S(2)}, u32[]{:S(2)}) collective-permute-start(f32[2,72,256]{2,1,0:T(8,128)S(1)} %get-tuple-element.22), channel_id=1, source_target_pairs={{0,8},{4,12},{8,0},{12,4},{1,9},{5,13},{9,1},{13,5},{2,10},{6,14},... | collective-permute-start | bytes 442376 | tf_op jit(solution)/shard_map/ppermute | solution.py:41
  46.5 9.5 %collective-permute-start.6 = (f32[2,72,256]{2,1,0:T(8,128)S(1)}, f32[2,72,256]{2,1,0:T(8,128)S(1)}, u32[]{:S(2)}, u32[]{:S(2)}) collective-permute-start(f32[2,72,256]{2,1,0:T(8,128)S(1)} %get-tuple-element.22), channel_id=1, source_target_pairs={{0,4},{4,0},{8,12},{12,8},{1,5},{5,1},{9,13},{13,9},{2,6},{6,2},{1... | collective-permute-start | bytes 442376 | tf_op jit(solution)/shard_map/ppermute | solution.py:41
  46.5 12.0 %collective-permute-start.8 = (f32[2,72,256]{2,1,0:T(8,128)S(1)}, f32[2,72,256]{2,1,0:T(8,128)S(1)}, u32[]{:S(2)}, u32[]{:S(2)}) collective-permute-start(f32[2,72,256]{2,1,0:T(8,128)S(1)} %get-tuple-element.22), channel_id=1, source_target_pairs={{0,12},{4,8},{8,4},{12,0},{1,13},{5,9},{9,5},{13,1},{2,14},{6,10},... | collective-permute-start | bytes 442376 | tf_op jit(solution)/shard_map/ppermute | solution.py:41
  54.5 19.2 %copy-start.3 = (f32[2,72,256]{2,1,0:T(8,128)}, f32[2,72,256]{2,1,0:T(8,128)S(1)}, u32[]{:S(2)}) copy-start(f32[2,72,256]{2,1,0:T(8,128)S(1)} %collective-permute-done.7) | copy-start | bytes 442372
  54.5 4.7 %collective-permute-start.13 = (f32[2,64,128]{2,1,0:T(8,128)S(1)}, f32[2,64,128]{2,1,0:T(8,128)S(1)}, u32[]{:S(2)}, u32[]{:S(2)}) collective-permute-start(f32[2,64,128]{2,1,0:T(8,128)S(1)} %get-tuple-element.19), channel_id=1, source_target_pairs={{0,2},{2,0},{1,3},{3,1},{4,6},{6,4},{5,7},{7,5},{8,10},{10,8},{9,1... | collective-permute-start | bytes 196616 | tf_op jit(solution)/shard_map/ppermute | solution.py:33
  56.0 5.2 %collective-permute-start.11 = (f32[1,2,72,256]{3,2,1,0:T(8,128)S(1)}, f32[1,2,72,256]{3,2,1,0:T(8,128)S(1)}, u32[]{:S(2)}, u32[]{:S(2)}) collective-permute-start(f32[1,2,72,256]{3,2,1,0:T(8,128)S(1)} %bitcast.14), channel_id=1, source_target_pairs={{0,1},{1,0},{2,3},{3,2},{4,5},{5,4},{6,7},{7,6},{8,9},{9,8},{10,11... | collective-permute-start | bytes 442376 | tf_op jit(solution)/shard_map/ppermute | solution.py:33
  58.5 3.3 %collective-permute-start.10 = (f32[1,2,72,256]{3,2,1,0:T(8,128)S(1)}, f32[1,2,72,256]{3,2,1,0:T(8,128)S(1)}, u32[]{:S(2)}, u32[]{:S(2)}) collective-permute-start(f32[1,2,72,256]{3,2,1,0:T(8,128)S(1)} %bitcast.16), channel_id=1, source_target_pairs={{0,1},{1,0},{2,3},{3,2},{4,5},{5,4},{6,7},{7,6},{8,9},{9,8},{10,11... | collective-permute-start | bytes 442376 | tf_op jit(solution)/shard_map/ppermute | solution.py:33
  58.5 0.7 copy-start.5
  59.2 5.8 %collective-permute-start.12 = (f32[1,2,72,256]{3,2,1,0:T(8,128)S(1)}, f32[1,2,72,256]{3,2,1,0:T(8,128)S(1)}, u32[]{:S(2)}, u32[]{:S(2)}) collective-permute-start(f32[1,2,72,256]{3,2,1,0:T(8,128)S(1)} %bitcast.18), channel_id=1, source_target_pairs={{0,1},{1,0},{2,3},{3,2},{4,5},{5,4},{6,7},{7,6},{8,9},{9,8},{10,11... | collective-permute-start | bytes 442376 | tf_op jit(solution)/shard_map/ppermute | solution.py:33
  59.7 0.6 copy-start.7
  61.2 0.7 copy-start.9
  61.9 5.3 %collective-permute-start.17 = (f32[1,2,64,128]{3,2,1,0:T(8,128)S(1)}, f32[1,2,64,128]{3,2,1,0:T(8,128)S(1)}, u32[]{:S(2)}, u32[]{:S(2)}) collective-permute-start(f32[1,2,64,128]{3,2,1,0:T(8,128)S(1)} %bitcast.12), channel_id=1, source_target_pairs={{0,1},{1,0},{2,3},{3,2},{4,5},{5,4},{6,7},{7,6},{8,9},{9,8},{10,11... | collective-permute-start | bytes 196616 | tf_op jit(solution)/shard_map/ppermute | solution.py:33
  61.9 0.7 copy-start.11
  62.5 6.5 %collective-permute-start.16 = (f32[2,64,128]{2,1,0:T(8,128)S(1)}, f32[2,64,128]{2,1,0:T(8,128)}, u32[]{:S(2)}, u32[]{:S(2)}) collective-permute-start(f32[2,64,128]{2,1,0:T(8,128)S(1)} %add.5), channel_id=1, source_target_pairs={{0,12},{4,8},{8,4},{12,0},{1,13},{5,9},{9,5},{13,1},{2,14},{6,10},... | collective-permute-start | bytes 196616 | tf_op jit(solution)/shard_map/ppermute | solution.py:41
  65.0 0.7 copy-start.13
  65.7 7.6 %collective-permute-start.15 = (f32[2,64,128]{2,1,0:T(8,128)S(1)}, f32[2,64,128]{2,1,0:T(8,128)}, u32[]{:S(2)}, u32[]{:S(2)}) collective-permute-start(f32[2,64,128]{2,1,0:T(8,128)S(1)} %add.5), channel_id=1, source_target_pairs={{0,8},{4,12},{8,0},{12,4},{1,9},{5,13},{9,1},{13,5},{2,10},{6,14},... | collective-permute-start | bytes 196616 | tf_op jit(solution)/shard_map/ppermute | solution.py:41
  67.8 5.8 %collective-permute-start.14 = (f32[2,64,128]{2,1,0:T(8,128)S(1)}, f32[2,64,128]{2,1,0:T(8,128)}, u32[]{:S(2)}, u32[]{:S(2)}) collective-permute-start(f32[2,64,128]{2,1,0:T(8,128)S(1)} %add.5), channel_id=1, source_target_pairs={{0,4},{4,0},{8,12},{12,8},{1,5},{5,1},{9,13},{13,9},{2,6},{6,2},{1... | collective-permute-start | bytes 196616 | tf_op jit(solution)/shard_map/ppermute | solution.py:41
  69.0 4.8 %collective-permute-start.20 = (f32[1,2,64,128]{3,2,1,0:T(8,128)}, f32[1,2,64,128]{3,2,1,0:T(8,128)}, u32[]{:S(2)}, u32[]{:S(2)}) collective-permute-start(f32[1,2,64,128]{3,2,1,0:T(8,128)} %bitcast.8.refs_25_), channel_id=1, source_target_pairs={{0,1},{1,0},{2,3},{3,2},{4,5},{5,4},{6,7},{7,6},{8,9},{9,8},{10,11... | collective-permute-start | bytes 196616 | tf_op jit(solution)/shard_map/ppermute | solution.py:33
  73.3 1.6 %collective-permute-start.19 = (f32[1,2,64,128]{3,2,1,0:T(8,128)}, f32[1,2,64,128]{3,2,1,0:T(8,128)}, u32[]{:S(2)}, u32[]{:S(2)}) collective-permute-start(f32[1,2,64,128]{3,2,1,0:T(8,128)} %bitcast.7.refs_24_), channel_id=1, source_target_pairs={{0,1},{1,0},{2,3},{3,2},{4,5},{5,4},{6,7},{7,6},{8,9},{9,8},{10,11... | collective-permute-start | bytes 196616 | tf_op jit(solution)/shard_map/ppermute | solution.py:33
  73.6 1.6 %collective-permute-start.18 = (f32[1,2,64,128]{3,2,1,0:T(8,128)}, f32[1,2,64,128]{3,2,1,0:T(8,128)}, u32[]{:S(2)}, u32[]{:S(2)}) collective-permute-start(f32[1,2,64,128]{3,2,1,0:T(8,128)} %bitcast.6.refs_23_), channel_id=1, source_target_pairs={{0,1},{1,0},{2,3},{3,2},{4,5},{5,4},{6,7},{7,6},{8,9},{9,8},{10,11... | collective-permute-start | bytes 196616 | tf_op jit(solution)/shard_map/ppermute | solution.py:33
  75.2 0.9 copy-start.4
  76.2 0.9 copy-start.6
  77.1 0.9 copy-start.8
  78.0 0.9 copy-start.10
  78.9 0.9 copy-start.12
  79.8 0.9 copy-start.14
  80.7 0.8 copy-start.16
  (2 other events, 1.2 us)

commit v2 on v1

v2 whole, which is shorter than its diff:
```python
import functools

import jax
import jax.numpy as jnp
from jax import lax
from jax.experimental import pallas as pl
from jax.experimental.pallas import tpu as pltpu
from jax.sharding import PartitionSpec as P

ITERS = 2
SMALL = 4
MIB = 1 << 20
EXTRA = 8

high = lax.Precision.HIGH
smem = pl.BlockSpec(memory_space=pltpu.SMEM)
vmem = pl.BlockSpec(memory_space=pltpu.VMEM)


def mm(a, b, contract=((1,), (0,))):
    return lax.dot_general(
        a, b, (contract, ((), ())), precision=high, preferred_element_type=jnp.float32
    )


def shifted(value, axis, steps):
    count = lax.axis_size(axis)
    initial, last = (max(0, -steps), min(count, count - steps))
    return lax.ppermute(value, axis, [(source, source + steps) for source in range(initial, last)])


def swapped(value, axis):
    return lax.ppermute(value, axis, [(0, 1), (1, 0)])


def owners_of(value):
    count = lax.axis_size("orb")
    if count > SMALL or count & (count - 1):
        return [lax.all_gather(value, "orb", axis=0, tiled=False)]
    return [value[None]] + [
        lax.ppermute(value, "orb", [(s, s ^ step) for s in range(count)])[None]
        for step in range(1, count)
    ]


def f32(flag):
    return flag.astype(jnp.float32)


class Sizes:
    def __init__(self, blocks, pno_coefficients, couplings):
        self.orbitals, self.paos, self.fits = blocks.shape
        self.pairs, self.pnos = pno_coefficients.shape[:2]
        self.links = couplings.shape[1]
        self.subs = lax.axis_size("sub")
        self.owners = lax.axis_size("orb")
        self.own = self.pairs * self.subs
        self.total = self.own * self.owners


anywhere = pl.BlockSpec(memory_space=pl.ANY)
held_out = pl.BlockSpec(memory_space=pltpu.HBM)


def call(kernel, outs, ins, args, scratch=(), limit=16, out_specs=None):
    return pl.pallas_call(
        kernel,
        out_shape=[jax.ShapeDtypeStruct(shape, jnp.float32) for shape in outs],
        in_specs=ins,
        out_specs=out_specs or [vmem] * len(outs),
        scratch_shapes=list(scratch),
        compiler_params=pltpu.CompilerParams(vmem_limit_bytes=limit * MIB),
    )(*args)


def started(sources, targets, sems, base=0):
    copies = [
        pltpu.make_async_copy(source, target, sems.at[base + index])
        for index, (source, target) in enumerate(zip(sources, targets))
    ]
    for copy in copies:
        copy.start()
    return copies


def wait(copies):
    for copy in copies:
        copy.wait()


def side_start(z, owner, sub, side):
    return owner * z.own + (sub if side == 0 else 1 - sub) * z.pairs


def scale_of(z, pair, level, first, second, ranks, occupied):
    n = z.pnos
    row_ids = lax.broadcasted_iota(jnp.int32, (n, n), 0)
    column_ids = lax.broadcasted_iota(jnp.int32, (n, n), 1)
    level = level * jnp.ones((n, 1), jnp.float32)
    rank = ranks[pair]
    kept = f32((row_ids < rank) & (column_ids < rank))
    return kept / (level + level.T - (occupied[first[pair]] + occupied[second[pair]]))


def coupled_of(z, pair, source, near, s, coupling, diag, slot):
    n = z.pnos
    for k in range(z.links):
        diag[slot, k * n : (k + 1) * n, k * n : (k + 1) * n] = source[near[pair, k]]
    inner = mm(s, diag[slot]) * coupling
    return mm(inner, s, ((1,), (1,)))


def each_owner(z, parts, owner, action):
    if len(parts) == 1 and z.owners > 1:
        @pl.loop(0, z.owners)
        def _(index):
            action(0, index, index)
    else:
        for step in range(len(parts)):
            action(step, 0, owner ^ step)


def left_kernel(z, first_in, c_in, map_in, e_in, b_in, lm_ref, e_ref, first, c_ref, map_ref, b_ref,
                sems):
    owner, sub = lax.axis_index("orb"), lax.axis_index("sub")
    copies = started([first_in, c_in, map_in, e_in], [first, c_ref, map_ref, e_ref], sems)
    blocks = started(
        [b_in.at[o] for o in range(z.orbitals)], [b_ref.at[o] for o in range(z.orbitals)], sems, 4
    )
    wait(copies)
    start = side_start(z, owner, sub, 0)
    rows = lax.broadcasted_iota(jnp.int32, (z.paos, z.paos), 0)
    for p in range(z.pairs):
        select = f32(map_ref[p : p + 1, :] == rows)
        lm_ref[p, :, z.fits :] = mm(c_ref[p], select, ((1,), (1,)))
    wait(blocks)
    for p in range(z.pairs):
        lm_ref[p, :, : z.fits] = mm(c_ref[p], b_ref[first[start + p] - owner * z.orbitals])


def here_kernel(z, second, lm_ref, other_ref, b_ref, right_ref, sums_ref):
    owner, sub = lax.axis_index("orb"), lax.axis_index("sub")
    for side, ref in enumerate((lm_ref, other_ref)):
        start = side_start(z, owner, sub, side)
        for p in range(z.pairs):
            j = second[start + p] - owner * z.orbitals
            local = jnp.where(j < z.orbitals, 1.0, 0.0)
            mapped = ref[p, :, z.fits :] * local
            right = mm(mapped, b_ref[jnp.minimum(j, z.orbitals - 1)])
            right_ref[side * z.pairs + p] = right
            if side == 0:
                sums_ref[:, p * z.pnos : (p + 1) * z.pnos] = mm(
                    ref[p, :, : z.fits], right, ((1,), (1,))
                )


def below_kernel(z, first, second, ranks, occupied, e_ref, e_below, below_ref, sums_ref, b_ref,
                 right_ref, both_ref):
    owner, sub = lax.axis_index("orb"), lax.axis_index("sub")
    own_start = side_start(z, owner, sub, 0)
    start = side_start(z, jnp.maximum(owner - 1, 0), sub, 0)
    n = z.pnos
    for p in range(z.pairs):
        lanes = slice(p * n, (p + 1) * n)
        scale = scale_of(z, own_start + p, e_ref[p : p + 1, :], first, second, ranks, occupied)
        both_ref[0, :, lanes] = -sums_ref[:, lanes] * scale
        j = second[start + p] - owner * z.orbitals
        held = jnp.where(j >= 0, 1.0, 0.0)
        mapped = below_ref[p, :, z.fits :] * held
        right = mm(mapped, b_ref[jnp.clip(j, 0, z.orbitals - 1)])
        right_ref[p] = right
        part = mm(below_ref[p, :, : z.fits], right, ((1,), (1,)))
        scale = scale_of(z, start + p, e_below[p : p + 1, :], first, second, ranks, occupied)
        both_ref[1, :, lanes] = -part * scale


def sweep_kernel(z, part_count, first, second, ranks, near, occupied, pack, pack_other, *refs):
    parts, others = refs[:part_count], refs[part_count : 2 * part_count]
    own_ref, start_ref, amps, diag = refs[2 * part_count :]
    owner, sub = lax.axis_index("orb"), lax.axis_index("sub")
    n = z.pnos
    diag[...] = jnp.zeros_like(diag)

    def collect(step, slot, who):
        for side, ref in ((0, parts[step]), (1, others[step])):
            start = side_start(z, who, sub, side)
            for p in range(z.pairs):
                amps[start + p] = ref[slot, 0, :, p * n : (p + 1) * n]

    def collect_above(step, slot, who):
        @pl.when(who > 0)
        def _():
            for side, ref in ((0, parts[step]), (1, others[step])):
                start = side_start(z, who - 1, sub, side)
                for p in range(z.pairs):
                    amps[start + p] = amps[start + p] + ref[slot, 1, :, p * n : (p + 1) * n]

    each_owner(z, parts, owner, collect)
    each_owner(z, parts, owner, collect_above)
    for side, ref in enumerate((pack, pack_other)):
        start = side_start(z, owner, sub, side)
        start_below = side_start(z, jnp.maximum(owner - 1, 0), sub, side)
        for p in range(z.pairs):
            pair, index = start + p, side * z.pairs + p
            begin = amps[pair]
            start_ref[index] = begin
            start_ref[z.own + index] = amps[start_below + p]
            scale = scale_of(z, pair, ref[p, n : n + 1, :n], first, second, ranks, occupied)
            coupled = coupled_of(
                z, pair, amps, near, ref[p, :n, :], ref[p, n + 1 : n + 2, :], diag, index
            )
            own_ref[sub if side == 0 else 1 - sub, :, p * n : (p + 1) * n] = begin + coupled * scale


def final_kernel(z, part_count, first, second, ranks, near, occupied, *refs):
    (c_in, c_other, lm_in, lm_other, below_in, below_other, here_in, down_in, down_other,
     pack_in, pack_other, pack_below, pack_below_other, start_ref) = refs[:14]
    parts = refs[14 : 14 + part_count]
    amp_ref, grad_ref, packs, amps, diag, c_ref, m_ref, rhs, down, rows_ref, sems = refs[
        14 + part_count :
    ]
    owner, sub = lax.axis_index("orb"), lax.axis_index("sub")
    n, pairs, own = z.pnos, z.pairs, z.own
    half = z.paos // z.subs
    at = pl.ds(pl.multiple_of(sub * half, half), half)
    mapped_at = pl.ds(pl.multiple_of(z.fits + sub * half, half), half)
    fits = pl.ds(0, z.fits)
    pack_copies = started(
        [pack_in, pack_other, pack_below, pack_below_other],
        [packs.at[pl.ds(i * pairs, pairs)] for i in range(4)],
        sems,
    )
    small_copies = started(
        [c_in.at[:, :, at], c_other.at[:, :, at], lm_in.at[:, :, mapped_at],
         lm_other.at[:, :, mapped_at], below_in.at[:, :, mapped_at],
         below_other.at[:, :, mapped_at]],
        [c_ref.at[pl.ds(0, pairs)], c_ref.at[pl.ds(pairs, pairs)]]
        + [m_ref.at[pl.ds(i * pairs, pairs)] for i in range(4)],
        sems, 4,
    )
    large_copies = started(
        [here_in, lm_in.at[:, :, fits], lm_other.at[:, :, fits], below_in.at[:, :, fits],
         below_other.at[:, :, fits], down_in, down_other],
        [rhs.at[pl.ds(0, own)]] + [rhs.at[pl.ds(own + i * pairs, pairs)] for i in range(4)]
        + [down.at[pl.ds(0, pairs)], down.at[pl.ds(pairs, pairs)]],
        sems, 10,
    )
    diag[...] = jnp.zeros_like(diag)

    def collect(step, slot, who):
        for which in range(own):
            amps[who * own + which] = parts[step][
                slot, which // pairs, :, (which % pairs) * n : (which % pairs + 1) * n
            ]

    each_owner(z, parts, owner, collect)
    wait(pack_copies)
    wait(small_copies)
    orbital_base = owner * z.orbitals

    def place(index, value, orbital):
        for o in range(z.orbitals):
            rows_ref[index * n : (index + 1) * n, o * half : (o + 1) * half] = jnp.where(
                orbital == o, value, 0.0
            )

    def weights_of(pair, index):
        scale = scale_of(z, pair, packs[index, n : n + 1, :n], first, second, ranks, occupied)
        coupled = coupled_of(
            z, pair, amps, near, packs[index, :n, :], packs[index, n + 1 : n + 2, :], diag,
            index % own,
        )
        found = start_ref[index] + coupled * scale
        return found, 2.0 * found - found.T

    for side in range(z.subs):
        for p in range(pairs):
            index = side * pairs + p
            pair = side_start(z, owner, sub, side) + p
            found, weights = weights_of(pair, index)
            if side == 0:
                amp_ref[p] = found
            place(index, mm(weights.T, c_ref[index]), first[pair] - orbital_base)
            place(own + index, mm(weights, m_ref[index]), second[pair] - orbital_base)
            pair = side_start(z, jnp.maximum(owner - 1, 0), sub, side) + p
            found, weights = weights_of(pair, own + index)
            place(2 * own + index, mm(weights, m_ref[own + index]), second[pair] - orbital_base)

    wait(large_copies)
    width = own * n
    step = 256
    for start in range(0, z.fits, step):
        columns = slice(start, start + step)
        right = (rhs[:own, :, columns] + down[:, :, columns]).reshape(width, -1)
        value = mm(rows_ref[:width], right, ((0,), (0,)))
        value += mm(rows_ref[width:], rhs[own:, :, columns].reshape(2 * width, -1), ((0,), (0,)))
        grad_ref[:, :, columns] = value.reshape(z.orbitals, half, step)


def body(
    blocks,
    pno_coefficients,
    domain_map,
    pair_first,
    pair_second,
    pno_ranks,
    neighbours,
    couplings,
    intersections,
    pno_energy,
    occ_energy,
):
    z = Sizes(blocks, pno_coefficients, couplings)
    n, wide, pairs, own = z.pnos, z.fits + z.paos, z.pairs, z.own
    half = z.paos // z.subs
    room = 24 + z.owners // 8 * 4

    def scratch(*shape):
        return pltpu.VMEM(shape, jnp.float32)

    lm, energy = call(
        functools.partial(left_kernel, z),
        [(pairs, n, wide), pno_energy.shape],
        [anywhere] * 5,
        (pair_first, pno_coefficients, domain_map, pno_energy, blocks),
        [
            pltpu.SMEM(pair_first.shape, jnp.int32),
            scratch(*pno_coefficients.shape),
            pltpu.VMEM(domain_map.shape, jnp.int32),
            scratch(*blocks.shape),
            pltpu.SemaphoreType.DMA((4 + z.orbitals,)),
        ],
    )
    below = shifted(lm, "orb", 1)
    energy_below = shifted(energy, "orb", 1)
    lm_other = swapped(lm, "sub")

    later = lax.optimization_barrier((intersections, couplings, pno_coefficients, energy))
    intersection, coupling, coefficients, energy = later
    pack = jnp.concatenate(
        [
            intersection.reshape(pairs, z.links, n, n)
            .transpose(0, 2, 1, 3)
            .reshape(pairs, n, z.links * n),
            jnp.pad(energy, ((0, 0), (0, (z.links - 1) * n)))[:, None, :],
            jnp.repeat(coupling, n, axis=1)[:, None, :],
            jnp.zeros((pairs, EXTRA - 2, z.links * n), jnp.float32),
        ],
        axis=1,
    )
    c_other = swapped(coefficients, "sub")
    pack_other = swapped(pack, "sub")

    right_here, sums = call(
        functools.partial(here_kernel, z),
        [(own, n, z.fits), (n, pairs * n)],
        [smem, vmem, vmem, vmem],
        (pair_second, lm, lm_other, blocks),
    )
    lists = (pair_first, pair_second, pno_ranks)
    right_below, both = call(
        functools.partial(below_kernel, z),
        [(pairs, n, z.fits), (2, n, pairs * n)],
        [smem] * 4 + [vmem] * 5,
        (*lists, occ_energy, energy, energy_below, below, sums, blocks),
    )
    if lax.axis_size("fit") == 2:
        both = both + swapped(both, "fit")
    else:
        both = lax.psum(both, "fit")
    parts = owners_of(both)
    others = [swapped(part, "sub") for part in parts]
    down = shifted(right_below, "orb", -1)
    pack_late, _ = lax.optimization_barrier((pack, both))
    pack_below = shifted(pack_late, "orb", 1)

    lists = (*lists, neighbours, occ_energy)
    args = (*lists, pack, pack_other, *parts, *others)
    square = (z.total, n, n)
    own_amps, start_amps = call(
        functools.partial(sweep_kernel, z, len(parts)),
        [(z.subs, n, pairs * n), (2 * own, n, n)],
        [smem] * 5 + [vmem] * (len(args) - 5),
        args,
        [scratch(*square), scratch(own, z.links * n, z.links * n)],
    )
    amps = owners_of(own_amps)

    down, below, pack_below, _ = lax.optimization_barrier((down, below, pack_below, own_amps))
    down_other = swapped(down, "sub")
    below_other = swapped(below, "sub")
    pack_below_other = swapped(pack_below, "sub")
    args = (
        *lists, pno_coefficients, c_other, lm, lm_other, below, below_other,
        right_here, down, down_other, pack, pack_other, pack_below, pack_below_other,
        start_amps, *amps,
    )
    amplitudes, gradient = call(
        functools.partial(final_kernel, z, len(amps)),
        [(pairs, n, n), (z.orbitals, half, z.fits)],
        [smem] * 5 + [anywhere] * 13 + [vmem] * (len(args) - 18),
        args,
        [
            scratch(2 * own, n + EXTRA, z.links * n),
            scratch(*square),
            scratch(own, z.links * n, z.links * n),
            scratch(own, n, half),
            scratch(2 * own, n, half),
            scratch(3 * own, n, z.fits),
            scratch(own, n, z.fits),
            scratch(3 * own * n, z.orbitals * half),
            pltpu.SemaphoreType.DMA((17,)),
        ],
        limit=room,
    )
    return (amplitudes.reshape(pairs, -1), gradient)


def solution(mesh):
    in_specs = (
        P(("groups", "orb"), None, "fit"),
        P(("groups", "orb", "sub"), None, None),
        P(("groups", "orb", "sub"), None),
        P("groups"),
        P("groups"),
        P("groups"),
        P("groups", None),
        P(("groups", "orb", "sub"), None),
        P(("groups", "orb", "sub"), None, None),
        P(("groups", "orb", "sub"), None),
        P("groups"),
    )
    out_specs = (P(("groups", "orb", "sub"), None), P(("groups", "orb"), "sub", "fit"))
    return jax.shard_map(body, mesh=mesh, in_specs=in_specs, out_specs=out_specs, check_vma=False)
```

time: 97.1 us -> 82.2 us (0.85)
  waiting for transfers between devices: 40.7 us -> 25 us
  starting transfers between devices: 17.9 us -> 26.8 us
  local copies, waits for them, and re-layouts: 17.2 us -> 9.92 us
  Pallas kernels: 19 us -> 17.2 us
    ppermute x2 -> x4, waiting for transfers between devices: 25 us -> 9.1 us  [shifted(): lax.ppermute(value, axis, [(source, source + steps) for source in range(i...]
    ppermute x2 -> x4, starting transfers between devices: 5.81 us -> 15 us  [shifted(): lax.ppermute(value, axis, [(source, source + steps) for source in range(i...]
    unnamed x59 -> x35, local copies, waits for them, and re-layouts: 14.8 us -> 6.1 us
    ppermute x13 -> x11, waiting for transfers between devices: 1.37 us -> 4.13 us  [swapped(): return lax.ppermute(value, axis, [(0, 1), (1, 0)])]
    ppermute x6, waiting for transfers between devices: 14.3 us -> 11.8 us  [owners_of(): lax.ppermute(value, 'orb', [(s, s ^ step) for s in range(count)])[None]]
    pallas_call x4 -> x5, Pallas kernels: 19 us -> 17.2 us  [call(): pl.pallas_call(kernel, out_shape=[jax.ShapeDtypeStruct(shape, jnp.float32...]
    reshape x4, local copies, waits for them, and re-layouts: 2.11 us -> 3.58 us  [the longest x2 2.02 us: body(): intersection.reshape(pairs, z.links, n, n).transpose(0, 2, 1, 3)]
    ppermute x13 -> x11, starting transfers between devices: 3.37 us -> 3.8 us  [swapped(): return lax.ppermute(value, axis, [(0, 1), (1, 0)])]
  transfers between devices with their start and end apart: 21 -> 21, of which waited for: 9 -> 9; matrix products, arithmetic and copies ran while one was open for 2% -> 6% of each run, Pallas kernels for 2% -> 6%
where the time goes in v2:
time: 82.2 us; the launch traced here: 81.7 us
  starting transfers between devices  26.8 us (33%)
  waiting for transfers between devices  25 us (30%)
  Pallas kernels  17.2 us (21%)
  local copies, waits for them, and re-layouts  9.92 us (12%)
  other arithmetic  1.83 us (2%)
  between operations  0.87 us (1%)
    pallas_call x5, Pallas kernels, call(): pl.pallas_call(kernel, out_shape=[jax.ShapeDtypeStruct(shape, jnp.float32...  17.2 us
    ppermute x4, starting transfers between devices, shifted(): lax.ppermute(value, axis, [(source, source + steps) for source in range(i...  15 us
    ppermute x6, waiting for transfers between devices, owners_of(): lax.ppermute(value, 'orb', [(s, s ^ step) for s in range(count)])[None]  11.8 us
    ppermute x4, waiting for transfers between devices, shifted(): lax.ppermute(value, axis, [(source, source + steps) for source in range(i...  9.1 us
    ppermute x6, starting transfers between devices, owners_of(): lax.ppermute(value, 'orb', [(s, s ^ step) for s in range(count)])[None]  8.03 us
    unnamed x35, local copies, waits for them, and re-layouts  6.1 us
    ppermute x11, waiting for transfers between devices, swapped(): return lax.ppermute(value, axis, [(0, 1), (1, 0)])  4.13 us
    ppermute x11, starting transfers between devices, swapped(): return lax.ppermute(value, axis, [(0, 1), (1, 0)])  3.8 us
  transfers between devices with their start and end apart: 21, of which 9 were waited for; matrix products, arithmetic and copies ran while one was open for 6% of the time, Pallas kernels for 6%

profile of v2, /device:TPU:0, one launch (start us, length us, event | category | flops | bytes accessed | tf_op | source)
XLA Modules:
  0.0 81.7 jit_solution(301629361901099499)
XLA Ops:
  0.6 1.6 %copy-done = f32[2,256,1024]{2,1,0:T(8,128)S(1)} copy-done((f32[2,256,1024]{2,1,0:T(8,128)S(1)}, f32[2,256,1024]{2,1,0:T(8,128)}, u32[]{:S(2)}) %copy-start) | copy-done | bytes 2097176
  2.2 0.9 %copy-done.2 = f32[2,64,256]{2,1,0:T(8,128)S(1)} copy-done((f32[2,64,256]{2,1,0:T(8,128)S(1)}, f32[2,64,256]{2,1,0:T(8,128)}, u32[]{:S(2)}) %copy-start.2) | copy-done | bytes 131096
  3.1 0.7 copy-done.8
  3.8 0.7 copy-done.12
  4.5 0.7 copy-done.13
  5.1 1.8 %shard_map.122 = (f32[2,64,1280]{2,1,0:T(8,128)S(1)}, f32[2,64]{1,0:T(2,128)S(1)}) custom-call(s32[16]{0:T(128)S(1)} %copy-done.8, f32[2,64,256]{2,1,0:T(8,128)S(1)} %copy-done.2, s32[2,256]{1,0:T(2,128)S(1)} %copy-done.12, f32[2,64]{1,0:T(2,128)S(1)} %copy-done.13, f32[2,256,1024]{2,1,0:T(8,128)S(1)} %copy-done), custom_call_target="tpu_custom_call" | custom-call | tf_op jit(solution)/shard_map/pallas_call | solution.py:66
  7.0 0.5 collective-permute-start.1
  7.5 4.5 %collective-permute-start.3 = (f32[2,64,1280]{2,1,0:T(8,128)S(1)}, f32[2,64,1280]{2,1,0:T(8,128)S(1)}, u32[]{:S(2)}, u32[]{:S(2)}) collective-permute-start(f32[2,64,1280]{2,1,0:T(8,128)S(1)} %get-tuple-element.22.lm_ref.refs_2_), channel_id=1, source_target_pairs={{0,4},{4,8},{8,12},{1,5},{5,9},{9,13},{2,6},{6,10},{10,14},{3,7},{... | collective-permute-start | bytes 1966088 | tf_op jit(solution)/shard_map/ppermute | solution.py:29
  12.1 3.4 %collective-permute-start.2 = (f32[2,64]{1,0:T(2,128)S(1)}, f32[2,64]{1,0:T(2,128)S(1)}, u32[]{:S(2)}, u32[]{:S(2)}) collective-permute-start(f32[2,64]{1,0:T(2,128)S(1)} %get-tuple-element.23.e_ref), channel_id=1, source_target_pairs={{0,4},{4,8},{8,12},{1,5},{5,9},{9,13},{2,6},{6,10},{10,14},{3,7},{... | collective-permute-start | bytes 1544 | tf_op jit(solution)/shard_map/ppermute | solution.py:29
  15.5 2.0 %shard_map.123 = (f32[4,64,1024]{2,1,0:T(8,128)S(1)}, f32[64,128]{1,0:T(8,128)S(1)}) custom-call(s32[16]{0:T(128)S(1)} %copy-done.7, f32[2,64,1280]{2,1,0:T(8,128)S(1)} %get-tuple-element.22.lm_ref.refs_2_, f32[2,64,1280]{2,1,0:T(8,128)S(1)} %collective-permute-done.1.other_ref.refs_3_, f32[2,256,1024]{2,1,0:T(8,128)S(1)} %copy-done.1), custom_call_target="tpu_custom_call" | custom-call | tf_op jit(solution)/shard_map/pallas_call | solution.py:66
  17.6 9.1 %collective-permute-done.2.e_below = f32[2,64]{1,0:T(2,128)S(1)} collective-permute-done((f32[2,64]{1,0:T(2,128)S(1)}, f32[2,64]{1,0:T(2,128)S(1)}, u32[]{:S(2)}, u32[]{:S(2)}) %collective-permute-start.2) | collective-permute-done | bytes 544 | tf_op jit(solution)/shard_map/ppermute | solution.py:29
  26.7 2.3 %shard_map.124 = (f32[2,64,1024]{2,1,0:T(8,128)}, f32[2,64,128]{2,1,0:T(8,128)S(1)}) custom-call(s32[16]{0:T(128)S(1)} %copy-done.9, s32[16]{0:T(128)S(1)} %copy-done.7, s32[16]{0:T(128)S(1)} %copy-done.10, f32[8]{0:T(128)S(1)} %copy-done.11, f32[2,64]{1,0:T(2,128)S(1)} %get-tuple-element.23.e_ref, f32[2,64]{1,0:T(2,128)S(1)} %collective-permute-done.2.e_below, ...), custom_call_target="tpu_custom_call" | custom-call | tf_op jit(solution)/shard_map/pallas_call | solution.py:66
  29.0 1.3 %collective-permute-start.4 = (f32[2,64,1024]{2,1,0:T(8,128)}, f32[2,64,1024]{2,1,0:T(8,128)}, u32[]{:S(2)}, u32[]{:S(2)}) collective-permute-start(f32[2,64,1024]{2,1,0:T(8,128)} %get-tuple-element.25), channel_id=1, source_target_pairs={{4,0},{8,4},{12,8},{5,1},{9,5},{13,9},{6,2},{10,6},{14,10},{7,3},{... | collective-permute-start | bytes 1572872 | tf_op jit(solution)/shard_map/ppermute | solution.py:29
  30.3 0.1 broadcast_in_dim.34
  30.4 0.1 broadcast_in_dim_reshape.3
  30.5 0.9 %reshape.13 = f32[2,4,64,64]{3,2,1,0:T(8,128)} reshape(f32[2,4,4096]{2,1,0:T(4,128)S(1)} %copy-done.14) | data formatting | bytes 262144 | tf_op jit(solution)/shard_map/reshape | solution.py:342
  31.4 1.1 %copy.17 = f32[2,4,64,64]{3,1,2,0:T(4,128)S(1)} copy(f32[2,4,64,64]{3,2,1,0:T(8,128)} %reshape.13) | data formatting | bytes 262144 | tf_op jit(solution)/shard_map/reshape | solution.py:342
  32.5 0.9 %reshape.14 = f32[2,64,256]{2,1,0:T(8,128)} reshape(f32[2,64,4,64]{3,2,1,0:T(4,128)S(1)} %bitcast.17) | data formatting | bytes 262144 | tf_op jit(solution)/shard_map/reshape | solution.py:344
  33.4 0.1 pad.8.clone
  33.4 1.0 %maximum_maximum_fusion.pack.refs_9_ = f32[2,72,256]{2,1,0:T(8,128)S(1)} fusion(f32[2,1,256]{2,1,0:T(1,128)S(1)} %broadcast_in_dim_reshape.3, f32[2,1,256]{2,1,0:T(1,128)S(1)} %broadcast_in_dim.33, f32[2,64,256]{2,1,0:T(8,128)} %reshape.14, f32[72]{0:T(128)S(1)} %pad.8.clone), kind=kLoop, calls=%fused_computation.1 | loop fusion | flops 110592 | bytes 282912 | tf_op jit(solution)/shard_map/concatenate | solution.py:340
  34.4 0.1 collective-permute-start.7
  34.5 1.6 %collective-permute-start.5 = (f32[2,64,128]{2,1,0:T(8,128)S(1)}, f32[2,64,128]{2,1,0:T(8,128)S(1)}, u32[]{:S(2)}, u32[]{:S(2)}) collective-permute-start(f32[2,64,128]{2,1,0:T(8,128)S(1)} %get-tuple-element.28), channel_id=1, source_target_pairs={{0,2},{2,0},{1,3},{3,1},{4,6},{6,4},{5,7},{7,5},{8,10},{10,8},{9,1... | collective-permute-start | bytes 196616 | tf_op jit(solution)/shard_map/ppermute | solution.py:33
  36.0 3.0 %collective-permute-done.5 = f32[2,64,128]{2,1,0:T(8,128)S(1)} collective-permute-done((f32[2,64,128]{2,1,0:T(8,128)S(1)}, f32[2,64,128]{2,1,0:T(8,128)S(1)}, u32[]{:S(2)}, u32[]{:S(2)}) %collective-permute-start.5) | collective-permute-done | bytes 65568 | tf_op jit(solution)/shard_map/ppermute | solution.py:33
  39.0 0.9 %add.5 = f32[2,64,128]{2,1,0:T(8,128)S(1)} add(f32[2,64,128]{2,1,0:T(8,128)} %copy-done.6, f32[2,64,128]{2,1,0:T(8,128)S(1)} %collective-permute-done.5) | non-fusion elementwise | flops 16384 | bytes 196608 | tf_op jit(solution)/shard_map/add | solution.py:368
  39.9 0.1 collective-permute-start.11
  39.9 5.7 %collective-permute-start.6 = (f32[2,72,256]{2,1,0:T(8,128)S(1)}, f32[2,72,256]{2,1,0:T(8,128)}, u32[]{:S(2)}, u32[]{:S(2)}) collective-permute-start(f32[2,72,256]{2,1,0:T(8,128)S(1)} %maximum_maximum_fusion.pack.refs_9_), channel_id=1, source_target_pairs={{0,4},{4,8},{8,12},{1,5},{5,9},{9,13},{2,6},{6,10},{10,14},{3,7},{... | collective-permute-start | bytes 442376 | tf_op jit(solution)/shard_map/ppermute | solution.py:29
  45.6 2.0 %collective-permute-start.10 = (f32[2,64,128]{2,1,0:T(8,128)S(1)}, f32[2,64,128]{2,1,0:T(8,128)}, u32[]{:S(2)}, u32[]{:S(2)}) collective-permute-start(f32[2,64,128]{2,1,0:T(8,128)S(1)} %add.5), channel_id=1, source_target_pairs={{0,12},{4,8},{8,4},{12,0},{1,13},{5,9},{9,5},{13,1},{2,14},{6,10},... | collective-permute-start | bytes 196616 | tf_op jit(solution)/shard_map/ppermute | solution.py:41
  47.6 1.3 %collective-permute-start.9 = (f32[2,64,128]{2,1,0:T(8,128)S(1)}, f32[2,64,128]{2,1,0:T(8,128)}, u32[]{:S(2)}, u32[]{:S(2)}) collective-permute-start(f32[2,64,128]{2,1,0:T(8,128)S(1)} %add.5), channel_id=1, source_target_pairs={{0,8},{4,12},{8,0},{12,4},{1,9},{5,13},{9,1},{13,5},{2,10},{6,14},... | collective-permute-start | bytes 196616 | tf_op jit(solution)/shard_map/ppermute | solution.py:41
  48.9 0.6 copy-done.4
  49.5 1.1 %collective-permute-start.8 = (f32[2,64,128]{2,1,0:T(8,128)S(1)}, f32[2,64,128]{2,1,0:T(8,128)}, u32[]{:S(2)}, u32[]{:S(2)}) collective-permute-start(f32[2,64,128]{2,1,0:T(8,128)S(1)} %add.5), channel_id=1, source_target_pairs={{0,4},{4,0},{8,12},{12,8},{1,5},{5,1},{9,13},{13,9},{2,6},{6,2},{1... | collective-permute-start | bytes 196616 | tf_op jit(solution)/shard_map/ppermute | solution.py:41
  50.6 1.2 %collective-permute-done.10 = f32[2,64,128]{2,1,0:T(8,128)} collective-permute-done((f32[2,64,128]{2,1,0:T(8,128)S(1)}, f32[2,64,128]{2,1,0:T(8,128)}, u32[]{:S(2)}, u32[]{:S(2)}) %collective-permute-start.10) | collective-permute-done | bytes 65568 | tf_op jit(solution)/shard_map/ppermute | solution.py:41
  51.9 3.7 %collective-permute-done.9 = f32[2,64,128]{2,1,0:T(8,128)} collective-permute-done((f32[2,64,128]{2,1,0:T(8,128)S(1)}, f32[2,64,128]{2,1,0:T(8,128)}, u32[]{:S(2)}, u32[]{:S(2)}) %collective-permute-start.9) | collective-permute-done | bytes 65568 | tf_op jit(solution)/shard_map/ppermute | solution.py:41
  55.6 0.5 collective-permute-start.12
  56.1 0.1 copy.15.near
  56.2 1.0 %collective-permute-done.13.refs_6_ = f32[1,2,64,128]{3,2,1,0:T(8,128)} collective-permute-done((f32[1,2,64,128]{3,2,1,0:T(8,128)}, f32[1,2,64,128]{3,2,1,0:T(8,128)}, u32[]{:S(2)}, u32[]{:S(2)}) %collective-permute-start.13) | collective-permute-done | bytes 65568 | tf_op jit(solution)/shard_map/ppermute | solution.py:33
  57.2 0.2 collective-permute-done.12.refs_5_
  57.4 0.8 %copy-done.5 = f32[1,2,64,128]{3,2,1,0:T(8,128)S(1)} copy-done((f32[1,2,64,128]{3,2,1,0:T(8,128)S(1)}, f32[1,2,64,128]{3,2,1,0:T(8,128)}, u32[]{:S(2)}) %copy-start.5) | copy-done | bytes 65560
  58.2 2.7 %shard_map.125 = (f32[2,64,128]{2,1,0:T(8,128)S(1)}, f32[8,64,64]{2,1,0:T(8,128)S(1)}) custom-call(s32[16]{0:T(128)S(1)} %copy-done.9, s32[16]{0:T(128)S(1)} %copy-done.7, s32[16]{0:T(128)S(1)} %copy-done.10, s32[16,4]{1,0:T(8,128)S(1)} %copy.15.near, f32[8]{0:T(128)S(1)} %copy-done.11, f32[2,72,256]{2,1,0:T(8,128)S(1)} %maximum_maximum_fusion.pack.refs_9_, ...), custom_call_target="tpu_custom_call" | custom-call | tf_op jit(solution)/shard_map/pallas_call | solution.py:66
  60.9 0.4 collective-permute-start.15
  61.4 0.2 collective-permute-start.16
  61.5 0.4 collective-permute-start
  61.9 0.2 collective-permute-start.17
  62.0 3.6 %collective-permute-start.20 = (f32[2,64,128]{2,1,0:T(8,128)S(1)}, f32[2,64,128]{2,1,0:T(8,128)S(1)}, u32[]{:S(2)}, u32[]{:S(2)}) collective-permute-start(f32[2,64,128]{2,1,0:T(8,128)S(1)} %get-tuple-element.30), channel_id=1, source_target_pairs={{0,12},{4,8},{8,4},{12,0},{1,13},{5,9},{9,5},{13,1},{2,14},{6,10},... | collective-permute-start | bytes 196616 | tf_op jit(solution)/shard_map/ppermute | solution.py:41
  65.7 2.6 %collective-permute-done.20 = f32[2,64,128]{2,1,0:T(8,128)S(1)} collective-permute-done((f32[2,64,128]{2,1,0:T(8,128)S(1)}, f32[2,64,128]{2,1,0:T(8,128)S(1)}, u32[]{:S(2)}, u32[]{:S(2)}) %collective-permute-start.20) | collective-permute-done | bytes 65568 | tf_op jit(solution)/shard_map/ppermute | solution.py:41
  68.3 2.9 %collective-permute-done.19 = f32[2,64,128]{2,1,0:T(8,128)S(1)} collective-permute-done((f32[2,64,128]{2,1,0:T(8,128)S(1)}, f32[2,64,128]{2,1,0:T(8,128)S(1)}, u32[]{:S(2)}, u32[]{:S(2)}) %collective-permute-start.19) | collective-permute-done | bytes 65568 | tf_op jit(solution)/shard_map/ppermute | solution.py:41
  71.2 1.4 %collective-permute-done.18 = f32[2,64,128]{2,1,0:T(8,128)S(1)} collective-permute-done((f32[2,64,128]{2,1,0:T(8,128)S(1)}, f32[2,64,128]{2,1,0:T(8,128)S(1)}, u32[]{:S(2)}, u32[]{:S(2)}) %collective-permute-start.18) | collective-permute-done | bytes 65568 | tf_op jit(solution)/shard_map/ppermute | solution.py:41
  72.5 8.4 %shard_map.126 = (f32[2,64,64]{2,1,0:T(8,128)S(1)}, f32[2,128,1024]{2,1,0:T(8,128)}) custom-call(s32[16]{0:T(128)S(1)} %copy-done.9, s32[16]{0:T(128)S(1)} %copy-done.7, s32[16]{0:T(128)S(1)} %copy-done.10, s32[16,4]{1,0:T(8,128)S(1)} %copy.15.near, f32[8]{0:T(128)S(1)} %copy-done.11, f32[2,64,256]{2,1,0:T(8,128)S(1)} %copy-done.3, ...), custom_call_target="tpu_custom_call" | custom-call | tf_op jit(solution)/shard_map/pallas_call | solution.py:66
  81.0 0.7 reshape.15
  (46 shorter events, 0.1 us)
Async XLA Ops:
  0.6 1.6 %copy-start = (f32[2,256,1024]{2,1,0:T(8,128)S(1)}, f32[2,256,1024]{2,1,0:T(8,128)}, u32[]{:S(2)}) copy-start(f32[2,256,1024]{2,1,0:T(8,128)} %b_ref.3) | copy-start | bytes 6291460
  2.2 0.9 %copy-start.2 = (f32[2,64,256]{2,1,0:T(8,128)S(1)}, f32[2,64,256]{2,1,0:T(8,128)}, u32[]{:S(2)}) copy-start(f32[2,64,256]{2,1,0:T(8,128)} %refs_0_.1) | copy-start | bytes 393220
  3.1 0.7 copy-start.8
  3.8 0.7 copy-start.12
  4.5 0.7 copy-start.13
  5.1 10.4 %copy-start.1 = (f32[2,256,1024]{2,1,0:T(8,128)S(1)}, f32[2,256,1024]{2,1,0:T(8,128)}, u32[]{:S(2)}) copy-start(f32[2,256,1024]{2,1,0:T(8,128)} %b_ref.3) | copy-start | bytes 6291460
  5.1 10.4 %copy-start.7 = (s32[16]{0:T(128)S(1)}, s32[16]{0:T(128)}, u32[]{:S(2)}) copy-start(s32[16]{0:T(128)} %second.7) | copy-start | bytes 196
  7.0 19.7 %copy-start.9 = (s32[16]{0:T(128)S(1)}, s32[16]{0:T(128)}, u32[]{:S(2)}) copy-start(s32[16]{0:T(128)} %first.5) | copy-start | bytes 196
  7.0 19.7 %copy-start.10 = (s32[16]{0:T(128)S(1)}, s32[16]{0:T(128)}, u32[]{:S(2)}) copy-start(s32[16]{0:T(128)} %ranks.5) | copy-start | bytes 196
  7.0 19.7 %copy-start.11 = (f32[8]{0:T(128)S(1)}, f32[8]{0:T(128)}, u32[]{:S(2)}) copy-start(f32[8]{0:T(128)} %occupied.5) | copy-start | bytes 100
  7.0 8.5 %collective-permute-start.1 = (f32[2,64,1280]{2,1,0:T(8,128)S(1)}, f32[2,64,1280]{2,1,0:T(8,128)S(1)}, u32[]{:S(2)}, u32[]{:S(2)}) collective-permute-start(f32[2,64,1280]{2,1,0:T(8,128)S(1)} %get-tuple-element.22.lm_ref.refs_2_), channel_id=1, source_target_pairs={{0,1},{1,0},{2,3},{3,2},{4,5},{5,4},{6,7},{7,6},{8,9},{9,8},{10,11... | collective-permute-start | bytes 1966088 | tf_op jit(solution)/shard_map/ppermute | solution.py:33
  7.5 19.2 %collective-permute-start.3 = (f32[2,64,1280]{2,1,0:T(8,128)S(1)}, f32[2,64,1280]{2,1,0:T(8,128)S(1)}, u32[]{:S(2)}, u32[]{:S(2)}) collective-permute-start(f32[2,64,1280]{2,1,0:T(8,128)S(1)} %get-tuple-element.22.lm_ref.refs_2_), channel_id=1, source_target_pairs={{0,4},{4,8},{8,12},{1,5},{5,9},{9,13},{2,6},{6,10},{10,14},{3,7},{... | collective-permute-start | bytes 1966088 | tf_op jit(solution)/shard_map/ppermute | solution.py:29
  12.1 14.6 %collective-permute-start.2 = (f32[2,64]{1,0:T(2,128)S(1)}, f32[2,64]{1,0:T(2,128)S(1)}, u32[]{:S(2)}, u32[]{:S(2)}) collective-permute-start(f32[2,64]{1,0:T(2,128)S(1)} %get-tuple-element.23.e_ref), channel_id=1, source_target_pairs={{0,4},{4,8},{8,12},{1,5},{5,9},{9,13},{2,6},{6,10},{10,14},{3,7},{... | collective-permute-start | bytes 1544 | tf_op jit(solution)/shard_map/ppermute | solution.py:29
  17.6 12.7 %copy-start.16 = (f32[2,4]{1,0:T(2,128)S(1)}, f32[2,4]{1,0:T(2,128)}, u32[]{:S(2)}) copy-start(f32[2,4]{1,0:T(2,128)} %param.18) | copy-start | bytes 100
  17.6 12.9 %copy-start.14 = (f32[2,4,4096]{2,1,0:T(4,128)S(1)}, f32[2,4,4096]{2,1,0:T(4,128)}, u32[]{:S(2)}) copy-start(f32[2,4,4096]{2,1,0:T(4,128)} %param.19) | copy-start | bytes 393220
  26.7 29.4 %copy-start.15 = (s32[16,4]{0,1:T(4,128)S(1)}, s32[16,4]{0,1:T(4,128)}, u32[]{:S(2)}) copy-start(s32[16,4]{0,1:T(4,128)} %param.17) | copy-start | bytes 772
  26.7 34.8 %copy-start.3 = (f32[2,64,256]{2,1,0:T(8,128)S(1)}, f32[2,64,256]{2,1,0:T(8,128)}, u32[]{:S(2)}) copy-start(f32[2,64,256]{2,1,0:T(8,128)} %refs_0_.1) | copy-start | bytes 393220
  29.0 7.1 %copy-start.6 = (f32[2,64,128]{2,1,0:T(8,128)}, f32[2,64,128]{2,1,0:T(8,128)S(1)}, u32[]{:S(2)}) copy-start(f32[2,64,128]{2,1,0:T(8,128)S(1)} %get-tuple-element.28) | copy-start | bytes 196612
  29.0 31.9 %collective-permute-start.4 = (f32[2,64,1024]{2,1,0:T(8,128)}, f32[2,64,1024]{2,1,0:T(8,128)}, u32[]{:S(2)}, u32[]{:S(2)}) collective-permute-start(f32[2,64,1024]{2,1,0:T(8,128)} %get-tuple-element.25), channel_id=1, source_target_pairs={{4,0},{8,4},{12,8},{5,1},{9,5},{13,9},{6,2},{10,6},{14,10},{7,3},{... | collective-permute-start | bytes 1572872 | tf_op jit(solution)/shard_map/ppermute | solution.py:29
  34.4 13.2 %collective-permute-start.7 = (f32[2,72,256]{2,1,0:T(8,128)S(1)}, f32[2,72,256]{2,1,0:T(8,128)S(1)}, u32[]{:S(2)}, u32[]{:S(2)}) collective-permute-start(f32[2,72,256]{2,1,0:T(8,128)S(1)} %maximum_maximum_fusion.pack.refs_9_), channel_id=1, source_target_pairs={{0,1},{1,0},{2,3},{3,2},{4,5},{5,4},{6,7},{7,6},{8,9},{9,8},{10,11... | collective-permute-start | bytes 442376 | tf_op jit(solution)/shard_map/ppermute | solution.py:33
  34.5 4.5 %collective-permute-start.5 = (f32[2,64,128]{2,1,0:T(8,128)S(1)}, f32[2,64,128]{2,1,0:T(8,128)S(1)}, u32[]{:S(2)}, u32[]{:S(2)}) collective-permute-start(f32[2,64,128]{2,1,0:T(8,128)S(1)} %get-tuple-element.28), channel_id=1, source_target_pairs={{0,2},{2,0},{1,3},{3,1},{4,6},{6,4},{5,7},{7,5},{8,10},{10,8},{9,1... | collective-permute-start | bytes 196616 | tf_op jit(solution)/shard_map/ppermute | solution.py:33
  39.9 9.1 %collective-permute-start.11 = (f32[1,2,64,128]{3,2,1,0:T(8,128)S(1)}, f32[1,2,64,128]{3,2,1,0:T(8,128)S(1)}, u32[]{:S(2)}, u32[]{:S(2)}) collective-permute-start(f32[1,2,64,128]{3,2,1,0:T(8,128)S(1)} %bitcast.11), channel_id=1, source_target_pairs={{0,1},{1,0},{2,3},{3,2},{4,5},{5,4},{6,7},{7,6},{8,9},{9,8},{10,11... | collective-permute-start | bytes 196616 | tf_op jit(solution)/shard_map/ppermute | solution.py:33
  39.9 21.0 %collective-permute-start.6 = (f32[2,72,256]{2,1,0:T(8,128)S(1)}, f32[2,72,256]{2,1,0:T(8,128)}, u32[]{:S(2)}, u32[]{:S(2)}) collective-permute-start(f32[2,72,256]{2,1,0:T(8,128)S(1)} %maximum_maximum_fusion.pack.refs_9_), channel_id=1, source_target_pairs={{0,4},{4,8},{8,12},{1,5},{5,9},{9,13},{2,6},{6,10},{10,14},{3,7},{... | collective-permute-start | bytes 442376 | tf_op jit(solution)/shard_map/ppermute | solution.py:29
  45.6 6.2 %collective-permute-start.10 = (f32[2,64,128]{2,1,0:T(8,128)S(1)}, f32[2,64,128]{2,1,0:T(8,128)}, u32[]{:S(2)}, u32[]{:S(2)}) collective-permute-start(f32[2,64,128]{2,1,0:T(8,128)S(1)} %add.5), channel_id=1, source_target_pairs={{0,12},{4,8},{8,4},{12,0},{1,13},{5,9},{9,5},{13,1},{2,14},{6,10},... | collective-permute-start | bytes 196616 | tf_op jit(solution)/shard_map/ppermute | solution.py:41
  47.6 8.0 %collective-permute-start.9 = (f32[2,64,128]{2,1,0:T(8,128)S(1)}, f32[2,64,128]{2,1,0:T(8,128)}, u32[]{:S(2)}, u32[]{:S(2)}) collective-permute-start(f32[2,64,128]{2,1,0:T(8,128)S(1)} %add.5), channel_id=1, source_target_pairs={{0,8},{4,12},{8,0},{12,4},{1,9},{5,13},{9,1},{13,5},{2,10},{6,14},... | collective-permute-start | bytes 196616 | tf_op jit(solution)/shard_map/ppermute | solution.py:41
  48.9 0.6 copy-start.4
  49.5 6.1 %collective-permute-start.8 = (f32[2,64,128]{2,1,0:T(8,128)S(1)}, f32[2,64,128]{2,1,0:T(8,128)}, u32[]{:S(2)}, u32[]{:S(2)}) collective-permute-start(f32[2,64,128]{2,1,0:T(8,128)S(1)} %add.5), channel_id=1, source_target_pairs={{0,4},{4,0},{8,12},{12,8},{1,5},{5,1},{9,13},{13,9},{2,6},{6,2},{1... | collective-permute-start | bytes 196616 | tf_op jit(solution)/shard_map/ppermute | solution.py:41
  51.9 4.4 %collective-permute-start.14 = (f32[1,2,64,128]{3,2,1,0:T(8,128)}, f32[1,2,64,128]{3,2,1,0:T(8,128)}, u32[]{:S(2)}, u32[]{:S(2)}) collective-permute-start(f32[1,2,64,128]{3,2,1,0:T(8,128)} %bitcast.4.refs_3_), channel_id=1, source_target_pairs={{0,1},{1,0},{2,3},{3,2},{4,5},{5,4},{6,7},{7,6},{8,9},{9,8},{10,11... | collective-permute-start | bytes 196616 | tf_op jit(solution)/shard_map/ppermute | solution.py:33
  55.6 1.6 %collective-permute-start.13 = (f32[1,2,64,128]{3,2,1,0:T(8,128)}, f32[1,2,64,128]{3,2,1,0:T(8,128)}, u32[]{:S(2)}, u32[]{:S(2)}) collective-permute-start(f32[1,2,64,128]{3,2,1,0:T(8,128)} %bitcast.3.refs_2_), channel_id=1, source_target_pairs={{0,1},{1,0},{2,3},{3,2},{4,5},{5,4},{6,7},{7,6},{8,9},{9,8},{10,11... | collective-permute-start | bytes 196616 | tf_op jit(solution)/shard_map/ppermute | solution.py:33
  55.6 1.8 %collective-permute-start.12 = (f32[1,2,64,128]{3,2,1,0:T(8,128)}, f32[1,2,64,128]{3,2,1,0:T(8,128)}, u32[]{:S(2)}, u32[]{:S(2)}) collective-permute-start(f32[1,2,64,128]{3,2,1,0:T(8,128)} %bitcast.2.refs_1_), channel_id=1, source_target_pairs={{0,1},{1,0},{2,3},{3,2},{4,5},{5,4},{6,7},{7,6},{8,9},{9,8},{10,11... | collective-permute-start | bytes 196616 | tf_op jit(solution)/shard_map/ppermute | solution.py:33
  57.4 0.8 %copy-start.5 = (f32[1,2,64,128]{3,2,1,0:T(8,128)S(1)}, f32[1,2,64,128]{3,2,1,0:T(8,128)}, u32[]{:S(2)}) copy-start(f32[1,2,64,128]{3,2,1,0:T(8,128)} %copy-done.4) | copy-start | bytes 196612
  60.9 11.6 %collective-permute-start.15 = (f32[2,64,1280]{2,1,0:T(8,128)S(1)}, f32[2,64,1280]{2,1,0:T(8,128)S(1)}, u32[]{:S(2)}, u32[]{:S(2)}) collective-permute-start(f32[2,64,1280]{2,1,0:T(8,128)S(1)} %collective-permute-done.3.below_ref.refs_4_), channel_id=1, source_target_pairs={{0,1},{1,0},{2,3},{3,2},{4,5},{5,4},{6,7},{7,6},{8,9},{9,8},{10,11... | collective-permute-start | bytes 1966088 | tf_op jit(solution)/shard_map/ppermute | solution.py:33
  61.4 11.2 %collective-permute-start.16 = (f32[2,64,1024]{2,1,0:T(8,128)}, f32[2,64,1024]{2,1,0:T(8,128)S(1)}, u32[]{:S(2)}, u32[]{:S(2)}) collective-permute-start(f32[2,64,1024]{2,1,0:T(8,128)} %collective-permute-done.4.refs_7_), channel_id=1, source_target_pairs={{0,1},{1,0},{2,3},{3,2},{4,5},{5,4},{6,7},{7,6},{8,9},{9,8},{10,11... | collective-permute-start | bytes 1572872 | tf_op jit(solution)/shard_map/ppermute | solution.py:33
  61.5 4.2 %collective-permute-start = (f32[2,64,256]{2,1,0:T(8,128)S(1)}, f32[2,64,256]{2,1,0:T(8,128)S(1)}, u32[]{:S(2)}, u32[]{:S(2)}) collective-permute-start(f32[2,64,256]{2,1,0:T(8,128)S(1)} %copy-done.3), channel_id=1, source_target_pairs={{0,1},{1,0},{2,3},{3,2},{4,5},{5,4},{6,7},{7,6},{8,9},{9,8},{10,11... | collective-permute-start | bytes 393224 | tf_op jit(solution)/shard_map/ppermute | solution.py:33
  61.9 10.7 %collective-permute-start.17 = (f32[2,72,256]{2,1,0:T(8,128)}, f32[2,72,256]{2,1,0:T(8,128)S(1)}, u32[]{:S(2)}, u32[]{:S(2)}) collective-permute-start(f32[2,72,256]{2,1,0:T(8,128)} %collective-permute-done.6.refs_11_), channel_id=1, source_target_pairs={{0,1},{1,0},{2,3},{3,2},{4,5},{5,4},{6,7},{7,6},{8,9},{9,8},{10,11... | collective-permute-start | bytes 442376 | tf_op jit(solution)/shard_map/ppermute | solution.py:33
  62.0 6.2 %collective-permute-start.20 = (f32[2,64,128]{2,1,0:T(8,128)S(1)}, f32[2,64,128]{2,1,0:T(8,128)S(1)}, u32[]{:S(2)}, u32[]{:S(2)}) collective-permute-start(f32[2,64,128]{2,1,0:T(8,128)S(1)} %get-tuple-element.30), channel_id=1, source_target_pairs={{0,12},{4,8},{8,4},{12,0},{1,13},{5,9},{9,5},{13,1},{2,14},{6,10},... | collective-permute-start | bytes 196616 | tf_op jit(solution)/shard_map/ppermute | solution.py:41
  65.7 5.5 %collective-permute-start.19 = (f32[2,64,128]{2,1,0:T(8,128)S(1)}, f32[2,64,128]{2,1,0:T(8,128)S(1)}, u32[]{:S(2)}, u32[]{:S(2)}) collective-permute-start(f32[2,64,128]{2,1,0:T(8,128)S(1)} %get-tuple-element.30), channel_id=1, source_target_pairs={{0,8},{4,12},{8,0},{12,4},{1,9},{5,13},{9,1},{13,5},{2,10},{6,14},... | collective-permute-start | bytes 196616 | tf_op jit(solution)/shard_map/ppermute | solution.py:41
  68.3 4.3 %collective-permute-start.18 = (f32[2,64,128]{2,1,0:T(8,128)S(1)}, f32[2,64,128]{2,1,0:T(8,128)S(1)}, u32[]{:S(2)}, u32[]{:S(2)}) collective-permute-start(f32[2,64,128]{2,1,0:T(8,128)S(1)} %get-tuple-element.30), channel_id=1, source_target_pairs={{0,4},{4,0},{8,12},{12,8},{1,5},{5,1},{9,13},{13,9},{2,6},{6,2},{1... | collective-permute-start | bytes 196616 | tf_op jit(solution)/shard_map/ppermute | solution.py:41

commit v3 on v2

v3 whole, which is shorter than its diff:
```python
import functools

import jax
import jax.numpy as jnp
from jax import lax
from jax.experimental import pallas as pl
from jax.experimental.pallas import tpu as pltpu
from jax.sharding import PartitionSpec as P

ITERS = 2
SMALL = 4
MIB = 1 << 20
EXTRA = 8

high = lax.Precision.HIGH
smem = pl.BlockSpec(memory_space=pltpu.SMEM)
vmem = pl.BlockSpec(memory_space=pltpu.VMEM)


def mm(a, b, contract=((1,), (0,))):
    return lax.dot_general(
        a, b, (contract, ((), ())), precision=high, preferred_element_type=jnp.float32
    )


def shifted(value, axis, steps):
    count = lax.axis_size(axis)
    initial, last = (max(0, -steps), min(count, count - steps))
    return lax.ppermute(value, axis, [(source, source + steps) for source in range(initial, last)])


def swapped(value, axis):
    return lax.ppermute(value, axis, [(0, 1), (1, 0)])


def owners_of(value):
    count = lax.axis_size("orb")
    if count > SMALL or count & (count - 1):
        return [lax.all_gather(value, "orb", axis=0, tiled=False)]
    return [value[None]] + [
        lax.ppermute(value, "orb", [(s, s ^ step) for s in range(count)])[None]
        for step in range(1, count)
    ]


def f32(flag):
    return flag.astype(jnp.float32)


class Sizes:
    def __init__(self, blocks, pno_coefficients, couplings):
        self.orbitals, self.paos, self.fits = blocks.shape
        self.pairs, self.pnos = pno_coefficients.shape[:2]
        self.links = couplings.shape[1]
        self.subs = lax.axis_size("sub")
        self.owners = lax.axis_size("orb")
        self.own = self.pairs * self.subs
        self.total = self.own * self.owners


anywhere = pl.BlockSpec(memory_space=pl.ANY)
held_out = pl.BlockSpec(memory_space=pltpu.HBM)


def call(kernel, outs, ins, args, scratch=(), limit=16, out_specs=None):
    return pl.pallas_call(
        kernel,
        out_shape=[jax.ShapeDtypeStruct(shape, jnp.float32) for shape in outs],
        in_specs=ins,
        out_specs=out_specs or [vmem] * len(outs),
        scratch_shapes=list(scratch),
        compiler_params=pltpu.CompilerParams(vmem_limit_bytes=limit * MIB),
    )(*args)


def started(sources, targets, sems, base=0):
    copies = [
        pltpu.make_async_copy(source, target, sems.at[base + index])
        for index, (source, target) in enumerate(zip(sources, targets))
    ]
    for copy in copies:
        copy.start()
    return copies


def wait(copies):
    for copy in copies:
        copy.wait()


def side_start(z, owner, sub, side):
    return owner * z.own + (sub if side == 0 else 1 - sub) * z.pairs


def scale_of(z, pair, level, first, second, ranks, occupied):
    n = z.pnos
    row_ids = lax.broadcasted_iota(jnp.int32, (n, n), 0)
    column_ids = lax.broadcasted_iota(jnp.int32, (n, n), 1)
    level = level * jnp.ones((n, 1), jnp.float32)
    rank = ranks[pair]
    kept = f32((row_ids < rank) & (column_ids < rank))
    return kept / (level + level.T - (occupied[first[pair]] + occupied[second[pair]]))


def split(value):
    high_part = value.astype(jnp.bfloat16)
    return high_part, (value - high_part.astype(jnp.float32)).astype(jnp.bfloat16)


def mm3(a, b, contract=((1,), (0,))):
    def one(x, y):
        return lax.dot_general(x, y, (contract, ((), ())), preferred_element_type=jnp.float32)

    return one(a[0], b[0]) + (one(a[0], b[1]) + one(a[1], b[0]))


def each_owner(z, parts, owner, action):
    if len(parts) == 1 and z.owners > 1:
        @pl.loop(0, z.owners)
        def _(index):
            action(0, index, index)
    else:
        for step in range(len(parts)):
            action(step, 0, owner ^ step)


def split_all(z, amps, amps_high, amps_low):
    def one(row):
        amps_high[row], amps_low[row] = split(amps[row])

    if z.owners <= SMALL:
        for row in range(z.own, z.own + z.total):
            one(row)
    else:
        @pl.loop(z.own, z.own + z.total)
        def _(row):
            one(row)


def coupled_of(z, pair_list, near, packs, amps_high, amps_low, diag_high, diag_low):
    n = z.pnos
    diag_high[...] = jnp.zeros_like(diag_high)
    diag_low[...] = jnp.zeros_like(diag_low)
    for index, pair in enumerate(pair_list):
        for k in range(z.links):
            row = near[pair, k] + z.own
            block = slice(k * n, (k + 1) * n)
            diag_high[index, block, block] = amps_high[row]
            diag_low[index, block, block] = amps_low[row]
    parts = [split(pack[:n, :]) for pack in packs]
    inner = [
        mm3(part, (diag_high[index], diag_low[index])) for index, part in enumerate(parts)
    ]
    inner = [split(value * pack[n : n + 1, :]) for value, pack in zip(inner, packs)]
    return [mm3(value, part, ((1,), (1,))) for value, part in zip(inner, parts)]


def mapped_kernel(z, c_in, map_in, e_in, mp_ref, c_ref, map_ref, e_ref, sems):
    n = z.pnos
    wait(started([c_in, map_in, e_in], [c_ref, map_ref, e_ref], sems))
    rows = lax.broadcasted_iota(jnp.int32, (z.paos, z.paos), 0)
    for p in range(z.pairs):
        select = f32(map_ref[p : p + 1, :] == rows).astype(jnp.bfloat16)
        c_high, c_low = split(c_ref[p])
        mp_ref[p, :n, :] = lax.dot_general(
            c_high, select, (((1,), (1,)), ((), ())), preferred_element_type=jnp.float32
        ) + lax.dot_general(
            c_low, select, (((1,), (1,)), ((), ())), preferred_element_type=jnp.float32
        )
        mp_ref[p, n:, :] = jnp.zeros((EXTRA, z.paos), jnp.float32)
        mp_ref[p, n : n + 1, :n] = e_ref[p : p + 1, :]


def left_kernel(z, first, c_ref, b_ref, order, left_ref):
    owner, sub = lax.axis_index("orb"), lax.axis_index("sub")
    start = side_start(z, owner, sub, 0)
    for p in range(z.pairs):
        left_ref[p] = mm(c_ref[p], b_ref[first[start + p] - owner * z.orbitals])


def below_kernel(z, second, mp_below, b_ref, right_ref):
    owner, sub = lax.axis_index("orb"), lax.axis_index("sub")
    start = side_start(z, jnp.maximum(owner - 1, 0), sub, 0)
    for p in range(z.pairs):
        j = second[start + p] - owner * z.orbitals
        held = jnp.where(j >= 0, 1.0, 0.0)
        mapped = mp_below[p, : z.pnos, :] * held
        right_ref[p] = mm(mapped, b_ref[jnp.clip(j, 0, z.orbitals - 1)])


def here_kernel(z, second, left_ref, mp_ref, mp_other, b_ref, pack, right_below, right_ref,
                sums_ref):
    owner, sub = lax.axis_index("orb"), lax.axis_index("sub")
    n = z.pnos
    for side, ref in enumerate((mp_ref, mp_other)):
        start = side_start(z, owner, sub, side)
        for p in range(z.pairs):
            j = second[start + p] - owner * z.orbitals
            local = jnp.where(j < z.orbitals, 1.0, 0.0)
            right = mm(ref[p, :n, :] * local, b_ref[jnp.minimum(j, z.orbitals - 1)])
            right_ref[side * z.pairs + p] = right
            if side == 0:
                sums_ref[:, p * n : (p + 1) * n] = mm(left_ref[p], right, ((1,), (1,)))


def sums_kernel(z, first, second, ranks, occupied, mp_ref, mp_below, left_below, right_below,
                sums_ref, both_ref):
    owner, sub = lax.axis_index("orb"), lax.axis_index("sub")
    own_start = side_start(z, owner, sub, 0)
    start = side_start(z, jnp.maximum(owner - 1, 0), sub, 0)
    n = z.pnos
    lists = (first, second, ranks, occupied)
    for p in range(z.pairs):
        lanes = slice(p * n, (p + 1) * n)
        scale = scale_of(z, own_start + p, mp_ref[p, n : n + 1, :n], *lists)
        both_ref[0, :, lanes] = -sums_ref[:, lanes] * scale
        part = mm(left_below[p], right_below[p], ((1,), (1,)))
        scale = scale_of(z, start + p, mp_below[p, n : n + 1, :n], *lists)
        both_ref[1, :, lanes] = -part * scale


def sweep_kernel(z, part_count, first, second, ranks, near, occupied, mp_ref, mp_other, pack,
                 pack_other, *refs):
    parts, others = refs[:part_count], refs[part_count : 2 * part_count]
    own_ref, start_ref, amps, amps_high, amps_low, diag_high, diag_low = refs[2 * part_count :]
    owner, sub = lax.axis_index("orb"), lax.axis_index("sub")
    n = z.pnos

    def collect(step, slot, who):
        for side, ref in ((0, parts[step]), (1, others[step])):
            row = side_start(z, who + 1, sub, side)
            for p in range(z.pairs):
                amps[row + p] = ref[slot, 0, :, p * n : (p + 1) * n]

    def collect_above(step, slot, who):
        for side, ref in ((0, parts[step]), (1, others[step])):
            row = side_start(z, who, sub, side)
            for p in range(z.pairs):
                amps[row + p] = amps[row + p] + ref[slot, 1, :, p * n : (p + 1) * n]

    amps[: z.own] = jnp.zeros((z.own, n, n), jnp.float32)
    each_owner(z, parts, owner, collect)
    each_owner(z, parts, owner, collect_above)
    split_all(z, amps, amps_high, amps_low)
    pair_list, scales = [], []
    for side, ref in enumerate((mp_ref, mp_other)):
        for p in range(z.pairs):
            pair = side_start(z, owner, sub, side) + p
            pair_list.append(pair)
            scales.append(
                scale_of(z, pair, ref[p, n : n + 1, :n], first, second, ranks, occupied)
            )
    packs = [ref.at[p] for ref in (pack, pack_other) for p in range(z.pairs)]
    coupled = coupled_of(z, pair_list, near, packs, amps_high, amps_low, diag_high, diag_low)
    for index, pair in enumerate(pair_list):
        side, p = divmod(index, z.pairs)
        begin = amps[pair + z.own]
        start_ref[index] = begin
        start_ref[z.own + index] = amps[
            side_start(z, jnp.maximum(owner - 1, 0), sub, side) + p + z.own
        ]
        own_ref[sub if side == 0 else 1 - sub, :, p * n : (p + 1) * n] = (
            begin + coupled[index] * scales[index]
        )


def final_kernel(z, part_count, first, second, ranks, near, occupied, *refs):
    (c_in, c_other, mp_in, mp_other, mp_below, mp_below_other, left_in, left_other, left_below,
     left_below_other, here_in, down_in, down_other, pack_in, pack_other, pack_below,
     pack_below_other, start_ref) = refs[:18]
    parts = refs[18 : 18 + part_count]
    (amp_ref, grad_out, packs, c_ref, m_ref, e_ref, rhs, down, grad, flat, amps, amps_high,
     amps_low, diag_high, diag_low, rows_high, rows_low, sems) = refs[18 + part_count :]
    owner, sub = lax.axis_index("orb"), lax.axis_index("sub")
    n, pairs, own = z.pnos, z.pairs, z.own
    half = z.paos // z.subs
    at = pl.ds(pl.multiple_of(sub * half, half), half)
    mapped_in = [mp_in, mp_other, mp_below, mp_below_other]

    def quarters(ref):
        return [ref.at[pl.ds(i * pairs, pairs)] for i in range(4)]

    pack_copies = started(
        [pack_in, pack_other, pack_below, pack_below_other]
        + [ref.at[:, pl.ds(n, EXTRA), :] for ref in mapped_in],
        quarters(packs) + quarters(e_ref),
        sems,
    )
    small_copies = started(
        [c_in.at[:, :, at], c_other.at[:, :, at]]
        + [ref.at[:, pl.ds(0, n), at] for ref in mapped_in],
        [c_ref.at[pl.ds(0, pairs)], c_ref.at[pl.ds(pairs, pairs)]] + quarters(m_ref),
        sems, 8,
    )
    large_copies = started(
        [here_in, left_in, left_other, left_below, left_below_other, down_in, down_other],
        [rhs.at[pl.ds(0, own)]] + [rhs.at[pl.ds(own + i * pairs, pairs)] for i in range(4)]
        + [down.at[pl.ds(0, pairs)], down.at[pl.ds(pairs, pairs)]],
        sems, 14,
    )

    def collect(step, slot, who):
        for which in range(own):
            amps[(who + 1) * own + which] = parts[step][
                slot, which // pairs, :, (which % pairs) * n : (which % pairs + 1) * n
            ]

    each_owner(z, parts, owner, collect)
    split_all(z, amps, amps_high, amps_low)
    pair_list = [
        side_start(z, who, sub, side) + p
        for who in (owner, jnp.maximum(owner - 1, 0))
        for side in range(z.subs)
        for p in range(pairs)
    ]
    wait(pack_copies)
    scales = [
        scale_of(z, pair, e_ref[index, 0:1, :n], first, second, ranks, occupied)
        for index, pair in enumerate(pair_list)
    ]
    coupled = coupled_of(
        z, pair_list, near, [packs.at[i] for i in range(2 * own)], amps_high, amps_low,
        diag_high, diag_low,
    )
    found = [
        start_ref[index] + value * scale
        for index, (value, scale) in enumerate(zip(coupled, scales))
    ]
    turned = [value.T for value in found]
    wait(small_copies)
    weights = [split(2.0 * a - b) for a, b in zip(found, turned)]
    weights_turned = [split(2.0 * b - a) for a, b in zip(found[:own], turned[:own])]
    terms = (
        [mm3(w, split(c_ref[i])) for i, w in enumerate(weights_turned)]
        + [mm3(w, split(m_ref[i])) for i, w in enumerate(weights)]
    )
    orbital_list = (
        [first[pair] - owner * z.orbitals for pair in pair_list[:own]]
        + [second[pair] - owner * z.orbitals for pair in pair_list]
    )
    for index in range(0, 3 * own, 2):
        for o in range(z.orbitals):
            block = jnp.concatenate(
                [
                    jnp.where(orbital_list[i] == o, terms[i], 0.0) for i in (index, index + 1)
                ]
            ).T
            place = (slice(o * half, (o + 1) * half), slice(index * n, (index + 2) * n))
            rows_high[place], rows_low[place] = split(block)

    for p in range(pairs):
        flat[p] = found[p]
        even = flat[p, pl.ds(0, n // 2, 2), :]
        odd = flat[p, pl.ds(1, n // 2, 2), :]
        lines = jnp.concatenate([even, odd], axis=1)
        for r in range(n // 2):
            amp_ref[p : p + 1, r * 2 * n : (r + 1) * 2 * n] = lines[r : r + 1, :]

    wait(large_copies)
    step = 256
    rows = (rows_high[...], rows_low[...])
    copies = []
    for index, start in enumerate(range(0, z.fits, step)):
        columns = slice(start, start + step)
        right = (rhs[:own, :, columns] + down[:, :, columns]).reshape(own * n, -1)
        factor = jnp.concatenate([right, rhs[own:, :, columns].reshape(2 * own * n, -1)])
        grad[:, :, columns] = mm3(rows, split(factor)).reshape(z.orbitals, half, step)
        window = pl.ds(start, step)
        copies += started(
            [grad.at[:, :, window]], [grad_out.at[:, :, window]], sems, 21 + index
        )
    wait(copies)


def gate(values, *after):
    return lax.optimization_barrier((tuple(values), after))[0]


def body(
    blocks,
    pno_coefficients,
    domain_map,
    pair_first,
    pair_second,
    pno_ranks,
    neighbours,
    couplings,
    intersections,
    pno_energy,
    occ_energy,
):
    z = Sizes(blocks, pno_coefficients, couplings)
    n, pairs, own, fits = z.pnos, z.pairs, z.own, z.fits
    half = z.paos // z.subs

    def scratch(*shape, kind=jnp.float32):
        return pltpu.VMEM(shape, kind)

    hbm = held_out
    (mp,) = call(
        functools.partial(mapped_kernel, z),
        [(pairs, n + EXTRA, z.paos)],
        [hbm] * 3,
        (pno_coefficients, domain_map, pno_energy),
        [
            scratch(*pno_coefficients.shape),
            pltpu.VMEM(domain_map.shape, jnp.int32),
            scratch(*pno_energy.shape),
            pltpu.SemaphoreType.DMA((3,)),
        ],
        limit=8,
    )
    mp_below = shifted(mp, "orb", 1)
    (left,) = call(
        functools.partial(left_kernel, z),
        [(pairs, n, fits)],
        [smem, vmem, vmem, anywhere],
        (pair_first, pno_coefficients, blocks, mp),
        limit=8,
    )
    left_below = shifted(left, "orb", 1)
    (right_below,) = call(
        functools.partial(below_kernel, z),
        [(pairs, n, fits)],
        [smem, vmem, vmem],
        (pair_second, mp_below, blocks),
        limit=8,
    )
    down = shifted(right_below, "orb", -1)

    intersection, coupling = gate((intersections, couplings), left)
    pack = jnp.concatenate(
        [
            intersection.reshape(pairs, z.links, n, n)
            .transpose(0, 2, 1, 3)
            .reshape(pairs, n, z.links * n),
            jnp.repeat(coupling, n, axis=1)[:, None, :],
            jnp.zeros((pairs, EXTRA - 1, z.links * n), jnp.float32),
        ],
        axis=1,
    )
    (coefficients,) = gate((pno_coefficients,), left)
    mp_other = swapped(mp, "sub")
    left_other = swapped(left, "sub")
    c_other = swapped(coefficients, "sub")
    pack_other = swapped(pack, "sub")
    pack_below = shifted(pack, "orb", 1)

    right_here, sums = call(
        functools.partial(here_kernel, z),
        [(own, n, fits), (n, pairs * n)],
        [smem, vmem, vmem, vmem, vmem, anywhere, anywhere],
        (pair_second, left, mp, mp_other, blocks, pack, right_below),
        limit=8,
    )
    lists = (pair_first, pair_second, pno_ranks)
    (both,) = call(
        functools.partial(sums_kernel, z),
        [(2, n, pairs * n)],
        [smem] * 4 + [vmem] * 5,
        (*lists, occ_energy, mp, mp_below, left_below, right_below, sums),
        limit=8,
    )
    if lax.axis_size("fit") == 2:
        both = both + swapped(both, "fit")
    else:
        both = lax.psum(both, "fit")
    parts = owners_of(both)
    others = [swapped(part, "sub") for part in parts]

    late = gate((mp_below, left_below, down, pack_below), both)
    mp_below_other, left_below_other, down_other, pack_below_other = [
        swapped(value, "sub") for value in late
    ]

    lists = (*lists, neighbours, occ_energy)
    args = (*lists, mp, mp_other, pack, pack_other, *parts, *others)
    rows = (z.total + own, n, n)
    bf16 = jnp.bfloat16
    wide = z.links * n
    own_amps, start_amps = call(
        functools.partial(sweep_kernel, z, len(parts)),
        [(z.subs, n, pairs * n), (2 * own, n, n)],
        [smem] * 5 + [vmem] * (len(args) - 5),
        args,
        [scratch(*rows), scratch(*rows, kind=bf16), scratch(*rows, kind=bf16)]
        + [scratch(own, wide, wide, kind=bf16)] * 2,
        limit=6 + z.owners // 2,
    )
    amps = owners_of(own_amps)

    args = (
        *lists, pno_coefficients, c_other, mp, mp_other, mp_below, mp_below_other,
        left, left_other, left_below, left_below_other, right_here, down, down_other,
        pack, pack_other, pack_below, pack_below_other, start_amps, *amps,
    )
    amplitudes, gradient = call(
        functools.partial(final_kernel, z, len(amps)),
        [(pairs, n * n), (z.orbitals, half, fits)],
        [smem] * 5 + [anywhere] * 17 + [vmem] * (len(args) - 22),
        args,
        [
            scratch(2 * own, n + EXTRA, wide),
            scratch(own, n, half),
            scratch(2 * own, n, half),
            scratch(2 * own, EXTRA, z.paos),
            scratch(3 * own, n, fits),
            scratch(own, n, fits),
            scratch(z.orbitals, half, fits),
            scratch(pairs, n, n),
            scratch(*rows),
            scratch(*rows, kind=bf16),
            scratch(*rows, kind=bf16),
        ]
        + [scratch(2 * own, wide, wide, kind=bf16)] * 2
        + [scratch(z.orbitals * half, 3 * own * n, kind=bf16)] * 2
        + [pltpu.SemaphoreType.DMA((21 + -(-fits // 256),))],
        limit=20 + z.owners // 2,
        out_specs=[vmem, hbm],
    )
    return (amplitudes, gradient)


def solution(mesh):
    in_specs = (
        P(("groups", "orb"), None, "fit"),
        P(("groups", "orb", "sub"), None, None),
        P(("groups", "orb", "sub"), None),
        P("groups"),
        P("groups"),
        P("groups"),
        P("groups", None),
        P(("groups", "orb", "sub"), None),
        P(("groups", "orb", "sub"), None, None),
        P(("groups", "orb", "sub"), None),
        P("groups"),
    )
    out_specs = (P(("groups", "orb", "sub"), None), P(("groups", "orb"), "sub", "fit"))
    return jax.shard_map(body, mesh=mesh, in_specs=in_specs, out_specs=out_specs, check_vma=False)
```

time: 82.2 us -> 82.5 us (level)
  starting transfers between devices: 26.8 us -> 22.3 us
  waiting for transfers between devices: 25 us -> 28.2 us
  local copies, waits for them, and re-layouts: 9.92 us -> 12.2 us
  other arithmetic: 1.83 us -> 0.99 us
    ppermute x6, waiting for transfers between devices: 11.8 us -> 22.8 us  [owners_of(): lax.ppermute(value, 'orb', [(s, s ^ step) for s in range(count)])[None]]
    ppermute x4, waiting for transfers between devices: 9.1 us -> 0.01 us  [shifted(): lax.ppermute(value, axis, [(source, source + steps) for source in range(i...]
    ppermute x6, starting transfers between devices: 8.03 us -> 2.49 us  [owners_of(): lax.ppermute(value, 'orb', [(s, s ^ step) for s in range(count)])[None]]
    unnamed x35 -> x41, local copies, waits for them, and re-layouts: 6.1 us -> 7.43 us
    ppermute x11 -> x13, waiting for transfers between devices: 4.13 us -> 5.42 us  [swapped(): return lax.ppermute(value, axis, [(0, 1), (1, 0)])]
    reshape x1, local copies, waits for them, and re-layouts: 0.86 us -> 1.85 us  [body(): pack = jnp.concatenate([intersection.reshape(pairs, z.links, n, n).transp...]
    ppermute x4, starting transfers between devices: 15 us -> 15.8 us  [shifted(): lax.ppermute(value, axis, [(source, source + steps) for source in range(i...]
    add x1, other arithmetic: 0.85 us -> 0.01 us  [body(): both = both + swapped(both, 'fit')]
  transfers between devices with their start and end apart: 21 -> 23, of which waited for: 9 -> 10; matrix products, arithmetic and copies ran while one was open for 6% -> 7% of each run, Pallas kernels for 6% -> 11%
where the time goes in v3:
time: 82.5 us; the launch traced here: 82 us
  waiting for transfers between devices  28.2 us (34%)
  starting transfers between devices  22.3 us (27%)
  Pallas kernels  17.4 us (21%)
  local copies, waits for them, and re-layouts  12.2 us (15%)
  other arithmetic  0.99 us (1%)
  between operations  0.91 us (1%)
    ppermute x6, waiting for transfers between devices, owners_of(): lax.ppermute(value, 'orb', [(s, s ^ step) for s in range(count)])[None]  22.8 us
    pallas_call x7, Pallas kernels, call(): pl.pallas_call(kernel, out_shape=[jax.ShapeDtypeStruct(shape, jnp.float32...  17.4 us
    ppermute x4, starting transfers between devices, shifted(): lax.ppermute(value, axis, [(source, source + steps) for source in range(i...  15.8 us
    unnamed x41, local copies, waits for them, and re-layouts  7.43 us
    ppermute x13, waiting for transfers between devices, swapped(): return lax.ppermute(value, axis, [(0, 1), (1, 0)])  5.42 us
    ppermute x13, starting transfers between devices, swapped(): return lax.ppermute(value, axis, [(0, 1), (1, 0)])  3.94 us
    reshape x2, local copies, waits for them, and re-layouts, body(): intersection.reshape(pairs, z.links, n, n).transpose(0, 2, 1, 3)  2.72 us
    ppermute x6, starting transfers between devices, owners_of(): lax.ppermute(value, 'orb', [(s, s ^ step) for s in range(count)])[None]  2.49 us
  transfers between devices with their start and end apart: 23, of which 10 were waited for; matrix products, arithmetic and copies ran while one was open for 7% of the time, Pallas kernels for 11%

profile of v3, /device:TPU:0, one launch (start us, length us, event | category | flops | bytes accessed | tf_op | source)
XLA Modules:
  0.0 82.0 jit_solution(11351537703496386917)
XLA Ops:
  0.7 0.7 copy-done.15
  1.3 0.7 copy-done.16
  2.0 1.3 %shard_map.122.order.mp_ref.refs_2_ = f32[2,72,256]{2,1,0:T(8,128)S(1)} custom-call(f32[2,64,256]{2,1,0:T(8,128)} %refs_0_.1, s32[2,256]{1,0:T(2,128)S(1)} %copy-done.15, f32[2,64]{1,0:T(2,128)S(1)} %copy-done.16), custom_call_target="tpu_custom_call" | custom-call | tf_op jit(solution)/shard_map/pallas_call | solution.py:66
  3.3 4.9 %collective-permute-start.2 = (f32[2,72,256]{2,1,0:T(8,128)S(1)}, f32[2,72,256]{2,1,0:T(8,128)S(1)}, u32[]{:S(2)}, u32[]{:S(2)}) collective-permute-start(f32[2,72,256]{2,1,0:T(8,128)S(1)} %shard_map.122.order.mp_ref.refs_2_), channel_id=1, source_target_pairs={{0,4},{4,8},{8,12},{1,5},{5,9},{9,13},{2,6},{6,10},{10,14},{3,7},{... | collective-permute-start | bytes 442376 | tf_op jit(solution)/shard_map/ppermute | solution.py:29
  8.2 1.6 %copy-done = f32[2,256,1024]{2,1,0:T(8,128)S(1)} copy-done((f32[2,256,1024]{2,1,0:T(8,128)S(1)}, f32[2,256,1024]{2,1,0:T(8,128)}, u32[]{:S(2)}) %copy-start) | copy-done | bytes 2097176
  9.8 0.7 copy-done.11
  10.5 1.8 %shard_map.123.left_ref.refs_6_ = f32[2,64,1024]{2,1,0:T(8,128)S(1)} custom-call(s32[16]{0:T(128)S(1)} %copy-done.11, f32[2,64,256]{2,1,0:T(8,128)} %refs_0_.1, f32[2,256,1024]{2,1,0:T(8,128)S(1)} %copy-done, f32[2,72,256]{2,1,0:T(8,128)S(1)} %shard_map.122.order.mp_ref.refs_2_), custom_call_target="tpu_custom_call" | custom-call | tf_op jit(solution)/shard_map/pallas_call | solution.py:66
  12.3 4.4 %collective-permute-start.3 = (f32[2,64,1024]{2,1,0:T(8,128)S(1)}, f32[2,64,1024]{2,1,0:T(8,128)}, u32[]{:S(2)}, u32[]{:S(2)}) collective-permute-start(f32[2,64,1024]{2,1,0:T(8,128)S(1)} %shard_map.123.left_ref.refs_6_), channel_id=1, source_target_pairs={{0,4},{4,8},{8,12},{1,5},{5,9},{9,13},{2,6},{6,10},{10,14},{3,7},{... | collective-permute-start | bytes 1572872 | tf_op jit(solution)/shard_map/ppermute | solution.py:29
  16.8 1.3 %shard_map.124.right_below = f32[2,64,1024]{2,1,0:T(8,128)S(1)} custom-call(s32[16]{0:T(128)S(1)} %copy-done.10, f32[2,72,256]{2,1,0:T(8,128)S(1)} %collective-permute-done.2.mp_below.refs_4_, f32[2,256,1024]{2,1,0:T(8,128)S(1)} %copy-done.1), custom_call_target="tpu_custom_call" | custom-call | tf_op jit(solution)/shard_map/pallas_call | solution.py:66
  18.1 1.3 %collective-permute-start.4 = (f32[2,64,1024]{2,1,0:T(8,128)S(1)}, f32[2,64,1024]{2,1,0:T(8,128)}, u32[]{:S(2)}, u32[]{:S(2)}) collective-permute-start(f32[2,64,1024]{2,1,0:T(8,128)S(1)} %shard_map.124.right_below), channel_id=1, source_target_pairs={{4,0},{8,4},{12,8},{5,1},{9,5},{13,9},{6,2},{10,6},{14,10},{7,3},{... | collective-permute-start | bytes 1572872 | tf_op jit(solution)/shard_map/ppermute | solution.py:29
  19.4 0.1 collective-permute-start.1
  19.6 0.1 broadcast_in_dim_reshape.3
  19.6 0.9 %reshape.10 = f32[2,4,64,64]{3,2,1,0:T(8,128)} reshape(f32[2,4,4096]{2,1,0:T(4,128)S(1)} %copy-done.17) | data formatting | bytes 262144 | tf_op jit(solution)/shard_map/reshape | solution.py:434
  20.5 1.8 %copy.17 = f32[2,4,64,64]{3,1,2,0:T(4,128)} copy(f32[2,4,64,64]{3,2,1,0:T(8,128)} %reshape.10) | data formatting | bytes 262144 | tf_op jit(solution)/shard_map/reshape | solution.py:434
  22.4 1.8 %reshape.11 = f32[2,64,256]{2,1,0:T(8,128)} reshape(f32[2,64,4,64]{3,2,1,0:T(4,128)} %bitcast.23) | data formatting | bytes 262144 | tf_op jit(solution)/shard_map/reshape | solution.py:436
  24.2 0.1 pad.2.clone
  24.3 1.0 %maximum_maximum_fusion.pack.refs_13_ = f32[2,72,256]{2,1,0:T(8,128)S(1)} fusion(f32[2,1,256]{2,1,0:T(1,128)S(1)} %broadcast_in_dim_reshape.3, f32[2,64,256]{2,1,0:T(8,128)} %reshape.11, f32[72]{0:T(128)S(1)} %pad.2.clone), kind=kLoop, calls=%fused_computation.1 | loop fusion | flops 73728 | bytes 280864 | tf_op jit(solution)/shard_map/concatenate | solution.py:432
  25.3 5.2 %collective-permute-start.5 = (f32[2,72,256]{2,1,0:T(8,128)S(1)}, f32[2,72,256]{2,1,0:T(8,128)}, u32[]{:S(2)}, u32[]{:S(2)}) collective-permute-start(f32[2,72,256]{2,1,0:T(8,128)S(1)} %maximum_maximum_fusion.pack.refs_13_), channel_id=1, source_target_pairs={{0,4},{4,8},{8,12},{1,5},{5,9},{9,13},{2,6},{6,10},{10,14},{3,7},{... | collective-permute-start | bytes 442376 | tf_op jit(solution)/shard_map/ppermute | solution.py:29
  30.5 0.2 collective-permute-start.8
  30.7 0.3 collective-permute-start.11
  31.0 2.4 %shard_map.125 = (f32[4,64,1024]{2,1,0:T(8,128)S(1)}, f32[64,128]{1,0:T(8,128)S(1)}) custom-call(s32[16]{0:T(128)S(1)} %copy-done.10, f32[2,64,1024]{2,1,0:T(8,128)S(1)} %shard_map.123.left_ref.refs_6_, f32[2,72,256]{2,1,0:T(8,128)S(1)} %shard_map.122.order.mp_ref.refs_2_, f32[2,72,256]{2,1,0:T(8,128)} %collective-permute-done.1.mp_other.refs_3_, ...), custom_call_target="tpu_custom_call" | custom-call | tf_op jit(solution)/shard_map/pallas_call | solution.py:66
  33.5 1.9 %shard_map.126 = f32[2,64,128]{2,1,0:T(8,128)S(1)} custom-call(s32[16]{0:T(128)S(1)} %copy-done.12, s32[16]{0:T(128)S(1)} %copy-done.10, s32[16]{0:T(128)S(1)} %copy-done.13, f32[8]{0:T(128)S(1)} %copy-done.14, f32[2,72,256]{2,1,0:T(8,128)S(1)} %shard_map.122.order.mp_ref.refs_2_, f32[2,72,256]{2,1,0:T(8,128)S(1)} %copy-done.3, ...), custom_call_target="tpu_custom_call" | custom-call | tf_op jit(solution)/shard_map/pallas_call | solution.py:66
  35.3 1.6 %collective-permute-start.6 = (f32[2,64,128]{2,1,0:T(8,128)S(1)}, f32[2,64,128]{2,1,0:T(8,128)S(1)}, u32[]{:S(2)}, u32[]{:S(2)}) collective-permute-start(f32[2,64,128]{2,1,0:T(8,128)S(1)} %shard_map.126), channel_id=1, source_target_pairs={{0,2},{2,0},{1,3},{3,1},{4,6},{6,4},{5,7},{7,5},{8,10},{10,8},{9,1... | collective-permute-start | bytes 196616 | tf_op jit(solution)/shard_map/ppermute | solution.py:33
  36.9 2.8 %collective-permute-done.6 = f32[2,64,128]{2,1,0:T(8,128)S(1)} collective-permute-done((f32[2,64,128]{2,1,0:T(8,128)S(1)}, f32[2,64,128]{2,1,0:T(8,128)S(1)}, u32[]{:S(2)}, u32[]{:S(2)}) %collective-permute-start.6) | collective-permute-done | bytes 65568 | tf_op jit(solution)/shard_map/ppermute | solution.py:33
  39.8 0.5 collective-permute-start.10
  40.3 0.1 collective-permute-start.16
  40.4 0.7 copy-done.7
  41.0 0.8 %collective-permute-done.16.refs_4_ = f32[1,2,64,128]{3,2,1,0:T(8,128)S(1)} collective-permute-done((f32[1,2,64,128]{3,2,1,0:T(8,128)S(1)}, f32[1,2,64,128]{3,2,1,0:T(8,128)S(1)}, u32[]{:S(2)}, u32[]{:S(2)}) %collective-permute-start.16) | collective-permute-done | bytes 65568 | tf_op jit(solution)/shard_map/ppermute | solution.py:33
  41.9 0.9 %collective-permute-start.14 = (f32[2,64,128]{2,1,0:T(8,128)S(1)}, f32[2,64,128]{2,1,0:T(8,128)S(1)}, u32[]{:S(2)}, u32[]{:S(2)}) collective-permute-start(f32[2,64,128]{2,1,0:T(8,128)S(1)} %add.3), channel_id=1, source_target_pairs={{0,8},{4,12},{8,0},{12,4},{1,9},{5,13},{9,1},{13,5},{2,10},{6,14},... | collective-permute-start | bytes 196616 | tf_op jit(solution)/shard_map/ppermute | solution.py:41
  42.7 5.1 %collective-permute-done.15 = f32[2,64,128]{2,1,0:T(8,128)S(1)} collective-permute-done((f32[2,64,128]{2,1,0:T(8,128)S(1)}, f32[2,64,128]{2,1,0:T(8,128)S(1)}, u32[]{:S(2)}, u32[]{:S(2)}) %collective-permute-start.15) | collective-permute-done | bytes 65568 | tf_op jit(solution)/shard_map/ppermute | solution.py:41
  47.8 1.9 %collective-permute-done.14 = f32[2,64,128]{2,1,0:T(8,128)S(1)} collective-permute-done((f32[2,64,128]{2,1,0:T(8,128)S(1)}, f32[2,64,128]{2,1,0:T(8,128)S(1)}, u32[]{:S(2)}, u32[]{:S(2)}) %collective-permute-start.14) | collective-permute-done | bytes 65568 | tf_op jit(solution)/shard_map/ppermute | solution.py:41
  49.7 2.4 %collective-permute-done.13 = f32[2,64,128]{2,1,0:T(8,128)S(1)} collective-permute-done((f32[2,64,128]{2,1,0:T(8,128)S(1)}, f32[2,64,128]{2,1,0:T(8,128)S(1)}, u32[]{:S(2)}, u32[]{:S(2)}) %collective-permute-start.13) | collective-permute-done | bytes 65568 | tf_op jit(solution)/shard_map/ppermute | solution.py:41
  52.1 0.5 collective-permute-start
  52.6 0.8 collective-permute-done.18.refs_6_
  53.4 0.1 collective-permute-start.17
  53.5 0.1 copy.15.near
  53.6 1.0 %collective-permute-done.17.refs_5_ = f32[1,2,64,128]{3,2,1,0:T(8,128)S(1)} collective-permute-done((f32[1,2,64,128]{3,2,1,0:T(8,128)S(1)}, f32[1,2,64,128]{3,2,1,0:T(8,128)S(1)}, u32[]{:S(2)}, u32[]{:S(2)}) %collective-permute-start.17) | collective-permute-done | bytes 65568 | tf_op jit(solution)/shard_map/ppermute | solution.py:33
  54.6 0.9 %copy-done.8 = f32[2,72,256]{2,1,0:T(8,128)S(1)} copy-done((f32[2,72,256]{2,1,0:T(8,128)S(1)}, f32[2,72,256]{2,1,0:T(8,128)}, u32[]{:S(2)}) %copy-start.8) | copy-done | bytes 147480
  55.5 2.0 %shard_map.127 = (f32[2,64,128]{2,1,0:T(8,128)S(1)}, f32[8,64,64]{2,1,0:T(8,128)S(1)}) custom-call(s32[16]{0:T(128)S(1)} %copy-done.12, s32[16]{0:T(128)S(1)} %copy-done.10, s32[16]{0:T(128)S(1)} %copy-done.13, s32[16,4]{1,0:T(8,128)S(1)} %copy.15.near, f32[8]{0:T(128)S(1)} %copy-done.14, f32[2,72,256]{2,1,0:T(8,128)S(1)} %shard_map.122.order.mp_ref.refs_2_, ...), custom_call_target="tpu_custom_call" | custom-call | tf_op jit(solution)/shard_map/pallas_call | solution.py:66
  57.5 0.8 %collective-permute-start.22 = (f32[2,64,128]{2,1,0:T(8,128)S(1)}, f32[2,64,128]{2,1,0:T(8,128)S(1)}, u32[]{:S(2)}, u32[]{:S(2)}) collective-permute-start(f32[2,64,128]{2,1,0:T(8,128)S(1)} %get-tuple-element.23), channel_id=1, source_target_pairs={{0,12},{4,8},{8,4},{12,0},{1,13},{5,9},{9,5},{13,1},{2,14},{6,10},... | collective-permute-start | bytes 196616 | tf_op jit(solution)/shard_map/ppermute | solution.py:41
  58.4 0.5 collective-permute-start.12
  58.9 4.8 %collective-permute-done.22 = f32[2,64,128]{2,1,0:T(8,128)S(1)} collective-permute-done((f32[2,64,128]{2,1,0:T(8,128)S(1)}, f32[2,64,128]{2,1,0:T(8,128)S(1)}, u32[]{:S(2)}, u32[]{:S(2)}) %collective-permute-start.22) | collective-permute-done | bytes 65568 | tf_op jit(solution)/shard_map/ppermute | solution.py:41
  63.6 0.8 collective-permute-start.21
  64.4 4.4 %collective-permute-done.21 = f32[2,64,128]{2,1,0:T(8,128)S(1)} collective-permute-done((f32[2,64,128]{2,1,0:T(8,128)S(1)}, f32[2,64,128]{2,1,0:T(8,128)S(1)}, u32[]{:S(2)}, u32[]{:S(2)}) %collective-permute-start.21) | collective-permute-done | bytes 65568 | tf_op jit(solution)/shard_map/ppermute | solution.py:41
  68.8 4.3 %collective-permute-done.20 = f32[2,64,128]{2,1,0:T(8,128)S(1)} collective-permute-done((f32[2,64,128]{2,1,0:T(8,128)S(1)}, f32[2,64,128]{2,1,0:T(8,128)S(1)}, u32[]{:S(2)}, u32[]{:S(2)}) %collective-permute-start.20) | collective-permute-done | bytes 65568 | tf_op jit(solution)/shard_map/ppermute | solution.py:41
  73.1 1.2 %copy-done.6 = f32[4,64,1024]{2,1,0:T(8,128)S(1)} copy-done((f32[4,64,1024]{2,1,0:T(8,128)S(1)}, f32[4,64,1024]{2,1,0:T(8,128)}, u32[]{:S(2)}) %copy-start.6) | copy-done | bytes 1048600
  74.3 0.9 %copy-done.9 = f32[2,72,256]{2,1,0:T(8,128)S(1)} copy-done((f32[2,72,256]{2,1,0:T(8,128)S(1)}, f32[2,72,256]{2,1,0:T(8,128)}, u32[]{:S(2)}) %copy-start.9) | copy-done | bytes 147480
  75.2 6.7 %shard_map.128 = (f32[2,4096]{1,0:T(2,128)}, f32[2,128,1024]{2,1,0:T(8,128)}) custom-call(s32[16]{0:T(128)S(1)} %copy-done.12, s32[16]{0:T(128)S(1)} %copy-done.10, s32[16]{0:T(128)S(1)} %copy-done.13, s32[16,4]{1,0:T(8,128)S(1)} %copy.15.near, f32[8]{0:T(128)S(1)} %copy-done.14, f32[2,64,256]{2,1,0:T(8,128)} %refs_0_.1, ...), custom_call_target="tpu_custom_call" | custom-call | tf_op jit(solution)/shard_map/pallas_call | solution.py:66
  (55 shorter events, 0.3 us)
Async XLA Ops:
  0.6 16.1 %copy-start.10 = (s32[16]{0:T(128)S(1)}, s32[16]{0:T(128)}, u32[]{:S(2)}) copy-start(s32[16]{0:T(128)} %second.9) | copy-start | bytes 196
  0.6 0.7 copy-start.15
  1.3 0.7 copy-start.16
  3.3 13.5 %collective-permute-start.2 = (f32[2,72,256]{2,1,0:T(8,128)S(1)}, f32[2,72,256]{2,1,0:T(8,128)S(1)}, u32[]{:S(2)}, u32[]{:S(2)}) collective-permute-start(f32[2,72,256]{2,1,0:T(8,128)S(1)} %shard_map.122.order.mp_ref.refs_2_), channel_id=1, source_target_pairs={{0,4},{4,8},{8,12},{1,5},{5,9},{9,13},{2,6},{6,10},{10,14},{3,7},{... | collective-permute-start | bytes 442376 | tf_op jit(solution)/shard_map/ppermute | solution.py:29
  8.2 1.6 %copy-start = (f32[2,256,1024]{2,1,0:T(8,128)S(1)}, f32[2,256,1024]{2,1,0:T(8,128)}, u32[]{:S(2)}) copy-start(f32[2,256,1024]{2,1,0:T(8,128)} %b_ref.5) | copy-start | bytes 6291460
  9.8 0.7 copy-start.11
  10.5 6.3 %copy-start.1 = (f32[2,256,1024]{2,1,0:T(8,128)S(1)}, f32[2,256,1024]{2,1,0:T(8,128)}, u32[]{:S(2)}) copy-start(f32[2,256,1024]{2,1,0:T(8,128)} %b_ref.5) | copy-start | bytes 6291460
  12.3 7.2 %copy-start.19 = (f32[2,4]{1,0:T(2,128)S(1)}, f32[2,4]{1,0:T(2,128)}, u32[]{:S(2)}) copy-start(f32[2,4]{1,0:T(2,128)} %param.18) | copy-start | bytes 100
  12.3 7.3 %copy-start.17 = (f32[2,4,4096]{2,1,0:T(4,128)S(1)}, f32[2,4,4096]{2,1,0:T(4,128)}, u32[]{:S(2)}) copy-start(f32[2,4,4096]{2,1,0:T(4,128)} %param.19) | copy-start | bytes 393220
  12.3 21.1 %collective-permute-start.3 = (f32[2,64,1024]{2,1,0:T(8,128)S(1)}, f32[2,64,1024]{2,1,0:T(8,128)}, u32[]{:S(2)}, u32[]{:S(2)}) collective-permute-start(f32[2,64,1024]{2,1,0:T(8,128)S(1)} %shard_map.123.left_ref.refs_6_), channel_id=1, source_target_pairs={{0,4},{4,8},{8,12},{1,5},{5,9},{9,13},{2,6},{6,10},{10,14},{3,7},{... | collective-permute-start | bytes 1572872 | tf_op jit(solution)/shard_map/ppermute | solution.py:29
  16.8 1.3 %copy-start.2 = (f32[2,72,256]{2,1,0:T(8,128)}, f32[2,72,256]{2,1,0:T(8,128)S(1)}, u32[]{:S(2)}) copy-start(f32[2,72,256]{2,1,0:T(8,128)S(1)} %collective-permute-done.2.mp_below.refs_4_) | copy-start | bytes 442372
  18.1 21.6 %collective-permute-start.4 = (f32[2,64,1024]{2,1,0:T(8,128)S(1)}, f32[2,64,1024]{2,1,0:T(8,128)}, u32[]{:S(2)}, u32[]{:S(2)}) collective-permute-start(f32[2,64,1024]{2,1,0:T(8,128)S(1)} %shard_map.124.right_below), channel_id=1, source_target_pairs={{4,0},{8,4},{12,8},{5,1},{9,5},{13,9},{6,2},{10,6},{14,10},{7,3},{... | collective-permute-start | bytes 1572872 | tf_op jit(solution)/shard_map/ppermute | solution.py:29
  19.4 11.3 %collective-permute-start.1 = (f32[2,72,256]{2,1,0:T(8,128)S(1)}, f32[2,72,256]{2,1,0:T(8,128)}, u32[]{:S(2)}, u32[]{:S(2)}) collective-permute-start(f32[2,72,256]{2,1,0:T(8,128)S(1)} %shard_map.122.order.mp_ref.refs_2_), channel_id=1, source_target_pairs={{0,1},{1,0},{2,3},{3,2},{4,5},{5,4},{6,7},{7,6},{8,9},{9,8},{10,11... | collective-permute-start | bytes 442376 | tf_op jit(solution)/shard_map/ppermute | solution.py:33
  22.4 11.1 %copy-start.12 = (s32[16]{0:T(128)S(1)}, s32[16]{0:T(128)}, u32[]{:S(2)}) copy-start(s32[16]{0:T(128)} %first.7) | copy-start | bytes 196
  22.4 11.1 %copy-start.13 = (s32[16]{0:T(128)S(1)}, s32[16]{0:T(128)}, u32[]{:S(2)}) copy-start(s32[16]{0:T(128)} %ranks.5) | copy-start | bytes 196
  22.4 11.1 %copy-start.14 = (f32[8]{0:T(128)S(1)}, f32[8]{0:T(128)}, u32[]{:S(2)}) copy-start(f32[8]{0:T(128)} %occupied.5) | copy-start | bytes 100
  24.2 9.3 %copy-start.3 = (f32[2,72,256]{2,1,0:T(8,128)S(1)}, f32[2,72,256]{2,1,0:T(8,128)}, u32[]{:S(2)}) copy-start(f32[2,72,256]{2,1,0:T(8,128)} %copy-done.2) | copy-start | bytes 442372
  25.3 28.2 %copy-start.18 = (s32[16,4]{0,1:T(4,128)S(1)}, s32[16,4]{0,1:T(4,128)}, u32[]{:S(2)}) copy-start(s32[16,4]{0,1:T(4,128)} %param.17) | copy-start | bytes 772
  25.3 14.4 %collective-permute-start.5 = (f32[2,72,256]{2,1,0:T(8,128)S(1)}, f32[2,72,256]{2,1,0:T(8,128)}, u32[]{:S(2)}, u32[]{:S(2)}) collective-permute-start(f32[2,72,256]{2,1,0:T(8,128)S(1)} %maximum_maximum_fusion.pack.refs_13_), channel_id=1, source_target_pairs={{0,4},{4,8},{8,12},{1,5},{5,9},{9,13},{2,6},{6,10},{10,14},{3,7},{... | collective-permute-start | bytes 442376 | tf_op jit(solution)/shard_map/ppermute | solution.py:29
  30.5 27.8 %collective-permute-start.8 = (f32[2,64,1024]{2,1,0:T(8,128)S(1)}, f32[2,64,1024]{2,1,0:T(8,128)}, u32[]{:S(2)}, u32[]{:S(2)}) collective-permute-start(f32[2,64,1024]{2,1,0:T(8,128)S(1)} %shard_map.123.left_ref.refs_6_), channel_id=1, source_target_pairs={{0,1},{1,0},{2,3},{3,2},{4,5},{5,4},{6,7},{7,6},{8,9},{9,8},{10,11... | collective-permute-start | bytes 1572872 | tf_op jit(solution)/shard_map/ppermute | solution.py:33
  30.7 9.7 %collective-permute-start.11 = (f32[2,72,256]{2,1,0:T(8,128)S(1)}, f32[2,72,256]{2,1,0:T(8,128)S(1)}, u32[]{:S(2)}, u32[]{:S(2)}) collective-permute-start(f32[2,72,256]{2,1,0:T(8,128)S(1)} %maximum_maximum_fusion.pack.refs_13_), channel_id=1, source_target_pairs={{0,1},{1,0},{2,3},{3,2},{4,5},{5,4},{6,7},{7,6},{8,9},{9,8},{10,11... | collective-permute-start | bytes 442376 | tf_op jit(solution)/shard_map/ppermute | solution.py:33
  33.4 7.0 %copy-start.5 = (f32[4,64,1024]{2,1,0:T(8,128)}, f32[4,64,1024]{2,1,0:T(8,128)S(1)}, u32[]{:S(2)}) copy-start(f32[4,64,1024]{2,1,0:T(8,128)S(1)} %get-tuple-element.19.refs_10_) | copy-start | bytes 3145732
  33.4 24.9 %copy-start.4 = (f32[2,72,256]{2,1,0:T(8,128)S(1)}, f32[2,72,256]{2,1,0:T(8,128)}, u32[]{:S(2)}) copy-start(f32[2,72,256]{2,1,0:T(8,128)} %copy-done.2) | copy-start | bytes 442372
  35.3 4.3 %collective-permute-start.6 = (f32[2,64,128]{2,1,0:T(8,128)S(1)}, f32[2,64,128]{2,1,0:T(8,128)S(1)}, u32[]{:S(2)}, u32[]{:S(2)}) collective-permute-start(f32[2,64,128]{2,1,0:T(8,128)S(1)} %shard_map.126), channel_id=1, source_target_pairs={{0,2},{2,0},{1,3},{3,1},{4,6},{6,4},{5,7},{7,5},{8,10},{10,8},{9,1... | collective-permute-start | bytes 196616 | tf_op jit(solution)/shard_map/ppermute | solution.py:33
  39.7 33.4 %collective-permute-start.9 = (f32[2,64,1024]{2,1,0:T(8,128)}, f32[2,64,1024]{2,1,0:T(8,128)S(1)}, u32[]{:S(2)}, u32[]{:S(2)}) collective-permute-start(f32[2,64,1024]{2,1,0:T(8,128)} %collective-permute-done.3.left_below.refs_8_), channel_id=1, source_target_pairs={{0,1},{1,0},{2,3},{3,2},{4,5},{5,4},{6,7},{7,6},{8,9},{9,8},{10,11... | collective-permute-start | bytes 1572872 | tf_op jit(solution)/shard_map/ppermute | solution.py:33
  39.8 33.3 %collective-permute-start.10 = (f32[2,64,1024]{2,1,0:T(8,128)}, f32[2,64,1024]{2,1,0:T(8,128)S(1)}, u32[]{:S(2)}, u32[]{:S(2)}) collective-permute-start(f32[2,64,1024]{2,1,0:T(8,128)} %collective-permute-done.4.refs_11_), channel_id=1, source_target_pairs={{0,1},{1,0},{2,3},{3,2},{4,5},{5,4},{6,7},{7,6},{8,9},{9,8},{10,11... | collective-permute-start | bytes 1572872 | tf_op jit(solution)/shard_map/ppermute | solution.py:33
  40.3 1.6 %collective-permute-start.16 = (f32[1,2,64,128]{3,2,1,0:T(8,128)S(1)}, f32[1,2,64,128]{3,2,1,0:T(8,128)S(1)}, u32[]{:S(2)}, u32[]{:S(2)}) collective-permute-start(f32[1,2,64,128]{3,2,1,0:T(8,128)S(1)} %bitcast.11), channel_id=1, source_target_pairs={{0,1},{1,0},{2,3},{3,2},{4,5},{5,4},{6,7},{7,6},{8,9},{9,8},{10,11... | collective-permute-start | bytes 196616 | tf_op jit(solution)/shard_map/ppermute | solution.py:33
  40.4 0.7 copy-start.7
  41.0 6.8 %collective-permute-start.15 = (f32[2,64,128]{2,1,0:T(8,128)S(1)}, f32[2,64,128]{2,1,0:T(8,128)S(1)}, u32[]{:S(2)}, u32[]{:S(2)}) collective-permute-start(f32[2,64,128]{2,1,0:T(8,128)S(1)} %add.3), channel_id=1, source_target_pairs={{0,12},{4,8},{8,4},{12,0},{1,13},{5,9},{9,5},{13,1},{2,14},{6,10},... | collective-permute-start | bytes 196616 | tf_op jit(solution)/shard_map/ppermute | solution.py:41
  41.9 7.9 %collective-permute-start.14 = (f32[2,64,128]{2,1,0:T(8,128)S(1)}, f32[2,64,128]{2,1,0:T(8,128)S(1)}, u32[]{:S(2)}, u32[]{:S(2)}) collective-permute-start(f32[2,64,128]{2,1,0:T(8,128)S(1)} %add.3), channel_id=1, source_target_pairs={{0,8},{4,12},{8,0},{12,4},{1,9},{5,13},{9,1},{13,5},{2,10},{6,14},... | collective-permute-start | bytes 196616 | tf_op jit(solution)/shard_map/ppermute | solution.py:41
  47.8 4.3 %collective-permute-start.13 = (f32[2,64,128]{2,1,0:T(8,128)S(1)}, f32[2,64,128]{2,1,0:T(8,128)S(1)}, u32[]{:S(2)}, u32[]{:S(2)}) collective-permute-start(f32[2,64,128]{2,1,0:T(8,128)S(1)} %add.3), channel_id=1, source_target_pairs={{0,4},{4,0},{8,12},{12,8},{1,5},{5,1},{9,13},{13,9},{2,6},{6,2},{1... | collective-permute-start | bytes 196616 | tf_op jit(solution)/shard_map/ppermute | solution.py:41
  49.7 2.4 %collective-permute-start.19 = (f32[1,2,64,128]{3,2,1,0:T(8,128)S(1)}, f32[1,2,64,128]{3,2,1,0:T(8,128)S(1)}, u32[]{:S(2)}, u32[]{:S(2)}) collective-permute-start(f32[1,2,64,128]{3,2,1,0:T(8,128)S(1)} %bitcast.17), channel_id=1, source_target_pairs={{0,1},{1,0},{2,3},{3,2},{4,5},{5,4},{6,7},{7,6},{8,9},{9,8},{10,11... | collective-permute-start | bytes 196616 | tf_op jit(solution)/shard_map/ppermute | solution.py:33
  52.1 1.3 %collective-permute-start.18 = (f32[1,2,64,128]{3,2,1,0:T(8,128)S(1)}, f32[1,2,64,128]{3,2,1,0:T(8,128)S(1)}, u32[]{:S(2)}, u32[]{:S(2)}) collective-permute-start(f32[1,2,64,128]{3,2,1,0:T(8,128)S(1)} %bitcast.19), channel_id=1, source_target_pairs={{0,1},{1,0},{2,3},{3,2},{4,5},{5,4},{6,7},{7,6},{8,9},{9,8},{10,11... | collective-permute-start | bytes 196616 | tf_op jit(solution)/shard_map/ppermute | solution.py:33
  52.1 6.2 %collective-permute-start = (f32[2,64,256]{2,1,0:T(8,128)}, f32[2,64,256]{2,1,0:T(8,128)S(1)}, u32[]{:S(2)}, u32[]{:S(2)}) collective-permute-start(f32[2,64,256]{2,1,0:T(8,128)} %refs_0_.1), channel_id=1, source_target_pairs={{0,1},{1,0},{2,3},{3,2},{4,5},{5,4},{6,7},{7,6},{8,9},{9,8},{10,11... | collective-permute-start | bytes 393224 | tf_op jit(solution)/shard_map/ppermute | solution.py:33
  53.4 1.3 %collective-permute-start.17 = (f32[1,2,64,128]{3,2,1,0:T(8,128)S(1)}, f32[1,2,64,128]{3,2,1,0:T(8,128)S(1)}, u32[]{:S(2)}, u32[]{:S(2)}) collective-permute-start(f32[1,2,64,128]{3,2,1,0:T(8,128)S(1)} %bitcast.21), channel_id=1, source_target_pairs={{0,1},{1,0},{2,3},{3,2},{4,5},{5,4},{6,7},{7,6},{8,9},{9,8},{10,11... | collective-permute-start | bytes 196616 | tf_op jit(solution)/shard_map/ppermute | solution.py:33
  54.6 0.9 %copy-start.8 = (f32[2,72,256]{2,1,0:T(8,128)S(1)}, f32[2,72,256]{2,1,0:T(8,128)}, u32[]{:S(2)}) copy-start(f32[2,72,256]{2,1,0:T(8,128)} %copy-done.7) | copy-start | bytes 442372
  57.5 6.1 %collective-permute-start.22 = (f32[2,64,128]{2,1,0:T(8,128)S(1)}, f32[2,64,128]{2,1,0:T(8,128)S(1)}, u32[]{:S(2)}, u32[]{:S(2)}) collective-permute-start(f32[2,64,128]{2,1,0:T(8,128)S(1)} %get-tuple-element.23), channel_id=1, source_target_pairs={{0,12},{4,8},{8,4},{12,0},{1,13},{5,9},{9,5},{13,1},{2,14},{6,10},... | collective-permute-start | bytes 196616 | tf_op jit(solution)/shard_map/ppermute | solution.py:41
  58.3 14.7 %collective-permute-start.7 = (f32[2,72,256]{2,1,0:T(8,128)S(1)}, f32[2,72,256]{2,1,0:T(8,128)S(1)}, u32[]{:S(2)}, u32[]{:S(2)}) collective-permute-start(f32[2,72,256]{2,1,0:T(8,128)S(1)} %copy-done.4), channel_id=1, source_target_pairs={{0,1},{1,0},{2,3},{3,2},{4,5},{5,4},{6,7},{7,6},{8,9},{9,8},{10,11... | collective-permute-start | bytes 442376 | tf_op jit(solution)/shard_map/ppermute | solution.py:33
  58.4 14.7 %collective-permute-start.12 = (f32[2,72,256]{2,1,0:T(8,128)}, f32[2,72,256]{2,1,0:T(8,128)S(1)}, u32[]{:S(2)}, u32[]{:S(2)}) collective-permute-start(f32[2,72,256]{2,1,0:T(8,128)} %collective-permute-done.5.refs_15_), channel_id=1, source_target_pairs={{0,1},{1,0},{2,3},{3,2},{4,5},{5,4},{6,7},{7,6},{8,9},{9,8},{10,11... | collective-permute-start | bytes 442376 | tf_op jit(solution)/shard_map/ppermute | solution.py:33
  63.6 5.2 %collective-permute-start.21 = (f32[2,64,128]{2,1,0:T(8,128)S(1)}, f32[2,64,128]{2,1,0:T(8,128)S(1)}, u32[]{:S(2)}, u32[]{:S(2)}) collective-permute-start(f32[2,64,128]{2,1,0:T(8,128)S(1)} %get-tuple-element.23), channel_id=1, source_target_pairs={{0,8},{4,12},{8,0},{12,4},{1,9},{5,13},{9,1},{13,5},{2,10},{6,14},... | collective-permute-start | bytes 196616 | tf_op jit(solution)/shard_map/ppermute | solution.py:41
  68.8 4.3 %collective-permute-start.20 = (f32[2,64,128]{2,1,0:T(8,128)S(1)}, f32[2,64,128]{2,1,0:T(8,128)S(1)}, u32[]{:S(2)}, u32[]{:S(2)}) collective-permute-start(f32[2,64,128]{2,1,0:T(8,128)S(1)} %get-tuple-element.23), channel_id=1, source_target_pairs={{0,4},{4,0},{8,12},{12,8},{1,5},{5,1},{9,13},{13,9},{2,6},{6,2},{1... | collective-permute-start | bytes 196616 | tf_op jit(solution)/shard_map/ppermute | solution.py:41
  73.1 1.2 %copy-start.6 = (f32[4,64,1024]{2,1,0:T(8,128)S(1)}, f32[4,64,1024]{2,1,0:T(8,128)}, u32[]{:S(2)}) copy-start(f32[4,64,1024]{2,1,0:T(8,128)} %copy-done.5) | copy-start | bytes 3145732
  74.3 0.9 %copy-start.9 = (f32[2,72,256]{2,1,0:T(8,128)S(1)}, f32[2,72,256]{2,1,0:T(8,128)}, u32[]{:S(2)}) copy-start(f32[2,72,256]{2,1,0:T(8,128)} %copy-done.7) | copy-start | bytes 442372

commit v4 on v3

v4 whole, which is shorter than its diff:
```python
import functools

import jax
import jax.numpy as jnp
from jax import lax
from jax.experimental import pallas as pl
from jax.experimental.pallas import tpu as pltpu
from jax.sharding import PartitionSpec as P

ITERS = 2
SMALL = 4
MIB = 1 << 20
EXTRA = 8

high = lax.Precision.HIGH
smem = pl.BlockSpec(memory_space=pltpu.SMEM)
vmem = pl.BlockSpec(memory_space=pltpu.VMEM)


def mm(a, b, contract=((1,), (0,))):
    return lax.dot_general(
        a, b, (contract, ((), ())), precision=high, preferred_element_type=jnp.float32
    )


def shifted(value, axis, steps):
    count = lax.axis_size(axis)
    initial, last = (max(0, -steps), min(count, count - steps))
    return lax.ppermute(value, axis, [(source, source + steps) for source in range(initial, last)])


def swapped(value, axis):
    return lax.ppermute(value, axis, [(0, 1), (1, 0)])


def everyone(value):
    return lax.all_to_all(value, ("orb", "sub"), 0, 0)


def f32(flag):
    return flag.astype(jnp.float32)


class Sizes:
    def __init__(self, blocks, pno_coefficients, couplings):
        self.orbitals, self.paos, self.fits = blocks.shape
        self.pairs, self.pnos = pno_coefficients.shape[:2]
        self.links = couplings.shape[1]
        self.subs = lax.axis_size("sub")
        self.owners = lax.axis_size("orb")
        self.own = self.pairs * self.subs
        self.total = self.own * self.owners


anywhere = pl.BlockSpec(memory_space=pl.ANY)
held_out = pl.BlockSpec(memory_space=pltpu.HBM)


def call(kernel, outs, ins, args, scratch=(), limit=16, out_specs=None):
    return pl.pallas_call(
        kernel,
        out_shape=[jax.ShapeDtypeStruct(shape, jnp.float32) for shape in outs],
        in_specs=ins,
        out_specs=out_specs or [vmem] * len(outs),
        scratch_shapes=list(scratch),
        compiler_params=pltpu.CompilerParams(vmem_limit_bytes=limit * MIB),
    )(*args)


def started(sources, targets, sems, base=0):
    copies = [
        pltpu.make_async_copy(source, target, sems.at[base + index])
        for index, (source, target) in enumerate(zip(sources, targets))
    ]
    for copy in copies:
        copy.start()
    return copies


def wait(copies):
    for copy in copies:
        copy.wait()


def side_start(z, owner, sub, side):
    return owner * z.own + (sub if side == 0 else 1 - sub) * z.pairs


def scale_of(z, pair, level, first, second, ranks, occupied):
    n = z.pnos
    row_ids = lax.broadcasted_iota(jnp.int32, (n, n), 0)
    column_ids = lax.broadcasted_iota(jnp.int32, (n, n), 1)
    level = level * jnp.ones((n, 1), jnp.float32)
    rank = ranks[pair]
    kept = f32((row_ids < rank) & (column_ids < rank))
    return kept / (level + level.T - (occupied[first[pair]] + occupied[second[pair]]))


def split(value):
    high_part = value.astype(jnp.bfloat16)
    return high_part, (value - high_part.astype(jnp.float32)).astype(jnp.bfloat16)


def mm3(a, b, contract=((1,), (0,))):
    def one(x, y):
        return lax.dot_general(x, y, (contract, ((), ())), preferred_element_type=jnp.float32)

    return one(a[0], b[0]) + (one(a[0], b[1]) + one(a[1], b[0]))


def split_all(z, amps, amps_high, amps_low):
    def one(row):
        amps_high[row], amps_low[row] = split(amps(row))

    if z.owners <= SMALL:
        for row in range(z.total):
            one(row)
    else:
        @pl.loop(0, z.total)
        def _(row):
            one(row)


def packed_pair(z, ref, row):
    if isinstance(row, int):
        side = row % z.pairs
        return ref[row // z.pairs, :, side * z.pnos : (side + 1) * z.pnos]
    block = ref[row // z.pairs]
    value = block[:, : z.pnos]
    for side in range(1, z.pairs):
        value = jnp.where(
            lax.rem(row, z.pairs) == side, block[:, side * z.pnos : (side + 1) * z.pnos], value
        )
    return value


def unpack(z, s_ref, index, block):
    n = z.pnos
    for k in range(0, z.links, 2):
        two = block[:, k * n : (k + 2) * n]
        for odd in range(2):
            part = two[:, odd * n : (odd + 1) * n]
            s_ref[index, k // 2, pl.ds(odd, n // 2, 2), :] = jnp.concatenate(
                [part[: n // 2], part[n // 2 :]], axis=1
            )


def unpacked(z, s_ref, index):
    return jnp.concatenate([s_ref[index, k] for k in range(z.links // 2)], axis=1)


def coupled_of(z, pair_list, near, s_ref, couplings, amps_high, amps_low, diag_high, diag_low):
    n = z.pnos
    diag_high[...] = jnp.zeros_like(diag_high)
    diag_low[...] = jnp.zeros_like(diag_low)
    for index, pair in enumerate(pair_list):
        for k in range(z.links):
            row = near[pair, k]
            block = slice(k * n, (k + 1) * n)
            diag_high[index, block, block] = amps_high[row]
            diag_low[index, block, block] = amps_low[row]
    parts = [split(unpacked(z, s_ref, index)) for index in range(len(pair_list))]
    inner = [
        mm3(part, (diag_high[index], diag_low[index])) for index, part in enumerate(parts)
    ]
    inner = [split(value * coupling) for value, coupling in zip(inner, couplings)]
    return [mm3(value, part, ((1,), (1,))) for value, part in zip(inner, parts)]


def mapped_kernel(z, c_in, map_in, e_in, coupling_in, b_in, mp_ref, b_ref, c_ref, map_ref, e_ref,
                  coupling, sems):
    n = z.pnos
    copies = started(
        [c_in, map_in, e_in, coupling_in, b_in], [c_ref, map_ref, e_ref, coupling, b_ref], sems
    )
    wait(copies[:4])
    rows = lax.broadcasted_iota(jnp.int32, (z.paos, z.paos), 0)
    lane_link = lax.broadcasted_iota(jnp.int32, (1, z.links * n), 1) // n
    for p in range(z.pairs):
        select = f32(map_ref[p : p + 1, :] == rows).astype(jnp.bfloat16)
        c_high, c_low = split(c_ref[p])
        mp_ref[p, :n, :] = lax.dot_general(
            c_high, select, (((1,), (1,)), ((), ())), preferred_element_type=jnp.float32
        ) + lax.dot_general(
            c_low, select, (((1,), (1,)), ((), ())), preferred_element_type=jnp.float32
        )
        mp_ref[p, n:, :] = jnp.zeros((EXTRA, z.paos), jnp.float32)
        mp_ref[p, n : n + 1, :n] = e_ref[p : p + 1, :]
        spread = jnp.zeros((1, z.links * n), jnp.float32)
        for k in range(z.links):
            spread = jnp.where(lane_link == k, coupling[p : p + 1, k : k + 1], spread)
        mp_ref[p, n + 1 : n + 2, :] = spread
    wait(copies[4:])


def left_kernel(z, first, c_ref, b_ref, q_ref, left_ref):
    owner, sub = lax.axis_index("orb"), lax.axis_index("sub")
    start = side_start(z, owner, sub, 0)
    for p in range(z.pairs):
        left_ref[p, :, : z.fits] = mm(c_ref[p], b_ref[first[start + p] - owner * z.orbitals])
        for k in range(0, z.links, 2):
            lanes = slice(z.fits + k * z.pnos, z.fits + (k + 2) * z.pnos)
            left_ref[p, :, lanes] = jnp.concatenate([q_ref[p, k], q_ref[p, k + 1]])


def below_kernel(z, second, mp_below, b_ref, right_ref):
    owner, sub = lax.axis_index("orb"), lax.axis_index("sub")
    start = side_start(z, jnp.maximum(owner - 1, 0), sub, 0)
    for p in range(z.pairs):
        j = second[start + p] - owner * z.orbitals
        held = jnp.where(j >= 0, 1.0, 0.0)
        mapped = mp_below[p, : z.pnos, :] * held
        right_ref[p] = mm(mapped, b_ref[jnp.clip(j, 0, z.orbitals - 1)])


def here_kernel(z, second, mp_ref, b_ref, right_below, left_other, c_other, right_ref):
    owner, sub = lax.axis_index("orb"), lax.axis_index("sub")
    start = side_start(z, owner, sub, 0)
    for p in range(z.pairs):
        j = second[start + p] - owner * z.orbitals
        local = jnp.where(j < z.orbitals, 1.0, 0.0)
        right_ref[p] = mm(
            mp_ref[p, : z.pnos, :] * local, b_ref[jnp.minimum(j, z.orbitals - 1)]
        )


def sums_kernel(z, first, second, ranks, occupied, mp_ref, left_ref, here_ref, down_ref, sums_ref,
                right_ref):
    owner, sub = lax.axis_index("orb"), lax.axis_index("sub")
    start = side_start(z, owner, sub, 0)
    n = z.pnos
    for p in range(z.pairs):
        right = here_ref[p] + down_ref[p]
        right_ref[p] = right
        scale = scale_of(
            z, start + p, mp_ref[p, n : n + 1, :n], first, second, ranks, occupied
        )
        part = mm(left_ref[p, :, : z.fits], right, ((1,), (1,)))
        sums_ref[:, p * n : (p + 1) * n] = -part * scale


def sweep_kernel(z, first, second, ranks, near, occupied, mp_ref, q_ref, all_ref, *refs):
    own_ref, amps_high, amps_low, diag_high, diag_low, s_ref = refs[-6:]
    owner, sub = lax.axis_index("orb"), lax.axis_index("sub")
    n = z.pnos
    split_all(z, functools.partial(packed_pair, z, all_ref), amps_high, amps_low)
    start = side_start(z, owner, sub, 0)
    pair_list = [start + p for p in range(z.pairs)]
    for p in range(z.pairs):
        unpack(z, s_ref, p, q_ref[p])
    scales = [
        scale_of(z, pair, mp_ref[p, n : n + 1, :n], first, second, ranks, occupied)
        for p, pair in enumerate(pair_list)
    ]
    couplings = [mp_ref[p, n + 1 : n + 2, :] for p in range(z.pairs)]
    coupled = coupled_of(
        z, pair_list, near, s_ref, couplings, amps_high, amps_low, diag_high, diag_low
    )
    begin = all_ref[owner * z.subs + sub]
    value = begin + jnp.concatenate([a * b for a, b in zip(coupled, scales)], axis=1)
    for copy in range(z.owners * z.subs):
        own_ref[copy] = value


def final_kernel(z, first, second, ranks, near, occupied, *refs):
    (c_in, c_other, mp_in, mp_other, mp_below, mp_below_other, left_in, left_other, left_below,
     left_below_other, right_in, right_other, start_ref, all_ref) = refs[:14]
    (amp_ref, grad_out, packs, c_ref, m_ref, e_ref, rhs, grad, flat, s_ref, amps_high, amps_low,
     diag_high, diag_low, rows_high, rows_low, sems) = refs[14:]
    owner, sub = lax.axis_index("orb"), lax.axis_index("sub")
    n, pairs, own = z.pnos, z.pairs, z.own
    half = z.paos // z.subs
    at = pl.ds(pl.multiple_of(sub * half, half), half)
    fits, links = pl.ds(0, z.fits), pl.ds(z.fits, z.links * n)
    mapped_in = [mp_in, mp_other, mp_below, mp_below_other]
    left_all = [left_in, left_other, left_below, left_below_other]

    def quarters(ref, base=0):
        return [ref.at[pl.ds(base + i * pairs, pairs)] for i in range(4)]

    pack_copies = started(
        [ref.at[:, :, links] for ref in left_all]
        + [ref.at[:, pl.ds(n, EXTRA), :] for ref in mapped_in],
        quarters(packs) + quarters(e_ref),
        sems,
    )
    small_copies = started(
        [c_in.at[:, :, at], c_other.at[:, :, at]]
        + [ref.at[:, pl.ds(0, n), at] for ref in mapped_in],
        [c_ref.at[pl.ds(0, pairs)], c_ref.at[pl.ds(pairs, pairs)]] + quarters(m_ref),
        sems, 8,
    )
    large_copies = started(
        [right_in, right_other] + [ref.at[:, :, fits] for ref in left_all],
        [rhs.at[pl.ds(0, pairs)], rhs.at[pl.ds(pairs, pairs)]] + quarters(rhs, own),
        sems, 14,
    )
    split_all(z, functools.partial(packed_pair, z, all_ref), amps_high, amps_low)
    pair_list = [
        side_start(z, who, sub, side) + p
        for who in (owner, jnp.maximum(owner - 1, 0))
        for side in range(z.subs)
        for p in range(pairs)
    ]
    wait(pack_copies)
    for index in range(2 * own):
        unpack(z, s_ref, index, packs[index])
    scales = [
        scale_of(z, pair, e_ref[index, 0:1, :n], first, second, ranks, occupied)
        for index, pair in enumerate(pair_list)
    ]
    couplings = [e_ref[index, 1:2, :] for index in range(2 * own)]
    coupled = coupled_of(
        z, pair_list, near, s_ref, couplings, amps_high, amps_low, diag_high, diag_low
    )
    found = []
    for base in range(0, 2 * own, pairs):
        block = start_ref[pair_list[base] // pairs]
        for p in range(pairs):
            index = base + p
            found.append(block[:, p * n : (p + 1) * n] + coupled[index] * scales[index])
    turned = [value.T for value in found]
    wait(small_copies)
    weights = [split(2.0 * a - b) for a, b in zip(found, turned)]
    weights_turned = [split(2.0 * b - a) for a, b in zip(found[:own], turned[:own])]
    terms = (
        [mm3(w, split(c_ref[i])) for i, w in enumerate(weights_turned)]
        + [mm3(w, split(m_ref[i])) for i, w in enumerate(weights)]
    )
    orbital_list = (
        [first[pair] - owner * z.orbitals for pair in pair_list[:own]]
        + [second[pair] - owner * z.orbitals for pair in pair_list]
    )
    for index in range(0, 3 * own, 2):
        for o in range(z.orbitals):
            block = jnp.concatenate(
                [
                    jnp.where(orbital_list[i] == o, terms[i], 0.0) for i in (index, index + 1)
                ]
            ).T
            place = (slice(o * half, (o + 1) * half), slice(index * n, (index + 2) * n))
            rows_high[place], rows_low[place] = split(block)

    for p in range(pairs):
        flat[p] = found[p]
        even = flat[p, pl.ds(0, n // 2, 2), :]
        odd = flat[p, pl.ds(1, n // 2, 2), :]
        lines = jnp.concatenate([even, odd], axis=1)
        for r in range(n // 2):
            amp_ref[p : p + 1, r * 2 * n : (r + 1) * 2 * n] = lines[r : r + 1, :]

    wait(large_copies)
    step = 256
    rows = (rows_high[...], rows_low[...])
    copies = []
    for index, start in enumerate(range(0, z.fits, step)):
        factor = rhs[:, :, start : start + step].reshape(3 * own * n, step)
        grad[:, :, start : start + step] = mm3(rows, split(factor)).reshape(
            z.orbitals, half, step
        )
        window = pl.ds(start, step)
        copies += started(
            [grad.at[:, :, window]], [grad_out.at[:, :, window]], sems, 20 + index
        )
    wait(copies)


def gate(values, *after):
    return lax.optimization_barrier((tuple(values), after))[0]


def body(
    blocks,
    pno_coefficients,
    domain_map,
    pair_first,
    pair_second,
    pno_ranks,
    neighbours,
    couplings,
    intersections,
    pno_energy,
    occ_energy,
):
    z = Sizes(blocks, pno_coefficients, couplings)
    n, pairs, own, fits = z.pnos, z.pairs, z.own, z.fits
    half = z.paos // z.subs
    devices = z.owners * z.subs
    wide = z.links * n

    def scratch(*shape, kind=jnp.float32):
        return pltpu.VMEM(shape, kind)

    hbm = held_out
    mp, held = call(
        functools.partial(mapped_kernel, z),
        [(pairs, n + EXTRA, z.paos), blocks.shape],
        [hbm] * 5,
        (pno_coefficients, domain_map, pno_energy, couplings, blocks),
        [
            scratch(*pno_coefficients.shape),
            pltpu.VMEM(domain_map.shape, jnp.int32),
            scratch(*pno_energy.shape),
            scratch(*couplings.shape),
            pltpu.SemaphoreType.DMA((5,)),
        ],
        limit=8,
    )
    mp_below = shifted(mp, "orb", 1)
    intersection, coefficients = gate((intersections, pno_coefficients), mp)
    (left,) = call(
        functools.partial(left_kernel, z),
        [(pairs, n, fits + wide)],
        [smem, vmem, vmem, vmem],
        (pair_first, coefficients, held,
         intersection.reshape(pairs, z.links, n // 2, 2 * n)),
        limit=8,
    )
    (right_below,) = call(
        functools.partial(below_kernel, z),
        [(pairs, n, fits)],
        [smem, vmem, vmem],
        (pair_second, mp_below, held),
        limit=8,
    )
    down = shifted(right_below, "orb", -1)
    left_late, mp_late, coefficients = gate((left, mp, coefficients), right_below)
    left_below = shifted(left_late, "orb", 1)
    mp_other = swapped(mp_late, "sub")
    left_other = swapped(left_late, "sub")
    c_other = swapped(coefficients, "sub")

    (right_here,) = call(
        functools.partial(here_kernel, z),
        [(pairs, n, fits)],
        [smem, vmem, vmem, anywhere, anywhere, anywhere],
        (pair_second, mp, held, right_below, left_other, c_other),
        limit=8,
    )
    lists = (pair_first, pair_second, pno_ranks)
    sums, right = call(
        functools.partial(sums_kernel, z),
        [(n, pairs * n), (pairs, n, fits)],
        [smem] * 4 + [vmem] * 4,
        (*lists, occ_energy, mp, left, right_here, down),
        limit=8,
    )
    if lax.axis_size("fit") == 2:
        sums = sums + swapped(sums, "fit")
    else:
        sums = lax.psum(sums, "fit")
    start_amps = everyone(jnp.broadcast_to(sums[None], (devices, *sums.shape)))

    mp_late, left_late, right_late = gate((mp_below, left_below, right), sums)
    mp_below_other, left_below_other, right_other = [
        swapped(value, "sub") for value in (mp_late, left_late, right_late)
    ]

    lists = (*lists, neighbours, occ_energy)
    rows = (z.total, n, n)
    bf16 = jnp.bfloat16
    (own_amps,) = call(
        functools.partial(sweep_kernel, z),
        [(devices, n, pairs * n)],
        [smem] * 5 + [vmem] * 3 + [anywhere] * 3,
        (*lists, mp, left[:, :, fits:], start_amps, mp_below_other, left_below_other, right_other),
        [scratch(*rows, kind=bf16), scratch(*rows, kind=bf16)]
        + [scratch(pairs, wide, wide, kind=bf16)] * 2
        + [scratch(pairs, z.links // 2, n, 2 * n)],
        limit=6 + z.owners // 2,
    )
    amps = everyone(own_amps)

    args = (
        *lists, pno_coefficients, c_other, mp, mp_other, mp_below, mp_below_other,
        left, left_other, left_below, left_below_other, right, right_other, start_amps, amps,
    )
    amplitudes, gradient = call(
        functools.partial(final_kernel, z),
        [(pairs, n * n), (z.orbitals, half, fits)],
        [smem] * 5 + [anywhere] * 12 + [vmem] * 2,
        args,
        [
            scratch(2 * own, n, wide),
            scratch(own, n, half),
            scratch(2 * own, n, half),
            scratch(2 * own, EXTRA, z.paos),
            scratch(3 * own, n, fits),
            scratch(z.orbitals, half, fits),
            scratch(pairs, n, n),
            scratch(2 * own, z.links // 2, n, 2 * n),
            scratch(*rows, kind=bf16),
            scratch(*rows, kind=bf16),
        ]
        + [scratch(2 * own, wide, wide, kind=bf16)] * 2
        + [scratch(z.orbitals * half, 3 * own * n, kind=bf16)] * 2
        + [pltpu.SemaphoreType.DMA((20 + -(-fits // 256),))],
        limit=20 + z.owners // 2,
        out_specs=[vmem, hbm],
    )
    return (amplitudes, gradient)


def solution(mesh):
    in_specs = (
        P(("groups", "orb"), None, "fit"),
        P(("groups", "orb", "sub"), None, None),
        P(("groups", "orb", "sub"), None),
        P("groups"),
        P("groups"),
        P("groups"),
        P("groups", None),
        P(("groups", "orb", "sub"), None),
        P(("groups", "orb", "sub"), None, None),
        P(("groups", "orb", "sub"), None),
        P("groups"),
    )
    out_specs = (P(("groups", "orb", "sub"), None), P(("groups", "orb"), "sub", "fit"))
    return jax.shard_map(body, mesh=mesh, in_specs=in_specs, out_specs=out_specs, check_vma=False)
```

time: 82.5 us -> 83 us (level)
  waiting for transfers between devices: 28.2 us -> 34.1 us
  Pallas kernels: 17.4 us -> 14.8 us
  local copies, waits for them, and re-layouts: 12.2 us -> 11.1 us
  other arithmetic: 0.99 us -> 0.01 us
  starting transfers between devices: 22.3 us -> 21.4 us
    ppermute x6 -> x0, waiting for transfers between devices: 22.8 us -> none  [owners_of(): lax.ppermute(value, 'orb', [(s, s ^ step) for s in range(count)])[None]]
    all_to_all x0 -> x2, waiting for transfers between devices: none -> 15.8 us  [everyone(): return lax.all_to_all(value, ('orb', 'sub'), 0, 0)]
    ppermute x4 -> x3, waiting for transfers between devices: 0.01 us -> 13.3 us  [shifted(): lax.ppermute(value, axis, [(source, source + steps) for source in range(i...]
    all_to_all x0 -> x2, starting transfers between devices: none -> 6.83 us  [everyone(): return lax.all_to_all(value, ('orb', 'sub'), 0, 0)]
    reshape x3 -> x1, local copies, waits for them, and re-layouts: 4.57 us -> 0.09 us  [body(): intersection.reshape(pairs, z.links, n // 2, 2 * n)]
    ppermute x4 -> x3, starting transfers between devices: 15.8 us -> 11.6 us  [shifted(): lax.ppermute(value, axis, [(source, source + steps) for source in range(i...]
    pallas_call x7, Pallas kernels: 17.4 us -> 14.8 us  [call(): pl.pallas_call(kernel, out_shape=[jax.ShapeDtypeStruct(shape, jnp.float32...]
    ppermute x6 -> x0, starting transfers between devices: 2.49 us -> none  [owners_of(): lax.ppermute(value, 'orb', [(s, s ^ step) for s in range(count)])[None]]
  transfers between devices with their start and end apart: 23 -> 12, of which waited for: 10 -> 8; matrix products, arithmetic and copies ran while one was open for 7% -> 2% of each run, Pallas kernels for 11% -> 5%
where the time goes in v4:
time: 83 us; the launch traced here: 82.4 us
  waiting for transfers between devices  34.1 us (41%)
  starting transfers between devices  21.4 us (26%)
  Pallas kernels  14.8 us (18%)
  local copies, waits for them, and re-layouts  11.1 us (13%)
  between operations  0.92 us (1%)
    all_to_all x2, waiting for transfers between devices, everyone(): return lax.all_to_all(value, ('orb', 'sub'), 0, 0)  15.8 us
    pallas_call x7, Pallas kernels, call(): pl.pallas_call(kernel, out_shape=[jax.ShapeDtypeStruct(shape, jnp.float32...  14.8 us
    ppermute x3, waiting for transfers between devices, shifted(): lax.ppermute(value, axis, [(source, source + steps) for source in range(i...  13.3 us
    ppermute x3, starting transfers between devices, shifted(): lax.ppermute(value, axis, [(source, source + steps) for source in range(i...  11.6 us
    unnamed x59, local copies, waits for them, and re-layouts  9.64 us
    all_to_all x2, starting transfers between devices, everyone(): return lax.all_to_all(value, ('orb', 'sub'), 0, 0)  6.83 us
    ppermute x7, waiting for transfers between devices, swapped(): return lax.ppermute(value, axis, [(0, 1), (1, 0)])  5.03 us
    ppermute x7, starting transfers between devices, swapped(): return lax.ppermute(value, axis, [(0, 1), (1, 0)])  2.99 us
  transfers between devices with their start and end apart: 12, of which 8 were waited for; matrix products, arithmetic and copies ran while one was open for 2% of the time, Pallas kernels for 5%

profile of v4, /device:TPU:0, one launch (start us, length us, event | category | flops | bytes accessed | tf_op | source)
XLA Modules:
  0.0 82.4 jit_solution(2522862683681406022)
XLA Ops:
  0.6 1.6 %copy-done = f32[2,256,1024]{2,1,0:T(8,128)S(1)} copy-done((f32[2,256,1024]{2,1,0:T(8,128)S(1)}, f32[2,256,1024]{2,1,0:T(8,128)}, u32[]{:S(2)}) %copy-start) | copy-done | bytes 2097176
  2.2 0.9 %copy-done.1 = f32[2,64,256]{2,1,0:T(8,128)S(1)} copy-done((f32[2,64,256]{2,1,0:T(8,128)S(1)}, f32[2,64,256]{2,1,0:T(8,128)}, u32[]{:S(2)}) %copy-start.1) | copy-done | bytes 131096
  3.1 0.7 copy-done.24
  3.8 0.7 copy-done.25
  4.5 0.7 copy-done.26
  5.2 0.6 shard_map.122
  5.8 0.0 copy-start.14
  5.8 4.9 %collective-permute-start = (f32[2,72,256]{2,1,0:T(8,128)S(1)}, f32[2,72,256]{2,1,0:T(8,128)S(1)}, u32[]{:S(2)}, u32[]{:S(2)}) collective-permute-start(f32[2,72,256]{2,1,0:T(8,128)S(1)} %get-tuple-element.19.mp_ref.refs_2_), channel_id=1, source_target_pairs={{0,4},{4,8},{8,12},{1,5},{5,9},{9,13},{2,6},{6,10},{10,14},{3,7},{... | collective-permute-start | bytes 442376 | tf_op jit(solution)/shard_map/ppermute | solution.py:29
  10.8 0.1 reshape.8.q_ref
  10.9 1.3 %shard_map.123.left_ref.refs_6_ = f32[2,64,1280]{2,1,0:T(8,128)S(1)} custom-call(s32[16]{0:T(128)S(1)} %copy-done.17, f32[2,64,256]{2,1,0:T(8,128)S(1)} %copy-done.2, f32[2,256,1024]{2,1,0:T(8,128)S(1)} %get-tuple-element.16.b_ref, f32[2,4,32,128]{3,2,1,0:T(8,128)S(1)} %reshape.8.q_ref), custom_call_target="tpu_custom_call" | custom-call | tf_op jit(solution)/shard_map/pallas_call | solution.py:60
  12.2 0.0 copy-start.3
  12.2 0.0 copy-start.15
  12.2 1.6 %collective-permute-done.mp_below.refs_4_ = f32[2,72,256]{2,1,0:T(8,128)S(1)} collective-permute-done((f32[2,72,256]{2,1,0:T(8,128)S(1)}, f32[2,72,256]{2,1,0:T(8,128)S(1)}, u32[]{:S(2)}, u32[]{:S(2)}) %collective-permute-start) | collective-permute-done | bytes 147488 | tf_op jit(solution)/shard_map/ppermute | solution.py:29
  13.9 1.3 %shard_map.124.right_below = f32[2,64,1024]{2,1,0:T(8,128)S(1)} custom-call(s32[16]{0:T(128)S(1)} %copy-done.14, f32[2,72,256]{2,1,0:T(8,128)S(1)} %collective-permute-done.mp_below.refs_4_, f32[2,256,1024]{2,1,0:T(8,128)S(1)} %get-tuple-element.16.b_ref), custom_call_target="tpu_custom_call" | custom-call | tf_op jit(solution)/shard_map/pallas_call | solution.py:60
  15.2 0.7 copy-done.5
  15.9 5.4 %collective-permute-start.3 = (f32[2,64,1280]{2,1,0:T(8,128)S(1)}, f32[2,64,1280]{2,1,0:T(8,128)}, u32[]{:S(2)}, u32[]{:S(2)}) collective-permute-start(f32[2,64,1280]{2,1,0:T(8,128)S(1)} %shard_map.123.left_ref.refs_6_), channel_id=1, source_target_pairs={{0,4},{4,8},{8,12},{1,5},{5,9},{9,13},{2,6},{6,10},{10,14},{3,7},{... | collective-permute-start | bytes 1966088 | tf_op jit(solution)/shard_map/ppermute | solution.py:29
  21.2 1.3 %collective-permute-start.5 = (f32[2,64,1024]{2,1,0:T(8,128)S(1)}, f32[2,64,1024]{2,1,0:T(8,128)S(1)}, u32[]{:S(2)}, u32[]{:S(2)}) collective-permute-start(f32[2,64,1024]{2,1,0:T(8,128)S(1)} %shard_map.124.right_below), channel_id=1, source_target_pairs={{4,0},{8,4},{12,8},{5,1},{9,5},{13,9},{6,2},{10,6},{14,10},{7,3},{... | collective-permute-start | bytes 1572872 | tf_op jit(solution)/shard_map/ppermute | solution.py:29
  22.5 0.1 collective-permute-start.1
  22.7 1.3 %collective-permute-done.1.c_other.refs_1_ = f32[2,64,256]{2,1,0:T(8,128)S(1)} collective-permute-done((f32[2,64,256]{2,1,0:T(8,128)S(1)}, f32[2,64,256]{2,1,0:T(8,128)S(1)}, u32[]{:S(2)}, u32[]{:S(2)}) %collective-permute-start.1) | collective-permute-done | bytes 131104 | tf_op jit(solution)/shard_map/ppermute | solution.py:33
  24.0 1.3 %shard_map.125.here_ref = f32[2,64,1024]{2,1,0:T(8,128)S(1)} custom-call(s32[16]{0:T(128)S(1)} %copy-done.15, f32[2,72,256]{2,1,0:T(8,128)S(1)} %get-tuple-element.19.mp_ref.refs_2_, f32[2,256,1024]{2,1,0:T(8,128)S(1)} %get-tuple-element.16.b_ref, f32[2,64,1024]{2,1,0:T(8,128)S(1)} %shard_map.124.right_below, ...), custom_call_target="tpu_custom_call" | custom-call | tf_op jit(solution)/shard_map/pallas_call | solution.py:60
  25.2 0.0 copy-start.28
  25.2 0.0 copy-start.16
  25.3 0.0 copy-start.19
  25.3 0.0 copy-start.23
  25.3 11.7 %collective-permute-done.5.down_ref = f32[2,64,1024]{2,1,0:T(8,128)S(1)} collective-permute-done((f32[2,64,1024]{2,1,0:T(8,128)S(1)}, f32[2,64,1024]{2,1,0:T(8,128)S(1)}, u32[]{:S(2)}, u32[]{:S(2)}) %collective-permute-start.5) | collective-permute-done | bytes 524320 | tf_op jit(solution)/shard_map/ppermute | solution.py:29
  37.0 1.6 %shard_map.126 = (f32[64,128]{1,0:T(8,128)S(1)}, f32[2,64,1024]{2,1,0:T(8,128)}) custom-call(s32[16]{0:T(128)S(1)} %copy-done.18, s32[16]{0:T(128)S(1)} %copy-done.15, s32[16]{0:T(128)S(1)} %copy-done.20, f32[8]{0:T(128)S(1)} %copy-done.22, f32[2,72,256]{2,1,0:T(8,128)S(1)} %get-tuple-element.19.mp_ref.refs_2_, ...), custom_call_target="tpu_custom_call" | custom-call | tf_op jit(solution)/shard_map/pallas_call | solution.py:60
  38.6 1.5 %collective-permute-start.6 = (f32[64,128]{1,0:T(8,128)S(1)}, f32[64,128]{1,0:T(8,128)S(1)}, u32[]{:S(2)}, u32[]{:S(2)}) collective-permute-start(f32[64,128]{1,0:T(8,128)S(1)} %get-tuple-element.22), channel_id=1, source_target_pairs={{0,2},{2,0},{1,3},{3,1},{4,6},{6,4},{5,7},{7,5},{8,10},{10,8},{9,1... | collective-permute-start | bytes 98312 | tf_op jit(solution)/shard_map/ppermute | solution.py:33
  40.1 2.4 %collective-permute-done.6 = f32[64,128]{1,0:T(8,128)S(1)} collective-permute-done((f32[64,128]{1,0:T(8,128)S(1)}, f32[64,128]{1,0:T(8,128)S(1)}, u32[]{:S(2)}, u32[]{:S(2)}) %collective-permute-start.6) | collective-permute-done | bytes 32800 | tf_op jit(solution)/shard_map/ppermute | solution.py:33
  42.6 0.1 collective-permute-start.8
  42.6 0.5 collective-permute-start.9
  43.1 0.7 broadcast_in_dim.2
  43.9 3.4 %all-to-all-start = ((f32[8,64,128]{2,1,0:T(8,128)}), f32[8,64,128]{2,1,0:T(8,128)S(1)}, u32[]{:S(2)}, u32[]{:S(2)}) async-start(f32[8,64,128]{2,1,0:T(8,128)} %broadcast_in_dim.2), calls=%async_computation | async-start | bytes 524288 | tf_op jit(solution)/shard_map/all_to_all | solution.py:37
  47.3 0.4 collective-permute-start.7
  47.7 0.7 slice.4.q_ref
  48.4 0.1 copy.14.near
  48.5 0.3 collective-permute-done.7.refs_0_.refs_5_
  48.7 8.2 %all-to-all-done.all_ref.refs_12_ = f32[8,64,128]{2,1,0:T(8,128)S(1)} async-done(((f32[8,64,128]{2,1,0:T(8,128)}), f32[8,64,128]{2,1,0:T(8,128)S(1)}, u32[]{:S(2)}, u32[]{:S(2)}) %all-to-all-start) | async-done | bytes 262176 | tf_op jit(solution)/shard_map/all_to_all | solution.py:37
  57.0 0.9 %copy-done.11 = f32[2,64,256]{2,1,0:T(8,128)S(1)} copy-done((f32[2,64,256]{2,1,0:T(8,128)S(1)}, f32[2,64,256]{2,1,0:T(8,128)}, u32[]{:S(2)}) %copy-start.11) | copy-done | bytes 131096
  57.9 2.2 %shard_map.127 = f32[8,64,128]{2,1,0:T(8,128)} custom-call(s32[16]{0:T(128)S(1)} %copy-done.19, s32[16]{0:T(128)S(1)} %copy-done.16, s32[16]{0:T(128)S(1)} %copy-done.21, s32[16,4]{1,0:T(8,128)S(1)} %copy.14.near, f32[8]{0:T(128)S(1)} %copy-done.23, f32[2,72,256]{2,1,0:T(8,128)S(1)} %get-tuple-element.19.mp_ref.refs_2_, f32[2,64,256]{2,1,0:T(8,128)S(1)} %copy-done.11, ...), custom_call_target="tpu_custom_call" | custom-call | tf_op jit(solution)/shard_map/pallas_call | solution.py:60
  60.1 3.4 %all-to-all-start.1 = ((f32[8,64,128]{2,1,0:T(8,128)}), f32[8,64,128]{2,1,0:T(8,128)S(1)}, u32[]{:S(2)}, u32[]{:S(2)}) async-start(f32[8,64,128]{2,1,0:T(8,128)} %shard_map.127), calls=%async_computation.1 | async-start | bytes 524288 | tf_op jit(solution)/shard_map/all_to_all | solution.py:37
  63.5 0.4 collective-permute-start.2
  63.9 1.0 %collective-permute-done.2.refs_3_ = f32[2,72,256]{2,1,0:T(8,128)S(1)} collective-permute-done((f32[2,72,256]{2,1,0:T(8,128)S(1)}, f32[2,72,256]{2,1,0:T(8,128)S(1)}, u32[]{:S(2)}, u32[]{:S(2)}) %collective-permute-start.2) | collective-permute-done | bytes 147488 | tf_op jit(solution)/shard_map/ppermute | solution.py:33
  65.0 0.7 copy-done.12
  65.6 7.6 %all-to-all-done.1.refs_13_ = f32[8,64,128]{2,1,0:T(8,128)S(1)} async-done(((f32[8,64,128]{2,1,0:T(8,128)}), f32[8,64,128]{2,1,0:T(8,128)S(1)}, u32[]{:S(2)}, u32[]{:S(2)}) %all-to-all-start.1) | async-done | bytes 262176 | tf_op jit(solution)/shard_map/all_to_all | solution.py:37
  73.2 0.9 %copy-done.8 = f32[2,72,256]{2,1,0:T(8,128)S(1)} copy-done((f32[2,72,256]{2,1,0:T(8,128)S(1)}, f32[2,72,256]{2,1,0:T(8,128)}, u32[]{:S(2)}) %copy-start.8) | copy-done | bytes 147480
  74.1 0.9 %copy-done.10 = f32[2,64,256]{2,1,0:T(8,128)S(1)} copy-done((f32[2,64,256]{2,1,0:T(8,128)S(1)}, f32[2,64,256]{2,1,0:T(8,128)}, u32[]{:S(2)}) %copy-start.10) | copy-done | bytes 131096
  75.0 0.9 %copy-done.13 = f32[2,72,256]{2,1,0:T(8,128)S(1)} copy-done((f32[2,72,256]{2,1,0:T(8,128)S(1)}, f32[2,72,256]{2,1,0:T(8,128)}, u32[]{:S(2)}) %copy-start.13) | copy-done | bytes 147480
  75.9 6.5 %shard_map.128 = (f32[2,4096]{1,0:T(2,128)}, f32[2,128,1024]{2,1,0:T(8,128)}) custom-call(s32[16]{0:T(128)S(1)} %copy-done.19, s32[16]{0:T(128)S(1)} %copy-done.16, s32[16]{0:T(128)S(1)} %copy-done.21, s32[16,4]{1,0:T(8,128)S(1)} %copy.14.near, f32[8]{0:T(128)S(1)} %copy-done.23, f32[2,64,256]{2,1,0:T(8,128)S(1)} %copy-done.4, f32[2,64,256]{2,1,0:T(8,128)S(1)} %copy-done.10, ...), custom_call_target="tpu_custom_call" | custom-call | tf_op jit(solution)/shard_map/pallas_call | solution.py:60
  (46 shorter events, 0.1 us)
Async XLA Ops:
  0.6 1.6 %copy-start = (f32[2,256,1024]{2,1,0:T(8,128)S(1)}, f32[2,256,1024]{2,1,0:T(8,128)}, u32[]{:S(2)}) copy-start(f32[2,256,1024]{2,1,0:T(8,128)} %b_in.1) | copy-start | bytes 6291460
  2.2 0.9 %copy-start.1 = (f32[2,64,256]{2,1,0:T(8,128)S(1)}, f32[2,64,256]{2,1,0:T(8,128)}, u32[]{:S(2)}) copy-start(f32[2,64,256]{2,1,0:T(8,128)} %refs_0_.1) | copy-start | bytes 393220
  3.1 0.7 copy-start.24
  3.8 0.7 copy-start.25
  4.5 0.7 copy-start.26
  5.2 5.6 %copy-start.27 = (f32[2,4,4096]{2,1,0:T(4,128)S(1)}, f32[2,4,4096]{2,1,0:T(4,128)}, u32[]{:S(2)}) copy-start(f32[2,4,4096]{2,1,0:T(4,128)} %param.19) | copy-start | bytes 393220
  5.2 5.7 %copy-start.2 = (f32[2,64,256]{2,1,0:T(8,128)S(1)}, f32[2,64,256]{2,1,0:T(8,128)}, u32[]{:S(2)}) copy-start(f32[2,64,256]{2,1,0:T(8,128)} %refs_0_.1) | copy-start | bytes 393220
  5.2 5.7 %copy-start.17 = (s32[16]{0:T(128)S(1)}, s32[16]{0:T(128)}, u32[]{:S(2)}) copy-start(s32[16]{0:T(128)} %first.7) | copy-start | bytes 196
  5.8 8.0 %copy-start.14 = (s32[16]{0:T(128)S(1)}, s32[16]{0:T(128)}, u32[]{:S(2)}) copy-start(s32[16]{0:T(128)} %second.9) | copy-start | bytes 196
  5.8 8.0 %collective-permute-start = (f32[2,72,256]{2,1,0:T(8,128)S(1)}, f32[2,72,256]{2,1,0:T(8,128)S(1)}, u32[]{:S(2)}, u32[]{:S(2)}) collective-permute-start(f32[2,72,256]{2,1,0:T(8,128)S(1)} %get-tuple-element.19.mp_ref.refs_2_), channel_id=1, source_target_pairs={{0,4},{4,8},{8,12},{1,5},{5,9},{9,13},{2,6},{6,10},{10,14},{3,7},{... | collective-permute-start | bytes 442376 | tf_op jit(solution)/shard_map/ppermute | solution.py:29
  12.2 10.3 %copy-start.3 = (f32[2,64,256]{2,1,0:T(8,128)S(1)}, f32[2,64,256]{2,1,0:T(8,128)}, u32[]{:S(2)}) copy-start(f32[2,64,256]{2,1,0:T(8,128)} %refs_0_.1) | copy-start | bytes 393220
  12.2 11.7 %copy-start.15 = (s32[16]{0:T(128)S(1)}, s32[16]{0:T(128)}, u32[]{:S(2)}) copy-start(s32[16]{0:T(128)} %second.9) | copy-start | bytes 196
  15.2 0.7 copy-start.5
  15.8 21.2 %copy-start.18 = (s32[16]{0:T(128)S(1)}, s32[16]{0:T(128)}, u32[]{:S(2)}) copy-start(s32[16]{0:T(128)} %first.7) | copy-start | bytes 196
  15.8 21.2 %copy-start.20 = (s32[16]{0:T(128)S(1)}, s32[16]{0:T(128)}, u32[]{:S(2)}) copy-start(s32[16]{0:T(128)} %ranks.5) | copy-start | bytes 196
  15.8 21.2 %copy-start.22 = (f32[8]{0:T(128)S(1)}, f32[8]{0:T(128)}, u32[]{:S(2)}) copy-start(f32[8]{0:T(128)} %occupied.5) | copy-start | bytes 100
  15.8 8.1 %collective-permute-start.4 = (f32[2,64,1280]{2,1,0:T(8,128)S(1)}, f32[2,64,1280]{2,1,0:T(8,128)S(1)}, u32[]{:S(2)}, u32[]{:S(2)}) collective-permute-start(f32[2,64,1280]{2,1,0:T(8,128)S(1)} %shard_map.123.left_ref.refs_6_), channel_id=1, source_target_pairs={{0,1},{1,0},{2,3},{3,2},{4,5},{5,4},{6,7},{7,6},{8,9},{9,8},{10,11... | collective-permute-start | bytes 1966088 | tf_op jit(solution)/shard_map/ppermute | solution.py:33
  15.9 26.7 %collective-permute-start.3 = (f32[2,64,1280]{2,1,0:T(8,128)S(1)}, f32[2,64,1280]{2,1,0:T(8,128)}, u32[]{:S(2)}, u32[]{:S(2)}) collective-permute-start(f32[2,64,1280]{2,1,0:T(8,128)S(1)} %shard_map.123.left_ref.refs_6_), channel_id=1, source_target_pairs={{0,4},{4,8},{8,12},{1,5},{5,9},{9,13},{2,6},{6,10},{10,14},{3,7},{... | collective-permute-start | bytes 1966088 | tf_op jit(solution)/shard_map/ppermute | solution.py:29
  21.2 15.8 %collective-permute-start.5 = (f32[2,64,1024]{2,1,0:T(8,128)S(1)}, f32[2,64,1024]{2,1,0:T(8,128)S(1)}, u32[]{:S(2)}, u32[]{:S(2)}) collective-permute-start(f32[2,64,1024]{2,1,0:T(8,128)S(1)} %shard_map.124.right_below), channel_id=1, source_target_pairs={{4,0},{8,4},{12,8},{5,1},{9,5},{13,9},{6,2},{10,6},{14,10},{7,3},{... | collective-permute-start | bytes 1572872 | tf_op jit(solution)/shard_map/ppermute | solution.py:29
  22.5 1.4 %collective-permute-start.1 = (f32[2,64,256]{2,1,0:T(8,128)S(1)}, f32[2,64,256]{2,1,0:T(8,128)S(1)}, u32[]{:S(2)}, u32[]{:S(2)}) collective-permute-start(f32[2,64,256]{2,1,0:T(8,128)S(1)} %copy-done.3), channel_id=1, source_target_pairs={{0,1},{1,0},{2,3},{3,2},{4,5},{5,4},{6,7},{7,6},{8,9},{9,8},{10,11... | collective-permute-start | bytes 393224 | tf_op jit(solution)/shard_map/ppermute | solution.py:33
  23.9 14.7 %copy-start.9 = (f32[2,64,256]{2,1,0:T(8,128)}, f32[2,64,256]{2,1,0:T(8,128)S(1)}, u32[]{:S(2)}) copy-start(f32[2,64,256]{2,1,0:T(8,128)S(1)} %collective-permute-done.1.c_other.refs_1_) | copy-start | bytes 393220
  25.2 22.1 %copy-start.6 = (f32[2,72,256]{2,1,0:T(8,128)S(1)}, f32[2,72,256]{2,1,0:T(8,128)}, u32[]{:S(2)}) copy-start(f32[2,72,256]{2,1,0:T(8,128)} %copy-done.5) | copy-start | bytes 442372
  25.2 23.1 %copy-start.28 = (s32[16,4]{0,1:T(4,128)S(1)}, s32[16,4]{0,1:T(4,128)}, u32[]{:S(2)}) copy-start(s32[16,4]{0,1:T(4,128)} %param.17) | copy-start | bytes 772
  25.2 31.7 %copy-start.16 = (s32[16]{0:T(128)S(1)}, s32[16]{0:T(128)}, u32[]{:S(2)}) copy-start(s32[16]{0:T(128)} %second.9) | copy-start | bytes 196
  25.3 31.7 %copy-start.19 = (s32[16]{0:T(128)S(1)}, s32[16]{0:T(128)}, u32[]{:S(2)}) copy-start(s32[16]{0:T(128)} %first.7) | copy-start | bytes 196
  25.3 31.7 %copy-start.21 = (s32[16]{0:T(128)S(1)}, s32[16]{0:T(128)}, u32[]{:S(2)}) copy-start(s32[16]{0:T(128)} %ranks.5) | copy-start | bytes 196
  25.3 31.7 %copy-start.23 = (f32[8]{0:T(128)S(1)}, f32[8]{0:T(128)}, u32[]{:S(2)}) copy-start(f32[8]{0:T(128)} %occupied.5) | copy-start | bytes 100
  38.6 34.5 %copy-start.4 = (f32[2,64,256]{2,1,0:T(8,128)S(1)}, f32[2,64,256]{2,1,0:T(8,128)}, u32[]{:S(2)}) copy-start(f32[2,64,256]{2,1,0:T(8,128)} %refs_0_.1) | copy-start | bytes 393220
  38.6 3.9 %collective-permute-start.6 = (f32[64,128]{1,0:T(8,128)S(1)}, f32[64,128]{1,0:T(8,128)S(1)}, u32[]{:S(2)}, u32[]{:S(2)}) collective-permute-start(f32[64,128]{1,0:T(8,128)S(1)} %get-tuple-element.22), channel_id=1, source_target_pairs={{0,2},{2,0},{1,3},{3,1},{4,6},{6,4},{5,7},{7,5},{8,10},{10,8},{9,1... | collective-permute-start | bytes 98312 | tf_op jit(solution)/shard_map/ppermute | solution.py:33
  42.6 14.4 %collective-permute-start.8 = (f32[2,64,1280]{2,1,0:T(8,128)}, f32[2,64,1280]{2,1,0:T(8,128)S(1)}, u32[]{:S(2)}, u32[]{:S(2)}) collective-permute-start(f32[2,64,1280]{2,1,0:T(8,128)} %collective-permute-done.3.refs_8_), channel_id=1, source_target_pairs={{0,1},{1,0},{2,3},{3,2},{4,5},{5,4},{6,7},{7,6},{8,9},{9,8},{10,11... | collective-permute-start | bytes 1966088 | tf_op jit(solution)/shard_map/ppermute | solution.py:33
  42.6 14.3 %collective-permute-start.9 = (f32[2,64,1024]{2,1,0:T(8,128)}, f32[2,64,1024]{2,1,0:T(8,128)S(1)}, u32[]{:S(2)}, u32[]{:S(2)}) collective-permute-start(f32[2,64,1024]{2,1,0:T(8,128)} %get-tuple-element.25.refs_10_), channel_id=1, source_target_pairs={{0,1},{1,0},{2,3},{3,2},{4,5},{5,4},{6,7},{7,6},{8,9},{9,8},{10,11... | collective-permute-start | bytes 1572872 | tf_op jit(solution)/shard_map/ppermute | solution.py:33
  43.9 13.1 %all-to-all-start = ((f32[8,64,128]{2,1,0:T(8,128)}), f32[8,64,128]{2,1,0:T(8,128)S(1)}, u32[]{:S(2)}, u32[]{:S(2)}) async-start(f32[8,64,128]{2,1,0:T(8,128)} %broadcast_in_dim.2), calls=%async_computation | async-start | bytes 524288 | tf_op jit(solution)/shard_map/all_to_all | solution.py:37
  47.3 1.4 %collective-permute-start.7 = (f32[2,72,256]{2,1,0:T(8,128)S(1)}, f32[2,72,256]{2,1,0:T(8,128)S(1)}, u32[]{:S(2)}, u32[]{:S(2)}) collective-permute-start(f32[2,72,256]{2,1,0:T(8,128)S(1)} %copy-done.6), channel_id=1, source_target_pairs={{0,1},{1,0},{2,3},{3,2},{4,5},{5,4},{6,7},{7,6},{8,9},{9,8},{10,11... | collective-permute-start | bytes 442376 | tf_op jit(solution)/shard_map/ppermute | solution.py:33
  48.7 11.4 %copy-start.7 = (f32[2,72,256]{2,1,0:T(8,128)}, f32[2,72,256]{2,1,0:T(8,128)S(1)}, u32[]{:S(2)}) copy-start(f32[2,72,256]{2,1,0:T(8,128)S(1)} %collective-permute-done.7.refs_0_.refs_5_) | copy-start | bytes 442372
  57.0 0.9 %copy-start.11 = (f32[2,64,256]{2,1,0:T(8,128)S(1)}, f32[2,64,256]{2,1,0:T(8,128)}, u32[]{:S(2)}) copy-start(f32[2,64,256]{2,1,0:T(8,128)} %slice.4.q_ref) | copy-start | bytes 393220
  60.1 13.1 %all-to-all-start.1 = ((f32[8,64,128]{2,1,0:T(8,128)}), f32[8,64,128]{2,1,0:T(8,128)S(1)}, u32[]{:S(2)}, u32[]{:S(2)}) async-start(f32[8,64,128]{2,1,0:T(8,128)} %shard_map.127), calls=%async_computation.1 | async-start | bytes 524288 | tf_op jit(solution)/shard_map/all_to_all | solution.py:37
  63.5 1.4 %collective-permute-start.2 = (f32[2,72,256]{2,1,0:T(8,128)S(1)}, f32[2,72,256]{2,1,0:T(8,128)S(1)}, u32[]{:S(2)}, u32[]{:S(2)}) collective-permute-start(f32[2,72,256]{2,1,0:T(8,128)S(1)} %get-tuple-element.19.mp_ref.refs_2_), channel_id=1, source_target_pairs={{0,1},{1,0},{2,3},{3,2},{4,5},{5,4},{6,7},{7,6},{8,9},{9,8},{10,11... | collective-permute-start | bytes 442376 | tf_op jit(solution)/shard_map/ppermute | solution.py:33
  65.0 0.7 copy-start.12
  73.2 0.9 %copy-start.8 = (f32[2,72,256]{2,1,0:T(8,128)S(1)}, f32[2,72,256]{2,1,0:T(8,128)}, u32[]{:S(2)}) copy-start(f32[2,72,256]{2,1,0:T(8,128)} %copy-done.7) | copy-start | bytes 442372
  74.1 0.9 %copy-start.10 = (f32[2,64,256]{2,1,0:T(8,128)S(1)}, f32[2,64,256]{2,1,0:T(8,128)}, u32[]{:S(2)}) copy-start(f32[2,64,256]{2,1,0:T(8,128)} %copy-done.9) | copy-start | bytes 393220
  75.0 0.9 %copy-start.13 = (f32[2,72,256]{2,1,0:T(8,128)S(1)}, f32[2,72,256]{2,1,0:T(8,128)}, u32[]{:S(2)}) copy-start(f32[2,72,256]{2,1,0:T(8,128)} %copy-done.12) | copy-start | bytes 442372

commit v5 on v4

v5 whole, which is shorter than its diff:
```python
import functools

import jax
import jax.numpy as jnp
from jax import lax
from jax.experimental import pallas as pl
from jax.experimental.pallas import tpu as pltpu
from jax.sharding import PartitionSpec as P

ITERS = 2
SMALL = 4
MIB = 1 << 20
EXTRA = 8

high = lax.Precision.HIGH
smem = pl.BlockSpec(memory_space=pltpu.SMEM)
vmem = pl.BlockSpec(memory_space=pltpu.VMEM)


def mm(a, b, contract=((1,), (0,))):
    return lax.dot_general(
        a, b, (contract, ((), ())), precision=high, preferred_element_type=jnp.float32
    )


def shifted(value, axis, steps):
    count = lax.axis_size(axis)
    initial, last = (max(0, -steps), min(count, count - steps))
    return lax.ppermute(value, axis, [(source, source + steps) for source in range(initial, last)])


def swapped(value, axis):
    return lax.ppermute(value, axis, [(0, 1), (1, 0)])


def f32(flag):
    return flag.astype(jnp.float32)


class Sizes:
    def __init__(self, blocks, pno_coefficients, couplings):
        self.orbitals, self.paos, self.fits = blocks.shape
        self.pairs, self.pnos = pno_coefficients.shape[:2]
        self.links = couplings.shape[1]
        self.subs = lax.axis_size("sub")
        self.owners = lax.axis_size("orb")
        self.fit_count = lax.axis_size("fit")
        self.own = self.pairs * self.subs
        self.total = self.own * self.owners


anywhere = pl.BlockSpec(memory_space=pl.ANY)
held_out = pl.BlockSpec(memory_space=pltpu.HBM)


def call(kernel, outs, ins, args, scratch=(), limit=16, out_specs=None):
    return pl.pallas_call(
        kernel,
        out_shape=[jax.ShapeDtypeStruct(shape, jnp.float32) for shape in outs],
        in_specs=ins,
        out_specs=out_specs or [vmem] * len(outs),
        scratch_shapes=list(scratch),
        compiler_params=pltpu.CompilerParams(vmem_limit_bytes=limit and limit * MIB),
    )(*args)


def started(sources, targets, sems, base=0):
    copies = [
        pltpu.make_async_copy(source, target, sems.at[base + index])
        for index, (source, target) in enumerate(zip(sources, targets))
    ]
    for copy in copies:
        copy.start()
    return copies


def wait(copies):
    for copy in copies:
        copy.wait()


def side_start(z, owner, sub, side):
    return owner * z.own + (sub if side == 0 else 1 - sub) * z.pairs


def scale_of(z, pair, level, first, second, ranks, occupied):
    n = z.pnos
    row_ids = lax.broadcasted_iota(jnp.int32, (n, n), 0)
    column_ids = lax.broadcasted_iota(jnp.int32, (n, n), 1)
    level = level * jnp.ones((n, 1), jnp.float32)
    rank = ranks[pair]
    kept = f32((row_ids < rank) & (column_ids < rank))
    return kept / (level + level.T - (occupied[first[pair]] + occupied[second[pair]]))


def split(value):
    high_part = value.astype(jnp.bfloat16)
    return high_part, (value - high_part.astype(jnp.float32)).astype(jnp.bfloat16)


def mm3(a, b, contract=((1,), (0,))):
    def one(x, y):
        return lax.dot_general(x, y, (contract, ((), ())), preferred_element_type=jnp.float32)

    return one(a[0], b[0]) + (one(a[0], b[1]) + one(a[1], b[0]))


def mapped_kernel(z, c_in, map_in, e_in, coupling_in, mp_ref, c_ref, map_ref, e_ref, coupling,
                  sems):
    n = z.pnos
    copies = started(
        [c_in, map_in, e_in, coupling_in], [c_ref, map_ref, e_ref, coupling], sems
    )
    wait(copies)
    rows = lax.broadcasted_iota(jnp.int32, (z.paos, z.paos), 0)
    lane_link = lax.broadcasted_iota(jnp.int32, (1, z.links * n), 1) // n
    for p in range(z.pairs):
        select = f32(map_ref[p : p + 1, :] == rows).astype(jnp.bfloat16)
        c_high, c_low = split(c_ref[p])
        mp_ref[p, :n, :] = lax.dot_general(
            c_high, select, (((1,), (1,)), ((), ())), preferred_element_type=jnp.float32
        ) + lax.dot_general(
            c_low, select, (((1,), (1,)), ((), ())), preferred_element_type=jnp.float32
        )
        mp_ref[p, n:, :] = jnp.zeros((EXTRA, z.paos), jnp.float32)
        mp_ref[p, n : n + 1, :n] = e_ref[p : p + 1, :]
        spread = jnp.zeros((1, z.links * n), jnp.float32)
        for k in range(z.links):
            spread = jnp.where(lane_link == k, coupling[p : p + 1, k : k + 1], spread)
        mp_ref[p, n + 1 : n + 2, :] = spread


def small(z):
    return z.owners <= SMALL and z.pairs == z.fit_count == 2


def each_pair(z, action):
    if z.owners <= SMALL:
        for pair in range(z.total):
            action(pair)
    else:
        @pl.loop(0, z.total)
        def _(pair):
            action(pair)


def pack_kernel(z, s_ref, mp_ref, order, out_ref):
    n = z.pnos
    line = 2 * n
    base = z.links * n // 2
    for slot in range(1 if small(z) else z.pairs):
        p = lax.axis_index("fit") if small(z) else slot
        at = 0 if small(z) else slot
        for r in range(n // 2):
            lines = s_ref[p, :, r * line : (r + 1) * line]
            for k in range(z.links):
                row = k * n // 2 + r
                out_ref[at, row : row + 1, :] = lines[k : k + 1, :]
        out_ref[at, base:, :] = jnp.zeros((EXTRA, line), jnp.float32)
        out_ref[at, base : base + 1, :] = mp_ref[p, n : n + 1, :line]
        for k in range(z.links // 2):
            out_ref[at, base + 1 + k : base + 2 + k, :] = mp_ref[
                p, n + 1 : n + 2, k * line : (k + 1) * line
            ]
    if small(z):
        for copy in range(1, z.owners):
            out_ref[copy] = out_ref[0]


def below_kernel(z, second, mp_below, b_ref, order, right_ref):
    owner, sub = lax.axis_index("orb"), lax.axis_index("sub")
    start = side_start(z, jnp.maximum(owner - 1, 0), sub, 0)
    for p in range(z.pairs):
        j = second[start + p] - owner * z.orbitals
        held = jnp.where(j >= 0, 1.0, 0.0)
        mapped = mp_below[p, : z.pnos, :] * held
        right_ref[p] = mm(mapped, b_ref[jnp.clip(j, 0, z.orbitals - 1)])


def left_kernel(z, first, c_ref, b_ref, left_ref):
    owner, sub = lax.axis_index("orb"), lax.axis_index("sub")
    start = side_start(z, owner, sub, 0)
    for p in range(z.pairs):
        left_ref[p] = mm(c_ref[p], b_ref[first[start + p] - owner * z.orbitals])


def here_kernel(z, second, mp_ref, b_ref, order, right_ref):
    owner, sub = lax.axis_index("orb"), lax.axis_index("sub")
    start = side_start(z, owner, sub, 0)
    for p in range(z.pairs):
        j = second[start + p] - owner * z.orbitals
        local = jnp.where(j < z.orbitals, 1.0, 0.0)
        right_ref[p] = mm(
            mp_ref[p, : z.pnos, :] * local, b_ref[jnp.minimum(j, z.orbitals - 1)]
        )


def sums_kernel(z, first, second, ranks, occupied, mp_ref, left_ref, here_ref, down_ref, *refs):
    sums_ref, right_ref = refs[-2:]
    owner, sub = lax.axis_index("orb"), lax.axis_index("sub")
    start = side_start(z, owner, sub, 0)
    n = z.pnos
    for p in range(z.pairs):
        right = here_ref[p] + down_ref[p]
        right_ref[p] = right
        scale = scale_of(
            z, start + p, mp_ref[p, n : n + 1, :n], first, second, ranks, occupied
        )
        part = mm(left_ref[p], right, ((1,), (1,)))
        sums_ref[:, p * n : (p + 1) * n] = -part * scale


def unpack_kernel(z, first, second, ranks, occupied, *refs):
    packs = refs[:-5]
    high_ref, low_ref, scale_ref, coupling_ref, rows = refs[-5:]
    sub, fit = lax.axis_index("sub"), lax.axis_index("fit")
    n = z.pnos
    base = z.links * n // 2

    def one(pair, block, slot):
        for k in range(0, z.links, 2):
            two = [block(k * n // 2, n // 2), block((k + 1) * n // 2, n // 2)]
            for odd in range(2):
                rows[slot, k // 2, pl.ds(odd, n // 2, 2), :] = jnp.concatenate(
                    [part[:, odd * n : (odd + 1) * n] for part in two], axis=1
                )
        s = jnp.concatenate([rows[slot, k] for k in range(z.links // 2)], axis=1)
        high_ref[pair], low_ref[pair] = split(s)
        extra = block(base, EXTRA)
        scale_ref[pair] = scale_of(z, pair, extra[0:1, :n], first, second, ranks, occupied)
        coupling_ref[pair, 0:1, :] = jnp.concatenate(
            [extra[1 + k : 2 + k, :] for k in range(z.links // 2)], axis=1
        )

    if small(z):
        for index, ref in enumerate(packs):
            side = sub if index < 2 else 1 - sub
            which = fit if index % 2 == 0 else 1 - fit
            for who in range(z.owners):
                one(
                    who * z.own + side * z.pairs + which,
                    lambda start, size: ref[who, start : start + size, :],
                    index * z.owners + who,
                )
    else:
        each_pair(
            z, lambda pair: one(pair, lambda start, size: packs[0][pair, pl.ds(start, size), :], 0)
        )


def coupled_of(z, index, pair, near, s, coupling, amps_high, amps_low, diag_high, diag_low):
    n = z.pnos
    for k in range(z.links):
        row = near[pair, k]
        block = slice(k * n, (k + 1) * n)
        diag_high[index, block, block] = amps_high[row]
        diag_low[index, block, block] = amps_low[row]
    return split(mm3(s, (diag_high[index], diag_low[index])) * coupling)


def final_kernel(z, first, second, near, *refs):
    start_count = 2 if small(z) else 1
    starts = refs[:start_count]
    s_high, s_low, scale_ref, coupling_ref = refs[start_count : start_count + 4]
    (c_in, c_other, mp_in, mp_other, mp_below, mp_below_other, left_in, left_other, left_below,
     left_below_other, right_in, right_other) = refs[start_count + 4 : start_count + 16]
    (amp_ref, grad_out, c_ref, m_ref, rhs, grad, flat, amps, amps_high, amps_low, next_high,
     next_low, diag_high, diag_low, rows_high, rows_low, sems) = refs[start_count + 16 :]
    owner, sub = lax.axis_index("orb"), lax.axis_index("sub")
    n, pairs, own = z.pnos, z.pairs, z.own
    half = z.paos // z.subs
    at = pl.ds(pl.multiple_of(sub * half, half), half)

    def quarters(ref, base=0):
        return [ref.at[pl.ds(base + i * pairs, pairs)] for i in range(4)]

    small_copies = started(
        [c_in.at[:, :, at], c_other.at[:, :, at]]
        + [ref.at[:, pl.ds(0, n), at] for ref in (mp_in, mp_other, mp_below, mp_below_other)],
        [c_ref.at[pl.ds(0, pairs)], c_ref.at[pl.ds(pairs, pairs)]] + quarters(m_ref),
        sems,
    )
    large_copies = started(
        [right_in, right_other, left_in, left_other, left_below, left_below_other],
        [rhs.at[pl.ds(0, pairs)], rhs.at[pl.ds(pairs, pairs)]] + quarters(rhs, own),
        sems, 6,
    )
    diag_high[...] = jnp.zeros_like(diag_high)
    diag_low[...] = jnp.zeros_like(diag_low)

    def begin(pair, value):
        amps[pair] = value
        amps_high[pair], amps_low[pair] = split(value)

    if small(z):
        for side, ref in ((sub, starts[0]), (1 - sub, starts[1])):
            for who in range(z.owners):
                for p in range(pairs):
                    begin(who * own + side * pairs + p, ref[who, :, p * n : (p + 1) * n])
    else:
        @pl.loop(0, z.owners * z.subs)
        def _(device):
            for p in range(pairs):
                begin(device * pairs + p, starts[0][device, :, p * n : (p + 1) * n])

    def s_of(pair):
        return s_high[pair], s_low[pair]

    def swept(index, pair, high_amps, low_amps):
        s = s_of(pair)
        inner = coupled_of(
            z, index, pair, near, s, coupling_ref[pair, 0:1, :], high_amps, low_amps, diag_high,
            diag_low,
        )
        return amps[pair] + mm3(inner, s, ((1,), (1,))) * scale_ref[pair]

    if z.owners <= SMALL:
        group = diag_high.shape[0]
        for base in range(0, z.total, group):
            pair_list = range(base, min(base + group, z.total))
            inner = [
                coupled_of(
                    z, index, pair, near, s_of(pair), coupling_ref[pair, 0:1, :], amps_high,
                    amps_low, diag_high, diag_low,
                )
                for index, pair in enumerate(pair_list)
            ]
            for value, pair in zip(inner, pair_list):
                coupled = mm3(value, s_of(pair), ((1,), (1,)))
                next_high[pair], next_low[pair] = split(amps[pair] + coupled * scale_ref[pair])
    else:
        @pl.loop(0, z.total)
        def _(pair):
            next_high[pair], next_low[pair] = split(swept(0, pair, amps_high, amps_low))

    pair_list = [
        side_start(z, who, sub, side) + p
        for who in (owner, jnp.maximum(owner - 1, 0))
        for side in range(z.subs)
        for p in range(pairs)
    ]
    inner = [
        coupled_of(
            z, index, pair, near, s_of(pair), coupling_ref[pair, 0:1, :], next_high, next_low,
            diag_high, diag_low,
        )
        for index, pair in enumerate(pair_list)
    ]
    found = [
        amps[pair] + mm3(value, s_of(pair), ((1,), (1,))) * scale_ref[pair]
        for value, pair in zip(inner, pair_list)
    ]
    turned = [value.T for value in found]
    wait(small_copies)
    weights = [split(2.0 * a - b) for a, b in zip(found, turned)]
    weights_turned = [split(2.0 * b - a) for a, b in zip(found[:own], turned[:own])]
    terms = (
        [mm3(w, split(c_ref[i])) for i, w in enumerate(weights_turned)]
        + [mm3(w, split(m_ref[i])) for i, w in enumerate(weights)]
    )
    orbital_list = (
        [first[pair] - owner * z.orbitals for pair in pair_list[:own]]
        + [second[pair] - owner * z.orbitals for pair in pair_list]
    )
    for index in range(0, 3 * own, 2):
        for o in range(z.orbitals):
            block = jnp.concatenate(
                [
                    jnp.where(orbital_list[i] == o, terms[i], 0.0) for i in (index, index + 1)
                ]
            ).T
            place = (slice(o * half, (o + 1) * half), slice(index * n, (index + 2) * n))
            rows_high[place], rows_low[place] = split(block)

    for p in range(pairs):
        flat[p] = found[p]
        even = flat[p, pl.ds(0, n // 2, 2), :]
        odd = flat[p, pl.ds(1, n // 2, 2), :]
        lines = jnp.concatenate([even, odd], axis=1)
        for r in range(n // 2):
            amp_ref[p : p + 1, r * 2 * n : (r + 1) * 2 * n] = lines[r : r + 1, :]

    wait(large_copies)
    step = 256
    rows = (rows_high[...], rows_low[...])
    copies = []
    for index, start in enumerate(range(0, z.fits, step)):
        factor = rhs[:, :, start : start + step].reshape(3 * own * n, step)
        grad[:, :, start : start + step] = mm3(rows, split(factor)).reshape(
            z.orbitals, half, step
        )
        window = pl.ds(start, step)
        copies += started(
            [grad.at[:, :, window]], [grad_out.at[:, :, window]], sems, 12 + index
        )
    wait(copies)


def gate(values, *after):
    return lax.optimization_barrier((tuple(values), after))[0]


def body(
    blocks,
    pno_coefficients,
    domain_map,
    pair_first,
    pair_second,
    pno_ranks,
    neighbours,
    couplings,
    intersections,
    pno_energy,
    occ_energy,
):
    z = Sizes(blocks, pno_coefficients, couplings)
    n, pairs, own, fits = z.pnos, z.pairs, z.own, z.fits
    half = z.paos // z.subs
    wide = z.links * n
    hbm = held_out
    bf16 = jnp.bfloat16
    more = 0 if z.owners <= SMALL else z.owners

    def scratch(*shape, kind=jnp.float32):
        return pltpu.VMEM(shape, kind)

    (mp,) = call(
        functools.partial(mapped_kernel, z),
        [(pairs, n + EXTRA, z.paos)],
        [hbm] * 4,
        (pno_coefficients, domain_map, pno_energy, couplings),
        [
            scratch(*pno_coefficients.shape),
            pltpu.VMEM(domain_map.shape, jnp.int32),
            scratch(*pno_energy.shape),
            scratch(*couplings.shape),
            pltpu.SemaphoreType.DMA((4,)),
        ],
        limit=None,
    )
    mp_below = shifted(mp, "orb", 1)
    pack_shape = (z.owners if small(z) else pairs, z.links * n // 2 + EXTRA, 2 * n)
    (pack,) = call(
        functools.partial(pack_kernel, z),
        [pack_shape],
        [vmem, vmem, anywhere],
        (intersections, mp, mp),
        limit=8,
    )
    if small(z):
        packs = [lax.all_to_all(pack, "orb", 0, 0)]
    else:
        packs = [lax.all_gather(pack, ("orb", "sub"), axis=0, tiled=True)]
    (right_below,) = call(
        functools.partial(below_kernel, z),
        [(pairs, n, fits)],
        [smem, vmem, vmem, anywhere],
        (pair_second, mp_below, blocks, pack),
        limit=8,
    )
    down = shifted(right_below, "orb", -1)
    (coefficients,) = gate((pno_coefficients,), right_below)
    (left,) = call(
        functools.partial(left_kernel, z),
        [(pairs, n, fits)],
        [smem, vmem, vmem],
        (pair_first, coefficients, blocks),
        limit=8,
    )
    (right_here,) = call(
        functools.partial(here_kernel, z),
        [(pairs, n, fits)],
        [smem, vmem, vmem, anywhere],
        (pair_second, mp, blocks, left),
        limit=8,
    )
    left_late, mp_late, coefficients = gate((left, mp, coefficients), right_here)
    left_below = shifted(left_late, "orb", 1)
    mp_other = swapped(mp_late, "sub")
    left_other = swapped(left_late, "sub")
    c_other = swapped(coefficients, "sub")
    if small(z):
        packs.append(swapped(gate(packs, right_here)[0], "fit"))

    lists = (pair_first, pair_second, pno_ranks)
    part, right = call(
        functools.partial(sums_kernel, z),
        [(n, pairs * n), (pairs, n, fits)],
        [smem] * 4 + [vmem] * 4 + [anywhere] * 3,
        (*lists, occ_energy, mp, left, right_here, down, left_other, mp_other, c_other),
        limit=8,
    )
    if small(z):
        packs += [swapped(value, "sub") for value in gate(packs, part)]
        sums = part + swapped(part, "fit")
        start_amps = [
            lax.all_to_all(jnp.broadcast_to(sums[None], (z.owners, *sums.shape)), "orb", 0, 0)
        ]
        start_amps.append(swapped(start_amps[0], "sub"))
    else:
        sums = lax.psum(part, "fit")
        start_amps = [lax.all_gather(sums, ("orb", "sub"), axis=0, tiled=False)]

    right_late, mp_late = gate((right, mp_below), part)
    (left_late,) = gate((left_below,), sums)
    right_other, mp_below_other, left_below_other = [
        swapped(value, "sub") for value in (right_late, mp_late, left_late)
    ]

    split_shape = jax.ShapeDtypeStruct((z.total, n, wide), bf16)
    unpacked = pl.pallas_call(
        functools.partial(unpack_kernel, z),
        out_shape=[
            split_shape,
            split_shape,
            jax.ShapeDtypeStruct((z.total, n, n), jnp.float32),
            jax.ShapeDtypeStruct((z.total, EXTRA, wide), jnp.float32),
        ],
        in_specs=[smem] * 4 + [vmem] * len(packs),
        out_specs=[vmem] * 4,
        scratch_shapes=[scratch(z.total if small(z) else 1, z.links // 2, n, 2 * n)],
        compiler_params=pltpu.CompilerParams(vmem_limit_bytes=(16 + more) * MIB),
    )(*lists, occ_energy, *packs)

    args = (
        pair_first, pair_second, neighbours, *start_amps, *unpacked,
        pno_coefficients, c_other, mp, mp_other, mp_below, mp_below_other,
        left, left_other, left_below, left_below_other, right, right_other,
    )
    group = own * 2
    square = (z.total, n, n)
    amplitudes, gradient = call(
        functools.partial(final_kernel, z),
        [(pairs, n * n), (z.orbitals, half, fits)],
        [smem] * 3 + [vmem] * (len(start_amps) + 4) + [hbm] * 12,
        args,
        [
            scratch(own, n, half),
            scratch(2 * own, n, half),
            scratch(3 * own, n, fits),
            scratch(z.orbitals, half, fits),
            scratch(pairs, n, n),
            scratch(*square),
        ]
        + [scratch(*square, kind=bf16)] * 4
        + [scratch(group, wide, wide, kind=bf16)] * 2
        + [scratch(z.orbitals * half, 3 * own * n, kind=bf16)] * 2
        + [pltpu.SemaphoreType.DMA((12 + -(-fits // 256),))],
        limit=40 + more // 2,
        out_specs=[vmem, hbm],
    )
    return (amplitudes, gradient)


def solution(mesh):
    in_specs = (
        P(("groups", "orb"), None, "fit"),
        P(("groups", "orb", "sub"), None, None),
        P(("groups", "orb", "sub"), None),
        P("groups"),
        P("groups"),
        P("groups"),
        P("groups", None),
        P(("groups", "orb", "sub"), None),
        P(("groups", "orb", "sub"), None, None),
        P(("groups", "orb", "sub"), None),
        P("groups"),
    )
    out_specs = (P(("groups", "orb", "sub"), None), P(("groups", "orb"), "sub", "fit"))
    return jax.shard_map(body, mesh=mesh, in_specs=in_specs, out_specs=out_specs, check_vma=False)
```

time: 83 us -> 66.7 us (0.80)
  waiting for transfers between devices: 34.1 us -> 16.9 us
  local copies, waits for them, and re-layouts: 11.1 us -> 6.77 us
  Pallas kernels: 14.8 us -> 18 us
  starting transfers between devices: 21.4 us -> 23.5 us
    all_to_all x2, waiting for transfers between devices: 15.8 us -> 5.86 us  [the longest x1 5.86 us: body(): lax.all_to_all(jnp.broadcast_to(sums[None], (z.owners, *sums.shape)), 'or...]
    ppermute x3, waiting for transfers between devices: 13.3 us -> 7.67 us  [shifted(): lax.ppermute(value, axis, [(source, source + steps) for source in range(i...]
    unnamed x59 -> x29, local copies, waits for them, and re-layouts: 9.64 us -> 6.1 us
    ppermute x7 -> x11, starting transfers between devices: 2.99 us -> 4.83 us  [swapped(): return lax.ppermute(value, axis, [(0, 1), (1, 0)])]
    pallas_call x0 -> x1, Pallas kernels: none -> 1.66 us  [body(): pl.pallas_call(functools.partial(unpack_kernel, z), out_shape=[split_shap...]
    ppermute x7 -> x11, waiting for transfers between devices: 5.03 us -> 3.41 us  [swapped(): return lax.ppermute(value, axis, [(0, 1), (1, 0)])]
    pallas_call x7, Pallas kernels: 14.8 us -> 16.3 us  [call(): pl.pallas_call(kernel, out_shape=[jax.ShapeDtypeStruct(shape, jnp.float32...]
    all_to_all x2, starting transfers between devices: 6.83 us -> 7.81 us  [the longest x1 3.95 us: body(): lax.all_to_all(jnp.broadcast_to(sums[None], (z.owners, *sums.shape)), 'or...]
  transfers between devices with their start and end apart: 12 -> 16, of which waited for: 8 -> 4; matrix products, arithmetic and copies ran while one was open for 2% -> 1% of each run, Pallas kernels for 5% -> 12%
where the time goes in v5:
time: 66.7 us; the launch traced here: 66 us
  starting transfers between devices  23.5 us (35%)
  Pallas kernels  18 us (27%)
  waiting for transfers between devices  16.9 us (25%)
  local copies, waits for them, and re-layouts  6.77 us (10%)
  between operations  0.86 us (1%)
    pallas_call x7, Pallas kernels, call(): pl.pallas_call(kernel, out_shape=[jax.ShapeDtypeStruct(shape, jnp.float32...  16.3 us
    ppermute x3, starting transfers between devices, shifted(): lax.ppermute(value, axis, [(source, source + steps) for source in range(i...  10.8 us
    ppermute x3, waiting for transfers between devices, shifted(): lax.ppermute(value, axis, [(source, source + steps) for source in range(i...  7.67 us
    unnamed x29, local copies, waits for them, and re-layouts  6.1 us
    all_to_all x1, waiting for transfers between devices, body(): lax.all_to_all(jnp.broadcast_to(sums[None], (z.owners, *sums.shape)), 'or...  5.86 us
    ppermute x11, starting transfers between devices, swapped(): return lax.ppermute(value, axis, [(0, 1), (1, 0)])  4.83 us
    all_to_all x1, starting transfers between devices, body(): lax.all_to_all(jnp.broadcast_to(sums[None], (z.owners, *sums.shape)), 'or...  3.95 us
    all_to_all x1, starting transfers between devices, body(): packs = [lax.all_to_all(pack, 'orb', 0, 0)]  3.86 us
  transfers between devices with their start and end apart: 16, of which 4 were waited for; matrix products, arithmetic and copies ran while one was open for 1% of the time, Pallas kernels for 12%

profile of v5, /device:TPU:0, one launch (start us, length us, event | category | flops | bytes accessed | tf_op | source)
XLA Modules:
  0.0 66.0 jit_solution(5674801172433162730)
XLA Ops:
  0.6 1.9 %shard_map.122.mp_ref.order.refs_8_ = f32[2,72,256]{2,1,0:T(8,128)} custom-call(f32[2,64,256]{2,1,0:T(8,128)} %refs_6_.1, s32[2,256]{1,0:T(2,128)} %map_in.1, f32[2,64]{1,0:T(2,128)} %e_in.1, f32[2,4]{1,0:T(2,128)} %coupling_in.1), custom_call_target="tpu_custom_call" | custom-call | tf_op jit(solution)/shard_map/pallas_call | solution.py:57
  2.5 4.9 %collective-permute-start = (f32[2,72,256]{2,1,0:T(8,128)}, f32[2,72,256]{2,1,0:T(8,128)S(1)}, u32[]{:S(2)}, u32[]{:S(2)}) collective-permute-start(f32[2,72,256]{2,1,0:T(8,128)} %shard_map.122.mp_ref.order.refs_8_), channel_id=1, source_target_pairs={{0,4},{4,8},{8,12},{1,5},{5,9},{9,13},{2,6},{6,10},{10,14},{3,7},{... | collective-permute-start | bytes 442376 | tf_op jit(solution)/shard_map/ppermute | solution.py:29
  7.5 0.9 %copy-done.2 = f32[2,72,256]{2,1,0:T(8,128)S(1)} copy-done((f32[2,72,256]{2,1,0:T(8,128)S(1)}, f32[2,72,256]{2,1,0:T(8,128)}, u32[]{:S(2)}) %copy-start.2) | copy-done | bytes 147480
  8.4 0.9 %copy-done.7 = f32[2,4,4096]{2,1,0:T(4,128)S(1)} copy-done((f32[2,4,4096]{2,1,0:T(4,128)S(1)}, f32[2,4,4096]{2,1,0:T(4,128)}, u32[]{:S(2)}) %copy-start.7) | copy-done | bytes 131096
  9.3 0.8 %shard_map.123.order = f32[4,136,128]{2,1,0:T(8,128)} custom-call(f32[2,4,4096]{2,1,0:T(4,128)S(1)} %copy-done.7, f32[2,72,256]{2,1,0:T(8,128)S(1)} %copy-done.2, f32[2,72,256]{2,1,0:T(8,128)S(1)} %copy-done.2), custom_call_target="tpu_custom_call" | custom-call | tf_op jit(solution)/shard_map/pallas_call | solution.py:57
  10.1 3.9 %all-to-all-start.1 = ((f32[4,136,128]{2,1,0:T(8,128)}), f32[4,136,128]{2,1,0:T(8,128)S(1)}, u32[]{:S(2)}, u32[]{:S(2)}) async-start(f32[4,136,128]{2,1,0:T(8,128)} %shard_map.123.order), calls=%async_computation.1 | async-start | bytes 557056 | tf_op jit(solution)/shard_map/all_to_all | solution.py:451
  13.9 0.0 collective-permute-done.mp_below.refs_10_
  13.9 1.6 %copy-done = f32[2,256,1024]{2,1,0:T(8,128)S(1)} copy-done((f32[2,256,1024]{2,1,0:T(8,128)S(1)}, f32[2,256,1024]{2,1,0:T(8,128)}, u32[]{:S(2)}) %copy-start) | copy-done | bytes 2097176
  15.5 0.7 copy-done.8
  16.2 1.3 %shard_map.124 = f32[2,64,1024]{2,1,0:T(8,128)S(1)} custom-call(s32[16]{0:T(128)S(1)} %copy-done.8, f32[2,72,256]{2,1,0:T(8,128)S(1)} %collective-permute-done.mp_below.refs_10_, f32[2,256,1024]{2,1,0:T(8,128)S(1)} %copy-done, f32[4,136,128]{2,1,0:T(8,128)} %shard_map.123.order), custom_call_target="tpu_custom_call" | custom-call | tf_op jit(solution)/shard_map/pallas_call | solution.py:57
  17.5 0.3 copy-done.1
  17.8 1.3 %shard_map.125.order.left_ref.refs_12_ = f32[2,64,1024]{2,1,0:T(8,128)S(1)} custom-call(s32[16]{0:T(128)S(1)} %copy-done.10, f32[2,64,256]{2,1,0:T(8,128)S(1)} %copy-done.4, f32[2,256,1024]{2,1,0:T(8,128)S(1)} %copy-done.1), custom_call_target="tpu_custom_call" | custom-call | tf_op jit(solution)/shard_map/pallas_call | solution.py:57
  19.1 0.0 copy-start.11
  19.1 0.0 copy-start.12
  19.1 1.3 %shard_map.126.here_ref = f32[2,64,1024]{2,1,0:T(8,128)S(1)} custom-call(s32[16]{0:T(128)S(1)} %copy-done.9, f32[2,72,256]{2,1,0:T(8,128)S(1)} %copy-done.3, f32[2,256,1024]{2,1,0:T(8,128)S(1)} %copy-done.1, f32[2,64,1024]{2,1,0:T(8,128)S(1)} %shard_map.125.order.left_ref.refs_12_), custom_call_target="tpu_custom_call" | custom-call | tf_op jit(solution)/shard_map/pallas_call | solution.py:57
  20.4 0.0 copy-start.13
  20.4 0.1 collective-permute-start.2
  20.5 1.3 %collective-permute-start.1 = (f32[2,64,1024]{2,1,0:T(8,128)S(1)}, f32[2,64,1024]{2,1,0:T(8,128)}, u32[]{:S(2)}, u32[]{:S(2)}) collective-permute-start(f32[2,64,1024]{2,1,0:T(8,128)S(1)} %shard_map.124), channel_id=1, source_target_pairs={{4,0},{8,4},{12,8},{5,1},{9,5},{13,9},{6,2},{10,6},{14,10},{7,3},{... | collective-permute-start | bytes 1572872 | tf_op jit(solution)/shard_map/ppermute | solution.py:29
  21.8 4.6 %collective-permute-start.11 = (f32[2,64,1024]{2,1,0:T(8,128)S(1)}, f32[2,64,1024]{2,1,0:T(8,128)S(1)}, u32[]{:S(2)}, u32[]{:S(2)}) collective-permute-start(f32[2,64,1024]{2,1,0:T(8,128)S(1)} %shard_map.125.order.left_ref.refs_12_), channel_id=1, source_target_pairs={{0,4},{4,8},{8,12},{1,5},{5,9},{9,13},{2,6},{6,10},{10,14},{3,7},{... | collective-permute-start | bytes 1572872 | tf_op jit(solution)/shard_map/ppermute | solution.py:29
  26.4 0.3 collective-permute-start.4
  26.6 0.3 collective-permute-start.3
  26.9 1.0 %collective-permute-done.4.refs_2_.refs_7_ = f32[2,64,256]{2,1,0:T(8,128)} collective-permute-done((f32[2,64,256]{2,1,0:T(8,128)S(1)}, f32[2,64,256]{2,1,0:T(8,128)}, u32[]{:S(2)}, u32[]{:S(2)}) %collective-permute-start.4) | collective-permute-done | bytes 131104 | tf_op jit(solution)/shard_map/ppermute | solution.py:33
  27.9 1.5 %collective-permute-start.7 = (f32[4,136,128]{2,1,0:T(8,128)S(1)}, f32[4,136,128]{2,1,0:T(8,128)S(1)}, u32[]{:S(2)}, u32[]{:S(2)}) collective-permute-start(f32[4,136,128]{2,1,0:T(8,128)S(1)} %all-to-all-done.1.refs_0_), channel_id=1, source_target_pairs={{0,2},{2,0},{1,3},{3,1},{4,6},{6,4},{5,7},{7,5},{8,10},{10,8},{9,1... | collective-permute-start | bytes 835592 | tf_op jit(solution)/shard_map/ppermute | solution.py:33
  29.4 0.0 collective-permute-done.3.refs_1_.refs_9_
  29.4 0.0 collective-permute-done.2.refs_0_.refs_13_
  29.4 7.7 %collective-permute-done.1.down_ref = f32[2,64,1024]{2,1,0:T(8,128)} collective-permute-done((f32[2,64,1024]{2,1,0:T(8,128)S(1)}, f32[2,64,1024]{2,1,0:T(8,128)}, u32[]{:S(2)}, u32[]{:S(2)}) %collective-permute-start.1) | collective-permute-done | bytes 524320 | tf_op jit(solution)/shard_map/ppermute | solution.py:29
  37.1 1.5 %shard_map.127 = (f32[64,128]{1,0:T(8,128)S(1)}, f32[2,64,1024]{2,1,0:T(8,128)S(1)}) custom-call(s32[16]{0:T(128)S(1)} %copy-done.10, s32[16]{0:T(128)S(1)} %copy-done.9, s32[16]{0:T(128)S(1)} %copy-done.11, f32[8]{0:T(128)S(1)} %copy-done.12, f32[2,72,256]{2,1,0:T(8,128)S(1)} %copy-done.3, f32[2,64,1024]{2,1,0:T(8,128)S(1)} %shard_map.125.order.left_ref.refs_12_, ...), custom_call_target="tpu_custom_call" | custom-call | tf_op jit(solution)/shard_map/pallas_call | solution.py:57
  38.6 1.6 %collective-permute-start.5 = (f32[64,128]{1,0:T(8,128)S(1)}, f32[64,128]{1,0:T(8,128)S(1)}, u32[]{:S(2)}, u32[]{:S(2)}) collective-permute-start(f32[64,128]{1,0:T(8,128)S(1)} %get-tuple-element.22), channel_id=1, source_target_pairs={{0,2},{2,0},{1,3},{3,1},{4,6},{6,4},{5,7},{7,5},{8,10},{10,8},{9,1... | collective-permute-start | bytes 98312 | tf_op jit(solution)/shard_map/ppermute | solution.py:33
  40.1 0.0 collective-permute-start.13
  40.1 2.4 %collective-permute-done.5 = f32[64,128]{1,0:T(8,128)S(1)} collective-permute-done((f32[64,128]{1,0:T(8,128)S(1)}, f32[64,128]{1,0:T(8,128)S(1)}, u32[]{:S(2)}, u32[]{:S(2)}) %collective-permute-start.5) | collective-permute-done | bytes 32800 | tf_op jit(solution)/shard_map/ppermute | solution.py:33
  42.6 0.0 collective-permute-done.11.refs_14_
  42.6 0.1 collective-permute-start.12
  42.6 0.0 collective-permute-done.7.refs_1_
  42.7 0.0 copy-start.5
  42.7 0.7 %copy-done.5 = f32[4,136,128]{2,1,0:T(8,128)} copy-done((f32[4,136,128]{2,1,0:T(8,128)}, f32[4,136,128]{2,1,0:T(8,128)S(1)}, u32[]{:S(2)}) %copy-start.5) | copy-done | bytes 278552
  43.4 0.5 collective-permute-start.8
  43.9 0.7 %broadcast_in_dim.2 = f32[4,64,128]{2,1,0:T(8,128)} broadcast(f32[64,128]{1,0:T(8,128)S(1)} %add.3), dimensions={1,2} | broadcast | bytes 163840 | tf_op jit(solution)/shard_map/broadcast_in_dim | solution.py:497
  44.5 4.0 %all-to-all-start = ((f32[4,64,128]{2,1,0:T(8,128)}), f32[4,64,128]{2,1,0:T(8,128)}, u32[]{:S(2)}, u32[]{:S(2)}) async-start(f32[4,64,128]{2,1,0:T(8,128)} %broadcast_in_dim.2), calls=%async_computation | async-start | bytes 262144 | tf_op jit(solution)/shard_map/all_to_all | solution.py:497
  48.5 0.1 collective-permute-start.9
  48.6 0.5 collective-permute-start.10
  49.1 5.9 %all-to-all-done.refs_0_ = f32[4,64,128]{2,1,0:T(8,128)} async-done(((f32[4,64,128]{2,1,0:T(8,128)}), f32[4,64,128]{2,1,0:T(8,128)}, u32[]{:S(2)}, u32[]{:S(2)}) %all-to-all-start) | async-done | bytes 131104 | tf_op jit(solution)/shard_map/all_to_all | solution.py:497
  54.9 0.0 collective-permute-done.8.refs_2_
  54.9 0.0 collective-permute-start.6
  54.9 0.1 copy.13.near
  55.0 0.0 collective-permute-done.9.refs_3_
  55.0 1.0 %copy-done.6 = f32[4,136,128]{2,1,0:T(8,128)S(1)} copy-done((f32[4,136,128]{2,1,0:T(8,128)S(1)}, f32[4,136,128]{2,1,0:T(8,128)}, u32[]{:S(2)}) %copy-start.6) | copy-done | bytes 278552
  56.0 1.7 %shard_map.128 = (bf16[16,64,256]{2,1,0:T(8,128)(2,1)S(1)}, bf16[16,64,256]{2,1,0:T(8,128)(2,1)S(1)}, f32[16,64,64]{2,1,0:T(8,128)S(1)}, f32[16,8,256]{2,1,0:T(8,128)S(1)}) custom-call(s32[16]{0:T(128)S(1)} %copy-done.10, s32[16]{0:T(128)S(1)} %copy-done.9, s32[16]{0:T(128)S(1)} %copy-done.11, f32[8]{0:T(128)S(1)} %copy-done.12, ...), custom_call_target="tpu_custom_call" | custom-call | tf_op jit(solution)/shard_map/pallas_call | solution.py:511
  57.7 8.3 %shard_map.129 = (f32[2,4096]{1,0:T(2,128)}, f32[2,128,1024]{2,1,0:T(8,128)}) custom-call(s32[16]{0:T(128)S(1)} %copy-done.10, s32[16]{0:T(128)S(1)} %copy-done.9, s32[16,4]{1,0:T(8,128)S(1)} %copy.13.near, f32[4,64,128]{2,1,0:T(8,128)} %all-to-all-done.refs_0_, f32[4,64,128]{2,1,0:T(8,128)} %collective-permute-done.6.refs_1_, ...), custom_call_target="tpu_custom_call" | custom-call | tf_op jit(solution)/shard_map/pallas_call | solution.py:57
  (23 shorter events, 0.0 us)
Async XLA Ops:
  2.5 11.4 %collective-permute-start = (f32[2,72,256]{2,1,0:T(8,128)}, f32[2,72,256]{2,1,0:T(8,128)S(1)}, u32[]{:S(2)}, u32[]{:S(2)}) collective-permute-start(f32[2,72,256]{2,1,0:T(8,128)} %shard_map.122.mp_ref.order.refs_8_), channel_id=1, source_target_pairs={{0,4},{4,8},{8,12},{1,5},{5,9},{9,13},{2,6},{6,10},{10,14},{3,7},{... | collective-permute-start | bytes 442376 | tf_op jit(solution)/shard_map/ppermute | solution.py:29
  7.5 0.9 %copy-start.2 = (f32[2,72,256]{2,1,0:T(8,128)S(1)}, f32[2,72,256]{2,1,0:T(8,128)}, u32[]{:S(2)}) copy-start(f32[2,72,256]{2,1,0:T(8,128)} %shard_map.122.mp_ref.order.refs_8_) | copy-start | bytes 442372
  8.4 0.9 %copy-start.7 = (f32[2,4,4096]{2,1,0:T(4,128)S(1)}, f32[2,4,4096]{2,1,0:T(4,128)}, u32[]{:S(2)}) copy-start(f32[2,4,4096]{2,1,0:T(4,128)} %s_ref.1) | copy-start | bytes 393220
  9.3 8.2 %copy-start.4 = (f32[2,64,256]{2,1,0:T(8,128)S(1)}, f32[2,64,256]{2,1,0:T(8,128)}, u32[]{:S(2)}) copy-start(f32[2,64,256]{2,1,0:T(8,128)} %refs_6_.1) | copy-start | bytes 393220
  9.3 8.2 %copy-start.10 = (s32[16]{0:T(128)S(1)}, s32[16]{0:T(128)}, u32[]{:S(2)}) copy-start(s32[16]{0:T(128)} %first.7) | copy-start | bytes 196
  10.1 16.9 %all-to-all-start.1 = ((f32[4,136,128]{2,1,0:T(8,128)}), f32[4,136,128]{2,1,0:T(8,128)S(1)}, u32[]{:S(2)}, u32[]{:S(2)}) async-start(f32[4,136,128]{2,1,0:T(8,128)} %shard_map.123.order), calls=%async_computation.1 | async-start | bytes 557056 | tf_op jit(solution)/shard_map/all_to_all | solution.py:451
  13.9 1.6 %copy-start = (f32[2,256,1024]{2,1,0:T(8,128)S(1)}, f32[2,256,1024]{2,1,0:T(8,128)}, u32[]{:S(2)}) copy-start(f32[2,256,1024]{2,1,0:T(8,128)} %b_ref.5) | copy-start | bytes 6291460
  15.5 0.7 copy-start.8
  16.2 1.6 %copy-start.1 = (f32[2,256,1024]{2,1,0:T(8,128)S(1)}, f32[2,256,1024]{2,1,0:T(8,128)}, u32[]{:S(2)}) copy-start(f32[2,256,1024]{2,1,0:T(8,128)} %b_ref.5) | copy-start | bytes 6291460
  17.8 1.3 %copy-start.3 = (f32[2,72,256]{2,1,0:T(8,128)S(1)}, f32[2,72,256]{2,1,0:T(8,128)}, u32[]{:S(2)}) copy-start(f32[2,72,256]{2,1,0:T(8,128)} %shard_map.122.mp_ref.order.refs_8_) | copy-start | bytes 442372
  17.8 1.3 %copy-start.9 = (s32[16]{0:T(128)S(1)}, s32[16]{0:T(128)}, u32[]{:S(2)}) copy-start(s32[16]{0:T(128)} %second.9) | copy-start | bytes 196
  19.1 18.0 %copy-start.11 = (s32[16]{0:T(128)S(1)}, s32[16]{0:T(128)}, u32[]{:S(2)}) copy-start(s32[16]{0:T(128)} %ranks.3) | copy-start | bytes 196
  19.1 18.0 %copy-start.12 = (f32[8]{0:T(128)S(1)}, f32[8]{0:T(128)}, u32[]{:S(2)}) copy-start(f32[8]{0:T(128)} %occupied.3) | copy-start | bytes 100
  20.4 34.6 %copy-start.13 = (s32[16,4]{0,1:T(4,128)S(1)}, s32[16,4]{0,1:T(4,128)}, u32[]{:S(2)}) copy-start(s32[16,4]{0,1:T(4,128)} %param.17) | copy-start | bytes 772
  20.4 9.0 %collective-permute-start.2 = (f32[2,64,1024]{2,1,0:T(8,128)S(1)}, f32[2,64,1024]{2,1,0:T(8,128)S(1)}, u32[]{:S(2)}, u32[]{:S(2)}) collective-permute-start(f32[2,64,1024]{2,1,0:T(8,128)S(1)} %shard_map.125.order.left_ref.refs_12_), channel_id=1, source_target_pairs={{0,1},{1,0},{2,3},{3,2},{4,5},{5,4},{6,7},{7,6},{8,9},{9,8},{10,11... | collective-permute-start | bytes 1572872 | tf_op jit(solution)/shard_map/ppermute | solution.py:33
  20.5 16.6 %collective-permute-start.1 = (f32[2,64,1024]{2,1,0:T(8,128)S(1)}, f32[2,64,1024]{2,1,0:T(8,128)}, u32[]{:S(2)}, u32[]{:S(2)}) collective-permute-start(f32[2,64,1024]{2,1,0:T(8,128)S(1)} %shard_map.124), channel_id=1, source_target_pairs={{4,0},{8,4},{12,8},{5,1},{9,5},{13,9},{6,2},{10,6},{14,10},{7,3},{... | collective-permute-start | bytes 1572872 | tf_op jit(solution)/shard_map/ppermute | solution.py:29
  21.8 20.8 %collective-permute-start.11 = (f32[2,64,1024]{2,1,0:T(8,128)S(1)}, f32[2,64,1024]{2,1,0:T(8,128)S(1)}, u32[]{:S(2)}, u32[]{:S(2)}) collective-permute-start(f32[2,64,1024]{2,1,0:T(8,128)S(1)} %shard_map.125.order.left_ref.refs_12_), channel_id=1, source_target_pairs={{0,4},{4,8},{8,12},{1,5},{5,9},{9,13},{2,6},{6,10},{10,14},{3,7},{... | collective-permute-start | bytes 1572872 | tf_op jit(solution)/shard_map/ppermute | solution.py:29
  26.4 1.5 %collective-permute-start.4 = (f32[2,64,256]{2,1,0:T(8,128)S(1)}, f32[2,64,256]{2,1,0:T(8,128)}, u32[]{:S(2)}, u32[]{:S(2)}) collective-permute-start(f32[2,64,256]{2,1,0:T(8,128)S(1)} %copy-done.4), channel_id=1, source_target_pairs={{0,1},{1,0},{2,3},{3,2},{4,5},{5,4},{6,7},{7,6},{8,9},{9,8},{10,11... | collective-permute-start | bytes 393224 | tf_op jit(solution)/shard_map/ppermute | solution.py:33
  26.6 2.8 %collective-permute-start.3 = (f32[2,72,256]{2,1,0:T(8,128)S(1)}, f32[2,72,256]{2,1,0:T(8,128)S(1)}, u32[]{:S(2)}, u32[]{:S(2)}) collective-permute-start(f32[2,72,256]{2,1,0:T(8,128)S(1)} %copy-done.3), channel_id=1, source_target_pairs={{0,1},{1,0},{2,3},{3,2},{4,5},{5,4},{6,7},{7,6},{8,9},{9,8},{10,11... | collective-permute-start | bytes 442376 | tf_op jit(solution)/shard_map/ppermute | solution.py:33
  27.9 14.7 %collective-permute-start.7 = (f32[4,136,128]{2,1,0:T(8,128)S(1)}, f32[4,136,128]{2,1,0:T(8,128)S(1)}, u32[]{:S(2)}, u32[]{:S(2)}) collective-permute-start(f32[4,136,128]{2,1,0:T(8,128)S(1)} %all-to-all-done.1.refs_0_), channel_id=1, source_target_pairs={{0,2},{2,0},{1,3},{3,1},{4,6},{6,4},{5,7},{7,5},{8,10},{10,8},{9,1... | collective-permute-start | bytes 835592 | tf_op jit(solution)/shard_map/ppermute | solution.py:33
  38.6 4.0 %collective-permute-start.5 = (f32[64,128]{1,0:T(8,128)S(1)}, f32[64,128]{1,0:T(8,128)S(1)}, u32[]{:S(2)}, u32[]{:S(2)}) collective-permute-start(f32[64,128]{1,0:T(8,128)S(1)} %get-tuple-element.22), channel_id=1, source_target_pairs={{0,2},{2,0},{1,3},{3,1},{4,6},{6,4},{5,7},{7,5},{8,10},{10,8},{9,1... | collective-permute-start | bytes 98312 | tf_op jit(solution)/shard_map/ppermute | solution.py:33
  40.1 17.5 %collective-permute-start.13 = (f32[2,64,1024]{2,1,0:T(8,128)S(1)}, f32[2,64,1024]{2,1,0:T(8,128)S(1)}, u32[]{:S(2)}, u32[]{:S(2)}) collective-permute-start(f32[2,64,1024]{2,1,0:T(8,128)S(1)} %get-tuple-element.33.refs_16_), channel_id=1, source_target_pairs={{0,1},{1,0},{2,3},{3,2},{4,5},{5,4},{6,7},{7,6},{8,9},{9,8},{10,11... | collective-permute-start | bytes 1572872 | tf_op jit(solution)/shard_map/ppermute | solution.py:33
  42.6 15.1 %collective-permute-start.12 = (f32[2,64,1024]{2,1,0:T(8,128)S(1)}, f32[2,64,1024]{2,1,0:T(8,128)}, u32[]{:S(2)}, u32[]{:S(2)}) collective-permute-start(f32[2,64,1024]{2,1,0:T(8,128)S(1)} %collective-permute-done.11.refs_14_), channel_id=1, source_target_pairs={{0,1},{1,0},{2,3},{3,2},{4,5},{5,4},{6,7},{7,6},{8,9},{9,8},{10,11... | collective-permute-start | bytes 1572872 | tf_op jit(solution)/shard_map/ppermute | solution.py:33
  42.7 0.7 %copy-start.5 = (f32[4,136,128]{2,1,0:T(8,128)}, f32[4,136,128]{2,1,0:T(8,128)S(1)}, u32[]{:S(2)}) copy-start(f32[4,136,128]{2,1,0:T(8,128)S(1)} %collective-permute-done.7.refs_1_) | copy-start | bytes 835588
  43.4 11.6 %collective-permute-start.8 = (f32[4,136,128]{2,1,0:T(8,128)S(1)}, f32[4,136,128]{2,1,0:T(8,128)}, u32[]{:S(2)}, u32[]{:S(2)}) collective-permute-start(f32[4,136,128]{2,1,0:T(8,128)S(1)} %all-to-all-done.1.refs_0_), channel_id=1, source_target_pairs={{0,1},{1,0},{2,3},{3,2},{4,5},{5,4},{6,7},{7,6},{8,9},{9,8},{10,11... | collective-permute-start | bytes 835592 | tf_op jit(solution)/shard_map/ppermute | solution.py:33
  44.5 10.4 %all-to-all-start = ((f32[4,64,128]{2,1,0:T(8,128)}), f32[4,64,128]{2,1,0:T(8,128)}, u32[]{:S(2)}, u32[]{:S(2)}) async-start(f32[4,64,128]{2,1,0:T(8,128)} %broadcast_in_dim.2), calls=%async_computation | async-start | bytes 262144 | tf_op jit(solution)/shard_map/all_to_all | solution.py:497
  48.5 6.5 %collective-permute-start.9 = (f32[4,136,128]{2,1,0:T(8,128)}, f32[4,136,128]{2,1,0:T(8,128)}, u32[]{:S(2)}, u32[]{:S(2)}) collective-permute-start(f32[4,136,128]{2,1,0:T(8,128)} %copy-done.5), channel_id=1, source_target_pairs={{0,1},{1,0},{2,3},{3,2},{4,5},{5,4},{6,7},{7,6},{8,9},{9,8},{10,11... | collective-permute-start | bytes 835592 | tf_op jit(solution)/shard_map/ppermute | solution.py:33
  48.6 9.1 %collective-permute-start.10 = (f32[2,72,256]{2,1,0:T(8,128)S(1)}, f32[2,72,256]{2,1,0:T(8,128)}, u32[]{:S(2)}, u32[]{:S(2)}) collective-permute-start(f32[2,72,256]{2,1,0:T(8,128)S(1)} %collective-permute-done.mp_below.refs_10_), channel_id=1, source_target_pairs={{0,1},{1,0},{2,3},{3,2},{4,5},{5,4},{6,7},{7,6},{8,9},{9,8},{10,11... | collective-permute-start | bytes 442376 | tf_op jit(solution)/shard_map/ppermute | solution.py:33
  54.9 2.7 %collective-permute-start.6 = (f32[4,64,128]{2,1,0:T(8,128)}, f32[4,64,128]{2,1,0:T(8,128)}, u32[]{:S(2)}, u32[]{:S(2)}) collective-permute-start(f32[4,64,128]{2,1,0:T(8,128)} %all-to-all-done.refs_0_), channel_id=1, source_target_pairs={{0,1},{1,0},{2,3},{3,2},{4,5},{5,4},{6,7},{7,6},{8,9},{9,8},{10,11... | collective-permute-start | bytes 393224 | tf_op jit(solution)/shard_map/ppermute | solution.py:33
  55.0 1.0 %copy-start.6 = (f32[4,136,128]{2,1,0:T(8,128)S(1)}, f32[4,136,128]{2,1,0:T(8,128)}, u32[]{:S(2)}) copy-start(f32[4,136,128]{2,1,0:T(8,128)} %copy-done.5) | copy-start | bytes 835588

commit v6 on v5

--- a/solution.py
+++ b/solution.py
@@ -13,6 +13,7 @@
 EXTRA = 8
 
 high = lax.Precision.HIGH
+LONG = pl.CostEstimate(flops=5 * 10**9, bytes_accessed=8 * MIB, transcendentals=0)
 smem = pl.BlockSpec(memory_space=pltpu.SMEM)
 vmem = pl.BlockSpec(memory_space=pltpu.VMEM)
 
@@ -53,13 +54,14 @@
 held_out = pl.BlockSpec(memory_space=pltpu.HBM)
 
 
-def call(kernel, outs, ins, args, scratch=(), limit=16, out_specs=None):
+def call(kernel, outs, ins, args, scratch=(), limit=16, out_specs=None, cost=None):
     return pl.pallas_call(
         kernel,
         out_shape=[jax.ShapeDtypeStruct(shape, jnp.float32) for shape in outs],
         in_specs=ins,
         out_specs=out_specs or [vmem] * len(outs),
         scratch_shapes=list(scratch),
+        cost_estimate=cost,
         compiler_params=pltpu.CompilerParams(vmem_limit_bytes=limit and limit * MIB),
     )(*args)
 
@@ -103,6 +105,20 @@
         return lax.dot_general(x, y, (contract, ((), ())), preferred_element_type=jnp.float32)
 
     return one(a[0], b[0]) + (one(a[0], b[1]) + one(a[1], b[0]))
+
+
+def small(z):
+    return z.owners <= SMALL and z.pairs == z.fit_count == 2
+
+
+def each_pair(z, action):
+    if z.owners <= SMALL:
+        for pair in range(z.total):
+            action(pair)
+    else:
+        @pl.loop(0, z.total)
+        def _(pair):
+            action(pair)
 
 
 def mapped_kernel(z, c_in, map_in, e_in, coupling_in, mp_ref, c_ref, map_ref, e_ref, coupling,
@@ -130,65 +146,52 @@
         mp_ref[p, n + 1 : n + 2, :] = spread
 
 
-def small(z):
-    return z.owners <= SMALL and z.pairs == z.fit_count == 2
-
-
-def each_pair(z, action):
-    if z.owners <= SMALL:
-        for pair in range(z.total):
-            action(pair)
-    else:
-        @pl.loop(0, z.total)
-        def _(pair):
-            action(pair)
-
-
-def pack_kernel(z, s_ref, mp_ref, order, out_ref):
+def pack_kernel(z, s_in, mp_in, pack_ref, s_ref, mp_ref, sems):
     n = z.pnos
     line = 2 * n
     base = z.links * n // 2
+    wait(started([s_in, mp_in.at[:, pl.ds(n, EXTRA), :]], [s_ref, mp_ref], sems))
     for slot in range(1 if small(z) else z.pairs):
         p = lax.axis_index("fit") if small(z) else slot
-        at = 0 if small(z) else slot
         for r in range(n // 2):
             lines = s_ref[p, :, r * line : (r + 1) * line]
             for k in range(z.links):
                 row = k * n // 2 + r
-                out_ref[at, row : row + 1, :] = lines[k : k + 1, :]
-        out_ref[at, base:, :] = jnp.zeros((EXTRA, line), jnp.float32)
-        out_ref[at, base : base + 1, :] = mp_ref[p, n : n + 1, :line]
+                pack_ref[slot, row : row + 1, :] = lines[k : k + 1, :]
+        pack_ref[slot, base:, :] = jnp.zeros((EXTRA, line), jnp.float32)
+        pack_ref[slot, base : base + 1, :] = mp_ref[p, 0:1, :line]
         for k in range(z.links // 2):
-            out_ref[at, base + 1 + k : base + 2 + k, :] = mp_ref[
-                p, n + 1 : n + 2, k * line : (k + 1) * line
+            pack_ref[slot, base + 1 + k : base + 2 + k, :] = mp_ref[
+                p, 1:2, k * line : (k + 1) * line
             ]
     if small(z):
         for copy in range(1, z.owners):
-            out_ref[copy] = out_ref[0]
-
-
-def below_kernel(z, second, mp_below, b_ref, order, right_ref):
+            pack_ref[copy] = pack_ref[0]
+
+
+def below_kernel(z, second_in, mp_below, b_in, order, right_ref, second, m_ref, b_ref, sems):
     owner, sub = lax.axis_index("orb"), lax.axis_index("sub")
     start = side_start(z, jnp.maximum(owner - 1, 0), sub, 0)
+    wait(started([second_in], [second], sems))
+    m_copies = started([mp_below.at[:, pl.ds(0, z.pnos), :]], [m_ref], sems)
+    b_copies, held = [], []
     for p in range(z.pairs):
         j = second[start + p] - owner * z.orbitals
-        held = jnp.where(j >= 0, 1.0, 0.0)
-        mapped = mp_below[p, : z.pnos, :] * held
-        right_ref[p] = mm(mapped, b_ref[jnp.clip(j, 0, z.orbitals - 1)])
-
-
-def left_kernel(z, first, c_ref, b_ref, left_ref):
+        held.append(jnp.where(j >= 0, 1.0, 0.0))
+        b_copies += started([b_in.at[jnp.clip(j, 0, z.orbitals - 1)]], [b_ref.at[p]], sems, 1 + p)
+    wait(m_copies)
+    for p in range(z.pairs):
+        wait(b_copies[p : p + 1])
+        right_ref[p] = mm(m_ref[p] * held[p], b_ref[p])
+
+
+def local_kernel(z, first, second, c_ref, mp_ref, b_ref, left_ref, right_ref):
     owner, sub = lax.axis_index("orb"), lax.axis_index("sub")
     start = side_start(z, owner, sub, 0)
+    base = owner * z.orbitals
     for p in range(z.pairs):
-        left_ref[p] = mm(c_ref[p], b_ref[first[start + p] - owner * z.orbitals])
-
-
-def here_kernel(z, second, mp_ref, b_ref, order, right_ref):
-    owner, sub = lax.axis_index("orb"), lax.axis_index("sub")
-    start = side_start(z, owner, sub, 0)
-    for p in range(z.pairs):
-        j = second[start + p] - owner * z.orbitals
+        left_ref[p] = mm(c_ref[p], b_ref[first[start + p] - base])
+        j = second[start + p] - base
         local = jnp.where(j < z.orbitals, 1.0, 0.0)
         right_ref[p] = mm(
             mp_ref[p, : z.pnos, :] * local, b_ref[jnp.minimum(j, z.orbitals - 1)]
@@ -424,6 +427,7 @@
     def scratch(*shape, kind=jnp.float32):
         return pltpu.VMEM(shape, kind)
 
+    pack_shape = (z.owners if small(z) else pairs, z.links * n // 2 + EXTRA, 2 * n)
     (mp,) = call(
         functools.partial(mapped_kernel, z),
         [(pairs, n + EXTRA, z.paos)],
@@ -439,13 +443,17 @@
         limit=None,
     )
     mp_below = shifted(mp, "orb", 1)
-    pack_shape = (z.owners if small(z) else pairs, z.links * n // 2 + EXTRA, 2 * n)
     (pack,) = call(
         functools.partial(pack_kernel, z),
         [pack_shape],
-        [vmem, vmem, anywhere],
-        (intersections, mp, mp),
-        limit=8,
+        [hbm] * 2,
+        (intersections, mp),
+        [
+            scratch(*intersections.shape),
+            scratch(pairs, EXTRA, z.paos),
+            pltpu.SemaphoreType.DMA((2,)),
+        ],
+        limit=None,
     )
     if small(z):
         packs = [lax.all_to_all(pack, "orb", 0, 0)]
@@ -454,25 +462,25 @@
     (right_below,) = call(
         functools.partial(below_kernel, z),
         [(pairs, n, fits)],
-        [smem, vmem, vmem, anywhere],
+        [hbm] * 4,
         (pair_second, mp_below, blocks, pack),
-        limit=8,
+        [
+            pltpu.SMEM(pair_second.shape, jnp.int32),
+            scratch(pairs, n, z.paos),
+            scratch(pairs, *blocks.shape[1:]),
+            pltpu.SemaphoreType.DMA((1 + pairs,)),
+        ],
+        limit=None,
     )
     down = shifted(right_below, "orb", -1)
     (coefficients,) = gate((pno_coefficients,), right_below)
-    (left,) = call(
-        functools.partial(left_kernel, z),
-        [(pairs, n, fits)],
-        [smem, vmem, vmem],
-        (pair_first, coefficients, blocks),
+    left, right_here = call(
+        functools.partial(local_kernel, z),
+        [(pairs, n, fits), (pairs, n, fits)],
+        [smem, smem, vmem, vmem, vmem],
+        (pair_first, pair_second, coefficients, mp, blocks),
         limit=8,
-    )
-    (right_here,) = call(
-        functools.partial(here_kernel, z),
-        [(pairs, n, fits)],
-        [smem, vmem, vmem, anywhere],
-        (pair_second, mp, blocks, left),
-        limit=8,
+        cost=LONG,
     )
     left_late, mp_late, coefficients = gate((left, mp, coefficients), right_here)
     left_below = shifted(left_late, "orb", 1)
@@ -480,33 +488,10 @@
     left_other = swapped(left_late, "sub")
     c_other = swapped(coefficients, "sub")
     if small(z):
-        packs.append(swapped(gate(packs, right_here)[0], "fit"))
+        packs.append(swapped(gate(packs, right_below)[0], "fit"))
+        packs += [swapped(value, "sub") for value in gate(packs, right_here)]
 
     lists = (pair_first, pair_second, pno_ranks)
-    part, right = call(
-        functools.partial(sums_kernel, z),
-        [(n, pairs * n), (pairs, n, fits)],
-        [smem] * 4 + [vmem] * 4 + [anywhere] * 3,
-        (*lists, occ_energy, mp, left, right_here, down, left_other, mp_other, c_other),
-        limit=8,
-    )
-    if small(z):
-        packs += [swapped(value, "sub") for value in gate(packs, part)]
-        sums = part + swapped(part, "fit")
-        start_amps = [
-            lax.all_to_all(jnp.broadcast_to(sums[None], (z.owners, *sums.shape)), "orb", 0, 0)
-        ]
-        start_amps.append(swapped(start_amps[0], "sub"))
-    else:
-        sums = lax.psum(part, "fit")
-        start_amps = [lax.all_gather(sums, ("orb", "sub"), axis=0, tiled=False)]
-
-    right_late, mp_late = gate((right, mp_below), part)
-    (left_late,) = gate((left_below,), sums)
-    right_other, mp_below_other, left_below_other = [
-        swapped(value, "sub") for value in (right_late, mp_late, left_late)
-    ]
-
     split_shape = jax.ShapeDtypeStruct((z.total, n, wide), bf16)
     unpacked = pl.pallas_call(
         functools.partial(unpack_kernel, z),
@@ -519,8 +504,33 @@
         in_specs=[smem] * 4 + [vmem] * len(packs),
         out_specs=[vmem] * 4,
         scratch_shapes=[scratch(z.total if small(z) else 1, z.links // 2, n, 2 * n)],
+        cost_estimate=LONG,
         compiler_params=pltpu.CompilerParams(vmem_limit_bytes=(16 + more) * MIB),
     )(*lists, occ_energy, *packs)
+
+    part, right = call(
+        functools.partial(sums_kernel, z),
+        [(n, pairs * n), (pairs, n, fits)],
+        [smem] * 4 + [vmem] * 4 + [anywhere] * 4,
+        (*lists, occ_energy, mp, left, right_here, down, left_other, mp_other, c_other,
+         unpacked[0]),
+        limit=8,
+    )
+    if small(z):
+        sums = part + swapped(part, "fit")
+        start_amps = [
+            lax.all_to_all(jnp.broadcast_to(sums[None], (z.owners, *sums.shape)), "orb", 0, 0)
+        ]
+        start_amps.append(swapped(start_amps[0], "sub"))
+    else:
+        sums = lax.psum(part, "fit")
+        start_amps = [lax.all_gather(sums, ("orb", "sub"), axis=0, tiled=False)]
+
+    right_late, mp_late = gate((right, mp_below), part)
+    (left_late,) = gate((left_below,), sums)
+    right_other, mp_below_other, left_below_other = [
+        swapped(value, "sub") for value in (right_late, mp_late, left_late)
+    ]
 
     args = (
         pair_first, pair_second, neighbours, *start_amps, *unpacked,

time: 66.7 us -> 78.4 us (1.18)
  waiting for transfers between devices: 16.9 us -> 24.8 us
  starting transfers between devices: 23.5 us -> 26.9 us
  Pallas kernels: 18 us -> 20.2 us
  local copies, waits for them, and re-layouts: 6.77 us -> 5.02 us
    ppermute x11, waiting for transfers between devices: 3.41 us -> 8.01 us  [swapped(): return lax.ppermute(value, axis, [(0, 1), (1, 0)])]
    ppermute x3, waiting for transfers between devices: 7.67 us -> 10.6 us  [shifted(): lax.ppermute(value, axis, [(source, source + steps) for source in range(i...]
    pallas_call x7 -> x6, Pallas kernels: 16.3 us -> 19 us  [call(): pl.pallas_call(kernel, out_shape=[jax.ShapeDtypeStruct(shape, jnp.float32...]
    all_to_all x1, starting transfers between devices: 3.86 us -> 6.33 us  [body(): packs = [lax.all_to_all(pack, 'orb', 0, 0)]]
    unnamed x29 -> x43, local copies, waits for them, and re-layouts: 6.1 us -> 4.36 us
    all_to_all x1, starting transfers between devices: 3.95 us -> 4.81 us  [body(): lax.all_to_all(jnp.broadcast_to(sums[None], (z.owners, *sums.shape)), 'or...]
  transfers between devices with their start and end apart: 16 -> 16, of which waited for: 4 -> 6; matrix products, arithmetic and copies ran while one was open for 1% -> 1% of each run, Pallas kernels for 12% -> 11%
where the time goes in v6:
time: 78.4 us; the launch traced here: 77.8 us
  starting transfers between devices  26.9 us (34%)
  waiting for transfers between devices  24.8 us (32%)
  Pallas kernels  20.2 us (26%)
  local copies, waits for them, and re-layouts  5.02 us (6%)
  between operations  0.92 us (1%)
    pallas_call x6, Pallas kernels, call(): pl.pallas_call(kernel, out_shape=[jax.ShapeDtypeStruct(shape, jnp.float32...  19 us
    ppermute x3, starting transfers between devices, shifted(): lax.ppermute(value, axis, [(source, source + steps) for source in range(i...  11.3 us
    ppermute x3, waiting for transfers between devices, shifted(): lax.ppermute(value, axis, [(source, source + steps) for source in range(i...  10.6 us
    ppermute x11, waiting for transfers between devices, swapped(): return lax.ppermute(value, axis, [(0, 1), (1, 0)])  8.01 us
    all_to_all x1, starting transfers between devices, body(): packs = [lax.all_to_all(pack, 'orb', 0, 0)]  6.33 us
    all_to_all x1, waiting for transfers between devices, body(): lax.all_to_all(jnp.broadcast_to(sums[None], (z.owners, *sums.shape)), 'or...  6.21 us
    all_to_all x1, starting transfers between devices, body(): lax.all_to_all(jnp.broadcast_to(sums[None], (z.owners, *sums.shape)), 'or...  4.81 us
    ppermute x11, starting transfers between devices, swapped(): return lax.ppermute(value, axis, [(0, 1), (1, 0)])  4.49 us
  transfers between devices with their start and end apart: 16, of which 6 were waited for; matrix products, arithmetic and copies ran while one was open for 1% of the time, Pallas kernels for 11%

profile of v6, /device:TPU:0, one launch (start us, length us, event | category | flops | bytes accessed | tf_op | source)
XLA Modules:
  0.0 77.8 jit_solution(5553353855488754041)
XLA Ops:
  0.6 1.9 %shard_map.122.mp_in.mp_ref.refs_8_ = f32[2,72,256]{2,1,0:T(8,128)} custom-call(f32[2,64,256]{2,1,0:T(8,128)} %refs_6_.1, s32[2,256]{1,0:T(2,128)} %map_in.1, f32[2,64]{1,0:T(2,128)} %e_in.1, f32[2,4]{1,0:T(2,128)} %coupling_in.1), custom_call_target="tpu_custom_call" | custom-call | tf_op jit(solution)/shard_map/pallas_call | solution.py:58
  2.5 0.0 copy-start.1
  2.6 0.0 copy-start.6
  2.6 0.0 copy-start.11
  2.6 0.0 copy-start.14
  2.6 1.8 %shard_map.123.order = f32[4,136,128]{2,1,0:T(8,128)} custom-call(f32[2,4,4096]{2,1,0:T(4,128)} %s_in.1, f32[2,72,256]{2,1,0:T(8,128)} %shard_map.122.mp_in.mp_ref.refs_8_), custom_call_target="tpu_custom_call" | custom-call | tf_op jit(solution)/shard_map/pallas_call | solution.py:58
  4.4 6.3 %all-to-all-start = ((f32[4,136,128]{2,1,0:T(8,128)}), f32[4,136,128]{2,1,0:T(8,128)S(1)}, u32[]{:S(2)}, u32[]{:S(2)}) async-start(f32[4,136,128]{2,1,0:T(8,128)} %shard_map.123.order), calls=%async_computation | async-start | bytes 557056 | tf_op jit(solution)/shard_map/all_to_all | solution.py:459
  10.8 3.9 %collective-permute-start = (f32[2,72,256]{2,1,0:T(8,128)}, f32[2,72,256]{2,1,0:T(8,128)S(1)}, u32[]{:S(2)}, u32[]{:S(2)}) collective-permute-start(f32[2,72,256]{2,1,0:T(8,128)} %shard_map.122.mp_in.mp_ref.refs_8_), channel_id=1, source_target_pairs={{0,4},{4,8},{8,12},{1,5},{5,9},{9,13},{2,6},{6,10},{10,14},{3,7},{... | collective-permute-start | bytes 442376 | tf_op jit(solution)/shard_map/ppermute | solution.py:30
  14.7 4.0 %collective-permute-done.mp_below.refs_10_ = f32[2,72,256]{2,1,0:T(8,128)S(1)} collective-permute-done((f32[2,72,256]{2,1,0:T(8,128)}, f32[2,72,256]{2,1,0:T(8,128)S(1)}, u32[]{:S(2)}, u32[]{:S(2)}) %collective-permute-start) | collective-permute-done | bytes 147488 | tf_op jit(solution)/shard_map/ppermute | solution.py:30
  18.7 0.7 copy-done.2
  19.3 3.6 %shard_map.124 = f32[2,64,1024]{2,1,0:T(8,128)} custom-call(s32[16]{0:T(128)} %second.7, f32[2,72,256]{2,1,0:T(8,128)} %copy-done.2, f32[2,256,1024]{2,1,0:T(8,128)} %b_ref.1, f32[4,136,128]{2,1,0:T(8,128)} %shard_map.123.order), custom_call_target="tpu_custom_call" | custom-call | tf_op jit(solution)/shard_map/pallas_call | solution.py:58
  23.0 0.0 copy-start.19
  23.0 0.0 copy-start.12
  23.0 0.0 copy-start.15
  23.0 0.0 copy-start.17
  23.0 0.0 copy-start.18
  23.0 1.6 %collective-permute-start.5 = (f32[4,136,128]{2,1,0:T(8,128)S(1)}, f32[4,136,128]{2,1,0:T(8,128)S(1)}, u32[]{:S(2)}, u32[]{:S(2)}) collective-permute-start(f32[4,136,128]{2,1,0:T(8,128)S(1)} %all-to-all-done.refs_0_), channel_id=1, source_target_pairs={{0,2},{2,0},{1,3},{3,1},{4,6},{6,4},{5,7},{7,5},{8,10},{10,8},{9,1... | collective-permute-start | bytes 835592 | tf_op jit(solution)/shard_map/ppermute | solution.py:34
  24.6 1.9 %shard_map.125 = (f32[2,64,1024]{2,1,0:T(8,128)S(1)}, f32[2,64,1024]{2,1,0:T(8,128)S(1)}) custom-call(s32[16]{0:T(128)S(1)} %copy-done.14, s32[16]{0:T(128)S(1)} %copy-done.11, f32[2,64,256]{2,1,0:T(8,128)S(1)} %copy-done.6, f32[2,72,256]{2,1,0:T(8,128)S(1)} %copy-done, f32[2,256,1024]{2,1,0:T(8,128)S(1)} %copy-done.1), custom_call_target="tpu_custom_call" | custom-call | flops 5000000000 | bytes 8388608 | tf_op jit(solution)/shard_map/pallas_call | solution.py:58
  26.5 4.2 %collective-permute-done.5.refs_1_ = f32[4,136,128]{2,1,0:T(8,128)S(1)} collective-permute-done((f32[4,136,128]{2,1,0:T(8,128)S(1)}, f32[4,136,128]{2,1,0:T(8,128)S(1)}, u32[]{:S(2)}, u32[]{:S(2)}) %collective-permute-start.5) | collective-permute-done | bytes 278560 | tf_op jit(solution)/shard_map/ppermute | solution.py:34
  30.7 0.0 collective-permute-start.6
  30.7 0.5 collective-permute-start.7
  31.2 1.3 %collective-permute-start.1 = (f32[2,64,1024]{2,1,0:T(8,128)S(1)}, f32[2,64,1024]{2,1,0:T(8,128)S(1)}, u32[]{:S(2)}, u32[]{:S(2)}) collective-permute-start(f32[2,64,1024]{2,1,0:T(8,128)S(1)} %copy-done.19), channel_id=1, source_target_pairs={{4,0},{8,4},{12,8},{5,1},{9,5},{13,9},{6,2},{10,6},{14,10},{7,3},{... | collective-permute-start | bytes 1572872 | tf_op jit(solution)/shard_map/ppermute | solution.py:30
  32.5 0.1 collective-permute-start.2
  32.6 6.1 %collective-permute-start.11 = (f32[2,64,1024]{2,1,0:T(8,128)S(1)}, f32[2,64,1024]{2,1,0:T(8,128)S(1)}, u32[]{:S(2)}, u32[]{:S(2)}) collective-permute-start(f32[2,64,1024]{2,1,0:T(8,128)S(1)} %get-tuple-element.23.left_ref.refs_12_), channel_id=1, source_target_pairs={{0,4},{4,8},{8,12},{1,5},{5,9},{9,13},{2,6},{6,10},{10,14},{3,7},{... | collective-permute-start | bytes 1572872 | tf_op jit(solution)/shard_map/ppermute | solution.py:30
  38.7 0.3 collective-permute-start.4
  39.0 0.3 collective-permute-start.3
  39.3 0.9 %copy-done.8 = f32[4,136,128]{2,1,0:T(8,128)S(1)} copy-done((f32[4,136,128]{2,1,0:T(8,128)S(1)}, f32[4,136,128]{2,1,0:T(8,128)}, u32[]{:S(2)}) %copy-start.8) | copy-done | bytes 278552
  40.2 1.2 %shard_map.126 = (bf16[16,64,256]{2,1,0:T(8,128)(2,1)S(1)}, bf16[16,64,256]{2,1,0:T(8,128)(2,1)S(1)}, f32[16,64,64]{2,1,0:T(8,128)S(1)}, f32[16,8,256]{2,1,0:T(8,128)S(1)}) custom-call(s32[16]{0:T(128)S(1)} %copy-done.15, s32[16]{0:T(128)S(1)} %copy-done.12, s32[16]{0:T(128)S(1)} %copy-done.17, f32[8]{0:T(128)S(1)} %copy-done.18, ...), custom_call_target="tpu_custom_call" | custom-call | flops 5000000000 | bytes 8388608 | tf_op jit(solution)/shard_map/pallas_call | solution.py:496
  41.4 0.6 copy-done.9
  42.1 0.0 copy-start.16
  42.1 0.0 collective-permute-done.4.refs_2_.refs_7_
  42.1 6.6 %collective-permute-done.1.down_ref = f32[2,64,1024]{2,1,0:T(8,128)S(1)} collective-permute-done((f32[2,64,1024]{2,1,0:T(8,128)S(1)}, f32[2,64,1024]{2,1,0:T(8,128)S(1)}, u32[]{:S(2)}, u32[]{:S(2)}) %collective-permute-start.1) | collective-permute-done | bytes 524320 | tf_op jit(solution)/shard_map/ppermute | solution.py:30
  48.7 0.0 collective-permute-done.2.refs_0_.refs_13_
  48.7 1.6 %shard_map.127 = (f32[64,128]{1,0:T(8,128)S(1)}, f32[2,64,1024]{2,1,0:T(8,128)}) custom-call(s32[16]{0:T(128)S(1)} %copy-done.15, s32[16]{0:T(128)S(1)} %copy-done.12, s32[16]{0:T(128)S(1)} %copy-done.17, f32[8]{0:T(128)S(1)} %copy-done.18, f32[2,72,256]{2,1,0:T(8,128)S(1)} %copy-done, f32[2,64,1024]{2,1,0:T(8,128)S(1)} %get-tuple-element.23.left_ref.refs_12_, ...), custom_call_target="tpu_custom_call" | custom-call | tf_op jit(solution)/shard_map/pallas_call | solution.py:58
  50.3 1.5 %collective-permute-start.8 = (f32[64,128]{1,0:T(8,128)S(1)}, f32[64,128]{1,0:T(8,128)S(1)}, u32[]{:S(2)}, u32[]{:S(2)}) collective-permute-start(f32[64,128]{1,0:T(8,128)S(1)} %get-tuple-element.30), channel_id=1, source_target_pairs={{0,2},{2,0},{1,3},{3,1},{4,6},{6,4},{5,7},{7,5},{8,10},{10,8},{9,1... | collective-permute-start | bytes 98312 | tf_op jit(solution)/shard_map/ppermute | solution.py:34
  51.8 2.4 %collective-permute-done.8 = f32[64,128]{1,0:T(8,128)S(1)} collective-permute-done((f32[64,128]{1,0:T(8,128)S(1)}, f32[64,128]{1,0:T(8,128)S(1)}, u32[]{:S(2)}, u32[]{:S(2)}) %collective-permute-start.8) | collective-permute-done | bytes 32800 | tf_op jit(solution)/shard_map/ppermute | solution.py:34
  54.2 0.1 collective-permute-start.12
  54.3 0.7 broadcast_in_dim.2
  55.0 4.8 %all-to-all-start.1 = ((f32[4,64,128]{2,1,0:T(8,128)}), f32[4,64,128]{2,1,0:T(8,128)S(1)}, u32[]{:S(2)}, u32[]{:S(2)}) async-start(f32[4,64,128]{2,1,0:T(8,128)} %broadcast_in_dim.2), calls=%async_computation.1 | async-start | bytes 262144 | tf_op jit(solution)/shard_map/all_to_all | solution.py:522
  59.8 0.2 collective-permute-start.10
  60.0 6.2 %all-to-all-done.1.refs_0_ = f32[4,64,128]{2,1,0:T(8,128)S(1)} async-done(((f32[4,64,128]{2,1,0:T(8,128)}), f32[4,64,128]{2,1,0:T(8,128)S(1)}, u32[]{:S(2)}, u32[]{:S(2)}) %all-to-all-start.1) | async-done | bytes 131104 | tf_op jit(solution)/shard_map/all_to_all | solution.py:522
  66.2 0.0 collective-permute-start.9
  66.2 0.1 copy.13.near
  66.3 1.4 %collective-permute-done.9.refs_1_ = f32[4,64,128]{2,1,0:T(8,128)} collective-permute-done((f32[4,64,128]{2,1,0:T(8,128)S(1)}, f32[4,64,128]{2,1,0:T(8,128)}, u32[]{:S(2)}, u32[]{:S(2)}) %collective-permute-start.9) | collective-permute-done | bytes 131104 | tf_op jit(solution)/shard_map/ppermute | solution.py:34
  67.7 0.0 copy-start.5
  67.7 1.0 %copy-done.5 = f32[16,64,64]{2,1,0:T(8,128)S(1)} copy-done((f32[16,64,64]{2,1,0:T(8,128)S(1)}, f32[16,64,64]{2,1,0:T(8,128)}, u32[]{:S(2)}) %copy-start.5) | copy-done | bytes 262168
  68.8 0.9 %copy-done.10 = f32[16,8,256]{2,1,0:T(8,128)S(1)} copy-done((f32[16,8,256]{2,1,0:T(8,128)S(1)}, f32[16,8,256]{2,1,0:T(8,128)}, u32[]{:S(2)}) %copy-start.10) | copy-done | bytes 131096
  69.7 8.2 %shard_map.128 = (f32[2,4096]{1,0:T(2,128)}, f32[2,128,1024]{2,1,0:T(8,128)}) custom-call(s32[16]{0:T(128)S(1)} %copy-done.16, s32[16]{0:T(128)S(1)} %copy-done.13, s32[16,4]{1,0:T(8,128)S(1)} %copy.13.near, f32[4,64,128]{2,1,0:T(8,128)S(1)} %all-to-all-done.1.refs_0_, f32[4,64,128]{2,1,0:T(8,128)} %collective-permute-done.9.refs_1_, ...), custom_call_target="tpu_custom_call" | custom-call | tf_op jit(solution)/shard_map/pallas_call | solution.py:58
  (36 shorter events, 0.1 us)
Async XLA Ops:
  2.5 22.0 %copy-start = (f32[2,72,256]{2,1,0:T(8,128)S(1)}, f32[2,72,256]{2,1,0:T(8,128)}, u32[]{:S(2)}) copy-start(f32[2,72,256]{2,1,0:T(8,128)} %shard_map.122.mp_in.mp_ref.refs_8_) | copy-start | bytes 442372
  2.5 22.0 %copy-start.1 = (f32[2,256,1024]{2,1,0:T(8,128)S(1)}, f32[2,256,1024]{2,1,0:T(8,128)}, u32[]{:S(2)}) copy-start(f32[2,256,1024]{2,1,0:T(8,128)} %b_ref.1) | copy-start | bytes 6291460
  2.6 22.0 %copy-start.6 = (f32[2,64,256]{2,1,0:T(8,128)S(1)}, f32[2,64,256]{2,1,0:T(8,128)}, u32[]{:S(2)}) copy-start(f32[2,64,256]{2,1,0:T(8,128)} %refs_6_.1) | copy-start | bytes 393220
  2.6 22.0 %copy-start.11 = (s32[16]{0:T(128)S(1)}, s32[16]{0:T(128)}, u32[]{:S(2)}) copy-start(s32[16]{0:T(128)} %second.7) | copy-start | bytes 196
  2.6 22.0 %copy-start.14 = (s32[16]{0:T(128)S(1)}, s32[16]{0:T(128)}, u32[]{:S(2)}) copy-start(s32[16]{0:T(128)} %first.7) | copy-start | bytes 196
  4.4 18.5 %all-to-all-start = ((f32[4,136,128]{2,1,0:T(8,128)}), f32[4,136,128]{2,1,0:T(8,128)S(1)}, u32[]{:S(2)}, u32[]{:S(2)}) async-start(f32[4,136,128]{2,1,0:T(8,128)} %shard_map.123.order), calls=%async_computation | async-start | bytes 557056 | tf_op jit(solution)/shard_map/all_to_all | solution.py:459
  10.8 7.9 %collective-permute-start = (f32[2,72,256]{2,1,0:T(8,128)}, f32[2,72,256]{2,1,0:T(8,128)S(1)}, u32[]{:S(2)}, u32[]{:S(2)}) collective-permute-start(f32[2,72,256]{2,1,0:T(8,128)} %shard_map.122.mp_in.mp_ref.refs_8_), channel_id=1, source_target_pairs={{0,4},{4,8},{8,12},{1,5},{5,9},{9,13},{2,6},{6,10},{10,14},{3,7},{... | collective-permute-start | bytes 442376 | tf_op jit(solution)/shard_map/ppermute | solution.py:30
  18.7 0.7 copy-start.2
  23.0 7.7 %copy-start.7 = (f32[4,136,128]{2,1,0:T(8,128)}, f32[4,136,128]{2,1,0:T(8,128)S(1)}, u32[]{:S(2)}) copy-start(f32[4,136,128]{2,1,0:T(8,128)S(1)} %all-to-all-done.refs_0_) | copy-start | bytes 835588
  23.0 8.3 %copy-start.19 = (f32[2,64,1024]{2,1,0:T(8,128)S(1)}, f32[2,64,1024]{2,1,0:T(8,128)}, u32[]{:S(2)}) copy-start(f32[2,64,1024]{2,1,0:T(8,128)} %shard_map.124) | copy-start | bytes 1572868
  23.0 16.3 %copy-start.12 = (s32[16]{0:T(128)S(1)}, s32[16]{0:T(128)}, u32[]{:S(2)}) copy-start(s32[16]{0:T(128)} %second.7) | copy-start | bytes 196
  23.0 16.3 %copy-start.15 = (s32[16]{0:T(128)S(1)}, s32[16]{0:T(128)}, u32[]{:S(2)}) copy-start(s32[16]{0:T(128)} %first.7) | copy-start | bytes 196
  23.0 16.3 %copy-start.17 = (s32[16]{0:T(128)S(1)}, s32[16]{0:T(128)}, u32[]{:S(2)}) copy-start(s32[16]{0:T(128)} %ranks.3) | copy-start | bytes 196
  23.0 16.3 %copy-start.18 = (f32[8]{0:T(128)S(1)}, f32[8]{0:T(128)}, u32[]{:S(2)}) copy-start(f32[8]{0:T(128)} %occupied.3) | copy-start | bytes 100
  23.0 7.7 %collective-permute-start.5 = (f32[4,136,128]{2,1,0:T(8,128)S(1)}, f32[4,136,128]{2,1,0:T(8,128)S(1)}, u32[]{:S(2)}, u32[]{:S(2)}) collective-permute-start(f32[4,136,128]{2,1,0:T(8,128)S(1)} %all-to-all-done.refs_0_), channel_id=1, source_target_pairs={{0,2},{2,0},{1,3},{3,1},{4,6},{6,4},{5,7},{7,5},{8,10},{10,8},{9,1... | collective-permute-start | bytes 835592 | tf_op jit(solution)/shard_map/ppermute | solution.py:34
  30.7 8.0 %collective-permute-start.6 = (f32[4,136,128]{2,1,0:T(8,128)S(1)}, f32[4,136,128]{2,1,0:T(8,128)S(1)}, u32[]{:S(2)}, u32[]{:S(2)}) collective-permute-start(f32[4,136,128]{2,1,0:T(8,128)S(1)} %all-to-all-done.refs_0_), channel_id=1, source_target_pairs={{0,1},{1,0},{2,3},{3,2},{4,5},{5,4},{6,7},{7,6},{8,9},{9,8},{10,11... | collective-permute-start | bytes 835592 | tf_op jit(solution)/shard_map/ppermute | solution.py:34
  30.7 8.2 %collective-permute-start.7 = (f32[4,136,128]{2,1,0:T(8,128)S(1)}, f32[4,136,128]{2,1,0:T(8,128)S(1)}, u32[]{:S(2)}, u32[]{:S(2)}) collective-permute-start(f32[4,136,128]{2,1,0:T(8,128)S(1)} %collective-permute-done.5.refs_1_), channel_id=1, source_target_pairs={{0,1},{1,0},{2,3},{3,2},{4,5},{5,4},{6,7},{7,6},{8,9},{9,8},{10,11... | collective-permute-start | bytes 835592 | tf_op jit(solution)/shard_map/ppermute | solution.py:34
  31.2 17.5 %collective-permute-start.1 = (f32[2,64,1024]{2,1,0:T(8,128)S(1)}, f32[2,64,1024]{2,1,0:T(8,128)S(1)}, u32[]{:S(2)}, u32[]{:S(2)}) collective-permute-start(f32[2,64,1024]{2,1,0:T(8,128)S(1)} %copy-done.19), channel_id=1, source_target_pairs={{4,0},{8,4},{12,8},{5,1},{9,5},{13,9},{6,2},{10,6},{14,10},{7,3},{... | collective-permute-start | bytes 1572872 | tf_op jit(solution)/shard_map/ppermute | solution.py:30
  32.5 16.2 %collective-permute-start.2 = (f32[2,64,1024]{2,1,0:T(8,128)S(1)}, f32[2,64,1024]{2,1,0:T(8,128)S(1)}, u32[]{:S(2)}, u32[]{:S(2)}) collective-permute-start(f32[2,64,1024]{2,1,0:T(8,128)S(1)} %get-tuple-element.23.left_ref.refs_12_), channel_id=1, source_target_pairs={{0,1},{1,0},{2,3},{3,2},{4,5},{5,4},{6,7},{7,6},{8,9},{9,8},{10,11... | collective-permute-start | bytes 1572872 | tf_op jit(solution)/shard_map/ppermute | solution.py:34
  32.6 21.6 %collective-permute-start.11 = (f32[2,64,1024]{2,1,0:T(8,128)S(1)}, f32[2,64,1024]{2,1,0:T(8,128)S(1)}, u32[]{:S(2)}, u32[]{:S(2)}) collective-permute-start(f32[2,64,1024]{2,1,0:T(8,128)S(1)} %get-tuple-element.23.left_ref.refs_12_), channel_id=1, source_target_pairs={{0,4},{4,8},{8,12},{1,5},{5,9},{9,13},{2,6},{6,10},{10,14},{3,7},{... | collective-permute-start | bytes 1572872 | tf_op jit(solution)/shard_map/ppermute | solution.py:30
  38.7 3.4 %collective-permute-start.4 = (f32[2,64,256]{2,1,0:T(8,128)S(1)}, f32[2,64,256]{2,1,0:T(8,128)S(1)}, u32[]{:S(2)}, u32[]{:S(2)}) collective-permute-start(f32[2,64,256]{2,1,0:T(8,128)S(1)} %copy-done.6), channel_id=1, source_target_pairs={{0,1},{1,0},{2,3},{3,2},{4,5},{5,4},{6,7},{7,6},{8,9},{9,8},{10,11... | collective-permute-start | bytes 393224 | tf_op jit(solution)/shard_map/ppermute | solution.py:34
  39.0 3.1 %collective-permute-start.3 = (f32[2,72,256]{2,1,0:T(8,128)S(1)}, f32[2,72,256]{2,1,0:T(8,128)S(1)}, u32[]{:S(2)}, u32[]{:S(2)}) collective-permute-start(f32[2,72,256]{2,1,0:T(8,128)S(1)} %copy-done), channel_id=1, source_target_pairs={{0,1},{1,0},{2,3},{3,2},{4,5},{5,4},{6,7},{7,6},{8,9},{9,8},{10,11... | collective-permute-start | bytes 442376 | tf_op jit(solution)/shard_map/ppermute | solution.py:34
  39.3 1.0 %copy-start.8 = (f32[4,136,128]{2,1,0:T(8,128)S(1)}, f32[4,136,128]{2,1,0:T(8,128)}, u32[]{:S(2)}) copy-start(f32[4,136,128]{2,1,0:T(8,128)} %copy-done.7) | copy-start | bytes 835588
  41.4 0.7 copy-start.9
  42.1 12.2 %copy-start.4 = (f32[16,64,64]{2,1,0:T(8,128)}, f32[16,64,64]{2,1,0:T(8,128)S(1)}, u32[]{:S(2)}) copy-start(f32[16,64,64]{2,1,0:T(8,128)S(1)} %get-tuple-element.32.refs_4_) | copy-start | bytes 786436
  42.1 17.7 %copy-start.3 = (f32[2,72,256]{2,1,0:T(8,128)S(1)}, f32[2,72,256]{2,1,0:T(8,128)}, u32[]{:S(2)}) copy-start(f32[2,72,256]{2,1,0:T(8,128)} %copy-done.2) | copy-start | bytes 442372
  42.1 24.2 %copy-start.20 = (s32[16,4]{0,1:T(4,128)S(1)}, s32[16,4]{0,1:T(4,128)}, u32[]{:S(2)}) copy-start(s32[16,4]{0,1:T(4,128)} %param.17) | copy-start | bytes 772
  42.1 25.6 %copy-start.13 = (s32[16]{0:T(128)S(1)}, s32[16]{0:T(128)}, u32[]{:S(2)}) copy-start(s32[16]{0:T(128)} %second.7) | copy-start | bytes 196
  42.1 25.6 %copy-start.16 = (s32[16]{0:T(128)S(1)}, s32[16]{0:T(128)}, u32[]{:S(2)}) copy-start(s32[16]{0:T(128)} %first.7) | copy-start | bytes 196
  50.3 3.9 %collective-permute-start.8 = (f32[64,128]{1,0:T(8,128)S(1)}, f32[64,128]{1,0:T(8,128)S(1)}, u32[]{:S(2)}, u32[]{:S(2)}) collective-permute-start(f32[64,128]{1,0:T(8,128)S(1)} %get-tuple-element.30), channel_id=1, source_target_pairs={{0,2},{2,0},{1,3},{3,1},{4,6},{6,4},{5,7},{7,5},{8,10},{10,8},{9,1... | collective-permute-start | bytes 98312 | tf_op jit(solution)/shard_map/ppermute | solution.py:34
  51.8 15.9 %collective-permute-start.13 = (f32[2,64,1024]{2,1,0:T(8,128)}, f32[2,64,1024]{2,1,0:T(8,128)}, u32[]{:S(2)}, u32[]{:S(2)}) collective-permute-start(f32[2,64,1024]{2,1,0:T(8,128)} %get-tuple-element.37.refs_16_), channel_id=1, source_target_pairs={{0,1},{1,0},{2,3},{3,2},{4,5},{5,4},{6,7},{7,6},{8,9},{9,8},{10,11... | collective-permute-start | bytes 1572872 | tf_op jit(solution)/shard_map/ppermute | solution.py:34
  54.2 13.5 %collective-permute-start.12 = (f32[2,64,1024]{2,1,0:T(8,128)S(1)}, f32[2,64,1024]{2,1,0:T(8,128)}, u32[]{:S(2)}, u32[]{:S(2)}) collective-permute-start(f32[2,64,1024]{2,1,0:T(8,128)S(1)} %collective-permute-done.11.refs_14_), channel_id=1, source_target_pairs={{0,1},{1,0},{2,3},{3,2},{4,5},{5,4},{6,7},{7,6},{8,9},{9,8},{10,11... | collective-permute-start | bytes 1572872 | tf_op jit(solution)/shard_map/ppermute | solution.py:34
  55.0 11.2 %all-to-all-start.1 = ((f32[4,64,128]{2,1,0:T(8,128)}), f32[4,64,128]{2,1,0:T(8,128)S(1)}, u32[]{:S(2)}, u32[]{:S(2)}) async-start(f32[4,64,128]{2,1,0:T(8,128)} %broadcast_in_dim.2), calls=%async_computation.1 | async-start | bytes 262144 | tf_op jit(solution)/shard_map/all_to_all | solution.py:522
  59.8 6.5 %collective-permute-start.10 = (f32[2,72,256]{2,1,0:T(8,128)S(1)}, f32[2,72,256]{2,1,0:T(8,128)}, u32[]{:S(2)}, u32[]{:S(2)}) collective-permute-start(f32[2,72,256]{2,1,0:T(8,128)S(1)} %copy-done.3), channel_id=1, source_target_pairs={{0,1},{1,0},{2,3},{3,2},{4,5},{5,4},{6,7},{7,6},{8,9},{9,8},{10,11... | collective-permute-start | bytes 442376 | tf_op jit(solution)/shard_map/ppermute | solution.py:34
  66.2 1.5 %collective-permute-start.9 = (f32[4,64,128]{2,1,0:T(8,128)S(1)}, f32[4,64,128]{2,1,0:T(8,128)}, u32[]{:S(2)}, u32[]{:S(2)}) collective-permute-start(f32[4,64,128]{2,1,0:T(8,128)S(1)} %all-to-all-done.1.refs_0_), channel_id=1, source_target_pairs={{0,1},{1,0},{2,3},{3,2},{4,5},{5,4},{6,7},{7,6},{8,9},{9,8},{10,11... | collective-permute-start | bytes 393224 | tf_op jit(solution)/shard_map/ppermute | solution.py:34
  67.7 1.0 %copy-start.5 = (f32[16,64,64]{2,1,0:T(8,128)S(1)}, f32[16,64,64]{2,1,0:T(8,128)}, u32[]{:S(2)}) copy-start(f32[16,64,64]{2,1,0:T(8,128)} %copy-done.4) | copy-start | bytes 786436
  68.8 0.9 %copy-start.10 = (f32[16,8,256]{2,1,0:T(8,128)S(1)}, f32[16,8,256]{2,1,0:T(8,128)}, u32[]{:S(2)}) copy-start(f32[16,8,256]{2,1,0:T(8,128)} %copy-done.9) | copy-start | bytes 393220

commit v7 on v6

--- a/solution.py
+++ b/solution.py
@@ -13,7 +13,7 @@
 EXTRA = 8
 
 high = lax.Precision.HIGH
-LONG = pl.CostEstimate(flops=5 * 10**9, bytes_accessed=8 * MIB, transcendentals=0)
+BRIEF = pl.CostEstimate(flops=1, bytes_accessed=1, transcendentals=0)
 smem = pl.BlockSpec(memory_space=pltpu.SMEM)
 vmem = pl.BlockSpec(memory_space=pltpu.VMEM)
 
@@ -54,7 +54,7 @@
 held_out = pl.BlockSpec(memory_space=pltpu.HBM)
 
 
-def call(kernel, outs, ins, args, scratch=(), limit=16, out_specs=None, cost=None):
+def call(kernel, outs, ins, args, scratch=(), limit=16, out_specs=None, cost=BRIEF):
     return pl.pallas_call(
         kernel,
         out_shape=[jax.ShapeDtypeStruct(shape, jnp.float32) for shape in outs],
@@ -480,16 +480,16 @@
         [smem, smem, vmem, vmem, vmem],
         (pair_first, pair_second, coefficients, mp, blocks),
         limit=8,
-        cost=LONG,
+        cost=BRIEF,
     )
     left_late, mp_late, coefficients = gate((left, mp, coefficients), right_here)
-    left_below = shifted(left_late, "orb", 1)
     mp_other = swapped(mp_late, "sub")
     left_other = swapped(left_late, "sub")
     c_other = swapped(coefficients, "sub")
     if small(z):
-        packs.append(swapped(gate(packs, right_below)[0], "fit"))
+        packs.append(swapped(gate(packs, right_here)[0], "fit"))
         packs += [swapped(value, "sub") for value in gate(packs, right_here)]
+    left_below = shifted(gate((left,), packs[1] if small(z) else right_here)[0], "orb", 1)
 
     lists = (pair_first, pair_second, pno_ranks)
     split_shape = jax.ShapeDtypeStruct((z.total, n, wide), bf16)
@@ -504,7 +504,7 @@
         in_specs=[smem] * 4 + [vmem] * len(packs),
         out_specs=[vmem] * 4,
         scratch_shapes=[scratch(z.total if small(z) else 1, z.links // 2, n, 2 * n)],
-        cost_estimate=LONG,
+        cost_estimate=BRIEF,
         compiler_params=pltpu.CompilerParams(vmem_limit_bytes=(16 + more) * MIB),
     )(*lists, occ_energy, *packs)
 

time: 78.4 us -> 77.9 us (level)
  local copies, waits for them, and re-layouts: 5.02 us -> 8.9 us
  waiting for transfers between devices: 24.8 us -> 22.5 us
  starting transfers between devices: 26.9 us -> 25.2 us
    ppermute x3, waiting for transfers between devices: 10.6 us -> 5.35 us  [shifted(): lax.ppermute(value, axis, [(source, source + steps) for source in range(i...]
    unnamed x43 -> x45, local copies, waits for them, and re-layouts: 4.36 us -> 8.23 us
    ppermute x11, waiting for transfers between devices: 8.01 us -> 10.9 us  [swapped(): return lax.ppermute(value, axis, [(0, 1), (1, 0)])]
    ppermute x11, starting transfers between devices: 4.49 us -> 3.29 us  [swapped(): return lax.ppermute(value, axis, [(0, 1), (1, 0)])]
  transfers between devices with their start and end apart: 16 -> 16, of which waited for: 6 -> 8; matrix products, arithmetic and copies ran while one was open for 1% -> 1% of each run, Pallas kernels for 11% -> 10%
where the time goes in v7:
time: 77.9 us; the launch traced here: 77.2 us
  starting transfers between devices  25.2 us (32%)
  waiting for transfers between devices  22.5 us (29%)
  Pallas kernels  19.7 us (25%)
  local copies, waits for them, and re-layouts  8.9 us (11%)
  between operations  0.91 us (1%)
    pallas_call x6, Pallas kernels, call(): pl.pallas_call(kernel, out_shape=[jax.ShapeDtypeStruct(shape, jnp.float32...  18.5 us
    ppermute x11, waiting for transfers between devices, swapped(): return lax.ppermute(value, axis, [(0, 1), (1, 0)])  10.9 us
    ppermute x3, starting transfers between devices, shifted(): lax.ppermute(value, axis, [(source, source + steps) for source in range(i...  10.8 us
    unnamed x45, local copies, waits for them, and re-layouts  8.23 us
    all_to_all x1, starting transfers between devices, body(): packs = [lax.all_to_all(pack, 'orb', 0, 0)]  6.33 us
    all_to_all x1, waiting for transfers between devices, body(): lax.all_to_all(jnp.broadcast_to(sums[None], (z.owners, *sums.shape)), 'or...  6.21 us
    ppermute x3, waiting for transfers between devices, shifted(): lax.ppermute(value, axis, [(source, source + steps) for source in range(i...  5.35 us
    all_to_all x1, starting transfers between devices, body(): lax.all_to_all(jnp.broadcast_to(sums[None], (z.owners, *sums.shape)), 'or...  4.81 us
  transfers between devices with their start and end apart: 16, of which 8 were waited for; matrix products, arithmetic and copies ran while one was open for 1% of the time, Pallas kernels for 10%

profile of v7, /device:TPU:0, one launch (start us, length us, event | category | flops | bytes accessed | tf_op | source)
XLA Modules:
  0.0 77.2 jit_solution(13646979155139560280)
XLA Ops:
  0.6 1.9 %shard_map.122.mp_in.mp_ref.refs_8_ = f32[2,72,256]{2,1,0:T(8,128)} custom-call(f32[2,64,256]{2,1,0:T(8,128)} %refs_6_.1, s32[2,256]{1,0:T(2,128)} %map_in.1, f32[2,64]{1,0:T(2,128)} %e_in.1, f32[2,4]{1,0:T(2,128)} %coupling_in.1), custom_call_target="tpu_custom_call" | custom-call | flops 1 | bytes 1 | tf_op jit(solution)/shard_map/pallas_call | solution.py:58
  2.5 0.0 copy-start
  2.5 0.0 copy-start.1
  2.6 0.0 copy-start.2
  2.6 0.0 copy-start.13
  2.6 0.0 copy-start.15
  2.6 1.8 %shard_map.123.order = f32[4,136,128]{2,1,0:T(8,128)} custom-call(f32[2,4,4096]{2,1,0:T(4,128)} %s_in.1, f32[2,72,256]{2,1,0:T(8,128)} %shard_map.122.mp_in.mp_ref.refs_8_), custom_call_target="tpu_custom_call" | custom-call | flops 1 | bytes 1 | tf_op jit(solution)/shard_map/pallas_call | solution.py:58
  4.4 6.3 %all-to-all-start = ((f32[4,136,128]{2,1,0:T(8,128)}), f32[4,136,128]{2,1,0:T(8,128)S(1)}, u32[]{:S(2)}, u32[]{:S(2)}) async-start(f32[4,136,128]{2,1,0:T(8,128)} %shard_map.123.order), calls=%async_computation | async-start | bytes 557056 | tf_op jit(solution)/shard_map/all_to_all | solution.py:459
  10.8 4.1 %collective-permute-start = (f32[2,72,256]{2,1,0:T(8,128)}, f32[2,72,256]{2,1,0:T(8,128)S(1)}, u32[]{:S(2)}, u32[]{:S(2)}) collective-permute-start(f32[2,72,256]{2,1,0:T(8,128)} %shard_map.122.mp_in.mp_ref.refs_8_), channel_id=1, source_target_pairs={{0,4},{4,8},{8,12},{1,5},{5,9},{9,13},{2,6},{6,10},{10,14},{3,7},{... | collective-permute-start | bytes 442376 | tf_op jit(solution)/shard_map/ppermute | solution.py:30
  14.8 3.8 %collective-permute-done.mp_below.refs_10_ = f32[2,72,256]{2,1,0:T(8,128)S(1)} collective-permute-done((f32[2,72,256]{2,1,0:T(8,128)}, f32[2,72,256]{2,1,0:T(8,128)S(1)}, u32[]{:S(2)}, u32[]{:S(2)}) %collective-permute-start) | collective-permute-done | bytes 147488 | tf_op jit(solution)/shard_map/ppermute | solution.py:30
  18.7 0.7 copy-done.3
  19.3 3.7 %shard_map.124 = f32[2,64,1024]{2,1,0:T(8,128)} custom-call(s32[16]{0:T(128)} %second.7, f32[2,72,256]{2,1,0:T(8,128)} %copy-done.3, f32[2,256,1024]{2,1,0:T(8,128)} %b_ref.1, f32[4,136,128]{2,1,0:T(8,128)} %shard_map.123.order), custom_call_target="tpu_custom_call" | custom-call | flops 1 | bytes 1 | tf_op jit(solution)/shard_map/pallas_call | solution.py:58
  23.1 1.9 %shard_map.125 = (f32[2,64,1024]{2,1,0:T(8,128)S(1)}, f32[2,64,1024]{2,1,0:T(8,128)S(1)}) custom-call(s32[16]{0:T(128)S(1)} %copy-done.15, s32[16]{0:T(128)S(1)} %copy-done.13, f32[2,64,256]{2,1,0:T(8,128)S(1)} %copy-done.2, f32[2,72,256]{2,1,0:T(8,128)S(1)} %copy-done.1, f32[2,256,1024]{2,1,0:T(8,128)S(1)} %copy-done), custom_call_target="tpu_custom_call" | custom-call | flops 1 | bytes 1 | tf_op jit(solution)/shard_map/pallas_call | solution.py:58
  25.0 0.0 copy-start.9
  25.0 0.8 %copy-done.9 = f32[2,64,1024]{2,1,0:T(8,128)} copy-done((f32[2,64,1024]{2,1,0:T(8,128)}, f32[2,64,1024]{2,1,0:T(8,128)S(1)}, u32[]{:S(2)}) %copy-start.9) | copy-done | bytes 524312
  25.8 1.5 %collective-permute-start.5 = (f32[4,136,128]{2,1,0:T(8,128)S(1)}, f32[4,136,128]{2,1,0:T(8,128)S(1)}, u32[]{:S(2)}, u32[]{:S(2)}) collective-permute-start(f32[4,136,128]{2,1,0:T(8,128)S(1)} %all-to-all-done.refs_0_), channel_id=1, source_target_pairs={{0,2},{2,0},{1,3},{3,1},{4,6},{6,4},{5,7},{7,5},{8,10},{10,8},{9,1... | collective-permute-start | bytes 835592 | tf_op jit(solution)/shard_map/ppermute | solution.py:34
  27.3 1.3 %collective-permute-start.1 = (f32[2,64,1024]{2,1,0:T(8,128)}, f32[2,64,1024]{2,1,0:T(8,128)S(1)}, u32[]{:S(2)}, u32[]{:S(2)}) collective-permute-start(f32[2,64,1024]{2,1,0:T(8,128)} %shard_map.124), channel_id=1, source_target_pairs={{4,0},{8,4},{12,8},{5,1},{9,5},{13,9},{6,2},{10,6},{14,10},{7,3},{... | collective-permute-start | bytes 1572872 | tf_op jit(solution)/shard_map/ppermute | solution.py:30
  28.6 0.1 collective-permute-start.2
  28.7 4.8 %collective-permute-done.5.refs_1_ = f32[4,136,128]{2,1,0:T(8,128)S(1)} collective-permute-done((f32[4,136,128]{2,1,0:T(8,128)S(1)}, f32[4,136,128]{2,1,0:T(8,128)S(1)}, u32[]{:S(2)}, u32[]{:S(2)}) %collective-permute-start.5) | collective-permute-done | bytes 278560 | tf_op jit(solution)/shard_map/ppermute | solution.py:34
  33.5 5.5 %collective-permute-start.11 = (f32[2,64,1024]{2,1,0:T(8,128)S(1)}, f32[2,64,1024]{2,1,0:T(8,128)S(1)}, u32[]{:S(2)}, u32[]{:S(2)}) collective-permute-start(f32[2,64,1024]{2,1,0:T(8,128)S(1)} %get-tuple-element.37.left_ref.refs_12_), channel_id=1, source_target_pairs={{0,4},{4,8},{8,12},{1,5},{5,9},{9,13},{2,6},{6,10},{10,14},{3,7},{... | collective-permute-start | bytes 1572872 | tf_op jit(solution)/shard_map/ppermute | solution.py:30
  39.0 0.1 collective-permute-start.6
  39.0 0.5 collective-permute-start.7
  39.5 1.0 %collective-permute-done.6.refs_2_ = f32[4,136,128]{2,1,0:T(8,128)S(1)} collective-permute-done((f32[4,136,128]{2,1,0:T(8,128)S(1)}, f32[4,136,128]{2,1,0:T(8,128)S(1)}, u32[]{:S(2)}, u32[]{:S(2)}) %collective-permute-start.6) | collective-permute-done | bytes 278560 | tf_op jit(solution)/shard_map/ppermute | solution.py:34
  40.6 0.1 collective-permute-start.3
  40.7 0.3 collective-permute-done.7.refs_3_
  41.0 0.1 collective-permute-start.4
  41.1 1.2 %shard_map.126 = (bf16[16,64,256]{2,1,0:T(8,128)(2,1)S(1)}, bf16[16,64,256]{2,1,0:T(8,128)(2,1)S(1)}, f32[16,64,64]{2,1,0:T(8,128)S(1)}, f32[16,8,256]{2,1,0:T(8,128)S(1)}) custom-call(s32[16]{0:T(128)S(1)} %copy-done.15, s32[16]{0:T(128)S(1)} %copy-done.13, s32[16]{0:T(128)S(1)} %copy-done.17, f32[8]{0:T(128)S(1)} %copy-done.19, ...), custom_call_target="tpu_custom_call" | custom-call | flops 1 | bytes 1 | tf_op jit(solution)/shard_map/pallas_call | solution.py:496
  42.3 0.0 collective-permute-done.4.refs_2_.refs_7_
  42.3 1.5 %collective-permute-done.1.down_ref = f32[2,64,1024]{2,1,0:T(8,128)S(1)} collective-permute-done((f32[2,64,1024]{2,1,0:T(8,128)}, f32[2,64,1024]{2,1,0:T(8,128)S(1)}, u32[]{:S(2)}, u32[]{:S(2)}) %collective-permute-start.1) | collective-permute-done | bytes 524320 | tf_op jit(solution)/shard_map/ppermute | solution.py:30
  43.9 1.0 %copy-done.10 = f32[2,64,1024]{2,1,0:T(8,128)S(1)} copy-done((f32[2,64,1024]{2,1,0:T(8,128)S(1)}, f32[2,64,1024]{2,1,0:T(8,128)}, u32[]{:S(2)}) %copy-start.10) | copy-done | bytes 524312
  44.9 0.7 copy-done.14
  45.6 0.7 copy-done.16
  46.2 0.7 copy-done.18
  46.9 0.7 copy-done.20
  47.5 1.0 %shard_map.127 = (f32[64,128]{1,0:T(8,128)S(1)}, f32[2,64,1024]{2,1,0:T(8,128)S(1)}) custom-call(s32[16]{0:T(128)S(1)} %copy-done.16, s32[16]{0:T(128)S(1)} %copy-done.14, s32[16]{0:T(128)S(1)} %copy-done.18, f32[8]{0:T(128)S(1)} %copy-done.20, f32[2,72,256]{2,1,0:T(8,128)S(1)} %copy-done.1, f32[2,64,1024]{2,1,0:T(8,128)S(1)} %get-tuple-element.37.left_ref.refs_12_, ...), custom_call_target="tpu_custom_call" | custom-call | flops 1 | bytes 1 | tf_op jit(solution)/shard_map/pallas_call | solution.py:58
  48.5 0.6 collective-permute-start.8
  49.1 3.4 %collective-permute-done.8 = f32[64,128]{1,0:T(8,128)S(1)} collective-permute-done((f32[64,128]{1,0:T(8,128)S(1)}, f32[64,128]{1,0:T(8,128)S(1)}, u32[]{:S(2)}, u32[]{:S(2)}) %collective-permute-start.8) | collective-permute-done | bytes 32800 | tf_op jit(solution)/shard_map/ppermute | solution.py:34
  52.5 0.1 collective-permute-start.12
  52.6 0.7 broadcast_in_dim.2
  53.3 4.8 %all-to-all-start.1 = ((f32[4,64,128]{2,1,0:T(8,128)}), f32[4,64,128]{2,1,0:T(8,128)S(1)}, u32[]{:S(2)}, u32[]{:S(2)}) async-start(f32[4,64,128]{2,1,0:T(8,128)} %broadcast_in_dim.2), calls=%async_computation.1 | async-start | bytes 262144 | tf_op jit(solution)/shard_map/all_to_all | solution.py:522
  58.1 0.2 collective-permute-start.10
  58.3 6.2 %all-to-all-done.1.refs_0_ = f32[4,64,128]{2,1,0:T(8,128)S(1)} async-done(((f32[4,64,128]{2,1,0:T(8,128)}), f32[4,64,128]{2,1,0:T(8,128)S(1)}, u32[]{:S(2)}, u32[]{:S(2)}) %all-to-all-start.1) | async-done | bytes 131104 | tf_op jit(solution)/shard_map/all_to_all | solution.py:522
  64.5 0.1 copy.13.near
  64.6 1.4 %collective-permute-done.9.refs_1_ = f32[4,64,128]{2,1,0:T(8,128)} collective-permute-done((f32[4,64,128]{2,1,0:T(8,128)S(1)}, f32[4,64,128]{2,1,0:T(8,128)}, u32[]{:S(2)}, u32[]{:S(2)}) %collective-permute-start.9) | collective-permute-done | bytes 131104 | tf_op jit(solution)/shard_map/ppermute | solution.py:34
  66.0 1.0 %copy-done.6 = bf16[16,64,256]{2,1,0:T(8,128)(2,1)S(1)} copy-done((bf16[16,64,256]{2,1,0:T(8,128)(2,1)S(1)}, bf16[16,64,256]{2,1,0:T(8,128)(2,1)}, u32[]{:S(2)}) %copy-start.6) | copy-done | bytes 524312
  67.1 1.0 %copy-done.8 = f32[16,64,64]{2,1,0:T(8,128)S(1)} copy-done((f32[16,64,64]{2,1,0:T(8,128)S(1)}, f32[16,64,64]{2,1,0:T(8,128)}, u32[]{:S(2)}) %copy-start.8) | copy-done | bytes 262168
  68.1 0.9 %copy-done.12 = f32[16,8,256]{2,1,0:T(8,128)S(1)} copy-done((f32[16,8,256]{2,1,0:T(8,128)S(1)}, f32[16,8,256]{2,1,0:T(8,128)}, u32[]{:S(2)}) %copy-start.12) | copy-done | bytes 131096
  69.0 8.2 %shard_map.128 = (f32[2,4096]{1,0:T(2,128)}, f32[2,128,1024]{2,1,0:T(8,128)}) custom-call(s32[16]{0:T(128)S(1)} %copy-done.16, s32[16]{0:T(128)S(1)} %copy-done.14, s32[16,4]{1,0:T(8,128)S(1)} %copy.13.near, f32[4,64,128]{2,1,0:T(8,128)S(1)} %all-to-all-done.1.refs_0_, f32[4,64,128]{2,1,0:T(8,128)} %collective-permute-done.9.refs_1_, ...), custom_call_target="tpu_custom_call" | custom-call | flops 1 | bytes 1 | tf_op jit(solution)/shard_map/pallas_call | solution.py:58
  (38 shorter events, 0.1 us)
Async XLA Ops:
  2.5 20.5 %copy-start = (f32[2,256,1024]{2,1,0:T(8,128)S(1)}, f32[2,256,1024]{2,1,0:T(8,128)}, u32[]{:S(2)}) copy-start(f32[2,256,1024]{2,1,0:T(8,128)} %b_ref.1) | copy-start | bytes 6291460
  2.5 20.5 %copy-start.1 = (f32[2,72,256]{2,1,0:T(8,128)S(1)}, f32[2,72,256]{2,1,0:T(8,128)}, u32[]{:S(2)}) copy-start(f32[2,72,256]{2,1,0:T(8,128)} %shard_map.122.mp_in.mp_ref.refs_8_) | copy-start | bytes 442372
  2.6 20.5 %copy-start.2 = (f32[2,64,256]{2,1,0:T(8,128)S(1)}, f32[2,64,256]{2,1,0:T(8,128)}, u32[]{:S(2)}) copy-start(f32[2,64,256]{2,1,0:T(8,128)} %refs_6_.1) | copy-start | bytes 393220
  2.6 20.5 %copy-start.13 = (s32[16]{0:T(128)S(1)}, s32[16]{0:T(128)}, u32[]{:S(2)}) copy-start(s32[16]{0:T(128)} %second.7) | copy-start | bytes 196
  2.6 20.5 %copy-start.15 = (s32[16]{0:T(128)S(1)}, s32[16]{0:T(128)}, u32[]{:S(2)}) copy-start(s32[16]{0:T(128)} %first.7) | copy-start | bytes 196
  4.4 21.3 %all-to-all-start = ((f32[4,136,128]{2,1,0:T(8,128)}), f32[4,136,128]{2,1,0:T(8,128)S(1)}, u32[]{:S(2)}, u32[]{:S(2)}) async-start(f32[4,136,128]{2,1,0:T(8,128)} %shard_map.123.order), calls=%async_computation | async-start | bytes 557056 | tf_op jit(solution)/shard_map/all_to_all | solution.py:459
  10.8 30.3 %copy-start.17 = (s32[16]{0:T(128)S(1)}, s32[16]{0:T(128)}, u32[]{:S(2)}) copy-start(s32[16]{0:T(128)} %ranks.3) | copy-start | bytes 196
  10.8 30.3 %copy-start.19 = (f32[8]{0:T(128)S(1)}, f32[8]{0:T(128)}, u32[]{:S(2)}) copy-start(f32[8]{0:T(128)} %occupied.3) | copy-start | bytes 100
  10.8 7.9 %collective-permute-start = (f32[2,72,256]{2,1,0:T(8,128)}, f32[2,72,256]{2,1,0:T(8,128)S(1)}, u32[]{:S(2)}, u32[]{:S(2)}) collective-permute-start(f32[2,72,256]{2,1,0:T(8,128)} %shard_map.122.mp_in.mp_ref.refs_8_), channel_id=1, source_target_pairs={{0,4},{4,8},{8,12},{1,5},{5,9},{9,13},{2,6},{6,10},{10,14},{3,7},{... | collective-permute-start | bytes 442376 | tf_op jit(solution)/shard_map/ppermute | solution.py:30
  18.7 0.7 copy-start.3
  25.0 0.8 %copy-start.9 = (f32[2,64,1024]{2,1,0:T(8,128)}, f32[2,64,1024]{2,1,0:T(8,128)S(1)}, u32[]{:S(2)}) copy-start(f32[2,64,1024]{2,1,0:T(8,128)S(1)} %get-tuple-element.23.here_ref) | copy-start | bytes 1572868
  25.8 7.7 %collective-permute-start.5 = (f32[4,136,128]{2,1,0:T(8,128)S(1)}, f32[4,136,128]{2,1,0:T(8,128)S(1)}, u32[]{:S(2)}, u32[]{:S(2)}) collective-permute-start(f32[4,136,128]{2,1,0:T(8,128)S(1)} %all-to-all-done.refs_0_), channel_id=1, source_target_pairs={{0,2},{2,0},{1,3},{3,1},{4,6},{6,4},{5,7},{7,5},{8,10},{10,8},{9,1... | collective-permute-start | bytes 835592 | tf_op jit(solution)/shard_map/ppermute | solution.py:34
  27.3 16.6 %collective-permute-start.1 = (f32[2,64,1024]{2,1,0:T(8,128)}, f32[2,64,1024]{2,1,0:T(8,128)S(1)}, u32[]{:S(2)}, u32[]{:S(2)}) collective-permute-start(f32[2,64,1024]{2,1,0:T(8,128)} %shard_map.124), channel_id=1, source_target_pairs={{4,0},{8,4},{12,8},{5,1},{9,5},{13,9},{6,2},{10,6},{14,10},{7,3},{... | collective-permute-start | bytes 1572872 | tf_op jit(solution)/shard_map/ppermute | solution.py:30
  28.5 29.6 %copy-start.4 = (f32[2,72,256]{2,1,0:T(8,128)S(1)}, f32[2,72,256]{2,1,0:T(8,128)}, u32[]{:S(2)}) copy-start(f32[2,72,256]{2,1,0:T(8,128)} %copy-done.3) | copy-start | bytes 442372
  28.6 36.0 %copy-start.21 = (s32[16,4]{0,1:T(4,128)S(1)}, s32[16,4]{0,1:T(4,128)}, u32[]{:S(2)}) copy-start(s32[16,4]{0,1:T(4,128)} %param.17) | copy-start | bytes 772
  28.6 15.3 %collective-permute-start.2 = (f32[2,64,1024]{2,1,0:T(8,128)S(1)}, f32[2,64,1024]{2,1,0:T(8,128)S(1)}, u32[]{:S(2)}, u32[]{:S(2)}) collective-permute-start(f32[2,64,1024]{2,1,0:T(8,128)S(1)} %get-tuple-element.37.left_ref.refs_12_), channel_id=1, source_target_pairs={{0,1},{1,0},{2,3},{3,2},{4,5},{5,4},{6,7},{7,6},{8,9},{9,8},{10,11... | collective-permute-start | bytes 1572872 | tf_op jit(solution)/shard_map/ppermute | solution.py:34
  33.5 19.1 %collective-permute-start.11 = (f32[2,64,1024]{2,1,0:T(8,128)S(1)}, f32[2,64,1024]{2,1,0:T(8,128)S(1)}, u32[]{:S(2)}, u32[]{:S(2)}) collective-permute-start(f32[2,64,1024]{2,1,0:T(8,128)S(1)} %get-tuple-element.37.left_ref.refs_12_), channel_id=1, source_target_pairs={{0,4},{4,8},{8,12},{1,5},{5,9},{9,13},{2,6},{6,10},{10,14},{3,7},{... | collective-permute-start | bytes 1572872 | tf_op jit(solution)/shard_map/ppermute | solution.py:30
  39.0 1.6 %collective-permute-start.6 = (f32[4,136,128]{2,1,0:T(8,128)S(1)}, f32[4,136,128]{2,1,0:T(8,128)S(1)}, u32[]{:S(2)}, u32[]{:S(2)}) collective-permute-start(f32[4,136,128]{2,1,0:T(8,128)S(1)} %all-to-all-done.refs_0_), channel_id=1, source_target_pairs={{0,1},{1,0},{2,3},{3,2},{4,5},{5,4},{6,7},{7,6},{8,9},{9,8},{10,11... | collective-permute-start | bytes 835592 | tf_op jit(solution)/shard_map/ppermute | solution.py:34
  39.0 1.9 %collective-permute-start.7 = (f32[4,136,128]{2,1,0:T(8,128)S(1)}, f32[4,136,128]{2,1,0:T(8,128)S(1)}, u32[]{:S(2)}, u32[]{:S(2)}) collective-permute-start(f32[4,136,128]{2,1,0:T(8,128)S(1)} %collective-permute-done.5.refs_1_), channel_id=1, source_target_pairs={{0,1},{1,0},{2,3},{3,2},{4,5},{5,4},{6,7},{7,6},{8,9},{9,8},{10,11... | collective-permute-start | bytes 835592 | tf_op jit(solution)/shard_map/ppermute | solution.py:34
  40.6 1.8 %collective-permute-start.3 = (f32[2,72,256]{2,1,0:T(8,128)S(1)}, f32[2,72,256]{2,1,0:T(8,128)S(1)}, u32[]{:S(2)}, u32[]{:S(2)}) collective-permute-start(f32[2,72,256]{2,1,0:T(8,128)S(1)} %copy-done.1), channel_id=1, source_target_pairs={{0,1},{1,0},{2,3},{3,2},{4,5},{5,4},{6,7},{7,6},{8,9},{9,8},{10,11... | collective-permute-start | bytes 442376 | tf_op jit(solution)/shard_map/ppermute | solution.py:34
  41.0 1.3 %collective-permute-start.4 = (f32[2,64,256]{2,1,0:T(8,128)S(1)}, f32[2,64,256]{2,1,0:T(8,128)S(1)}, u32[]{:S(2)}, u32[]{:S(2)}) collective-permute-start(f32[2,64,256]{2,1,0:T(8,128)S(1)} %copy-done.2), channel_id=1, source_target_pairs={{0,1},{1,0},{2,3},{3,2},{4,5},{5,4},{6,7},{7,6},{8,9},{9,8},{10,11... | collective-permute-start | bytes 393224 | tf_op jit(solution)/shard_map/ppermute | solution.py:34
  42.3 10.2 %copy-start.5 = (bf16[16,64,256]{2,1,0:T(8,128)(2,1)}, bf16[16,64,256]{2,1,0:T(8,128)(2,1)S(1)}, u32[]{:S(2)}) copy-start(bf16[16,64,256]{2,1,0:T(8,128)(2,1)S(1)} %get-tuple-element.32.refs_3_) | copy-start | bytes 1572868
  42.3 10.3 %copy-start.7 = (f32[16,64,64]{2,1,0:T(8,128)}, f32[16,64,64]{2,1,0:T(8,128)S(1)}, u32[]{:S(2)}) copy-start(f32[16,64,64]{2,1,0:T(8,128)S(1)} %get-tuple-element.33.refs_4_) | copy-start | bytes 786436
  42.3 11.0 %copy-start.11 = (f32[16,8,256]{2,1,0:T(8,128)}, f32[16,8,256]{2,1,0:T(8,128)S(1)}, u32[]{:S(2)}) copy-start(f32[16,8,256]{2,1,0:T(8,128)S(1)} %get-tuple-element.34.refs_5_) | copy-start | bytes 393220
  43.9 1.0 %copy-start.10 = (f32[2,64,1024]{2,1,0:T(8,128)S(1)}, f32[2,64,1024]{2,1,0:T(8,128)}, u32[]{:S(2)}) copy-start(f32[2,64,1024]{2,1,0:T(8,128)} %copy-done.9) | copy-start | bytes 1572868
  44.9 0.7 copy-start.14
  45.6 0.7 copy-start.16
  46.2 0.7 copy-start.18
  46.9 0.7 copy-start.20
  48.5 4.0 %collective-permute-start.8 = (f32[64,128]{1,0:T(8,128)S(1)}, f32[64,128]{1,0:T(8,128)S(1)}, u32[]{:S(2)}, u32[]{:S(2)}) collective-permute-start(f32[64,128]{1,0:T(8,128)S(1)} %get-tuple-element.31), channel_id=1, source_target_pairs={{0,2},{2,0},{1,3},{3,1},{4,6},{6,4},{5,7},{7,5},{8,10},{10,8},{9,1... | collective-permute-start | bytes 98312 | tf_op jit(solution)/shard_map/ppermute | solution.py:34
  49.1 16.9 %collective-permute-start.13 = (f32[2,64,1024]{2,1,0:T(8,128)S(1)}, f32[2,64,1024]{2,1,0:T(8,128)}, u32[]{:S(2)}, u32[]{:S(2)}) collective-permute-start(f32[2,64,1024]{2,1,0:T(8,128)S(1)} %get-tuple-element.39.refs_16_), channel_id=1, source_target_pairs={{0,1},{1,0},{2,3},{3,2},{4,5},{5,4},{6,7},{7,6},{8,9},{9,8},{10,11... | collective-permute-start | bytes 1572872 | tf_op jit(solution)/shard_map/ppermute | solution.py:34
  52.5 13.5 %collective-permute-start.12 = (f32[2,64,1024]{2,1,0:T(8,128)S(1)}, f32[2,64,1024]{2,1,0:T(8,128)}, u32[]{:S(2)}, u32[]{:S(2)}) collective-permute-start(f32[2,64,1024]{2,1,0:T(8,128)S(1)} %collective-permute-done.11.refs_14_), channel_id=1, source_target_pairs={{0,1},{1,0},{2,3},{3,2},{4,5},{5,4},{6,7},{7,6},{8,9},{9,8},{10,11... | collective-permute-start | bytes 1572872 | tf_op jit(solution)/shard_map/ppermute | solution.py:34
  53.3 11.2 %all-to-all-start.1 = ((f32[4,64,128]{2,1,0:T(8,128)}), f32[4,64,128]{2,1,0:T(8,128)S(1)}, u32[]{:S(2)}, u32[]{:S(2)}) async-start(f32[4,64,128]{2,1,0:T(8,128)} %broadcast_in_dim.2), calls=%async_computation.1 | async-start | bytes 262144 | tf_op jit(solution)/shard_map/all_to_all | solution.py:522
  58.1 6.5 %collective-permute-start.10 = (f32[2,72,256]{2,1,0:T(8,128)S(1)}, f32[2,72,256]{2,1,0:T(8,128)}, u32[]{:S(2)}, u32[]{:S(2)}) collective-permute-start(f32[2,72,256]{2,1,0:T(8,128)S(1)} %copy-done.4), channel_id=1, source_target_pairs={{0,1},{1,0},{2,3},{3,2},{4,5},{5,4},{6,7},{7,6},{8,9},{9,8},{10,11... | collective-permute-start | bytes 442376 | tf_op jit(solution)/shard_map/ppermute | solution.py:34
  64.5 1.5 %collective-permute-start.9 = (f32[4,64,128]{2,1,0:T(8,128)S(1)}, f32[4,64,128]{2,1,0:T(8,128)}, u32[]{:S(2)}, u32[]{:S(2)}) collective-permute-start(f32[4,64,128]{2,1,0:T(8,128)S(1)} %all-to-all-done.1.refs_0_), channel_id=1, source_target_pairs={{0,1},{1,0},{2,3},{3,2},{4,5},{5,4},{6,7},{7,6},{8,9},{9,8},{10,11... | collective-permute-start | bytes 393224 | tf_op jit(solution)/shard_map/ppermute | solution.py:34
  66.0 1.0 %copy-start.6 = (bf16[16,64,256]{2,1,0:T(8,128)(2,1)S(1)}, bf16[16,64,256]{2,1,0:T(8,128)(2,1)}, u32[]{:S(2)}) copy-start(bf16[16,64,256]{2,1,0:T(8,128)(2,1)} %copy-done.5) | copy-start | bytes 1572868
  67.1 1.0 %copy-start.8 = (f32[16,64,64]{2,1,0:T(8,128)S(1)}, f32[16,64,64]{2,1,0:T(8,128)}, u32[]{:S(2)}) copy-start(f32[16,64,64]{2,1,0:T(8,128)} %copy-done.7) | copy-start | bytes 786436
  68.1 0.9 %copy-start.12 = (f32[16,8,256]{2,1,0:T(8,128)S(1)}, f32[16,8,256]{2,1,0:T(8,128)}, u32[]{:S(2)}) copy-start(f32[16,8,256]{2,1,0:T(8,128)} %copy-done.11) | copy-start | bytes 393220

commit v8 on v7

--- a/solution.py
+++ b/solution.py
@@ -169,20 +169,14 @@
             pack_ref[copy] = pack_ref[0]
 
 
-def below_kernel(z, second_in, mp_below, b_in, order, right_ref, second, m_ref, b_ref, sems):
+def below_kernel(z, second, mp_below, b_ref, right_ref):
     owner, sub = lax.axis_index("orb"), lax.axis_index("sub")
     start = side_start(z, jnp.maximum(owner - 1, 0), sub, 0)
-    wait(started([second_in], [second], sems))
-    m_copies = started([mp_below.at[:, pl.ds(0, z.pnos), :]], [m_ref], sems)
-    b_copies, held = [], []
     for p in range(z.pairs):
         j = second[start + p] - owner * z.orbitals
-        held.append(jnp.where(j >= 0, 1.0, 0.0))
-        b_copies += started([b_in.at[jnp.clip(j, 0, z.orbitals - 1)]], [b_ref.at[p]], sems, 1 + p)
-    wait(m_copies)
-    for p in range(z.pairs):
-        wait(b_copies[p : p + 1])
-        right_ref[p] = mm(m_ref[p] * held[p], b_ref[p])
+        held = jnp.where(j >= 0, 1.0, 0.0)
+        mapped = mp_below[p, : z.pnos, :] * held
+        right_ref[p] = mm(mapped, b_ref[jnp.clip(j, 0, z.orbitals - 1)])
 
 
 def local_kernel(z, first, second, c_ref, mp_ref, b_ref, left_ref, right_ref):
@@ -213,42 +207,21 @@
         sums_ref[:, p * n : (p + 1) * n] = -part * scale
 
 
-def unpack_kernel(z, first, second, ranks, occupied, *refs):
-    packs = refs[:-5]
-    high_ref, low_ref, scale_ref, coupling_ref, rows = refs[-5:]
-    sub, fit = lax.axis_index("sub"), lax.axis_index("fit")
+def unpack(z, pair, block, rows, slot, s_high, s_low, scale_ref, coupling_ref, lists):
     n = z.pnos
-    base = z.links * n // 2
-
-    def one(pair, block, slot):
-        for k in range(0, z.links, 2):
-            two = [block(k * n // 2, n // 2), block((k + 1) * n // 2, n // 2)]
-            for odd in range(2):
-                rows[slot, k // 2, pl.ds(odd, n // 2, 2), :] = jnp.concatenate(
-                    [part[:, odd * n : (odd + 1) * n] for part in two], axis=1
-                )
-        s = jnp.concatenate([rows[slot, k] for k in range(z.links // 2)], axis=1)
-        high_ref[pair], low_ref[pair] = split(s)
-        extra = block(base, EXTRA)
-        scale_ref[pair] = scale_of(z, pair, extra[0:1, :n], first, second, ranks, occupied)
-        coupling_ref[pair, 0:1, :] = jnp.concatenate(
-            [extra[1 + k : 2 + k, :] for k in range(z.links // 2)], axis=1
-        )
-
-    if small(z):
-        for index, ref in enumerate(packs):
-            side = sub if index < 2 else 1 - sub
-            which = fit if index % 2 == 0 else 1 - fit
-            for who in range(z.owners):
-                one(
-                    who * z.own + side * z.pairs + which,
-                    lambda start, size: ref[who, start : start + size, :],
-                    index * z.owners + who,
-                )
-    else:
-        each_pair(
-            z, lambda pair: one(pair, lambda start, size: packs[0][pair, pl.ds(start, size), :], 0)
-        )
+    for k in range(0, z.links, 2):
+        two = [block(k * n // 2, n // 2), block((k + 1) * n // 2, n // 2)]
+        for odd in range(2):
+            rows[slot, k // 2, pl.ds(odd, n // 2, 2), :] = jnp.concatenate(
+                [part[:, odd * n : (odd + 1) * n] for part in two], axis=1
+            )
+    s = jnp.concatenate([rows[slot, k] for k in range(z.links // 2)], axis=1)
+    s_high[pair], s_low[pair] = split(s)
+    extra = block(z.links * n // 2, EXTRA)
+    scale_ref[pair] = scale_of(z, pair, extra[0:1, :n], *lists)
+    coupling_ref[pair, 0:1, :] = jnp.concatenate(
+        [extra[1 + k : 2 + k, :] for k in range(z.links // 2)], axis=1
+    )
 
 
 def coupled_of(z, index, pair, near, s, coupling, amps_high, amps_low, diag_high, diag_low):
@@ -261,32 +234,36 @@
     return split(mm3(s, (diag_high[index], diag_low[index])) * coupling)
 
 
-def final_kernel(z, first, second, near, *refs):
-    start_count = 2 if small(z) else 1
+def final_kernel(z, first, second, ranks, near, occupied, *refs):
+    start_count, pack_count = (2, 4) if small(z) else (1, 1)
     starts = refs[:start_count]
-    s_high, s_low, scale_ref, coupling_ref = refs[start_count : start_count + 4]
+    pack_in = refs[start_count : start_count + pack_count]
     (c_in, c_other, mp_in, mp_other, mp_below, mp_below_other, left_in, left_other, left_below,
-     left_below_other, right_in, right_other) = refs[start_count + 4 : start_count + 16]
-    (amp_ref, grad_out, c_ref, m_ref, rhs, grad, flat, amps, amps_high, amps_low, next_high,
-     next_low, diag_high, diag_low, rows_high, rows_low, sems) = refs[start_count + 16 :]
+     left_below_other, right_in, right_other) = refs[start_count + pack_count :][:12]
+    (amp_ref, grad_out, packs, s_high, s_low, scale_ref, coupling_ref, s_rows, c_ref, m_ref, rhs,
+     grad, flat, amps, amps_high, amps_low, next_high, next_low, diag_high, diag_low, rows_high,
+     rows_low, sems) = refs[start_count + pack_count + 12 :]
     owner, sub = lax.axis_index("orb"), lax.axis_index("sub")
+    fit = lax.axis_index("fit")
     n, pairs, own = z.pnos, z.pairs, z.own
     half = z.paos // z.subs
     at = pl.ds(pl.multiple_of(sub * half, half), half)
+    lists = (first, second, ranks, occupied)
 
     def quarters(ref, base=0):
         return [ref.at[pl.ds(base + i * pairs, pairs)] for i in range(4)]
 
+    pack_copies = started(pack_in, [packs.at[i] for i in range(pack_count)], sems)
     small_copies = started(
         [c_in.at[:, :, at], c_other.at[:, :, at]]
         + [ref.at[:, pl.ds(0, n), at] for ref in (mp_in, mp_other, mp_below, mp_below_other)],
         [c_ref.at[pl.ds(0, pairs)], c_ref.at[pl.ds(pairs, pairs)]] + quarters(m_ref),
-        sems,
+        sems, 4,
     )
     large_copies = started(
         [right_in, right_other, left_in, left_other, left_below, left_below_other],
         [rhs.at[pl.ds(0, pairs)], rhs.at[pl.ds(pairs, pairs)]] + quarters(rhs, own),
-        sems, 6,
+        sems, 10,
     )
     diag_high[...] = jnp.zeros_like(diag_high)
     diag_low[...] = jnp.zeros_like(diag_low)
@@ -305,6 +282,25 @@
         def _(device):
             for p in range(pairs):
                 begin(device * pairs + p, starts[0][device, :, p * n : (p + 1) * n])
+
+    wait(pack_copies)
+    if small(z):
+        for index in range(pack_count):
+            side = sub if index < 2 else 1 - sub
+            which = fit if index % 2 == 0 else 1 - fit
+            for who in range(z.owners):
+                unpack(
+                    z, who * own + side * pairs + which,
+                    lambda start, size: packs[index, who, start : start + size, :], s_rows,
+                    index * z.owners + who, s_high, s_low, scale_ref, coupling_ref, lists,
+                )
+    else:
+        @pl.loop(0, z.total)
+        def _(pair):
+            unpack(
+                z, pair, lambda start, size: packs[0, pair, pl.ds(start, size), :], s_rows, 0,
+                s_high, s_low, scale_ref, coupling_ref, lists,
+            )
 
     def s_of(pair):
         return s_high[pair], s_low[pair]
@@ -394,7 +390,7 @@
         )
         window = pl.ds(start, step)
         copies += started(
-            [grad.at[:, :, window]], [grad_out.at[:, :, window]], sems, 12 + index
+            [grad.at[:, :, window]], [grad_out.at[:, :, window]], sems, 16 + index
         )
     wait(copies)
 
@@ -443,85 +439,63 @@
         limit=None,
     )
     mp_below = shifted(mp, "orb", 1)
+    left, right_here = call(
+        functools.partial(local_kernel, z),
+        [(pairs, n, fits), (pairs, n, fits)],
+        [smem, smem, vmem, vmem, vmem],
+        (pair_first, pair_second, pno_coefficients, mp, blocks),
+        limit=8,
+    )
+    (right_below,) = call(
+        functools.partial(below_kernel, z),
+        [(pairs, n, fits)],
+        [smem, vmem, vmem],
+        (pair_second, gate((mp_below,), left)[0], blocks),
+        limit=8,
+    )
+    down = shifted(right_below, "orb", -1)
+    late = gate((intersections, mp, left, pno_coefficients), right_below)
+    intersection, mp_late, left_late, coefficients = late
     (pack,) = call(
         functools.partial(pack_kernel, z),
         [pack_shape],
         [hbm] * 2,
-        (intersections, mp),
+        (intersection, mp_late),
         [
             scratch(*intersections.shape),
             scratch(pairs, EXTRA, z.paos),
             pltpu.SemaphoreType.DMA((2,)),
         ],
-        limit=None,
+        limit=8,
     )
     if small(z):
         packs = [lax.all_to_all(pack, "orb", 0, 0)]
     else:
         packs = [lax.all_gather(pack, ("orb", "sub"), axis=0, tiled=True)]
-    (right_below,) = call(
-        functools.partial(below_kernel, z),
-        [(pairs, n, fits)],
-        [hbm] * 4,
-        (pair_second, mp_below, blocks, pack),
-        [
-            pltpu.SMEM(pair_second.shape, jnp.int32),
-            scratch(pairs, n, z.paos),
-            scratch(pairs, *blocks.shape[1:]),
-            pltpu.SemaphoreType.DMA((1 + pairs,)),
-        ],
-        limit=None,
-    )
-    down = shifted(right_below, "orb", -1)
-    (coefficients,) = gate((pno_coefficients,), right_below)
-    left, right_here = call(
-        functools.partial(local_kernel, z),
-        [(pairs, n, fits), (pairs, n, fits)],
-        [smem, smem, vmem, vmem, vmem],
-        (pair_first, pair_second, coefficients, mp, blocks),
-        limit=8,
-        cost=BRIEF,
-    )
-    left_late, mp_late, coefficients = gate((left, mp, coefficients), right_here)
+    left_below = shifted(left_late, "orb", 1)
     mp_other = swapped(mp_late, "sub")
     left_other = swapped(left_late, "sub")
     c_other = swapped(coefficients, "sub")
-    if small(z):
-        packs.append(swapped(gate(packs, right_here)[0], "fit"))
-        packs += [swapped(value, "sub") for value in gate(packs, right_here)]
-    left_below = shifted(gate((left,), packs[1] if small(z) else right_here)[0], "orb", 1)
 
     lists = (pair_first, pair_second, pno_ranks)
-    split_shape = jax.ShapeDtypeStruct((z.total, n, wide), bf16)
-    unpacked = pl.pallas_call(
-        functools.partial(unpack_kernel, z),
-        out_shape=[
-            split_shape,
-            split_shape,
-            jax.ShapeDtypeStruct((z.total, n, n), jnp.float32),
-            jax.ShapeDtypeStruct((z.total, EXTRA, wide), jnp.float32),
-        ],
-        in_specs=[smem] * 4 + [vmem] * len(packs),
-        out_specs=[vmem] * 4,
-        scratch_shapes=[scratch(z.total if small(z) else 1, z.links // 2, n, 2 * n)],
-        cost_estimate=BRIEF,
-        compiler_params=pltpu.CompilerParams(vmem_limit_bytes=(16 + more) * MIB),
-    )(*lists, occ_energy, *packs)
-
+    (down,) = gate((down,), mp_other, left_other, c_other)
     part, right = call(
         functools.partial(sums_kernel, z),
         [(n, pairs * n), (pairs, n, fits)],
-        [smem] * 4 + [vmem] * 4 + [anywhere] * 4,
-        (*lists, occ_energy, mp, left, right_here, down, left_other, mp_other, c_other,
-         unpacked[0]),
+        [smem] * 4 + [vmem] * 4,
+        (*lists, occ_energy, mp, left, right_here, down),
         limit=8,
     )
+    (pack_late,) = gate(packs, part)
     if small(z):
+        packs = [pack_late, swapped(pack_late, "fit")]
+        packs.append(swapped(pack_late, "sub"))
         sums = part + swapped(part, "fit")
         start_amps = [
             lax.all_to_all(jnp.broadcast_to(sums[None], (z.owners, *sums.shape)), "orb", 0, 0)
         ]
         start_amps.append(swapped(start_amps[0], "sub"))
+        packs.append(swapped(gate(packs[1:2], start_amps[0])[0], "sub"))
     else:
         sums = lax.psum(part, "fit")
         start_amps = [lax.all_gather(sums, ("orb", "sub"), axis=0, tiled=False)]
@@ -533,18 +507,23 @@
     ]
 
     args = (
-        pair_first, pair_second, neighbours, *start_amps, *unpacked,
+        *lists, neighbours, occ_energy, *start_amps, *packs,
         pno_coefficients, c_other, mp, mp_other, mp_below, mp_below_other,
         left, left_other, left_below, left_below_other, right, right_other,
     )
-    group = own * 2
     square = (z.total, n, n)
     amplitudes, gradient = call(
         functools.partial(final_kernel, z),
         [(pairs, n * n), (z.orbitals, half, fits)],
-        [smem] * 3 + [vmem] * (len(start_amps) + 4) + [hbm] * 12,
+        [smem] * 5 + [vmem] * len(start_amps) + [hbm] * (12 + len(packs)),
         args,
         [
+            scratch(len(packs), *packs[0].shape),
+            scratch(z.total, n, wide, kind=bf16),
+            scratch(z.total, n, wide, kind=bf16),
+            scratch(*square),
+            scratch(z.total, EXTRA, wide),
+            scratch(z.total if small(z) else 1, z.links // 2, n, 2 * n),
             scratch(own, n, half),
             scratch(2 * own, n, half),
             scratch(3 * own, n, fits),
@@ -553,9 +532,9 @@
             scratch(*square),
         ]
         + [scratch(*square, kind=bf16)] * 4
-        + [scratch(group, wide, wide, kind=bf16)] * 2
+        + [scratch(2 * own, wide, wide, kind=bf16)] * 2
         + [scratch(z.orbitals * half, 3 * own * n, kind=bf16)] * 2
-        + [pltpu.SemaphoreType.DMA((12 + -(-fits // 256),))],
+        + [pltpu.SemaphoreType.DMA((16 + -(-fits // 256),))],
         limit=40 + more // 2,
         out_specs=[vmem, hbm],
     )

time: 77.9 us -> 67.4 us (0.87)
  waiting for transfers between devices: 22.5 us -> 13.2 us
  Pallas kernels: 19.7 us -> 16.8 us
  local copies, waits for them, and re-layouts: 8.9 us -> 10.4 us
    ppermute x11, waiting for transfers between devices: 10.9 us -> 2.36 us  [swapped(): return lax.ppermute(value, axis, [(0, 1), (1, 0)])]
    all_to_all x1, starting transfers between devices: 6.33 us -> 3.87 us  [body(): packs = [lax.all_to_all(pack, 'orb', 0, 0)]]
    ppermute x3, waiting for transfers between devices: 5.35 us -> 3.23 us  [shifted(): lax.ppermute(value, axis, [(source, source + steps) for source in range(i...]
    all_to_all x1, waiting for transfers between devices: 0.01 us -> 2.01 us  [body(): packs = [lax.all_to_all(pack, 'orb', 0, 0)]]
    ppermute x11, starting transfers between devices: 3.29 us -> 5.14 us  [swapped(): return lax.ppermute(value, axis, [(0, 1), (1, 0)])]
    pallas_call x6, Pallas kernels: 18.5 us -> 16.8 us  [call(): pl.pallas_call(kernel, out_shape=[jax.ShapeDtypeStruct(shape, jnp.float32...]
    unnamed x45 -> x41, local copies, waits for them, and re-layouts: 8.23 us -> 9.78 us
    pallas_call x1 -> x0, Pallas kernels: 1.16 us -> none  [body(): pl.pallas_call(functools.partial(unpack_kernel, z), out_shape=[split_shap...]
  transfers between devices with their start and end apart: 16 -> 16, of which waited for: 8 -> 5; matrix products, arithmetic and copies ran while one was open for 1% -> 1% of each run, Pallas kernels for 10% -> 6%
where the time goes in v8:
time: 67.4 us; the launch traced here: 66.8 us
  starting transfers between devices  25.6 us (38%)
  Pallas kernels  16.8 us (25%)
  waiting for transfers between devices  13.2 us (20%)
  local copies, waits for them, and re-layouts  10.4 us (15%)
  between operations  0.83 us (1%)
    pallas_call x6, Pallas kernels, call(): pl.pallas_call(kernel, out_shape=[jax.ShapeDtypeStruct(shape, jnp.float32...  16.8 us
    ppermute x3, starting transfers between devices, shifted(): lax.ppermute(value, axis, [(source, source + steps) for source in range(i...  10.9 us
    unnamed x41, local copies, waits for them, and re-layouts  9.78 us
    all_to_all x1, starting transfers between devices, body(): lax.all_to_all(jnp.broadcast_to(sums[None], (z.owners, *sums.shape)), 'or...  5.62 us
    all_to_all x1, waiting for transfers between devices, body(): lax.all_to_all(jnp.broadcast_to(sums[None], (z.owners, *sums.shape)), 'or...  5.58 us
    ppermute x11, starting transfers between devices, swapped(): return lax.ppermute(value, axis, [(0, 1), (1, 0)])  5.14 us
    all_to_all x1, starting transfers between devices, body(): packs = [lax.all_to_all(pack, 'orb', 0, 0)]  3.87 us
    ppermute x3, waiting for transfers between devices, shifted(): lax.ppermute(value, axis, [(source, source + steps) for source in range(i...  3.23 us
  transfers between devices with their start and end apart: 16, of which 5 were waited for; matrix products, arithmetic and copies ran while one was open for 1% of the time, Pallas kernels for 6%

profile of v8, /device:TPU:0, one launch (start us, length us, event | category | flops | bytes accessed | tf_op | source)
XLA Modules:
  0.0 66.8 jit_solution(2955956208925974657)
XLA Ops:
  0.6 0.0 copy-start.14
  0.6 1.9 %shard_map.122.mp_ref.mp_in.refs_8_ = f32[2,72,256]{2,1,0:T(8,128)} custom-call(f32[2,64,256]{2,1,0:T(8,128)} %refs_6_.1, s32[2,256]{1,0:T(2,128)} %map_in.1, f32[2,64]{1,0:T(2,128)} %e_in.1, f32[2,4]{1,0:T(2,128)} %coupling_in.1), custom_call_target="tpu_custom_call" | custom-call | flops 1 | bytes 1 | tf_op jit(solution)/shard_map/pallas_call | solution.py:58
  2.5 4.9 %collective-permute-start = (f32[2,72,256]{2,1,0:T(8,128)}, f32[2,72,256]{2,1,0:T(8,128)S(1)}, u32[]{:S(2)}, u32[]{:S(2)}) collective-permute-start(f32[2,72,256]{2,1,0:T(8,128)} %shard_map.122.mp_ref.mp_in.refs_8_), channel_id=1, source_target_pairs={{0,4},{4,8},{8,12},{1,5},{5,9},{9,13},{2,6},{6,10},{10,14},{3,7},{... | collective-permute-start | bytes 442376 | tf_op jit(solution)/shard_map/ppermute | solution.py:30
  7.5 0.0 copy-start
  7.5 1.6 %copy-done = f32[2,256,1024]{2,1,0:T(8,128)S(1)} copy-done((f32[2,256,1024]{2,1,0:T(8,128)S(1)}, f32[2,256,1024]{2,1,0:T(8,128)}, u32[]{:S(2)}) %copy-start) | copy-done | bytes 2097176
  9.1 0.9 %copy-done.2 = f32[2,72,256]{2,1,0:T(8,128)S(1)} copy-done((f32[2,72,256]{2,1,0:T(8,128)S(1)}, f32[2,72,256]{2,1,0:T(8,128)}, u32[]{:S(2)}) %copy-start.2) | copy-done | bytes 147480
  10.0 0.9 %copy-done.4 = f32[2,64,256]{2,1,0:T(8,128)S(1)} copy-done((f32[2,64,256]{2,1,0:T(8,128)S(1)}, f32[2,64,256]{2,1,0:T(8,128)}, u32[]{:S(2)}) %copy-start.4) | copy-done | bytes 131096
  10.9 0.7 copy-done.13
  11.6 0.7 copy-done.15
  12.2 1.9 %shard_map.123 = (f32[2,64,1024]{2,1,0:T(8,128)S(1)}, f32[2,64,1024]{2,1,0:T(8,128)S(1)}) custom-call(s32[16]{0:T(128)S(1)} %copy-done.15, s32[16]{0:T(128)S(1)} %copy-done.13, f32[2,64,256]{2,1,0:T(8,128)S(1)} %copy-done.4, f32[2,72,256]{2,1,0:T(8,128)S(1)} %copy-done.2, f32[2,256,1024]{2,1,0:T(8,128)S(1)} %copy-done), custom_call_target="tpu_custom_call" | custom-call | flops 1 | bytes 1 | tf_op jit(solution)/shard_map/pallas_call | solution.py:58
  14.1 0.0 copy-start.5
  14.2 0.0 copy-start.16
  14.2 0.0 copy-start.17
  14.2 0.0 copy-start.18
  14.2 0.0 collective-permute-done.mp_below.refs_10_
  14.2 2.1 %shard_map.124 = f32[2,64,1024]{2,1,0:T(8,128)} custom-call(s32[16]{0:T(128)S(1)} %copy-done.14, f32[2,72,256]{2,1,0:T(8,128)S(1)} %collective-permute-done.mp_below.refs_10_, f32[2,256,1024]{2,1,0:T(8,128)S(1)} %copy-done.1), custom_call_target="tpu_custom_call" | custom-call | flops 1 | bytes 1 | tf_op jit(solution)/shard_map/pallas_call | solution.py:58
  16.3 1.4 %collective-permute-start.1 = (f32[2,64,1024]{2,1,0:T(8,128)}, f32[2,64,1024]{2,1,0:T(8,128)S(1)}, u32[]{:S(2)}, u32[]{:S(2)}) collective-permute-start(f32[2,64,1024]{2,1,0:T(8,128)} %shard_map.124), channel_id=1, source_target_pairs={{4,0},{8,4},{12,8},{5,1},{9,5},{13,9},{6,2},{10,6},{14,10},{7,3},{... | collective-permute-start | bytes 1572872 | tf_op jit(solution)/shard_map/ppermute | solution.py:30
  17.7 4.6 %collective-permute-start.11 = (f32[2,64,1024]{2,1,0:T(8,128)S(1)}, f32[2,64,1024]{2,1,0:T(8,128)S(1)}, u32[]{:S(2)}, u32[]{:S(2)}) collective-permute-start(f32[2,64,1024]{2,1,0:T(8,128)S(1)} %get-tuple-element.21.left_ref.refs_12_), channel_id=1, source_target_pairs={{0,4},{4,8},{8,12},{1,5},{5,9},{9,13},{2,6},{6,10},{10,14},{3,7},{... | collective-permute-start | bytes 1572872 | tf_op jit(solution)/shard_map/ppermute | solution.py:30
  22.4 1.0 %shard_map.126 = f32[4,136,128]{2,1,0:T(8,128)} custom-call(f32[2,4,4096]{2,1,0:T(4,128)S(1)} %copy-done.10, f32[2,72,256]{2,1,0:T(8,128)S(1)} %copy-done.2), custom_call_target="tpu_custom_call" | custom-call | flops 1 | bytes 1 | tf_op jit(solution)/shard_map/pallas_call | solution.py:58
  23.3 3.9 %all-to-all-start.1 = ((f32[4,136,128]{2,1,0:T(8,128)}), f32[4,136,128]{2,1,0:T(8,128)S(1)}, u32[]{:S(2)}, u32[]{:S(2)}) async-start(f32[4,136,128]{2,1,0:T(8,128)} %shard_map.126), calls=%async_computation.1 | async-start | bytes 557056 | tf_op jit(solution)/shard_map/all_to_all | solution.py:472
  27.2 0.5 collective-permute-start.4
  27.7 1.0 %collective-permute-done.4.refs_7_ = f32[2,64,256]{2,1,0:T(8,128)S(1)} collective-permute-done((f32[2,64,256]{2,1,0:T(8,128)S(1)}, f32[2,64,256]{2,1,0:T(8,128)S(1)}, u32[]{:S(2)}, u32[]{:S(2)}) %collective-permute-start.4) | collective-permute-done | bytes 131104 | tf_op jit(solution)/shard_map/ppermute | solution.py:34
  28.8 0.6 copy-done.11
  29.4 0.0 collective-permute-done.2.refs_9_
  29.4 0.7 copy-done.8
  30.1 3.2 %collective-permute-done.1.down_ref = f32[2,64,1024]{2,1,0:T(8,128)S(1)} collective-permute-done((f32[2,64,1024]{2,1,0:T(8,128)}, f32[2,64,1024]{2,1,0:T(8,128)S(1)}, u32[]{:S(2)}, u32[]{:S(2)}) %collective-permute-start.1) | collective-permute-done | bytes 524320 | tf_op jit(solution)/shard_map/ppermute | solution.py:30
  33.3 0.8 %copy-done.6 = f32[2,64,1024]{2,1,0:T(8,128)} copy-done((f32[2,64,1024]{2,1,0:T(8,128)}, f32[2,64,1024]{2,1,0:T(8,128)S(1)}, u32[]{:S(2)}) %copy-start.6) | copy-done | bytes 524312
  34.1 1.0 %copy-done.7 = f32[2,64,1024]{2,1,0:T(8,128)S(1)} copy-done((f32[2,64,1024]{2,1,0:T(8,128)S(1)}, f32[2,64,1024]{2,1,0:T(8,128)}, u32[]{:S(2)}) %copy-start.7) | copy-done | bytes 524312
  35.1 1.0 %shard_map.125 = (f32[64,128]{1,0:T(8,128)S(1)}, f32[2,64,1024]{2,1,0:T(8,128)S(1)}) custom-call(s32[16]{0:T(128)S(1)} %copy-done.16, s32[16]{0:T(128)S(1)} %copy-done.14, s32[16]{0:T(128)S(1)} %copy-done.17, f32[8]{0:T(128)S(1)} %copy-done.18, f32[2,72,256]{2,1,0:T(8,128)S(1)} %copy-done.3, f32[2,64,1024]{2,1,0:T(8,128)S(1)} %get-tuple-element.21.left_ref.refs_12_, ...), custom_call_target="tpu_custom_call" | custom-call | flops 1 | bytes 1 | tf_op jit(solution)/shard_map/pallas_call | solution.py:58
  36.2 1.6 %collective-permute-start.5 = (f32[64,128]{1,0:T(8,128)S(1)}, f32[64,128]{1,0:T(8,128)S(1)}, u32[]{:S(2)}, u32[]{:S(2)}) collective-permute-start(f32[64,128]{1,0:T(8,128)S(1)} %get-tuple-element.24), channel_id=1, source_target_pairs={{0,2},{2,0},{1,3},{3,1},{4,6},{6,4},{5,7},{7,5},{8,10},{10,8},{9,1... | collective-permute-start | bytes 98312 | tf_op jit(solution)/shard_map/ppermute | solution.py:34
  37.7 2.0 %all-to-all-done.1.refs_2_ = f32[4,136,128]{2,1,0:T(8,128)S(1)} async-done(((f32[4,136,128]{2,1,0:T(8,128)}), f32[4,136,128]{2,1,0:T(8,128)S(1)}, u32[]{:S(2)}, u32[]{:S(2)}) %all-to-all-start.1) | async-done | bytes 278560 | tf_op jit(solution)/shard_map/all_to_all | solution.py:472
  39.7 1.5 %collective-permute-start.7 = (f32[4,136,128]{2,1,0:T(8,128)S(1)}, f32[4,136,128]{2,1,0:T(8,128)}, u32[]{:S(2)}, u32[]{:S(2)}) collective-permute-start(f32[4,136,128]{2,1,0:T(8,128)S(1)} %all-to-all-done.1.refs_2_), channel_id=1, source_target_pairs={{0,2},{2,0},{1,3},{3,1},{4,6},{6,4},{5,7},{7,5},{8,10},{10,8},{9,1... | collective-permute-start | bytes 835592 | tf_op jit(solution)/shard_map/ppermute | solution.py:34
  41.2 0.0 collective-permute-start.13
  41.2 0.0 collective-permute-done.5
  41.2 0.6 collective-permute-start.12
  41.8 0.7 broadcast_in_dim.2
  42.5 5.6 %all-to-all-start = ((f32[4,64,128]{2,1,0:T(8,128)}), f32[4,64,128]{2,1,0:T(8,128)S(1)}, u32[]{:S(2)}, u32[]{:S(2)}) async-start(f32[4,64,128]{2,1,0:T(8,128)} %broadcast_in_dim.2), calls=%async_computation | async-start | bytes 262144 | tf_op jit(solution)/shard_map/all_to_all | solution.py:495
  48.1 0.0 collective-permute-start.8
  48.1 0.5 collective-permute-start.10
  48.6 5.6 %all-to-all-done.refs_0_ = f32[4,64,128]{2,1,0:T(8,128)S(1)} async-done(((f32[4,64,128]{2,1,0:T(8,128)}), f32[4,64,128]{2,1,0:T(8,128)S(1)}, u32[]{:S(2)}, u32[]{:S(2)}) %all-to-all-start) | async-done | bytes 131104 | tf_op jit(solution)/shard_map/all_to_all | solution.py:495
  54.2 0.0 collective-permute-done.7.refs_3_
  54.2 0.5 collective-permute-start.6
  54.7 0.1 copy.13.near
  54.8 1.3 %collective-permute-done.6.refs_1_ = f32[4,64,128]{2,1,0:T(8,128)} collective-permute-done((f32[4,64,128]{2,1,0:T(8,128)S(1)}, f32[4,64,128]{2,1,0:T(8,128)}, u32[]{:S(2)}, u32[]{:S(2)}) %collective-permute-start.6) | collective-permute-done | bytes 131104 | tf_op jit(solution)/shard_map/ppermute | solution.py:34
  56.1 0.0 collective-permute-done.9.refs_5_
  56.1 0.9 %copy-done.9 = f32[2,72,256]{2,1,0:T(8,128)S(1)} copy-done((f32[2,72,256]{2,1,0:T(8,128)S(1)}, f32[2,72,256]{2,1,0:T(8,128)}, u32[]{:S(2)}) %copy-start.9) | copy-done | bytes 147480
  57.0 0.9 %copy-done.12 = f32[2,64,256]{2,1,0:T(8,128)S(1)} copy-done((f32[2,64,256]{2,1,0:T(8,128)S(1)}, f32[2,64,256]{2,1,0:T(8,128)}, u32[]{:S(2)}) %copy-start.12) | copy-done | bytes 131096
  57.9 8.9 %shard_map.127 = (f32[2,4096]{1,0:T(2,128)}, f32[2,128,1024]{2,1,0:T(8,128)}) custom-call(s32[16]{0:T(128)S(1)} %copy-done.16, s32[16]{0:T(128)S(1)} %copy-done.14, s32[16]{0:T(128)S(1)} %copy-done.17, s32[16,4]{1,0:T(8,128)S(1)} %copy.13.near, f32[8]{0:T(128)S(1)} %copy-done.18, f32[4,64,128]{2,1,0:T(8,128)S(1)} %all-to-all-done.refs_0_, ...), custom_call_target="tpu_custom_call" | custom-call | flops 1 | bytes 1 | tf_op jit(solution)/shard_map/pallas_call | solution.py:58
  (33 shorter events, 0.1 us)
Async XLA Ops:
  0.6 13.6 %copy-start.14 = (s32[16]{0:T(128)S(1)}, s32[16]{0:T(128)}, u32[]{:S(2)}) copy-start(s32[16]{0:T(128)} %second.7) | copy-start | bytes 196
  2.5 11.6 %collective-permute-start = (f32[2,72,256]{2,1,0:T(8,128)}, f32[2,72,256]{2,1,0:T(8,128)S(1)}, u32[]{:S(2)}, u32[]{:S(2)}) collective-permute-start(f32[2,72,256]{2,1,0:T(8,128)} %shard_map.122.mp_ref.mp_in.refs_8_), channel_id=1, source_target_pairs={{0,4},{4,8},{8,12},{1,5},{5,9},{9,13},{2,6},{6,10},{10,14},{3,7},{... | collective-permute-start | bytes 442376 | tf_op jit(solution)/shard_map/ppermute | solution.py:30
  7.5 1.6 %copy-start = (f32[2,256,1024]{2,1,0:T(8,128)S(1)}, f32[2,256,1024]{2,1,0:T(8,128)}, u32[]{:S(2)}) copy-start(f32[2,256,1024]{2,1,0:T(8,128)} %b_ref.3) | copy-start | bytes 6291460
  9.1 0.9 %copy-start.2 = (f32[2,72,256]{2,1,0:T(8,128)S(1)}, f32[2,72,256]{2,1,0:T(8,128)}, u32[]{:S(2)}) copy-start(f32[2,72,256]{2,1,0:T(8,128)} %shard_map.122.mp_ref.mp_in.refs_8_) | copy-start | bytes 442372
  10.0 0.9 %copy-start.4 = (f32[2,64,256]{2,1,0:T(8,128)S(1)}, f32[2,64,256]{2,1,0:T(8,128)}, u32[]{:S(2)}) copy-start(f32[2,64,256]{2,1,0:T(8,128)} %refs_6_.1) | copy-start | bytes 393220
  10.9 0.7 copy-start.13
  11.6 0.7 copy-start.15
  12.2 2.0 %copy-start.1 = (f32[2,256,1024]{2,1,0:T(8,128)S(1)}, f32[2,256,1024]{2,1,0:T(8,128)}, u32[]{:S(2)}) copy-start(f32[2,256,1024]{2,1,0:T(8,128)} %b_ref.3) | copy-start | bytes 6291460
  12.2 10.1 %copy-start.10 = (f32[2,4,4096]{2,1,0:T(4,128)S(1)}, f32[2,4,4096]{2,1,0:T(4,128)}, u32[]{:S(2)}) copy-start(f32[2,4,4096]{2,1,0:T(4,128)} %s_in) | copy-start | bytes 393220
  14.1 13.1 %copy-start.3 = (f32[2,72,256]{2,1,0:T(8,128)S(1)}, f32[2,72,256]{2,1,0:T(8,128)}, u32[]{:S(2)}) copy-start(f32[2,72,256]{2,1,0:T(8,128)} %shard_map.122.mp_ref.mp_in.refs_8_) | copy-start | bytes 442372
  14.1 13.1 %copy-start.5 = (f32[2,64,256]{2,1,0:T(8,128)S(1)}, f32[2,64,256]{2,1,0:T(8,128)}, u32[]{:S(2)}) copy-start(f32[2,64,256]{2,1,0:T(8,128)} %refs_6_.1) | copy-start | bytes 393220
  14.2 19.9 %copy-start.16 = (s32[16]{0:T(128)S(1)}, s32[16]{0:T(128)}, u32[]{:S(2)}) copy-start(s32[16]{0:T(128)} %first.5) | copy-start | bytes 196
  14.2 19.9 %copy-start.17 = (s32[16]{0:T(128)S(1)}, s32[16]{0:T(128)}, u32[]{:S(2)}) copy-start(s32[16]{0:T(128)} %ranks.3) | copy-start | bytes 196
  14.2 19.9 %copy-start.18 = (f32[8]{0:T(128)S(1)}, f32[8]{0:T(128)}, u32[]{:S(2)}) copy-start(f32[8]{0:T(128)} %occupied.3) | copy-start | bytes 100
  16.3 38.4 %copy-start.19 = (s32[16,4]{0,1:T(4,128)S(1)}, s32[16,4]{0,1:T(4,128)}, u32[]{:S(2)}) copy-start(s32[16,4]{0,1:T(4,128)} %param.17) | copy-start | bytes 772
  16.3 13.7 %collective-permute-start.3 = (f32[2,64,1024]{2,1,0:T(8,128)S(1)}, f32[2,64,1024]{2,1,0:T(8,128)S(1)}, u32[]{:S(2)}, u32[]{:S(2)}) collective-permute-start(f32[2,64,1024]{2,1,0:T(8,128)S(1)} %get-tuple-element.21.left_ref.refs_12_), channel_id=1, source_target_pairs={{0,1},{1,0},{2,3},{3,2},{4,5},{5,4},{6,7},{7,6},{8,9},{9,8},{10,11... | collective-permute-start | bytes 1572872 | tf_op jit(solution)/shard_map/ppermute | solution.py:34
  16.3 17.0 %collective-permute-start.1 = (f32[2,64,1024]{2,1,0:T(8,128)}, f32[2,64,1024]{2,1,0:T(8,128)S(1)}, u32[]{:S(2)}, u32[]{:S(2)}) collective-permute-start(f32[2,64,1024]{2,1,0:T(8,128)} %shard_map.124), channel_id=1, source_target_pairs={{4,0},{8,4},{12,8},{5,1},{9,5},{13,9},{6,2},{10,6},{14,10},{7,3},{... | collective-permute-start | bytes 1572872 | tf_op jit(solution)/shard_map/ppermute | solution.py:30
  17.7 23.5 %collective-permute-start.11 = (f32[2,64,1024]{2,1,0:T(8,128)S(1)}, f32[2,64,1024]{2,1,0:T(8,128)S(1)}, u32[]{:S(2)}, u32[]{:S(2)}) collective-permute-start(f32[2,64,1024]{2,1,0:T(8,128)S(1)} %get-tuple-element.21.left_ref.refs_12_), channel_id=1, source_target_pairs={{0,4},{4,8},{8,12},{1,5},{5,9},{9,13},{2,6},{6,10},{10,14},{3,7},{... | collective-permute-start | bytes 1572872 | tf_op jit(solution)/shard_map/ppermute | solution.py:30
  23.3 16.4 %all-to-all-start.1 = ((f32[4,136,128]{2,1,0:T(8,128)}), f32[4,136,128]{2,1,0:T(8,128)S(1)}, u32[]{:S(2)}, u32[]{:S(2)}) async-start(f32[4,136,128]{2,1,0:T(8,128)} %shard_map.126), calls=%async_computation.1 | async-start | bytes 557056 | tf_op jit(solution)/shard_map/all_to_all | solution.py:472
  27.2 2.2 %collective-permute-start.2 = (f32[2,72,256]{2,1,0:T(8,128)S(1)}, f32[2,72,256]{2,1,0:T(8,128)S(1)}, u32[]{:S(2)}, u32[]{:S(2)}) collective-permute-start(f32[2,72,256]{2,1,0:T(8,128)S(1)} %copy-done.3), channel_id=1, source_target_pairs={{0,1},{1,0},{2,3},{3,2},{4,5},{5,4},{6,7},{7,6},{8,9},{9,8},{10,11... | collective-permute-start | bytes 442376 | tf_op jit(solution)/shard_map/ppermute | solution.py:34
  27.2 1.5 %collective-permute-start.4 = (f32[2,64,256]{2,1,0:T(8,128)S(1)}, f32[2,64,256]{2,1,0:T(8,128)S(1)}, u32[]{:S(2)}, u32[]{:S(2)}) collective-permute-start(f32[2,64,256]{2,1,0:T(8,128)S(1)} %copy-done.5), channel_id=1, source_target_pairs={{0,1},{1,0},{2,3},{3,2},{4,5},{5,4},{6,7},{7,6},{8,9},{9,8},{10,11... | collective-permute-start | bytes 393224 | tf_op jit(solution)/shard_map/ppermute | solution.py:34
  28.8 0.6 copy-start.11
  29.4 0.7 copy-start.8
  33.3 0.8 %copy-start.6 = (f32[2,64,1024]{2,1,0:T(8,128)}, f32[2,64,1024]{2,1,0:T(8,128)S(1)}, u32[]{:S(2)}) copy-start(f32[2,64,1024]{2,1,0:T(8,128)S(1)} %collective-permute-done.1.down_ref) | copy-start | bytes 1572868
  34.1 1.0 %copy-start.7 = (f32[2,64,1024]{2,1,0:T(8,128)S(1)}, f32[2,64,1024]{2,1,0:T(8,128)}, u32[]{:S(2)}) copy-start(f32[2,64,1024]{2,1,0:T(8,128)} %copy-done.6) | copy-start | bytes 1572868
  36.2 5.1 %collective-permute-start.5 = (f32[64,128]{1,0:T(8,128)S(1)}, f32[64,128]{1,0:T(8,128)S(1)}, u32[]{:S(2)}, u32[]{:S(2)}) collective-permute-start(f32[64,128]{1,0:T(8,128)S(1)} %get-tuple-element.24), channel_id=1, source_target_pairs={{0,2},{2,0},{1,3},{3,1},{4,6},{6,4},{5,7},{7,5},{8,10},{10,8},{9,1... | collective-permute-start | bytes 98312 | tf_op jit(solution)/shard_map/ppermute | solution.py:34
  39.7 14.5 %collective-permute-start.7 = (f32[4,136,128]{2,1,0:T(8,128)S(1)}, f32[4,136,128]{2,1,0:T(8,128)}, u32[]{:S(2)}, u32[]{:S(2)}) collective-permute-start(f32[4,136,128]{2,1,0:T(8,128)S(1)} %all-to-all-done.1.refs_2_), channel_id=1, source_target_pairs={{0,2},{2,0},{1,3},{3,1},{4,6},{6,4},{5,7},{7,5},{8,10},{10,8},{9,1... | collective-permute-start | bytes 835592 | tf_op jit(solution)/shard_map/ppermute | solution.py:34
  41.2 14.9 %collective-permute-start.13 = (f32[2,64,1024]{2,1,0:T(8,128)S(1)}, f32[2,64,1024]{2,1,0:T(8,128)S(1)}, u32[]{:S(2)}, u32[]{:S(2)}) collective-permute-start(f32[2,64,1024]{2,1,0:T(8,128)S(1)} %get-tuple-element.31.refs_16_), channel_id=1, source_target_pairs={{0,1},{1,0},{2,3},{3,2},{4,5},{5,4},{6,7},{7,6},{8,9},{9,8},{10,11... | collective-permute-start | bytes 1572872 | tf_op jit(solution)/shard_map/ppermute | solution.py:34
  41.2 14.8 %collective-permute-start.12 = (f32[2,64,1024]{2,1,0:T(8,128)S(1)}, f32[2,64,1024]{2,1,0:T(8,128)}, u32[]{:S(2)}, u32[]{:S(2)}) collective-permute-start(f32[2,64,1024]{2,1,0:T(8,128)S(1)} %collective-permute-done.11.refs_14_), channel_id=1, source_target_pairs={{0,1},{1,0},{2,3},{3,2},{4,5},{5,4},{6,7},{7,6},{8,9},{9,8},{10,11... | collective-permute-start | bytes 1572872 | tf_op jit(solution)/shard_map/ppermute | solution.py:34
  42.5 11.7 %all-to-all-start = ((f32[4,64,128]{2,1,0:T(8,128)}), f32[4,64,128]{2,1,0:T(8,128)S(1)}, u32[]{:S(2)}, u32[]{:S(2)}) async-start(f32[4,64,128]{2,1,0:T(8,128)} %broadcast_in_dim.2), calls=%async_computation | async-start | bytes 262144 | tf_op jit(solution)/shard_map/all_to_all | solution.py:495
  48.1 6.7 %collective-permute-start.8 = (f32[4,136,128]{2,1,0:T(8,128)S(1)}, f32[4,136,128]{2,1,0:T(8,128)}, u32[]{:S(2)}, u32[]{:S(2)}) collective-permute-start(f32[4,136,128]{2,1,0:T(8,128)S(1)} %all-to-all-done.1.refs_2_), channel_id=1, source_target_pairs={{0,1},{1,0},{2,3},{3,2},{4,5},{5,4},{6,7},{7,6},{8,9},{9,8},{10,11... | collective-permute-start | bytes 835592 | tf_op jit(solution)/shard_map/ppermute | solution.py:34
  48.1 6.1 %collective-permute-start.10 = (f32[2,72,256]{2,1,0:T(8,128)S(1)}, f32[2,72,256]{2,1,0:T(8,128)}, u32[]{:S(2)}, u32[]{:S(2)}) collective-permute-start(f32[2,72,256]{2,1,0:T(8,128)S(1)} %collective-permute-done.mp_below.refs_10_), channel_id=1, source_target_pairs={{0,1},{1,0},{2,3},{3,2},{4,5},{5,4},{6,7},{7,6},{8,9},{9,8},{10,11... | collective-permute-start | bytes 442376 | tf_op jit(solution)/shard_map/ppermute | solution.py:34
  54.2 1.9 %collective-permute-start.9 = (f32[4,136,128]{2,1,0:T(8,128)}, f32[4,136,128]{2,1,0:T(8,128)}, u32[]{:S(2)}, u32[]{:S(2)}) collective-permute-start(f32[4,136,128]{2,1,0:T(8,128)} %collective-permute-done.7.refs_3_), channel_id=1, source_target_pairs={{0,1},{1,0},{2,3},{3,2},{4,5},{5,4},{6,7},{7,6},{8,9},{9,8},{10,11... | collective-permute-start | bytes 835592 | tf_op jit(solution)/shard_map/ppermute | solution.py:34
  54.2 1.9 %collective-permute-start.6 = (f32[4,64,128]{2,1,0:T(8,128)S(1)}, f32[4,64,128]{2,1,0:T(8,128)}, u32[]{:S(2)}, u32[]{:S(2)}) collective-permute-start(f32[4,64,128]{2,1,0:T(8,128)S(1)} %all-to-all-done.refs_0_), channel_id=1, source_target_pairs={{0,1},{1,0},{2,3},{3,2},{4,5},{5,4},{6,7},{7,6},{8,9},{9,8},{10,11... | collective-permute-start | bytes 393224 | tf_op jit(solution)/shard_map/ppermute | solution.py:34
  56.1 0.9 %copy-start.9 = (f32[2,72,256]{2,1,0:T(8,128)S(1)}, f32[2,72,256]{2,1,0:T(8,128)}, u32[]{:S(2)}) copy-start(f32[2,72,256]{2,1,0:T(8,128)} %copy-done.8) | copy-start | bytes 442372
  57.0 0.9 %copy-start.12 = (f32[2,64,256]{2,1,0:T(8,128)S(1)}, f32[2,64,256]{2,1,0:T(8,128)}, u32[]{:S(2)}) copy-start(f32[2,64,256]{2,1,0:T(8,128)} %copy-done.11) | copy-start | bytes 393220

commit v9 on v8

--- a/solution.py
+++ b/solution.py
@@ -439,23 +439,23 @@
         limit=None,
     )
     mp_below = shifted(mp, "orb", 1)
+    (right_below,) = call(
+        functools.partial(below_kernel, z),
+        [(pairs, n, fits)],
+        [smem, vmem, vmem],
+        (pair_second, mp_below, blocks),
+        limit=8,
+    )
+    down = shifted(right_below, "orb", -1)
+    late = gate((intersections, mp, pno_coefficients), right_below)
+    intersection, mp_late, coefficients = late
     left, right_here = call(
         functools.partial(local_kernel, z),
         [(pairs, n, fits), (pairs, n, fits)],
         [smem, smem, vmem, vmem, vmem],
-        (pair_first, pair_second, pno_coefficients, mp, blocks),
+        (pair_first, pair_second, coefficients, mp_late, blocks),
         limit=8,
     )
-    (right_below,) = call(
-        functools.partial(below_kernel, z),
-        [(pairs, n, fits)],
-        [smem, vmem, vmem],
-        (pair_second, gate((mp_below,), left)[0], blocks),
-        limit=8,
-    )
-    down = shifted(right_below, "orb", -1)
-    late = gate((intersections, mp, left, pno_coefficients), right_below)
-    intersection, mp_late, left_late, coefficients = late
     (pack,) = call(
         functools.partial(pack_kernel, z),
         [pack_shape],
@@ -472,13 +472,13 @@
         packs = [lax.all_to_all(pack, "orb", 0, 0)]
     else:
         packs = [lax.all_gather(pack, ("orb", "sub"), axis=0, tiled=True)]
-    left_below = shifted(left_late, "orb", 1)
+    left_below = shifted(gate((left,), pack)[0], "orb", 1)
     mp_other = swapped(mp_late, "sub")
-    left_other = swapped(left_late, "sub")
+    left_other = swapped(left, "sub")
     c_other = swapped(coefficients, "sub")
 
     lists = (pair_first, pair_second, pno_ranks)
-    (down,) = gate((down,), mp_other, left_other, c_other)
+    (down,) = gate((down,), packs[0], mp_other, left_other, c_other)
     part, right = call(
         functools.partial(sums_kernel, z),
         [(n, pairs * n), (pairs, n, fits)],
@@ -535,7 +535,7 @@
         + [scratch(2 * own, wide, wide, kind=bf16)] * 2
         + [scratch(z.orbitals * half, 3 * own * n, kind=bf16)] * 2
         + [pltpu.SemaphoreType.DMA((16 + -(-fits // 256),))],
-        limit=40 + more // 2,
+        limit=60,
         out_specs=[vmem, hbm],
     )
     return (amplitudes, gradient)

time: 67.4 us -> 72.5 us (1.076)
  waiting for transfers between devices: 13.2 us -> 23.8 us
  local copies, waits for them, and re-layouts: 10.4 us -> 4.5 us
  starting transfers between devices: 25.6 us -> 26.7 us
    all_to_all x1, waiting for transfers between devices: 2.01 us -> 10.5 us  [body(): packs = [lax.all_to_all(pack, 'orb', 0, 0)]]
    unnamed x41 -> x45, local copies, waits for them, and re-layouts: 9.78 us -> 3.83 us
    all_to_all x1, starting transfers between devices: 5.62 us -> 7.45 us  [body(): lax.all_to_all(jnp.broadcast_to(sums[None], (z.owners, *sums.shape)), 'or...]
    ppermute x11, waiting for transfers between devices: 2.36 us -> 3.97 us  [swapped(): return lax.ppermute(value, axis, [(0, 1), (1, 0)])]
    ppermute x11, starting transfers between devices: 5.14 us -> 3.75 us  [swapped(): return lax.ppermute(value, axis, [(0, 1), (1, 0)])]
    ppermute x3, starting transfers between devices: 10.9 us -> 11.9 us  [shifted(): lax.ppermute(value, axis, [(source, source + steps) for source in range(i...]
  transfers between devices with their start and end apart: 16 -> 16, of which waited for: 5 -> 7; matrix products, arithmetic and copies ran while one was open for 1% -> 2% of each run, Pallas kernels for 6% -> 5%
where the time goes in v9:
time: 72.5 us; the launch traced here: 72.1 us
  starting transfers between devices  26.7 us (37%)
  waiting for transfers between devices  23.8 us (33%)
  Pallas kernels  16.2 us (22%)
  local copies, waits for them, and re-layouts  4.5 us (6%)
  between operations  0.93 us (1%)
    pallas_call x6, Pallas kernels, call(): pl.pallas_call(kernel, out_shape=[jax.ShapeDtypeStruct(shape, jnp.float32...  16.2 us
    ppermute x3, starting transfers between devices, shifted(): lax.ppermute(value, axis, [(source, source + steps) for source in range(i...  11.9 us
    all_to_all x1, waiting for transfers between devices, body(): packs = [lax.all_to_all(pack, 'orb', 0, 0)]  10.5 us
    all_to_all x1, starting transfers between devices, body(): lax.all_to_all(jnp.broadcast_to(sums[None], (z.owners, *sums.shape)), 'or...  7.45 us
    all_to_all x1, waiting for transfers between devices, body(): lax.all_to_all(jnp.broadcast_to(sums[None], (z.owners, *sums.shape)), 'or...  5.91 us
    ppermute x11, waiting for transfers between devices, swapped(): return lax.ppermute(value, axis, [(0, 1), (1, 0)])  3.97 us
    unnamed x45, local copies, waits for them, and re-layouts  3.83 us
    ppermute x11, starting transfers between devices, swapped(): return lax.ppermute(value, axis, [(0, 1), (1, 0)])  3.75 us
  transfers between devices with their start and end apart: 16, of which 7 were waited for; matrix products, arithmetic and copies ran while one was open for 2% of the time, Pallas kernels for 5%

profile of v9, /device:TPU:0, one launch (start us, length us, event | category | flops | bytes accessed | tf_op | source)
XLA Modules:
  0.0 72.1 jit_solution(4745986915026761156)
XLA Ops:
  0.6 0.0 copy-start.4
  0.6 0.0 copy-start.9
  0.7 0.0 copy-start.10
  0.7 2.0 %shard_map.122.mp_ref.mp_in.refs_8_ = f32[2,72,256]{2,1,0:T(8,128)} custom-call(f32[2,64,256]{2,1,0:T(8,128)} %refs_6_.1, s32[2,256]{1,0:T(2,128)} %map_in.1, f32[2,64]{1,0:T(2,128)} %e_in.1, f32[2,4]{1,0:T(2,128)} %coupling_in.1), custom_call_target="tpu_custom_call" | custom-call | flops 1 | bytes 1 | tf_op jit(solution)/shard_map/pallas_call | solution.py:58
  2.7 4.9 %collective-permute-start = (f32[2,72,256]{2,1,0:T(8,128)}, f32[2,72,256]{2,1,0:T(8,128)S(1)}, u32[]{:S(2)}, u32[]{:S(2)}) collective-permute-start(f32[2,72,256]{2,1,0:T(8,128)} %shard_map.122.mp_ref.mp_in.refs_8_), channel_id=1, source_target_pairs={{0,4},{4,8},{8,12},{1,5},{5,9},{9,13},{2,6},{6,10},{10,14},{3,7},{... | collective-permute-start | bytes 442376 | tf_op jit(solution)/shard_map/ppermute | solution.py:30
  7.6 3.4 %collective-permute-done.mp_below.refs_10_ = f32[2,72,256]{2,1,0:T(8,128)S(1)} collective-permute-done((f32[2,72,256]{2,1,0:T(8,128)}, f32[2,72,256]{2,1,0:T(8,128)S(1)}, u32[]{:S(2)}, u32[]{:S(2)}) %collective-permute-start) | collective-permute-done | bytes 147488 | tf_op jit(solution)/shard_map/ppermute | solution.py:30
  11.0 1.6 %copy-done = f32[2,256,1024]{2,1,0:T(8,128)S(1)} copy-done((f32[2,256,1024]{2,1,0:T(8,128)S(1)}, f32[2,256,1024]{2,1,0:T(8,128)}, u32[]{:S(2)}) %copy-start) | copy-done | bytes 2097176
  12.6 0.7 copy-done.8
  13.3 1.3 %shard_map.123 = f32[2,64,1024]{2,1,0:T(8,128)S(1)} custom-call(s32[16]{0:T(128)S(1)} %copy-done.8, f32[2,72,256]{2,1,0:T(8,128)S(1)} %collective-permute-done.mp_below.refs_10_, f32[2,256,1024]{2,1,0:T(8,128)S(1)} %copy-done), custom_call_target="tpu_custom_call" | custom-call | flops 1 | bytes 1 | tf_op jit(solution)/shard_map/pallas_call | solution.py:58
  14.6 0.0 copy-start.11
  14.6 0.0 copy-start.12
  14.6 1.3 %collective-permute-start.1 = (f32[2,64,1024]{2,1,0:T(8,128)S(1)}, f32[2,64,1024]{2,1,0:T(8,128)S(1)}, u32[]{:S(2)}, u32[]{:S(2)}) collective-permute-start(f32[2,64,1024]{2,1,0:T(8,128)S(1)} %shard_map.123), channel_id=1, source_target_pairs={{4,0},{8,4},{12,8},{5,1},{9,5},{13,9},{6,2},{10,6},{14,10},{7,3},{... | collective-permute-start | bytes 1572872 | tf_op jit(solution)/shard_map/ppermute | solution.py:30
  15.9 1.9 %shard_map.124 = (f32[2,64,1024]{2,1,0:T(8,128)S(1)}, f32[2,64,1024]{2,1,0:T(8,128)S(1)}) custom-call(s32[16]{0:T(128)S(1)} %copy-done.10, s32[16]{0:T(128)S(1)} %copy-done.9, f32[2,64,256]{2,1,0:T(8,128)S(1)} %copy-done.4, f32[2,72,256]{2,1,0:T(8,128)S(1)} %copy-done.2, f32[2,256,1024]{2,1,0:T(8,128)S(1)} %copy-done.1), custom_call_target="tpu_custom_call" | custom-call | flops 1 | bytes 1 | tf_op jit(solution)/shard_map/pallas_call | solution.py:58
  17.9 0.0 copy-start.21
  17.9 0.1 collective-permute-start.3
  18.0 1.0 %shard_map.125 = f32[4,136,128]{2,1,0:T(8,128)} custom-call(f32[2,4,4096]{2,1,0:T(4,128)S(1)} %copy-done.7, f32[2,72,256]{2,1,0:T(8,128)S(1)} %copy-done.2), custom_call_target="tpu_custom_call" | custom-call | flops 1 | bytes 1 | tf_op jit(solution)/shard_map/pallas_call | solution.py:58
  18.9 5.7 %collective-permute-start.11 = (f32[2,64,1024]{2,1,0:T(8,128)S(1)}, f32[2,64,1024]{2,1,0:T(8,128)}, u32[]{:S(2)}, u32[]{:S(2)}) collective-permute-start(f32[2,64,1024]{2,1,0:T(8,128)S(1)} %get-tuple-element.27.left_ref.refs_12_), channel_id=1, source_target_pairs={{0,4},{4,8},{8,12},{1,5},{5,9},{9,13},{2,6},{6,10},{10,14},{3,7},{... | collective-permute-start | bytes 1572872 | tf_op jit(solution)/shard_map/ppermute | solution.py:30
  24.7 3.6 %all-to-all-start = ((f32[4,136,128]{2,1,0:T(8,128)}), f32[4,136,128]{2,1,0:T(8,128)S(1)}, u32[]{:S(2)}, u32[]{:S(2)}) async-start(f32[4,136,128]{2,1,0:T(8,128)} %shard_map.125), calls=%async_computation | async-start | bytes 557056 | tf_op jit(solution)/shard_map/all_to_all | solution.py:472
  28.2 0.2 collective-permute-start.2
  28.4 0.4 collective-permute-start.4
  28.7 1.0 %collective-permute-done.4.refs_7_ = f32[2,64,256]{2,1,0:T(8,128)S(1)} collective-permute-done((f32[2,64,256]{2,1,0:T(8,128)S(1)}, f32[2,64,256]{2,1,0:T(8,128)S(1)}, u32[]{:S(2)}, u32[]{:S(2)}) %collective-permute-start.4) | collective-permute-done | bytes 131104 | tf_op jit(solution)/shard_map/ppermute | solution.py:34
  29.8 0.0 collective-permute-done.2.refs_9_
  29.8 10.5 %all-to-all-done.refs_2_ = f32[4,136,128]{2,1,0:T(8,128)S(1)} async-done(((f32[4,136,128]{2,1,0:T(8,128)}), f32[4,136,128]{2,1,0:T(8,128)S(1)}, u32[]{:S(2)}, u32[]{:S(2)}) %all-to-all-start) | async-done | bytes 278560 | tf_op jit(solution)/shard_map/all_to_all | solution.py:472
  40.3 0.0 collective-permute-done.1.down_ref
  40.3 0.0 collective-permute-done.3.refs_13_
  40.3 1.0 %shard_map.126 = (f32[64,128]{1,0:T(8,128)S(1)}, f32[2,64,1024]{2,1,0:T(8,128)S(1)}) custom-call(s32[16]{0:T(128)S(1)} %copy-done.10, s32[16]{0:T(128)S(1)} %copy-done.9, s32[16]{0:T(128)S(1)} %copy-done.11, f32[8]{0:T(128)S(1)} %copy-done.12, f32[2,72,256]{2,1,0:T(8,128)S(1)} %copy-done.2, f32[2,64,1024]{2,1,0:T(8,128)S(1)} %get-tuple-element.27.left_ref.refs_12_, ...), custom_call_target="tpu_custom_call" | custom-call | flops 1 | bytes 1 | tf_op jit(solution)/shard_map/pallas_call | solution.py:58
  41.3 1.6 %collective-permute-start.5 = (f32[64,128]{1,0:T(8,128)S(1)}, f32[64,128]{1,0:T(8,128)S(1)}, u32[]{:S(2)}, u32[]{:S(2)}) collective-permute-start(f32[64,128]{1,0:T(8,128)S(1)} %get-tuple-element.22), channel_id=1, source_target_pairs={{0,2},{2,0},{1,3},{3,1},{4,6},{6,4},{5,7},{7,5},{8,10},{10,8},{9,1... | collective-permute-start | bytes 98312 | tf_op jit(solution)/shard_map/ppermute | solution.py:34
  42.9 0.5 collective-permute-start.7
  43.4 0.0 collective-permute-start.13
  43.4 2.2 %collective-permute-done.5 = f32[64,128]{1,0:T(8,128)S(1)} collective-permute-done((f32[64,128]{1,0:T(8,128)S(1)}, f32[64,128]{1,0:T(8,128)S(1)}, u32[]{:S(2)}, u32[]{:S(2)}) %collective-permute-start.5) | collective-permute-done | bytes 32800 | tf_op jit(solution)/shard_map/ppermute | solution.py:34
  45.7 0.0 collective-permute-done.11.refs_14_
  45.7 0.1 collective-permute-start.12
  45.8 0.7 broadcast_in_dim.2
  46.4 7.4 %all-to-all-start.1 = ((f32[4,64,128]{2,1,0:T(8,128)}), f32[4,64,128]{2,1,0:T(8,128)S(1)}, u32[]{:S(2)}, u32[]{:S(2)}) async-start(f32[4,64,128]{2,1,0:T(8,128)} %broadcast_in_dim.2), calls=%async_computation.1 | async-start | bytes 262144 | tf_op jit(solution)/shard_map/all_to_all | solution.py:495
  53.9 0.2 collective-permute-start.8
  54.1 0.3 collective-permute-start.10
  54.4 5.9 %all-to-all-done.1.refs_0_ = f32[4,64,128]{2,1,0:T(8,128)S(1)} async-done(((f32[4,64,128]{2,1,0:T(8,128)}), f32[4,64,128]{2,1,0:T(8,128)S(1)}, u32[]{:S(2)}, u32[]{:S(2)}) %all-to-all-start.1) | async-done | bytes 131104 | tf_op jit(solution)/shard_map/all_to_all | solution.py:495
  60.3 0.0 collective-permute-done.7.refs_3_
  60.3 0.0 collective-permute-start.9
  60.3 0.0 collective-permute-done.10.refs_11_
  60.3 0.5 collective-permute-start.6
  60.8 0.7 copy.13.near
  61.5 0.5 collective-permute-done.6.refs_1_
  62.1 0.1 collective-permute-done.9.refs_5_
  62.3 0.5 copy-done.20
  62.7 0.2 copy-done.15
  62.9 0.2 copy-done.16
  63.1 9.0 %shard_map.127 = (f32[2,4096]{1,0:T(2,128)}, f32[2,128,1024]{2,1,0:T(8,128)}) custom-call(s32[16]{0:T(128)} %first.5, s32[16]{0:T(128)} %second.7, s32[16]{0:T(128)} %ranks.3, s32[16,4]{1,0:T(8,128)} %copy.13.near, f32[8]{0:T(128)} %occupied.3, f32[4,64,128]{2,1,0:T(8,128)} %copy-done.17, f32[4,64,128]{2,1,0:T(8,128)} %copy-done.20, ...), custom_call_target="tpu_custom_call" | custom-call | flops 1 | bytes 1 | tf_op jit(solution)/shard_map/pallas_call | solution.py:58
  (37 shorter events, 0.1 us)
Async XLA Ops:
  0.6 15.3 %copy-start.4 = (f32[2,64,256]{2,1,0:T(8,128)S(1)}, f32[2,64,256]{2,1,0:T(8,128)}, u32[]{:S(2)}) copy-start(f32[2,64,256]{2,1,0:T(8,128)} %refs_6_.1) | copy-start | bytes 393220
  0.6 15.3 %copy-start.9 = (s32[16]{0:T(128)S(1)}, s32[16]{0:T(128)}, u32[]{:S(2)}) copy-start(s32[16]{0:T(128)} %second.7) | copy-start | bytes 196
  0.7 15.3 %copy-start.10 = (s32[16]{0:T(128)S(1)}, s32[16]{0:T(128)}, u32[]{:S(2)}) copy-start(s32[16]{0:T(128)} %first.5) | copy-start | bytes 196
  0.7 17.3 %copy-start.7 = (f32[2,4,4096]{2,1,0:T(4,128)S(1)}, f32[2,4,4096]{2,1,0:T(4,128)}, u32[]{:S(2)}) copy-start(f32[2,4,4096]{2,1,0:T(4,128)} %s_in) | copy-start | bytes 393220
  2.7 8.3 %collective-permute-start = (f32[2,72,256]{2,1,0:T(8,128)}, f32[2,72,256]{2,1,0:T(8,128)S(1)}, u32[]{:S(2)}, u32[]{:S(2)}) collective-permute-start(f32[2,72,256]{2,1,0:T(8,128)} %shard_map.122.mp_ref.mp_in.refs_8_), channel_id=1, source_target_pairs={{0,4},{4,8},{8,12},{1,5},{5,9},{9,13},{2,6},{6,10},{10,14},{3,7},{... | collective-permute-start | bytes 442376 | tf_op jit(solution)/shard_map/ppermute | solution.py:30
  11.0 1.6 %copy-start = (f32[2,256,1024]{2,1,0:T(8,128)S(1)}, f32[2,256,1024]{2,1,0:T(8,128)}, u32[]{:S(2)}) copy-start(f32[2,256,1024]{2,1,0:T(8,128)} %b_ref.3) | copy-start | bytes 6291460
  12.6 0.7 copy-start.8
  13.3 40.8 %copy-start.5 = (f32[2,72,256]{2,1,0:T(8,128)}, f32[2,72,256]{2,1,0:T(8,128)S(1)}, u32[]{:S(2)}) copy-start(f32[2,72,256]{2,1,0:T(8,128)S(1)} %collective-permute-done.mp_below.refs_10_) | copy-start | bytes 442372
  13.3 2.7 %copy-start.1 = (f32[2,256,1024]{2,1,0:T(8,128)S(1)}, f32[2,256,1024]{2,1,0:T(8,128)}, u32[]{:S(2)}) copy-start(f32[2,256,1024]{2,1,0:T(8,128)} %b_ref.3) | copy-start | bytes 6291460
  13.3 2.7 %copy-start.2 = (f32[2,72,256]{2,1,0:T(8,128)S(1)}, f32[2,72,256]{2,1,0:T(8,128)}, u32[]{:S(2)}) copy-start(f32[2,72,256]{2,1,0:T(8,128)} %shard_map.122.mp_ref.mp_in.refs_8_) | copy-start | bytes 442372
  14.6 25.7 %copy-start.11 = (s32[16]{0:T(128)S(1)}, s32[16]{0:T(128)}, u32[]{:S(2)}) copy-start(s32[16]{0:T(128)} %ranks.3) | copy-start | bytes 196
  14.6 25.7 %copy-start.12 = (f32[8]{0:T(128)S(1)}, f32[8]{0:T(128)}, u32[]{:S(2)}) copy-start(f32[8]{0:T(128)} %occupied.3) | copy-start | bytes 100
  14.6 25.7 %collective-permute-start.1 = (f32[2,64,1024]{2,1,0:T(8,128)S(1)}, f32[2,64,1024]{2,1,0:T(8,128)S(1)}, u32[]{:S(2)}, u32[]{:S(2)}) collective-permute-start(f32[2,64,1024]{2,1,0:T(8,128)S(1)} %shard_map.123), channel_id=1, source_target_pairs={{4,0},{8,4},{12,8},{5,1},{9,5},{13,9},{6,2},{10,6},{14,10},{7,3},{... | collective-permute-start | bytes 1572872 | tf_op jit(solution)/shard_map/ppermute | solution.py:30
  17.9 44.3 %copy-start.3 = (f32[2,64,1024]{2,1,0:T(8,128)}, f32[2,64,1024]{2,1,0:T(8,128)S(1)}, u32[]{:S(2)}) copy-start(f32[2,64,1024]{2,1,0:T(8,128)S(1)} %get-tuple-element.27.left_ref.refs_12_) | copy-start | bytes 1572868
  17.9 43.0 %copy-start.21 = (s32[16,4]{0,1:T(4,128)S(1)}, s32[16,4]{0,1:T(4,128)}, u32[]{:S(2)}) copy-start(s32[16,4]{0,1:T(4,128)} %param.17) | copy-start | bytes 772
  17.9 22.4 %collective-permute-start.3 = (f32[2,64,1024]{2,1,0:T(8,128)S(1)}, f32[2,64,1024]{2,1,0:T(8,128)S(1)}, u32[]{:S(2)}, u32[]{:S(2)}) collective-permute-start(f32[2,64,1024]{2,1,0:T(8,128)S(1)} %get-tuple-element.27.left_ref.refs_12_), channel_id=1, source_target_pairs={{0,1},{1,0},{2,3},{3,2},{4,5},{5,4},{6,7},{7,6},{8,9},{9,8},{10,11... | collective-permute-start | bytes 1572872 | tf_op jit(solution)/shard_map/ppermute | solution.py:34
  18.9 26.7 %collective-permute-start.11 = (f32[2,64,1024]{2,1,0:T(8,128)S(1)}, f32[2,64,1024]{2,1,0:T(8,128)}, u32[]{:S(2)}, u32[]{:S(2)}) collective-permute-start(f32[2,64,1024]{2,1,0:T(8,128)S(1)} %get-tuple-element.27.left_ref.refs_12_), channel_id=1, source_target_pairs={{0,4},{4,8},{8,12},{1,5},{5,9},{9,13},{2,6},{6,10},{10,14},{3,7},{... | collective-permute-start | bytes 1572872 | tf_op jit(solution)/shard_map/ppermute | solution.py:30
  24.7 15.6 %all-to-all-start = ((f32[4,136,128]{2,1,0:T(8,128)}), f32[4,136,128]{2,1,0:T(8,128)S(1)}, u32[]{:S(2)}, u32[]{:S(2)}) async-start(f32[4,136,128]{2,1,0:T(8,128)} %shard_map.125), calls=%async_computation | async-start | bytes 557056 | tf_op jit(solution)/shard_map/all_to_all | solution.py:472
  28.2 1.6 %collective-permute-start.2 = (f32[2,72,256]{2,1,0:T(8,128)S(1)}, f32[2,72,256]{2,1,0:T(8,128)}, u32[]{:S(2)}, u32[]{:S(2)}) collective-permute-start(f32[2,72,256]{2,1,0:T(8,128)S(1)} %copy-done.2), channel_id=1, source_target_pairs={{0,1},{1,0},{2,3},{3,2},{4,5},{5,4},{6,7},{7,6},{8,9},{9,8},{10,11... | collective-permute-start | bytes 442376 | tf_op jit(solution)/shard_map/ppermute | solution.py:34
  28.4 1.4 %collective-permute-start.4 = (f32[2,64,256]{2,1,0:T(8,128)S(1)}, f32[2,64,256]{2,1,0:T(8,128)S(1)}, u32[]{:S(2)}, u32[]{:S(2)}) collective-permute-start(f32[2,64,256]{2,1,0:T(8,128)S(1)} %copy-done.4), channel_id=1, source_target_pairs={{0,1},{1,0},{2,3},{3,2},{4,5},{5,4},{6,7},{7,6},{8,9},{9,8},{10,11... | collective-permute-start | bytes 393224 | tf_op jit(solution)/shard_map/ppermute | solution.py:34
  29.8 32.4 %copy-start.19 = (f32[2,64,256]{2,1,0:T(8,128)}, f32[2,64,256]{2,1,0:T(8,128)S(1)}, u32[]{:S(2)}) copy-start(f32[2,64,256]{2,1,0:T(8,128)S(1)} %collective-permute-done.4.refs_7_) | copy-start | bytes 393220
  40.3 21.9 %copy-start.13 = (f32[4,136,128]{2,1,0:T(8,128)}, f32[4,136,128]{2,1,0:T(8,128)S(1)}, u32[]{:S(2)}) copy-start(f32[4,136,128]{2,1,0:T(8,128)S(1)} %all-to-all-done.refs_2_) | copy-start | bytes 835588
  40.3 21.9 %copy-start.14 = (f32[2,64,1024]{2,1,0:T(8,128)}, f32[2,64,1024]{2,1,0:T(8,128)S(1)}, u32[]{:S(2)}) copy-start(f32[2,64,1024]{2,1,0:T(8,128)S(1)} %collective-permute-done.3.refs_13_) | copy-start | bytes 1572868
  41.3 20.9 %copy-start.6 = (f32[2,64,1024]{2,1,0:T(8,128)}, f32[2,64,1024]{2,1,0:T(8,128)S(1)}, u32[]{:S(2)}) copy-start(f32[2,64,1024]{2,1,0:T(8,128)S(1)} %get-tuple-element.29.refs_16_) | copy-start | bytes 1572868
  41.3 4.3 %collective-permute-start.5 = (f32[64,128]{1,0:T(8,128)S(1)}, f32[64,128]{1,0:T(8,128)S(1)}, u32[]{:S(2)}, u32[]{:S(2)}) collective-permute-start(f32[64,128]{1,0:T(8,128)S(1)} %get-tuple-element.22), channel_id=1, source_target_pairs={{0,2},{2,0},{1,3},{3,1},{4,6},{6,4},{5,7},{7,5},{8,10},{10,8},{9,1... | collective-permute-start | bytes 98312 | tf_op jit(solution)/shard_map/ppermute | solution.py:34
  42.9 17.4 %collective-permute-start.7 = (f32[4,136,128]{2,1,0:T(8,128)S(1)}, f32[4,136,128]{2,1,0:T(8,128)}, u32[]{:S(2)}, u32[]{:S(2)}) collective-permute-start(f32[4,136,128]{2,1,0:T(8,128)S(1)} %all-to-all-done.refs_2_), channel_id=1, source_target_pairs={{0,2},{2,0},{1,3},{3,1},{4,6},{6,4},{5,7},{7,5},{8,10},{10,8},{9,1... | collective-permute-start | bytes 835592 | tf_op jit(solution)/shard_map/ppermute | solution.py:34
  43.4 18.6 %collective-permute-start.13 = (f32[2,64,1024]{2,1,0:T(8,128)S(1)}, f32[2,64,1024]{2,1,0:T(8,128)S(1)}, u32[]{:S(2)}, u32[]{:S(2)}) collective-permute-start(f32[2,64,1024]{2,1,0:T(8,128)S(1)} %get-tuple-element.29.refs_16_), channel_id=1, source_target_pairs={{0,1},{1,0},{2,3},{3,2},{4,5},{5,4},{6,7},{7,6},{8,9},{9,8},{10,11... | collective-permute-start | bytes 1572872 | tf_op jit(solution)/shard_map/ppermute | solution.py:34
  45.7 16.4 %collective-permute-start.12 = (f32[2,64,1024]{2,1,0:T(8,128)}, f32[2,64,1024]{2,1,0:T(8,128)S(1)}, u32[]{:S(2)}, u32[]{:S(2)}) collective-permute-start(f32[2,64,1024]{2,1,0:T(8,128)} %collective-permute-done.11.refs_14_), channel_id=1, source_target_pairs={{0,1},{1,0},{2,3},{3,2},{4,5},{5,4},{6,7},{7,6},{8,9},{9,8},{10,11... | collective-permute-start | bytes 1572872 | tf_op jit(solution)/shard_map/ppermute | solution.py:34
  46.4 13.9 %all-to-all-start.1 = ((f32[4,64,128]{2,1,0:T(8,128)}), f32[4,64,128]{2,1,0:T(8,128)S(1)}, u32[]{:S(2)}, u32[]{:S(2)}) async-start(f32[4,64,128]{2,1,0:T(8,128)} %broadcast_in_dim.2), calls=%async_computation.1 | async-start | bytes 262144 | tf_op jit(solution)/shard_map/all_to_all | solution.py:495
  53.9 7.6 %collective-permute-start.8 = (f32[4,136,128]{2,1,0:T(8,128)S(1)}, f32[4,136,128]{2,1,0:T(8,128)}, u32[]{:S(2)}, u32[]{:S(2)}) collective-permute-start(f32[4,136,128]{2,1,0:T(8,128)S(1)} %all-to-all-done.refs_2_), channel_id=1, source_target_pairs={{0,1},{1,0},{2,3},{3,2},{4,5},{5,4},{6,7},{7,6},{8,9},{9,8},{10,11... | collective-permute-start | bytes 835592 | tf_op jit(solution)/shard_map/ppermute | solution.py:34
  54.1 6.2 %collective-permute-start.10 = (f32[2,72,256]{2,1,0:T(8,128)S(1)}, f32[2,72,256]{2,1,0:T(8,128)S(1)}, u32[]{:S(2)}, u32[]{:S(2)}) collective-permute-start(f32[2,72,256]{2,1,0:T(8,128)S(1)} %collective-permute-done.mp_below.refs_10_), channel_id=1, source_target_pairs={{0,1},{1,0},{2,3},{3,2},{4,5},{5,4},{6,7},{7,6},{8,9},{9,8},{10,11... | collective-permute-start | bytes 442376 | tf_op jit(solution)/shard_map/ppermute | solution.py:34
  60.3 1.9 %copy-start.17 = (f32[4,64,128]{2,1,0:T(8,128)}, f32[4,64,128]{2,1,0:T(8,128)S(1)}, u32[]{:S(2)}) copy-start(f32[4,64,128]{2,1,0:T(8,128)S(1)} %all-to-all-done.1.refs_0_) | copy-start | bytes 393220
  60.3 1.9 %collective-permute-start.9 = (f32[4,136,128]{2,1,0:T(8,128)}, f32[4,136,128]{2,1,0:T(8,128)}, u32[]{:S(2)}, u32[]{:S(2)}) collective-permute-start(f32[4,136,128]{2,1,0:T(8,128)} %collective-permute-done.7.refs_3_), channel_id=1, source_target_pairs={{0,1},{1,0},{2,3},{3,2},{4,5},{5,4},{6,7},{7,6},{8,9},{9,8},{10,11... | collective-permute-start | bytes 835592 | tf_op jit(solution)/shard_map/ppermute | solution.py:34
  60.3 1.9 %copy-start.18 = (f32[2,72,256]{2,1,0:T(8,128)}, f32[2,72,256]{2,1,0:T(8,128)S(1)}, u32[]{:S(2)}) copy-start(f32[2,72,256]{2,1,0:T(8,128)S(1)} %collective-permute-done.10.refs_11_) | copy-start | bytes 442372
  60.3 1.7 %collective-permute-start.6 = (f32[4,64,128]{2,1,0:T(8,128)S(1)}, f32[4,64,128]{2,1,0:T(8,128)S(1)}, u32[]{:S(2)}, u32[]{:S(2)}) collective-permute-start(f32[4,64,128]{2,1,0:T(8,128)S(1)} %all-to-all-done.1.refs_0_), channel_id=1, source_target_pairs={{0,1},{1,0},{2,3},{3,2},{4,5},{5,4},{6,7},{7,6},{8,9},{9,8},{10,11... | collective-permute-start | bytes 393224 | tf_op jit(solution)/shard_map/ppermute | solution.py:34
  62.0 0.7 copy-start.20
  62.1 0.8 %copy-start.15 = (f32[2,64,1024]{2,1,0:T(8,128)}, f32[2,64,1024]{2,1,0:T(8,128)S(1)}, u32[]{:S(2)}) copy-start(f32[2,64,1024]{2,1,0:T(8,128)S(1)} %collective-permute-done.13.refs_17_) | copy-start | bytes 1572868
  62.1 1.0 %copy-start.16 = (f32[2,64,1024]{2,1,0:T(8,128)}, f32[2,64,1024]{2,1,0:T(8,128)S(1)}, u32[]{:S(2)}) copy-start(f32[2,64,1024]{2,1,0:T(8,128)S(1)} %collective-permute-done.12.refs_15_) | copy-start | bytes 1572868

commit v10 on v9

--- a/solution.py
+++ b/solution.py
@@ -54,7 +54,7 @@
 held_out = pl.BlockSpec(memory_space=pltpu.HBM)
 
 
-def call(kernel, outs, ins, args, scratch=(), limit=16, out_specs=None, cost=BRIEF):
+def call(kernel, outs, ins, args, scratch=(), limit=16, out_specs=None, cost=None):
     return pl.pallas_call(
         kernel,
         out_shape=[jax.ShapeDtypeStruct(shape, jnp.float32) for shape in outs],
@@ -227,7 +227,7 @@
 def coupled_of(z, index, pair, near, s, coupling, amps_high, amps_low, diag_high, diag_low):
     n = z.pnos
     for k in range(z.links):
-        row = near[pair, k]
+        row = near[k, pair]
         block = slice(k * n, (k + 1) * n)
         diag_high[index, block, block] = amps_high[row]
         diag_low[index, block, block] = amps_low[row]
@@ -439,46 +439,48 @@
         limit=None,
     )
     mp_below = shifted(mp, "orb", 1)
+    (pack,) = call(
+        functools.partial(pack_kernel, z),
+        [pack_shape],
+        [hbm] * 2,
+        (intersections, mp),
+        [
+            scratch(*intersections.shape),
+            scratch(pairs, EXTRA, z.paos),
+            pltpu.SemaphoreType.DMA((2,)),
+        ],
+        limit=None,
+    )
+    if small(z):
+        packs = [lax.all_to_all(pack, "orb", 0, 0)]
+    else:
+        packs = [lax.all_gather(pack, ("orb", "sub"), axis=0, tiled=True)]
     (right_below,) = call(
         functools.partial(below_kernel, z),
         [(pairs, n, fits)],
         [smem, vmem, vmem],
-        (pair_second, mp_below, blocks),
+        (pair_second, gate((mp_below,), pack)[0], blocks),
         limit=8,
     )
     down = shifted(right_below, "orb", -1)
-    late = gate((intersections, mp, pno_coefficients), right_below)
-    intersection, mp_late, coefficients = late
+    mp_late, coefficients = gate((mp, pno_coefficients), right_below)
     left, right_here = call(
         functools.partial(local_kernel, z),
         [(pairs, n, fits), (pairs, n, fits)],
         [smem, smem, vmem, vmem, vmem],
         (pair_first, pair_second, coefficients, mp_late, blocks),
         limit=8,
-    )
-    (pack,) = call(
-        functools.partial(pack_kernel, z),
-        [pack_shape],
-        [hbm] * 2,
-        (intersection, mp_late),
-        [
-            scratch(*intersections.shape),
-            scratch(pairs, EXTRA, z.paos),
-            pltpu.SemaphoreType.DMA((2,)),
-        ],
-        limit=8,
+        cost=BRIEF,
     )
     if small(z):
-        packs = [lax.all_to_all(pack, "orb", 0, 0)]
-    else:
-        packs = [lax.all_gather(pack, ("orb", "sub"), axis=0, tiled=True)]
-    left_below = shifted(gate((left,), pack)[0], "orb", 1)
-    mp_other = swapped(mp_late, "sub")
+        packs.append(swapped(gate(packs, right_here)[0], "fit"))
+    left_below = shifted(left, "orb", 1)
+    mp_other = swapped(gate((mp,), right_here)[0], "sub")
     left_other = swapped(left, "sub")
-    c_other = swapped(coefficients, "sub")
+    c_other = swapped(gate((coefficients,), right_here)[0], "sub")
 
     lists = (pair_first, pair_second, pno_ranks)
-    (down,) = gate((down,), packs[0], mp_other, left_other, c_other)
+    (down,) = gate((down,), mp_other, left_other, c_other)
     part, right = call(
         functools.partial(sums_kernel, z),
         [(n, pairs * n), (pairs, n, fits)],
@@ -486,16 +488,13 @@
         (*lists, occ_energy, mp, left, right_here, down),
         limit=8,
     )
-    (pack_late,) = gate(packs, part)
     if small(z):
-        packs = [pack_late, swapped(pack_late, "fit")]
-        packs.append(swapped(pack_late, "sub"))
+        packs += [swapped(value, "sub") for value in gate(packs, part)]
         sums = part + swapped(part, "fit")
         start_amps = [
             lax.all_to_all(jnp.broadcast_to(sums[None], (z.owners, *sums.shape)), "orb", 0, 0)
         ]
         start_amps.append(swapped(start_amps[0], "sub"))
-        packs.append(swapped(gate(packs[1:2], start_amps[0])[0], "sub"))
     else:
         sums = lax.psum(part, "fit")
         start_amps = [lax.all_gather(sums, ("orb", "sub"), axis=0, tiled=False)]
@@ -507,7 +506,7 @@
     ]
 
     args = (
-        *lists, neighbours, occ_energy, *start_amps, *packs,
+        *lists, neighbours.T, occ_energy, *start_amps, *packs,
         pno_coefficients, c_other, mp, mp_other, mp_below, mp_below_other,
         left, left_other, left_below, left_below_other, right, right_other,
     )

time: 72.5 us -> 74.8 us (1.032)
  waiting for transfers between devices: 23.8 us -> 26.1 us
    ppermute x11, waiting for transfers between devices: 3.97 us -> 7.79 us  [swapped(): return lax.ppermute(value, axis, [(0, 1), (1, 0)])]
    ppermute x3, waiting for transfers between devices: 3.4 us -> 1.7 us  [shifted(): lax.ppermute(value, axis, [(source, source + steps) for source in range(i...]
    all_to_all x1, waiting for transfers between devices: 10.5 us -> 11.6 us  [body(): packs = [lax.all_to_all(pack, 'orb', 0, 0)]]
    all_to_all x1, waiting for transfers between devices: 5.91 us -> 5.05 us  [body(): lax.all_to_all(jnp.broadcast_to(sums[None], (z.owners, *sums.shape)), 'or...]
    unnamed x45 -> x40, local copies, waits for them, and re-layouts: 3.83 us -> 3.23 us
  transfers between devices with their start and end apart: 16 -> 16, of which waited for: 7 -> 6; matrix products, arithmetic and copies ran while one was open for 2% -> 1% of each run, Pallas kernels for 5% -> 6%
where the time goes in v10:
time: 74.8 us; the launch traced here: 74.4 us
  starting transfers between devices  26.5 us (35%)
  waiting for transfers between devices  26.1 us (35%)
  Pallas kernels  16.9 us (23%)
  local copies, waits for them, and re-layouts  3.9 us (5%)
  between operations  0.93 us (1%)
    pallas_call x6, Pallas kernels, call(): pl.pallas_call(kernel, out_shape=[jax.ShapeDtypeStruct(shape, jnp.float32...  16.9 us
    ppermute x3, starting transfers between devices, shifted(): lax.ppermute(value, axis, [(source, source + steps) for source in range(i...  12.1 us
    all_to_all x1, waiting for transfers between devices, body(): packs = [lax.all_to_all(pack, 'orb', 0, 0)]  11.6 us
    ppermute x11, waiting for transfers between devices, swapped(): return lax.ppermute(value, axis, [(0, 1), (1, 0)])  7.79 us
    all_to_all x1, starting transfers between devices, body(): lax.all_to_all(jnp.broadcast_to(sums[None], (z.owners, *sums.shape)), 'or...  7.44 us
    all_to_all x1, waiting for transfers between devices, body(): lax.all_to_all(jnp.broadcast_to(sums[None], (z.owners, *sums.shape)), 'or...  5.05 us
    all_to_all x1, starting transfers between devices, body(): packs = [lax.all_to_all(pack, 'orb', 0, 0)]  3.55 us
    ppermute x11, starting transfers between devices, swapped(): return lax.ppermute(value, axis, [(0, 1), (1, 0)])  3.48 us
  transfers between devices with their start and end apart: 16, of which 6 were waited for; matrix products, arithmetic and copies ran while one was open for 1% of the time, Pallas kernels for 6%

profile of v10, /device:TPU:0, one launch (start us, length us, event | category | flops | bytes accessed | tf_op | source)
XLA Modules:
  0.0 74.4 jit_solution(16331074549306752871)
XLA Ops:
  0.6 0.0 copy-start.4
  0.6 0.0 copy-start.8
  0.7 0.0 copy-start.9
  0.7 2.0 %shard_map.122.mp_in.mp_ref.refs_8_ = f32[2,72,256]{2,1,0:T(8,128)} custom-call(f32[2,64,256]{2,1,0:T(8,128)} %refs_6_.1, s32[2,256]{1,0:T(2,128)} %map_in.1, f32[2,64]{1,0:T(2,128)} %e_in.1, f32[2,4]{1,0:T(2,128)} %coupling_in.1), custom_call_target="tpu_custom_call" | custom-call | tf_op jit(solution)/shard_map/pallas_call | solution.py:58
  2.6 5.1 %collective-permute-start = (f32[2,72,256]{2,1,0:T(8,128)}, f32[2,72,256]{2,1,0:T(8,128)S(1)}, u32[]{:S(2)}, u32[]{:S(2)}) collective-permute-start(f32[2,72,256]{2,1,0:T(8,128)} %shard_map.122.mp_in.mp_ref.refs_8_), channel_id=1, source_target_pairs={{0,4},{4,8},{8,12},{1,5},{5,9},{9,13},{2,6},{6,10},{10,14},{3,7},{... | collective-permute-start | bytes 442376 | tf_op jit(solution)/shard_map/ppermute | solution.py:30
  7.7 1.7 %shard_map.123 = f32[4,136,128]{2,1,0:T(8,128)} custom-call(f32[2,4,4096]{2,1,0:T(4,128)} %s_in.1, f32[2,72,256]{2,1,0:T(8,128)} %shard_map.122.mp_in.mp_ref.refs_8_), custom_call_target="tpu_custom_call" | custom-call | tf_op jit(solution)/shard_map/pallas_call | solution.py:58
  9.4 1.7 %collective-permute-done.mp_below.refs_10_ = f32[2,72,256]{2,1,0:T(8,128)S(1)} collective-permute-done((f32[2,72,256]{2,1,0:T(8,128)}, f32[2,72,256]{2,1,0:T(8,128)S(1)}, u32[]{:S(2)}, u32[]{:S(2)}) %collective-permute-start) | collective-permute-done | bytes 147488 | tf_op jit(solution)/shard_map/ppermute | solution.py:30
  11.1 1.6 %copy-done = f32[2,256,1024]{2,1,0:T(8,128)S(1)} copy-done((f32[2,256,1024]{2,1,0:T(8,128)S(1)}, f32[2,256,1024]{2,1,0:T(8,128)}, u32[]{:S(2)}) %copy-start) | copy-done | bytes 2097176
  12.7 0.7 copy-done.7
  13.4 1.3 %shard_map.124 = f32[2,64,1024]{2,1,0:T(8,128)S(1)} custom-call(s32[16]{0:T(128)S(1)} %copy-done.7, f32[2,72,256]{2,1,0:T(8,128)S(1)} %collective-permute-done.mp_below.refs_10_, f32[2,256,1024]{2,1,0:T(8,128)S(1)} %copy-done), custom_call_target="tpu_custom_call" | custom-call | tf_op jit(solution)/shard_map/pallas_call | solution.py:58
  14.7 0.0 copy-start.10
  14.7 0.0 copy-start.11
  14.7 1.3 %collective-permute-start.1 = (f32[2,64,1024]{2,1,0:T(8,128)S(1)}, f32[2,64,1024]{2,1,0:T(8,128)S(1)}, u32[]{:S(2)}, u32[]{:S(2)}) collective-permute-start(f32[2,64,1024]{2,1,0:T(8,128)S(1)} %shard_map.124), channel_id=1, source_target_pairs={{4,0},{8,4},{12,8},{5,1},{9,5},{13,9},{6,2},{10,6},{14,10},{7,3},{... | collective-permute-start | bytes 1572872 | tf_op jit(solution)/shard_map/ppermute | solution.py:30
  16.0 1.9 %shard_map.125 = (f32[2,64,1024]{2,1,0:T(8,128)S(1)}, f32[2,64,1024]{2,1,0:T(8,128)S(1)}) custom-call(s32[16]{0:T(128)S(1)} %copy-done.9, s32[16]{0:T(128)S(1)} %copy-done.8, f32[2,64,256]{2,1,0:T(8,128)S(1)} %copy-done.4, f32[2,72,256]{2,1,0:T(8,128)S(1)} %copy-done.2, f32[2,256,1024]{2,1,0:T(8,128)S(1)} %copy-done.1), custom_call_target="tpu_custom_call" | custom-call | flops 1 | bytes 1 | tf_op jit(solution)/shard_map/pallas_call | solution.py:58
  18.0 0.1 collective-permute-start.3
  18.1 5.7 %collective-permute-start.11 = (f32[2,64,1024]{2,1,0:T(8,128)S(1)}, f32[2,64,1024]{2,1,0:T(8,128)}, u32[]{:S(2)}, u32[]{:S(2)}) collective-permute-start(f32[2,64,1024]{2,1,0:T(8,128)S(1)} %get-tuple-element.21.left_ref.refs_12_), channel_id=1, source_target_pairs={{0,4},{4,8},{8,12},{1,5},{5,9},{9,13},{2,6},{6,10},{10,14},{3,7},{... | collective-permute-start | bytes 1572872 | tf_op jit(solution)/shard_map/ppermute | solution.py:30
  23.8 3.5 %all-to-all-start.1 = ((f32[4,136,128]{2,1,0:T(8,128)}), f32[4,136,128]{2,1,0:T(8,128)S(1)}, u32[]{:S(2)}, u32[]{:S(2)}) async-start(f32[4,136,128]{2,1,0:T(8,128)} %shard_map.123), calls=%async_computation.1 | async-start | bytes 557056 | tf_op jit(solution)/shard_map/all_to_all | solution.py:455
  27.3 0.2 collective-permute-start.2
  27.5 0.3 collective-permute-start.4
  27.8 11.6 %all-to-all-done.1.refs_2_ = f32[4,136,128]{2,1,0:T(8,128)S(1)} async-done(((f32[4,136,128]{2,1,0:T(8,128)}), f32[4,136,128]{2,1,0:T(8,128)S(1)}, u32[]{:S(2)}, u32[]{:S(2)}) %all-to-all-start.1) | async-done | bytes 278560 | tf_op jit(solution)/shard_map/all_to_all | solution.py:455
  39.4 0.0 collective-permute-done.4.refs_7_
  39.4 1.5 %collective-permute-start.7 = (f32[4,136,128]{2,1,0:T(8,128)S(1)}, f32[4,136,128]{2,1,0:T(8,128)}, u32[]{:S(2)}, u32[]{:S(2)}) collective-permute-start(f32[4,136,128]{2,1,0:T(8,128)S(1)} %all-to-all-done.1.refs_2_), channel_id=1, source_target_pairs={{0,2},{2,0},{1,3},{3,1},{4,6},{6,4},{5,7},{7,5},{8,10},{10,8},{9,1... | collective-permute-start | bytes 835592 | tf_op jit(solution)/shard_map/ppermute | solution.py:34
  40.9 0.0 collective-permute-done.2.refs_9_
  40.9 0.0 collective-permute-done.1.down_ref
  40.9 0.0 collective-permute-done.3.refs_13_
  41.0 1.0 %shard_map.126 = (f32[64,128]{1,0:T(8,128)S(1)}, f32[2,64,1024]{2,1,0:T(8,128)S(1)}) custom-call(s32[16]{0:T(128)S(1)} %copy-done.9, s32[16]{0:T(128)S(1)} %copy-done.8, s32[16]{0:T(128)S(1)} %copy-done.10, f32[8]{0:T(128)S(1)} %copy-done.11, f32[2,72,256]{2,1,0:T(8,128)S(1)} %copy-done.2, f32[2,64,1024]{2,1,0:T(8,128)S(1)} %get-tuple-element.21.left_ref.refs_12_, ...), custom_call_target="tpu_custom_call" | custom-call | tf_op jit(solution)/shard_map/pallas_call | solution.py:58
  42.0 0.6 collective-permute-start.5
  42.6 0.0 collective-permute-start.13
  42.6 5.8 %collective-permute-done.5 = f32[64,128]{1,0:T(8,128)S(1)} collective-permute-done((f32[64,128]{1,0:T(8,128)S(1)}, f32[64,128]{1,0:T(8,128)S(1)}, u32[]{:S(2)}, u32[]{:S(2)}) %collective-permute-start.5) | collective-permute-done | bytes 32800 | tf_op jit(solution)/shard_map/ppermute | solution.py:34
  48.4 0.0 collective-permute-done.11.refs_14_
  48.4 0.1 collective-permute-start.12
  48.5 0.7 broadcast_in_dim.2
  49.1 7.4 %all-to-all-start = ((f32[4,64,128]{2,1,0:T(8,128)}), f32[4,64,128]{2,1,0:T(8,128)S(1)}, u32[]{:S(2)}, u32[]{:S(2)}) async-start(f32[4,64,128]{2,1,0:T(8,128)} %broadcast_in_dim.2), calls=%async_computation | async-start | bytes 262144 | tf_op jit(solution)/shard_map/all_to_all | solution.py:495
  56.6 0.2 collective-permute-start.10
  56.8 0.0 collective-permute-done.7.refs_3_
  56.8 0.3 collective-permute-start.8
  57.1 0.2 collective-permute-start.9
  57.3 0.6 collective-permute-done.10.refs_11_
  58.0 5.0 %all-to-all-done.refs_0_ = f32[4,64,128]{2,1,0:T(8,128)S(1)} async-done(((f32[4,64,128]{2,1,0:T(8,128)}), f32[4,64,128]{2,1,0:T(8,128)S(1)}, u32[]{:S(2)}, u32[]{:S(2)}) %all-to-all-start) | async-done | bytes 131104 | tf_op jit(solution)/shard_map/all_to_all | solution.py:495
  63.0 0.0 collective-permute-start.6
  63.0 0.0 collective-permute-done.9.refs_5_
  63.0 1.3 %collective-permute-done.6.refs_1_ = f32[4,64,128]{2,1,0:T(8,128)S(1)} collective-permute-done((f32[4,64,128]{2,1,0:T(8,128)S(1)}, f32[4,64,128]{2,1,0:T(8,128)S(1)}, u32[]{:S(2)}, u32[]{:S(2)}) %collective-permute-start.6) | collective-permute-done | bytes 131104 | tf_op jit(solution)/shard_map/ppermute | solution.py:34
  64.4 0.0 collective-permute-done.13.refs_17_
  64.4 0.0 collective-permute-done.12.refs_15_
  64.5 0.6 copy-done.19
  65.0 0.2 copy-done.14
  65.2 0.2 copy-done.15
  65.4 9.0 %shard_map.127 = (f32[2,4096]{1,0:T(2,128)}, f32[2,128,1024]{2,1,0:T(8,128)}) custom-call(s32[16]{0:T(128)} %first.5, s32[16]{0:T(128)} %second.7, s32[16]{0:T(128)} %ranks.3, s32[4,16]{1,0:T(4,128)} %bitcast.1, f32[8]{0:T(128)} %occupied.3, f32[4,64,128]{2,1,0:T(8,128)} %copy-done.16, f32[4,64,128]{2,1,0:T(8,128)} %copy-done.19, f32[4,136,128]{2,1,0:T(8,128)} %copy-done.12, ...), custom_call_target="tpu_custom_call" | custom-call | tf_op jit(solution)/shard_map/pallas_call | solution.py:58
  (32 shorter events, 0.1 us)
Async XLA Ops:
  0.6 15.4 %copy-start.4 = (f32[2,64,256]{2,1,0:T(8,128)S(1)}, f32[2,64,256]{2,1,0:T(8,128)}, u32[]{:S(2)}) copy-start(f32[2,64,256]{2,1,0:T(8,128)} %refs_6_.1) | copy-start | bytes 393220
  0.6 15.4 %copy-start.8 = (s32[16]{0:T(128)S(1)}, s32[16]{0:T(128)}, u32[]{:S(2)}) copy-start(s32[16]{0:T(128)} %second.7) | copy-start | bytes 196
  0.7 15.4 %copy-start.9 = (s32[16]{0:T(128)S(1)}, s32[16]{0:T(128)}, u32[]{:S(2)}) copy-start(s32[16]{0:T(128)} %first.5) | copy-start | bytes 196
  2.6 13.4 %copy-start.2 = (f32[2,72,256]{2,1,0:T(8,128)S(1)}, f32[2,72,256]{2,1,0:T(8,128)}, u32[]{:S(2)}) copy-start(f32[2,72,256]{2,1,0:T(8,128)} %shard_map.122.mp_in.mp_ref.refs_8_) | copy-start | bytes 442372
  2.6 8.5 %collective-permute-start = (f32[2,72,256]{2,1,0:T(8,128)}, f32[2,72,256]{2,1,0:T(8,128)S(1)}, u32[]{:S(2)}, u32[]{:S(2)}) collective-permute-start(f32[2,72,256]{2,1,0:T(8,128)} %shard_map.122.mp_in.mp_ref.refs_8_), channel_id=1, source_target_pairs={{0,4},{4,8},{8,12},{1,5},{5,9},{9,13},{2,6},{6,10},{10,14},{3,7},{... | collective-permute-start | bytes 442376 | tf_op jit(solution)/shard_map/ppermute | solution.py:30
  11.1 1.6 %copy-start = (f32[2,256,1024]{2,1,0:T(8,128)S(1)}, f32[2,256,1024]{2,1,0:T(8,128)}, u32[]{:S(2)}) copy-start(f32[2,256,1024]{2,1,0:T(8,128)} %b_ref.3) | copy-start | bytes 6291460
  12.7 0.7 copy-start.7
  13.4 43.2 %copy-start.5 = (f32[2,72,256]{2,1,0:T(8,128)}, f32[2,72,256]{2,1,0:T(8,128)S(1)}, u32[]{:S(2)}) copy-start(f32[2,72,256]{2,1,0:T(8,128)S(1)} %collective-permute-done.mp_below.refs_10_) | copy-start | bytes 442372
  13.4 2.7 %copy-start.1 = (f32[2,256,1024]{2,1,0:T(8,128)S(1)}, f32[2,256,1024]{2,1,0:T(8,128)}, u32[]{:S(2)}) copy-start(f32[2,256,1024]{2,1,0:T(8,128)} %b_ref.3) | copy-start | bytes 6291460
  14.7 26.3 %copy-start.10 = (s32[16]{0:T(128)S(1)}, s32[16]{0:T(128)}, u32[]{:S(2)}) copy-start(s32[16]{0:T(128)} %ranks.3) | copy-start | bytes 196
  14.7 26.3 %copy-start.11 = (f32[8]{0:T(128)S(1)}, f32[8]{0:T(128)}, u32[]{:S(2)}) copy-start(f32[8]{0:T(128)} %occupied.3) | copy-start | bytes 100
  14.7 26.2 %collective-permute-start.1 = (f32[2,64,1024]{2,1,0:T(8,128)S(1)}, f32[2,64,1024]{2,1,0:T(8,128)S(1)}, u32[]{:S(2)}, u32[]{:S(2)}) collective-permute-start(f32[2,64,1024]{2,1,0:T(8,128)S(1)} %shard_map.124), channel_id=1, source_target_pairs={{4,0},{8,4},{12,8},{5,1},{9,5},{13,9},{6,2},{10,6},{14,10},{7,3},{... | collective-permute-start | bytes 1572872 | tf_op jit(solution)/shard_map/ppermute | solution.py:30
  18.0 46.4 %copy-start.3 = (f32[2,64,1024]{2,1,0:T(8,128)}, f32[2,64,1024]{2,1,0:T(8,128)S(1)}, u32[]{:S(2)}) copy-start(f32[2,64,1024]{2,1,0:T(8,128)S(1)} %get-tuple-element.21.left_ref.refs_12_) | copy-start | bytes 1572868
  18.0 23.0 %collective-permute-start.3 = (f32[2,64,1024]{2,1,0:T(8,128)S(1)}, f32[2,64,1024]{2,1,0:T(8,128)S(1)}, u32[]{:S(2)}, u32[]{:S(2)}) collective-permute-start(f32[2,64,1024]{2,1,0:T(8,128)S(1)} %get-tuple-element.21.left_ref.refs_12_), channel_id=1, source_target_pairs={{0,1},{1,0},{2,3},{3,2},{4,5},{5,4},{6,7},{7,6},{8,9},{9,8},{10,11... | collective-permute-start | bytes 1572872 | tf_op jit(solution)/shard_map/ppermute | solution.py:34
  18.1 30.3 %collective-permute-start.11 = (f32[2,64,1024]{2,1,0:T(8,128)S(1)}, f32[2,64,1024]{2,1,0:T(8,128)}, u32[]{:S(2)}, u32[]{:S(2)}) collective-permute-start(f32[2,64,1024]{2,1,0:T(8,128)S(1)} %get-tuple-element.21.left_ref.refs_12_), channel_id=1, source_target_pairs={{0,4},{4,8},{8,12},{1,5},{5,9},{9,13},{2,6},{6,10},{10,14},{3,7},{... | collective-permute-start | bytes 1572872 | tf_op jit(solution)/shard_map/ppermute | solution.py:30
  23.8 15.6 %all-to-all-start.1 = ((f32[4,136,128]{2,1,0:T(8,128)}), f32[4,136,128]{2,1,0:T(8,128)S(1)}, u32[]{:S(2)}, u32[]{:S(2)}) async-start(f32[4,136,128]{2,1,0:T(8,128)} %shard_map.123), calls=%async_computation.1 | async-start | bytes 557056 | tf_op jit(solution)/shard_map/all_to_all | solution.py:455
  27.3 13.6 %collective-permute-start.2 = (f32[2,72,256]{2,1,0:T(8,128)S(1)}, f32[2,72,256]{2,1,0:T(8,128)S(1)}, u32[]{:S(2)}, u32[]{:S(2)}) collective-permute-start(f32[2,72,256]{2,1,0:T(8,128)S(1)} %copy-done.2), channel_id=1, source_target_pairs={{0,1},{1,0},{2,3},{3,2},{4,5},{5,4},{6,7},{7,6},{8,9},{9,8},{10,11... | collective-permute-start | bytes 442376 | tf_op jit(solution)/shard_map/ppermute | solution.py:34
  27.5 11.9 %collective-permute-start.4 = (f32[2,64,256]{2,1,0:T(8,128)S(1)}, f32[2,64,256]{2,1,0:T(8,128)}, u32[]{:S(2)}, u32[]{:S(2)}) collective-permute-start(f32[2,64,256]{2,1,0:T(8,128)S(1)} %copy-done.4), channel_id=1, source_target_pairs={{0,1},{1,0},{2,3},{3,2},{4,5},{5,4},{6,7},{7,6},{8,9},{9,8},{10,11... | collective-permute-start | bytes 393224 | tf_op jit(solution)/shard_map/ppermute | solution.py:34
  39.4 25.0 %copy-start.12 = (f32[4,136,128]{2,1,0:T(8,128)}, f32[4,136,128]{2,1,0:T(8,128)S(1)}, u32[]{:S(2)}) copy-start(f32[4,136,128]{2,1,0:T(8,128)S(1)} %all-to-all-done.1.refs_2_) | copy-start | bytes 835588
  39.4 17.4 %collective-permute-start.7 = (f32[4,136,128]{2,1,0:T(8,128)S(1)}, f32[4,136,128]{2,1,0:T(8,128)}, u32[]{:S(2)}, u32[]{:S(2)}) collective-permute-start(f32[4,136,128]{2,1,0:T(8,128)S(1)} %all-to-all-done.1.refs_2_), channel_id=1, source_target_pairs={{0,2},{2,0},{1,3},{3,1},{4,6},{6,4},{5,7},{7,5},{8,10},{10,8},{9,1... | collective-permute-start | bytes 835592 | tf_op jit(solution)/shard_map/ppermute | solution.py:34
  40.9 23.5 %copy-start.17 = (f32[2,72,256]{2,1,0:T(8,128)}, f32[2,72,256]{2,1,0:T(8,128)S(1)}, u32[]{:S(2)}) copy-start(f32[2,72,256]{2,1,0:T(8,128)S(1)} %collective-permute-done.2.refs_9_) | copy-start | bytes 442372
  41.0 23.5 %copy-start.13 = (f32[2,64,1024]{2,1,0:T(8,128)}, f32[2,64,1024]{2,1,0:T(8,128)S(1)}, u32[]{:S(2)}) copy-start(f32[2,64,1024]{2,1,0:T(8,128)S(1)} %collective-permute-done.3.refs_13_) | copy-start | bytes 1572868
  42.0 22.5 %copy-start.6 = (f32[2,64,1024]{2,1,0:T(8,128)}, f32[2,64,1024]{2,1,0:T(8,128)S(1)}, u32[]{:S(2)}) copy-start(f32[2,64,1024]{2,1,0:T(8,128)S(1)} %get-tuple-element.33.refs_16_) | copy-start | bytes 1572868
  42.0 6.4 %collective-permute-start.5 = (f32[64,128]{1,0:T(8,128)S(1)}, f32[64,128]{1,0:T(8,128)S(1)}, u32[]{:S(2)}, u32[]{:S(2)}) collective-permute-start(f32[64,128]{1,0:T(8,128)S(1)} %get-tuple-element.26), channel_id=1, source_target_pairs={{0,2},{2,0},{1,3},{3,1},{4,6},{6,4},{5,7},{7,5},{8,10},{10,8},{9,1... | collective-permute-start | bytes 98312 | tf_op jit(solution)/shard_map/ppermute | solution.py:34
  42.6 21.8 %collective-permute-start.13 = (f32[2,64,1024]{2,1,0:T(8,128)S(1)}, f32[2,64,1024]{2,1,0:T(8,128)S(1)}, u32[]{:S(2)}, u32[]{:S(2)}) collective-permute-start(f32[2,64,1024]{2,1,0:T(8,128)S(1)} %get-tuple-element.33.refs_16_), channel_id=1, source_target_pairs={{0,1},{1,0},{2,3},{3,2},{4,5},{5,4},{6,7},{7,6},{8,9},{9,8},{10,11... | collective-permute-start | bytes 1572872 | tf_op jit(solution)/shard_map/ppermute | solution.py:34
  48.4 16.0 %collective-permute-start.12 = (f32[2,64,1024]{2,1,0:T(8,128)}, f32[2,64,1024]{2,1,0:T(8,128)S(1)}, u32[]{:S(2)}, u32[]{:S(2)}) collective-permute-start(f32[2,64,1024]{2,1,0:T(8,128)} %collective-permute-done.11.refs_14_), channel_id=1, source_target_pairs={{0,1},{1,0},{2,3},{3,2},{4,5},{5,4},{6,7},{7,6},{8,9},{9,8},{10,11... | collective-permute-start | bytes 1572872 | tf_op jit(solution)/shard_map/ppermute | solution.py:34
  49.1 13.9 %all-to-all-start = ((f32[4,64,128]{2,1,0:T(8,128)}), f32[4,64,128]{2,1,0:T(8,128)S(1)}, u32[]{:S(2)}, u32[]{:S(2)}) async-start(f32[4,64,128]{2,1,0:T(8,128)} %broadcast_in_dim.2), calls=%async_computation | async-start | bytes 262144 | tf_op jit(solution)/shard_map/all_to_all | solution.py:495
  56.6 1.4 %collective-permute-start.10 = (f32[2,72,256]{2,1,0:T(8,128)S(1)}, f32[2,72,256]{2,1,0:T(8,128)S(1)}, u32[]{:S(2)}, u32[]{:S(2)}) collective-permute-start(f32[2,72,256]{2,1,0:T(8,128)S(1)} %collective-permute-done.mp_below.refs_10_), channel_id=1, source_target_pairs={{0,1},{1,0},{2,3},{3,2},{4,5},{5,4},{6,7},{7,6},{8,9},{9,8},{10,11... | collective-permute-start | bytes 442376 | tf_op jit(solution)/shard_map/ppermute | solution.py:34
  56.8 6.2 %collective-permute-start.8 = (f32[4,136,128]{2,1,0:T(8,128)S(1)}, f32[4,136,128]{2,1,0:T(8,128)}, u32[]{:S(2)}, u32[]{:S(2)}) collective-permute-start(f32[4,136,128]{2,1,0:T(8,128)S(1)} %all-to-all-done.1.refs_2_), channel_id=1, source_target_pairs={{0,1},{1,0},{2,3},{3,2},{4,5},{5,4},{6,7},{7,6},{8,9},{9,8},{10,11... | collective-permute-start | bytes 835592 | tf_op jit(solution)/shard_map/ppermute | solution.py:34
  57.1 5.9 %collective-permute-start.9 = (f32[4,136,128]{2,1,0:T(8,128)}, f32[4,136,128]{2,1,0:T(8,128)}, u32[]{:S(2)}, u32[]{:S(2)}) collective-permute-start(f32[4,136,128]{2,1,0:T(8,128)} %collective-permute-done.7.refs_3_), channel_id=1, source_target_pairs={{0,1},{1,0},{2,3},{3,2},{4,5},{5,4},{6,7},{7,6},{8,9},{9,8},{10,11... | collective-permute-start | bytes 835592 | tf_op jit(solution)/shard_map/ppermute | solution.py:34
  58.0 6.5 %copy-start.18 = (f32[2,72,256]{2,1,0:T(8,128)}, f32[2,72,256]{2,1,0:T(8,128)S(1)}, u32[]{:S(2)}) copy-start(f32[2,72,256]{2,1,0:T(8,128)S(1)} %collective-permute-done.10.refs_11_) | copy-start | bytes 442372
  63.0 1.4 %copy-start.16 = (f32[4,64,128]{2,1,0:T(8,128)}, f32[4,64,128]{2,1,0:T(8,128)S(1)}, u32[]{:S(2)}) copy-start(f32[4,64,128]{2,1,0:T(8,128)S(1)} %all-to-all-done.refs_0_) | copy-start | bytes 393220
  63.0 1.3 %collective-permute-start.6 = (f32[4,64,128]{2,1,0:T(8,128)S(1)}, f32[4,64,128]{2,1,0:T(8,128)S(1)}, u32[]{:S(2)}, u32[]{:S(2)}) collective-permute-start(f32[4,64,128]{2,1,0:T(8,128)S(1)} %all-to-all-done.refs_0_), channel_id=1, source_target_pairs={{0,1},{1,0},{2,3},{3,2},{4,5},{5,4},{6,7},{7,6},{8,9},{9,8},{10,11... | collective-permute-start | bytes 393224 | tf_op jit(solution)/shard_map/ppermute | solution.py:34
  64.4 0.7 copy-start.19
  64.4 0.8 %copy-start.14 = (f32[2,64,1024]{2,1,0:T(8,128)}, f32[2,64,1024]{2,1,0:T(8,128)S(1)}, u32[]{:S(2)}) copy-start(f32[2,64,1024]{2,1,0:T(8,128)S(1)} %collective-permute-done.13.refs_17_) | copy-start | bytes 1572868
  64.4 1.0 %copy-start.15 = (f32[2,64,1024]{2,1,0:T(8,128)}, f32[2,64,1024]{2,1,0:T(8,128)S(1)}, u32[]{:S(2)}) copy-start(f32[2,64,1024]{2,1,0:T(8,128)S(1)} %collective-permute-done.12.refs_15_) | copy-start | bytes 1572868

commit v11 on v10

--- a/solution.py
+++ b/solution.py
@@ -169,7 +169,7 @@
             pack_ref[copy] = pack_ref[0]
 
 
-def below_kernel(z, second, mp_below, b_ref, right_ref):
+def below_kernel(z, second, mp_below, b_ref, order, right_ref):
     owner, sub = lax.axis_index("orb"), lax.axis_index("sub")
     start = side_start(z, jnp.maximum(owner - 1, 0), sub, 0)
     for p in range(z.pairs):
@@ -439,6 +439,7 @@
         limit=None,
     )
     mp_below = shifted(mp, "orb", 1)
+    pack_shape = (z.owners if small(z) else pairs, z.links * n // 2 + EXTRA, 2 * n)
     (pack,) = call(
         functools.partial(pack_kernel, z),
         [pack_shape],
@@ -458,34 +459,33 @@
     (right_below,) = call(
         functools.partial(below_kernel, z),
         [(pairs, n, fits)],
-        [smem, vmem, vmem],
-        (pair_second, gate((mp_below,), pack)[0], blocks),
+        [smem, vmem, vmem, anywhere],
+        (pair_second, mp_below, blocks, pack),
         limit=8,
     )
     down = shifted(right_below, "orb", -1)
-    mp_late, coefficients = gate((mp, pno_coefficients), right_below)
+    (coefficients,) = gate((pno_coefficients,), right_below)
     left, right_here = call(
         functools.partial(local_kernel, z),
         [(pairs, n, fits), (pairs, n, fits)],
         [smem, smem, vmem, vmem, vmem],
-        (pair_first, pair_second, coefficients, mp_late, blocks),
+        (pair_first, pair_second, coefficients, mp, blocks),
         limit=8,
-        cost=BRIEF,
-    )
+    )
+    left_late, mp_late, coefficients = gate((left, mp, coefficients), right_here)
+    left_below = shifted(left_late, "orb", 1)
+    mp_other = swapped(mp_late, "sub")
+    left_other = swapped(left_late, "sub")
+    c_other = swapped(coefficients, "sub")
     if small(z):
         packs.append(swapped(gate(packs, right_here)[0], "fit"))
-    left_below = shifted(left, "orb", 1)
-    mp_other = swapped(gate((mp,), right_here)[0], "sub")
-    left_other = swapped(left, "sub")
-    c_other = swapped(gate((coefficients,), right_here)[0], "sub")
 
     lists = (pair_first, pair_second, pno_ranks)
-    (down,) = gate((down,), mp_other, left_other, c_other)
     part, right = call(
         functools.partial(sums_kernel, z),
         [(n, pairs * n), (pairs, n, fits)],
-        [smem] * 4 + [vmem] * 4,
-        (*lists, occ_energy, mp, left, right_here, down),
+        [smem] * 4 + [vmem] * 4 + [anywhere] * 3,
+        (*lists, occ_energy, mp, left, right_here, down, left_other, mp_other, c_other),
         limit=8,
     )
     if small(z):

time: 74.8 us -> 75.3 us (level)
  starting transfers between devices: 26.5 us -> 27.4 us
where the time goes in v11:
time: 75.3 us; the launch traced here: 74.8 us
  starting transfers between devices  27.4 us (36%)
  waiting for transfers between devices  25.7 us (34%)
  Pallas kernels  16.8 us (22%)
  local copies, waits for them, and re-layouts  3.9 us (5%)
  between operations  0.94 us (1%)
    pallas_call x6, Pallas kernels, call(): pl.pallas_call(kernel, out_shape=[jax.ShapeDtypeStruct(shape, jnp.float32...  16.8 us
    ppermute x3, starting transfers between devices, shifted(): lax.ppermute(value, axis, [(source, source + steps) for source in range(i...  12.2 us
    all_to_all x1, waiting for transfers between devices, body(): packs = [lax.all_to_all(pack, 'orb', 0, 0)]  11 us
    ppermute x11, waiting for transfers between devices, swapped(): return lax.ppermute(value, axis, [(0, 1), (1, 0)])  7.99 us
    all_to_all x1, starting transfers between devices, body(): lax.all_to_all(jnp.broadcast_to(sums[None], (z.owners, *sums.shape)), 'or...  7.55 us
    all_to_all x1, waiting for transfers between devices, body(): lax.all_to_all(jnp.broadcast_to(sums[None], (z.owners, *sums.shape)), 'or...  5.05 us
    all_to_all x1, starting transfers between devices, body(): packs = [lax.all_to_all(pack, 'orb', 0, 0)]  4.1 us
    ppermute x11, starting transfers between devices, swapped(): return lax.ppermute(value, axis, [(0, 1), (1, 0)])  3.54 us
  transfers between devices with their start and end apart: 16, of which 6 were waited for; matrix products, arithmetic and copies ran while one was open for 1% of the time, Pallas kernels for 6%

profile of v11, /device:TPU:0, one launch (start us, length us, event | category | flops | bytes accessed | tf_op | source)
XLA Modules:
  0.0 74.8 jit_solution(2239627037991080374)
XLA Ops:
  0.6 0.0 copy-start.5
  0.6 0.0 copy-start.12
  0.7 2.0 %shard_map.122.mp_in.mp_ref.refs_8_ = f32[2,72,256]{2,1,0:T(8,128)} custom-call(f32[2,64,256]{2,1,0:T(8,128)} %refs_6_.1, s32[2,256]{1,0:T(2,128)} %map_in.1, f32[2,64]{1,0:T(2,128)} %e_in.1, f32[2,4]{1,0:T(2,128)} %coupling_in.1), custom_call_target="tpu_custom_call" | custom-call | tf_op jit(solution)/shard_map/pallas_call | solution.py:58
  2.6 5.1 %collective-permute-start = (f32[2,72,256]{2,1,0:T(8,128)}, f32[2,72,256]{2,1,0:T(8,128)S(1)}, u32[]{:S(2)}, u32[]{:S(2)}) collective-permute-start(f32[2,72,256]{2,1,0:T(8,128)} %shard_map.122.mp_in.mp_ref.refs_8_), channel_id=1, source_target_pairs={{0,4},{4,8},{8,12},{1,5},{5,9},{9,13},{2,6},{6,10},{10,14},{3,7},{... | collective-permute-start | bytes 442376 | tf_op jit(solution)/shard_map/ppermute | solution.py:30
  7.7 1.7 %shard_map.123.order = f32[4,136,128]{2,1,0:T(8,128)} custom-call(f32[2,4,4096]{2,1,0:T(4,128)} %s_in.1, f32[2,72,256]{2,1,0:T(8,128)} %shard_map.122.mp_in.mp_ref.refs_8_), custom_call_target="tpu_custom_call" | custom-call | tf_op jit(solution)/shard_map/pallas_call | solution.py:58
  9.4 1.7 %collective-permute-done.mp_below.refs_10_ = f32[2,72,256]{2,1,0:T(8,128)S(1)} collective-permute-done((f32[2,72,256]{2,1,0:T(8,128)}, f32[2,72,256]{2,1,0:T(8,128)S(1)}, u32[]{:S(2)}, u32[]{:S(2)}) %collective-permute-start) | collective-permute-done | bytes 147488 | tf_op jit(solution)/shard_map/ppermute | solution.py:30
  11.1 1.6 %copy-done = f32[2,256,1024]{2,1,0:T(8,128)S(1)} copy-done((f32[2,256,1024]{2,1,0:T(8,128)S(1)}, f32[2,256,1024]{2,1,0:T(8,128)}, u32[]{:S(2)}) %copy-start) | copy-done | bytes 2097176
  12.7 0.7 copy-done.10
  13.3 1.3 %shard_map.124 = f32[2,64,1024]{2,1,0:T(8,128)S(1)} custom-call(s32[16]{0:T(128)S(1)} %copy-done.10, f32[2,72,256]{2,1,0:T(8,128)S(1)} %collective-permute-done.mp_below.refs_10_, f32[2,256,1024]{2,1,0:T(8,128)S(1)} %copy-done, f32[4,136,128]{2,1,0:T(8,128)} %shard_map.123.order), custom_call_target="tpu_custom_call" | custom-call | tf_op jit(solution)/shard_map/pallas_call | solution.py:58
  14.7 0.0 copy-start.11
  14.7 0.0 copy-start.13
  14.7 0.0 copy-start.14
  14.7 1.4 %collective-permute-start.1 = (f32[2,64,1024]{2,1,0:T(8,128)S(1)}, f32[2,64,1024]{2,1,0:T(8,128)S(1)}, u32[]{:S(2)}, u32[]{:S(2)}) collective-permute-start(f32[2,64,1024]{2,1,0:T(8,128)S(1)} %shard_map.124), channel_id=1, source_target_pairs={{4,0},{8,4},{12,8},{5,1},{9,5},{13,9},{6,2},{10,6},{14,10},{7,3},{... | collective-permute-start | bytes 1572872 | tf_op jit(solution)/shard_map/ppermute | solution.py:30
  16.2 1.9 %shard_map.125 = (f32[2,64,1024]{2,1,0:T(8,128)S(1)}, f32[2,64,1024]{2,1,0:T(8,128)S(1)}) custom-call(s32[16]{0:T(128)S(1)} %copy-done.12, s32[16]{0:T(128)S(1)} %copy-done.10, f32[2,64,256]{2,1,0:T(8,128)S(1)} %copy-done.5, f32[2,72,256]{2,1,0:T(8,128)S(1)} %copy-done.2, f32[2,256,1024]{2,1,0:T(8,128)S(1)} %copy-done.1), custom_call_target="tpu_custom_call" | custom-call | tf_op jit(solution)/shard_map/pallas_call | solution.py:58
  18.1 0.1 collective-permute-start.2
  18.2 5.7 %collective-permute-start.11 = (f32[2,64,1024]{2,1,0:T(8,128)S(1)}, f32[2,64,1024]{2,1,0:T(8,128)}, u32[]{:S(2)}, u32[]{:S(2)}) collective-permute-start(f32[2,64,1024]{2,1,0:T(8,128)S(1)} %get-tuple-element.19.left_ref.refs_12_), channel_id=1, source_target_pairs={{0,4},{4,8},{8,12},{1,5},{5,9},{9,13},{2,6},{6,10},{10,14},{3,7},{... | collective-permute-start | bytes 1572872 | tf_op jit(solution)/shard_map/ppermute | solution.py:30
  23.9 4.1 %all-to-all-start.1 = ((f32[4,136,128]{2,1,0:T(8,128)}), f32[4,136,128]{2,1,0:T(8,128)}, u32[]{:S(2)}, u32[]{:S(2)}) async-start(f32[4,136,128]{2,1,0:T(8,128)} %shard_map.123.order), calls=%async_computation.1 | async-start | bytes 557056 | tf_op jit(solution)/shard_map/all_to_all | solution.py:456
  28.0 0.3 collective-permute-start.3
  28.3 0.3 collective-permute-start.4
  28.6 11.0 %all-to-all-done.1.refs_2_ = f32[4,136,128]{2,1,0:T(8,128)} async-done(((f32[4,136,128]{2,1,0:T(8,128)}), f32[4,136,128]{2,1,0:T(8,128)}, u32[]{:S(2)}, u32[]{:S(2)}) %all-to-all-start.1) | async-done | bytes 278560 | tf_op jit(solution)/shard_map/all_to_all | solution.py:456
  39.5 0.0 collective-permute-done.4.refs_2_.refs_7_
  39.5 1.5 %collective-permute-start.7 = (f32[4,136,128]{2,1,0:T(8,128)}, f32[4,136,128]{2,1,0:T(8,128)}, u32[]{:S(2)}, u32[]{:S(2)}) collective-permute-start(f32[4,136,128]{2,1,0:T(8,128)} %all-to-all-done.1.refs_2_), channel_id=1, source_target_pairs={{0,2},{2,0},{1,3},{3,1},{4,6},{6,4},{5,7},{7,5},{8,10},{10,8},{9,1... | collective-permute-start | bytes 835592 | tf_op jit(solution)/shard_map/ppermute | solution.py:34
  41.0 0.0 collective-permute-done.3.refs_1_.refs_9_
  41.0 0.0 collective-permute-done.1.down_ref
  41.0 0.0 collective-permute-done.2.refs_0_.refs_13_
  41.1 1.0 %shard_map.126 = (f32[64,128]{1,0:T(8,128)S(1)}, f32[2,64,1024]{2,1,0:T(8,128)S(1)}) custom-call(s32[16]{0:T(128)S(1)} %copy-done.12, s32[16]{0:T(128)S(1)} %copy-done.11, s32[16]{0:T(128)S(1)} %copy-done.13, f32[8]{0:T(128)S(1)} %copy-done.14, f32[2,72,256]{2,1,0:T(8,128)S(1)} %copy-done.2, f32[2,64,1024]{2,1,0:T(8,128)S(1)} %get-tuple-element.19.left_ref.refs_12_, ...), custom_call_target="tpu_custom_call" | custom-call | tf_op jit(solution)/shard_map/pallas_call | solution.py:58
  42.1 0.6 collective-permute-start.5
  42.7 0.0 collective-permute-start.13
  42.7 6.0 %collective-permute-done.5 = f32[64,128]{1,0:T(8,128)S(1)} collective-permute-done((f32[64,128]{1,0:T(8,128)S(1)}, f32[64,128]{1,0:T(8,128)S(1)}, u32[]{:S(2)}, u32[]{:S(2)}) %collective-permute-start.5) | collective-permute-done | bytes 32800 | tf_op jit(solution)/shard_map/ppermute | solution.py:34
  48.7 0.0 collective-permute-done.11.refs_14_
  48.7 0.1 collective-permute-start.12
  48.8 0.7 broadcast_in_dim.2
  49.5 7.5 %all-to-all-start = ((f32[4,64,128]{2,1,0:T(8,128)}), f32[4,64,128]{2,1,0:T(8,128)S(1)}, u32[]{:S(2)}, u32[]{:S(2)}) async-start(f32[4,64,128]{2,1,0:T(8,128)} %broadcast_in_dim.2), calls=%async_computation | async-start | bytes 262144 | tf_op jit(solution)/shard_map/all_to_all | solution.py:495
  57.0 0.2 collective-permute-start.10
  57.2 0.0 collective-permute-done.7.refs_3_
  57.2 0.3 collective-permute-start.8
  57.5 0.2 collective-permute-start.9
  57.8 0.6 collective-permute-done.10.refs_11_
  58.4 5.0 %all-to-all-done.refs_0_ = f32[4,64,128]{2,1,0:T(8,128)S(1)} async-done(((f32[4,64,128]{2,1,0:T(8,128)}), f32[4,64,128]{2,1,0:T(8,128)S(1)}, u32[]{:S(2)}, u32[]{:S(2)}) %all-to-all-start) | async-done | bytes 131104 | tf_op jit(solution)/shard_map/all_to_all | solution.py:495
  63.4 0.0 collective-permute-start.6
  63.4 0.0 collective-permute-done.8.refs_4_
  63.5 1.3 %collective-permute-done.6.refs_1_ = f32[4,64,128]{2,1,0:T(8,128)S(1)} collective-permute-done((f32[4,64,128]{2,1,0:T(8,128)S(1)}, f32[4,64,128]{2,1,0:T(8,128)S(1)}, u32[]{:S(2)}, u32[]{:S(2)}) %collective-permute-start.6) | collective-permute-done | bytes 131104 | tf_op jit(solution)/shard_map/ppermute | solution.py:34
  64.8 0.0 collective-permute-done.13.refs_17_
  64.8 0.0 collective-permute-done.12.refs_15_
  64.9 0.6 copy-done.19
  65.4 0.2 copy-done.15
  65.6 0.2 copy-done.16
  65.8 9.0 %shard_map.127 = (f32[2,4096]{1,0:T(2,128)}, f32[2,128,1024]{2,1,0:T(8,128)}) custom-call(s32[16]{0:T(128)} %first.5, s32[16]{0:T(128)} %second.7, s32[16]{0:T(128)} %ranks.3, s32[4,16]{1,0:T(4,128)} %bitcast.1, f32[8]{0:T(128)} %occupied.3, f32[4,64,128]{2,1,0:T(8,128)} %copy-done.17, f32[4,64,128]{2,1,0:T(8,128)} %copy-done.19, ...), custom_call_target="tpu_custom_call" | custom-call | tf_op jit(solution)/shard_map/pallas_call | solution.py:58
  (32 shorter events, 0.1 us)
Async XLA Ops:
  0.6 15.5 %copy-start.5 = (f32[2,64,256]{2,1,0:T(8,128)S(1)}, f32[2,64,256]{2,1,0:T(8,128)}, u32[]{:S(2)}) copy-start(f32[2,64,256]{2,1,0:T(8,128)} %refs_6_.1) | copy-start | bytes 393220
  0.6 15.5 %copy-start.12 = (s32[16]{0:T(128)S(1)}, s32[16]{0:T(128)}, u32[]{:S(2)}) copy-start(s32[16]{0:T(128)} %first.5) | copy-start | bytes 196
  2.6 13.5 %copy-start.2 = (f32[2,72,256]{2,1,0:T(8,128)S(1)}, f32[2,72,256]{2,1,0:T(8,128)}, u32[]{:S(2)}) copy-start(f32[2,72,256]{2,1,0:T(8,128)} %shard_map.122.mp_in.mp_ref.refs_8_) | copy-start | bytes 442372
  2.6 8.5 %collective-permute-start = (f32[2,72,256]{2,1,0:T(8,128)}, f32[2,72,256]{2,1,0:T(8,128)S(1)}, u32[]{:S(2)}, u32[]{:S(2)}) collective-permute-start(f32[2,72,256]{2,1,0:T(8,128)} %shard_map.122.mp_in.mp_ref.refs_8_), channel_id=1, source_target_pairs={{0,4},{4,8},{8,12},{1,5},{5,9},{9,13},{2,6},{6,10},{10,14},{3,7},{... | collective-permute-start | bytes 442376 | tf_op jit(solution)/shard_map/ppermute | solution.py:30
  11.1 1.6 %copy-start = (f32[2,256,1024]{2,1,0:T(8,128)S(1)}, f32[2,256,1024]{2,1,0:T(8,128)}, u32[]{:S(2)}) copy-start(f32[2,256,1024]{2,1,0:T(8,128)} %b_ref.3) | copy-start | bytes 6291460
  12.7 0.7 copy-start.10
  13.3 43.7 %copy-start.6 = (f32[2,72,256]{2,1,0:T(8,128)}, f32[2,72,256]{2,1,0:T(8,128)S(1)}, u32[]{:S(2)}) copy-start(f32[2,72,256]{2,1,0:T(8,128)S(1)} %collective-permute-done.mp_below.refs_10_) | copy-start | bytes 442372
  13.3 2.8 %copy-start.1 = (f32[2,256,1024]{2,1,0:T(8,128)S(1)}, f32[2,256,1024]{2,1,0:T(8,128)}, u32[]{:S(2)}) copy-start(f32[2,256,1024]{2,1,0:T(8,128)} %b_ref.3) | copy-start | bytes 6291460
  14.7 26.4 %copy-start.11 = (s32[16]{0:T(128)S(1)}, s32[16]{0:T(128)}, u32[]{:S(2)}) copy-start(s32[16]{0:T(128)} %second.7) | copy-start | bytes 196
  14.7 26.4 %copy-start.13 = (s32[16]{0:T(128)S(1)}, s32[16]{0:T(128)}, u32[]{:S(2)}) copy-start(s32[16]{0:T(128)} %ranks.3) | copy-start | bytes 196
  14.7 26.4 %copy-start.14 = (f32[8]{0:T(128)S(1)}, f32[8]{0:T(128)}, u32[]{:S(2)}) copy-start(f32[8]{0:T(128)} %occupied.3) | copy-start | bytes 100
  14.7 26.3 %collective-permute-start.1 = (f32[2,64,1024]{2,1,0:T(8,128)S(1)}, f32[2,64,1024]{2,1,0:T(8,128)S(1)}, u32[]{:S(2)}, u32[]{:S(2)}) collective-permute-start(f32[2,64,1024]{2,1,0:T(8,128)S(1)} %shard_map.124), channel_id=1, source_target_pairs={{4,0},{8,4},{12,8},{5,1},{9,5},{13,9},{6,2},{10,6},{14,10},{7,3},{... | collective-permute-start | bytes 1572872 | tf_op jit(solution)/shard_map/ppermute | solution.py:30
  18.1 46.7 %copy-start.3 = (f32[2,64,1024]{2,1,0:T(8,128)}, f32[2,64,1024]{2,1,0:T(8,128)S(1)}, u32[]{:S(2)}) copy-start(f32[2,64,1024]{2,1,0:T(8,128)S(1)} %get-tuple-element.19.left_ref.refs_12_) | copy-start | bytes 1572868
  18.1 22.9 %collective-permute-start.2 = (f32[2,64,1024]{2,1,0:T(8,128)S(1)}, f32[2,64,1024]{2,1,0:T(8,128)S(1)}, u32[]{:S(2)}, u32[]{:S(2)}) collective-permute-start(f32[2,64,1024]{2,1,0:T(8,128)S(1)} %get-tuple-element.19.left_ref.refs_12_), channel_id=1, source_target_pairs={{0,1},{1,0},{2,3},{3,2},{4,5},{5,4},{6,7},{7,6},{8,9},{9,8},{10,11... | collective-permute-start | bytes 1572872 | tf_op jit(solution)/shard_map/ppermute | solution.py:34
  18.2 30.6 %collective-permute-start.11 = (f32[2,64,1024]{2,1,0:T(8,128)S(1)}, f32[2,64,1024]{2,1,0:T(8,128)}, u32[]{:S(2)}, u32[]{:S(2)}) collective-permute-start(f32[2,64,1024]{2,1,0:T(8,128)S(1)} %get-tuple-element.19.left_ref.refs_12_), channel_id=1, source_target_pairs={{0,4},{4,8},{8,12},{1,5},{5,9},{9,13},{2,6},{6,10},{10,14},{3,7},{... | collective-permute-start | bytes 1572872 | tf_op jit(solution)/shard_map/ppermute | solution.py:30
  23.9 15.6 %all-to-all-start.1 = ((f32[4,136,128]{2,1,0:T(8,128)}), f32[4,136,128]{2,1,0:T(8,128)}, u32[]{:S(2)}, u32[]{:S(2)}) async-start(f32[4,136,128]{2,1,0:T(8,128)} %shard_map.123.order), calls=%async_computation.1 | async-start | bytes 557056 | tf_op jit(solution)/shard_map/all_to_all | solution.py:456
  28.0 13.0 %collective-permute-start.3 = (f32[2,72,256]{2,1,0:T(8,128)S(1)}, f32[2,72,256]{2,1,0:T(8,128)S(1)}, u32[]{:S(2)}, u32[]{:S(2)}) collective-permute-start(f32[2,72,256]{2,1,0:T(8,128)S(1)} %copy-done.2), channel_id=1, source_target_pairs={{0,1},{1,0},{2,3},{3,2},{4,5},{5,4},{6,7},{7,6},{8,9},{9,8},{10,11... | collective-permute-start | bytes 442376 | tf_op jit(solution)/shard_map/ppermute | solution.py:34
  28.3 11.3 %collective-permute-start.4 = (f32[2,64,256]{2,1,0:T(8,128)S(1)}, f32[2,64,256]{2,1,0:T(8,128)S(1)}, u32[]{:S(2)}, u32[]{:S(2)}) collective-permute-start(f32[2,64,256]{2,1,0:T(8,128)S(1)} %copy-done.5), channel_id=1, source_target_pairs={{0,1},{1,0},{2,3},{3,2},{4,5},{5,4},{6,7},{7,6},{8,9},{9,8},{10,11... | collective-permute-start | bytes 393224 | tf_op jit(solution)/shard_map/ppermute | solution.py:34
  39.5 25.3 %copy-start.9 = (f32[2,64,256]{2,1,0:T(8,128)}, f32[2,64,256]{2,1,0:T(8,128)S(1)}, u32[]{:S(2)}) copy-start(f32[2,64,256]{2,1,0:T(8,128)S(1)} %collective-permute-done.4.refs_2_.refs_7_) | copy-start | bytes 393220
  39.5 17.7 %collective-permute-start.7 = (f32[4,136,128]{2,1,0:T(8,128)}, f32[4,136,128]{2,1,0:T(8,128)}, u32[]{:S(2)}, u32[]{:S(2)}) collective-permute-start(f32[4,136,128]{2,1,0:T(8,128)} %all-to-all-done.1.refs_2_), channel_id=1, source_target_pairs={{0,2},{2,0},{1,3},{3,1},{4,6},{6,4},{5,7},{7,5},{8,10},{10,8},{9,1... | collective-permute-start | bytes 835592 | tf_op jit(solution)/shard_map/ppermute | solution.py:34
  41.0 23.8 %copy-start.7 = (f32[2,72,256]{2,1,0:T(8,128)}, f32[2,72,256]{2,1,0:T(8,128)S(1)}, u32[]{:S(2)}) copy-start(f32[2,72,256]{2,1,0:T(8,128)S(1)} %collective-permute-done.3.refs_1_.refs_9_) | copy-start | bytes 442372
  41.1 23.8 %copy-start.4 = (f32[2,64,1024]{2,1,0:T(8,128)}, f32[2,64,1024]{2,1,0:T(8,128)S(1)}, u32[]{:S(2)}) copy-start(f32[2,64,1024]{2,1,0:T(8,128)S(1)} %collective-permute-done.2.refs_0_.refs_13_) | copy-start | bytes 1572868
  42.1 22.8 %copy-start.8 = (f32[2,64,1024]{2,1,0:T(8,128)}, f32[2,64,1024]{2,1,0:T(8,128)S(1)}, u32[]{:S(2)}) copy-start(f32[2,64,1024]{2,1,0:T(8,128)S(1)} %get-tuple-element.29.refs_16_) | copy-start | bytes 1572868
  42.1 6.6 %collective-permute-start.5 = (f32[64,128]{1,0:T(8,128)S(1)}, f32[64,128]{1,0:T(8,128)S(1)}, u32[]{:S(2)}, u32[]{:S(2)}) collective-permute-start(f32[64,128]{1,0:T(8,128)S(1)} %get-tuple-element.22), channel_id=1, source_target_pairs={{0,2},{2,0},{1,3},{3,1},{4,6},{6,4},{5,7},{7,5},{8,10},{10,8},{9,1... | collective-permute-start | bytes 98312 | tf_op jit(solution)/shard_map/ppermute | solution.py:34
  42.7 22.1 %collective-permute-start.13 = (f32[2,64,1024]{2,1,0:T(8,128)S(1)}, f32[2,64,1024]{2,1,0:T(8,128)S(1)}, u32[]{:S(2)}, u32[]{:S(2)}) collective-permute-start(f32[2,64,1024]{2,1,0:T(8,128)S(1)} %get-tuple-element.29.refs_16_), channel_id=1, source_target_pairs={{0,1},{1,0},{2,3},{3,2},{4,5},{5,4},{6,7},{7,6},{8,9},{9,8},{10,11... | collective-permute-start | bytes 1572872 | tf_op jit(solution)/shard_map/ppermute | solution.py:34
  48.7 16.1 %collective-permute-start.12 = (f32[2,64,1024]{2,1,0:T(8,128)}, f32[2,64,1024]{2,1,0:T(8,128)S(1)}, u32[]{:S(2)}, u32[]{:S(2)}) collective-permute-start(f32[2,64,1024]{2,1,0:T(8,128)} %collective-permute-done.11.refs_14_), channel_id=1, source_target_pairs={{0,1},{1,0},{2,3},{3,2},{4,5},{5,4},{6,7},{7,6},{8,9},{9,8},{10,11... | collective-permute-start | bytes 1572872 | tf_op jit(solution)/shard_map/ppermute | solution.py:34
  49.5 14.0 %all-to-all-start = ((f32[4,64,128]{2,1,0:T(8,128)}), f32[4,64,128]{2,1,0:T(8,128)S(1)}, u32[]{:S(2)}, u32[]{:S(2)}) async-start(f32[4,64,128]{2,1,0:T(8,128)} %broadcast_in_dim.2), calls=%async_computation | async-start | bytes 262144 | tf_op jit(solution)/shard_map/all_to_all | solution.py:495
  57.0 1.4 %collective-permute-start.10 = (f32[2,72,256]{2,1,0:T(8,128)S(1)}, f32[2,72,256]{2,1,0:T(8,128)S(1)}, u32[]{:S(2)}, u32[]{:S(2)}) collective-permute-start(f32[2,72,256]{2,1,0:T(8,128)S(1)} %collective-permute-done.mp_below.refs_10_), channel_id=1, source_target_pairs={{0,1},{1,0},{2,3},{3,2},{4,5},{5,4},{6,7},{7,6},{8,9},{9,8},{10,11... | collective-permute-start | bytes 442376 | tf_op jit(solution)/shard_map/ppermute | solution.py:34
  57.2 6.2 %collective-permute-start.8 = (f32[4,136,128]{2,1,0:T(8,128)}, f32[4,136,128]{2,1,0:T(8,128)}, u32[]{:S(2)}, u32[]{:S(2)}) collective-permute-start(f32[4,136,128]{2,1,0:T(8,128)} %all-to-all-done.1.refs_2_), channel_id=1, source_target_pairs={{0,1},{1,0},{2,3},{3,2},{4,5},{5,4},{6,7},{7,6},{8,9},{9,8},{10,11... | collective-permute-start | bytes 835592 | tf_op jit(solution)/shard_map/ppermute | solution.py:34
  57.5 5.9 %collective-permute-start.9 = (f32[4,136,128]{2,1,0:T(8,128)}, f32[4,136,128]{2,1,0:T(8,128)}, u32[]{:S(2)}, u32[]{:S(2)}) collective-permute-start(f32[4,136,128]{2,1,0:T(8,128)} %collective-permute-done.7.refs_3_), channel_id=1, source_target_pairs={{0,1},{1,0},{2,3},{3,2},{4,5},{5,4},{6,7},{7,6},{8,9},{9,8},{10,11... | collective-permute-start | bytes 835592 | tf_op jit(solution)/shard_map/ppermute | solution.py:34
  58.4 6.5 %copy-start.18 = (f32[2,72,256]{2,1,0:T(8,128)}, f32[2,72,256]{2,1,0:T(8,128)S(1)}, u32[]{:S(2)}) copy-start(f32[2,72,256]{2,1,0:T(8,128)S(1)} %collective-permute-done.10.refs_11_) | copy-start | bytes 442372
  63.4 1.4 %copy-start.17 = (f32[4,64,128]{2,1,0:T(8,128)}, f32[4,64,128]{2,1,0:T(8,128)S(1)}, u32[]{:S(2)}) copy-start(f32[4,64,128]{2,1,0:T(8,128)S(1)} %all-to-all-done.refs_0_) | copy-start | bytes 393220
  63.4 1.3 %collective-permute-start.6 = (f32[4,64,128]{2,1,0:T(8,128)S(1)}, f32[4,64,128]{2,1,0:T(8,128)S(1)}, u32[]{:S(2)}, u32[]{:S(2)}) collective-permute-start(f32[4,64,128]{2,1,0:T(8,128)S(1)} %all-to-all-done.refs_0_), channel_id=1, source_target_pairs={{0,1},{1,0},{2,3},{3,2},{4,5},{5,4},{6,7},{7,6},{8,9},{9,8},{10,11... | collective-permute-start | bytes 393224 | tf_op jit(solution)/shard_map/ppermute | solution.py:34
  64.8 0.7 copy-start.19
  64.8 0.8 %copy-start.15 = (f32[2,64,1024]{2,1,0:T(8,128)}, f32[2,64,1024]{2,1,0:T(8,128)S(1)}, u32[]{:S(2)}) copy-start(f32[2,64,1024]{2,1,0:T(8,128)S(1)} %collective-permute-done.13.refs_17_) | copy-start | bytes 1572868
  64.8 1.0 %copy-start.16 = (f32[2,64,1024]{2,1,0:T(8,128)}, f32[2,64,1024]{2,1,0:T(8,128)S(1)}, u32[]{:S(2)}) copy-start(f32[2,64,1024]{2,1,0:T(8,128)S(1)} %collective-permute-done.12.refs_15_) | copy-start | bytes 1572868

commit v12 on v10

--- a/solution.py
+++ b/solution.py
@@ -236,11 +236,11 @@
 
 def final_kernel(z, first, second, ranks, near, occupied, *refs):
     start_count, pack_count = (2, 4) if small(z) else (1, 1)
-    starts = refs[:start_count]
+    starts_in = refs[:start_count]
     pack_in = refs[start_count : start_count + pack_count]
     (c_in, c_other, mp_in, mp_other, mp_below, mp_below_other, left_in, left_other, left_below,
      left_below_other, right_in, right_other) = refs[start_count + pack_count :][:12]
-    (amp_ref, grad_out, packs, s_high, s_low, scale_ref, coupling_ref, s_rows, c_ref, m_ref, rhs,
+    (amp_out, grad_out, starts, amp_ref, packs, s_high, s_low, scale_ref, coupling_ref, s_rows, c_ref, m_ref, rhs,
      grad, flat, amps, amps_high, amps_low, next_high, next_low, diag_high, diag_low, rows_high,
      rows_low, sems) = refs[start_count + pack_count + 12 :]
     owner, sub = lax.axis_index("orb"), lax.axis_index("sub")
@@ -253,6 +253,7 @@
     def quarters(ref, base=0):
         return [ref.at[pl.ds(base + i * pairs, pairs)] for i in range(4)]
 
+    start_copies = started(starts_in, [starts.at[i] for i in range(start_count)], sems, 16)
     pack_copies = started(pack_in, [packs.at[i] for i in range(pack_count)], sems)
     small_copies = started(
         [c_in.at[:, :, at], c_other.at[:, :, at]]
@@ -268,20 +269,25 @@
     diag_high[...] = jnp.zeros_like(diag_high)
     diag_low[...] = jnp.zeros_like(diag_low)
 
+    wait(start_copies)
+
     def begin(pair, value):
         amps[pair] = value
         amps_high[pair], amps_low[pair] = split(value)
 
     if small(z):
-        for side, ref in ((sub, starts[0]), (1 - sub, starts[1])):
+        for index, side in enumerate((sub, 1 - sub)):
             for who in range(z.owners):
                 for p in range(pairs):
-                    begin(who * own + side * pairs + p, ref[who, :, p * n : (p + 1) * n])
+                    begin(
+                        who * own + side * pairs + p,
+                        starts[index, who, :, p * n : (p + 1) * n],
+                    )
     else:
         @pl.loop(0, z.owners * z.subs)
         def _(device):
             for p in range(pairs):
-                begin(device * pairs + p, starts[0][device, :, p * n : (p + 1) * n])
+                begin(device * pairs + p, starts[0, device, :, p * n : (p + 1) * n])
 
     wait(pack_copies)
     if small(z):
@@ -378,11 +384,11 @@
         lines = jnp.concatenate([even, odd], axis=1)
         for r in range(n // 2):
             amp_ref[p : p + 1, r * 2 * n : (r + 1) * 2 * n] = lines[r : r + 1, :]
+    copies = started([amp_ref], [amp_out], sems, 18)
 
     wait(large_copies)
     step = 256
     rows = (rows_high[...], rows_low[...])
-    copies = []
     for index, start in enumerate(range(0, z.fits, step)):
         factor = rhs[:, :, start : start + step].reshape(3 * own * n, step)
         grad[:, :, start : start + step] = mm3(rows, split(factor)).reshape(
@@ -390,7 +396,7 @@
         )
         window = pl.ds(start, step)
         copies += started(
-            [grad.at[:, :, window]], [grad_out.at[:, :, window]], sems, 16 + index
+            [grad.at[:, :, window]], [grad_out.at[:, :, window]], sems, 19 + index
         )
     wait(copies)
 
@@ -472,9 +478,7 @@
         limit=8,
         cost=BRIEF,
     )
-    if small(z):
-        packs.append(swapped(gate(packs, right_here)[0], "fit"))
-    left_below = shifted(left, "orb", 1)
+    left_below = shifted(gate((left,), packs[0])[0], "orb", 1)
     mp_other = swapped(gate((mp,), right_here)[0], "sub")
     left_other = swapped(left, "sub")
     c_other = swapped(gate((coefficients,), right_here)[0], "sub")
@@ -489,12 +493,15 @@
         limit=8,
     )
     if small(z):
-        packs += [swapped(value, "sub") for value in gate(packs, part)]
+        packs.append(None)
+        packs.append(swapped(gate(packs[:1], part)[0], "sub"))
         sums = part + swapped(part, "fit")
+        packs[1] = swapped(gate(packs[:1], sums)[0], "fit")
         start_amps = [
             lax.all_to_all(jnp.broadcast_to(sums[None], (z.owners, *sums.shape)), "orb", 0, 0)
         ]
         start_amps.append(swapped(start_amps[0], "sub"))
+        packs.append(swapped(gate(packs[1:2], start_amps[0])[0], "sub"))
     else:
         sums = lax.psum(part, "fit")
         start_amps = [lax.all_gather(sums, ("orb", "sub"), axis=0, tiled=False)]
@@ -514,9 +521,11 @@
     amplitudes, gradient = call(
         functools.partial(final_kernel, z),
         [(pairs, n * n), (z.orbitals, half, fits)],
-        [smem] * 5 + [vmem] * len(start_amps) + [hbm] * (12 + len(packs)),
+        [smem] * 5 + [hbm] * (12 + len(start_amps) + len(packs)),
         args,
         [
+            scratch(len(start_amps), *start_amps[0].shape),
+            scratch(pairs, n * n),
             scratch(len(packs), *packs[0].shape),
             scratch(z.total, n, wide, kind=bf16),
             scratch(z.total, n, wide, kind=bf16),
@@ -533,9 +542,9 @@
         + [scratch(*square, kind=bf16)] * 4
         + [scratch(2 * own, wide, wide, kind=bf16)] * 2
         + [scratch(z.orbitals * half, 3 * own * n, kind=bf16)] * 2
-        + [pltpu.SemaphoreType.DMA((16 + -(-fits // 256),))],
+        + [pltpu.SemaphoreType.DMA((19 + -(-fits // 256),))],
         limit=60,
-        out_specs=[vmem, hbm],
+        out_specs=[hbm, hbm],
     )
     return (amplitudes, gradient)
 

time: 74.8 us -> 69.4 us (0.928)
  waiting for transfers between devices: 26.1 us -> 19.5 us
  starting transfers between devices: 26.5 us -> 28.3 us
    all_to_all x1, waiting for transfers between devices: 11.6 us -> 0.01 us  [body(): packs = [lax.all_to_all(pack, 'orb', 0, 0)]]
    ppermute x3, waiting for transfers between devices: 1.7 us -> 9 us  [shifted(): lax.ppermute(value, axis, [(source, source + steps) for source in range(i...]
    ppermute x11, waiting for transfers between devices: 7.79 us -> 4.72 us  [swapped(): return lax.ppermute(value, axis, [(0, 1), (1, 0)])]
    all_to_all x1, starting transfers between devices: 3.55 us -> 6.46 us  [body(): packs = [lax.all_to_all(pack, 'orb', 0, 0)]]
    all_to_all x1, starting transfers between devices: 7.44 us -> 4.81 us  [body(): lax.all_to_all(jnp.broadcast_to(sums[None], (z.owners, *sums.shape)), 'or...]
    ppermute x11, starting transfers between devices: 3.48 us -> 5.2 us  [swapped(): return lax.ppermute(value, axis, [(0, 1), (1, 0)])]
    unnamed x40 -> x46, local copies, waits for them, and re-layouts: 3.23 us -> 3.33 us
where the time goes in v12:
time: 69.4 us; the launch traced here: 68.9 us
  starting transfers between devices  28.3 us (41%)
  waiting for transfers between devices  19.5 us (28%)
  Pallas kernels  16.2 us (23%)
  local copies, waits for them, and re-layouts  4 us (6%)
  between operations  0.96 us (1%)
    pallas_call x6, Pallas kernels, call(): pl.pallas_call(kernel, out_shape=[jax.ShapeDtypeStruct(shape, jnp.float32...  16.2 us
    ppermute x3, starting transfers between devices, shifted(): lax.ppermute(value, axis, [(source, source + steps) for source in range(i...  11.8 us
    ppermute x3, waiting for transfers between devices, shifted(): lax.ppermute(value, axis, [(source, source + steps) for source in range(i...  9 us
    all_to_all x1, starting transfers between devices, body(): packs = [lax.all_to_all(pack, 'orb', 0, 0)]  6.46 us
    all_to_all x1, waiting for transfers between devices, body(): lax.all_to_all(jnp.broadcast_to(sums[None], (z.owners, *sums.shape)), 'or...  5.76 us
    ppermute x11, starting transfers between devices, swapped(): return lax.ppermute(value, axis, [(0, 1), (1, 0)])  5.2 us
    all_to_all x1, starting transfers between devices, body(): lax.all_to_all(jnp.broadcast_to(sums[None], (z.owners, *sums.shape)), 'or...  4.81 us
    ppermute x11, waiting for transfers between devices, swapped(): return lax.ppermute(value, axis, [(0, 1), (1, 0)])  4.72 us
  transfers between devices with their start and end apart: 16, of which 6 were waited for; matrix products, arithmetic and copies ran while one was open for 1% of the time, Pallas kernels for 6%

profile of v12, /device:TPU:0, one launch (start us, length us, event | category | flops | bytes accessed | tf_op | source)
XLA Modules:
  0.0 68.9 jit_solution(5396814928489128481)
XLA Ops:
  0.6 0.0 copy-start.4
  0.6 0.0 copy-start.9
  0.7 1.9 %shard_map.122.mp_in.mp_ref.refs_8_ = f32[2,72,256]{2,1,0:T(8,128)} custom-call(f32[2,64,256]{2,1,0:T(8,128)} %refs_6_.1, s32[2,256]{1,0:T(2,128)} %map_in.1, f32[2,64]{1,0:T(2,128)} %e_in.1, f32[2,4]{1,0:T(2,128)} %coupling_in.1), custom_call_target="tpu_custom_call" | custom-call | tf_op jit(solution)/shard_map/pallas_call | solution.py:58
  2.6 1.7 %shard_map.123 = f32[4,136,128]{2,1,0:T(8,128)} custom-call(f32[2,4,4096]{2,1,0:T(4,128)} %s_in.1, f32[2,72,256]{2,1,0:T(8,128)} %shard_map.122.mp_in.mp_ref.refs_8_), custom_call_target="tpu_custom_call" | custom-call | tf_op jit(solution)/shard_map/pallas_call | solution.py:58
  4.4 0.0 copy-start.8
  4.4 0.0 copy-start.10
  4.4 0.0 copy-start.11
  4.4 6.5 %all-to-all-start.1 = ((f32[4,136,128]{2,1,0:T(8,128)}), f32[4,136,128]{2,1,0:T(8,128)S(1)}, u32[]{:S(2)}, u32[]{:S(2)}) async-start(f32[4,136,128]{2,1,0:T(8,128)} %shard_map.123), calls=%async_computation.1 | async-start | bytes 557056 | tf_op jit(solution)/shard_map/all_to_all | solution.py:461
  10.9 3.9 %collective-permute-start = (f32[2,72,256]{2,1,0:T(8,128)}, f32[2,72,256]{2,1,0:T(8,128)S(1)}, u32[]{:S(2)}, u32[]{:S(2)}) collective-permute-start(f32[2,72,256]{2,1,0:T(8,128)} %shard_map.122.mp_in.mp_ref.refs_8_), channel_id=1, source_target_pairs={{0,4},{4,8},{8,12},{1,5},{5,9},{9,13},{2,6},{6,10},{10,14},{3,7},{... | collective-permute-start | bytes 442376 | tf_op jit(solution)/shard_map/ppermute | solution.py:30
  14.8 4.0 %collective-permute-done.mp_below.refs_10_ = f32[2,72,256]{2,1,0:T(8,128)S(1)} collective-permute-done((f32[2,72,256]{2,1,0:T(8,128)}, f32[2,72,256]{2,1,0:T(8,128)S(1)}, u32[]{:S(2)}, u32[]{:S(2)}) %collective-permute-start) | collective-permute-done | bytes 147488 | tf_op jit(solution)/shard_map/ppermute | solution.py:30
  18.8 1.6 %copy-done = f32[2,256,1024]{2,1,0:T(8,128)S(1)} copy-done((f32[2,256,1024]{2,1,0:T(8,128)S(1)}, f32[2,256,1024]{2,1,0:T(8,128)}, u32[]{:S(2)}) %copy-start) | copy-done | bytes 2097176
  20.3 0.7 copy-done.7
  21.0 1.3 %shard_map.124 = f32[2,64,1024]{2,1,0:T(8,128)S(1)} custom-call(s32[16]{0:T(128)S(1)} %copy-done.7, f32[2,72,256]{2,1,0:T(8,128)S(1)} %collective-permute-done.mp_below.refs_10_, f32[2,256,1024]{2,1,0:T(8,128)S(1)} %copy-done), custom_call_target="tpu_custom_call" | custom-call | tf_op jit(solution)/shard_map/pallas_call | solution.py:58
  22.3 1.3 %collective-permute-start.1 = (f32[2,64,1024]{2,1,0:T(8,128)S(1)}, f32[2,64,1024]{2,1,0:T(8,128)S(1)}, u32[]{:S(2)}, u32[]{:S(2)}) collective-permute-start(f32[2,64,1024]{2,1,0:T(8,128)S(1)} %shard_map.124), channel_id=1, source_target_pairs={{4,0},{8,4},{12,8},{5,1},{9,5},{13,9},{6,2},{10,6},{14,10},{7,3},{... | collective-permute-start | bytes 1572872 | tf_op jit(solution)/shard_map/ppermute | solution.py:30
  23.6 1.9 %shard_map.125 = (f32[2,64,1024]{2,1,0:T(8,128)S(1)}, f32[2,64,1024]{2,1,0:T(8,128)S(1)}) custom-call(s32[16]{0:T(128)S(1)} %copy-done.9, s32[16]{0:T(128)S(1)} %copy-done.7, f32[2,64,256]{2,1,0:T(8,128)S(1)} %copy-done.4, f32[2,72,256]{2,1,0:T(8,128)S(1)} %copy-done.2, f32[2,256,1024]{2,1,0:T(8,128)S(1)} %copy-done.1), custom_call_target="tpu_custom_call" | custom-call | flops 1 | bytes 1 | tf_op jit(solution)/shard_map/pallas_call | solution.py:58
  25.6 0.1 collective-permute-start.3
  25.7 0.0 all-to-all-done.1.refs_2_
  25.7 6.6 %collective-permute-start.11 = (f32[2,64,1024]{2,1,0:T(8,128)S(1)}, f32[2,64,1024]{2,1,0:T(8,128)}, u32[]{:S(2)}, u32[]{:S(2)}) collective-permute-start(f32[2,64,1024]{2,1,0:T(8,128)S(1)} %get-tuple-element.33.left_ref.refs_12_), channel_id=1, source_target_pairs={{0,4},{4,8},{8,12},{1,5},{5,9},{9,13},{2,6},{6,10},{10,14},{3,7},{... | collective-permute-start | bytes 1572872 | tf_op jit(solution)/shard_map/ppermute | solution.py:30
  32.3 0.2 collective-permute-start.2
  32.5 0.3 collective-permute-start.4
  32.8 1.0 %collective-permute-done.4.refs_7_ = f32[2,64,256]{2,1,0:T(8,128)S(1)} collective-permute-done((f32[2,64,256]{2,1,0:T(8,128)S(1)}, f32[2,64,256]{2,1,0:T(8,128)S(1)}, u32[]{:S(2)}, u32[]{:S(2)}) %collective-permute-start.4) | collective-permute-done | bytes 131104 | tf_op jit(solution)/shard_map/ppermute | solution.py:34
  33.8 0.0 collective-permute-done.2.refs_9_
  33.8 5.0 %collective-permute-done.1.down_ref = f32[2,64,1024]{2,1,0:T(8,128)S(1)} collective-permute-done((f32[2,64,1024]{2,1,0:T(8,128)S(1)}, f32[2,64,1024]{2,1,0:T(8,128)S(1)}, u32[]{:S(2)}, u32[]{:S(2)}) %collective-permute-start.1) | collective-permute-done | bytes 524320 | tf_op jit(solution)/shard_map/ppermute | solution.py:30
  38.9 0.0 collective-permute-done.3.refs_13_
  38.9 1.0 %shard_map.126 = (f32[64,128]{1,0:T(8,128)S(1)}, f32[2,64,1024]{2,1,0:T(8,128)S(1)}) custom-call(s32[16]{0:T(128)S(1)} %copy-done.9, s32[16]{0:T(128)S(1)} %copy-done.8, s32[16]{0:T(128)S(1)} %copy-done.10, f32[8]{0:T(128)S(1)} %copy-done.11, f32[2,72,256]{2,1,0:T(8,128)S(1)} %copy-done.2, f32[2,64,1024]{2,1,0:T(8,128)S(1)} %get-tuple-element.33.left_ref.refs_12_, ...), custom_call_target="tpu_custom_call" | custom-call | tf_op jit(solution)/shard_map/pallas_call | solution.py:58
  39.9 1.6 %collective-permute-start.5 = (f32[64,128]{1,0:T(8,128)S(1)}, f32[64,128]{1,0:T(8,128)S(1)}, u32[]{:S(2)}, u32[]{:S(2)}) collective-permute-start(f32[64,128]{1,0:T(8,128)S(1)} %get-tuple-element.27), channel_id=1, source_target_pairs={{0,2},{2,0},{1,3},{3,1},{4,6},{6,4},{5,7},{7,5},{8,10},{10,8},{9,1... | collective-permute-start | bytes 98312 | tf_op jit(solution)/shard_map/ppermute | solution.py:34
  41.5 2.4 %collective-permute-done.5 = f32[64,128]{1,0:T(8,128)S(1)} collective-permute-done((f32[64,128]{1,0:T(8,128)S(1)}, f32[64,128]{1,0:T(8,128)S(1)}, u32[]{:S(2)}, u32[]{:S(2)}) %collective-permute-start.5) | collective-permute-done | bytes 32800 | tf_op jit(solution)/shard_map/ppermute | solution.py:34
  43.9 1.5 %collective-permute-start.7 = (f32[4,136,128]{2,1,0:T(8,128)S(1)}, f32[4,136,128]{2,1,0:T(8,128)S(1)}, u32[]{:S(2)}, u32[]{:S(2)}) collective-permute-start(f32[4,136,128]{2,1,0:T(8,128)S(1)} %all-to-all-done.1.refs_2_), channel_id=1, source_target_pairs={{0,2},{2,0},{1,3},{3,1},{4,6},{6,4},{5,7},{7,5},{8,10},{10,8},{9,1... | collective-permute-start | bytes 835592 | tf_op jit(solution)/shard_map/ppermute | solution.py:34
  45.4 0.0 collective-permute-start.13
  45.4 0.0 collective-permute-done.11.refs_14_
  45.4 0.5 collective-permute-start.12
  45.9 0.7 broadcast_in_dim.2
  46.6 4.8 %all-to-all-start = ((f32[4,64,128]{2,1,0:T(8,128)}), f32[4,64,128]{2,1,0:T(8,128)S(1)}, u32[]{:S(2)}, u32[]{:S(2)}) async-start(f32[4,64,128]{2,1,0:T(8,128)} %broadcast_in_dim.2), calls=%async_computation | async-start | bytes 262144 | tf_op jit(solution)/shard_map/all_to_all | solution.py:501
  51.4 0.0 collective-permute-start.10
  51.4 0.5 collective-permute-start.8
  51.9 5.8 %all-to-all-done.refs_0_ = f32[4,64,128]{2,1,0:T(8,128)S(1)} async-done(((f32[4,64,128]{2,1,0:T(8,128)}), f32[4,64,128]{2,1,0:T(8,128)S(1)}, u32[]{:S(2)}, u32[]{:S(2)}) %all-to-all-start) | async-done | bytes 131104 | tf_op jit(solution)/shard_map/all_to_all | solution.py:501
  57.7 0.0 collective-permute-done.7.refs_3_
  57.7 0.1 collective-permute-start.9
  57.7 0.0 collective-permute-done.10.refs_11_
  57.8 0.5 collective-permute-start.6
  58.2 0.0 collective-permute-done.8.refs_4_
  58.2 1.2 %collective-permute-done.6.refs_1_ = f32[4,64,128]{2,1,0:T(8,128)S(1)} collective-permute-done((f32[4,64,128]{2,1,0:T(8,128)S(1)}, f32[4,64,128]{2,1,0:T(8,128)S(1)}, u32[]{:S(2)}, u32[]{:S(2)}) %collective-permute-start.6) | collective-permute-done | bytes 131104 | tf_op jit(solution)/shard_map/ppermute | solution.py:34
  59.5 0.0 collective-permute-done.13.refs_17_
  59.6 0.5 copy-done.22
  60.1 0.2 copy-done.13
  60.3 0.1 copy-done.18
  60.4 0.2 copy-done.14
  60.6 8.3 %shard_map.127 = (f32[2,4096]{1,0:T(2,128)}, f32[2,128,1024]{2,1,0:T(8,128)}) custom-call(s32[16]{0:T(128)} %first.5, s32[16]{0:T(128)} %second.7, s32[16]{0:T(128)} %ranks.3, s32[4,16]{1,0:T(4,128)} %bitcast.1, f32[8]{0:T(128)} %occupied.3, f32[4,64,128]{2,1,0:T(8,128)} %copy-done.15, f32[4,64,128]{2,1,0:T(8,128)} %copy-done.22, f32[4,136,128]{2,1,0:T(8,128)} %copy-done.12, ...), custom_call_target="tpu_custom_call" | custom-call | tf_op jit(solution)/shard_map/pallas_call | solution.py:58
  (38 shorter events, 0.1 us)
Async XLA Ops:
  0.6 23.0 %copy-start.4 = (f32[2,64,256]{2,1,0:T(8,128)S(1)}, f32[2,64,256]{2,1,0:T(8,128)}, u32[]{:S(2)}) copy-start(f32[2,64,256]{2,1,0:T(8,128)} %refs_6_.1) | copy-start | bytes 393220
  0.6 23.0 %copy-start.9 = (s32[16]{0:T(128)S(1)}, s32[16]{0:T(128)}, u32[]{:S(2)}) copy-start(s32[16]{0:T(128)} %first.5) | copy-start | bytes 196
  2.6 21.0 %copy-start.2 = (f32[2,72,256]{2,1,0:T(8,128)S(1)}, f32[2,72,256]{2,1,0:T(8,128)}, u32[]{:S(2)}) copy-start(f32[2,72,256]{2,1,0:T(8,128)} %shard_map.122.mp_in.mp_ref.refs_8_) | copy-start | bytes 442372
  4.4 34.5 %copy-start.8 = (s32[16]{0:T(128)S(1)}, s32[16]{0:T(128)}, u32[]{:S(2)}) copy-start(s32[16]{0:T(128)} %second.7) | copy-start | bytes 196
  4.4 34.5 %copy-start.10 = (s32[16]{0:T(128)S(1)}, s32[16]{0:T(128)}, u32[]{:S(2)}) copy-start(s32[16]{0:T(128)} %ranks.3) | copy-start | bytes 196
  4.4 34.5 %copy-start.11 = (f32[8]{0:T(128)S(1)}, f32[8]{0:T(128)}, u32[]{:S(2)}) copy-start(f32[8]{0:T(128)} %occupied.3) | copy-start | bytes 100
  4.4 21.3 %all-to-all-start.1 = ((f32[4,136,128]{2,1,0:T(8,128)}), f32[4,136,128]{2,1,0:T(8,128)S(1)}, u32[]{:S(2)}, u32[]{:S(2)}) async-start(f32[4,136,128]{2,1,0:T(8,128)} %shard_map.123), calls=%async_computation.1 | async-start | bytes 557056 | tf_op jit(solution)/shard_map/all_to_all | solution.py:461
  10.9 7.9 %collective-permute-start = (f32[2,72,256]{2,1,0:T(8,128)}, f32[2,72,256]{2,1,0:T(8,128)S(1)}, u32[]{:S(2)}, u32[]{:S(2)}) collective-permute-start(f32[2,72,256]{2,1,0:T(8,128)} %shard_map.122.mp_in.mp_ref.refs_8_), channel_id=1, source_target_pairs={{0,4},{4,8},{8,12},{1,5},{5,9},{9,13},{2,6},{6,10},{10,14},{3,7},{... | collective-permute-start | bytes 442376 | tf_op jit(solution)/shard_map/ppermute | solution.py:30
  18.8 1.6 %copy-start = (f32[2,256,1024]{2,1,0:T(8,128)S(1)}, f32[2,256,1024]{2,1,0:T(8,128)}, u32[]{:S(2)}) copy-start(f32[2,256,1024]{2,1,0:T(8,128)} %b_ref.3) | copy-start | bytes 6291460
  20.3 0.7 copy-start.7
  21.0 30.4 %copy-start.5 = (f32[2,72,256]{2,1,0:T(8,128)}, f32[2,72,256]{2,1,0:T(8,128)S(1)}, u32[]{:S(2)}) copy-start(f32[2,72,256]{2,1,0:T(8,128)S(1)} %collective-permute-done.mp_below.refs_10_) | copy-start | bytes 442372
  21.0 2.6 %copy-start.1 = (f32[2,256,1024]{2,1,0:T(8,128)S(1)}, f32[2,256,1024]{2,1,0:T(8,128)}, u32[]{:S(2)}) copy-start(f32[2,256,1024]{2,1,0:T(8,128)} %b_ref.3) | copy-start | bytes 6291460
  22.3 16.5 %collective-permute-start.1 = (f32[2,64,1024]{2,1,0:T(8,128)S(1)}, f32[2,64,1024]{2,1,0:T(8,128)S(1)}, u32[]{:S(2)}, u32[]{:S(2)}) collective-permute-start(f32[2,64,1024]{2,1,0:T(8,128)S(1)} %shard_map.124), channel_id=1, source_target_pairs={{4,0},{8,4},{12,8},{5,1},{9,5},{13,9},{6,2},{10,6},{14,10},{7,3},{... | collective-permute-start | bytes 1572872 | tf_op jit(solution)/shard_map/ppermute | solution.py:30
  25.6 33.9 %copy-start.3 = (f32[2,64,1024]{2,1,0:T(8,128)}, f32[2,64,1024]{2,1,0:T(8,128)S(1)}, u32[]{:S(2)}) copy-start(f32[2,64,1024]{2,1,0:T(8,128)S(1)} %get-tuple-element.33.left_ref.refs_12_) | copy-start | bytes 1572868
  25.6 13.3 %collective-permute-start.3 = (f32[2,64,1024]{2,1,0:T(8,128)S(1)}, f32[2,64,1024]{2,1,0:T(8,128)}, u32[]{:S(2)}, u32[]{:S(2)}) collective-permute-start(f32[2,64,1024]{2,1,0:T(8,128)S(1)} %get-tuple-element.33.left_ref.refs_12_), channel_id=1, source_target_pairs={{0,1},{1,0},{2,3},{3,2},{4,5},{5,4},{6,7},{7,6},{8,9},{9,8},{10,11... | collective-permute-start | bytes 1572872 | tf_op jit(solution)/shard_map/ppermute | solution.py:34
  25.7 33.9 %copy-start.12 = (f32[4,136,128]{2,1,0:T(8,128)}, f32[4,136,128]{2,1,0:T(8,128)S(1)}, u32[]{:S(2)}) copy-start(f32[4,136,128]{2,1,0:T(8,128)S(1)} %all-to-all-done.1.refs_2_) | copy-start | bytes 835588
  25.7 19.7 %collective-permute-start.11 = (f32[2,64,1024]{2,1,0:T(8,128)S(1)}, f32[2,64,1024]{2,1,0:T(8,128)}, u32[]{:S(2)}, u32[]{:S(2)}) collective-permute-start(f32[2,64,1024]{2,1,0:T(8,128)S(1)} %get-tuple-element.33.left_ref.refs_12_), channel_id=1, source_target_pairs={{0,4},{4,8},{8,12},{1,5},{5,9},{9,13},{2,6},{6,10},{10,14},{3,7},{... | collective-permute-start | bytes 1572872 | tf_op jit(solution)/shard_map/ppermute | solution.py:30
  32.3 1.6 %collective-permute-start.2 = (f32[2,72,256]{2,1,0:T(8,128)S(1)}, f32[2,72,256]{2,1,0:T(8,128)S(1)}, u32[]{:S(2)}, u32[]{:S(2)}) collective-permute-start(f32[2,72,256]{2,1,0:T(8,128)S(1)} %copy-done.2), channel_id=1, source_target_pairs={{0,1},{1,0},{2,3},{3,2},{4,5},{5,4},{6,7},{7,6},{8,9},{9,8},{10,11... | collective-permute-start | bytes 442376 | tf_op jit(solution)/shard_map/ppermute | solution.py:34
  32.5 1.4 %collective-permute-start.4 = (f32[2,64,256]{2,1,0:T(8,128)S(1)}, f32[2,64,256]{2,1,0:T(8,128)S(1)}, u32[]{:S(2)}, u32[]{:S(2)}) collective-permute-start(f32[2,64,256]{2,1,0:T(8,128)S(1)} %copy-done.4), channel_id=1, source_target_pairs={{0,1},{1,0},{2,3},{3,2},{4,5},{5,4},{6,7},{7,6},{8,9},{9,8},{10,11... | collective-permute-start | bytes 393224 | tf_op jit(solution)/shard_map/ppermute | solution.py:34
  33.8 5.0 %copy-start.21 = (f32[2,64,256]{2,1,0:T(8,128)}, f32[2,64,256]{2,1,0:T(8,128)S(1)}, u32[]{:S(2)}) copy-start(f32[2,64,256]{2,1,0:T(8,128)S(1)} %collective-permute-done.4.refs_7_) | copy-start | bytes 393220
  33.8 25.7 %copy-start.19 = (f32[2,72,256]{2,1,0:T(8,128)}, f32[2,72,256]{2,1,0:T(8,128)S(1)}, u32[]{:S(2)}) copy-start(f32[2,72,256]{2,1,0:T(8,128)S(1)} %collective-permute-done.2.refs_9_) | copy-start | bytes 442372
  39.9 19.6 %copy-start.6 = (f32[2,64,1024]{2,1,0:T(8,128)}, f32[2,64,1024]{2,1,0:T(8,128)S(1)}, u32[]{:S(2)}) copy-start(f32[2,64,1024]{2,1,0:T(8,128)S(1)} %get-tuple-element.35.refs_16_) | copy-start | bytes 1572868
  39.9 4.0 %collective-permute-start.5 = (f32[64,128]{1,0:T(8,128)S(1)}, f32[64,128]{1,0:T(8,128)S(1)}, u32[]{:S(2)}, u32[]{:S(2)}) collective-permute-start(f32[64,128]{1,0:T(8,128)S(1)} %get-tuple-element.27), channel_id=1, source_target_pairs={{0,2},{2,0},{1,3},{3,1},{4,6},{6,4},{5,7},{7,5},{8,10},{10,8},{9,1... | collective-permute-start | bytes 98312 | tf_op jit(solution)/shard_map/ppermute | solution.py:34
  43.9 13.8 %collective-permute-start.7 = (f32[4,136,128]{2,1,0:T(8,128)S(1)}, f32[4,136,128]{2,1,0:T(8,128)S(1)}, u32[]{:S(2)}, u32[]{:S(2)}) collective-permute-start(f32[4,136,128]{2,1,0:T(8,128)S(1)} %all-to-all-done.1.refs_2_), channel_id=1, source_target_pairs={{0,2},{2,0},{1,3},{3,1},{4,6},{6,4},{5,7},{7,5},{8,10},{10,8},{9,1... | collective-permute-start | bytes 835592 | tf_op jit(solution)/shard_map/ppermute | solution.py:34
  45.4 14.1 %collective-permute-start.13 = (f32[2,64,1024]{2,1,0:T(8,128)S(1)}, f32[2,64,1024]{2,1,0:T(8,128)S(1)}, u32[]{:S(2)}, u32[]{:S(2)}) collective-permute-start(f32[2,64,1024]{2,1,0:T(8,128)S(1)} %get-tuple-element.35.refs_16_), channel_id=1, source_target_pairs={{0,1},{1,0},{2,3},{3,2},{4,5},{5,4},{6,7},{7,6},{8,9},{9,8},{10,11... | collective-permute-start | bytes 1572872 | tf_op jit(solution)/shard_map/ppermute | solution.py:34
  45.4 14.1 %collective-permute-start.12 = (f32[2,64,1024]{2,1,0:T(8,128)}, f32[2,64,1024]{2,1,0:T(8,128)S(1)}, u32[]{:S(2)}, u32[]{:S(2)}) collective-permute-start(f32[2,64,1024]{2,1,0:T(8,128)} %collective-permute-done.11.refs_14_), channel_id=1, source_target_pairs={{0,1},{1,0},{2,3},{3,2},{4,5},{5,4},{6,7},{7,6},{8,9},{9,8},{10,11... | collective-permute-start | bytes 1572872 | tf_op jit(solution)/shard_map/ppermute | solution.py:34
  46.6 11.1 %all-to-all-start = ((f32[4,64,128]{2,1,0:T(8,128)}), f32[4,64,128]{2,1,0:T(8,128)S(1)}, u32[]{:S(2)}, u32[]{:S(2)}) async-start(f32[4,64,128]{2,1,0:T(8,128)} %broadcast_in_dim.2), calls=%async_computation | async-start | bytes 262144 | tf_op jit(solution)/shard_map/all_to_all | solution.py:501
  51.4 6.4 %collective-permute-start.10 = (f32[2,72,256]{2,1,0:T(8,128)S(1)}, f32[2,72,256]{2,1,0:T(8,128)S(1)}, u32[]{:S(2)}, u32[]{:S(2)}) collective-permute-start(f32[2,72,256]{2,1,0:T(8,128)S(1)} %collective-permute-done.mp_below.refs_10_), channel_id=1, source_target_pairs={{0,1},{1,0},{2,3},{3,2},{4,5},{5,4},{6,7},{7,6},{8,9},{9,8},{10,11... | collective-permute-start | bytes 442376 | tf_op jit(solution)/shard_map/ppermute | solution.py:34
  51.4 6.9 %collective-permute-start.8 = (f32[4,136,128]{2,1,0:T(8,128)S(1)}, f32[4,136,128]{2,1,0:T(8,128)S(1)}, u32[]{:S(2)}, u32[]{:S(2)}) collective-permute-start(f32[4,136,128]{2,1,0:T(8,128)S(1)} %all-to-all-done.1.refs_2_), channel_id=1, source_target_pairs={{0,1},{1,0},{2,3},{3,2},{4,5},{5,4},{6,7},{7,6},{8,9},{9,8},{10,11... | collective-permute-start | bytes 835592 | tf_op jit(solution)/shard_map/ppermute | solution.py:34
  57.7 1.9 %copy-start.15 = (f32[4,64,128]{2,1,0:T(8,128)}, f32[4,64,128]{2,1,0:T(8,128)S(1)}, u32[]{:S(2)}) copy-start(f32[4,64,128]{2,1,0:T(8,128)S(1)} %all-to-all-done.refs_0_) | copy-start | bytes 393220
  57.7 1.9 %copy-start.16 = (f32[4,136,128]{2,1,0:T(8,128)}, f32[4,136,128]{2,1,0:T(8,128)S(1)}, u32[]{:S(2)}) copy-start(f32[4,136,128]{2,1,0:T(8,128)S(1)} %collective-permute-done.7.refs_3_) | copy-start | bytes 835588
  57.7 1.8 %collective-permute-start.9 = (f32[4,136,128]{2,1,0:T(8,128)S(1)}, f32[4,136,128]{2,1,0:T(8,128)S(1)}, u32[]{:S(2)}, u32[]{:S(2)}) collective-permute-start(f32[4,136,128]{2,1,0:T(8,128)S(1)} %collective-permute-done.7.refs_3_), channel_id=1, source_target_pairs={{0,1},{1,0},{2,3},{3,2},{4,5},{5,4},{6,7},{7,6},{8,9},{9,8},{10,11... | collective-permute-start | bytes 835592 | tf_op jit(solution)/shard_map/ppermute | solution.py:34
  57.7 1.8 %copy-start.20 = (f32[2,72,256]{2,1,0:T(8,128)}, f32[2,72,256]{2,1,0:T(8,128)S(1)}, u32[]{:S(2)}) copy-start(f32[2,72,256]{2,1,0:T(8,128)S(1)} %collective-permute-done.10.refs_11_) | copy-start | bytes 442372
  57.8 1.7 %collective-permute-start.6 = (f32[4,64,128]{2,1,0:T(8,128)S(1)}, f32[4,64,128]{2,1,0:T(8,128)S(1)}, u32[]{:S(2)}, u32[]{:S(2)}) collective-permute-start(f32[4,64,128]{2,1,0:T(8,128)S(1)} %all-to-all-done.refs_0_), channel_id=1, source_target_pairs={{0,1},{1,0},{2,3},{3,2},{4,5},{5,4},{6,7},{7,6},{8,9},{9,8},{10,11... | collective-permute-start | bytes 393224 | tf_op jit(solution)/shard_map/ppermute | solution.py:34
  58.2 1.3 %copy-start.17 = (f32[4,136,128]{2,1,0:T(8,128)}, f32[4,136,128]{2,1,0:T(8,128)S(1)}, u32[]{:S(2)}) copy-start(f32[4,136,128]{2,1,0:T(8,128)S(1)} %collective-permute-done.8.refs_4_) | copy-start | bytes 835588
  59.5 0.7 copy-start.22
  59.5 0.8 %copy-start.13 = (f32[2,64,1024]{2,1,0:T(8,128)}, f32[2,64,1024]{2,1,0:T(8,128)S(1)}, u32[]{:S(2)}) copy-start(f32[2,64,1024]{2,1,0:T(8,128)S(1)} %collective-permute-done.13.refs_17_) | copy-start | bytes 1572868
  59.5 0.9 %copy-start.18 = (f32[4,136,128]{2,1,0:T(8,128)}, f32[4,136,128]{2,1,0:T(8,128)S(1)}, u32[]{:S(2)}) copy-start(f32[4,136,128]{2,1,0:T(8,128)S(1)} %collective-permute-done.9.refs_5_) | copy-start | bytes 835588
  59.5 1.1 %copy-start.14 = (f32[2,64,1024]{2,1,0:T(8,128)}, f32[2,64,1024]{2,1,0:T(8,128)S(1)}, u32[]{:S(2)}) copy-start(f32[2,64,1024]{2,1,0:T(8,128)S(1)} %collective-permute-done.12.refs_15_) | copy-start | bytes 1572868

commit v13 on v12

--- a/solution.py
+++ b/solution.py
@@ -478,7 +478,6 @@
         limit=8,
         cost=BRIEF,
     )
-    left_below = shifted(gate((left,), packs[0])[0], "orb", 1)
     mp_other = swapped(gate((mp,), right_here)[0], "sub")
     left_other = swapped(left, "sub")
     c_other = swapped(gate((coefficients,), right_here)[0], "sub")
@@ -496,7 +495,7 @@
         packs.append(None)
         packs.append(swapped(gate(packs[:1], part)[0], "sub"))
         sums = part + swapped(part, "fit")
-        packs[1] = swapped(gate(packs[:1], sums)[0], "fit")
+        packs[1] = swapped(gate(packs[:1], part)[0], "fit")
         start_amps = [
             lax.all_to_all(jnp.broadcast_to(sums[None], (z.owners, *sums.shape)), "orb", 0, 0)
         ]
@@ -507,7 +506,8 @@
         start_amps = [lax.all_gather(sums, ("orb", "sub"), axis=0, tiled=False)]
 
     right_late, mp_late = gate((right, mp_below), part)
-    (left_late,) = gate((left_below,), sums)
+    left_below = shifted(gate((left,), part)[0], "orb", 1)
+    (left_late,) = gate((left_below,), start_amps[0])
     right_other, mp_below_other, left_below_other = [
         swapped(value, "sub") for value in (right_late, mp_late, left_late)
     ]

time: 69.4 us -> 65.6 us (0.945)
  starting transfers between devices: 28.3 us -> 26.1 us
  waiting for transfers between devices: 19.5 us -> 17.4 us
    all_to_all x1, starting transfers between devices: 4.81 us -> 3.33 us  [body(): lax.all_to_all(jnp.broadcast_to(sums[None], (z.owners, *sums.shape)), 'or...]
    all_to_all x1, waiting for transfers between devices: 5.76 us -> 4.31 us  [body(): lax.all_to_all(jnp.broadcast_to(sums[None], (z.owners, *sums.shape)), 'or...]
    ppermute x3, waiting for transfers between devices: 9 us -> 7.58 us  [shifted(): lax.ppermute(value, axis, [(source, source + steps) for source in range(i...]
    ppermute x11, waiting for transfers between devices: 4.72 us -> 5.51 us  [swapped(): return lax.ppermute(value, axis, [(0, 1), (1, 0)])]
  transfers between devices with their start and end apart: 16 -> 16, of which waited for: 6 -> 7; matrix products, arithmetic and copies ran while one was open for 1% -> 1% of each run, Pallas kernels for 6% -> 7%
where the time goes in v13:
time: 65.6 us; the launch traced here: 65.1 us
  starting transfers between devices  26.1 us (40%)
  waiting for transfers between devices  17.4 us (27%)
  Pallas kernels  16.1 us (25%)
  local copies, waits for them, and re-layouts  4.49 us (7%)
  between operations  0.95 us (1%)
    pallas_call x6, Pallas kernels, call(): pl.pallas_call(kernel, out_shape=[jax.ShapeDtypeStruct(shape, jnp.float32...  16.1 us
    ppermute x3, starting transfers between devices, shifted(): lax.ppermute(value, axis, [(source, source + steps) for source in range(i...  11.2 us
    ppermute x3, waiting for transfers between devices, shifted(): lax.ppermute(value, axis, [(source, source + steps) for source in range(i...  7.58 us
    all_to_all x1, starting transfers between devices, body(): packs = [lax.all_to_all(pack, 'orb', 0, 0)]  6.76 us
    ppermute x11, waiting for transfers between devices, swapped(): return lax.ppermute(value, axis, [(0, 1), (1, 0)])  5.51 us
    ppermute x11, starting transfers between devices, swapped(): return lax.ppermute(value, axis, [(0, 1), (1, 0)])  4.83 us
    all_to_all x1, waiting for transfers between devices, body(): lax.all_to_all(jnp.broadcast_to(sums[None], (z.owners, *sums.shape)), 'or...  4.31 us
    unnamed x46, local copies, waits for them, and re-layouts  3.79 us
  transfers between devices with their start and end apart: 16, of which 7 were waited for; matrix products, arithmetic and copies ran while one was open for 1% of the time, Pallas kernels for 7%

profile of v13, /device:TPU:0, one launch (start us, length us, event | category | flops | bytes accessed | tf_op | source)
XLA Modules:
  0.0 65.1 jit_solution(11417919334730163520)
XLA Ops:
  0.6 0.0 copy-start.4
  0.6 0.0 copy-start.8
  0.7 0.0 copy-start.9
  0.7 2.0 %shard_map.122.mp_in.mp_ref.refs_8_ = f32[2,72,256]{2,1,0:T(8,128)} custom-call(f32[2,64,256]{2,1,0:T(8,128)} %refs_6_.1, s32[2,256]{1,0:T(2,128)} %map_in.1, f32[2,64]{1,0:T(2,128)} %e_in.1, f32[2,4]{1,0:T(2,128)} %coupling_in.1), custom_call_target="tpu_custom_call" | custom-call | tf_op jit(solution)/shard_map/pallas_call | solution.py:58
  2.6 5.1 %collective-permute-start = (f32[2,72,256]{2,1,0:T(8,128)}, f32[2,72,256]{2,1,0:T(8,128)S(1)}, u32[]{:S(2)}, u32[]{:S(2)}) collective-permute-start(f32[2,72,256]{2,1,0:T(8,128)} %shard_map.122.mp_in.mp_ref.refs_8_), channel_id=1, source_target_pairs={{0,4},{4,8},{8,12},{1,5},{5,9},{9,13},{2,6},{6,10},{10,14},{3,7},{... | collective-permute-start | bytes 442376 | tf_op jit(solution)/shard_map/ppermute | solution.py:30
  7.7 1.7 %shard_map.123 = f32[4,136,128]{2,1,0:T(8,128)} custom-call(f32[2,4,4096]{2,1,0:T(4,128)} %s_in.1, f32[2,72,256]{2,1,0:T(8,128)} %shard_map.122.mp_in.mp_ref.refs_8_), custom_call_target="tpu_custom_call" | custom-call | tf_op jit(solution)/shard_map/pallas_call | solution.py:58
  9.4 1.7 %collective-permute-done.mp_below.refs_10_ = f32[2,72,256]{2,1,0:T(8,128)S(1)} collective-permute-done((f32[2,72,256]{2,1,0:T(8,128)}, f32[2,72,256]{2,1,0:T(8,128)S(1)}, u32[]{:S(2)}, u32[]{:S(2)}) %collective-permute-start) | collective-permute-done | bytes 147488 | tf_op jit(solution)/shard_map/ppermute | solution.py:30
  11.1 1.6 %copy-done = f32[2,256,1024]{2,1,0:T(8,128)S(1)} copy-done((f32[2,256,1024]{2,1,0:T(8,128)S(1)}, f32[2,256,1024]{2,1,0:T(8,128)}, u32[]{:S(2)}) %copy-start) | copy-done | bytes 2097176
  12.7 0.7 %copy-done.7 = s32[16]{0:T(128)S(1)} copy-done((s32[16]{0:T(128)S(1)}, s32[16]{0:T(128)}, u32[]{:S(2)}) %copy-start.7) | copy-done | bytes 88
  13.4 1.3 %shard_map.124 = f32[2,64,1024]{2,1,0:T(8,128)S(1)} custom-call(s32[16]{0:T(128)S(1)} %copy-done.7, f32[2,72,256]{2,1,0:T(8,128)S(1)} %collective-permute-done.mp_below.refs_10_, f32[2,256,1024]{2,1,0:T(8,128)S(1)} %copy-done), custom_call_target="tpu_custom_call" | custom-call | tf_op jit(solution)/shard_map/pallas_call | solution.py:58
  14.7 0.0 copy-start.10
  14.7 0.0 copy-start.11
  14.7 1.3 %collective-permute-start.1 = (f32[2,64,1024]{2,1,0:T(8,128)S(1)}, f32[2,64,1024]{2,1,0:T(8,128)S(1)}, u32[]{:S(2)}, u32[]{:S(2)}) collective-permute-start(f32[2,64,1024]{2,1,0:T(8,128)S(1)} %shard_map.124), channel_id=1, source_target_pairs={{4,0},{8,4},{12,8},{5,1},{9,5},{13,9},{6,2},{10,6},{14,10},{7,3},{... | collective-permute-start | bytes 1572872 | tf_op jit(solution)/shard_map/ppermute | solution.py:30
  16.0 1.9 %shard_map.125 = (f32[2,64,1024]{2,1,0:T(8,128)S(1)}, f32[2,64,1024]{2,1,0:T(8,128)S(1)}) custom-call(s32[16]{0:T(128)S(1)} %copy-done.9, s32[16]{0:T(128)S(1)} %copy-done.8, f32[2,64,256]{2,1,0:T(8,128)S(1)} %copy-done.4, f32[2,72,256]{2,1,0:T(8,128)S(1)} %copy-done.2, f32[2,256,1024]{2,1,0:T(8,128)S(1)} %copy-done.1), custom_call_target="tpu_custom_call" | custom-call | flops 1 | bytes 1 | tf_op jit(solution)/shard_map/pallas_call | solution.py:58
  18.0 0.1 collective-permute-start.3
  18.1 0.5 collective-permute-start.2
  18.6 0.1 collective-permute-start.4
  18.6 6.8 %all-to-all-start.1 = ((f32[4,136,128]{2,1,0:T(8,128)}), f32[4,136,128]{2,1,0:T(8,128)S(1)}, u32[]{:S(2)}, u32[]{:S(2)}) async-start(f32[4,136,128]{2,1,0:T(8,128)} %shard_map.123), calls=%async_computation.1 | async-start | bytes 557056 | tf_op jit(solution)/shard_map/all_to_all | solution.py:461
  25.4 0.0 collective-permute-done.4.refs_7_
  25.4 0.0 collective-permute-done.2.refs_9_
  25.4 5.9 %collective-permute-done.1.down_ref = f32[2,64,1024]{2,1,0:T(8,128)S(1)} collective-permute-done((f32[2,64,1024]{2,1,0:T(8,128)S(1)}, f32[2,64,1024]{2,1,0:T(8,128)S(1)}, u32[]{:S(2)}, u32[]{:S(2)}) %collective-permute-start.1) | collective-permute-done | bytes 524320 | tf_op jit(solution)/shard_map/ppermute | solution.py:30
  31.3 0.0 collective-permute-done.3.refs_13_
  31.3 1.0 %shard_map.126 = (f32[64,128]{1,0:T(8,128)S(1)}, f32[2,64,1024]{2,1,0:T(8,128)S(1)}) custom-call(s32[16]{0:T(128)S(1)} %copy-done.9, s32[16]{0:T(128)S(1)} %copy-done.8, s32[16]{0:T(128)S(1)} %copy-done.10, f32[8]{0:T(128)S(1)} %copy-done.11, f32[2,72,256]{2,1,0:T(8,128)S(1)} %copy-done.2, f32[2,64,1024]{2,1,0:T(8,128)S(1)} %get-tuple-element.31.left_ref.refs_12_, ...), custom_call_target="tpu_custom_call" | custom-call | tf_op jit(solution)/shard_map/pallas_call | solution.py:58
  32.3 4.8 %collective-permute-start.11 = (f32[2,64,1024]{2,1,0:T(8,128)S(1)}, f32[2,64,1024]{2,1,0:T(8,128)S(1)}, u32[]{:S(2)}, u32[]{:S(2)}) collective-permute-start(f32[2,64,1024]{2,1,0:T(8,128)S(1)} %get-tuple-element.31.left_ref.refs_12_), channel_id=1, source_target_pairs={{0,4},{4,8},{8,12},{1,5},{5,9},{9,13},{2,6},{6,10},{10,14},{3,7},{... | collective-permute-start | bytes 1572872 | tf_op jit(solution)/shard_map/ppermute | solution.py:30
  37.2 1.6 %collective-permute-start.5 = (f32[64,128]{1,0:T(8,128)S(1)}, f32[64,128]{1,0:T(8,128)S(1)}, u32[]{:S(2)}, u32[]{:S(2)}) collective-permute-start(f32[64,128]{1,0:T(8,128)S(1)} %get-tuple-element.26), channel_id=1, source_target_pairs={{0,2},{2,0},{1,3},{3,1},{4,6},{6,4},{5,7},{7,5},{8,10},{10,8},{9,1... | collective-permute-start | bytes 98312 | tf_op jit(solution)/shard_map/ppermute | solution.py:34
  38.8 2.4 %collective-permute-done.5 = f32[64,128]{1,0:T(8,128)S(1)} collective-permute-done((f32[64,128]{1,0:T(8,128)S(1)}, f32[64,128]{1,0:T(8,128)S(1)}, u32[]{:S(2)}, u32[]{:S(2)}) %collective-permute-start.5) | collective-permute-done | bytes 32800 | tf_op jit(solution)/shard_map/ppermute | solution.py:34
  41.2 0.0 all-to-all-done.1.refs_2_
  41.2 0.7 %broadcast_in_dim.2 = f32[4,64,128]{2,1,0:T(8,128)} broadcast(f32[64,128]{1,0:T(8,128)S(1)} %add.3), dimensions={1,2} | broadcast | bytes 163840 | tf_op jit(solution)/shard_map/broadcast_in_dim | solution.py:500
  41.9 3.3 %all-to-all-start = ((f32[4,64,128]{2,1,0:T(8,128)}), f32[4,64,128]{2,1,0:T(8,128)S(1)}, u32[]{:S(2)}, u32[]{:S(2)}) async-start(f32[4,64,128]{2,1,0:T(8,128)} %broadcast_in_dim.2), calls=%async_computation | async-start | bytes 262144 | tf_op jit(solution)/shard_map/all_to_all | solution.py:500
  45.2 1.6 %collective-permute-start.7 = (f32[4,136,128]{2,1,0:T(8,128)S(1)}, f32[4,136,128]{2,1,0:T(8,128)}, u32[]{:S(2)}, u32[]{:S(2)}) collective-permute-start(f32[4,136,128]{2,1,0:T(8,128)S(1)} %all-to-all-done.1.refs_2_), channel_id=1, source_target_pairs={{0,2},{2,0},{1,3},{3,1},{4,6},{6,4},{5,7},{7,5},{8,10},{10,8},{9,1... | collective-permute-start | bytes 835592 | tf_op jit(solution)/shard_map/ppermute | solution.py:34
  46.8 0.0 collective-permute-start.13
  46.8 4.3 %all-to-all-done.refs_0_ = f32[4,64,128]{2,1,0:T(8,128)S(1)} async-done(((f32[4,64,128]{2,1,0:T(8,128)}), f32[4,64,128]{2,1,0:T(8,128)S(1)}, u32[]{:S(2)}, u32[]{:S(2)}) %all-to-all-start) | async-done | bytes 131104 | tf_op jit(solution)/shard_map/all_to_all | solution.py:500
  51.1 0.0 collective-permute-done.11.refs_14_
  51.1 0.1 collective-permute-start.12
  51.2 0.5 collective-permute-start.8
  51.7 0.1 collective-permute-start.10
  51.8 0.2 collective-permute-done.7.refs_3_
  51.9 0.3 collective-permute-start.9
  52.2 1.7 %collective-permute-done.10.refs_11_ = f32[2,72,256]{2,1,0:T(8,128)S(1)} collective-permute-done((f32[2,72,256]{2,1,0:T(8,128)S(1)}, f32[2,72,256]{2,1,0:T(8,128)S(1)}, u32[]{:S(2)}, u32[]{:S(2)}) %collective-permute-start.10) | collective-permute-done | bytes 147488 | tf_op jit(solution)/shard_map/ppermute | solution.py:34
  53.9 0.1 collective-permute-start.6
  54.1 0.0 collective-permute-done.8.refs_4_
  54.1 1.2 %collective-permute-done.6.refs_1_ = f32[4,64,128]{2,1,0:T(8,128)S(1)} collective-permute-done((f32[4,64,128]{2,1,0:T(8,128)S(1)}, f32[4,64,128]{2,1,0:T(8,128)S(1)}, u32[]{:S(2)}, u32[]{:S(2)}) %collective-permute-start.6) | collective-permute-done | bytes 131104 | tf_op jit(solution)/shard_map/ppermute | solution.py:34
  55.3 0.0 collective-permute-done.13.refs_17_
  55.3 0.0 collective-permute-done.9.refs_5_
  55.3 0.7 %copy-done.19 = f32[4,136,128]{2,1,0:T(8,128)} copy-done((f32[4,136,128]{2,1,0:T(8,128)}, f32[4,136,128]{2,1,0:T(8,128)S(1)}, u32[]{:S(2)}) %copy-start.19) | copy-done | bytes 278552
  56.1 0.1 copy-done.15
  56.2 0.6 copy-done.16
  56.8 8.3 %shard_map.127 = (f32[2,4096]{1,0:T(2,128)}, f32[2,128,1024]{2,1,0:T(8,128)}) custom-call(s32[16]{0:T(128)} %first.5, s32[16]{0:T(128)} %second.7, s32[16]{0:T(128)} %ranks.3, s32[4,16]{1,0:T(4,128)} %bitcast.1, f32[8]{0:T(128)} %occupied.3, f32[4,64,128]{2,1,0:T(8,128)} %copy-done.17, f32[4,64,128]{2,1,0:T(8,128)} %copy-done.22, f32[4,136,128]{2,1,0:T(8,128)} %copy-done.12, ...), custom_call_target="tpu_custom_call" | custom-call | tf_op jit(solution)/shard_map/pallas_call | solution.py:58
  (38 shorter events, 0.1 us)
Async XLA Ops:
  0.6 15.4 %copy-start.4 = (f32[2,64,256]{2,1,0:T(8,128)S(1)}, f32[2,64,256]{2,1,0:T(8,128)}, u32[]{:S(2)}) copy-start(f32[2,64,256]{2,1,0:T(8,128)} %refs_6_.1) | copy-start | bytes 393220
  0.6 15.4 %copy-start.8 = (s32[16]{0:T(128)S(1)}, s32[16]{0:T(128)}, u32[]{:S(2)}) copy-start(s32[16]{0:T(128)} %second.7) | copy-start | bytes 196
  0.7 15.4 %copy-start.9 = (s32[16]{0:T(128)S(1)}, s32[16]{0:T(128)}, u32[]{:S(2)}) copy-start(s32[16]{0:T(128)} %first.5) | copy-start | bytes 196
  2.6 13.4 %copy-start.2 = (f32[2,72,256]{2,1,0:T(8,128)S(1)}, f32[2,72,256]{2,1,0:T(8,128)}, u32[]{:S(2)}) copy-start(f32[2,72,256]{2,1,0:T(8,128)} %shard_map.122.mp_in.mp_ref.refs_8_) | copy-start | bytes 442372
  2.6 8.5 %collective-permute-start = (f32[2,72,256]{2,1,0:T(8,128)}, f32[2,72,256]{2,1,0:T(8,128)S(1)}, u32[]{:S(2)}, u32[]{:S(2)}) collective-permute-start(f32[2,72,256]{2,1,0:T(8,128)} %shard_map.122.mp_in.mp_ref.refs_8_), channel_id=1, source_target_pairs={{0,4},{4,8},{8,12},{1,5},{5,9},{9,13},{2,6},{6,10},{10,14},{3,7},{... | collective-permute-start | bytes 442376 | tf_op jit(solution)/shard_map/ppermute | solution.py:30
  11.1 1.6 %copy-start = (f32[2,256,1024]{2,1,0:T(8,128)S(1)}, f32[2,256,1024]{2,1,0:T(8,128)}, u32[]{:S(2)}) copy-start(f32[2,256,1024]{2,1,0:T(8,128)} %b_ref.3) | copy-start | bytes 6291460
  12.7 0.7 %copy-start.7 = (s32[16]{0:T(128)S(1)}, s32[16]{0:T(128)}, u32[]{:S(2)}) copy-start(s32[16]{0:T(128)} %second.7) | copy-start | bytes 196
  13.4 38.3 %copy-start.5 = (f32[2,72,256]{2,1,0:T(8,128)}, f32[2,72,256]{2,1,0:T(8,128)S(1)}, u32[]{:S(2)}) copy-start(f32[2,72,256]{2,1,0:T(8,128)S(1)} %collective-permute-done.mp_below.refs_10_) | copy-start | bytes 442372
  13.4 2.7 %copy-start.1 = (f32[2,256,1024]{2,1,0:T(8,128)S(1)}, f32[2,256,1024]{2,1,0:T(8,128)}, u32[]{:S(2)}) copy-start(f32[2,256,1024]{2,1,0:T(8,128)} %b_ref.3) | copy-start | bytes 6291460
  14.7 16.6 %copy-start.10 = (s32[16]{0:T(128)S(1)}, s32[16]{0:T(128)}, u32[]{:S(2)}) copy-start(s32[16]{0:T(128)} %ranks.3) | copy-start | bytes 196
  14.7 16.6 %copy-start.11 = (f32[8]{0:T(128)S(1)}, f32[8]{0:T(128)}, u32[]{:S(2)}) copy-start(f32[8]{0:T(128)} %occupied.3) | copy-start | bytes 100
  14.7 16.6 %collective-permute-start.1 = (f32[2,64,1024]{2,1,0:T(8,128)S(1)}, f32[2,64,1024]{2,1,0:T(8,128)S(1)}, u32[]{:S(2)}, u32[]{:S(2)}) collective-permute-start(f32[2,64,1024]{2,1,0:T(8,128)S(1)} %shard_map.124), channel_id=1, source_target_pairs={{4,0},{8,4},{12,8},{5,1},{9,5},{13,9},{6,2},{10,6},{14,10},{7,3},{... | collective-permute-start | bytes 1572872 | tf_op jit(solution)/shard_map/ppermute | solution.py:30
  18.0 38.1 %copy-start.3 = (f32[2,64,1024]{2,1,0:T(8,128)}, f32[2,64,1024]{2,1,0:T(8,128)S(1)}, u32[]{:S(2)}) copy-start(f32[2,64,1024]{2,1,0:T(8,128)S(1)} %get-tuple-element.31.left_ref.refs_12_) | copy-start | bytes 1572868
  18.0 13.3 %collective-permute-start.3 = (f32[2,64,1024]{2,1,0:T(8,128)S(1)}, f32[2,64,1024]{2,1,0:T(8,128)S(1)}, u32[]{:S(2)}, u32[]{:S(2)}) collective-permute-start(f32[2,64,1024]{2,1,0:T(8,128)S(1)} %get-tuple-element.31.left_ref.refs_12_), channel_id=1, source_target_pairs={{0,1},{1,0},{2,3},{3,2},{4,5},{5,4},{6,7},{7,6},{8,9},{9,8},{10,11... | collective-permute-start | bytes 1572872 | tf_op jit(solution)/shard_map/ppermute | solution.py:34
  18.1 7.3 %collective-permute-start.2 = (f32[2,72,256]{2,1,0:T(8,128)S(1)}, f32[2,72,256]{2,1,0:T(8,128)S(1)}, u32[]{:S(2)}, u32[]{:S(2)}) collective-permute-start(f32[2,72,256]{2,1,0:T(8,128)S(1)} %copy-done.2), channel_id=1, source_target_pairs={{0,1},{1,0},{2,3},{3,2},{4,5},{5,4},{6,7},{7,6},{8,9},{9,8},{10,11... | collective-permute-start | bytes 442376 | tf_op jit(solution)/shard_map/ppermute | solution.py:34
  18.6 6.8 %collective-permute-start.4 = (f32[2,64,256]{2,1,0:T(8,128)S(1)}, f32[2,64,256]{2,1,0:T(8,128)}, u32[]{:S(2)}, u32[]{:S(2)}) collective-permute-start(f32[2,64,256]{2,1,0:T(8,128)S(1)} %copy-done.4), channel_id=1, source_target_pairs={{0,1},{1,0},{2,3},{3,2},{4,5},{5,4},{6,7},{7,6},{8,9},{9,8},{10,11... | collective-permute-start | bytes 393224 | tf_op jit(solution)/shard_map/ppermute | solution.py:34
  18.6 22.5 %all-to-all-start.1 = ((f32[4,136,128]{2,1,0:T(8,128)}), f32[4,136,128]{2,1,0:T(8,128)S(1)}, u32[]{:S(2)}, u32[]{:S(2)}) async-start(f32[4,136,128]{2,1,0:T(8,128)} %shard_map.123), calls=%async_computation.1 | async-start | bytes 557056 | tf_op jit(solution)/shard_map/all_to_all | solution.py:461
  25.4 30.6 %copy-start.20 = (f32[2,72,256]{2,1,0:T(8,128)}, f32[2,72,256]{2,1,0:T(8,128)S(1)}, u32[]{:S(2)}) copy-start(f32[2,72,256]{2,1,0:T(8,128)S(1)} %collective-permute-done.2.refs_9_) | copy-start | bytes 442372
  31.3 24.7 %copy-start.13 = (f32[2,64,1024]{2,1,0:T(8,128)}, f32[2,64,1024]{2,1,0:T(8,128)S(1)}, u32[]{:S(2)}) copy-start(f32[2,64,1024]{2,1,0:T(8,128)S(1)} %collective-permute-done.3.refs_13_) | copy-start | bytes 1572868
  32.3 23.7 %copy-start.6 = (f32[2,64,1024]{2,1,0:T(8,128)}, f32[2,64,1024]{2,1,0:T(8,128)S(1)}, u32[]{:S(2)}) copy-start(f32[2,64,1024]{2,1,0:T(8,128)S(1)} %get-tuple-element.33.refs_16_) | copy-start | bytes 1572868
  32.3 18.8 %collective-permute-start.11 = (f32[2,64,1024]{2,1,0:T(8,128)S(1)}, f32[2,64,1024]{2,1,0:T(8,128)S(1)}, u32[]{:S(2)}, u32[]{:S(2)}) collective-permute-start(f32[2,64,1024]{2,1,0:T(8,128)S(1)} %get-tuple-element.31.left_ref.refs_12_), channel_id=1, source_target_pairs={{0,4},{4,8},{8,12},{1,5},{5,9},{9,13},{2,6},{6,10},{10,14},{3,7},{... | collective-permute-start | bytes 1572872 | tf_op jit(solution)/shard_map/ppermute | solution.py:30
  37.2 4.0 %collective-permute-start.5 = (f32[64,128]{1,0:T(8,128)S(1)}, f32[64,128]{1,0:T(8,128)S(1)}, u32[]{:S(2)}, u32[]{:S(2)}) collective-permute-start(f32[64,128]{1,0:T(8,128)S(1)} %get-tuple-element.26), channel_id=1, source_target_pairs={{0,2},{2,0},{1,3},{3,1},{4,6},{6,4},{5,7},{7,5},{8,10},{10,8},{9,1... | collective-permute-start | bytes 98312 | tf_op jit(solution)/shard_map/ppermute | solution.py:34
  41.2 14.9 %copy-start.12 = (f32[4,136,128]{2,1,0:T(8,128)}, f32[4,136,128]{2,1,0:T(8,128)S(1)}, u32[]{:S(2)}) copy-start(f32[4,136,128]{2,1,0:T(8,128)S(1)} %all-to-all-done.1.refs_2_) | copy-start | bytes 835588
  41.9 9.2 %all-to-all-start = ((f32[4,64,128]{2,1,0:T(8,128)}), f32[4,64,128]{2,1,0:T(8,128)S(1)}, u32[]{:S(2)}, u32[]{:S(2)}) async-start(f32[4,64,128]{2,1,0:T(8,128)} %broadcast_in_dim.2), calls=%async_computation | async-start | bytes 262144 | tf_op jit(solution)/shard_map/all_to_all | solution.py:500
  45.2 6.7 %collective-permute-start.7 = (f32[4,136,128]{2,1,0:T(8,128)S(1)}, f32[4,136,128]{2,1,0:T(8,128)}, u32[]{:S(2)}, u32[]{:S(2)}) collective-permute-start(f32[4,136,128]{2,1,0:T(8,128)S(1)} %all-to-all-done.1.refs_2_), channel_id=1, source_target_pairs={{0,2},{2,0},{1,3},{3,1},{4,6},{6,4},{5,7},{7,5},{8,10},{10,8},{9,1... | collective-permute-start | bytes 835592 | tf_op jit(solution)/shard_map/ppermute | solution.py:34
  46.8 8.5 %collective-permute-start.13 = (f32[2,64,1024]{2,1,0:T(8,128)S(1)}, f32[2,64,1024]{2,1,0:T(8,128)S(1)}, u32[]{:S(2)}, u32[]{:S(2)}) collective-permute-start(f32[2,64,1024]{2,1,0:T(8,128)S(1)} %get-tuple-element.33.refs_16_), channel_id=1, source_target_pairs={{0,1},{1,0},{2,3},{3,2},{4,5},{5,4},{6,7},{7,6},{8,9},{9,8},{10,11... | collective-permute-start | bytes 1572872 | tf_op jit(solution)/shard_map/ppermute | solution.py:34
  51.1 5.0 %copy-start.17 = (f32[4,64,128]{2,1,0:T(8,128)}, f32[4,64,128]{2,1,0:T(8,128)S(1)}, u32[]{:S(2)}) copy-start(f32[4,64,128]{2,1,0:T(8,128)S(1)} %all-to-all-done.refs_0_) | copy-start | bytes 393220
  51.1 5.0 %copy-start.14 = (f32[2,64,1024]{2,1,0:T(8,128)}, f32[2,64,1024]{2,1,0:T(8,128)S(1)}, u32[]{:S(2)}) copy-start(f32[2,64,1024]{2,1,0:T(8,128)S(1)} %collective-permute-done.11.refs_14_) | copy-start | bytes 1572868
  51.1 4.2 %collective-permute-start.12 = (f32[2,64,1024]{2,1,0:T(8,128)S(1)}, f32[2,64,1024]{2,1,0:T(8,128)S(1)}, u32[]{:S(2)}, u32[]{:S(2)}) collective-permute-start(f32[2,64,1024]{2,1,0:T(8,128)S(1)} %collective-permute-done.11.refs_14_), channel_id=1, source_target_pairs={{0,1},{1,0},{2,3},{3,2},{4,5},{5,4},{6,7},{7,6},{8,9},{9,8},{10,11... | collective-permute-start | bytes 1572872 | tf_op jit(solution)/shard_map/ppermute | solution.py:34
  51.2 2.9 %collective-permute-start.8 = (f32[4,136,128]{2,1,0:T(8,128)S(1)}, f32[4,136,128]{2,1,0:T(8,128)S(1)}, u32[]{:S(2)}, u32[]{:S(2)}) collective-permute-start(f32[4,136,128]{2,1,0:T(8,128)S(1)} %all-to-all-done.1.refs_2_), channel_id=1, source_target_pairs={{0,1},{1,0},{2,3},{3,2},{4,5},{5,4},{6,7},{7,6},{8,9},{9,8},{10,11... | collective-permute-start | bytes 835592 | tf_op jit(solution)/shard_map/ppermute | solution.py:34
  51.7 2.2 %collective-permute-start.10 = (f32[2,72,256]{2,1,0:T(8,128)S(1)}, f32[2,72,256]{2,1,0:T(8,128)S(1)}, u32[]{:S(2)}, u32[]{:S(2)}) collective-permute-start(f32[2,72,256]{2,1,0:T(8,128)S(1)} %collective-permute-done.mp_below.refs_10_), channel_id=1, source_target_pairs={{0,1},{1,0},{2,3},{3,2},{4,5},{5,4},{6,7},{7,6},{8,9},{9,8},{10,11... | collective-permute-start | bytes 442376 | tf_op jit(solution)/shard_map/ppermute | solution.py:34
  51.9 3.3 %collective-permute-start.9 = (f32[4,136,128]{2,1,0:T(8,128)}, f32[4,136,128]{2,1,0:T(8,128)S(1)}, u32[]{:S(2)}, u32[]{:S(2)}) collective-permute-start(f32[4,136,128]{2,1,0:T(8,128)} %collective-permute-done.7.refs_3_), channel_id=1, source_target_pairs={{0,1},{1,0},{2,3},{3,2},{4,5},{5,4},{6,7},{7,6},{8,9},{9,8},{10,11... | collective-permute-start | bytes 835592 | tf_op jit(solution)/shard_map/ppermute | solution.py:34
  53.9 2.2 %copy-start.21 = (f32[2,72,256]{2,1,0:T(8,128)}, f32[2,72,256]{2,1,0:T(8,128)S(1)}, u32[]{:S(2)}) copy-start(f32[2,72,256]{2,1,0:T(8,128)S(1)} %collective-permute-done.10.refs_11_) | copy-start | bytes 442372
  53.9 1.3 %collective-permute-start.6 = (f32[4,64,128]{2,1,0:T(8,128)S(1)}, f32[4,64,128]{2,1,0:T(8,128)S(1)}, u32[]{:S(2)}, u32[]{:S(2)}) collective-permute-start(f32[4,64,128]{2,1,0:T(8,128)S(1)} %all-to-all-done.refs_0_), channel_id=1, source_target_pairs={{0,1},{1,0},{2,3},{3,2},{4,5},{5,4},{6,7},{7,6},{8,9},{9,8},{10,11... | collective-permute-start | bytes 393224 | tf_op jit(solution)/shard_map/ppermute | solution.py:34
  54.1 1.2 %copy-start.18 = (f32[4,136,128]{2,1,0:T(8,128)}, f32[4,136,128]{2,1,0:T(8,128)S(1)}, u32[]{:S(2)}) copy-start(f32[4,136,128]{2,1,0:T(8,128)S(1)} %collective-permute-done.8.refs_4_) | copy-start | bytes 835588
  55.3 0.8 %copy-start.22 = (f32[4,64,128]{2,1,0:T(8,128)}, f32[4,64,128]{2,1,0:T(8,128)S(1)}, u32[]{:S(2)}) copy-start(f32[4,64,128]{2,1,0:T(8,128)S(1)} %collective-permute-done.6.refs_1_) | copy-start | bytes 393220
  55.3 0.9 %copy-start.15 = (f32[2,64,1024]{2,1,0:T(8,128)}, f32[2,64,1024]{2,1,0:T(8,128)S(1)}, u32[]{:S(2)}) copy-start(f32[2,64,1024]{2,1,0:T(8,128)S(1)} %collective-permute-done.13.refs_17_) | copy-start | bytes 1572868
  55.3 0.8 %copy-start.19 = (f32[4,136,128]{2,1,0:T(8,128)}, f32[4,136,128]{2,1,0:T(8,128)S(1)}, u32[]{:S(2)}) copy-start(f32[4,136,128]{2,1,0:T(8,128)S(1)} %collective-permute-done.9.refs_5_) | copy-start | bytes 835588
  56.0 0.8 %copy-start.16 = (f32[2,64,1024]{2,1,0:T(8,128)}, f32[2,64,1024]{2,1,0:T(8,128)S(1)}, u32[]{:S(2)}) copy-start(f32[2,64,1024]{2,1,0:T(8,128)S(1)} %collective-permute-done.12.refs_15_) | copy-start | bytes 1572868

commit v14 on v13

--- a/solution.py
+++ b/solution.py
@@ -457,10 +457,6 @@
         ],
         limit=None,
     )
-    if small(z):
-        packs = [lax.all_to_all(pack, "orb", 0, 0)]
-    else:
-        packs = [lax.all_gather(pack, ("orb", "sub"), axis=0, tiled=True)]
     (right_below,) = call(
         functools.partial(below_kernel, z),
         [(pairs, n, fits)],
@@ -469,7 +465,14 @@
         limit=8,
     )
     down = shifted(right_below, "orb", -1)
-    mp_late, coefficients = gate((mp, pno_coefficients), right_below)
+    mp_late, coefficients, pack, mp_below_late = gate(
+        (mp, pno_coefficients, pack, mp_below), right_below
+    )
+    mp_below_other = swapped(mp_below_late, "sub")
+    if small(z):
+        packs = [lax.all_to_all(pack, "orb", 0, 0)]
+    else:
+        packs = [lax.all_gather(pack, ("orb", "sub"), axis=0, tiled=True)]
     left, right_here = call(
         functools.partial(local_kernel, z),
         [(pairs, n, fits), (pairs, n, fits)],
@@ -483,7 +486,7 @@
     c_other = swapped(gate((coefficients,), right_here)[0], "sub")
 
     lists = (pair_first, pair_second, pno_ranks)
-    (down,) = gate((down,), mp_other, left_other, c_other)
+    (down,) = gate((down,), mp_other, left_other, c_other, mp_below_other)
     part, right = call(
         functools.partial(sums_kernel, z),
         [(n, pairs * n), (pairs, n, fits)],
@@ -495,6 +498,7 @@
         packs.append(None)
         packs.append(swapped(gate(packs[:1], part)[0], "sub"))
         sums = part + swapped(part, "fit")
+        (sums,) = gate((sums,), packs[2])
         packs[1] = swapped(gate(packs[:1], part)[0], "fit")
         start_amps = [
             lax.all_to_all(jnp.broadcast_to(sums[None], (z.owners, *sums.shape)), "orb", 0, 0)
@@ -505,12 +509,9 @@
         sums = lax.psum(part, "fit")
         start_amps = [lax.all_gather(sums, ("orb", "sub"), axis=0, tiled=False)]
 
-    right_late, mp_late = gate((right, mp_below), part)
-    left_below = shifted(gate((left,), part)[0], "orb", 1)
-    (left_late,) = gate((left_below,), start_amps[0])
-    right_other, mp_below_other, left_below_other = [
-        swapped(value, "sub") for value in (right_late, mp_late, left_late)
-    ]
+    right_other = swapped(right, "sub")
+    left_below = shifted(gate((left,), right_other)[0], "orb", 1)
+    left_below_other = swapped(gate((left_below,), start_amps[0])[0], "sub")
 
     args = (
         *lists, neighbours.T, occ_energy, *start_amps, *packs,

time: 65.6 us -> 73.4 us (1.12)
  waiting for transfers between devices: 17.4 us -> 28.9 us
  starting transfers between devices: 26.1 us -> 22.5 us
    all_to_all x1, waiting for transfers between devices: 0.01 us -> 5.9 us  [body(): packs = [lax.all_to_all(pack, 'orb', 0, 0)]]
    ppermute x3, waiting for transfers between devices: 7.58 us -> 11.1 us  [shifted(): lax.ppermute(value, axis, [(source, source + steps) for source in range(i...]
    all_to_all x1, starting transfers between devices: 6.76 us -> 4.03 us  [body(): packs = [lax.all_to_all(pack, 'orb', 0, 0)]]
    ppermute x11, waiting for transfers between devices: 5.51 us -> 7.26 us  [swapped(): return lax.ppermute(value, axis, [(0, 1), (1, 0)])]
    ppermute x3, starting transfers between devices: 11.2 us -> 10.3 us  [shifted(): lax.ppermute(value, axis, [(source, source + steps) for source in range(i...]
    unnamed x46 -> x48, local copies, waits for them, and re-layouts: 3.79 us -> 3.76 us
  transfers between devices with their start and end apart: 16 -> 16, of which waited for: 7 -> 9; matrix products, arithmetic and copies ran while one was open for 1% -> 1% of each run, Pallas kernels for 7% -> 5%
where the time goes in v14:
time: 73.4 us; the launch traced here: 72.9 us
  waiting for transfers between devices  28.9 us (39%)
  starting transfers between devices  22.5 us (31%)
  Pallas kernels  16.1 us (22%)
  local copies, waits for them, and re-layouts  4.47 us (6%)
  between operations  0.93 us (1%)
    pallas_call x6, Pallas kernels, call(): pl.pallas_call(kernel, out_shape=[jax.ShapeDtypeStruct(shape, jnp.float32...  16.1 us
    ppermute x3, waiting for transfers between devices, shifted(): lax.ppermute(value, axis, [(source, source + steps) for source in range(i...  11.1 us
    ppermute x3, starting transfers between devices, shifted(): lax.ppermute(value, axis, [(source, source + steps) for source in range(i...  10.3 us
    ppermute x11, waiting for transfers between devices, swapped(): return lax.ppermute(value, axis, [(0, 1), (1, 0)])  7.26 us
    all_to_all x1, waiting for transfers between devices, body(): packs = [lax.all_to_all(pack, 'orb', 0, 0)]  5.9 us
    ppermute x11, starting transfers between devices, swapped(): return lax.ppermute(value, axis, [(0, 1), (1, 0)])  4.71 us
    all_to_all x1, waiting for transfers between devices, body(): lax.all_to_all(jnp.broadcast_to(sums[None], (z.owners, *sums.shape)), 'or...  4.58 us
    all_to_all x1, starting transfers between devices, body(): packs = [lax.all_to_all(pack, 'orb', 0, 0)]  4.03 us
  transfers between devices with their start and end apart: 16, of which 9 were waited for; matrix products, arithmetic and copies ran while one was open for 1% of the time, Pallas kernels for 5%

profile of v14, /device:TPU:0, one launch (start us, length us, event | category | flops | bytes accessed | tf_op | source)
XLA Modules:
  0.0 72.9 jit_solution(3316438048216528373)
XLA Ops:
  0.6 0.0 copy-start.4
  0.6 0.0 copy-start.8
  0.7 0.0 copy-start.9
  0.7 1.9 %shard_map.122.mp_in.mp_ref.refs_8_ = f32[2,72,256]{2,1,0:T(8,128)} custom-call(f32[2,64,256]{2,1,0:T(8,128)} %refs_6_.1, s32[2,256]{1,0:T(2,128)} %map_in.1, f32[2,64]{1,0:T(2,128)} %e_in.1, f32[2,4]{1,0:T(2,128)} %coupling_in.1), custom_call_target="tpu_custom_call" | custom-call | tf_op jit(solution)/shard_map/pallas_call | solution.py:58
  2.6 0.0 copy-start.2
  2.6 5.1 %collective-permute-start = (f32[2,72,256]{2,1,0:T(8,128)}, f32[2,72,256]{2,1,0:T(8,128)S(1)}, u32[]{:S(2)}, u32[]{:S(2)}) collective-permute-start(f32[2,72,256]{2,1,0:T(8,128)} %shard_map.122.mp_in.mp_ref.refs_8_), channel_id=1, source_target_pairs={{0,4},{4,8},{8,12},{1,5},{5,9},{9,13},{2,6},{6,10},{10,14},{3,7},{... | collective-permute-start | bytes 442376 | tf_op jit(solution)/shard_map/ppermute | solution.py:30
  7.7 1.7 %shard_map.123 = f32[4,136,128]{2,1,0:T(8,128)} custom-call(f32[2,4,4096]{2,1,0:T(4,128)} %s_in.1, f32[2,72,256]{2,1,0:T(8,128)} %shard_map.122.mp_in.mp_ref.refs_8_), custom_call_target="tpu_custom_call" | custom-call | tf_op jit(solution)/shard_map/pallas_call | solution.py:58
  9.4 1.7 %collective-permute-done.mp_below.refs_10_ = f32[2,72,256]{2,1,0:T(8,128)S(1)} collective-permute-done((f32[2,72,256]{2,1,0:T(8,128)}, f32[2,72,256]{2,1,0:T(8,128)S(1)}, u32[]{:S(2)}, u32[]{:S(2)}) %collective-permute-start) | collective-permute-done | bytes 147488 | tf_op jit(solution)/shard_map/ppermute | solution.py:30
  11.1 1.6 %copy-done = f32[2,256,1024]{2,1,0:T(8,128)S(1)} copy-done((f32[2,256,1024]{2,1,0:T(8,128)S(1)}, f32[2,256,1024]{2,1,0:T(8,128)}, u32[]{:S(2)}) %copy-start) | copy-done | bytes 2097176
  12.7 0.7 copy-done.7
  13.4 1.3 %shard_map.124 = f32[2,64,1024]{2,1,0:T(8,128)S(1)} custom-call(s32[16]{0:T(128)S(1)} %copy-done.7, f32[2,72,256]{2,1,0:T(8,128)S(1)} %collective-permute-done.mp_below.refs_10_, f32[2,256,1024]{2,1,0:T(8,128)S(1)} %copy-done), custom_call_target="tpu_custom_call" | custom-call | tf_op jit(solution)/shard_map/pallas_call | solution.py:58
  14.7 1.3 %collective-permute-start.1 = (f32[2,64,1024]{2,1,0:T(8,128)S(1)}, f32[2,64,1024]{2,1,0:T(8,128)S(1)}, u32[]{:S(2)}, u32[]{:S(2)}) collective-permute-start(f32[2,64,1024]{2,1,0:T(8,128)S(1)} %shard_map.124), channel_id=1, source_target_pairs={{4,0},{8,4},{12,8},{5,1},{9,5},{13,9},{6,2},{10,6},{14,10},{7,3},{... | collective-permute-start | bytes 1572872 | tf_op jit(solution)/shard_map/ppermute | solution.py:30
  16.0 1.9 %shard_map.125 = (f32[2,64,1024]{2,1,0:T(8,128)S(1)}, f32[2,64,1024]{2,1,0:T(8,128)S(1)}) custom-call(s32[16]{0:T(128)S(1)} %copy-done.9, s32[16]{0:T(128)S(1)} %copy-done.8, f32[2,64,256]{2,1,0:T(8,128)S(1)} %copy-done.4, f32[2,72,256]{2,1,0:T(8,128)S(1)} %copy-done.2, f32[2,256,1024]{2,1,0:T(8,128)S(1)} %copy-done.1), custom_call_target="tpu_custom_call" | custom-call | flops 1 | bytes 1 | tf_op jit(solution)/shard_map/pallas_call | solution.py:58
  17.9 0.1 collective-permute-start.3
  18.0 0.5 collective-permute-start.5
  18.5 0.1 collective-permute-start.2
  18.6 0.4 collective-permute-start.4
  19.0 1.5 %collective-permute-done.4.refs_7_ = f32[2,64,256]{2,1,0:T(8,128)S(1)} collective-permute-done((f32[2,64,256]{2,1,0:T(8,128)S(1)}, f32[2,64,256]{2,1,0:T(8,128)S(1)}, u32[]{:S(2)}, u32[]{:S(2)}) %collective-permute-start.4) | collective-permute-done | bytes 131104 | tf_op jit(solution)/shard_map/ppermute | solution.py:34
  20.5 0.0 collective-permute-done.5.refs_11_
  20.5 0.0 collective-permute-done.2.refs_9_
  20.6 9.4 %collective-permute-done.1.down_ref = f32[2,64,1024]{2,1,0:T(8,128)S(1)} collective-permute-done((f32[2,64,1024]{2,1,0:T(8,128)S(1)}, f32[2,64,1024]{2,1,0:T(8,128)S(1)}, u32[]{:S(2)}, u32[]{:S(2)}) %collective-permute-start.1) | collective-permute-done | bytes 524320 | tf_op jit(solution)/shard_map/ppermute | solution.py:30
  30.0 0.0 collective-permute-done.3.refs_13_
  30.0 1.0 %shard_map.126 = (f32[64,128]{1,0:T(8,128)S(1)}, f32[2,64,1024]{2,1,0:T(8,128)S(1)}) custom-call(s32[16]{0:T(128)S(1)} %copy-done.9, s32[16]{0:T(128)S(1)} %copy-done.8, s32[16]{0:T(128)S(1)} %copy-done.10, f32[8]{0:T(128)S(1)} %copy-done.11, f32[2,72,256]{2,1,0:T(8,128)S(1)} %copy-done.2, f32[2,64,1024]{2,1,0:T(8,128)S(1)} %get-tuple-element.34.left_ref.refs_12_, ...), custom_call_target="tpu_custom_call" | custom-call | tf_op jit(solution)/shard_map/pallas_call | solution.py:58
  31.0 0.1 collective-permute-start.11
  31.1 4.0 %all-to-all-start = ((f32[4,136,128]{2,1,0:T(8,128)}), f32[4,136,128]{2,1,0:T(8,128)S(1)}, u32[]{:S(2)}, u32[]{:S(2)}) async-start(f32[4,136,128]{2,1,0:T(8,128)} %shard_map.123), calls=%async_computation | async-start | bytes 557056 | tf_op jit(solution)/shard_map/all_to_all | solution.py:473
  35.2 0.0 collective-permute-done.11.refs_17_
  35.2 3.9 %collective-permute-start.12 = (f32[2,64,1024]{2,1,0:T(8,128)S(1)}, f32[2,64,1024]{2,1,0:T(8,128)S(1)}, u32[]{:S(2)}, u32[]{:S(2)}) collective-permute-start(f32[2,64,1024]{2,1,0:T(8,128)S(1)} %get-tuple-element.34.left_ref.refs_12_), channel_id=1, source_target_pairs={{0,4},{4,8},{8,12},{1,5},{5,9},{9,13},{2,6},{6,10},{10,14},{3,7},{... | collective-permute-start | bytes 1572872 | tf_op jit(solution)/shard_map/ppermute | solution.py:30
  39.1 5.9 %all-to-all-done.refs_2_ = f32[4,136,128]{2,1,0:T(8,128)S(1)} async-done(((f32[4,136,128]{2,1,0:T(8,128)}), f32[4,136,128]{2,1,0:T(8,128)S(1)}, u32[]{:S(2)}, u32[]{:S(2)}) %all-to-all-start) | async-done | bytes 278560 | tf_op jit(solution)/shard_map/all_to_all | solution.py:473
  45.0 0.0 collective-permute-start.7
  45.0 1.5 %collective-permute-start.6 = (f32[64,128]{1,0:T(8,128)S(1)}, f32[64,128]{1,0:T(8,128)S(1)}, u32[]{:S(2)}, u32[]{:S(2)}) collective-permute-start(f32[64,128]{1,0:T(8,128)S(1)} %get-tuple-element.28), channel_id=1, source_target_pairs={{0,2},{2,0},{1,3},{3,1},{4,6},{6,4},{5,7},{7,5},{8,10},{10,8},{9,1... | collective-permute-start | bytes 98312 | tf_op jit(solution)/shard_map/ppermute | solution.py:34
  46.5 2.4 %collective-permute-done.6 = f32[64,128]{1,0:T(8,128)S(1)} collective-permute-done((f32[64,128]{1,0:T(8,128)S(1)}, f32[64,128]{1,0:T(8,128)S(1)}, u32[]{:S(2)}, u32[]{:S(2)}) %collective-permute-start.6) | collective-permute-done | bytes 32800 | tf_op jit(solution)/shard_map/ppermute | solution.py:34
  48.9 0.0 collective-permute-done.7.refs_4_
  49.0 0.7 broadcast_in_dim.2
  49.7 3.5 %all-to-all-start.1 = ((f32[4,64,128]{2,1,0:T(8,128)}), f32[4,64,128]{2,1,0:T(8,128)S(1)}, u32[]{:S(2)}, u32[]{:S(2)}) async-start(f32[4,64,128]{2,1,0:T(8,128)} %broadcast_in_dim.2), calls=%async_computation.1 | async-start | bytes 262144 | tf_op jit(solution)/shard_map/all_to_all | solution.py:504
  53.1 1.5 %collective-permute-start.9 = (f32[4,136,128]{2,1,0:T(8,128)S(1)}, f32[4,136,128]{2,1,0:T(8,128)}, u32[]{:S(2)}, u32[]{:S(2)}) collective-permute-start(f32[4,136,128]{2,1,0:T(8,128)S(1)} %all-to-all-done.refs_2_), channel_id=1, source_target_pairs={{0,2},{2,0},{1,3},{3,1},{4,6},{6,4},{5,7},{7,5},{8,10},{10,8},{9,1... | collective-permute-start | bytes 835592 | tf_op jit(solution)/shard_map/ppermute | solution.py:34
  54.6 4.6 %all-to-all-done.1.refs_0_ = f32[4,64,128]{2,1,0:T(8,128)S(1)} async-done(((f32[4,64,128]{2,1,0:T(8,128)}), f32[4,64,128]{2,1,0:T(8,128)S(1)}, u32[]{:S(2)}, u32[]{:S(2)}) %all-to-all-start.1) | async-done | bytes 131104 | tf_op jit(solution)/shard_map/all_to_all | solution.py:504
  59.2 0.0 collective-permute-done.12.refs_14_
  59.2 0.1 collective-permute-start.13
  59.3 1.9 %collective-permute-done.9.refs_3_ = f32[4,136,128]{2,1,0:T(8,128)} collective-permute-done((f32[4,136,128]{2,1,0:T(8,128)S(1)}, f32[4,136,128]{2,1,0:T(8,128)}, u32[]{:S(2)}, u32[]{:S(2)}) %collective-permute-start.9) | collective-permute-done | bytes 278560 | tf_op jit(solution)/shard_map/ppermute | solution.py:34
  61.2 0.0 collective-permute-start.10
  61.2 0.5 collective-permute-start.8
  61.7 1.1 %collective-permute-done.8.refs_1_ = f32[4,64,128]{2,1,0:T(8,128)S(1)} collective-permute-done((f32[4,64,128]{2,1,0:T(8,128)S(1)}, f32[4,64,128]{2,1,0:T(8,128)S(1)}, u32[]{:S(2)}, u32[]{:S(2)}) %collective-permute-start.8) | collective-permute-done | bytes 131104 | tf_op jit(solution)/shard_map/ppermute | solution.py:34
  62.8 0.4 collective-permute-done.10.refs_5_
  63.1 0.0 collective-permute-done.13.refs_15_
  63.1 0.3 copy-done.23
  63.4 0.5 copy-done.19
  63.9 0.7 copy-done.16
  64.6 8.3 %shard_map.127 = (f32[2,4096]{1,0:T(2,128)}, f32[2,128,1024]{2,1,0:T(8,128)}) custom-call(s32[16]{0:T(128)} %first.5, s32[16]{0:T(128)} %second.7, s32[16]{0:T(128)} %ranks.3, s32[4,16]{1,0:T(4,128)} %bitcast.1, f32[8]{0:T(128)} %occupied.3, f32[4,64,128]{2,1,0:T(8,128)} %copy-done.17, f32[4,64,128]{2,1,0:T(8,128)} %copy-done.23, f32[4,136,128]{2,1,0:T(8,128)} %copy-done.12, ...), custom_call_target="tpu_custom_call" | custom-call | tf_op jit(solution)/shard_map/pallas_call | solution.py:58
  (40 shorter events, 0.1 us)
Async XLA Ops:
  0.6 15.3 %copy-start.4 = (f32[2,64,256]{2,1,0:T(8,128)S(1)}, f32[2,64,256]{2,1,0:T(8,128)}, u32[]{:S(2)}) copy-start(f32[2,64,256]{2,1,0:T(8,128)} %refs_6_.1) | copy-start | bytes 393220
  0.6 15.3 %copy-start.8 = (s32[16]{0:T(128)S(1)}, s32[16]{0:T(128)}, u32[]{:S(2)}) copy-start(s32[16]{0:T(128)} %second.7) | copy-start | bytes 196
  0.7 15.3 %copy-start.9 = (s32[16]{0:T(128)S(1)}, s32[16]{0:T(128)}, u32[]{:S(2)}) copy-start(s32[16]{0:T(128)} %first.5) | copy-start | bytes 196
  2.6 13.4 %copy-start.2 = (f32[2,72,256]{2,1,0:T(8,128)S(1)}, f32[2,72,256]{2,1,0:T(8,128)}, u32[]{:S(2)}) copy-start(f32[2,72,256]{2,1,0:T(8,128)} %shard_map.122.mp_in.mp_ref.refs_8_) | copy-start | bytes 442372
  2.6 8.5 %collective-permute-start = (f32[2,72,256]{2,1,0:T(8,128)}, f32[2,72,256]{2,1,0:T(8,128)S(1)}, u32[]{:S(2)}, u32[]{:S(2)}) collective-permute-start(f32[2,72,256]{2,1,0:T(8,128)} %shard_map.122.mp_in.mp_ref.refs_8_), channel_id=1, source_target_pairs={{0,4},{4,8},{8,12},{1,5},{5,9},{9,13},{2,6},{6,10},{10,14},{3,7},{... | collective-permute-start | bytes 442376 | tf_op jit(solution)/shard_map/ppermute | solution.py:30
  11.1 1.6 %copy-start = (f32[2,256,1024]{2,1,0:T(8,128)S(1)}, f32[2,256,1024]{2,1,0:T(8,128)}, u32[]{:S(2)}) copy-start(f32[2,256,1024]{2,1,0:T(8,128)} %b_ref.3) | copy-start | bytes 6291460
  12.7 0.7 copy-start.7
  13.3 4.7 %copy-start.5 = (f32[2,72,256]{2,1,0:T(8,128)}, f32[2,72,256]{2,1,0:T(8,128)S(1)}, u32[]{:S(2)}) copy-start(f32[2,72,256]{2,1,0:T(8,128)S(1)} %collective-permute-done.mp_below.refs_10_) | copy-start | bytes 442372
  13.3 2.7 %copy-start.1 = (f32[2,256,1024]{2,1,0:T(8,128)S(1)}, f32[2,256,1024]{2,1,0:T(8,128)}, u32[]{:S(2)}) copy-start(f32[2,256,1024]{2,1,0:T(8,128)} %b_ref.3) | copy-start | bytes 6291460
  13.3 16.6 %copy-start.10 = (s32[16]{0:T(128)S(1)}, s32[16]{0:T(128)}, u32[]{:S(2)}) copy-start(s32[16]{0:T(128)} %ranks.3) | copy-start | bytes 196
  13.4 16.6 %copy-start.11 = (f32[8]{0:T(128)S(1)}, f32[8]{0:T(128)}, u32[]{:S(2)}) copy-start(f32[8]{0:T(128)} %occupied.3) | copy-start | bytes 100
  14.7 15.3 %collective-permute-start.1 = (f32[2,64,1024]{2,1,0:T(8,128)S(1)}, f32[2,64,1024]{2,1,0:T(8,128)S(1)}, u32[]{:S(2)}, u32[]{:S(2)}) collective-permute-start(f32[2,64,1024]{2,1,0:T(8,128)S(1)} %shard_map.124), channel_id=1, source_target_pairs={{4,0},{8,4},{12,8},{5,1},{9,5},{13,9},{6,2},{10,6},{14,10},{7,3},{... | collective-permute-start | bytes 1572872 | tf_op jit(solution)/shard_map/ppermute | solution.py:30
  17.9 45.9 %copy-start.3 = (f32[2,64,1024]{2,1,0:T(8,128)}, f32[2,64,1024]{2,1,0:T(8,128)S(1)}, u32[]{:S(2)}) copy-start(f32[2,64,1024]{2,1,0:T(8,128)S(1)} %get-tuple-element.34.left_ref.refs_12_) | copy-start | bytes 1572868
  17.9 12.0 %collective-permute-start.3 = (f32[2,64,1024]{2,1,0:T(8,128)S(1)}, f32[2,64,1024]{2,1,0:T(8,128)S(1)}, u32[]{:S(2)}, u32[]{:S(2)}) collective-permute-start(f32[2,64,1024]{2,1,0:T(8,128)S(1)} %get-tuple-element.34.left_ref.refs_12_), channel_id=1, source_target_pairs={{0,1},{1,0},{2,3},{3,2},{4,5},{5,4},{6,7},{7,6},{8,9},{9,8},{10,11... | collective-permute-start | bytes 1572872 | tf_op jit(solution)/shard_map/ppermute | solution.py:34
  18.0 2.5 %collective-permute-start.5 = (f32[2,72,256]{2,1,0:T(8,128)S(1)}, f32[2,72,256]{2,1,0:T(8,128)S(1)}, u32[]{:S(2)}, u32[]{:S(2)}) collective-permute-start(f32[2,72,256]{2,1,0:T(8,128)S(1)} %collective-permute-done.mp_below.refs_10_), channel_id=1, source_target_pairs={{0,1},{1,0},{2,3},{3,2},{4,5},{5,4},{6,7},{7,6},{8,9},{9,8},{10,11... | collective-permute-start | bytes 442376 | tf_op jit(solution)/shard_map/ppermute | solution.py:34
  18.5 2.0 %collective-permute-start.2 = (f32[2,72,256]{2,1,0:T(8,128)S(1)}, f32[2,72,256]{2,1,0:T(8,128)S(1)}, u32[]{:S(2)}, u32[]{:S(2)}) collective-permute-start(f32[2,72,256]{2,1,0:T(8,128)S(1)} %copy-done.2), channel_id=1, source_target_pairs={{0,1},{1,0},{2,3},{3,2},{4,5},{5,4},{6,7},{7,6},{8,9},{9,8},{10,11... | collective-permute-start | bytes 442376 | tf_op jit(solution)/shard_map/ppermute | solution.py:34
  18.6 1.9 %collective-permute-start.4 = (f32[2,64,256]{2,1,0:T(8,128)S(1)}, f32[2,64,256]{2,1,0:T(8,128)S(1)}, u32[]{:S(2)}, u32[]{:S(2)}) collective-permute-start(f32[2,64,256]{2,1,0:T(8,128)S(1)} %copy-done.4), channel_id=1, source_target_pairs={{0,1},{1,0},{2,3},{3,2},{4,5},{5,4},{6,7},{7,6},{8,9},{9,8},{10,11... | collective-permute-start | bytes 393224 | tf_op jit(solution)/shard_map/ppermute | solution.py:34
  20.5 10.6 %copy-start.22 = (f32[2,64,256]{2,1,0:T(8,128)}, f32[2,64,256]{2,1,0:T(8,128)S(1)}, u32[]{:S(2)}) copy-start(f32[2,64,256]{2,1,0:T(8,128)S(1)} %collective-permute-done.4.refs_7_) | copy-start | bytes 393220
  20.5 43.3 %copy-start.20 = (f32[2,72,256]{2,1,0:T(8,128)}, f32[2,72,256]{2,1,0:T(8,128)S(1)}, u32[]{:S(2)}) copy-start(f32[2,72,256]{2,1,0:T(8,128)S(1)} %collective-permute-done.5.refs_11_) | copy-start | bytes 442372
  20.5 10.5 %copy-start.21 = (f32[2,72,256]{2,1,0:T(8,128)}, f32[2,72,256]{2,1,0:T(8,128)S(1)}, u32[]{:S(2)}) copy-start(f32[2,72,256]{2,1,0:T(8,128)S(1)} %collective-permute-done.2.refs_9_) | copy-start | bytes 442372
  30.0 33.9 %copy-start.13 = (f32[2,64,1024]{2,1,0:T(8,128)}, f32[2,64,1024]{2,1,0:T(8,128)S(1)}, u32[]{:S(2)}) copy-start(f32[2,64,1024]{2,1,0:T(8,128)S(1)} %collective-permute-done.3.refs_13_) | copy-start | bytes 1572868
  31.0 32.8 %copy-start.6 = (f32[2,64,1024]{2,1,0:T(8,128)}, f32[2,64,1024]{2,1,0:T(8,128)S(1)}, u32[]{:S(2)}) copy-start(f32[2,64,1024]{2,1,0:T(8,128)S(1)} %get-tuple-element.33.refs_16_) | copy-start | bytes 1572868
  31.0 4.1 %collective-permute-start.11 = (f32[2,64,1024]{2,1,0:T(8,128)S(1)}, f32[2,64,1024]{2,1,0:T(8,128)S(1)}, u32[]{:S(2)}, u32[]{:S(2)}) collective-permute-start(f32[2,64,1024]{2,1,0:T(8,128)S(1)} %get-tuple-element.33.refs_16_), channel_id=1, source_target_pairs={{0,1},{1,0},{2,3},{3,2},{4,5},{5,4},{6,7},{7,6},{8,9},{9,8},{10,11... | collective-permute-start | bytes 1572872 | tf_op jit(solution)/shard_map/ppermute | solution.py:34
  31.1 13.9 %all-to-all-start = ((f32[4,136,128]{2,1,0:T(8,128)}), f32[4,136,128]{2,1,0:T(8,128)S(1)}, u32[]{:S(2)}, u32[]{:S(2)}) async-start(f32[4,136,128]{2,1,0:T(8,128)} %shard_map.123), calls=%async_computation | async-start | bytes 557056 | tf_op jit(solution)/shard_map/all_to_all | solution.py:473
  35.2 28.7 %copy-start.14 = (f32[2,64,1024]{2,1,0:T(8,128)}, f32[2,64,1024]{2,1,0:T(8,128)S(1)}, u32[]{:S(2)}) copy-start(f32[2,64,1024]{2,1,0:T(8,128)S(1)} %collective-permute-done.11.refs_17_) | copy-start | bytes 1572868
  35.2 24.1 %collective-permute-start.12 = (f32[2,64,1024]{2,1,0:T(8,128)S(1)}, f32[2,64,1024]{2,1,0:T(8,128)S(1)}, u32[]{:S(2)}, u32[]{:S(2)}) collective-permute-start(f32[2,64,1024]{2,1,0:T(8,128)S(1)} %get-tuple-element.34.left_ref.refs_12_), channel_id=1, source_target_pairs={{0,4},{4,8},{8,12},{1,5},{5,9},{9,13},{2,6},{6,10},{10,14},{3,7},{... | collective-permute-start | bytes 1572872 | tf_op jit(solution)/shard_map/ppermute | solution.py:30
  45.0 18.9 %copy-start.12 = (f32[4,136,128]{2,1,0:T(8,128)}, f32[4,136,128]{2,1,0:T(8,128)S(1)}, u32[]{:S(2)}) copy-start(f32[4,136,128]{2,1,0:T(8,128)S(1)} %all-to-all-done.refs_2_) | copy-start | bytes 835588
  45.0 3.9 %collective-permute-start.7 = (f32[4,136,128]{2,1,0:T(8,128)S(1)}, f32[4,136,128]{2,1,0:T(8,128)S(1)}, u32[]{:S(2)}, u32[]{:S(2)}) collective-permute-start(f32[4,136,128]{2,1,0:T(8,128)S(1)} %all-to-all-done.refs_2_), channel_id=1, source_target_pairs={{0,1},{1,0},{2,3},{3,2},{4,5},{5,4},{6,7},{7,6},{8,9},{9,8},{10,11... | collective-permute-start | bytes 835592 | tf_op jit(solution)/shard_map/ppermute | solution.py:34
  45.0 3.9 %collective-permute-start.6 = (f32[64,128]{1,0:T(8,128)S(1)}, f32[64,128]{1,0:T(8,128)S(1)}, u32[]{:S(2)}, u32[]{:S(2)}) collective-permute-start(f32[64,128]{1,0:T(8,128)S(1)} %get-tuple-element.28), channel_id=1, source_target_pairs={{0,2},{2,0},{1,3},{3,1},{4,6},{6,4},{5,7},{7,5},{8,10},{10,8},{9,1... | collective-permute-start | bytes 98312 | tf_op jit(solution)/shard_map/ppermute | solution.py:34
  49.0 14.9 %copy-start.18 = (f32[4,136,128]{2,1,0:T(8,128)}, f32[4,136,128]{2,1,0:T(8,128)S(1)}, u32[]{:S(2)}) copy-start(f32[4,136,128]{2,1,0:T(8,128)S(1)} %collective-permute-done.7.refs_4_) | copy-start | bytes 835588
  49.7 9.5 %all-to-all-start.1 = ((f32[4,64,128]{2,1,0:T(8,128)}), f32[4,64,128]{2,1,0:T(8,128)S(1)}, u32[]{:S(2)}, u32[]{:S(2)}) async-start(f32[4,64,128]{2,1,0:T(8,128)} %broadcast_in_dim.2), calls=%async_computation.1 | async-start | bytes 262144 | tf_op jit(solution)/shard_map/all_to_all | solution.py:504
  53.1 8.0 %collective-permute-start.9 = (f32[4,136,128]{2,1,0:T(8,128)S(1)}, f32[4,136,128]{2,1,0:T(8,128)}, u32[]{:S(2)}, u32[]{:S(2)}) collective-permute-start(f32[4,136,128]{2,1,0:T(8,128)S(1)} %all-to-all-done.refs_2_), channel_id=1, source_target_pairs={{0,2},{2,0},{1,3},{3,1},{4,6},{6,4},{5,7},{7,5},{8,10},{10,8},{9,1... | collective-permute-start | bytes 835592 | tf_op jit(solution)/shard_map/ppermute | solution.py:34
  59.2 4.7 %copy-start.17 = (f32[4,64,128]{2,1,0:T(8,128)}, f32[4,64,128]{2,1,0:T(8,128)S(1)}, u32[]{:S(2)}) copy-start(f32[4,64,128]{2,1,0:T(8,128)S(1)} %all-to-all-done.1.refs_0_) | copy-start | bytes 393220
  59.2 4.7 %copy-start.15 = (f32[2,64,1024]{2,1,0:T(8,128)}, f32[2,64,1024]{2,1,0:T(8,128)S(1)}, u32[]{:S(2)}) copy-start(f32[2,64,1024]{2,1,0:T(8,128)S(1)} %collective-permute-done.12.refs_14_) | copy-start | bytes 1572868
  59.2 3.9 %collective-permute-start.13 = (f32[2,64,1024]{2,1,0:T(8,128)S(1)}, f32[2,64,1024]{2,1,0:T(8,128)S(1)}, u32[]{:S(2)}, u32[]{:S(2)}) collective-permute-start(f32[2,64,1024]{2,1,0:T(8,128)S(1)} %collective-permute-done.12.refs_14_), channel_id=1, source_target_pairs={{0,1},{1,0},{2,3},{3,2},{4,5},{5,4},{6,7},{7,6},{8,9},{9,8},{10,11... | collective-permute-start | bytes 1572872 | tf_op jit(solution)/shard_map/ppermute | solution.py:34
  61.2 2.0 %collective-permute-start.10 = (f32[4,136,128]{2,1,0:T(8,128)}, f32[4,136,128]{2,1,0:T(8,128)S(1)}, u32[]{:S(2)}, u32[]{:S(2)}) collective-permute-start(f32[4,136,128]{2,1,0:T(8,128)} %collective-permute-done.9.refs_3_), channel_id=1, source_target_pairs={{0,1},{1,0},{2,3},{3,2},{4,5},{5,4},{6,7},{7,6},{8,9},{9,8},{10,11... | collective-permute-start | bytes 835592 | tf_op jit(solution)/shard_map/ppermute | solution.py:34
  61.2 1.6 %collective-permute-start.8 = (f32[4,64,128]{2,1,0:T(8,128)S(1)}, f32[4,64,128]{2,1,0:T(8,128)S(1)}, u32[]{:S(2)}, u32[]{:S(2)}) collective-permute-start(f32[4,64,128]{2,1,0:T(8,128)S(1)} %all-to-all-done.1.refs_0_), channel_id=1, source_target_pairs={{0,1},{1,0},{2,3},{3,2},{4,5},{5,4},{6,7},{7,6},{8,9},{9,8},{10,11... | collective-permute-start | bytes 393224 | tf_op jit(solution)/shard_map/ppermute | solution.py:34
  62.7 0.6 copy-start.23
  63.1 0.7 copy-start.19
  63.9 0.8 %copy-start.16 = (f32[2,64,1024]{2,1,0:T(8,128)}, f32[2,64,1024]{2,1,0:T(8,128)S(1)}, u32[]{:S(2)}) copy-start(f32[2,64,1024]{2,1,0:T(8,128)S(1)} %collective-permute-done.13.refs_15_) | copy-start | bytes 1572868

commit v15 on v13

--- a/solution.py
+++ b/solution.py
@@ -469,7 +469,8 @@
         limit=8,
     )
     down = shifted(right_below, "orb", -1)
-    mp_late, coefficients = gate((mp, pno_coefficients), right_below)
+    mp_late, coefficients, mp_below_late = gate((mp, pno_coefficients, mp_below), right_below)
+    mp_below_other = swapped(mp_below_late, "sub")
     left, right_here = call(
         functools.partial(local_kernel, z),
         [(pairs, n, fits), (pairs, n, fits)],
@@ -478,12 +479,13 @@
         limit=8,
         cost=BRIEF,
     )
+    left_below = shifted(left, "orb", 1)
     mp_other = swapped(gate((mp,), right_here)[0], "sub")
     left_other = swapped(left, "sub")
     c_other = swapped(gate((coefficients,), right_here)[0], "sub")
 
     lists = (pair_first, pair_second, pno_ranks)
-    (down,) = gate((down,), mp_other, left_other, c_other)
+    (down,) = gate((down,), mp_other, left_other, c_other, mp_below_other)
     part, right = call(
         functools.partial(sums_kernel, z),
         [(n, pairs * n), (pairs, n, fits)],
@@ -505,12 +507,8 @@
         sums = lax.psum(part, "fit")
         start_amps = [lax.all_gather(sums, ("orb", "sub"), axis=0, tiled=False)]
 
-    right_late, mp_late = gate((right, mp_below), part)
-    left_below = shifted(gate((left,), part)[0], "orb", 1)
-    (left_late,) = gate((left_below,), start_amps[0])
-    right_other, mp_below_other, left_below_other = [
-        swapped(value, "sub") for value in (right_late, mp_late, left_late)
-    ]
+    right_other = swapped(right, "sub")
+    left_below_other = swapped(gate((left_below,), sums)[0], "sub")
 
     args = (
         *lists, neighbours.T, occ_energy, *start_amps, *packs,

time: 65.6 us -> 67.4 us (1.027)
  starting transfers between devices: 26.1 us -> 28 us
    all_to_all x1, waiting for transfers between devices: 0.01 us -> 5.99 us  [body(): packs = [lax.all_to_all(pack, 'orb', 0, 0)]]
    ppermute x3, waiting for transfers between devices: 7.58 us -> 1.7 us  [shifted(): lax.ppermute(value, axis, [(source, source + steps) for source in range(i...]
    all_to_all x1, starting transfers between devices: 3.33 us -> 7.44 us  [body(): lax.all_to_all(jnp.broadcast_to(sums[None], (z.owners, *sums.shape)), 'or...]
    all_to_all x1, starting transfers between devices: 6.76 us -> 3.56 us  [body(): packs = [lax.all_to_all(pack, 'orb', 0, 0)]]
    ppermute x11, waiting for transfers between devices: 5.51 us -> 3.41 us  [swapped(): return lax.ppermute(value, axis, [(0, 1), (1, 0)])]
    all_to_all x1, waiting for transfers between devices: 4.31 us -> 6.08 us  [body(): lax.all_to_all(jnp.broadcast_to(sums[None], (z.owners, *sums.shape)), 'or...]
    ppermute x3, starting transfers between devices: 11.2 us -> 12.1 us  [shifted(): lax.ppermute(value, axis, [(source, source + steps) for source in range(i...]
    unnamed x46 -> x44, local copies, waits for them, and re-layouts: 3.79 us -> 3.97 us
  transfers between devices with their start and end apart: 16 -> 16, of which waited for: 7 -> 6; matrix products, arithmetic and copies ran while one was open for 1% -> 1% of each run, Pallas kernels for 7% -> 7%
where the time goes in v15:
time: 67.4 us; the launch traced here: 66.9 us
  starting transfers between devices  28 us (42%)
  waiting for transfers between devices  17.2 us (26%)
  Pallas kernels  16.2 us (24%)
  local copies, waits for them, and re-layouts  4.64 us (7%)
  between operations  0.92 us (1%)
    pallas_call x6, Pallas kernels, call(): pl.pallas_call(kernel, out_shape=[jax.ShapeDtypeStruct(shape, jnp.float32...  16.2 us
    ppermute x3, starting transfers between devices, shifted(): lax.ppermute(value, axis, [(source, source + steps) for source in range(i...  12.1 us
    all_to_all x1, starting transfers between devices, body(): lax.all_to_all(jnp.broadcast_to(sums[None], (z.owners, *sums.shape)), 'or...  7.44 us
    all_to_all x1, waiting for transfers between devices, body(): lax.all_to_all(jnp.broadcast_to(sums[None], (z.owners, *sums.shape)), 'or...  6.08 us
    all_to_all x1, waiting for transfers between devices, body(): packs = [lax.all_to_all(pack, 'orb', 0, 0)]  5.99 us
    ppermute x11, starting transfers between devices, swapped(): return lax.ppermute(value, axis, [(0, 1), (1, 0)])  4.94 us
    unnamed x44, local copies, waits for them, and re-layouts  3.97 us
    all_to_all x1, starting transfers between devices, body(): packs = [lax.all_to_all(pack, 'orb', 0, 0)]  3.56 us
  transfers between devices with their start and end apart: 16, of which 6 were waited for; matrix products, arithmetic and copies ran while one was open for 1% of the time, Pallas kernels for 7%

profile of v15, /device:TPU:0, one launch (start us, length us, event | category | flops | bytes accessed | tf_op | source)
XLA Modules:
  0.0 66.9 jit_solution(12438574069315283773)
XLA Ops:
  0.6 0.0 copy-start.4
  0.6 0.0 copy-start.8
  0.7 0.0 copy-start.9
  0.7 2.0 %shard_map.122.mp_in.mp_ref.refs_8_ = f32[2,72,256]{2,1,0:T(8,128)} custom-call(f32[2,64,256]{2,1,0:T(8,128)} %refs_6_.1, s32[2,256]{1,0:T(2,128)} %map_in.1, f32[2,64]{1,0:T(2,128)} %e_in.1, f32[2,4]{1,0:T(2,128)} %coupling_in.1), custom_call_target="tpu_custom_call" | custom-call | tf_op jit(solution)/shard_map/pallas_call | solution.py:58
  2.6 5.1 %collective-permute-start = (f32[2,72,256]{2,1,0:T(8,128)}, f32[2,72,256]{2,1,0:T(8,128)S(1)}, u32[]{:S(2)}, u32[]{:S(2)}) collective-permute-start(f32[2,72,256]{2,1,0:T(8,128)} %shard_map.122.mp_in.mp_ref.refs_8_), channel_id=1, source_target_pairs={{0,4},{4,8},{8,12},{1,5},{5,9},{9,13},{2,6},{6,10},{10,14},{3,7},{... | collective-permute-start | bytes 442376 | tf_op jit(solution)/shard_map/ppermute | solution.py:30
  7.7 1.7 %shard_map.123 = f32[4,136,128]{2,1,0:T(8,128)} custom-call(f32[2,4,4096]{2,1,0:T(4,128)} %s_in.1, f32[2,72,256]{2,1,0:T(8,128)} %shard_map.122.mp_in.mp_ref.refs_8_), custom_call_target="tpu_custom_call" | custom-call | tf_op jit(solution)/shard_map/pallas_call | solution.py:58
  9.4 1.7 %collective-permute-done.mp_below.refs_10_ = f32[2,72,256]{2,1,0:T(8,128)S(1)} collective-permute-done((f32[2,72,256]{2,1,0:T(8,128)}, f32[2,72,256]{2,1,0:T(8,128)S(1)}, u32[]{:S(2)}, u32[]{:S(2)}) %collective-permute-start) | collective-permute-done | bytes 147488 | tf_op jit(solution)/shard_map/ppermute | solution.py:30
  11.1 1.6 %copy-done = f32[2,256,1024]{2,1,0:T(8,128)S(1)} copy-done((f32[2,256,1024]{2,1,0:T(8,128)S(1)}, f32[2,256,1024]{2,1,0:T(8,128)}, u32[]{:S(2)}) %copy-start) | copy-done | bytes 2097176
  12.7 0.7 copy-done.7
  13.4 1.3 %shard_map.124 = f32[2,64,1024]{2,1,0:T(8,128)S(1)} custom-call(s32[16]{0:T(128)S(1)} %copy-done.7, f32[2,72,256]{2,1,0:T(8,128)S(1)} %collective-permute-done.mp_below.refs_10_, f32[2,256,1024]{2,1,0:T(8,128)S(1)} %copy-done), custom_call_target="tpu_custom_call" | custom-call | tf_op jit(solution)/shard_map/pallas_call | solution.py:58
  14.7 0.0 copy-start.10
  14.7 0.0 copy-start.11
  14.7 1.3 %collective-permute-start.1 = (f32[2,64,1024]{2,1,0:T(8,128)S(1)}, f32[2,64,1024]{2,1,0:T(8,128)S(1)}, u32[]{:S(2)}, u32[]{:S(2)}) collective-permute-start(f32[2,64,1024]{2,1,0:T(8,128)S(1)} %shard_map.124), channel_id=1, source_target_pairs={{4,0},{8,4},{12,8},{5,1},{9,5},{13,9},{6,2},{10,6},{14,10},{7,3},{... | collective-permute-start | bytes 1572872 | tf_op jit(solution)/shard_map/ppermute | solution.py:30
  16.0 1.9 %shard_map.125 = (f32[2,64,1024]{2,1,0:T(8,128)S(1)}, f32[2,64,1024]{2,1,0:T(8,128)S(1)}) custom-call(s32[16]{0:T(128)S(1)} %copy-done.9, s32[16]{0:T(128)S(1)} %copy-done.8, f32[2,64,256]{2,1,0:T(8,128)S(1)} %copy-done.4, f32[2,72,256]{2,1,0:T(8,128)S(1)} %copy-done.2, f32[2,256,1024]{2,1,0:T(8,128)S(1)} %copy-done.1), custom_call_target="tpu_custom_call" | custom-call | flops 1 | bytes 1 | tf_op jit(solution)/shard_map/pallas_call | solution.py:58
  18.0 0.1 collective-permute-start.3
  18.1 5.7 %collective-permute-start.11 = (f32[2,64,1024]{2,1,0:T(8,128)S(1)}, f32[2,64,1024]{2,1,0:T(8,128)}, u32[]{:S(2)}, u32[]{:S(2)}) collective-permute-start(f32[2,64,1024]{2,1,0:T(8,128)S(1)} %get-tuple-element.19.left_ref.refs_12_), channel_id=1, source_target_pairs={{0,4},{4,8},{8,12},{1,5},{5,9},{9,13},{2,6},{6,10},{10,14},{3,7},{... | collective-permute-start | bytes 1572872 | tf_op jit(solution)/shard_map/ppermute | solution.py:30
  23.8 3.6 %all-to-all-start.1 = ((f32[4,136,128]{2,1,0:T(8,128)}), f32[4,136,128]{2,1,0:T(8,128)S(1)}, u32[]{:S(2)}, u32[]{:S(2)}) async-start(f32[4,136,128]{2,1,0:T(8,128)} %shard_map.123), calls=%async_computation.1 | async-start | bytes 557056 | tf_op jit(solution)/shard_map/all_to_all | solution.py:461
  27.3 0.2 collective-permute-start.4
  27.5 0.3 collective-permute-start.5
  27.8 1.0 %collective-permute-done.4.refs_7_ = f32[2,64,256]{2,1,0:T(8,128)} collective-permute-done((f32[2,64,256]{2,1,0:T(8,128)S(1)}, f32[2,64,256]{2,1,0:T(8,128)}, u32[]{:S(2)}, u32[]{:S(2)}) %collective-permute-start.4) | collective-permute-done | bytes 131104 | tf_op jit(solution)/shard_map/ppermute | solution.py:34
  28.8 0.2 collective-permute-start.2
  29.0 0.0 collective-permute-done.5.refs_11_
  29.0 1.2 %collective-permute-done.2.refs_9_ = f32[2,72,256]{2,1,0:T(8,128)S(1)} collective-permute-done((f32[2,72,256]{2,1,0:T(8,128)S(1)}, f32[2,72,256]{2,1,0:T(8,128)S(1)}, u32[]{:S(2)}, u32[]{:S(2)}) %collective-permute-start.2) | collective-permute-done | bytes 147488 | tf_op jit(solution)/shard_map/ppermute | solution.py:34
  30.2 0.0 collective-permute-done.1.down_ref
  30.2 0.7 copy-done.20
  30.8 0.0 collective-permute-done.3.refs_13_
  30.8 1.0 %shard_map.126 = (f32[64,128]{1,0:T(8,128)S(1)}, f32[2,64,1024]{2,1,0:T(8,128)S(1)}) custom-call(s32[16]{0:T(128)S(1)} %copy-done.9, s32[16]{0:T(128)S(1)} %copy-done.8, s32[16]{0:T(128)S(1)} %copy-done.10, f32[8]{0:T(128)S(1)} %copy-done.11, f32[2,72,256]{2,1,0:T(8,128)S(1)} %copy-done.2, f32[2,64,1024]{2,1,0:T(8,128)S(1)} %get-tuple-element.19.left_ref.refs_12_, ...), custom_call_target="tpu_custom_call" | custom-call | tf_op jit(solution)/shard_map/pallas_call | solution.py:58
  31.9 1.6 %collective-permute-start.6 = (f32[64,128]{1,0:T(8,128)S(1)}, f32[64,128]{1,0:T(8,128)S(1)}, u32[]{:S(2)}, u32[]{:S(2)}) collective-permute-start(f32[64,128]{1,0:T(8,128)S(1)} %get-tuple-element.25), channel_id=1, source_target_pairs={{0,2},{2,0},{1,3},{3,1},{4,6},{6,4},{5,7},{7,5},{8,10},{10,8},{9,1... | collective-permute-start | bytes 98312 | tf_op jit(solution)/shard_map/ppermute | solution.py:34
  33.4 6.0 %all-to-all-done.1.refs_2_ = f32[4,136,128]{2,1,0:T(8,128)S(1)} async-done(((f32[4,136,128]{2,1,0:T(8,128)}), f32[4,136,128]{2,1,0:T(8,128)S(1)}, u32[]{:S(2)}, u32[]{:S(2)}) %all-to-all-start.1) | async-done | bytes 278560 | tf_op jit(solution)/shard_map/all_to_all | solution.py:461
  39.4 1.5 %collective-permute-start.8 = (f32[4,136,128]{2,1,0:T(8,128)S(1)}, f32[4,136,128]{2,1,0:T(8,128)S(1)}, u32[]{:S(2)}, u32[]{:S(2)}) collective-permute-start(f32[4,136,128]{2,1,0:T(8,128)S(1)} %all-to-all-done.1.refs_2_), channel_id=1, source_target_pairs={{0,2},{2,0},{1,3},{3,1},{4,6},{6,4},{5,7},{7,5},{8,10},{10,8},{9,1... | collective-permute-start | bytes 835592 | tf_op jit(solution)/shard_map/ppermute | solution.py:34
  40.9 0.0 collective-permute-start.13
  40.9 0.0 collective-permute-done.6
  40.9 0.0 collective-permute-done.11.refs_14_
  40.9 0.6 collective-permute-start.12
  41.5 0.7 broadcast_in_dim.2
  42.2 7.4 %all-to-all-start = ((f32[4,64,128]{2,1,0:T(8,128)}), f32[4,64,128]{2,1,0:T(8,128)S(1)}, u32[]{:S(2)}, u32[]{:S(2)}) async-start(f32[4,64,128]{2,1,0:T(8,128)} %broadcast_in_dim.2), calls=%async_computation | async-start | bytes 262144 | tf_op jit(solution)/shard_map/all_to_all | solution.py:502
  49.6 0.0 collective-permute-start.9
  49.6 6.1 %all-to-all-done.refs_0_ = f32[4,64,128]{2,1,0:T(8,128)S(1)} async-done(((f32[4,64,128]{2,1,0:T(8,128)}), f32[4,64,128]{2,1,0:T(8,128)S(1)}, u32[]{:S(2)}, u32[]{:S(2)}) %all-to-all-start) | async-done | bytes 131104 | tf_op jit(solution)/shard_map/all_to_all | solution.py:502
  55.7 0.0 collective-permute-done.8.refs_3_
  55.7 0.1 collective-permute-start.10
  55.8 0.5 collective-permute-start.7
  56.3 1.2 %collective-permute-done.7.refs_1_ = f32[4,64,128]{2,1,0:T(8,128)S(1)} collective-permute-done((f32[4,64,128]{2,1,0:T(8,128)S(1)}, f32[4,64,128]{2,1,0:T(8,128)S(1)}, u32[]{:S(2)}, u32[]{:S(2)}) %collective-permute-start.7) | collective-permute-done | bytes 131104 | tf_op jit(solution)/shard_map/ppermute | solution.py:34
  57.5 0.0 collective-permute-done.12.refs_15_
  57.6 0.5 copy-done.21
  58.2 0.2 copy-done.13
  58.4 0.2 copy-done.14
  58.5 0.1 copy-done.18
  58.6 8.3 %shard_map.127 = (f32[2,4096]{1,0:T(2,128)}, f32[2,128,1024]{2,1,0:T(8,128)}) custom-call(s32[16]{0:T(128)} %first.5, s32[16]{0:T(128)} %second.7, s32[16]{0:T(128)} %ranks.3, s32[4,16]{1,0:T(4,128)} %bitcast.1, f32[8]{0:T(128)} %occupied.3, f32[4,64,128]{2,1,0:T(8,128)} %copy-done.15, f32[4,64,128]{2,1,0:T(8,128)} %copy-done.21, f32[4,136,128]{2,1,0:T(8,128)} %copy-done.12, ...), custom_call_target="tpu_custom_call" | custom-call | tf_op jit(solution)/shard_map/pallas_call | solution.py:58
  (36 shorter events, 0.1 us)
Async XLA Ops:
  0.6 15.4 %copy-start.4 = (f32[2,64,256]{2,1,0:T(8,128)S(1)}, f32[2,64,256]{2,1,0:T(8,128)}, u32[]{:S(2)}) copy-start(f32[2,64,256]{2,1,0:T(8,128)} %refs_6_.1) | copy-start | bytes 393220
  0.6 15.4 %copy-start.8 = (s32[16]{0:T(128)S(1)}, s32[16]{0:T(128)}, u32[]{:S(2)}) copy-start(s32[16]{0:T(128)} %second.7) | copy-start | bytes 196
  0.7 15.4 %copy-start.9 = (s32[16]{0:T(128)S(1)}, s32[16]{0:T(128)}, u32[]{:S(2)}) copy-start(s32[16]{0:T(128)} %first.5) | copy-start | bytes 196
  2.6 13.4 %copy-start.2 = (f32[2,72,256]{2,1,0:T(8,128)S(1)}, f32[2,72,256]{2,1,0:T(8,128)}, u32[]{:S(2)}) copy-start(f32[2,72,256]{2,1,0:T(8,128)} %shard_map.122.mp_in.mp_ref.refs_8_) | copy-start | bytes 442372
  2.6 8.5 %collective-permute-start = (f32[2,72,256]{2,1,0:T(8,128)}, f32[2,72,256]{2,1,0:T(8,128)S(1)}, u32[]{:S(2)}, u32[]{:S(2)}) collective-permute-start(f32[2,72,256]{2,1,0:T(8,128)} %shard_map.122.mp_in.mp_ref.refs_8_), channel_id=1, source_target_pairs={{0,4},{4,8},{8,12},{1,5},{5,9},{9,13},{2,6},{6,10},{10,14},{3,7},{... | collective-permute-start | bytes 442376 | tf_op jit(solution)/shard_map/ppermute | solution.py:30
  11.1 1.6 %copy-start = (f32[2,256,1024]{2,1,0:T(8,128)S(1)}, f32[2,256,1024]{2,1,0:T(8,128)}, u32[]{:S(2)}) copy-start(f32[2,256,1024]{2,1,0:T(8,128)} %b_ref.3) | copy-start | bytes 6291460
  12.7 0.7 copy-start.7
  13.4 14.1 %copy-start.5 = (f32[2,72,256]{2,1,0:T(8,128)}, f32[2,72,256]{2,1,0:T(8,128)S(1)}, u32[]{:S(2)}) copy-start(f32[2,72,256]{2,1,0:T(8,128)S(1)} %collective-permute-done.mp_below.refs_10_) | copy-start | bytes 442372
  13.4 2.7 %copy-start.1 = (f32[2,256,1024]{2,1,0:T(8,128)S(1)}, f32[2,256,1024]{2,1,0:T(8,128)}, u32[]{:S(2)}) copy-start(f32[2,256,1024]{2,1,0:T(8,128)} %b_ref.3) | copy-start | bytes 6291460
  14.7 16.2 %copy-start.10 = (s32[16]{0:T(128)S(1)}, s32[16]{0:T(128)}, u32[]{:S(2)}) copy-start(s32[16]{0:T(128)} %ranks.3) | copy-start | bytes 196
  14.7 16.2 %copy-start.11 = (f32[8]{0:T(128)S(1)}, f32[8]{0:T(128)}, u32[]{:S(2)}) copy-start(f32[8]{0:T(128)} %occupied.3) | copy-start | bytes 100
  14.7 15.5 %collective-permute-start.1 = (f32[2,64,1024]{2,1,0:T(8,128)S(1)}, f32[2,64,1024]{2,1,0:T(8,128)S(1)}, u32[]{:S(2)}, u32[]{:S(2)}) collective-permute-start(f32[2,64,1024]{2,1,0:T(8,128)S(1)} %shard_map.124), channel_id=1, source_target_pairs={{4,0},{8,4},{12,8},{5,1},{9,5},{13,9},{6,2},{10,6},{14,10},{7,3},{... | collective-permute-start | bytes 1572872 | tf_op jit(solution)/shard_map/ppermute | solution.py:30
  18.0 39.6 %copy-start.3 = (f32[2,64,1024]{2,1,0:T(8,128)}, f32[2,64,1024]{2,1,0:T(8,128)S(1)}, u32[]{:S(2)}) copy-start(f32[2,64,1024]{2,1,0:T(8,128)S(1)} %get-tuple-element.19.left_ref.refs_12_) | copy-start | bytes 1572868
  18.0 12.9 %collective-permute-start.3 = (f32[2,64,1024]{2,1,0:T(8,128)S(1)}, f32[2,64,1024]{2,1,0:T(8,128)}, u32[]{:S(2)}, u32[]{:S(2)}) collective-permute-start(f32[2,64,1024]{2,1,0:T(8,128)S(1)} %get-tuple-element.19.left_ref.refs_12_), channel_id=1, source_target_pairs={{0,1},{1,0},{2,3},{3,2},{4,5},{5,4},{6,7},{7,6},{8,9},{9,8},{10,11... | collective-permute-start | bytes 1572872 | tf_op jit(solution)/shard_map/ppermute | solution.py:34
  18.1 22.9 %collective-permute-start.11 = (f32[2,64,1024]{2,1,0:T(8,128)S(1)}, f32[2,64,1024]{2,1,0:T(8,128)}, u32[]{:S(2)}, u32[]{:S(2)}) collective-permute-start(f32[2,64,1024]{2,1,0:T(8,128)S(1)} %get-tuple-element.19.left_ref.refs_12_), channel_id=1, source_target_pairs={{0,4},{4,8},{8,12},{1,5},{5,9},{9,13},{2,6},{6,10},{10,14},{3,7},{... | collective-permute-start | bytes 1572872 | tf_op jit(solution)/shard_map/ppermute | solution.py:30
  23.8 15.7 %all-to-all-start.1 = ((f32[4,136,128]{2,1,0:T(8,128)}), f32[4,136,128]{2,1,0:T(8,128)S(1)}, u32[]{:S(2)}, u32[]{:S(2)}) async-start(f32[4,136,128]{2,1,0:T(8,128)} %shard_map.123), calls=%async_computation.1 | async-start | bytes 557056 | tf_op jit(solution)/shard_map/all_to_all | solution.py:461
  27.3 1.5 %collective-permute-start.4 = (f32[2,64,256]{2,1,0:T(8,128)S(1)}, f32[2,64,256]{2,1,0:T(8,128)}, u32[]{:S(2)}, u32[]{:S(2)}) collective-permute-start(f32[2,64,256]{2,1,0:T(8,128)S(1)} %copy-done.4), channel_id=1, source_target_pairs={{0,1},{1,0},{2,3},{3,2},{4,5},{5,4},{6,7},{7,6},{8,9},{9,8},{10,11... | collective-permute-start | bytes 393224 | tf_op jit(solution)/shard_map/ppermute | solution.py:34
  27.5 1.5 %collective-permute-start.5 = (f32[2,72,256]{2,1,0:T(8,128)S(1)}, f32[2,72,256]{2,1,0:T(8,128)S(1)}, u32[]{:S(2)}, u32[]{:S(2)}) collective-permute-start(f32[2,72,256]{2,1,0:T(8,128)S(1)} %collective-permute-done.mp_below.refs_10_), channel_id=1, source_target_pairs={{0,1},{1,0},{2,3},{3,2},{4,5},{5,4},{6,7},{7,6},{8,9},{9,8},{10,11... | collective-permute-start | bytes 442376 | tf_op jit(solution)/shard_map/ppermute | solution.py:34
  28.8 1.4 %collective-permute-start.2 = (f32[2,72,256]{2,1,0:T(8,128)S(1)}, f32[2,72,256]{2,1,0:T(8,128)S(1)}, u32[]{:S(2)}, u32[]{:S(2)}) collective-permute-start(f32[2,72,256]{2,1,0:T(8,128)S(1)} %copy-done.2), channel_id=1, source_target_pairs={{0,1},{1,0},{2,3},{3,2},{4,5},{5,4},{6,7},{7,6},{8,9},{9,8},{10,11... | collective-permute-start | bytes 442376 | tf_op jit(solution)/shard_map/ppermute | solution.py:34
  29.0 28.6 %copy-start.19 = (f32[2,72,256]{2,1,0:T(8,128)}, f32[2,72,256]{2,1,0:T(8,128)S(1)}, u32[]{:S(2)}) copy-start(f32[2,72,256]{2,1,0:T(8,128)S(1)} %collective-permute-done.5.refs_11_) | copy-start | bytes 442372
  30.2 0.7 copy-start.20
  31.9 25.7 %copy-start.6 = (f32[2,64,1024]{2,1,0:T(8,128)}, f32[2,64,1024]{2,1,0:T(8,128)S(1)}, u32[]{:S(2)}) copy-start(f32[2,64,1024]{2,1,0:T(8,128)S(1)} %get-tuple-element.29.refs_16_) | copy-start | bytes 1572868
  31.9 9.0 %collective-permute-start.6 = (f32[64,128]{1,0:T(8,128)S(1)}, f32[64,128]{1,0:T(8,128)S(1)}, u32[]{:S(2)}, u32[]{:S(2)}) collective-permute-start(f32[64,128]{1,0:T(8,128)S(1)} %get-tuple-element.25), channel_id=1, source_target_pairs={{0,2},{2,0},{1,3},{3,1},{4,6},{6,4},{5,7},{7,5},{8,10},{10,8},{9,1... | collective-permute-start | bytes 98312 | tf_op jit(solution)/shard_map/ppermute | solution.py:34
  39.4 18.2 %copy-start.12 = (f32[4,136,128]{2,1,0:T(8,128)}, f32[4,136,128]{2,1,0:T(8,128)S(1)}, u32[]{:S(2)}) copy-start(f32[4,136,128]{2,1,0:T(8,128)S(1)} %all-to-all-done.1.refs_2_) | copy-start | bytes 835588
  39.4 16.3 %collective-permute-start.8 = (f32[4,136,128]{2,1,0:T(8,128)S(1)}, f32[4,136,128]{2,1,0:T(8,128)S(1)}, u32[]{:S(2)}, u32[]{:S(2)}) collective-permute-start(f32[4,136,128]{2,1,0:T(8,128)S(1)} %all-to-all-done.1.refs_2_), channel_id=1, source_target_pairs={{0,2},{2,0},{1,3},{3,1},{4,6},{6,4},{5,7},{7,5},{8,10},{10,8},{9,1... | collective-permute-start | bytes 835592 | tf_op jit(solution)/shard_map/ppermute | solution.py:34
  40.9 16.6 %collective-permute-start.13 = (f32[2,64,1024]{2,1,0:T(8,128)S(1)}, f32[2,64,1024]{2,1,0:T(8,128)S(1)}, u32[]{:S(2)}, u32[]{:S(2)}) collective-permute-start(f32[2,64,1024]{2,1,0:T(8,128)S(1)} %get-tuple-element.29.refs_16_), channel_id=1, source_target_pairs={{0,1},{1,0},{2,3},{3,2},{4,5},{5,4},{6,7},{7,6},{8,9},{9,8},{10,11... | collective-permute-start | bytes 1572872 | tf_op jit(solution)/shard_map/ppermute | solution.py:34
  40.9 16.6 %collective-permute-start.12 = (f32[2,64,1024]{2,1,0:T(8,128)}, f32[2,64,1024]{2,1,0:T(8,128)S(1)}, u32[]{:S(2)}, u32[]{:S(2)}) collective-permute-start(f32[2,64,1024]{2,1,0:T(8,128)} %collective-permute-done.11.refs_14_), channel_id=1, source_target_pairs={{0,1},{1,0},{2,3},{3,2},{4,5},{5,4},{6,7},{7,6},{8,9},{9,8},{10,11... | collective-permute-start | bytes 1572872 | tf_op jit(solution)/shard_map/ppermute | solution.py:34
  42.2 13.5 %all-to-all-start = ((f32[4,64,128]{2,1,0:T(8,128)}), f32[4,64,128]{2,1,0:T(8,128)S(1)}, u32[]{:S(2)}, u32[]{:S(2)}) async-start(f32[4,64,128]{2,1,0:T(8,128)} %broadcast_in_dim.2), calls=%async_computation | async-start | bytes 262144 | tf_op jit(solution)/shard_map/all_to_all | solution.py:502
  49.6 6.7 %collective-permute-start.9 = (f32[4,136,128]{2,1,0:T(8,128)S(1)}, f32[4,136,128]{2,1,0:T(8,128)S(1)}, u32[]{:S(2)}, u32[]{:S(2)}) collective-permute-start(f32[4,136,128]{2,1,0:T(8,128)S(1)} %all-to-all-done.1.refs_2_), channel_id=1, source_target_pairs={{0,1},{1,0},{2,3},{3,2},{4,5},{5,4},{6,7},{7,6},{8,9},{9,8},{10,11... | collective-permute-start | bytes 835592 | tf_op jit(solution)/shard_map/ppermute | solution.py:34
  55.7 1.9 %copy-start.15 = (f32[4,64,128]{2,1,0:T(8,128)}, f32[4,64,128]{2,1,0:T(8,128)S(1)}, u32[]{:S(2)}) copy-start(f32[4,64,128]{2,1,0:T(8,128)S(1)} %all-to-all-done.refs_0_) | copy-start | bytes 393220
  55.7 1.9 %copy-start.16 = (f32[4,136,128]{2,1,0:T(8,128)}, f32[4,136,128]{2,1,0:T(8,128)S(1)}, u32[]{:S(2)}) copy-start(f32[4,136,128]{2,1,0:T(8,128)S(1)} %collective-permute-done.8.refs_3_) | copy-start | bytes 835588
  55.7 1.8 %collective-permute-start.10 = (f32[4,136,128]{2,1,0:T(8,128)S(1)}, f32[4,136,128]{2,1,0:T(8,128)S(1)}, u32[]{:S(2)}, u32[]{:S(2)}) collective-permute-start(f32[4,136,128]{2,1,0:T(8,128)S(1)} %collective-permute-done.8.refs_3_), channel_id=1, source_target_pairs={{0,1},{1,0},{2,3},{3,2},{4,5},{5,4},{6,7},{7,6},{8,9},{9,8},{10,11... | collective-permute-start | bytes 835592 | tf_op jit(solution)/shard_map/ppermute | solution.py:34
  55.8 1.7 %collective-permute-start.7 = (f32[4,64,128]{2,1,0:T(8,128)S(1)}, f32[4,64,128]{2,1,0:T(8,128)S(1)}, u32[]{:S(2)}, u32[]{:S(2)}) collective-permute-start(f32[4,64,128]{2,1,0:T(8,128)S(1)} %all-to-all-done.refs_0_), channel_id=1, source_target_pairs={{0,1},{1,0},{2,3},{3,2},{4,5},{5,4},{6,7},{7,6},{8,9},{9,8},{10,11... | collective-permute-start | bytes 393224 | tf_op jit(solution)/shard_map/ppermute | solution.py:34
  56.3 1.3 %copy-start.17 = (f32[4,136,128]{2,1,0:T(8,128)}, f32[4,136,128]{2,1,0:T(8,128)S(1)}, u32[]{:S(2)}) copy-start(f32[4,136,128]{2,1,0:T(8,128)S(1)} %collective-permute-done.9.refs_4_) | copy-start | bytes 835588
  57.5 0.7 copy-start.21
  57.5 0.8 %copy-start.13 = (f32[2,64,1024]{2,1,0:T(8,128)}, f32[2,64,1024]{2,1,0:T(8,128)S(1)}, u32[]{:S(2)}) copy-start(f32[2,64,1024]{2,1,0:T(8,128)S(1)} %collective-permute-done.13.refs_17_) | copy-start | bytes 1572868
  57.5 1.0 %copy-start.14 = (f32[2,64,1024]{2,1,0:T(8,128)}, f32[2,64,1024]{2,1,0:T(8,128)S(1)}, u32[]{:S(2)}) copy-start(f32[2,64,1024]{2,1,0:T(8,128)S(1)} %collective-permute-done.12.refs_15_) | copy-start | bytes 1572868
  57.6 1.1 %copy-start.18 = (f32[4,136,128]{2,1,0:T(8,128)}, f32[4,136,128]{2,1,0:T(8,128)S(1)}, u32[]{:S(2)}) copy-start(f32[4,136,128]{2,1,0:T(8,128)S(1)} %collective-permute-done.10.refs_5_) | copy-start | bytes 835588

commit v16 on v15

--- a/solution.py
+++ b/solution.py
@@ -169,7 +169,7 @@
             pack_ref[copy] = pack_ref[0]
 
 
-def below_kernel(z, second, mp_below, b_ref, right_ref):
+def below_kernel(z, second, mp_below, b_ref, touched, right_ref):
     owner, sub = lax.axis_index("orb"), lax.axis_index("sub")
     start = side_start(z, jnp.maximum(owner - 1, 0), sub, 0)
     for p in range(z.pairs):
@@ -177,6 +177,10 @@
         held = jnp.where(j >= 0, 1.0, 0.0)
         mapped = mp_below[p, : z.pnos, :] * held
         right_ref[p] = mm(mapped, b_ref[jnp.clip(j, 0, z.orbitals - 1)])
+
+
+def early_kernel(z, second, mp_ref, b_ref, out_ref):
+    out_ref[...] = b_ref[0, :EXTRA, :128] + mp_ref[...] + second[0].astype(jnp.float32)
 
 
 def local_kernel(z, first, second, c_ref, mp_ref, b_ref, left_ref, right_ref):
@@ -461,11 +465,18 @@
         packs = [lax.all_to_all(pack, "orb", 0, 0)]
     else:
         packs = [lax.all_gather(pack, ("orb", "sub"), axis=0, tiled=True)]
+    (touched,) = call(
+        functools.partial(early_kernel, z),
+        [(EXTRA, 128)],
+        [smem, vmem, vmem],
+        (pair_second, mp[0, :EXTRA, :128], blocks),
+        limit=8,
+    )
     (right_below,) = call(
         functools.partial(below_kernel, z),
         [(pairs, n, fits)],
-        [smem, vmem, vmem],
-        (pair_second, gate((mp_below,), pack)[0], blocks),
+        [smem, vmem, vmem, vmem],
+        (pair_second, gate((mp_below,), pack)[0], blocks, touched),
         limit=8,
     )
     down = shifted(right_below, "orb", -1)
@@ -479,7 +490,6 @@
         limit=8,
         cost=BRIEF,
     )
-    left_below = shifted(left, "orb", 1)
     mp_other = swapped(gate((mp,), right_here)[0], "sub")
     left_other = swapped(left, "sub")
     c_other = swapped(gate((coefficients,), right_here)[0], "sub")
@@ -507,8 +517,12 @@
         sums = lax.psum(part, "fit")
         start_amps = [lax.all_gather(sums, ("orb", "sub"), axis=0, tiled=False)]
 
-    right_other = swapped(right, "sub")
-    left_below_other = swapped(gate((left_below,), sums)[0], "sub")
+    (right_late,) = gate((right,), part)
+    left_below = shifted(gate((left,), part)[0], "orb", 1)
+    (left_late,) = gate((left_below,), start_amps[0])
+    right_other, left_below_other = [
+        swapped(value, "sub") for value in (right_late, left_late)
+    ]
 
     args = (
         *lists, neighbours.T, occ_energy, *start_amps, *packs,

time: 67.4 us -> 63.2 us (0.938)
  waiting for transfers between devices: 17.2 us -> 14.5 us
  starting transfers between devices: 28 us -> 25.6 us
    all_to_all x1, waiting for transfers between devices: 5.99 us -> 0.01 us  [body(): packs = [lax.all_to_all(pack, 'orb', 0, 0)]]
    ppermute x3, waiting for transfers between devices: 1.7 us -> 5.85 us  [shifted(): lax.ppermute(value, axis, [(source, source + steps) for source in range(i...]
    all_to_all x1, starting transfers between devices: 7.44 us -> 3.33 us  [body(): lax.all_to_all(jnp.broadcast_to(sums[None], (z.owners, *sums.shape)), 'or...]
    all_to_all x1, starting transfers between devices: 3.56 us -> 5.96 us  [body(): packs = [lax.all_to_all(pack, 'orb', 0, 0)]]
    all_to_all x1, waiting for transfers between devices: 6.08 us -> 4.33 us  [body(): lax.all_to_all(jnp.broadcast_to(sums[None], (z.owners, *sums.shape)), 'or...]
    ppermute x3, starting transfers between devices: 12.1 us -> 11 us  [shifted(): lax.ppermute(value, axis, [(source, source + steps) for source in range(i...]
    ppermute x11, waiting for transfers between devices: 3.41 us -> 4.31 us  [swapped(): return lax.ppermute(value, axis, [(0, 1), (1, 0)])]
    squeeze x0 -> x1, local copies, waits for them, and re-layouts: none -> 0.68 us  [body(): mp[0, :EXTRA, :128]]
  transfers between devices with their start and end apart: 16 -> 16, of which waited for: 6 -> 6; matrix products, arithmetic and copies ran while one was open for 1% -> 2% of each run, Pallas kernels for 7% -> 8%
where the time goes in v16:
time: 63.2 us; the launch traced here: 62.7 us
  starting transfers between devices  25.6 us (41%)
  Pallas kernels  16.6 us (26%)
  waiting for transfers between devices  14.5 us (23%)
  local copies, waits for them, and re-layouts  5.05 us (8%)
  between operations  0.96 us (2%)
    pallas_call x7, Pallas kernels, call(): pl.pallas_call(kernel, out_shape=[jax.ShapeDtypeStruct(shape, jnp.float32...  16.6 us
    ppermute x3, starting transfers between devices, shifted(): lax.ppermute(value, axis, [(source, source + steps) for source in range(i...  11 us
    all_to_all x1, starting transfers between devices, body(): packs = [lax.all_to_all(pack, 'orb', 0, 0)]  5.96 us
    ppermute x3, waiting for transfers between devices, shifted(): lax.ppermute(value, axis, [(source, source + steps) for source in range(i...  5.85 us
    ppermute x11, starting transfers between devices, swapped(): return lax.ppermute(value, axis, [(0, 1), (1, 0)])  5.25 us
    all_to_all x1, waiting for transfers between devices, body(): lax.all_to_all(jnp.broadcast_to(sums[None], (z.owners, *sums.shape)), 'or...  4.33 us
    ppermute x11, waiting for transfers between devices, swapped(): return lax.ppermute(value, axis, [(0, 1), (1, 0)])  4.31 us
    unnamed x48, local copies, waits for them, and re-layouts  3.67 us
  transfers between devices with their start and end apart: 16, of which 6 were waited for; matrix products, arithmetic and copies ran while one was open for 2% of the time, Pallas kernels for 8%

profile of v16, /device:TPU:0, one launch (start us, length us, event | category | flops | bytes accessed | tf_op | source)
XLA Modules:
  0.0 62.7 jit_solution(17522489963322961417)
XLA Ops:
  0.6 1.9 %shard_map.122.mp_in.mp_ref.refs_8_ = f32[2,72,256]{2,1,0:T(8,128)} custom-call(f32[2,64,256]{2,1,0:T(8,128)} %refs_6_.1, s32[2,256]{1,0:T(2,128)} %map_in.1, f32[2,64]{1,0:T(2,128)} %e_in.1, f32[2,4]{1,0:T(2,128)} %coupling_in.1), custom_call_target="tpu_custom_call" | custom-call | tf_op jit(solution)/shard_map/pallas_call | solution.py:58
  2.5 4.9 %collective-permute-start = (f32[2,72,256]{2,1,0:T(8,128)}, f32[2,72,256]{2,1,0:T(8,128)S(1)}, u32[]{:S(2)}, u32[]{:S(2)}) collective-permute-start(f32[2,72,256]{2,1,0:T(8,128)} %shard_map.122.mp_in.mp_ref.refs_8_), channel_id=1, source_target_pairs={{0,4},{4,8},{8,12},{1,5},{5,9},{9,13},{2,6},{6,10},{10,14},{3,7},{... | collective-permute-start | bytes 442376 | tf_op jit(solution)/shard_map/ppermute | solution.py:30
  7.5 1.7 %shard_map.123 = f32[4,136,128]{2,1,0:T(8,128)} custom-call(f32[2,4,4096]{2,1,0:T(4,128)} %s_in.1, f32[2,72,256]{2,1,0:T(8,128)} %shard_map.122.mp_in.mp_ref.refs_8_), custom_call_target="tpu_custom_call" | custom-call | tf_op jit(solution)/shard_map/pallas_call | solution.py:58
  9.2 0.7 %slice_bitcast_fusion.mp_ref = f32[8,128]{1,0:T(8,128)S(1)} fusion(f32[2,72,256]{2,1,0:T(8,128)} %shard_map.122.mp_in.mp_ref.refs_8_), kind=kLoop, calls=%fused_computation | loop fusion | bytes 8192 | tf_op jit(solution)/shard_map/squeeze | solution.py:472
  9.8 1.6 %copy-done = f32[2,256,1024]{2,1,0:T(8,128)S(1)} copy-done((f32[2,256,1024]{2,1,0:T(8,128)S(1)}, f32[2,256,1024]{2,1,0:T(8,128)}, u32[]{:S(2)}) %copy-start) | copy-done | bytes 2097176
  11.4 0.7 %copy-done.7 = s32[16]{0:T(128)S(1)} copy-done((s32[16]{0:T(128)S(1)}, s32[16]{0:T(128)}, u32[]{:S(2)}) %copy-start.7) | copy-done | bytes 88
  12.1 0.0 copy-start.9
  12.1 0.5 shard_map.124.touched
  12.7 0.0 collective-permute-done.mp_below.refs_10_
  12.7 1.3 %shard_map.125 = f32[2,64,1024]{2,1,0:T(8,128)S(1)} custom-call(s32[16]{0:T(128)S(1)} %copy-done.7, f32[2,72,256]{2,1,0:T(8,128)S(1)} %collective-permute-done.mp_below.refs_10_, f32[2,256,1024]{2,1,0:T(8,128)S(1)} %copy-done, f32[8,128]{1,0:T(8,128)S(1)} %shard_map.124.touched), custom_call_target="tpu_custom_call" | custom-call | tf_op jit(solution)/shard_map/pallas_call | solution.py:58
  14.0 0.0 copy-start.10
  14.0 0.0 copy-start.11
  14.0 1.3 %collective-permute-start.1 = (f32[2,64,1024]{2,1,0:T(8,128)S(1)}, f32[2,64,1024]{2,1,0:T(8,128)S(1)}, u32[]{:S(2)}, u32[]{:S(2)}) collective-permute-start(f32[2,64,1024]{2,1,0:T(8,128)S(1)} %shard_map.125), channel_id=1, source_target_pairs={{4,0},{8,4},{12,8},{5,1},{9,5},{13,9},{6,2},{10,6},{14,10},{7,3},{... | collective-permute-start | bytes 1572872 | tf_op jit(solution)/shard_map/ppermute | solution.py:30
  15.4 1.9 %shard_map.126 = (f32[2,64,1024]{2,1,0:T(8,128)S(1)}, f32[2,64,1024]{2,1,0:T(8,128)S(1)}) custom-call(s32[16]{0:T(128)S(1)} %copy-done.9, s32[16]{0:T(128)S(1)} %copy-done.8, f32[2,64,256]{2,1,0:T(8,128)S(1)} %copy-done.4, f32[2,72,256]{2,1,0:T(8,128)S(1)} %copy-done.2, f32[2,256,1024]{2,1,0:T(8,128)S(1)} %copy-done.1), custom_call_target="tpu_custom_call" | custom-call | flops 1 | bytes 1 | tf_op jit(solution)/shard_map/pallas_call | solution.py:58
  17.3 0.1 collective-permute-start.3
  17.4 0.5 collective-permute-start.5
  17.9 0.1 collective-permute-start.2
  18.0 0.4 collective-permute-start.4
  18.4 6.0 %all-to-all-start.1 = ((f32[4,136,128]{2,1,0:T(8,128)}), f32[4,136,128]{2,1,0:T(8,128)S(1)}, u32[]{:S(2)}, u32[]{:S(2)}) async-start(f32[4,136,128]{2,1,0:T(8,128)} %shard_map.123), calls=%async_computation.1 | async-start | bytes 557056 | tf_op jit(solution)/shard_map/all_to_all | solution.py:465
  24.3 0.0 collective-permute-done.4.refs_7_
  24.4 0.0 collective-permute-done.5.refs_11_
  24.4 0.0 collective-permute-done.2.refs_9_
  24.4 5.8 %collective-permute-done.1.down_ref = f32[2,64,1024]{2,1,0:T(8,128)S(1)} collective-permute-done((f32[2,64,1024]{2,1,0:T(8,128)S(1)}, f32[2,64,1024]{2,1,0:T(8,128)S(1)}, u32[]{:S(2)}, u32[]{:S(2)}) %collective-permute-start.1) | collective-permute-done | bytes 524320 | tf_op jit(solution)/shard_map/ppermute | solution.py:30
  30.2 0.0 collective-permute-done.3.refs_13_
  30.3 1.0 %shard_map.127 = (f32[64,128]{1,0:T(8,128)S(1)}, f32[2,64,1024]{2,1,0:T(8,128)S(1)}) custom-call(s32[16]{0:T(128)S(1)} %copy-done.9, s32[16]{0:T(128)S(1)} %copy-done.8, s32[16]{0:T(128)S(1)} %copy-done.10, f32[8]{0:T(128)S(1)} %copy-done.11, f32[2,72,256]{2,1,0:T(8,128)S(1)} %copy-done.2, f32[2,64,1024]{2,1,0:T(8,128)S(1)} %get-tuple-element.30.left_ref.refs_12_, ...), custom_call_target="tpu_custom_call" | custom-call | tf_op jit(solution)/shard_map/pallas_call | solution.py:58
  31.3 4.8 %collective-permute-start.11 = (f32[2,64,1024]{2,1,0:T(8,128)S(1)}, f32[2,64,1024]{2,1,0:T(8,128)S(1)}, u32[]{:S(2)}, u32[]{:S(2)}) collective-permute-start(f32[2,64,1024]{2,1,0:T(8,128)S(1)} %get-tuple-element.30.left_ref.refs_12_), channel_id=1, source_target_pairs={{0,4},{4,8},{8,12},{1,5},{5,9},{9,13},{2,6},{6,10},{10,14},{3,7},{... | collective-permute-start | bytes 1572872 | tf_op jit(solution)/shard_map/ppermute | solution.py:30
  36.1 1.6 %collective-permute-start.6 = (f32[64,128]{1,0:T(8,128)S(1)}, f32[64,128]{1,0:T(8,128)S(1)}, u32[]{:S(2)}, u32[]{:S(2)}) collective-permute-start(f32[64,128]{1,0:T(8,128)S(1)} %get-tuple-element.27), channel_id=1, source_target_pairs={{0,2},{2,0},{1,3},{3,1},{4,6},{6,4},{5,7},{7,5},{8,10},{10,8},{9,1... | collective-permute-start | bytes 98312 | tf_op jit(solution)/shard_map/ppermute | solution.py:34
  37.6 2.4 %collective-permute-done.6 = f32[64,128]{1,0:T(8,128)S(1)} collective-permute-done((f32[64,128]{1,0:T(8,128)S(1)}, f32[64,128]{1,0:T(8,128)S(1)}, u32[]{:S(2)}, u32[]{:S(2)}) %collective-permute-start.6) | collective-permute-done | bytes 32800 | tf_op jit(solution)/shard_map/ppermute | solution.py:34
  40.1 0.0 all-to-all-done.1.refs_2_
  40.1 0.7 %broadcast_in_dim.2 = f32[4,64,128]{2,1,0:T(8,128)} broadcast(f32[64,128]{1,0:T(8,128)S(1)} %add.3), dimensions={1,2} | broadcast | bytes 163840 | tf_op jit(solution)/shard_map/broadcast_in_dim | solution.py:512
  40.8 3.3 %all-to-all-start = ((f32[4,64,128]{2,1,0:T(8,128)}), f32[4,64,128]{2,1,0:T(8,128)S(1)}, u32[]{:S(2)}, u32[]{:S(2)}) async-start(f32[4,64,128]{2,1,0:T(8,128)} %broadcast_in_dim.2), calls=%async_computation | async-start | bytes 262144 | tf_op jit(solution)/shard_map/all_to_all | solution.py:512
  44.1 1.6 %collective-permute-start.8 = (f32[4,136,128]{2,1,0:T(8,128)S(1)}, f32[4,136,128]{2,1,0:T(8,128)S(1)}, u32[]{:S(2)}, u32[]{:S(2)}) collective-permute-start(f32[4,136,128]{2,1,0:T(8,128)S(1)} %all-to-all-done.1.refs_2_), channel_id=1, source_target_pairs={{0,2},{2,0},{1,3},{3,1},{4,6},{6,4},{5,7},{7,5},{8,10},{10,8},{9,1... | collective-permute-start | bytes 835592 | tf_op jit(solution)/shard_map/ppermute | solution.py:34
  45.7 0.0 collective-permute-start.13
  45.7 4.3 %all-to-all-done.refs_0_ = f32[4,64,128]{2,1,0:T(8,128)S(1)} async-done(((f32[4,64,128]{2,1,0:T(8,128)}), f32[4,64,128]{2,1,0:T(8,128)S(1)}, u32[]{:S(2)}, u32[]{:S(2)}) %all-to-all-start) | async-done | bytes 131104 | tf_op jit(solution)/shard_map/all_to_all | solution.py:512
  50.0 0.0 collective-permute-done.11.refs_14_
  50.0 0.1 collective-permute-start.12
  50.1 0.5 collective-permute-start.9
  50.6 0.1 collective-permute-done.8.refs_3_
  50.7 0.0 collective-permute-start.10
  50.7 0.5 collective-permute-start.7
  51.2 1.1 %collective-permute-done.9.refs_4_ = f32[4,136,128]{2,1,0:T(8,128)S(1)} collective-permute-done((f32[4,136,128]{2,1,0:T(8,128)S(1)}, f32[4,136,128]{2,1,0:T(8,128)S(1)}, u32[]{:S(2)}, u32[]{:S(2)}) %collective-permute-start.9) | collective-permute-done | bytes 278560 | tf_op jit(solution)/shard_map/ppermute | solution.py:34
  52.4 0.6 collective-permute-done.7.refs_1_
  53.0 0.0 collective-permute-done.12.refs_15_
  53.0 0.6 copy-done.23
  53.7 0.2 copy-done.14
  53.8 0.1 copy-done.19
  53.9 0.5 copy-done.15
  54.4 8.3 %shard_map.128 = (f32[2,4096]{1,0:T(2,128)}, f32[2,128,1024]{2,1,0:T(8,128)}) custom-call(s32[16]{0:T(128)} %first.5, s32[16]{0:T(128)} %second.9, s32[16]{0:T(128)} %ranks.3, s32[4,16]{1,0:T(4,128)} %bitcast.3, f32[8]{0:T(128)} %occupied.3, f32[4,64,128]{2,1,0:T(8,128)} %copy-done.16, f32[4,64,128]{2,1,0:T(8,128)} %copy-done.23, f32[4,136,128]{2,1,0:T(8,128)} %copy-done.12, ...), custom_call_target="tpu_custom_call" | custom-call | tf_op jit(solution)/shard_map/pallas_call | solution.py:58
  (42 shorter events, 0.1 us)
Async XLA Ops:
  2.5 10.1 %collective-permute-start = (f32[2,72,256]{2,1,0:T(8,128)}, f32[2,72,256]{2,1,0:T(8,128)S(1)}, u32[]{:S(2)}, u32[]{:S(2)}) collective-permute-start(f32[2,72,256]{2,1,0:T(8,128)} %shard_map.122.mp_in.mp_ref.refs_8_), channel_id=1, source_target_pairs={{0,4},{4,8},{8,12},{1,5},{5,9},{9,13},{2,6},{6,10},{10,14},{3,7},{... | collective-permute-start | bytes 442376 | tf_op jit(solution)/shard_map/ppermute | solution.py:30
  9.8 1.6 %copy-start = (f32[2,256,1024]{2,1,0:T(8,128)S(1)}, f32[2,256,1024]{2,1,0:T(8,128)}, u32[]{:S(2)}) copy-start(f32[2,256,1024]{2,1,0:T(8,128)} %b_ref.5) | copy-start | bytes 6291460
  11.4 0.7 %copy-start.7 = (s32[16]{0:T(128)S(1)}, s32[16]{0:T(128)}, u32[]{:S(2)}) copy-start(s32[16]{0:T(128)} %second.9) | copy-start | bytes 196
  12.1 3.2 %copy-start.1 = (f32[2,256,1024]{2,1,0:T(8,128)S(1)}, f32[2,256,1024]{2,1,0:T(8,128)}, u32[]{:S(2)}) copy-start(f32[2,256,1024]{2,1,0:T(8,128)} %b_ref.5) | copy-start | bytes 6291460
  12.1 3.2 %copy-start.2 = (f32[2,72,256]{2,1,0:T(8,128)S(1)}, f32[2,72,256]{2,1,0:T(8,128)}, u32[]{:S(2)}) copy-start(f32[2,72,256]{2,1,0:T(8,128)} %shard_map.122.mp_in.mp_ref.refs_8_) | copy-start | bytes 442372
  12.1 3.2 %copy-start.4 = (f32[2,64,256]{2,1,0:T(8,128)S(1)}, f32[2,64,256]{2,1,0:T(8,128)}, u32[]{:S(2)}) copy-start(f32[2,64,256]{2,1,0:T(8,128)} %refs_6_.1) | copy-start | bytes 393220
  12.1 3.3 %copy-start.8 = (s32[16]{0:T(128)S(1)}, s32[16]{0:T(128)}, u32[]{:S(2)}) copy-start(s32[16]{0:T(128)} %second.9) | copy-start | bytes 196
  12.1 3.3 %copy-start.9 = (s32[16]{0:T(128)S(1)}, s32[16]{0:T(128)}, u32[]{:S(2)}) copy-start(s32[16]{0:T(128)} %first.5) | copy-start | bytes 196
  12.7 4.7 %copy-start.5 = (f32[2,72,256]{2,1,0:T(8,128)}, f32[2,72,256]{2,1,0:T(8,128)S(1)}, u32[]{:S(2)}) copy-start(f32[2,72,256]{2,1,0:T(8,128)S(1)} %collective-permute-done.mp_below.refs_10_) | copy-start | bytes 442372
  14.0 16.3 %copy-start.10 = (s32[16]{0:T(128)S(1)}, s32[16]{0:T(128)}, u32[]{:S(2)}) copy-start(s32[16]{0:T(128)} %ranks.3) | copy-start | bytes 196
  14.0 16.2 %copy-start.11 = (f32[8]{0:T(128)S(1)}, f32[8]{0:T(128)}, u32[]{:S(2)}) copy-start(f32[8]{0:T(128)} %occupied.3) | copy-start | bytes 100
  14.0 16.2 %collective-permute-start.1 = (f32[2,64,1024]{2,1,0:T(8,128)S(1)}, f32[2,64,1024]{2,1,0:T(8,128)S(1)}, u32[]{:S(2)}, u32[]{:S(2)}) collective-permute-start(f32[2,64,1024]{2,1,0:T(8,128)S(1)} %shard_map.125), channel_id=1, source_target_pairs={{4,0},{8,4},{12,8},{5,1},{9,5},{13,9},{6,2},{10,6},{14,10},{7,3},{... | collective-permute-start | bytes 1572872 | tf_op jit(solution)/shard_map/ppermute | solution.py:30
  17.3 36.3 %copy-start.3 = (f32[2,64,1024]{2,1,0:T(8,128)}, f32[2,64,1024]{2,1,0:T(8,128)S(1)}, u32[]{:S(2)}) copy-start(f32[2,64,1024]{2,1,0:T(8,128)S(1)} %get-tuple-element.30.left_ref.refs_12_) | copy-start | bytes 1572868
  17.3 12.9 %collective-permute-start.3 = (f32[2,64,1024]{2,1,0:T(8,128)S(1)}, f32[2,64,1024]{2,1,0:T(8,128)}, u32[]{:S(2)}, u32[]{:S(2)}) collective-permute-start(f32[2,64,1024]{2,1,0:T(8,128)S(1)} %get-tuple-element.30.left_ref.refs_12_), channel_id=1, source_target_pairs={{0,1},{1,0},{2,3},{3,2},{4,5},{5,4},{6,7},{7,6},{8,9},{9,8},{10,11... | collective-permute-start | bytes 1572872 | tf_op jit(solution)/shard_map/ppermute | solution.py:34
  17.4 7.0 %collective-permute-start.5 = (f32[2,72,256]{2,1,0:T(8,128)S(1)}, f32[2,72,256]{2,1,0:T(8,128)S(1)}, u32[]{:S(2)}, u32[]{:S(2)}) collective-permute-start(f32[2,72,256]{2,1,0:T(8,128)S(1)} %collective-permute-done.mp_below.refs_10_), channel_id=1, source_target_pairs={{0,1},{1,0},{2,3},{3,2},{4,5},{5,4},{6,7},{7,6},{8,9},{9,8},{10,11... | collective-permute-start | bytes 442376 | tf_op jit(solution)/shard_map/ppermute | solution.py:34
  17.9 6.5 %collective-permute-start.2 = (f32[2,72,256]{2,1,0:T(8,128)S(1)}, f32[2,72,256]{2,1,0:T(8,128)S(1)}, u32[]{:S(2)}, u32[]{:S(2)}) collective-permute-start(f32[2,72,256]{2,1,0:T(8,128)S(1)} %copy-done.2), channel_id=1, source_target_pairs={{0,1},{1,0},{2,3},{3,2},{4,5},{5,4},{6,7},{7,6},{8,9},{9,8},{10,11... | collective-permute-start | bytes 442376 | tf_op jit(solution)/shard_map/ppermute | solution.py:34
  18.0 6.4 %collective-permute-start.4 = (f32[2,64,256]{2,1,0:T(8,128)S(1)}, f32[2,64,256]{2,1,0:T(8,128)S(1)}, u32[]{:S(2)}, u32[]{:S(2)}) collective-permute-start(f32[2,64,256]{2,1,0:T(8,128)S(1)} %copy-done.4), channel_id=1, source_target_pairs={{0,1},{1,0},{2,3},{3,2},{4,5},{5,4},{6,7},{7,6},{8,9},{9,8},{10,11... | collective-permute-start | bytes 393224 | tf_op jit(solution)/shard_map/ppermute | solution.py:34
  18.4 21.7 %all-to-all-start.1 = ((f32[4,136,128]{2,1,0:T(8,128)}), f32[4,136,128]{2,1,0:T(8,128)S(1)}, u32[]{:S(2)}, u32[]{:S(2)}) async-start(f32[4,136,128]{2,1,0:T(8,128)} %shard_map.123), calls=%async_computation.1 | async-start | bytes 557056 | tf_op jit(solution)/shard_map/all_to_all | solution.py:465
  24.4 16.4 %copy-start.22 = (f32[2,64,256]{2,1,0:T(8,128)}, f32[2,64,256]{2,1,0:T(8,128)S(1)}, u32[]{:S(2)}) copy-start(f32[2,64,256]{2,1,0:T(8,128)S(1)} %collective-permute-done.4.refs_7_) | copy-start | bytes 393220
  24.4 29.3 %copy-start.20 = (f32[2,72,256]{2,1,0:T(8,128)}, f32[2,72,256]{2,1,0:T(8,128)S(1)}, u32[]{:S(2)}) copy-start(f32[2,72,256]{2,1,0:T(8,128)S(1)} %collective-permute-done.5.refs_11_) | copy-start | bytes 442372
  24.4 5.9 %copy-start.21 = (f32[2,72,256]{2,1,0:T(8,128)}, f32[2,72,256]{2,1,0:T(8,128)S(1)}, u32[]{:S(2)}) copy-start(f32[2,72,256]{2,1,0:T(8,128)S(1)} %collective-permute-done.2.refs_9_) | copy-start | bytes 442372
  31.3 22.4 %copy-start.6 = (f32[2,64,1024]{2,1,0:T(8,128)}, f32[2,64,1024]{2,1,0:T(8,128)S(1)}, u32[]{:S(2)}) copy-start(f32[2,64,1024]{2,1,0:T(8,128)S(1)} %get-tuple-element.33.refs_16_) | copy-start | bytes 1572868
  31.3 18.7 %collective-permute-start.11 = (f32[2,64,1024]{2,1,0:T(8,128)S(1)}, f32[2,64,1024]{2,1,0:T(8,128)S(1)}, u32[]{:S(2)}, u32[]{:S(2)}) collective-permute-start(f32[2,64,1024]{2,1,0:T(8,128)S(1)} %get-tuple-element.30.left_ref.refs_12_), channel_id=1, source_target_pairs={{0,4},{4,8},{8,12},{1,5},{5,9},{9,13},{2,6},{6,10},{10,14},{3,7},{... | collective-permute-start | bytes 1572872 | tf_op jit(solution)/shard_map/ppermute | solution.py:30
  36.1 4.0 %collective-permute-start.6 = (f32[64,128]{1,0:T(8,128)S(1)}, f32[64,128]{1,0:T(8,128)S(1)}, u32[]{:S(2)}, u32[]{:S(2)}) collective-permute-start(f32[64,128]{1,0:T(8,128)S(1)} %get-tuple-element.27), channel_id=1, source_target_pairs={{0,2},{2,0},{1,3},{3,1},{4,6},{6,4},{5,7},{7,5},{8,10},{10,8},{9,1... | collective-permute-start | bytes 98312 | tf_op jit(solution)/shard_map/ppermute | solution.py:34
  40.1 13.6 %copy-start.12 = (f32[4,136,128]{2,1,0:T(8,128)}, f32[4,136,128]{2,1,0:T(8,128)S(1)}, u32[]{:S(2)}) copy-start(f32[4,136,128]{2,1,0:T(8,128)S(1)} %all-to-all-done.1.refs_2_) | copy-start | bytes 835588
  40.8 9.2 %all-to-all-start = ((f32[4,64,128]{2,1,0:T(8,128)}), f32[4,64,128]{2,1,0:T(8,128)S(1)}, u32[]{:S(2)}, u32[]{:S(2)}) async-start(f32[4,64,128]{2,1,0:T(8,128)} %broadcast_in_dim.2), calls=%async_computation | async-start | bytes 262144 | tf_op jit(solution)/shard_map/all_to_all | solution.py:512
  44.1 6.6 %collective-permute-start.8 = (f32[4,136,128]{2,1,0:T(8,128)S(1)}, f32[4,136,128]{2,1,0:T(8,128)S(1)}, u32[]{:S(2)}, u32[]{:S(2)}) collective-permute-start(f32[4,136,128]{2,1,0:T(8,128)S(1)} %all-to-all-done.1.refs_2_), channel_id=1, source_target_pairs={{0,2},{2,0},{1,3},{3,1},{4,6},{6,4},{5,7},{7,5},{8,10},{10,8},{9,1... | collective-permute-start | bytes 835592 | tf_op jit(solution)/shard_map/ppermute | solution.py:34
  45.7 7.3 %collective-permute-start.13 = (f32[2,64,1024]{2,1,0:T(8,128)S(1)}, f32[2,64,1024]{2,1,0:T(8,128)S(1)}, u32[]{:S(2)}, u32[]{:S(2)}) collective-permute-start(f32[2,64,1024]{2,1,0:T(8,128)S(1)} %get-tuple-element.33.refs_16_), channel_id=1, source_target_pairs={{0,1},{1,0},{2,3},{3,2},{4,5},{5,4},{6,7},{7,6},{8,9},{9,8},{10,11... | collective-permute-start | bytes 1572872 | tf_op jit(solution)/shard_map/ppermute | solution.py:34
  50.0 3.6 %copy-start.16 = (f32[4,64,128]{2,1,0:T(8,128)}, f32[4,64,128]{2,1,0:T(8,128)S(1)}, u32[]{:S(2)}) copy-start(f32[4,64,128]{2,1,0:T(8,128)S(1)} %all-to-all-done.refs_0_) | copy-start | bytes 393220
  50.0 3.6 %copy-start.13 = (f32[2,64,1024]{2,1,0:T(8,128)}, f32[2,64,1024]{2,1,0:T(8,128)S(1)}, u32[]{:S(2)}) copy-start(f32[2,64,1024]{2,1,0:T(8,128)S(1)} %collective-permute-done.11.refs_14_) | copy-start | bytes 1572868
  50.0 3.0 %collective-permute-start.12 = (f32[2,64,1024]{2,1,0:T(8,128)S(1)}, f32[2,64,1024]{2,1,0:T(8,128)S(1)}, u32[]{:S(2)}, u32[]{:S(2)}) collective-permute-start(f32[2,64,1024]{2,1,0:T(8,128)S(1)} %collective-permute-done.11.refs_14_), channel_id=1, source_target_pairs={{0,1},{1,0},{2,3},{3,2},{4,5},{5,4},{6,7},{7,6},{8,9},{9,8},{10,11... | collective-permute-start | bytes 1572872 | tf_op jit(solution)/shard_map/ppermute | solution.py:34
  50.1 2.3 %collective-permute-start.9 = (f32[4,136,128]{2,1,0:T(8,128)S(1)}, f32[4,136,128]{2,1,0:T(8,128)S(1)}, u32[]{:S(2)}, u32[]{:S(2)}) collective-permute-start(f32[4,136,128]{2,1,0:T(8,128)S(1)} %all-to-all-done.1.refs_2_), channel_id=1, source_target_pairs={{0,1},{1,0},{2,3},{3,2},{4,5},{5,4},{6,7},{7,6},{8,9},{9,8},{10,11... | collective-permute-start | bytes 835592 | tf_op jit(solution)/shard_map/ppermute | solution.py:34
  50.7 2.9 %copy-start.17 = (f32[4,136,128]{2,1,0:T(8,128)}, f32[4,136,128]{2,1,0:T(8,128)S(1)}, u32[]{:S(2)}) copy-start(f32[4,136,128]{2,1,0:T(8,128)S(1)} %collective-permute-done.8.refs_3_) | copy-start | bytes 835588
  50.7 2.2 %collective-permute-start.10 = (f32[4,136,128]{2,1,0:T(8,128)S(1)}, f32[4,136,128]{2,1,0:T(8,128)S(1)}, u32[]{:S(2)}, u32[]{:S(2)}) collective-permute-start(f32[4,136,128]{2,1,0:T(8,128)S(1)} %collective-permute-done.8.refs_3_), channel_id=1, source_target_pairs={{0,1},{1,0},{2,3},{3,2},{4,5},{5,4},{6,7},{7,6},{8,9},{9,8},{10,11... | collective-permute-start | bytes 835592 | tf_op jit(solution)/shard_map/ppermute | solution.py:34
  50.7 2.2 %collective-permute-start.7 = (f32[4,64,128]{2,1,0:T(8,128)S(1)}, f32[4,64,128]{2,1,0:T(8,128)S(1)}, u32[]{:S(2)}, u32[]{:S(2)}) collective-permute-start(f32[4,64,128]{2,1,0:T(8,128)S(1)} %all-to-all-done.refs_0_), channel_id=1, source_target_pairs={{0,1},{1,0},{2,3},{3,2},{4,5},{5,4},{6,7},{7,6},{8,9},{9,8},{10,11... | collective-permute-start | bytes 393224 | tf_op jit(solution)/shard_map/ppermute | solution.py:34
  52.4 1.3 %copy-start.18 = (f32[4,136,128]{2,1,0:T(8,128)}, f32[4,136,128]{2,1,0:T(8,128)S(1)}, u32[]{:S(2)}) copy-start(f32[4,136,128]{2,1,0:T(8,128)S(1)} %collective-permute-done.9.refs_4_) | copy-start | bytes 835588
  53.0 0.6 %copy-start.23 = (f32[4,64,128]{2,1,0:T(8,128)}, f32[4,64,128]{2,1,0:T(8,128)S(1)}, u32[]{:S(2)}) copy-start(f32[4,64,128]{2,1,0:T(8,128)S(1)} %collective-permute-done.7.refs_1_) | copy-start | bytes 393220
  53.0 0.9 %copy-start.14 = (f32[2,64,1024]{2,1,0:T(8,128)}, f32[2,64,1024]{2,1,0:T(8,128)S(1)}, u32[]{:S(2)}) copy-start(f32[2,64,1024]{2,1,0:T(8,128)S(1)} %collective-permute-done.13.refs_17_) | copy-start | bytes 1572868
  53.0 0.9 %copy-start.19 = (f32[4,136,128]{2,1,0:T(8,128)}, f32[4,136,128]{2,1,0:T(8,128)S(1)}, u32[]{:S(2)}) copy-start(f32[4,136,128]{2,1,0:T(8,128)S(1)} %collective-permute-done.10.refs_5_) | copy-start | bytes 835588
  53.6 0.8 %copy-start.15 = (f32[2,64,1024]{2,1,0:T(8,128)}, f32[2,64,1024]{2,1,0:T(8,128)S(1)}, u32[]{:S(2)}) copy-start(f32[2,64,1024]{2,1,0:T(8,128)S(1)} %collective-permute-done.12.refs_15_) | copy-start | bytes 1572868

commit v17 on v16

--- a/solution.py
+++ b/solution.py
@@ -519,7 +519,7 @@
 
     (right_late,) = gate((right,), part)
     left_below = shifted(gate((left,), part)[0], "orb", 1)
-    (left_late,) = gate((left_below,), start_amps[0])
+    (left_late,) = gate((left_below,), start_amps[-1])
     right_other, left_below_other = [
         swapped(value, "sub") for value in (right_late, left_late)
     ]
@@ -555,7 +555,7 @@
         + [scratch(2 * own, wide, wide, kind=bf16)] * 2
         + [scratch(z.orbitals * half, 3 * own * n, kind=bf16)] * 2
         + [pltpu.SemaphoreType.DMA((19 + -(-fits // 256),))],
-        limit=60,
+        limit=44,
         out_specs=[hbm, hbm],
     )
     return (amplitudes, gradient)

time: 63.2 us -> 74.7 us (1.18)
  the two profiles are of different devices: /device:TPU:0 before, /device:TPU:29 now
where the time goes in v17:
time: 74.7 us; the launch traced here: 74.3 us
  starting transfers between devices  36.7 us (49%)
  Pallas kernels  16.6 us (22%)
  waiting for transfers between devices  16.5 us (22%)
  local copies, waits for them, and re-layouts  3.63 us (5%)
  between operations  0.79 us (1%)
    ppermute x11, starting transfers between devices, swapped(): return lax.ppermute(value, axis, [(0, 1), (1, 0)])  19.4 us
    pallas_call x7, Pallas kernels, call(): pl.pallas_call(kernel, out_shape=[jax.ShapeDtypeStruct(shape, jnp.float32...  16.6 us
    ppermute x3, starting transfers between devices, shifted(): lax.ppermute(value, axis, [(source, source + steps) for source in range(i...  6.31 us
    all_to_all x1, waiting for transfers between devices, body(): packs = [lax.all_to_all(pack, 'orb', 0, 0)]  5.65 us
    all_to_all x1, starting transfers between devices, body(): lax.all_to_all(jnp.broadcast_to(sums[None], (z.owners, *sums.shape)), 'or...  5.56 us
    all_to_all x1, starting transfers between devices, body(): packs = [lax.all_to_all(pack, 'orb', 0, 0)]  5.35 us
    ppermute x3, waiting for transfers between devices, shifted(): lax.ppermute(value, axis, [(source, source + steps) for source in range(i...  5.03 us
    ppermute x11, waiting for transfers between devices, swapped(): return lax.ppermute(value, axis, [(0, 1), (1, 0)])  4.32 us
  transfers between devices with their start and end apart: 16, of which 7 were waited for; matrix products, arithmetic and copies ran while one was open for 1% of the time, Pallas kernels for 6%

profile of v17, /device:TPU:29, one launch (start us, length us, event | category | flops | bytes accessed | tf_op | source)
XLA Modules:
  0.0 74.3 jit_solution(12656003911992000149)
XLA Ops:
  0.6 1.9 %shard_map.122.mp_in.mp_ref.refs_8_ = f32[2,72,256]{2,1,0:T(8,128)} custom-call(f32[2,64,256]{2,1,0:T(8,128)} %refs_6_.1, s32[2,256]{1,0:T(2,128)} %map_in.1, f32[2,64]{1,0:T(2,128)} %e_in.1, f32[2,4]{1,0:T(2,128)} %coupling_in.1), custom_call_target="tpu_custom_call" | custom-call | tf_op jit(solution)/shard_map/pallas_call | solution.py:58
  2.5 1.3 %collective-permute-start = (f32[2,72,256]{2,1,0:T(8,128)}, f32[2,72,256]{2,1,0:T(8,128)S(1)}, u32[]{:S(2)}, u32[]{:S(2)}) collective-permute-start(f32[2,72,256]{2,1,0:T(8,128)} %shard_map.122.mp_in.mp_ref.refs_8_), channel_id=1, source_target_pairs={{0,4},{4,8},{8,12},{1,5},{5,9},{9,13},{2,6},{6,10},{10,14},{3,7},{... | collective-permute-start | bytes 442376 | tf_op jit(solution)/shard_map/ppermute | solution.py:30
  3.8 1.7 %shard_map.123 = f32[4,136,128]{2,1,0:T(8,128)} custom-call(f32[2,4,4096]{2,1,0:T(4,128)} %s_in.1, f32[2,72,256]{2,1,0:T(8,128)} %shard_map.122.mp_in.mp_ref.refs_8_), custom_call_target="tpu_custom_call" | custom-call | tf_op jit(solution)/shard_map/pallas_call | solution.py:58
  5.5 0.7 slice_bitcast_fusion.mp_ref
  6.2 1.6 %copy-done = f32[2,256,1024]{2,1,0:T(8,128)S(1)} copy-done((f32[2,256,1024]{2,1,0:T(8,128)S(1)}, f32[2,256,1024]{2,1,0:T(8,128)}, u32[]{:S(2)}) %copy-start) | copy-done | bytes 2097176
  7.8 0.7 copy-done.4
  8.5 0.5 shard_map.124.touched
  9.0 0.0 copy-start.5
  9.0 0.0 copy-start.8
  9.1 0.0 copy-start.9
  9.1 0.3 collective-permute-done.mp_below.refs_10_
  9.4 1.3 %shard_map.125 = f32[2,64,1024]{2,1,0:T(8,128)S(1)} custom-call(s32[16]{0:T(128)S(1)} %copy-done.4, f32[2,72,256]{2,1,0:T(8,128)S(1)} %collective-permute-done.mp_below.refs_10_, f32[2,256,1024]{2,1,0:T(8,128)S(1)} %copy-done, f32[8,128]{1,0:T(8,128)S(1)} %shard_map.124.touched), custom_call_target="tpu_custom_call" | custom-call | tf_op jit(solution)/shard_map/pallas_call | solution.py:58
  10.7 0.0 copy-start.7
  10.7 3.7 %collective-permute-start.1 = (f32[2,64,1024]{2,1,0:T(8,128)S(1)}, f32[2,64,1024]{2,1,0:T(8,128)S(1)}, u32[]{:S(2)}, u32[]{:S(2)}) collective-permute-start(f32[2,64,1024]{2,1,0:T(8,128)S(1)} %shard_map.125), channel_id=1, source_target_pairs={{4,0},{8,4},{12,8},{5,1},{9,5},{13,9},{6,2},{10,6},{14,10},{7,3},{... | collective-permute-start | bytes 1572872 | tf_op jit(solution)/shard_map/ppermute | solution.py:30
  14.5 2.0 %shard_map.126 = (f32[2,64,1024]{2,1,0:T(8,128)S(1)}, f32[2,64,1024]{2,1,0:T(8,128)S(1)}) custom-call(s32[16]{0:T(128)S(1)} %copy-done.6, s32[16]{0:T(128)S(1)} %copy-done.4, f32[2,64,256]{2,1,0:T(8,128)S(1)} %copy-done.3, f32[2,72,256]{2,1,0:T(8,128)S(1)} %copy-done.2, f32[2,256,1024]{2,1,0:T(8,128)S(1)} %copy-done.1), custom_call_target="tpu_custom_call" | custom-call | flops 1 | bytes 1 | tf_op jit(solution)/shard_map/pallas_call | solution.py:58
  16.5 1.3 %collective-permute-start.3 = (f32[2,64,1024]{2,1,0:T(8,128)S(1)}, f32[2,64,1024]{2,1,0:T(8,128)S(1)}, u32[]{:S(2)}, u32[]{:S(2)}) collective-permute-start(f32[2,64,1024]{2,1,0:T(8,128)S(1)} %get-tuple-element.30.left_ref.refs_12_), channel_id=1, source_target_pairs={{0,1},{1,0},{2,3},{3,2},{4,5},{5,4},{6,7},{7,6},{8,9},{9,8},{10,11... | collective-permute-start | bytes 1572872 | tf_op jit(solution)/shard_map/ppermute | solution.py:34
  17.8 0.1 collective-permute-start.5
  17.9 0.4 collective-permute-start.2
  18.3 0.1 collective-permute-start.4
  18.4 1.6 %collective-permute-done.4.refs_7_ = f32[2,64,256]{2,1,0:T(8,128)S(1)} collective-permute-done((f32[2,64,256]{2,1,0:T(8,128)S(1)}, f32[2,64,256]{2,1,0:T(8,128)S(1)}, u32[]{:S(2)}, u32[]{:S(2)}) %collective-permute-start.4) | collective-permute-done | bytes 131104 | tf_op jit(solution)/shard_map/ppermute | solution.py:34
  19.9 0.0 collective-permute-done.5.refs_11_
  19.9 0.0 collective-permute-done.2.refs_9_
  19.9 4.7 %collective-permute-done.1.down_ref = f32[2,64,1024]{2,1,0:T(8,128)S(1)} collective-permute-done((f32[2,64,1024]{2,1,0:T(8,128)S(1)}, f32[2,64,1024]{2,1,0:T(8,128)S(1)}, u32[]{:S(2)}, u32[]{:S(2)}) %collective-permute-start.1) | collective-permute-done | bytes 524320 | tf_op jit(solution)/shard_map/ppermute | solution.py:30
  24.7 0.0 collective-permute-done.3.refs_13_
  24.7 0.0 copy-done.8
  24.7 1.0 %shard_map.127 = (f32[64,128]{1,0:T(8,128)S(1)}, f32[2,64,1024]{2,1,0:T(8,128)S(1)}) custom-call(s32[16]{0:T(128)S(1)} %copy-done.6, s32[16]{0:T(128)S(1)} %copy-done.5, s32[16]{0:T(128)S(1)} %copy-done.8, f32[8]{0:T(128)S(1)} %copy-done.9, f32[2,72,256]{2,1,0:T(8,128)S(1)} %copy-done.2, f32[2,64,1024]{2,1,0:T(8,128)S(1)} %get-tuple-element.30.left_ref.refs_12_, ...), custom_call_target="tpu_custom_call" | custom-call | tf_op jit(solution)/shard_map/pallas_call | solution.py:58
  25.7 1.3 %collective-permute-start.6 = (f32[64,128]{1,0:T(8,128)S(1)}, f32[64,128]{1,0:T(8,128)S(1)}, u32[]{:S(2)}, u32[]{:S(2)}) collective-permute-start(f32[64,128]{1,0:T(8,128)S(1)} %get-tuple-element.27), channel_id=1, source_target_pairs={{0,2},{2,0},{1,3},{3,1},{4,6},{6,4},{5,7},{7,5},{8,10},{10,8},{9,1... | collective-permute-start | bytes 98312 | tf_op jit(solution)/shard_map/ppermute | solution.py:34
  27.0 1.6 %collective-permute-done.6 = f32[64,128]{1,0:T(8,128)S(1)} collective-permute-done((f32[64,128]{1,0:T(8,128)S(1)}, f32[64,128]{1,0:T(8,128)S(1)}, u32[]{:S(2)}, u32[]{:S(2)}) %collective-permute-start.6) | collective-permute-done | bytes 32800 | tf_op jit(solution)/shard_map/ppermute | solution.py:34
  28.5 0.7 broadcast_in_dim.2
  29.2 5.6 %all-to-all-start = ((f32[4,64,128]{2,1,0:T(8,128)}), f32[4,64,128]{2,1,0:T(8,128)S(1)}, u32[]{:S(2)}, u32[]{:S(2)}) async-start(f32[4,64,128]{2,1,0:T(8,128)} %broadcast_in_dim.2), calls=%async_computation | async-start | bytes 262144 | tf_op jit(solution)/shard_map/all_to_all | solution.py:512
  34.7 1.3 %collective-permute-start.11 = (f32[2,64,1024]{2,1,0:T(8,128)S(1)}, f32[2,64,1024]{2,1,0:T(8,128)S(1)}, u32[]{:S(2)}, u32[]{:S(2)}) collective-permute-start(f32[2,64,1024]{2,1,0:T(8,128)S(1)} %get-tuple-element.30.left_ref.refs_12_), channel_id=1, source_target_pairs={{0,4},{4,8},{8,12},{1,5},{5,9},{9,13},{2,6},{6,10},{10,14},{3,7},{... | collective-permute-start | bytes 1572872 | tf_op jit(solution)/shard_map/ppermute | solution.py:30
  36.0 1.6 %all-to-all-done.refs_0_ = f32[4,64,128]{2,1,0:T(8,128)S(1)} async-done(((f32[4,64,128]{2,1,0:T(8,128)}), f32[4,64,128]{2,1,0:T(8,128)S(1)}, u32[]{:S(2)}, u32[]{:S(2)}) %all-to-all-start) | async-done | bytes 131104 | tf_op jit(solution)/shard_map/all_to_all | solution.py:512
  37.6 5.4 %all-to-all-start.1 = ((f32[4,136,128]{2,1,0:T(8,128)}), f32[4,136,128]{2,1,0:T(8,128)S(1)}, u32[]{:S(2)}, u32[]{:S(2)}) async-start(f32[4,136,128]{2,1,0:T(8,128)} %shard_map.123), calls=%async_computation.1 | async-start | bytes 557056 | tf_op jit(solution)/shard_map/all_to_all | solution.py:465
  42.9 4.9 %collective-permute-start.7 = (f32[4,64,128]{2,1,0:T(8,128)S(1)}, f32[4,64,128]{2,1,0:T(8,128)S(1)}, u32[]{:S(2)}, u32[]{:S(2)}) collective-permute-start(f32[4,64,128]{2,1,0:T(8,128)S(1)} %all-to-all-done.refs_0_), channel_id=1, source_target_pairs={{0,1},{1,0},{2,3},{3,2},{4,5},{5,4},{6,7},{7,6},{8,9},{9,8},{10,11... | collective-permute-start | bytes 393224 | tf_op jit(solution)/shard_map/ppermute | solution.py:34
  47.8 5.7 %all-to-all-done.1.refs_2_ = f32[4,136,128]{2,1,0:T(8,128)S(1)} async-done(((f32[4,136,128]{2,1,0:T(8,128)}), f32[4,136,128]{2,1,0:T(8,128)S(1)}, u32[]{:S(2)}, u32[]{:S(2)}) %all-to-all-start.1) | async-done | bytes 278560 | tf_op jit(solution)/shard_map/all_to_all | solution.py:465
  53.5 1.2 %collective-permute-start.8 = (f32[4,136,128]{2,1,0:T(8,128)S(1)}, f32[4,136,128]{2,1,0:T(8,128)S(1)}, u32[]{:S(2)}, u32[]{:S(2)}) collective-permute-start(f32[4,136,128]{2,1,0:T(8,128)S(1)} %all-to-all-done.1.refs_2_), channel_id=1, source_target_pairs={{0,2},{2,0},{1,3},{3,1},{4,6},{6,4},{5,7},{7,5},{8,10},{10,8},{9,1... | collective-permute-start | bytes 835592 | tf_op jit(solution)/shard_map/ppermute | solution.py:34
  54.7 5.2 %collective-permute-start.13 = (f32[2,64,1024]{2,1,0:T(8,128)S(1)}, f32[2,64,1024]{2,1,0:T(8,128)S(1)}, u32[]{:S(2)}, u32[]{:S(2)}) collective-permute-start(f32[2,64,1024]{2,1,0:T(8,128)S(1)} %get-tuple-element.33.refs_16_), channel_id=1, source_target_pairs={{0,1},{1,0},{2,3},{3,2},{4,5},{5,4},{6,7},{7,6},{8,9},{9,8},{10,11... | collective-permute-start | bytes 1572872 | tf_op jit(solution)/shard_map/ppermute | solution.py:34
  59.8 0.0 collective-permute-done.7.refs_1_
  59.8 0.0 collective-permute-done.11.refs_14_
  59.8 0.1 collective-permute-start.12
  59.9 0.4 collective-permute-start.9
  60.3 0.0 collective-permute-done.8.refs_3_
  60.3 4.5 %collective-permute-start.10 = (f32[4,136,128]{2,1,0:T(8,128)S(1)}, f32[4,136,128]{2,1,0:T(8,128)S(1)}, u32[]{:S(2)}, u32[]{:S(2)}) collective-permute-start(f32[4,136,128]{2,1,0:T(8,128)S(1)} %collective-permute-done.8.refs_3_), channel_id=1, source_target_pairs={{0,1},{1,0},{2,3},{3,2},{4,5},{5,4},{6,7},{7,6},{8,9},{9,8},{10,11... | collective-permute-start | bytes 835592 | tf_op jit(solution)/shard_map/ppermute | solution.py:34
  64.9 0.0 collective-permute-done.9.refs_4_
  64.9 0.0 collective-permute-done.13.refs_17_
  64.9 1.2 %collective-permute-done.10.refs_5_ = f32[4,136,128]{2,1,0:T(8,128)S(1)} collective-permute-done((f32[4,136,128]{2,1,0:T(8,128)S(1)}, f32[4,136,128]{2,1,0:T(8,128)S(1)}, u32[]{:S(2)}, u32[]{:S(2)}) %collective-permute-start.10) | collective-permute-done | bytes 278560 | tf_op jit(solution)/shard_map/ppermute | solution.py:34
  66.1 0.0 collective-permute-done.12.refs_15_
  66.1 8.2 %shard_map.128 = (f32[2,4096]{1,0:T(2,128)}, f32[2,128,1024]{2,1,0:T(8,128)}) custom-call(s32[16]{0:T(128)S(1)} %copy-done.6, s32[16]{0:T(128)S(1)} %copy-done.5, s32[16]{0:T(128)S(1)} %copy-done.8, s32[4,16]{1,0:T(4,128)S(1)} %bitcast.3, f32[8]{0:T(128)S(1)} %copy-done.9, f32[4,64,128]{2,1,0:T(8,128)S(1)} %all-to-all-done.refs_0_, ...), custom_call_target="tpu_custom_call" | custom-call | tf_op jit(solution)/shard_map/pallas_call | solution.py:58
  (14 shorter events, 0.0 us)
Async XLA Ops:
  2.5 6.8 %collective-permute-start = (f32[2,72,256]{2,1,0:T(8,128)}, f32[2,72,256]{2,1,0:T(8,128)S(1)}, u32[]{:S(2)}, u32[]{:S(2)}) collective-permute-start(f32[2,72,256]{2,1,0:T(8,128)} %shard_map.122.mp_in.mp_ref.refs_8_), channel_id=1, source_target_pairs={{0,4},{4,8},{8,12},{1,5},{5,9},{9,13},{2,6},{6,10},{10,14},{3,7},{... | collective-permute-start | bytes 442376 | tf_op jit(solution)/shard_map/ppermute | solution.py:30
  6.2 1.6 %copy-start = (f32[2,256,1024]{2,1,0:T(8,128)S(1)}, f32[2,256,1024]{2,1,0:T(8,128)}, u32[]{:S(2)}) copy-start(f32[2,256,1024]{2,1,0:T(8,128)} %b_ref.5) | copy-start | bytes 6291460
  7.8 0.7 copy-start.4
  8.5 6.0 %copy-start.1 = (f32[2,256,1024]{2,1,0:T(8,128)S(1)}, f32[2,256,1024]{2,1,0:T(8,128)}, u32[]{:S(2)}) copy-start(f32[2,256,1024]{2,1,0:T(8,128)} %b_ref.5) | copy-start | bytes 6291460
  8.5 6.0 %copy-start.2 = (f32[2,72,256]{2,1,0:T(8,128)S(1)}, f32[2,72,256]{2,1,0:T(8,128)}, u32[]{:S(2)}) copy-start(f32[2,72,256]{2,1,0:T(8,128)} %shard_map.122.mp_in.mp_ref.refs_8_) | copy-start | bytes 442372
  8.5 6.0 %copy-start.3 = (f32[2,64,256]{2,1,0:T(8,128)S(1)}, f32[2,64,256]{2,1,0:T(8,128)}, u32[]{:S(2)}) copy-start(f32[2,64,256]{2,1,0:T(8,128)} %refs_6_.1) | copy-start | bytes 393220
  8.5 6.0 %copy-start.6 = (s32[16]{0:T(128)S(1)}, s32[16]{0:T(128)}, u32[]{:S(2)}) copy-start(s32[16]{0:T(128)} %first.5) | copy-start | bytes 196
  9.0 15.6 %copy-start.5 = (s32[16]{0:T(128)S(1)}, s32[16]{0:T(128)}, u32[]{:S(2)}) copy-start(s32[16]{0:T(128)} %second.9) | copy-start | bytes 196
  9.0 15.6 %copy-start.8 = (s32[16]{0:T(128)S(1)}, s32[16]{0:T(128)}, u32[]{:S(2)}) copy-start(s32[16]{0:T(128)} %ranks.3) | copy-start | bytes 196
  9.1 15.6 %copy-start.9 = (f32[8]{0:T(128)S(1)}, f32[8]{0:T(128)}, u32[]{:S(2)}) copy-start(f32[8]{0:T(128)} %occupied.3) | copy-start | bytes 100
  10.7 55.4 %copy-start.7 = (s32[16,4]{0,1:T(4,128)S(1)}, s32[16,4]{0,1:T(4,128)}, u32[]{:S(2)}) copy-start(s32[16,4]{0,1:T(4,128)} %param.17) | copy-start | bytes 772
  10.7 14.0 %collective-permute-start.1 = (f32[2,64,1024]{2,1,0:T(8,128)S(1)}, f32[2,64,1024]{2,1,0:T(8,128)S(1)}, u32[]{:S(2)}, u32[]{:S(2)}) collective-permute-start(f32[2,64,1024]{2,1,0:T(8,128)S(1)} %shard_map.125), channel_id=1, source_target_pairs={{4,0},{8,4},{12,8},{5,1},{9,5},{13,9},{6,2},{10,6},{14,10},{7,3},{... | collective-permute-start | bytes 1572872 | tf_op jit(solution)/shard_map/ppermute | solution.py:30
  16.5 8.2 %collective-permute-start.3 = (f32[2,64,1024]{2,1,0:T(8,128)S(1)}, f32[2,64,1024]{2,1,0:T(8,128)S(1)}, u32[]{:S(2)}, u32[]{:S(2)}) collective-permute-start(f32[2,64,1024]{2,1,0:T(8,128)S(1)} %get-tuple-element.30.left_ref.refs_12_), channel_id=1, source_target_pairs={{0,1},{1,0},{2,3},{3,2},{4,5},{5,4},{6,7},{7,6},{8,9},{9,8},{10,11... | collective-permute-start | bytes 1572872 | tf_op jit(solution)/shard_map/ppermute | solution.py:34
  17.8 2.1 %collective-permute-start.5 = (f32[2,72,256]{2,1,0:T(8,128)S(1)}, f32[2,72,256]{2,1,0:T(8,128)S(1)}, u32[]{:S(2)}, u32[]{:S(2)}) collective-permute-start(f32[2,72,256]{2,1,0:T(8,128)S(1)} %collective-permute-done.mp_below.refs_10_), channel_id=1, source_target_pairs={{0,1},{1,0},{2,3},{3,2},{4,5},{5,4},{6,7},{7,6},{8,9},{9,8},{10,11... | collective-permute-start | bytes 442376 | tf_op jit(solution)/shard_map/ppermute | solution.py:34
  17.9 2.1 %collective-permute-start.2 = (f32[2,72,256]{2,1,0:T(8,128)S(1)}, f32[2,72,256]{2,1,0:T(8,128)S(1)}, u32[]{:S(2)}, u32[]{:S(2)}) collective-permute-start(f32[2,72,256]{2,1,0:T(8,128)S(1)} %copy-done.2), channel_id=1, source_target_pairs={{0,1},{1,0},{2,3},{3,2},{4,5},{5,4},{6,7},{7,6},{8,9},{9,8},{10,11... | collective-permute-start | bytes 442376 | tf_op jit(solution)/shard_map/ppermute | solution.py:34
  18.3 1.6 %collective-permute-start.4 = (f32[2,64,256]{2,1,0:T(8,128)S(1)}, f32[2,64,256]{2,1,0:T(8,128)S(1)}, u32[]{:S(2)}, u32[]{:S(2)}) collective-permute-start(f32[2,64,256]{2,1,0:T(8,128)S(1)} %copy-done.3), channel_id=1, source_target_pairs={{0,1},{1,0},{2,3},{3,2},{4,5},{5,4},{6,7},{7,6},{8,9},{9,8},{10,11... | collective-permute-start | bytes 393224 | tf_op jit(solution)/shard_map/ppermute | solution.py:34
  25.7 2.8 %collective-permute-start.6 = (f32[64,128]{1,0:T(8,128)S(1)}, f32[64,128]{1,0:T(8,128)S(1)}, u32[]{:S(2)}, u32[]{:S(2)}) collective-permute-start(f32[64,128]{1,0:T(8,128)S(1)} %get-tuple-element.27), channel_id=1, source_target_pairs={{0,2},{2,0},{1,3},{3,1},{4,6},{6,4},{5,7},{7,5},{8,10},{10,8},{9,1... | collective-permute-start | bytes 98312 | tf_op jit(solution)/shard_map/ppermute | solution.py:34
  29.2 8.4 %all-to-all-start = ((f32[4,64,128]{2,1,0:T(8,128)}), f32[4,64,128]{2,1,0:T(8,128)S(1)}, u32[]{:S(2)}, u32[]{:S(2)}) async-start(f32[4,64,128]{2,1,0:T(8,128)} %broadcast_in_dim.2), calls=%async_computation | async-start | bytes 262144 | tf_op jit(solution)/shard_map/all_to_all | solution.py:512
  34.7 25.1 %collective-permute-start.11 = (f32[2,64,1024]{2,1,0:T(8,128)S(1)}, f32[2,64,1024]{2,1,0:T(8,128)S(1)}, u32[]{:S(2)}, u32[]{:S(2)}) collective-permute-start(f32[2,64,1024]{2,1,0:T(8,128)S(1)} %get-tuple-element.30.left_ref.refs_12_), channel_id=1, source_target_pairs={{0,4},{4,8},{8,12},{1,5},{5,9},{9,13},{2,6},{6,10},{10,14},{3,7},{... | collective-permute-start | bytes 1572872 | tf_op jit(solution)/shard_map/ppermute | solution.py:30
  37.6 15.9 %all-to-all-start.1 = ((f32[4,136,128]{2,1,0:T(8,128)}), f32[4,136,128]{2,1,0:T(8,128)S(1)}, u32[]{:S(2)}, u32[]{:S(2)}) async-start(f32[4,136,128]{2,1,0:T(8,128)} %shard_map.123), calls=%async_computation.1 | async-start | bytes 557056 | tf_op jit(solution)/shard_map/all_to_all | solution.py:465
  42.9 16.9 %collective-permute-start.7 = (f32[4,64,128]{2,1,0:T(8,128)S(1)}, f32[4,64,128]{2,1,0:T(8,128)S(1)}, u32[]{:S(2)}, u32[]{:S(2)}) collective-permute-start(f32[4,64,128]{2,1,0:T(8,128)S(1)} %all-to-all-done.refs_0_), channel_id=1, source_target_pairs={{0,1},{1,0},{2,3},{3,2},{4,5},{5,4},{6,7},{7,6},{8,9},{9,8},{10,11... | collective-permute-start | bytes 393224 | tf_op jit(solution)/shard_map/ppermute | solution.py:34
  53.5 6.9 %collective-permute-start.8 = (f32[4,136,128]{2,1,0:T(8,128)S(1)}, f32[4,136,128]{2,1,0:T(8,128)S(1)}, u32[]{:S(2)}, u32[]{:S(2)}) collective-permute-start(f32[4,136,128]{2,1,0:T(8,128)S(1)} %all-to-all-done.1.refs_2_), channel_id=1, source_target_pairs={{0,2},{2,0},{1,3},{3,1},{4,6},{6,4},{5,7},{7,5},{8,10},{10,8},{9,1... | collective-permute-start | bytes 835592 | tf_op jit(solution)/shard_map/ppermute | solution.py:34
  54.7 10.2 %collective-permute-start.13 = (f32[2,64,1024]{2,1,0:T(8,128)S(1)}, f32[2,64,1024]{2,1,0:T(8,128)S(1)}, u32[]{:S(2)}, u32[]{:S(2)}) collective-permute-start(f32[2,64,1024]{2,1,0:T(8,128)S(1)} %get-tuple-element.33.refs_16_), channel_id=1, source_target_pairs={{0,1},{1,0},{2,3},{3,2},{4,5},{5,4},{6,7},{7,6},{8,9},{9,8},{10,11... | collective-permute-start | bytes 1572872 | tf_op jit(solution)/shard_map/ppermute | solution.py:34
  59.8 6.2 %collective-permute-start.12 = (f32[2,64,1024]{2,1,0:T(8,128)S(1)}, f32[2,64,1024]{2,1,0:T(8,128)S(1)}, u32[]{:S(2)}, u32[]{:S(2)}) collective-permute-start(f32[2,64,1024]{2,1,0:T(8,128)S(1)} %collective-permute-done.11.refs_14_), channel_id=1, source_target_pairs={{0,1},{1,0},{2,3},{3,2},{4,5},{5,4},{6,7},{7,6},{8,9},{9,8},{10,11... | collective-permute-start | bytes 1572872 | tf_op jit(solution)/shard_map/ppermute | solution.py:34
  59.9 5.0 %collective-permute-start.9 = (f32[4,136,128]{2,1,0:T(8,128)S(1)}, f32[4,136,128]{2,1,0:T(8,128)S(1)}, u32[]{:S(2)}, u32[]{:S(2)}) collective-permute-start(f32[4,136,128]{2,1,0:T(8,128)S(1)} %all-to-all-done.1.refs_2_), channel_id=1, source_target_pairs={{0,1},{1,0},{2,3},{3,2},{4,5},{5,4},{6,7},{7,6},{8,9},{9,8},{10,11... | collective-permute-start | bytes 835592 | tf_op jit(solution)/shard_map/ppermute | solution.py:34
  60.3 5.7 %collective-permute-start.10 = (f32[4,136,128]{2,1,0:T(8,128)S(1)}, f32[4,136,128]{2,1,0:T(8,128)S(1)}, u32[]{:S(2)}, u32[]{:S(2)}) collective-permute-start(f32[4,136,128]{2,1,0:T(8,128)S(1)} %collective-permute-done.8.refs_3_), channel_id=1, source_target_pairs={{0,1},{1,0},{2,3},{3,2},{4,5},{5,4},{6,7},{7,6},{8,9},{9,8},{10,11... | collective-permute-start | bytes 835592 | tf_op jit(solution)/shard_map/ppermute | solution.py:34

commit v18 on v17

--- a/solution.py
+++ b/solution.py
@@ -519,7 +519,7 @@
 
     (right_late,) = gate((right,), part)
     left_below = shifted(gate((left,), part)[0], "orb", 1)
-    (left_late,) = gate((left_below,), start_amps[-1])
+    (left_late,) = gate((left_below,), start_amps[0])
     right_other, left_below_other = [
         swapped(value, "sub") for value in (right_late, left_late)
     ]

time: 74.7 us -> 63 us (0.84)
  the two profiles are of different devices: /device:TPU:29 before, /device:TPU:0 now
where the time goes in v18:
time: 63 us; the launch traced here: 62.4 us
  starting transfers between devices  25.6 us (41%)
  Pallas kernels  16.8 us (27%)
  waiting for transfers between devices  14.6 us (23%)
  local copies, waits for them, and re-layouts  4.55 us (7%)
  between operations  0.84 us (1%)
    pallas_call x7, Pallas kernels, call(): pl.pallas_call(kernel, out_shape=[jax.ShapeDtypeStruct(shape, jnp.float32...  16.8 us
    ppermute x3, starting transfers between devices, shifted(): lax.ppermute(value, axis, [(source, source + steps) for source in range(i...  11.1 us
    all_to_all x1, starting transfers between devices, body(): packs = [lax.all_to_all(pack, 'orb', 0, 0)]  5.97 us
    ppermute x3, waiting for transfers between devices, shifted(): lax.ppermute(value, axis, [(source, source + steps) for source in range(i...  5.8 us
    ppermute x11, starting transfers between devices, swapped(): return lax.ppermute(value, axis, [(0, 1), (1, 0)])  5.21 us
    ppermute x11, waiting for transfers between devices, swapped(): return lax.ppermute(value, axis, [(0, 1), (1, 0)])  4.52 us
    all_to_all x1, waiting for transfers between devices, body(): lax.all_to_all(jnp.broadcast_to(sums[None], (z.owners, *sums.shape)), 'or...  4.33 us
    all_to_all x1, starting transfers between devices, body(): lax.all_to_all(jnp.broadcast_to(sums[None], (z.owners, *sums.shape)), 'or...  3.33 us
  transfers between devices with their start and end apart: 16, of which 7 were waited for; matrix products, arithmetic and copies ran while one was open for 2% of the time, Pallas kernels for 8%

profile of v18, /device:TPU:0, one launch (start us, length us, event | category | flops | bytes accessed | tf_op | source)
XLA Modules:
  0.0 62.4 jit_solution(13146945940851691454)
XLA Ops:
  0.6 1.9 %shard_map.122.mp_in.mp_ref.refs_8_ = f32[2,72,256]{2,1,0:T(8,128)} custom-call(f32[2,64,256]{2,1,0:T(8,128)} %refs_6_.1, s32[2,256]{1,0:T(2,128)} %map_in.1, f32[2,64]{1,0:T(2,128)} %e_in.1, f32[2,4]{1,0:T(2,128)} %coupling_in.1), custom_call_target="tpu_custom_call" | custom-call | tf_op jit(solution)/shard_map/pallas_call | solution.py:58
  2.5 4.9 %collective-permute-start = (f32[2,72,256]{2,1,0:T(8,128)}, f32[2,72,256]{2,1,0:T(8,128)S(1)}, u32[]{:S(2)}, u32[]{:S(2)}) collective-permute-start(f32[2,72,256]{2,1,0:T(8,128)} %shard_map.122.mp_in.mp_ref.refs_8_), channel_id=1, source_target_pairs={{0,4},{4,8},{8,12},{1,5},{5,9},{9,13},{2,6},{6,10},{10,14},{3,7},{... | collective-permute-start | bytes 442376 | tf_op jit(solution)/shard_map/ppermute | solution.py:30
  7.5 1.7 %shard_map.123 = f32[4,136,128]{2,1,0:T(8,128)} custom-call(f32[2,4,4096]{2,1,0:T(4,128)} %s_in.1, f32[2,72,256]{2,1,0:T(8,128)} %shard_map.122.mp_in.mp_ref.refs_8_), custom_call_target="tpu_custom_call" | custom-call | tf_op jit(solution)/shard_map/pallas_call | solution.py:58
  9.2 0.7 %slice_bitcast_fusion.mp_ref = f32[8,128]{1,0:T(8,128)S(1)} fusion(f32[2,72,256]{2,1,0:T(8,128)} %shard_map.122.mp_in.mp_ref.refs_8_), kind=kLoop, calls=%fused_computation | loop fusion | bytes 8192 | tf_op jit(solution)/shard_map/squeeze | solution.py:472
  9.9 1.6 %copy-done = f32[2,256,1024]{2,1,0:T(8,128)S(1)} copy-done((f32[2,256,1024]{2,1,0:T(8,128)S(1)}, f32[2,256,1024]{2,1,0:T(8,128)}, u32[]{:S(2)}) %copy-start) | copy-done | bytes 2097176
  11.5 0.7 %copy-done.6 = s32[16]{0:T(128)S(1)} copy-done((s32[16]{0:T(128)S(1)}, s32[16]{0:T(128)}, u32[]{:S(2)}) %copy-start.6) | copy-done | bytes 88
  12.1 0.5 shard_map.124.touched
  12.7 0.0 collective-permute-done.mp_below.refs_10_
  12.7 1.3 %shard_map.125 = f32[2,64,1024]{2,1,0:T(8,128)S(1)} custom-call(s32[16]{0:T(128)S(1)} %copy-done.6, f32[2,72,256]{2,1,0:T(8,128)S(1)} %collective-permute-done.mp_below.refs_10_, f32[2,256,1024]{2,1,0:T(8,128)S(1)} %copy-done, f32[8,128]{1,0:T(8,128)S(1)} %shard_map.124.touched), custom_call_target="tpu_custom_call" | custom-call | tf_op jit(solution)/shard_map/pallas_call | solution.py:58
  14.0 0.0 copy-start.7
  14.0 0.0 copy-start.10
  14.0 0.0 copy-start.11
  14.1 0.0 copy-start.9
  14.1 1.4 %collective-permute-start.1 = (f32[2,64,1024]{2,1,0:T(8,128)S(1)}, f32[2,64,1024]{2,1,0:T(8,128)S(1)}, u32[]{:S(2)}, u32[]{:S(2)}) collective-permute-start(f32[2,64,1024]{2,1,0:T(8,128)S(1)} %shard_map.125), channel_id=1, source_target_pairs={{4,0},{8,4},{12,8},{5,1},{9,5},{13,9},{6,2},{10,6},{14,10},{7,3},{... | collective-permute-start | bytes 1572872 | tf_op jit(solution)/shard_map/ppermute | solution.py:30
  15.5 2.0 %shard_map.126 = (f32[2,64,1024]{2,1,0:T(8,128)S(1)}, f32[2,64,1024]{2,1,0:T(8,128)S(1)}) custom-call(s32[16]{0:T(128)S(1)} %copy-done.8, s32[16]{0:T(128)S(1)} %copy-done.6, f32[2,64,256]{2,1,0:T(8,128)S(1)} %copy-done.3, f32[2,72,256]{2,1,0:T(8,128)S(1)} %copy-done.2, f32[2,256,1024]{2,1,0:T(8,128)S(1)} %copy-done.1), custom_call_target="tpu_custom_call" | custom-call | flops 1 | bytes 1 | tf_op jit(solution)/shard_map/pallas_call | solution.py:58
  17.5 0.1 collective-permute-start.3
  17.6 0.5 collective-permute-start.5
  18.1 0.1 collective-permute-start.2
  18.2 0.4 collective-permute-start.4
  18.6 6.0 %all-to-all-start.1 = ((f32[4,136,128]{2,1,0:T(8,128)}), f32[4,136,128]{2,1,0:T(8,128)S(1)}, u32[]{:S(2)}, u32[]{:S(2)}) async-start(f32[4,136,128]{2,1,0:T(8,128)} %shard_map.123), calls=%async_computation.1 | async-start | bytes 557056 | tf_op jit(solution)/shard_map/all_to_all | solution.py:465
  24.6 0.0 collective-permute-done.4.refs_7_
  24.6 0.0 collective-permute-done.5.refs_11_
  24.6 0.0 collective-permute-done.2.refs_9_
  24.6 5.8 %collective-permute-done.1.down_ref = f32[2,64,1024]{2,1,0:T(8,128)S(1)} collective-permute-done((f32[2,64,1024]{2,1,0:T(8,128)S(1)}, f32[2,64,1024]{2,1,0:T(8,128)S(1)}, u32[]{:S(2)}, u32[]{:S(2)}) %collective-permute-start.1) | collective-permute-done | bytes 524320 | tf_op jit(solution)/shard_map/ppermute | solution.py:30
  30.4 0.0 collective-permute-done.3.refs_13_
  30.4 1.0 %shard_map.127 = (f32[64,128]{1,0:T(8,128)S(1)}, f32[2,64,1024]{2,1,0:T(8,128)S(1)}) custom-call(s32[16]{0:T(128)S(1)} %copy-done.8, s32[16]{0:T(128)S(1)} %copy-done.7, s32[16]{0:T(128)S(1)} %copy-done.10, f32[8]{0:T(128)S(1)} %copy-done.11, f32[2,72,256]{2,1,0:T(8,128)S(1)} %copy-done.2, f32[2,64,1024]{2,1,0:T(8,128)S(1)} %get-tuple-element.30.left_ref.refs_12_, ...), custom_call_target="tpu_custom_call" | custom-call | tf_op jit(solution)/shard_map/pallas_call | solution.py:58
  31.4 4.8 %collective-permute-start.11 = (f32[2,64,1024]{2,1,0:T(8,128)S(1)}, f32[2,64,1024]{2,1,0:T(8,128)S(1)}, u32[]{:S(2)}, u32[]{:S(2)}) collective-permute-start(f32[2,64,1024]{2,1,0:T(8,128)S(1)} %get-tuple-element.30.left_ref.refs_12_), channel_id=1, source_target_pairs={{0,4},{4,8},{8,12},{1,5},{5,9},{9,13},{2,6},{6,10},{10,14},{3,7},{... | collective-permute-start | bytes 1572872 | tf_op jit(solution)/shard_map/ppermute | solution.py:30
  36.2 1.6 %collective-permute-start.6 = (f32[64,128]{1,0:T(8,128)S(1)}, f32[64,128]{1,0:T(8,128)S(1)}, u32[]{:S(2)}, u32[]{:S(2)}) collective-permute-start(f32[64,128]{1,0:T(8,128)S(1)} %get-tuple-element.27), channel_id=1, source_target_pairs={{0,2},{2,0},{1,3},{3,1},{4,6},{6,4},{5,7},{7,5},{8,10},{10,8},{9,1... | collective-permute-start | bytes 98312 | tf_op jit(solution)/shard_map/ppermute | solution.py:34
  37.8 2.4 %collective-permute-done.6 = f32[64,128]{1,0:T(8,128)S(1)} collective-permute-done((f32[64,128]{1,0:T(8,128)S(1)}, f32[64,128]{1,0:T(8,128)S(1)}, u32[]{:S(2)}, u32[]{:S(2)}) %collective-permute-start.6) | collective-permute-done | bytes 32800 | tf_op jit(solution)/shard_map/ppermute | solution.py:34
  40.2 0.0 all-to-all-done.1.refs_2_
  40.2 0.7 %broadcast_in_dim.2 = f32[4,64,128]{2,1,0:T(8,128)} broadcast(f32[64,128]{1,0:T(8,128)S(1)} %add.3), dimensions={1,2} | broadcast | bytes 163840 | tf_op jit(solution)/shard_map/broadcast_in_dim | solution.py:512
  40.9 3.3 %all-to-all-start = ((f32[4,64,128]{2,1,0:T(8,128)}), f32[4,64,128]{2,1,0:T(8,128)S(1)}, u32[]{:S(2)}, u32[]{:S(2)}) async-start(f32[4,64,128]{2,1,0:T(8,128)} %broadcast_in_dim.2), calls=%async_computation | async-start | bytes 262144 | tf_op jit(solution)/shard_map/all_to_all | solution.py:512
  44.2 1.6 %collective-permute-start.8 = (f32[4,136,128]{2,1,0:T(8,128)S(1)}, f32[4,136,128]{2,1,0:T(8,128)}, u32[]{:S(2)}, u32[]{:S(2)}) collective-permute-start(f32[4,136,128]{2,1,0:T(8,128)S(1)} %all-to-all-done.1.refs_2_), channel_id=1, source_target_pairs={{0,2},{2,0},{1,3},{3,1},{4,6},{6,4},{5,7},{7,5},{8,10},{10,8},{9,1... | collective-permute-start | bytes 835592 | tf_op jit(solution)/shard_map/ppermute | solution.py:34
  45.8 0.0 collective-permute-start.13
  45.8 4.3 %all-to-all-done.refs_0_ = f32[4,64,128]{2,1,0:T(8,128)S(1)} async-done(((f32[4,64,128]{2,1,0:T(8,128)}), f32[4,64,128]{2,1,0:T(8,128)S(1)}, u32[]{:S(2)}, u32[]{:S(2)}) %all-to-all-start) | async-done | bytes 131104 | tf_op jit(solution)/shard_map/all_to_all | solution.py:512
  50.1 0.0 collective-permute-done.11.refs_14_
  50.1 0.0 collective-permute-start.12
  50.1 0.5 collective-permute-start.9
  50.6 0.3 collective-permute-done.8.refs_3_
  51.0 0.0 collective-permute-start.10
  51.0 0.5 collective-permute-start.7
  51.5 1.0 %collective-permute-done.9.refs_4_ = f32[4,136,128]{2,1,0:T(8,128)S(1)} collective-permute-done((f32[4,136,128]{2,1,0:T(8,128)S(1)}, f32[4,136,128]{2,1,0:T(8,128)S(1)}, u32[]{:S(2)}, u32[]{:S(2)}) %collective-permute-start.9) | collective-permute-done | bytes 278560 | tf_op jit(solution)/shard_map/ppermute | solution.py:34
  52.4 0.4 collective-permute-done.7.refs_1_
  52.8 0.0 collective-permute-done.13.refs_17_
  52.8 0.4 collective-permute-done.10.refs_5_
  53.2 0.0 collective-permute-done.12.refs_15_
  53.2 0.9 %copy-done.5 = f32[2,72,256]{2,1,0:T(8,128)S(1)} copy-done((f32[2,72,256]{2,1,0:T(8,128)S(1)}, f32[2,72,256]{2,1,0:T(8,128)}, u32[]{:S(2)}) %copy-start.5) | copy-done | bytes 147480
  54.1 8.3 %shard_map.128 = (f32[2,4096]{1,0:T(2,128)}, f32[2,128,1024]{2,1,0:T(8,128)}) custom-call(s32[16]{0:T(128)S(1)} %copy-done.8, s32[16]{0:T(128)S(1)} %copy-done.7, s32[16]{0:T(128)S(1)} %copy-done.10, s32[4,16]{1,0:T(4,128)S(1)} %bitcast.3, f32[8]{0:T(128)S(1)} %copy-done.11, f32[4,64,128]{2,1,0:T(8,128)S(1)} %all-to-all-done.refs_0_, ...), custom_call_target="tpu_custom_call" | custom-call | tf_op jit(solution)/shard_map/pallas_call | solution.py:58
  (18 shorter events, 0.0 us)
Async XLA Ops:
  2.5 10.1 %collective-permute-start = (f32[2,72,256]{2,1,0:T(8,128)}, f32[2,72,256]{2,1,0:T(8,128)S(1)}, u32[]{:S(2)}, u32[]{:S(2)}) collective-permute-start(f32[2,72,256]{2,1,0:T(8,128)} %shard_map.122.mp_in.mp_ref.refs_8_), channel_id=1, source_target_pairs={{0,4},{4,8},{8,12},{1,5},{5,9},{9,13},{2,6},{6,10},{10,14},{3,7},{... | collective-permute-start | bytes 442376 | tf_op jit(solution)/shard_map/ppermute | solution.py:30
  9.9 1.6 %copy-start = (f32[2,256,1024]{2,1,0:T(8,128)S(1)}, f32[2,256,1024]{2,1,0:T(8,128)}, u32[]{:S(2)}) copy-start(f32[2,256,1024]{2,1,0:T(8,128)} %b_ref.5) | copy-start | bytes 6291460
  11.5 0.7 %copy-start.6 = (s32[16]{0:T(128)S(1)}, s32[16]{0:T(128)}, u32[]{:S(2)}) copy-start(s32[16]{0:T(128)} %second.9) | copy-start | bytes 196
  12.1 3.4 %copy-start.1 = (f32[2,256,1024]{2,1,0:T(8,128)S(1)}, f32[2,256,1024]{2,1,0:T(8,128)}, u32[]{:S(2)}) copy-start(f32[2,256,1024]{2,1,0:T(8,128)} %b_ref.5) | copy-start | bytes 6291460
  12.1 3.4 %copy-start.2 = (f32[2,72,256]{2,1,0:T(8,128)S(1)}, f32[2,72,256]{2,1,0:T(8,128)}, u32[]{:S(2)}) copy-start(f32[2,72,256]{2,1,0:T(8,128)} %shard_map.122.mp_in.mp_ref.refs_8_) | copy-start | bytes 442372
  12.1 3.4 %copy-start.3 = (f32[2,64,256]{2,1,0:T(8,128)S(1)}, f32[2,64,256]{2,1,0:T(8,128)}, u32[]{:S(2)}) copy-start(f32[2,64,256]{2,1,0:T(8,128)} %refs_6_.1) | copy-start | bytes 393220
  12.1 3.4 %copy-start.8 = (s32[16]{0:T(128)S(1)}, s32[16]{0:T(128)}, u32[]{:S(2)}) copy-start(s32[16]{0:T(128)} %first.5) | copy-start | bytes 196
  14.0 16.4 %copy-start.7 = (s32[16]{0:T(128)S(1)}, s32[16]{0:T(128)}, u32[]{:S(2)}) copy-start(s32[16]{0:T(128)} %second.9) | copy-start | bytes 196
  14.0 16.4 %copy-start.10 = (s32[16]{0:T(128)S(1)}, s32[16]{0:T(128)}, u32[]{:S(2)}) copy-start(s32[16]{0:T(128)} %ranks.3) | copy-start | bytes 196
  14.0 16.4 %copy-start.11 = (f32[8]{0:T(128)S(1)}, f32[8]{0:T(128)}, u32[]{:S(2)}) copy-start(f32[8]{0:T(128)} %occupied.3) | copy-start | bytes 100
  14.1 39.2 %copy-start.9 = (s32[16,4]{0,1:T(4,128)S(1)}, s32[16,4]{0,1:T(4,128)}, u32[]{:S(2)}) copy-start(s32[16,4]{0,1:T(4,128)} %param.17) | copy-start | bytes 772
  14.1 16.3 %collective-permute-start.1 = (f32[2,64,1024]{2,1,0:T(8,128)S(1)}, f32[2,64,1024]{2,1,0:T(8,128)S(1)}, u32[]{:S(2)}, u32[]{:S(2)}) collective-permute-start(f32[2,64,1024]{2,1,0:T(8,128)S(1)} %shard_map.125), channel_id=1, source_target_pairs={{4,0},{8,4},{12,8},{5,1},{9,5},{13,9},{6,2},{10,6},{14,10},{7,3},{... | collective-permute-start | bytes 1572872 | tf_op jit(solution)/shard_map/ppermute | solution.py:30
  17.5 12.9 %collective-permute-start.3 = (f32[2,64,1024]{2,1,0:T(8,128)S(1)}, f32[2,64,1024]{2,1,0:T(8,128)S(1)}, u32[]{:S(2)}, u32[]{:S(2)}) collective-permute-start(f32[2,64,1024]{2,1,0:T(8,128)S(1)} %get-tuple-element.30.left_ref.refs_12_), channel_id=1, source_target_pairs={{0,1},{1,0},{2,3},{3,2},{4,5},{5,4},{6,7},{7,6},{8,9},{9,8},{10,11... | collective-permute-start | bytes 1572872 | tf_op jit(solution)/shard_map/ppermute | solution.py:34
  17.6 7.0 %collective-permute-start.5 = (f32[2,72,256]{2,1,0:T(8,128)S(1)}, f32[2,72,256]{2,1,0:T(8,128)S(1)}, u32[]{:S(2)}, u32[]{:S(2)}) collective-permute-start(f32[2,72,256]{2,1,0:T(8,128)S(1)} %collective-permute-done.mp_below.refs_10_), channel_id=1, source_target_pairs={{0,1},{1,0},{2,3},{3,2},{4,5},{5,4},{6,7},{7,6},{8,9},{9,8},{10,11... | collective-permute-start | bytes 442376 | tf_op jit(solution)/shard_map/ppermute | solution.py:34
  18.1 6.5 %collective-permute-start.2 = (f32[2,72,256]{2,1,0:T(8,128)S(1)}, f32[2,72,256]{2,1,0:T(8,128)}, u32[]{:S(2)}, u32[]{:S(2)}) collective-permute-start(f32[2,72,256]{2,1,0:T(8,128)S(1)} %copy-done.2), channel_id=1, source_target_pairs={{0,1},{1,0},{2,3},{3,2},{4,5},{5,4},{6,7},{7,6},{8,9},{9,8},{10,11... | collective-permute-start | bytes 442376 | tf_op jit(solution)/shard_map/ppermute | solution.py:34
  18.2 6.4 %collective-permute-start.4 = (f32[2,64,256]{2,1,0:T(8,128)S(1)}, f32[2,64,256]{2,1,0:T(8,128)}, u32[]{:S(2)}, u32[]{:S(2)}) collective-permute-start(f32[2,64,256]{2,1,0:T(8,128)S(1)} %copy-done.3), channel_id=1, source_target_pairs={{0,1},{1,0},{2,3},{3,2},{4,5},{5,4},{6,7},{7,6},{8,9},{9,8},{10,11... | collective-permute-start | bytes 393224 | tf_op jit(solution)/shard_map/ppermute | solution.py:34
  18.6 21.6 %all-to-all-start.1 = ((f32[4,136,128]{2,1,0:T(8,128)}), f32[4,136,128]{2,1,0:T(8,128)S(1)}, u32[]{:S(2)}, u32[]{:S(2)}) async-start(f32[4,136,128]{2,1,0:T(8,128)} %shard_map.123), calls=%async_computation.1 | async-start | bytes 557056 | tf_op jit(solution)/shard_map/all_to_all | solution.py:465
  24.6 16.3 %copy-start.4 = (f32[2,72,256]{2,1,0:T(8,128)}, f32[2,72,256]{2,1,0:T(8,128)S(1)}, u32[]{:S(2)}) copy-start(f32[2,72,256]{2,1,0:T(8,128)S(1)} %collective-permute-done.5.refs_11_) | copy-start | bytes 442372
  31.4 18.7 %collective-permute-start.11 = (f32[2,64,1024]{2,1,0:T(8,128)S(1)}, f32[2,64,1024]{2,1,0:T(8,128)S(1)}, u32[]{:S(2)}, u32[]{:S(2)}) collective-permute-start(f32[2,64,1024]{2,1,0:T(8,128)S(1)} %get-tuple-element.30.left_ref.refs_12_), channel_id=1, source_target_pairs={{0,4},{4,8},{8,12},{1,5},{5,9},{9,13},{2,6},{6,10},{10,14},{3,7},{... | collective-permute-start | bytes 1572872 | tf_op jit(solution)/shard_map/ppermute | solution.py:30
  36.2 4.0 %collective-permute-start.6 = (f32[64,128]{1,0:T(8,128)S(1)}, f32[64,128]{1,0:T(8,128)S(1)}, u32[]{:S(2)}, u32[]{:S(2)}) collective-permute-start(f32[64,128]{1,0:T(8,128)S(1)} %get-tuple-element.27), channel_id=1, source_target_pairs={{0,2},{2,0},{1,3},{3,1},{4,6},{6,4},{5,7},{7,5},{8,10},{10,8},{9,1... | collective-permute-start | bytes 98312 | tf_op jit(solution)/shard_map/ppermute | solution.py:34
  40.9 9.2 %all-to-all-start = ((f32[4,64,128]{2,1,0:T(8,128)}), f32[4,64,128]{2,1,0:T(8,128)S(1)}, u32[]{:S(2)}, u32[]{:S(2)}) async-start(f32[4,64,128]{2,1,0:T(8,128)} %broadcast_in_dim.2), calls=%async_computation | async-start | bytes 262144 | tf_op jit(solution)/shard_map/all_to_all | solution.py:512
  44.2 6.7 %collective-permute-start.8 = (f32[4,136,128]{2,1,0:T(8,128)S(1)}, f32[4,136,128]{2,1,0:T(8,128)}, u32[]{:S(2)}, u32[]{:S(2)}) collective-permute-start(f32[4,136,128]{2,1,0:T(8,128)S(1)} %all-to-all-done.1.refs_2_), channel_id=1, source_target_pairs={{0,2},{2,0},{1,3},{3,1},{4,6},{6,4},{5,7},{7,5},{8,10},{10,8},{9,1... | collective-permute-start | bytes 835592 | tf_op jit(solution)/shard_map/ppermute | solution.py:34
  45.8 7.0 %collective-permute-start.13 = (f32[2,64,1024]{2,1,0:T(8,128)S(1)}, f32[2,64,1024]{2,1,0:T(8,128)S(1)}, u32[]{:S(2)}, u32[]{:S(2)}) collective-permute-start(f32[2,64,1024]{2,1,0:T(8,128)S(1)} %get-tuple-element.33.refs_16_), channel_id=1, source_target_pairs={{0,1},{1,0},{2,3},{3,2},{4,5},{5,4},{6,7},{7,6},{8,9},{9,8},{10,11... | collective-permute-start | bytes 1572872 | tf_op jit(solution)/shard_map/ppermute | solution.py:34
  50.1 3.1 %collective-permute-start.12 = (f32[2,64,1024]{2,1,0:T(8,128)S(1)}, f32[2,64,1024]{2,1,0:T(8,128)S(1)}, u32[]{:S(2)}, u32[]{:S(2)}) collective-permute-start(f32[2,64,1024]{2,1,0:T(8,128)S(1)} %collective-permute-done.11.refs_14_), channel_id=1, source_target_pairs={{0,1},{1,0},{2,3},{3,2},{4,5},{5,4},{6,7},{7,6},{8,9},{9,8},{10,11... | collective-permute-start | bytes 1572872 | tf_op jit(solution)/shard_map/ppermute | solution.py:34
  50.1 2.3 %collective-permute-start.9 = (f32[4,136,128]{2,1,0:T(8,128)S(1)}, f32[4,136,128]{2,1,0:T(8,128)S(1)}, u32[]{:S(2)}, u32[]{:S(2)}) collective-permute-start(f32[4,136,128]{2,1,0:T(8,128)S(1)} %all-to-all-done.1.refs_2_), channel_id=1, source_target_pairs={{0,1},{1,0},{2,3},{3,2},{4,5},{5,4},{6,7},{7,6},{8,9},{9,8},{10,11... | collective-permute-start | bytes 835592 | tf_op jit(solution)/shard_map/ppermute | solution.py:34
  51.0 2.3 %collective-permute-start.10 = (f32[4,136,128]{2,1,0:T(8,128)}, f32[4,136,128]{2,1,0:T(8,128)S(1)}, u32[]{:S(2)}, u32[]{:S(2)}) collective-permute-start(f32[4,136,128]{2,1,0:T(8,128)} %collective-permute-done.8.refs_3_), channel_id=1, source_target_pairs={{0,1},{1,0},{2,3},{3,2},{4,5},{5,4},{6,7},{7,6},{8,9},{9,8},{10,11... | collective-permute-start | bytes 835592 | tf_op jit(solution)/shard_map/ppermute | solution.py:34
  51.0 1.9 %collective-permute-start.7 = (f32[4,64,128]{2,1,0:T(8,128)S(1)}, f32[4,64,128]{2,1,0:T(8,128)S(1)}, u32[]{:S(2)}, u32[]{:S(2)}) collective-permute-start(f32[4,64,128]{2,1,0:T(8,128)S(1)} %all-to-all-done.refs_0_), channel_id=1, source_target_pairs={{0,1},{1,0},{2,3},{3,2},{4,5},{5,4},{6,7},{7,6},{8,9},{9,8},{10,11... | collective-permute-start | bytes 393224 | tf_op jit(solution)/shard_map/ppermute | solution.py:34
  53.2 0.9 %copy-start.5 = (f32[2,72,256]{2,1,0:T(8,128)S(1)}, f32[2,72,256]{2,1,0:T(8,128)}, u32[]{:S(2)}) copy-start(f32[2,72,256]{2,1,0:T(8,128)} %copy-done.4) | copy-start | bytes 442372

commit v19 on v18

--- a/solution.py
+++ b/solution.py
@@ -228,14 +228,14 @@
     )
 
 
-def coupled_of(z, index, pair, near, s, coupling, amps_high, amps_low, diag_high, diag_low):
+def coupled_of(z, pair, near, s, coupling, amps_high, amps_low):
     n = z.pnos
+    parts = []
     for k in range(z.links):
         row = near[k, pair]
-        block = slice(k * n, (k + 1) * n)
-        diag_high[index, block, block] = amps_high[row]
-        diag_low[index, block, block] = amps_low[row]
-    return split(mm3(s, (diag_high[index], diag_low[index])) * coupling)
+        lanes = slice(k * n, (k + 1) * n)
+        parts.append(mm3((s[0][:, lanes], s[1][:, lanes]), (amps_high[row], amps_low[row])))
+    return split(jnp.concatenate(parts, axis=1) * coupling)
 
 
 def final_kernel(z, first, second, ranks, near, occupied, *refs):
@@ -245,8 +245,7 @@
     (c_in, c_other, mp_in, mp_other, mp_below, mp_below_other, left_in, left_other, left_below,
      left_below_other, right_in, right_other) = refs[start_count + pack_count :][:12]
     (amp_out, grad_out, starts, amp_ref, packs, s_high, s_low, scale_ref, coupling_ref, s_rows, c_ref, m_ref, rhs,
-     grad, flat, amps, amps_high, amps_low, next_high, next_low, diag_high, diag_low, rows_high,
-     rows_low, sems) = refs[start_count + pack_count + 12 :]
+     grad, flat, amps, amps_high, amps_low, next_high, next_low, rows_high, rows_low, sems) = refs[start_count + pack_count + 12 :]
     owner, sub = lax.axis_index("orb"), lax.axis_index("sub")
     fit = lax.axis_index("fit")
     n, pairs, own = z.pnos, z.pairs, z.own
@@ -270,9 +269,6 @@
         [rhs.at[pl.ds(0, pairs)], rhs.at[pl.ds(pairs, pairs)]] + quarters(rhs, own),
         sems, 10,
     )
-    diag_high[...] = jnp.zeros_like(diag_high)
-    diag_low[...] = jnp.zeros_like(diag_low)
-
     wait(start_copies)
 
     def begin(pair, value):
@@ -315,24 +311,22 @@
     def s_of(pair):
         return s_high[pair], s_low[pair]
 
-    def swept(index, pair, high_amps, low_amps):
+    def swept(pair, high_amps, low_amps):
         s = s_of(pair)
         inner = coupled_of(
-            z, index, pair, near, s, coupling_ref[pair, 0:1, :], high_amps, low_amps, diag_high,
-            diag_low,
+            z, pair, near, s, coupling_ref[pair, 0:1, :], high_amps, low_amps
         )
         return amps[pair] + mm3(inner, s, ((1,), (1,))) * scale_ref[pair]
 
     if z.owners <= SMALL:
-        group = diag_high.shape[0]
+        group = 2 * own
         for base in range(0, z.total, group):
             pair_list = range(base, min(base + group, z.total))
             inner = [
                 coupled_of(
-                    z, index, pair, near, s_of(pair), coupling_ref[pair, 0:1, :], amps_high,
-                    amps_low, diag_high, diag_low,
+                    z, pair, near, s_of(pair), coupling_ref[pair, 0:1, :], amps_high, amps_low
                 )
-                for index, pair in enumerate(pair_list)
+                for pair in pair_list
             ]
             for value, pair in zip(inner, pair_list):
                 coupled = mm3(value, s_of(pair), ((1,), (1,)))
@@ -340,7 +334,7 @@
     else:
         @pl.loop(0, z.total)
         def _(pair):
-            next_high[pair], next_low[pair] = split(swept(0, pair, amps_high, amps_low))
+            next_high[pair], next_low[pair] = split(swept(pair, amps_high, amps_low))
 
     pair_list = [
         side_start(z, who, sub, side) + p
@@ -349,11 +343,8 @@
         for p in range(pairs)
     ]
     inner = [
-        coupled_of(
-            z, index, pair, near, s_of(pair), coupling_ref[pair, 0:1, :], next_high, next_low,
-            diag_high, diag_low,
-        )
-        for index, pair in enumerate(pair_list)
+        coupled_of(z, pair, near, s_of(pair), coupling_ref[pair, 0:1, :], next_high, next_low)
+        for pair in pair_list
     ]
     found = [
         amps[pair] + mm3(value, s_of(pair), ((1,), (1,))) * scale_ref[pair]
@@ -552,7 +543,6 @@
             scratch(*square),
         ]
         + [scratch(*square, kind=bf16)] * 4
-        + [scratch(2 * own, wide, wide, kind=bf16)] * 2
         + [scratch(z.orbitals * half, 3 * own * n, kind=bf16)] * 2
         + [pltpu.SemaphoreType.DMA((19 + -(-fits // 256),))],
         limit=44,

time: 63 us -> 62.6 us (level)
  no operation moved by 1% of the time
where the time goes in v19:
time: 62.6 us; the launch traced here: 62.1 us
  starting transfers between devices  25.6 us (41%)
  Pallas kernels  16.4 us (26%)
  waiting for transfers between devices  14.6 us (23%)
  local copies, waits for them, and re-layouts  4.55 us (7%)
  between operations  0.84 us (1%)
    pallas_call x7, Pallas kernels, call(): pl.pallas_call(kernel, out_shape=[jax.ShapeDtypeStruct(shape, jnp.float32...  16.4 us
    ppermute x3, starting transfers between devices, shifted(): lax.ppermute(value, axis, [(source, source + steps) for source in range(i...  11.1 us
    all_to_all x1, starting transfers between devices, body(): packs = [lax.all_to_all(pack, 'orb', 0, 0)]  5.97 us
    ppermute x3, waiting for transfers between devices, shifted(): lax.ppermute(value, axis, [(source, source + steps) for source in range(i...  5.8 us
    ppermute x11, starting transfers between devices, swapped(): return lax.ppermute(value, axis, [(0, 1), (1, 0)])  5.21 us
    ppermute x11, waiting for transfers between devices, swapped(): return lax.ppermute(value, axis, [(0, 1), (1, 0)])  4.52 us
    all_to_all x1, waiting for transfers between devices, body(): lax.all_to_all(jnp.broadcast_to(sums[None], (z.owners, *sums.shape)), 'or...  4.33 us
    all_to_all x1, starting transfers between devices, body(): lax.all_to_all(jnp.broadcast_to(sums[None], (z.owners, *sums.shape)), 'or...  3.33 us
  transfers between devices with their start and end apart: 16, of which 7 were waited for; matrix products, arithmetic and copies ran while one was open for 2% of the time, Pallas kernels for 8%

profile of v19, /device:TPU:0, one launch (start us, length us, event | category | flops | bytes accessed | tf_op | source)
XLA Modules:
  0.0 62.1 jit_solution(10124781213934202512)
XLA Ops:
  0.6 1.9 %shard_map.122.mp_in.mp_ref.refs_8_ = f32[2,72,256]{2,1,0:T(8,128)} custom-call(f32[2,64,256]{2,1,0:T(8,128)} %refs_6_.1, s32[2,256]{1,0:T(2,128)} %map_in.1, f32[2,64]{1,0:T(2,128)} %e_in.1, f32[2,4]{1,0:T(2,128)} %coupling_in.1), custom_call_target="tpu_custom_call" | custom-call | tf_op jit(solution)/shard_map/pallas_call | solution.py:58
  2.5 4.9 %collective-permute-start = (f32[2,72,256]{2,1,0:T(8,128)}, f32[2,72,256]{2,1,0:T(8,128)S(1)}, u32[]{:S(2)}, u32[]{:S(2)}) collective-permute-start(f32[2,72,256]{2,1,0:T(8,128)} %shard_map.122.mp_in.mp_ref.refs_8_), channel_id=1, source_target_pairs={{0,4},{4,8},{8,12},{1,5},{5,9},{9,13},{2,6},{6,10},{10,14},{3,7},{... | collective-permute-start | bytes 442376 | tf_op jit(solution)/shard_map/ppermute | solution.py:30
  7.5 1.7 %shard_map.123 = f32[4,136,128]{2,1,0:T(8,128)} custom-call(f32[2,4,4096]{2,1,0:T(4,128)} %s_in.1, f32[2,72,256]{2,1,0:T(8,128)} %shard_map.122.mp_in.mp_ref.refs_8_), custom_call_target="tpu_custom_call" | custom-call | tf_op jit(solution)/shard_map/pallas_call | solution.py:58
  9.2 0.7 %slice_bitcast_fusion.mp_ref = f32[8,128]{1,0:T(8,128)S(1)} fusion(f32[2,72,256]{2,1,0:T(8,128)} %shard_map.122.mp_in.mp_ref.refs_8_), kind=kLoop, calls=%fused_computation | loop fusion | bytes 8192 | tf_op jit(solution)/shard_map/squeeze | solution.py:463
  9.9 1.6 %copy-done = f32[2,256,1024]{2,1,0:T(8,128)S(1)} copy-done((f32[2,256,1024]{2,1,0:T(8,128)S(1)}, f32[2,256,1024]{2,1,0:T(8,128)}, u32[]{:S(2)}) %copy-start) | copy-done | bytes 2097176
  11.5 0.7 %copy-done.6 = s32[16]{0:T(128)S(1)} copy-done((s32[16]{0:T(128)S(1)}, s32[16]{0:T(128)}, u32[]{:S(2)}) %copy-start.6) | copy-done | bytes 88
  12.1 0.5 shard_map.124.touched
  12.7 0.0 collective-permute-done.mp_below.refs_10_
  12.7 1.3 %shard_map.125 = f32[2,64,1024]{2,1,0:T(8,128)S(1)} custom-call(s32[16]{0:T(128)S(1)} %copy-done.6, f32[2,72,256]{2,1,0:T(8,128)S(1)} %collective-permute-done.mp_below.refs_10_, f32[2,256,1024]{2,1,0:T(8,128)S(1)} %copy-done, f32[8,128]{1,0:T(8,128)S(1)} %shard_map.124.touched), custom_call_target="tpu_custom_call" | custom-call | tf_op jit(solution)/shard_map/pallas_call | solution.py:58
  14.0 0.0 copy-start.7
  14.0 0.0 copy-start.10
  14.0 0.0 copy-start.11
  14.1 0.0 copy-start.9
  14.1 1.4 %collective-permute-start.1 = (f32[2,64,1024]{2,1,0:T(8,128)S(1)}, f32[2,64,1024]{2,1,0:T(8,128)S(1)}, u32[]{:S(2)}, u32[]{:S(2)}) collective-permute-start(f32[2,64,1024]{2,1,0:T(8,128)S(1)} %shard_map.125), channel_id=1, source_target_pairs={{4,0},{8,4},{12,8},{5,1},{9,5},{13,9},{6,2},{10,6},{14,10},{7,3},{... | collective-permute-start | bytes 1572872 | tf_op jit(solution)/shard_map/ppermute | solution.py:30
  15.5 2.0 %shard_map.126 = (f32[2,64,1024]{2,1,0:T(8,128)S(1)}, f32[2,64,1024]{2,1,0:T(8,128)S(1)}) custom-call(s32[16]{0:T(128)S(1)} %copy-done.8, s32[16]{0:T(128)S(1)} %copy-done.6, f32[2,64,256]{2,1,0:T(8,128)S(1)} %copy-done.3, f32[2,72,256]{2,1,0:T(8,128)S(1)} %copy-done.2, f32[2,256,1024]{2,1,0:T(8,128)S(1)} %copy-done.1), custom_call_target="tpu_custom_call" | custom-call | flops 1 | bytes 1 | tf_op jit(solution)/shard_map/pallas_call | solution.py:58
  17.5 0.1 collective-permute-start.3
  17.6 0.5 collective-permute-start.5
  18.1 0.1 collective-permute-start.2
  18.2 0.4 collective-permute-start.4
  18.6 6.0 %all-to-all-start.1 = ((f32[4,136,128]{2,1,0:T(8,128)}), f32[4,136,128]{2,1,0:T(8,128)S(1)}, u32[]{:S(2)}, u32[]{:S(2)}) async-start(f32[4,136,128]{2,1,0:T(8,128)} %shard_map.123), calls=%async_computation.1 | async-start | bytes 557056 | tf_op jit(solution)/shard_map/all_to_all | solution.py:456
  24.6 0.0 collective-permute-done.4.refs_7_
  24.6 0.0 collective-permute-done.5.refs_11_
  24.6 0.0 collective-permute-done.2.refs_9_
  24.6 5.8 %collective-permute-done.1.down_ref = f32[2,64,1024]{2,1,0:T(8,128)S(1)} collective-permute-done((f32[2,64,1024]{2,1,0:T(8,128)S(1)}, f32[2,64,1024]{2,1,0:T(8,128)S(1)}, u32[]{:S(2)}, u32[]{:S(2)}) %collective-permute-start.1) | collective-permute-done | bytes 524320 | tf_op jit(solution)/shard_map/ppermute | solution.py:30
  30.4 0.0 collective-permute-done.3.refs_13_
  30.4 1.0 %shard_map.127 = (f32[64,128]{1,0:T(8,128)S(1)}, f32[2,64,1024]{2,1,0:T(8,128)S(1)}) custom-call(s32[16]{0:T(128)S(1)} %copy-done.8, s32[16]{0:T(128)S(1)} %copy-done.7, s32[16]{0:T(128)S(1)} %copy-done.10, f32[8]{0:T(128)S(1)} %copy-done.11, f32[2,72,256]{2,1,0:T(8,128)S(1)} %copy-done.2, f32[2,64,1024]{2,1,0:T(8,128)S(1)} %get-tuple-element.30.left_ref.refs_12_, ...), custom_call_target="tpu_custom_call" | custom-call | tf_op jit(solution)/shard_map/pallas_call | solution.py:58
  31.4 4.8 %collective-permute-start.11 = (f32[2,64,1024]{2,1,0:T(8,128)S(1)}, f32[2,64,1024]{2,1,0:T(8,128)S(1)}, u32[]{:S(2)}, u32[]{:S(2)}) collective-permute-start(f32[2,64,1024]{2,1,0:T(8,128)S(1)} %get-tuple-element.30.left_ref.refs_12_), channel_id=1, source_target_pairs={{0,4},{4,8},{8,12},{1,5},{5,9},{9,13},{2,6},{6,10},{10,14},{3,7},{... | collective-permute-start | bytes 1572872 | tf_op jit(solution)/shard_map/ppermute | solution.py:30
  36.2 1.6 %collective-permute-start.6 = (f32[64,128]{1,0:T(8,128)S(1)}, f32[64,128]{1,0:T(8,128)S(1)}, u32[]{:S(2)}, u32[]{:S(2)}) collective-permute-start(f32[64,128]{1,0:T(8,128)S(1)} %get-tuple-element.27), channel_id=1, source_target_pairs={{0,2},{2,0},{1,3},{3,1},{4,6},{6,4},{5,7},{7,5},{8,10},{10,8},{9,1... | collective-permute-start | bytes 98312 | tf_op jit(solution)/shard_map/ppermute | solution.py:34
  37.8 2.4 %collective-permute-done.6 = f32[64,128]{1,0:T(8,128)S(1)} collective-permute-done((f32[64,128]{1,0:T(8,128)S(1)}, f32[64,128]{1,0:T(8,128)S(1)}, u32[]{:S(2)}, u32[]{:S(2)}) %collective-permute-start.6) | collective-permute-done | bytes 32800 | tf_op jit(solution)/shard_map/ppermute | solution.py:34
  40.2 0.0 all-to-all-done.1.refs_2_
  40.2 0.7 %broadcast_in_dim.2 = f32[4,64,128]{2,1,0:T(8,128)} broadcast(f32[64,128]{1,0:T(8,128)S(1)} %add.3), dimensions={1,2} | broadcast | bytes 163840 | tf_op jit(solution)/shard_map/broadcast_in_dim | solution.py:503
  40.9 3.3 %all-to-all-start = ((f32[4,64,128]{2,1,0:T(8,128)}), f32[4,64,128]{2,1,0:T(8,128)S(1)}, u32[]{:S(2)}, u32[]{:S(2)}) async-start(f32[4,64,128]{2,1,0:T(8,128)} %broadcast_in_dim.2), calls=%async_computation | async-start | bytes 262144 | tf_op jit(solution)/shard_map/all_to_all | solution.py:503
  44.2 1.6 %collective-permute-start.8 = (f32[4,136,128]{2,1,0:T(8,128)S(1)}, f32[4,136,128]{2,1,0:T(8,128)}, u32[]{:S(2)}, u32[]{:S(2)}) collective-permute-start(f32[4,136,128]{2,1,0:T(8,128)S(1)} %all-to-all-done.1.refs_2_), channel_id=1, source_target_pairs={{0,2},{2,0},{1,3},{3,1},{4,6},{6,4},{5,7},{7,5},{8,10},{10,8},{9,1... | collective-permute-start | bytes 835592 | tf_op jit(solution)/shard_map/ppermute | solution.py:34
  45.8 0.0 collective-permute-start.13
  45.8 4.3 %all-to-all-done.refs_0_ = f32[4,64,128]{2,1,0:T(8,128)S(1)} async-done(((f32[4,64,128]{2,1,0:T(8,128)}), f32[4,64,128]{2,1,0:T(8,128)S(1)}, u32[]{:S(2)}, u32[]{:S(2)}) %all-to-all-start) | async-done | bytes 131104 | tf_op jit(solution)/shard_map/all_to_all | solution.py:503
  50.1 0.0 collective-permute-done.11.refs_14_
  50.1 0.0 collective-permute-start.12
  50.1 0.5 collective-permute-start.9
  50.6 0.3 collective-permute-done.8.refs_3_
  51.0 0.0 collective-permute-start.10
  51.0 0.5 collective-permute-start.7
  51.5 1.0 %collective-permute-done.9.refs_4_ = f32[4,136,128]{2,1,0:T(8,128)S(1)} collective-permute-done((f32[4,136,128]{2,1,0:T(8,128)S(1)}, f32[4,136,128]{2,1,0:T(8,128)S(1)}, u32[]{:S(2)}, u32[]{:S(2)}) %collective-permute-start.9) | collective-permute-done | bytes 278560 | tf_op jit(solution)/shard_map/ppermute | solution.py:34
  52.4 0.4 collective-permute-done.7.refs_1_
  52.8 0.0 collective-permute-done.13.refs_17_
  52.8 0.4 collective-permute-done.10.refs_5_
  53.2 0.0 collective-permute-done.12.refs_15_
  53.2 0.9 %copy-done.5 = f32[2,72,256]{2,1,0:T(8,128)S(1)} copy-done((f32[2,72,256]{2,1,0:T(8,128)S(1)}, f32[2,72,256]{2,1,0:T(8,128)}, u32[]{:S(2)}) %copy-start.5) | copy-done | bytes 147480
  54.1 7.9 %shard_map.128 = (f32[2,4096]{1,0:T(2,128)}, f32[2,128,1024]{2,1,0:T(8,128)}) custom-call(s32[16]{0:T(128)S(1)} %copy-done.8, s32[16]{0:T(128)S(1)} %copy-done.7, s32[16]{0:T(128)S(1)} %copy-done.10, s32[4,16]{1,0:T(4,128)S(1)} %bitcast.3, f32[8]{0:T(128)S(1)} %copy-done.11, f32[4,64,128]{2,1,0:T(8,128)S(1)} %all-to-all-done.refs_0_, ...), custom_call_target="tpu_custom_call" | custom-call | tf_op jit(solution)/shard_map/pallas_call | solution.py:58
  (18 shorter events, 0.0 us)
Async XLA Ops:
  2.5 10.1 %collective-permute-start = (f32[2,72,256]{2,1,0:T(8,128)}, f32[2,72,256]{2,1,0:T(8,128)S(1)}, u32[]{:S(2)}, u32[]{:S(2)}) collective-permute-start(f32[2,72,256]{2,1,0:T(8,128)} %shard_map.122.mp_in.mp_ref.refs_8_), channel_id=1, source_target_pairs={{0,4},{4,8},{8,12},{1,5},{5,9},{9,13},{2,6},{6,10},{10,14},{3,7},{... | collective-permute-start | bytes 442376 | tf_op jit(solution)/shard_map/ppermute | solution.py:30
  9.9 1.6 %copy-start = (f32[2,256,1024]{2,1,0:T(8,128)S(1)}, f32[2,256,1024]{2,1,0:T(8,128)}, u32[]{:S(2)}) copy-start(f32[2,256,1024]{2,1,0:T(8,128)} %b_ref.5) | copy-start | bytes 6291460
  11.5 0.7 %copy-start.6 = (s32[16]{0:T(128)S(1)}, s32[16]{0:T(128)}, u32[]{:S(2)}) copy-start(s32[16]{0:T(128)} %second.9) | copy-start | bytes 196
  12.1 3.4 %copy-start.1 = (f32[2,256,1024]{2,1,0:T(8,128)S(1)}, f32[2,256,1024]{2,1,0:T(8,128)}, u32[]{:S(2)}) copy-start(f32[2,256,1024]{2,1,0:T(8,128)} %b_ref.5) | copy-start | bytes 6291460
  12.1 3.4 %copy-start.2 = (f32[2,72,256]{2,1,0:T(8,128)S(1)}, f32[2,72,256]{2,1,0:T(8,128)}, u32[]{:S(2)}) copy-start(f32[2,72,256]{2,1,0:T(8,128)} %shard_map.122.mp_in.mp_ref.refs_8_) | copy-start | bytes 442372
  12.1 3.4 %copy-start.3 = (f32[2,64,256]{2,1,0:T(8,128)S(1)}, f32[2,64,256]{2,1,0:T(8,128)}, u32[]{:S(2)}) copy-start(f32[2,64,256]{2,1,0:T(8,128)} %refs_6_.1) | copy-start | bytes 393220
  12.1 3.4 %copy-start.8 = (s32[16]{0:T(128)S(1)}, s32[16]{0:T(128)}, u32[]{:S(2)}) copy-start(s32[16]{0:T(128)} %first.5) | copy-start | bytes 196
  14.0 16.4 %copy-start.7 = (s32[16]{0:T(128)S(1)}, s32[16]{0:T(128)}, u32[]{:S(2)}) copy-start(s32[16]{0:T(128)} %second.9) | copy-start | bytes 196
  14.0 16.4 %copy-start.10 = (s32[16]{0:T(128)S(1)}, s32[16]{0:T(128)}, u32[]{:S(2)}) copy-start(s32[16]{0:T(128)} %ranks.3) | copy-start | bytes 196
  14.0 16.4 %copy-start.11 = (f32[8]{0:T(128)S(1)}, f32[8]{0:T(128)}, u32[]{:S(2)}) copy-start(f32[8]{0:T(128)} %occupied.3) | copy-start | bytes 100
  14.1 39.2 %copy-start.9 = (s32[16,4]{0,1:T(4,128)S(1)}, s32[16,4]{0,1:T(4,128)}, u32[]{:S(2)}) copy-start(s32[16,4]{0,1:T(4,128)} %param.17) | copy-start | bytes 772
  14.1 16.3 %collective-permute-start.1 = (f32[2,64,1024]{2,1,0:T(8,128)S(1)}, f32[2,64,1024]{2,1,0:T(8,128)S(1)}, u32[]{:S(2)}, u32[]{:S(2)}) collective-permute-start(f32[2,64,1024]{2,1,0:T(8,128)S(1)} %shard_map.125), channel_id=1, source_target_pairs={{4,0},{8,4},{12,8},{5,1},{9,5},{13,9},{6,2},{10,6},{14,10},{7,3},{... | collective-permute-start | bytes 1572872 | tf_op jit(solution)/shard_map/ppermute | solution.py:30
  17.5 12.9 %collective-permute-start.3 = (f32[2,64,1024]{2,1,0:T(8,128)S(1)}, f32[2,64,1024]{2,1,0:T(8,128)S(1)}, u32[]{:S(2)}, u32[]{:S(2)}) collective-permute-start(f32[2,64,1024]{2,1,0:T(8,128)S(1)} %get-tuple-element.30.left_ref.refs_12_), channel_id=1, source_target_pairs={{0,1},{1,0},{2,3},{3,2},{4,5},{5,4},{6,7},{7,6},{8,9},{9,8},{10,11... | collective-permute-start | bytes 1572872 | tf_op jit(solution)/shard_map/ppermute | solution.py:34
  17.6 7.0 %collective-permute-start.5 = (f32[2,72,256]{2,1,0:T(8,128)S(1)}, f32[2,72,256]{2,1,0:T(8,128)S(1)}, u32[]{:S(2)}, u32[]{:S(2)}) collective-permute-start(f32[2,72,256]{2,1,0:T(8,128)S(1)} %collective-permute-done.mp_below.refs_10_), channel_id=1, source_target_pairs={{0,1},{1,0},{2,3},{3,2},{4,5},{5,4},{6,7},{7,6},{8,9},{9,8},{10,11... | collective-permute-start | bytes 442376 | tf_op jit(solution)/shard_map/ppermute | solution.py:34
  18.1 6.5 %collective-permute-start.2 = (f32[2,72,256]{2,1,0:T(8,128)S(1)}, f32[2,72,256]{2,1,0:T(8,128)}, u32[]{:S(2)}, u32[]{:S(2)}) collective-permute-start(f32[2,72,256]{2,1,0:T(8,128)S(1)} %copy-done.2), channel_id=1, source_target_pairs={{0,1},{1,0},{2,3},{3,2},{4,5},{5,4},{6,7},{7,6},{8,9},{9,8},{10,11... | collective-permute-start | bytes 442376 | tf_op jit(solution)/shard_map/ppermute | solution.py:34
  18.2 6.4 %collective-permute-start.4 = (f32[2,64,256]{2,1,0:T(8,128)S(1)}, f32[2,64,256]{2,1,0:T(8,128)}, u32[]{:S(2)}, u32[]{:S(2)}) collective-permute-start(f32[2,64,256]{2,1,0:T(8,128)S(1)} %copy-done.3), channel_id=1, source_target_pairs={{0,1},{1,0},{2,3},{3,2},{4,5},{5,4},{6,7},{7,6},{8,9},{9,8},{10,11... | collective-permute-start | bytes 393224 | tf_op jit(solution)/shard_map/ppermute | solution.py:34
  18.6 21.6 %all-to-all-start.1 = ((f32[4,136,128]{2,1,0:T(8,128)}), f32[4,136,128]{2,1,0:T(8,128)S(1)}, u32[]{:S(2)}, u32[]{:S(2)}) async-start(f32[4,136,128]{2,1,0:T(8,128)} %shard_map.123), calls=%async_computation.1 | async-start | bytes 557056 | tf_op jit(solution)/shard_map/all_to_all | solution.py:456
  24.6 16.3 %copy-start.4 = (f32[2,72,256]{2,1,0:T(8,128)}, f32[2,72,256]{2,1,0:T(8,128)S(1)}, u32[]{:S(2)}) copy-start(f32[2,72,256]{2,1,0:T(8,128)S(1)} %collective-permute-done.5.refs_11_) | copy-start | bytes 442372
  31.4 18.7 %collective-permute-start.11 = (f32[2,64,1024]{2,1,0:T(8,128)S(1)}, f32[2,64,1024]{2,1,0:T(8,128)S(1)}, u32[]{:S(2)}, u32[]{:S(2)}) collective-permute-start(f32[2,64,1024]{2,1,0:T(8,128)S(1)} %get-tuple-element.30.left_ref.refs_12_), channel_id=1, source_target_pairs={{0,4},{4,8},{8,12},{1,5},{5,9},{9,13},{2,6},{6,10},{10,14},{3,7},{... | collective-permute-start | bytes 1572872 | tf_op jit(solution)/shard_map/ppermute | solution.py:30
  36.2 4.0 %collective-permute-start.6 = (f32[64,128]{1,0:T(8,128)S(1)}, f32[64,128]{1,0:T(8,128)S(1)}, u32[]{:S(2)}, u32[]{:S(2)}) collective-permute-start(f32[64,128]{1,0:T(8,128)S(1)} %get-tuple-element.27), channel_id=1, source_target_pairs={{0,2},{2,0},{1,3},{3,1},{4,6},{6,4},{5,7},{7,5},{8,10},{10,8},{9,1... | collective-permute-start | bytes 98312 | tf_op jit(solution)/shard_map/ppermute | solution.py:34
  40.9 9.2 %all-to-all-start = ((f32[4,64,128]{2,1,0:T(8,128)}), f32[4,64,128]{2,1,0:T(8,128)S(1)}, u32[]{:S(2)}, u32[]{:S(2)}) async-start(f32[4,64,128]{2,1,0:T(8,128)} %broadcast_in_dim.2), calls=%async_computation | async-start | bytes 262144 | tf_op jit(solution)/shard_map/all_to_all | solution.py:503
  44.2 6.7 %collective-permute-start.8 = (f32[4,136,128]{2,1,0:T(8,128)S(1)}, f32[4,136,128]{2,1,0:T(8,128)}, u32[]{:S(2)}, u32[]{:S(2)}) collective-permute-start(f32[4,136,128]{2,1,0:T(8,128)S(1)} %all-to-all-done.1.refs_2_), channel_id=1, source_target_pairs={{0,2},{2,0},{1,3},{3,1},{4,6},{6,4},{5,7},{7,5},{8,10},{10,8},{9,1... | collective-permute-start | bytes 835592 | tf_op jit(solution)/shard_map/ppermute | solution.py:34
  45.8 7.0 %collective-permute-start.13 = (f32[2,64,1024]{2,1,0:T(8,128)S(1)}, f32[2,64,1024]{2,1,0:T(8,128)S(1)}, u32[]{:S(2)}, u32[]{:S(2)}) collective-permute-start(f32[2,64,1024]{2,1,0:T(8,128)S(1)} %get-tuple-element.33.refs_16_), channel_id=1, source_target_pairs={{0,1},{1,0},{2,3},{3,2},{4,5},{5,4},{6,7},{7,6},{8,9},{9,8},{10,11... | collective-permute-start | bytes 1572872 | tf_op jit(solution)/shard_map/ppermute | solution.py:34
  50.1 3.1 %collective-permute-start.12 = (f32[2,64,1024]{2,1,0:T(8,128)S(1)}, f32[2,64,1024]{2,1,0:T(8,128)S(1)}, u32[]{:S(2)}, u32[]{:S(2)}) collective-permute-start(f32[2,64,1024]{2,1,0:T(8,128)S(1)} %collective-permute-done.11.refs_14_), channel_id=1, source_target_pairs={{0,1},{1,0},{2,3},{3,2},{4,5},{5,4},{6,7},{7,6},{8,9},{9,8},{10,11... | collective-permute-start | bytes 1572872 | tf_op jit(solution)/shard_map/ppermute | solution.py:34
  50.1 2.3 %collective-permute-start.9 = (f32[4,136,128]{2,1,0:T(8,128)S(1)}, f32[4,136,128]{2,1,0:T(8,128)S(1)}, u32[]{:S(2)}, u32[]{:S(2)}) collective-permute-start(f32[4,136,128]{2,1,0:T(8,128)S(1)} %all-to-all-done.1.refs_2_), channel_id=1, source_target_pairs={{0,1},{1,0},{2,3},{3,2},{4,5},{5,4},{6,7},{7,6},{8,9},{9,8},{10,11... | collective-permute-start | bytes 835592 | tf_op jit(solution)/shard_map/ppermute | solution.py:34
  51.0 2.3 %collective-permute-start.10 = (f32[4,136,128]{2,1,0:T(8,128)}, f32[4,136,128]{2,1,0:T(8,128)S(1)}, u32[]{:S(2)}, u32[]{:S(2)}) collective-permute-start(f32[4,136,128]{2,1,0:T(8,128)} %collective-permute-done.8.refs_3_), channel_id=1, source_target_pairs={{0,1},{1,0},{2,3},{3,2},{4,5},{5,4},{6,7},{7,6},{8,9},{9,8},{10,11... | collective-permute-start | bytes 835592 | tf_op jit(solution)/shard_map/ppermute | solution.py:34
  51.0 1.9 %collective-permute-start.7 = (f32[4,64,128]{2,1,0:T(8,128)S(1)}, f32[4,64,128]{2,1,0:T(8,128)S(1)}, u32[]{:S(2)}, u32[]{:S(2)}) collective-permute-start(f32[4,64,128]{2,1,0:T(8,128)S(1)} %all-to-all-done.refs_0_), channel_id=1, source_target_pairs={{0,1},{1,0},{2,3},{3,2},{4,5},{5,4},{6,7},{7,6},{8,9},{9,8},{10,11... | collective-permute-start | bytes 393224 | tf_op jit(solution)/shard_map/ppermute | solution.py:34
  53.2 0.9 %copy-start.5 = (f32[2,72,256]{2,1,0:T(8,128)S(1)}, f32[2,72,256]{2,1,0:T(8,128)}, u32[]{:S(2)}) copy-start(f32[2,72,256]{2,1,0:T(8,128)} %copy-done.4) | copy-start | bytes 442372

commit v20 on v19

--- a/solution.py
+++ b/solution.py
@@ -179,8 +179,8 @@
         right_ref[p] = mm(mapped, b_ref[jnp.clip(j, 0, z.orbitals - 1)])
 
 
-def early_kernel(z, second, mp_ref, b_ref, out_ref):
-    out_ref[...] = b_ref[0, :EXTRA, :128] + mp_ref[...] + second[0].astype(jnp.float32)
+def early_kernel(z, second, b_ref, out_ref):
+    out_ref[...] = b_ref[0, :EXTRA, :128] + second[0].astype(jnp.float32)
 
 
 def local_kernel(z, first, second, c_ref, mp_ref, b_ref, left_ref, right_ref):
@@ -459,8 +459,8 @@
     (touched,) = call(
         functools.partial(early_kernel, z),
         [(EXTRA, 128)],
-        [smem, vmem, vmem],
-        (pair_second, mp[0, :EXTRA, :128], blocks),
+        [smem, vmem],
+        (gate((pair_second,), mp)[0], blocks),
         limit=8,
     )
     (right_below,) = call(

time: 62.6 us -> 61.9 us (0.989)
  local copies, waits for them, and re-layouts: 4.55 us -> 3.86 us
    squeeze x1 -> x0, local copies, waits for them, and re-layouts: 0.68 us -> none  [body(): mp[0, :EXTRA, :128]]
  transfers between devices with their start and end apart: 16 -> 16, of which waited for: 7 -> 7; matrix products, arithmetic and copies ran while one was open for 2% -> 1% of each run, Pallas kernels for 8% -> 9%
where the time goes in v20:
time: 61.9 us; the launch traced here: 61.4 us
  starting transfers between devices  25.6 us (41%)
  Pallas kernels  16.4 us (26%)
  waiting for transfers between devices  14.6 us (24%)
  local copies, waits for them, and re-layouts  3.86 us (6%)
  between operations  0.85 us (1%)
    pallas_call x7, Pallas kernels, call(): pl.pallas_call(kernel, out_shape=[jax.ShapeDtypeStruct(shape, jnp.float32...  16.4 us
    ppermute x3, starting transfers between devices, shifted(): lax.ppermute(value, axis, [(source, source + steps) for source in range(i...  11.1 us
    all_to_all x1, starting transfers between devices, body(): packs = [lax.all_to_all(pack, 'orb', 0, 0)]  5.97 us
    ppermute x3, waiting for transfers between devices, shifted(): lax.ppermute(value, axis, [(source, source + steps) for source in range(i...  5.8 us
    ppermute x11, starting transfers between devices, swapped(): return lax.ppermute(value, axis, [(0, 1), (1, 0)])  5.21 us
    ppermute x11, waiting for transfers between devices, swapped(): return lax.ppermute(value, axis, [(0, 1), (1, 0)])  4.52 us
    all_to_all x1, waiting for transfers between devices, body(): lax.all_to_all(jnp.broadcast_to(sums[None], (z.owners, *sums.shape)), 'or...  4.33 us
    all_to_all x1, starting transfers between devices, body(): lax.all_to_all(jnp.broadcast_to(sums[None], (z.owners, *sums.shape)), 'or...  3.33 us
  transfers between devices with their start and end apart: 16, of which 7 were waited for; matrix products, arithmetic and copies ran while one was open for 1% of the time, Pallas kernels for 9%

profile of v20, /device:TPU:0, one launch (start us, length us, event | category | flops | bytes accessed | tf_op | source)
XLA Modules:
  0.0 61.4 jit_solution(10154397088701003058)
XLA Ops:
  0.6 1.9 %shard_map.122.mp_in.mp_ref.refs_8_ = f32[2,72,256]{2,1,0:T(8,128)} custom-call(f32[2,64,256]{2,1,0:T(8,128)} %refs_6_.1, s32[2,256]{1,0:T(2,128)} %map_in.1, f32[2,64]{1,0:T(2,128)} %e_in.1, f32[2,4]{1,0:T(2,128)} %coupling_in.1), custom_call_target="tpu_custom_call" | custom-call | tf_op jit(solution)/shard_map/pallas_call | solution.py:58
  2.5 4.9 %collective-permute-start = (f32[2,72,256]{2,1,0:T(8,128)}, f32[2,72,256]{2,1,0:T(8,128)S(1)}, u32[]{:S(2)}, u32[]{:S(2)}) collective-permute-start(f32[2,72,256]{2,1,0:T(8,128)} %shard_map.122.mp_in.mp_ref.refs_8_), channel_id=1, source_target_pairs={{0,4},{4,8},{8,12},{1,5},{5,9},{9,13},{2,6},{6,10},{10,14},{3,7},{... | collective-permute-start | bytes 442376 | tf_op jit(solution)/shard_map/ppermute | solution.py:30
  7.5 1.7 %shard_map.123 = f32[4,136,128]{2,1,0:T(8,128)} custom-call(f32[2,4,4096]{2,1,0:T(4,128)} %s_in.1, f32[2,72,256]{2,1,0:T(8,128)} %shard_map.122.mp_in.mp_ref.refs_8_), custom_call_target="tpu_custom_call" | custom-call | tf_op jit(solution)/shard_map/pallas_call | solution.py:58
  9.2 0.0 copy-start
  9.2 1.6 %copy-done = f32[2,256,1024]{2,1,0:T(8,128)S(1)} copy-done((f32[2,256,1024]{2,1,0:T(8,128)S(1)}, f32[2,256,1024]{2,1,0:T(8,128)}, u32[]{:S(2)}) %copy-start) | copy-done | bytes 2097176
  10.8 0.7 %copy-done.6 = s32[16]{0:T(128)S(1)} copy-done((s32[16]{0:T(128)S(1)}, s32[16]{0:T(128)}, u32[]{:S(2)}) %copy-start.6) | copy-done | bytes 88
  11.4 0.5 shard_map.124.touched
  12.0 0.0 collective-permute-done.mp_below.refs_10_
  12.0 1.3 %shard_map.125 = f32[2,64,1024]{2,1,0:T(8,128)S(1)} custom-call(s32[16]{0:T(128)S(1)} %copy-done.6, f32[2,72,256]{2,1,0:T(8,128)S(1)} %collective-permute-done.mp_below.refs_10_, f32[2,256,1024]{2,1,0:T(8,128)S(1)} %copy-done, f32[8,128]{1,0:T(8,128)S(1)} %shard_map.124.touched), custom_call_target="tpu_custom_call" | custom-call | tf_op jit(solution)/shard_map/pallas_call | solution.py:58
  13.3 0.0 copy-start.7
  13.3 0.0 copy-start.10
  13.4 0.0 copy-start.11
  13.4 0.0 copy-start.9
  13.4 1.4 %collective-permute-start.1 = (f32[2,64,1024]{2,1,0:T(8,128)S(1)}, f32[2,64,1024]{2,1,0:T(8,128)S(1)}, u32[]{:S(2)}, u32[]{:S(2)}) collective-permute-start(f32[2,64,1024]{2,1,0:T(8,128)S(1)} %shard_map.125), channel_id=1, source_target_pairs={{4,0},{8,4},{12,8},{5,1},{9,5},{13,9},{6,2},{10,6},{14,10},{7,3},{... | collective-permute-start | bytes 1572872 | tf_op jit(solution)/shard_map/ppermute | solution.py:30
  14.9 2.0 %shard_map.126 = (f32[2,64,1024]{2,1,0:T(8,128)S(1)}, f32[2,64,1024]{2,1,0:T(8,128)S(1)}) custom-call(s32[16]{0:T(128)S(1)} %copy-done.8, s32[16]{0:T(128)S(1)} %copy-done.6, f32[2,64,256]{2,1,0:T(8,128)S(1)} %copy-done.3, f32[2,72,256]{2,1,0:T(8,128)S(1)} %copy-done.2, f32[2,256,1024]{2,1,0:T(8,128)S(1)} %copy-done.1), custom_call_target="tpu_custom_call" | custom-call | flops 1 | bytes 1 | tf_op jit(solution)/shard_map/pallas_call | solution.py:58
  16.9 0.1 collective-permute-start.3
  16.9 0.5 collective-permute-start.5
  17.4 0.1 collective-permute-start.2
  17.5 0.4 collective-permute-start.4
  17.9 6.0 %all-to-all-start.1 = ((f32[4,136,128]{2,1,0:T(8,128)}), f32[4,136,128]{2,1,0:T(8,128)S(1)}, u32[]{:S(2)}, u32[]{:S(2)}) async-start(f32[4,136,128]{2,1,0:T(8,128)} %shard_map.123), calls=%async_computation.1 | async-start | bytes 557056 | tf_op jit(solution)/shard_map/all_to_all | solution.py:456
  23.9 0.0 collective-permute-done.4.refs_7_
  23.9 0.0 collective-permute-done.5.refs_11_
  23.9 0.0 collective-permute-done.2.refs_9_
  23.9 5.8 %collective-permute-done.1.down_ref = f32[2,64,1024]{2,1,0:T(8,128)S(1)} collective-permute-done((f32[2,64,1024]{2,1,0:T(8,128)S(1)}, f32[2,64,1024]{2,1,0:T(8,128)S(1)}, u32[]{:S(2)}, u32[]{:S(2)}) %collective-permute-start.1) | collective-permute-done | bytes 524320 | tf_op jit(solution)/shard_map/ppermute | solution.py:30
  29.7 0.0 collective-permute-done.3.refs_13_
  29.8 1.0 %shard_map.127 = (f32[64,128]{1,0:T(8,128)S(1)}, f32[2,64,1024]{2,1,0:T(8,128)S(1)}) custom-call(s32[16]{0:T(128)S(1)} %copy-done.8, s32[16]{0:T(128)S(1)} %copy-done.7, s32[16]{0:T(128)S(1)} %copy-done.10, f32[8]{0:T(128)S(1)} %copy-done.11, f32[2,72,256]{2,1,0:T(8,128)S(1)} %copy-done.2, f32[2,64,1024]{2,1,0:T(8,128)S(1)} %get-tuple-element.32.left_ref.refs_12_, ...), custom_call_target="tpu_custom_call" | custom-call | tf_op jit(solution)/shard_map/pallas_call | solution.py:58
  30.8 4.8 %collective-permute-start.11 = (f32[2,64,1024]{2,1,0:T(8,128)S(1)}, f32[2,64,1024]{2,1,0:T(8,128)S(1)}, u32[]{:S(2)}, u32[]{:S(2)}) collective-permute-start(f32[2,64,1024]{2,1,0:T(8,128)S(1)} %get-tuple-element.32.left_ref.refs_12_), channel_id=1, source_target_pairs={{0,4},{4,8},{8,12},{1,5},{5,9},{9,13},{2,6},{6,10},{10,14},{3,7},{... | collective-permute-start | bytes 1572872 | tf_op jit(solution)/shard_map/ppermute | solution.py:30
  35.6 1.6 %collective-permute-start.6 = (f32[64,128]{1,0:T(8,128)S(1)}, f32[64,128]{1,0:T(8,128)S(1)}, u32[]{:S(2)}, u32[]{:S(2)}) collective-permute-start(f32[64,128]{1,0:T(8,128)S(1)} %get-tuple-element.29), channel_id=1, source_target_pairs={{0,2},{2,0},{1,3},{3,1},{4,6},{6,4},{5,7},{7,5},{8,10},{10,8},{9,1... | collective-permute-start | bytes 98312 | tf_op jit(solution)/shard_map/ppermute | solution.py:34
  37.1 2.4 %collective-permute-done.6 = f32[64,128]{1,0:T(8,128)S(1)} collective-permute-done((f32[64,128]{1,0:T(8,128)S(1)}, f32[64,128]{1,0:T(8,128)S(1)}, u32[]{:S(2)}, u32[]{:S(2)}) %collective-permute-start.6) | collective-permute-done | bytes 32800 | tf_op jit(solution)/shard_map/ppermute | solution.py:34
  39.5 0.0 all-to-all-done.1.refs_2_
  39.5 0.7 %broadcast_in_dim.2 = f32[4,64,128]{2,1,0:T(8,128)} broadcast(f32[64,128]{1,0:T(8,128)S(1)} %add.3), dimensions={1,2} | broadcast | bytes 163840 | tf_op jit(solution)/shard_map/broadcast_in_dim | solution.py:503
  40.2 3.3 %all-to-all-start = ((f32[4,64,128]{2,1,0:T(8,128)}), f32[4,64,128]{2,1,0:T(8,128)S(1)}, u32[]{:S(2)}, u32[]{:S(2)}) async-start(f32[4,64,128]{2,1,0:T(8,128)} %broadcast_in_dim.2), calls=%async_computation | async-start | bytes 262144 | tf_op jit(solution)/shard_map/all_to_all | solution.py:503
  43.6 1.6 %collective-permute-start.8 = (f32[4,136,128]{2,1,0:T(8,128)S(1)}, f32[4,136,128]{2,1,0:T(8,128)}, u32[]{:S(2)}, u32[]{:S(2)}) collective-permute-start(f32[4,136,128]{2,1,0:T(8,128)S(1)} %all-to-all-done.1.refs_2_), channel_id=1, source_target_pairs={{0,2},{2,0},{1,3},{3,1},{4,6},{6,4},{5,7},{7,5},{8,10},{10,8},{9,1... | collective-permute-start | bytes 835592 | tf_op jit(solution)/shard_map/ppermute | solution.py:34
  45.1 0.0 collective-permute-start.13
  45.1 4.3 %all-to-all-done.refs_0_ = f32[4,64,128]{2,1,0:T(8,128)S(1)} async-done(((f32[4,64,128]{2,1,0:T(8,128)}), f32[4,64,128]{2,1,0:T(8,128)S(1)}, u32[]{:S(2)}, u32[]{:S(2)}) %all-to-all-start) | async-done | bytes 131104 | tf_op jit(solution)/shard_map/all_to_all | solution.py:503
  49.4 0.0 collective-permute-done.11.refs_14_
  49.4 0.0 collective-permute-start.12
  49.4 0.5 collective-permute-start.9
  50.0 0.3 collective-permute-done.8.refs_3_
  50.3 0.0 collective-permute-start.10
  50.3 0.5 collective-permute-start.7
  50.8 1.0 %collective-permute-done.9.refs_4_ = f32[4,136,128]{2,1,0:T(8,128)S(1)} collective-permute-done((f32[4,136,128]{2,1,0:T(8,128)S(1)}, f32[4,136,128]{2,1,0:T(8,128)S(1)}, u32[]{:S(2)}, u32[]{:S(2)}) %collective-permute-start.9) | collective-permute-done | bytes 278560 | tf_op jit(solution)/shard_map/ppermute | solution.py:34
  51.8 0.4 collective-permute-done.7.refs_1_
  52.1 0.0 collective-permute-done.13.refs_17_
  52.1 0.4 collective-permute-done.10.refs_5_
  52.5 0.0 collective-permute-done.12.refs_15_
  52.6 0.9 %copy-done.5 = f32[2,72,256]{2,1,0:T(8,128)S(1)} copy-done((f32[2,72,256]{2,1,0:T(8,128)S(1)}, f32[2,72,256]{2,1,0:T(8,128)}, u32[]{:S(2)}) %copy-start.5) | copy-done | bytes 147480
  53.5 7.9 %shard_map.128 = (f32[2,4096]{1,0:T(2,128)}, f32[2,128,1024]{2,1,0:T(8,128)}) custom-call(s32[16]{0:T(128)S(1)} %copy-done.8, s32[16]{0:T(128)S(1)} %copy-done.7, s32[16]{0:T(128)S(1)} %copy-done.10, s32[4,16]{1,0:T(4,128)S(1)} %bitcast.1, f32[8]{0:T(128)S(1)} %copy-done.11, f32[4,64,128]{2,1,0:T(8,128)S(1)} %all-to-all-done.refs_0_, ...), custom_call_target="tpu_custom_call" | custom-call | tf_op jit(solution)/shard_map/pallas_call | solution.py:58
  (17 shorter events, 0.0 us)
Async XLA Ops:
  2.5 9.5 %collective-permute-start = (f32[2,72,256]{2,1,0:T(8,128)}, f32[2,72,256]{2,1,0:T(8,128)S(1)}, u32[]{:S(2)}, u32[]{:S(2)}) collective-permute-start(f32[2,72,256]{2,1,0:T(8,128)} %shard_map.122.mp_in.mp_ref.refs_8_), channel_id=1, source_target_pairs={{0,4},{4,8},{8,12},{1,5},{5,9},{9,13},{2,6},{6,10},{10,14},{3,7},{... | collective-permute-start | bytes 442376 | tf_op jit(solution)/shard_map/ppermute | solution.py:30
  9.2 1.6 %copy-start = (f32[2,256,1024]{2,1,0:T(8,128)S(1)}, f32[2,256,1024]{2,1,0:T(8,128)}, u32[]{:S(2)}) copy-start(f32[2,256,1024]{2,1,0:T(8,128)} %b_ref.5) | copy-start | bytes 6291460
  10.8 0.7 %copy-start.6 = (s32[16]{0:T(128)S(1)}, s32[16]{0:T(128)}, u32[]{:S(2)}) copy-start(s32[16]{0:T(128)} %second.8) | copy-start | bytes 196
  11.4 3.4 %copy-start.1 = (f32[2,256,1024]{2,1,0:T(8,128)S(1)}, f32[2,256,1024]{2,1,0:T(8,128)}, u32[]{:S(2)}) copy-start(f32[2,256,1024]{2,1,0:T(8,128)} %b_ref.5) | copy-start | bytes 6291460
  11.4 3.4 %copy-start.2 = (f32[2,72,256]{2,1,0:T(8,128)S(1)}, f32[2,72,256]{2,1,0:T(8,128)}, u32[]{:S(2)}) copy-start(f32[2,72,256]{2,1,0:T(8,128)} %shard_map.122.mp_in.mp_ref.refs_8_) | copy-start | bytes 442372
  11.4 3.4 %copy-start.3 = (f32[2,64,256]{2,1,0:T(8,128)S(1)}, f32[2,64,256]{2,1,0:T(8,128)}, u32[]{:S(2)}) copy-start(f32[2,64,256]{2,1,0:T(8,128)} %refs_6_.1) | copy-start | bytes 393220
  11.4 3.4 %copy-start.8 = (s32[16]{0:T(128)S(1)}, s32[16]{0:T(128)}, u32[]{:S(2)}) copy-start(s32[16]{0:T(128)} %first.5) | copy-start | bytes 196
  13.3 16.4 %copy-start.7 = (s32[16]{0:T(128)S(1)}, s32[16]{0:T(128)}, u32[]{:S(2)}) copy-start(s32[16]{0:T(128)} %second.8) | copy-start | bytes 196
  13.3 16.4 %copy-start.10 = (s32[16]{0:T(128)S(1)}, s32[16]{0:T(128)}, u32[]{:S(2)}) copy-start(s32[16]{0:T(128)} %ranks.3) | copy-start | bytes 196
  13.4 16.4 %copy-start.11 = (f32[8]{0:T(128)S(1)}, f32[8]{0:T(128)}, u32[]{:S(2)}) copy-start(f32[8]{0:T(128)} %occupied.3) | copy-start | bytes 100
  13.4 39.2 %copy-start.9 = (s32[16,4]{0,1:T(4,128)S(1)}, s32[16,4]{0,1:T(4,128)}, u32[]{:S(2)}) copy-start(s32[16,4]{0,1:T(4,128)} %param.17) | copy-start | bytes 772
  13.4 16.3 %collective-permute-start.1 = (f32[2,64,1024]{2,1,0:T(8,128)S(1)}, f32[2,64,1024]{2,1,0:T(8,128)S(1)}, u32[]{:S(2)}, u32[]{:S(2)}) collective-permute-start(f32[2,64,1024]{2,1,0:T(8,128)S(1)} %shard_map.125), channel_id=1, source_target_pairs={{4,0},{8,4},{12,8},{5,1},{9,5},{13,9},{6,2},{10,6},{14,10},{7,3},{... | collective-permute-start | bytes 1572872 | tf_op jit(solution)/shard_map/ppermute | solution.py:30
  16.9 12.9 %collective-permute-start.3 = (f32[2,64,1024]{2,1,0:T(8,128)S(1)}, f32[2,64,1024]{2,1,0:T(8,128)S(1)}, u32[]{:S(2)}, u32[]{:S(2)}) collective-permute-start(f32[2,64,1024]{2,1,0:T(8,128)S(1)} %get-tuple-element.32.left_ref.refs_12_), channel_id=1, source_target_pairs={{0,1},{1,0},{2,3},{3,2},{4,5},{5,4},{6,7},{7,6},{8,9},{9,8},{10,11... | collective-permute-start | bytes 1572872 | tf_op jit(solution)/shard_map/ppermute | solution.py:34
  16.9 7.0 %collective-permute-start.5 = (f32[2,72,256]{2,1,0:T(8,128)S(1)}, f32[2,72,256]{2,1,0:T(8,128)S(1)}, u32[]{:S(2)}, u32[]{:S(2)}) collective-permute-start(f32[2,72,256]{2,1,0:T(8,128)S(1)} %collective-permute-done.mp_below.refs_10_), channel_id=1, source_target_pairs={{0,1},{1,0},{2,3},{3,2},{4,5},{5,4},{6,7},{7,6},{8,9},{9,8},{10,11... | collective-permute-start | bytes 442376 | tf_op jit(solution)/shard_map/ppermute | solution.py:34
  17.4 6.5 %collective-permute-start.2 = (f32[2,72,256]{2,1,0:T(8,128)S(1)}, f32[2,72,256]{2,1,0:T(8,128)}, u32[]{:S(2)}, u32[]{:S(2)}) collective-permute-start(f32[2,72,256]{2,1,0:T(8,128)S(1)} %copy-done.2), channel_id=1, source_target_pairs={{0,1},{1,0},{2,3},{3,2},{4,5},{5,4},{6,7},{7,6},{8,9},{9,8},{10,11... | collective-permute-start | bytes 442376 | tf_op jit(solution)/shard_map/ppermute | solution.py:34
  17.5 6.4 %collective-permute-start.4 = (f32[2,64,256]{2,1,0:T(8,128)S(1)}, f32[2,64,256]{2,1,0:T(8,128)}, u32[]{:S(2)}, u32[]{:S(2)}) collective-permute-start(f32[2,64,256]{2,1,0:T(8,128)S(1)} %copy-done.3), channel_id=1, source_target_pairs={{0,1},{1,0},{2,3},{3,2},{4,5},{5,4},{6,7},{7,6},{8,9},{9,8},{10,11... | collective-permute-start | bytes 393224 | tf_op jit(solution)/shard_map/ppermute | solution.py:34
  17.9 21.6 %all-to-all-start.1 = ((f32[4,136,128]{2,1,0:T(8,128)}), f32[4,136,128]{2,1,0:T(8,128)S(1)}, u32[]{:S(2)}, u32[]{:S(2)}) async-start(f32[4,136,128]{2,1,0:T(8,128)} %shard_map.123), calls=%async_computation.1 | async-start | bytes 557056 | tf_op jit(solution)/shard_map/all_to_all | solution.py:456
  23.9 16.3 %copy-start.4 = (f32[2,72,256]{2,1,0:T(8,128)}, f32[2,72,256]{2,1,0:T(8,128)S(1)}, u32[]{:S(2)}) copy-start(f32[2,72,256]{2,1,0:T(8,128)S(1)} %collective-permute-done.5.refs_11_) | copy-start | bytes 442372
  30.8 18.7 %collective-permute-start.11 = (f32[2,64,1024]{2,1,0:T(8,128)S(1)}, f32[2,64,1024]{2,1,0:T(8,128)S(1)}, u32[]{:S(2)}, u32[]{:S(2)}) collective-permute-start(f32[2,64,1024]{2,1,0:T(8,128)S(1)} %get-tuple-element.32.left_ref.refs_12_), channel_id=1, source_target_pairs={{0,4},{4,8},{8,12},{1,5},{5,9},{9,13},{2,6},{6,10},{10,14},{3,7},{... | collective-permute-start | bytes 1572872 | tf_op jit(solution)/shard_map/ppermute | solution.py:30
  35.6 4.0 %collective-permute-start.6 = (f32[64,128]{1,0:T(8,128)S(1)}, f32[64,128]{1,0:T(8,128)S(1)}, u32[]{:S(2)}, u32[]{:S(2)}) collective-permute-start(f32[64,128]{1,0:T(8,128)S(1)} %get-tuple-element.29), channel_id=1, source_target_pairs={{0,2},{2,0},{1,3},{3,1},{4,6},{6,4},{5,7},{7,5},{8,10},{10,8},{9,1... | collective-permute-start | bytes 98312 | tf_op jit(solution)/shard_map/ppermute | solution.py:34
  40.2 9.2 %all-to-all-start = ((f32[4,64,128]{2,1,0:T(8,128)}), f32[4,64,128]{2,1,0:T(8,128)S(1)}, u32[]{:S(2)}, u32[]{:S(2)}) async-start(f32[4,64,128]{2,1,0:T(8,128)} %broadcast_in_dim.2), calls=%async_computation | async-start | bytes 262144 | tf_op jit(solution)/shard_map/all_to_all | solution.py:503
  43.6 6.7 %collective-permute-start.8 = (f32[4,136,128]{2,1,0:T(8,128)S(1)}, f32[4,136,128]{2,1,0:T(8,128)}, u32[]{:S(2)}, u32[]{:S(2)}) collective-permute-start(f32[4,136,128]{2,1,0:T(8,128)S(1)} %all-to-all-done.1.refs_2_), channel_id=1, source_target_pairs={{0,2},{2,0},{1,3},{3,1},{4,6},{6,4},{5,7},{7,5},{8,10},{10,8},{9,1... | collective-permute-start | bytes 835592 | tf_op jit(solution)/shard_map/ppermute | solution.py:34
  45.1 7.0 %collective-permute-start.13 = (f32[2,64,1024]{2,1,0:T(8,128)S(1)}, f32[2,64,1024]{2,1,0:T(8,128)S(1)}, u32[]{:S(2)}, u32[]{:S(2)}) collective-permute-start(f32[2,64,1024]{2,1,0:T(8,128)S(1)} %get-tuple-element.35.refs_16_), channel_id=1, source_target_pairs={{0,1},{1,0},{2,3},{3,2},{4,5},{5,4},{6,7},{7,6},{8,9},{9,8},{10,11... | collective-permute-start | bytes 1572872 | tf_op jit(solution)/shard_map/ppermute | solution.py:34
  49.4 3.1 %collective-permute-start.12 = (f32[2,64,1024]{2,1,0:T(8,128)S(1)}, f32[2,64,1024]{2,1,0:T(8,128)S(1)}, u32[]{:S(2)}, u32[]{:S(2)}) collective-permute-start(f32[2,64,1024]{2,1,0:T(8,128)S(1)} %collective-permute-done.11.refs_14_), channel_id=1, source_target_pairs={{0,1},{1,0},{2,3},{3,2},{4,5},{5,4},{6,7},{7,6},{8,9},{9,8},{10,11... | collective-permute-start | bytes 1572872 | tf_op jit(solution)/shard_map/ppermute | solution.py:34
  49.4 2.3 %collective-permute-start.9 = (f32[4,136,128]{2,1,0:T(8,128)S(1)}, f32[4,136,128]{2,1,0:T(8,128)S(1)}, u32[]{:S(2)}, u32[]{:S(2)}) collective-permute-start(f32[4,136,128]{2,1,0:T(8,128)S(1)} %all-to-all-done.1.refs_2_), channel_id=1, source_target_pairs={{0,1},{1,0},{2,3},{3,2},{4,5},{5,4},{6,7},{7,6},{8,9},{9,8},{10,11... | collective-permute-start | bytes 835592 | tf_op jit(solution)/shard_map/ppermute | solution.py:34
  50.3 2.3 %collective-permute-start.10 = (f32[4,136,128]{2,1,0:T(8,128)}, f32[4,136,128]{2,1,0:T(8,128)S(1)}, u32[]{:S(2)}, u32[]{:S(2)}) collective-permute-start(f32[4,136,128]{2,1,0:T(8,128)} %collective-permute-done.8.refs_3_), channel_id=1, source_target_pairs={{0,1},{1,0},{2,3},{3,2},{4,5},{5,4},{6,7},{7,6},{8,9},{9,8},{10,11... | collective-permute-start | bytes 835592 | tf_op jit(solution)/shard_map/ppermute | solution.py:34
  50.3 1.9 %collective-permute-start.7 = (f32[4,64,128]{2,1,0:T(8,128)S(1)}, f32[4,64,128]{2,1,0:T(8,128)S(1)}, u32[]{:S(2)}, u32[]{:S(2)}) collective-permute-start(f32[4,64,128]{2,1,0:T(8,128)S(1)} %all-to-all-done.refs_0_), channel_id=1, source_target_pairs={{0,1},{1,0},{2,3},{3,2},{4,5},{5,4},{6,7},{7,6},{8,9},{9,8},{10,11... | collective-permute-start | bytes 393224 | tf_op jit(solution)/shard_map/ppermute | solution.py:34
  52.6 0.9 %copy-start.5 = (f32[2,72,256]{2,1,0:T(8,128)S(1)}, f32[2,72,256]{2,1,0:T(8,128)}, u32[]{:S(2)}) copy-start(f32[2,72,256]{2,1,0:T(8,128)} %copy-done.4) | copy-start | bytes 442372
